TPU v7x, 32 devices: a whole 2x2x4 slice. The times are simulated.
32 devices in a mesh: pool: 2 (over y), row: 4 (over z), col: 4 (over x, core).
Axes of the slice: x: 2, y: 2, z: 4, core: 2. Of those that a mesh axis runs over, the one named last changes fastest.
Arguments:
- trial_vectors: bfloat16 [256, 16384], P('col', ('pool', 'row')), parts along dimension 1, may hold values from -6 to 6
- hamiltonian_blocks: bfloat16 [128, 9, 128, 128], P(('pool', 'row')), parts along dimension 0, may hold values from -0.09375 to 0.09375
- correlation_offset: bfloat16 [128, 9, 128, 128], P(('pool', 'row')), parts along dimension 0, may hold values from -0.0625 to 0.0625
- block_columns: int32 [128, 9], P(('pool', 'row')), parts along dimension 0, may hold values from 0 to 63, as said below
- block_phases: int32 [128, 9], P(('pool', 'row')), parts along dimension 0, may hold values from 0 to 1
- block_sizes: int32 [128], P(('pool', 'row')), parts along dimension 0, may hold values from 64 to 128
- shift: float32 [2], P('pool'), parts along dimension 0, may hold values from -0.25 to 0.25
- halfwidth: float32 [2], P('pool'), parts along dimension 0, may hold values from 0.6 to 0.9
Outputs:
- basis: bfloat16 [256, 16384], P('col', ('pool', 'row')), parts along dimension 1
- reduced_h: float32 [512, 256], P('pool', 'col'), parts along dimension 0
There are 2 independent parts, one for each index of `pool`. A program takes and returns all parts, laid end to end along the dimension named above; each array names one. Nothing has to cross between parts.
Inputs may be any that keep to these rules, and one draw needn't show every extreme that they name: `block_columns`: counted periodically over 64 block rows, every entry of row r lies within 5 of r; the first three slots of row r hold r, r - 5 and r + 5, in this order, and no row holds a block column twice.
All inputs are finite; a program needn't handle non-finite values.
Results may differ from a plain program's by a relative error of at most 0.013.
Values may be sent and summed in bfloat16 or wider, within the bound.
No kernel may reach another device: no remote copies, remote signals or barrier semaphores. Data moves between devices by JAX's collectives and lax.ppermute only.
A program may use at most 64 MiB of HBM per device.

v0:
```python
import functools

import jax
import jax.numpy as jnp
from jax import lax
from jax.experimental import pallas as pl
from jax.experimental.pallas import tpu as pltpu
from jax.sharding import PartitionSpec as P

HALF_BAND = 5
DEGREE = 4
CORES = 2
PANEL = 32
GROUP = 8

BF16 = jnp.bfloat16
F32 = jnp.float32
NT = (((1,), (1,)), ((), ()))
TN = (((0,), (0,)), ((), ()))

SMEM = pl.BlockSpec(memory_space=pltpu.SMEM)
VMEM = pl.BlockSpec(memory_space=pltpu.VMEM)


def vmem(shape, dtype):
    return pltpu.VMEM(shape, dtype)


def fill_ext(core, own, intra, inter, ext):
    half = own.shape[0]
    ext[HALF_BAND : HALF_BAND + half] = own[...]
    ext[pl.ds((half + HALF_BAND) * (1 - core), HALF_BAND)] = intra[...]
    ext[pl.ds((half + HALF_BAND) * core, HALF_BAND)] = inter[...]


def picked(index, ext, row, slots):
    return jnp.concatenate([ext[index[row, s]] for s in range(slots)], axis=1)


def row_matrix(blocks, row, slots):
    return jnp.concatenate([blocks[row, s] for s in range(slots)], axis=1)


def send_ends(core, full, intra_out, inter_out):
    spare = full.shape[0] - HALF_BAND
    intra_out[...] = full[pl.ds(spare * (1 - core), HALF_BAND)]
    inter_out[...] = full[pl.ds(spare * core, HALF_BAND)]


def both_rows(index, ext, ham, ovl, row):
    slots = ham.shape[1]
    orbs = ham.shape[2]
    matrix = jnp.concatenate([row_matrix(ham, row, slots), row_matrix(ovl, row, slots)], axis=0)
    image = lax.dot_general(picked(index, ext, row, slots), matrix, NT, preferred_element_type=F32)
    return image[:, :orbs], image[:, orbs:]


def one_row(index, ext, ovl, row):
    slots = ovl.shape[1]
    return lax.dot_general(
        picked(index, ext, row, slots), row_matrix(ovl, row, slots), NT, preferred_element_type=F32
    )


def scaled_kernel(index, ints, scal, own, intra, inter, ham, ovl, out, intra_out, inter_out, ext):
    core = ints[0]
    fill_ext(core, own, intra, inter, ext)
    shift, inv = scal[0], scal[1]
    for row in range(own.shape[0]):
        image_h, image_e = both_rows(index, ext, ham, ovl, row)
        mine = own[row].astype(F32)
        out[row] = ((image_h - shift * (mine + image_e)) * inv).astype(BF16)
    send_ends(core, out, intra_out, inter_out)


def term_kernel(index, ints, own, intra, inter, ovl, out, intra_out, inter_out, ext):
    core = ints[0]
    fill_ext(core, own, intra, inter, ext)
    for row in range(own.shape[0]):
        out[row] = (-one_row(index, ext, ovl, row)).astype(BF16)
    send_ends(core, out, intra_out, inter_out)


def update_kernel(first, index, ints, own, intra, inter, scaled, *rest):
    if first:
        ovl, out, intra_out, inter_out, ext = rest
    else:
        previous, ovl, out, intra_out, inter_out, ext = rest
    core = ints[0]
    fill_ext(core, own, intra, inter, ext)
    lane = lax.broadcasted_iota(jnp.int32, own.shape[1:], 1)
    for row in range(own.shape[0]):
        filtered = scaled[row].astype(F32) + own[row].astype(F32) - one_row(index, ext, ovl, row)
        if not first:
            filtered = 2.0 * filtered - previous[row].astype(F32)
        out[row] = jnp.where(lane < ints[2 + row], filtered, 0.0).astype(BF16)
    send_ends(core, out, intra_out, inter_out)


def gram_kernel(others, index, ints, own, intra, inter, *rest):
    y_others, (ham, ovl, keep, send, ext, images, both) = rest[:others], rest[others:]
    core, chip = ints[0], ints[1]
    fill_ext(core, own, intra, inter, ext)
    half, _, orbs = own.shape
    for row in range(half):
        image_h, image_e = both_rows(index, ext, ham, ovl, row)
        images[0, :, row * orbs : (row + 1) * orbs] = (own[row].astype(F32) + image_e).astype(BF16)
        images[1, :, row * orbs : (row + 1) * orbs] = image_h.astype(BF16)
    for step, vecs in enumerate((own, *y_others)):
        where = lax.rem(chip + step, others + 1)
        flat = jnp.concatenate([vecs[row] for row in range(half)], axis=1)
        for matrix in range(2):
            both[matrix, where] = lax.dot_general(
                images[matrix], flat, NT, preferred_element_type=F32
            )
    keep[...] = both[core]
    send[...] = both[1 - core]


def split3(value):
    high = value.astype(BF16)
    rest = value - high.astype(F32)
    middle = rest.astype(BF16)
    low = (rest - middle.astype(F32)).astype(BF16)
    return high, middle, low


def reciprocal(value):
    guess = pl.reciprocal(value, approx=True)
    return guess * (2.0 - value * guess)


def panel_inverse(block):
    lane = lax.broadcasted_iota(jnp.int32, (PANEL, 128), 1)
    rows = lax.broadcasted_iota(jnp.int32, (PANEL, 128), 0)
    work = jnp.where(lane < PANEL, block, jnp.where(lax.rem(lane, PANEL) == rows, 1.0, 0.0))
    pieces = [work[g * GROUP : (g + 1) * GROUP] for g in range(PANEL // GROUP)]
    sub = lax.broadcasted_iota(jnp.int32, (GROUP, 128), 0)
    groups = PANEL // GROUP
    pivots = []
    for g in range(groups):
        columns = [
            [
                jnp.broadcast_to(pieces[v][:, g * GROUP + j : g * GROUP + j + 1], (GROUP, 128))
                for v in range(g, groups)
            ]
            for j in range(GROUP)
        ]
        pivot = jnp.ones((GROUP, 128), F32)
        for j in range(GROUP):
            at = jnp.broadcast_to(columns[j][0][j : j + 1], (GROUP, 128))
            pivot = jnp.where(sub == j, at, pivot)
            inv = reciprocal(at)
            factors = [c * inv for c in columns[j]]
            factors[0] = jnp.where(sub > j, factors[0], 0.0)
            for later in range(j + 1, GROUP):
                top = jnp.broadcast_to(columns[later][0][j : j + 1], (GROUP, 128))
                columns[later] = [c - f * top for c, f in zip(columns[later], factors)]
            top = jnp.broadcast_to(pieces[g][j : j + 1], (GROUP, 128))
            for v in range(g, groups):
                pieces[v] = pieces[v] - factors[v - g] * top
        pivots.append(pivot)
    pivot = jnp.concatenate(pivots, axis=0)
    root = lax.rsqrt(pivot)
    root = root * (1.5 - 0.5 * ((pivot * root) * root))
    return jnp.concatenate(pieces, axis=0) * root


def factor(work, inverse):
    size = work.shape[0]
    wide = lax.broadcasted_iota(jnp.int32, (PANEL, size), 1)
    tall = lax.broadcasted_iota(jnp.int32, (PANEL, size), 0)
    lane = lax.broadcasted_iota(jnp.int32, (PANEL, 128), 1)
    zero = jnp.zeros((PANEL, size), BF16)
    for start in range(0, size, PANEL):
        rows = work[start : start + PANEL, :]
        tile = start // 128 * 128
        block = work[start : start + PANEL, tile : tile + 128]
        if start % 128:
            block = pltpu.roll(block, 128 - start % 128, axis=1)
        t_high, t_mid, t_low = split3(panel_inverse(block))
        first = jnp.where(lane < 2 * PANEL, t_high, jnp.where(lane < 3 * PANEL, t_mid, t_low))
        second = jnp.where(lane < 2 * PANEL, t_high, jnp.where(lane < 3 * PANEL, t_mid, t_high))
        left = jnp.concatenate([first, second], axis=1)
        spread = jnp.where(lax.rem(wide, 128) < PANEL, jnp.zeros_like(left[:, :1]), jnp.ones_like(left[:, :1]))
        left = left * spread[:, : left.shape[1]]
        inside = (wide >= start) & (wide < start + PANEL)
        rows = jnp.where(inside, jnp.where(wide - start == tall, 1.0, 0.0), rows)
        r_high, r_mid, r_low = split3(rows)
        right = jnp.concatenate([zero, r_high, r_high, r_high, zero, r_mid, r_mid, r_low], axis=0)
        new = jnp.dot(left, right, preferred_element_type=F32)
        inverse[start : start + PANEL, :] = jnp.where(wide < start + PANEL, new, 0.0)
        after = start + PANEL
        if after < size:
            high, middle, low = split3(new)
            base = after // 128 * 128
            lhs = jnp.concatenate([high, high, middle, middle, high, low], axis=0)[:, base:]
            rhs = jnp.concatenate([high, middle, high, middle, low, high], axis=0)
            change = lax.dot_general(lhs, rhs, TN, preferred_element_type=F32)[after - base :]
            columns = lax.broadcasted_iota(jnp.int32, change.shape, 1)
            old = work[after:, :]
            work[after:, :] = jnp.where((columns >= start) & (columns < after), 0.0, old) - change


def finish_kernel(chips, scale, ints, *refs):
    mine, theirs = refs[:chips], refs[chips : 2 * chips]
    (y_mine, y_theirs, basis, reduced, pair, work, inverse) = (
        refs[2 * chips : 3 * chips],
        refs[3 * chips : 4 * chips],
        *refs[4 * chips :],
    )
    core, chip, col = ints[0], ints[1], ints[2]
    vecs = y_mine[0].shape[1]
    half, orbs = y_mine[0].shape[0], y_mine[0].shape[2]
    local_vecs = basis.shape[0]
    for step in range(chips):
        where = pl.multiple_of(lax.rem(chip + step, chips) * vecs, vecs)
        for k in range(chips):
            pair[core, pl.ds(where, vecs), k * vecs : (k + 1) * vecs] = mine[step][k]
            pair[1 - core, pl.ds(where, vecs), k * vecs : (k + 1) * vecs] = theirs[step][k]
    work[...] = (pair[0] + pair[0].T) * scale
    factor(work, inverse)
    start = pl.multiple_of(col * local_vecs, local_vecs)
    own_rows = inverse[pl.ds(start, local_vecs), :]
    gram_h = (pair[1] + pair[1].T) * scale
    half_way = lax.dot_general(
        gram_h, own_rows, NT, precision=lax.Precision.HIGHEST, preferred_element_type=F32
    )
    reduced[...] = jnp.dot(
        inverse[...], half_way, precision=lax.Precision.HIGHEST, preferred_element_type=F32
    )
    rotation = own_rows.astype(BF16)
    turned = []
    for step in range(chips):
        which = lax.rem(chip + step, chips)
        part = rotation[:, :vecs]
        for k in range(1, chips):
            part = jnp.where(which == k, rotation[:, k * vecs : (k + 1) * vecs], part)
        turned.append(part)
    turned = jnp.concatenate(turned, axis=1)
    for which, group in ((core, y_mine), (1 - core, y_theirs)):
        for row in range(half):
            everything = jnp.concatenate([group[step][row] for step in range(chips)], axis=0)
            result = jnp.dot(turned, everything, preferred_element_type=F32).astype(BF16)
            at = pl.multiple_of((which * half + row) * orbs, orbs)
            basis[:, pl.ds(at, orbs)] = result


def local(
    trial_vectors,
    hamiltonian_blocks,
    correlation_offset,
    block_columns,
    block_phases,
    block_sizes,
    shift,
    halfwidth,
):
    blocks_dev, slots = block_columns.shape
    orbs = hamiltonian_blocks.shape[2]
    num_rows, num_cols = lax.axis_size("row"), lax.axis_size("col")
    total_blocks = blocks_dev * num_rows
    half = blocks_dev // CORES
    chips = num_cols // CORES
    local_vecs = trial_vectors.shape[0]
    vecs = local_vecs * CORES
    size = local_vecs * num_cols
    row, col = lax.axis_index("row"), lax.axis_index("col")
    core, chip = col % CORES, col // CORES

    def swap_cores(value):
        return lax.ppermute(value, "col", [(c, c ^ 1) for c in range(num_cols)])

    def swap_chips(value):
        pairs = []
        for r in range(num_rows):
            for x in range(chips):
                upper = r * num_cols + x * CORES + 1
                lower = (r + 1) % num_rows * num_cols + x * CORES
                pairs += [(upper, lower), (lower, upper)]
        return lax.ppermute(value, ("row", "col"), pairs)

    def from_chip(value, step):
        pairs = [((c + step * CORES) % num_cols, c) for c in range(num_cols)]
        return lax.ppermute(value, "col", pairs)

    live = jnp.arange(orbs, dtype=jnp.int32)[None, :] < block_sizes[:, None]
    blocks = jnp.swapaxes(trial_vectors.reshape(local_vecs, blocks_dev, orbs), 0, 1)
    blocks = jnp.where(live[:, None, :], blocks, jnp.zeros((), BF16))
    got = swap_cores(lax.dynamic_slice_in_dim(blocks, (1 - core) * half, half, 0))
    own = lax.dynamic_slice_in_dim(blocks, core * half, half, 0)
    current = jnp.where(
        core == 0, jnp.concatenate([own, got], axis=1), jnp.concatenate([got, own], axis=1)
    )
    spare = half - HALF_BAND
    ends = (
        lax.dynamic_slice_in_dim(current, spare * (1 - core), HALF_BAND, 0),
        lax.dynamic_slice_in_dim(current, spare * core, HALF_BAND, 0),
    )

    def own_half(value):
        return lax.dynamic_slice_in_dim(value, core * half, half, 0)

    sign = (1 - 2 * own_half(block_phases)).astype(BF16)[:, :, None, None]
    ham = pltpu.with_memory_space_constraint(own_half(hamiltonian_blocks) * sign, pltpu.VMEM)
    ovl = pltpu.with_memory_space_constraint(own_half(correlation_offset) * sign, pltpu.VMEM)
    local_rows = jnp.arange(half, dtype=jnp.int32)[:, None]
    global_rows = row * blocks_dev + core * half + local_rows
    index = local_rows + (own_half(block_columns) - global_rows + HALF_BAND) % total_blocks
    ints = jnp.concatenate(
        [jnp.stack([core, chip]).astype(jnp.int32), own_half(block_sizes).astype(jnp.int32)]
    )
    scal = jnp.concatenate([shift, 1.0 / halfwidth])

    state = jax.ShapeDtypeStruct((half, vecs, orbs), BF16)
    end = jax.ShapeDtypeStruct((HALF_BAND, vecs, orbs), BF16)
    ext = pltpu.VMEM((half + 2 * HALF_BAND, vecs, orbs), BF16)
    params = pltpu.CompilerParams(vmem_limit_bytes=16 << 20)

    def step_call(kernel, name, scalars, arrays):
        return pl.pallas_call(
            kernel,
            name=name,
            out_shape=(state, end, end),
            in_specs=[SMEM] * len(scalars) + [VMEM] * len(arrays),
            out_specs=(VMEM, VMEM, VMEM),
            scratch_shapes=[ext],
            compiler_params=params,
        )(*scalars, *arrays)

    def exchange(ends):
        inter = swap_chips(ends[1])
        return swap_cores(ends[0]), inter

    previous = current
    for degree in range(DEGREE):
        halo = exchange(ends)
        scaled, *ends = step_call(
            scaled_kernel, "scaled", (index, ints, scal), (current, *halo, ham, ovl)
        )
        halo = exchange(ends)
        term, *ends = step_call(term_kernel, "term", (index, ints), (scaled, *halo, ovl))
        halo = exchange(ends)
        first = degree == 0
        arrays = (term, *halo, scaled) + (() if first else (previous,)) + (ovl,)
        updated, *ends = step_call(
            functools.partial(update_kernel, first), "update", (index, ints), arrays
        )
        previous, current = current, updated

    halo = exchange(ends)
    y_mine = [current] + [from_chip(current, step) for step in range(1, chips)]
    part = jax.ShapeDtypeStruct((chips, vecs, vecs), F32)
    keep, send = pl.pallas_call(
        functools.partial(gram_kernel, chips - 1),
        name="gram",
        out_shape=(part, part),
        in_specs=[SMEM] * 2 + [VMEM] * (4 + chips),
        out_specs=(VMEM, VMEM),
        scratch_shapes=[
            ext,
            pltpu.VMEM((2, vecs, half * orbs), BF16),
            pltpu.VMEM((2, chips, vecs, vecs), F32),
        ],
        compiler_params=params,
    )(index, ints, current, *halo, *y_mine[1:], ham, ovl)
    summed = keep + swap_cores(send)
    if num_rows & (num_rows - 1):
        summed = lax.psum(summed, "row")
    else:
        bit = 1
        while bit < num_rows:
            summed = summed + lax.ppermute(
                summed, "row", [(r, r ^ bit) for r in range(num_rows)]
            )
            bit *= 2
    mine = [summed] + [from_chip(summed, step) for step in range(1, chips)]
    theirs = [swap_cores(value) for value in mine]
    y_theirs = [swap_cores(value) for value in y_mine]
    basis, reduced = pl.pallas_call(
        functools.partial(finish_kernel, chips, 0.5 / (total_blocks * orbs)),
        name="finish",
        out_shape=(
            jax.ShapeDtypeStruct((local_vecs, blocks_dev * orbs), BF16),
            jax.ShapeDtypeStruct((size, local_vecs), F32),
        ),
        in_specs=[SMEM] + [VMEM] * (4 * chips),
        out_specs=(VMEM, VMEM),
        scratch_shapes=[
            pltpu.VMEM((2, size, size), F32),
            pltpu.VMEM((size, size), F32),
            pltpu.VMEM((size, size), F32),
        ],
        compiler_params=params,
    )(jnp.stack([core, chip, col]).astype(jnp.int32), *mine, *theirs, *y_mine, *y_theirs)
    return basis, reduced


def solution(mesh):
    return jax.shard_map(
        local,
        mesh=mesh,
        in_specs=(
            P("col", ("pool", "row")),
            P(("pool", "row"), None, None, None),
            P(("pool", "row"), None, None, None),
            P(("pool", "row"), None),
            P(("pool", "row"), None),
            P(("pool", "row")),
            P("pool"),
            P("pool"),
        ),
        out_specs=(P("col", ("pool", "row")), P("pool", "col")),
        check_vma=False,
    )
```

profile of v0, /device:TPU:0, one launch (start us, length us, event | category | flops | bytes accessed | tf_op | source)
XLA Modules:
  0.0 164.7 jit_solution(14227180176383391376)
XLA Ops:
  4.3 4.2 %dynamic-slice_multiply_fusion = (bf16[8,9,128,128]{3,2,1,0:T(8,128)(2,1)S(1)}, bf16[8,9,128,128]{3,2,1,0:T(8,128)(2,1)}) fusion(bf16[16,9,128,128]{3,2,1,0:T(8,128)(2,1)} %param.10, s32[]{:T(128)S(6)} %select_n.49, bf16[8,9]{1,0:T(8,128)(2,1)S(1)} %subtract_convert_fusion, bf16[16,9,128,128]{3,2,1,0:T(8,128)(2,1)} %param.9), kind=kLoop, calls=%fused_computation | loop fusion | flops 2359296 | bytes 9437332 | tf_op jit(solution)/shard_map/mul | solution.py:306
  8.7 4.8 %collective-permute-start.2 = (bf16[5,128,128]{2,1,0:T(8,128)(2,1)S(1)}, bf16[5,128,128]{2,1,0:T(8,128)(2,1)S(1)}, u32[]{:S(2)}, u32[]{:S(2)}) collective-permute-start(bf16[5,128,128]{2,1,0:T(8,128)(2,1)S(1)} %get-tuple-element.82), channel_id=1, source_target_pairs={{1,4},{4,1},{3,6},{6,3},{5,8},{8,5},{7,10},{10,7},{9,12},{12,9},{1... | collective-permute-start | bytes 491528 | tf_op jit(solution)/shard_map/ppermute | solution.py:281
  13.7 3.8 %collective-permute-done.2.inter = bf16[5,128,128]{2,1,0:T(8,128)(2,1)S(1)} collective-permute-done((bf16[5,128,128]{2,1,0:T(8,128)(2,1)S(1)}, bf16[5,128,128]{2,1,0:T(8,128)(2,1)S(1)}, u32[]{:S(2)}, u32[]{:S(2)}) %collective-permute-start.2) | collective-permute-done | bytes 163872 | tf_op jit(solution)/shard_map/ppermute | solution.py:281
  17.5 1.7 %copy-done.1 = bf16[8,9,128,128]{3,2,1,0:T(8,128)(2,1)S(1)} copy-done((bf16[8,9,128,128]{3,2,1,0:T(8,128)(2,1)S(1)}, bf16[8,9,128,128]{3,2,1,0:T(8,128)(2,1)}, u32[]{:S(2)}) %copy-start.1) | copy-done | bytes 2359320
  19.2 2.3 %scaled.4 = (bf16[8,128,128]{2,1,0:T(8,128)(2,1)S(1)}, bf16[5,128,128]{2,1,0:T(8,128)(2,1)S(1)}, bf16[5,128,128]{2,1,0:T(8,128)(2,1)S(1)}) custom-call(s32[8,9]{1,0:T(8,128)S(1)} %fusion.1.index, s32[10]{0:T(128)S(1)} %pad_add_fusion.1.ints, f32[2]{0:T(128)S(1)} %pad_maximum_fusion.scal, bf16[8,128,128]{2,1,0:T(8,128)(2,1)S(1)} %maximum_select_fusion.own.rest_0_, ...), custom_call_target="tpu_custom_call" | custom-call | tf_op jit(solution)/shard_map/scaled/pallas_call | solution.py:321
  21.6 2.6 %collective-permute-start.4 = (bf16[5,128,128]{2,1,0:T(8,128)(2,1)S(1)}, bf16[5,128,128]{2,1,0:T(8,128)(2,1)S(1)}, u32[]{:S(2)}, u32[]{:S(2)}) collective-permute-start(bf16[5,128,128]{2,1,0:T(8,128)(2,1)S(1)} %get-tuple-element.42), channel_id=1, source_target_pairs={{1,4},{4,1},{3,6},{6,3},{5,8},{8,5},{7,10},{10,7},{9,12},{12,9},{1... | collective-permute-start | bytes 491528 | tf_op jit(solution)/shard_map/ppermute | solution.py:281
  24.1 5.4 %collective-permute-done.4.inter = bf16[5,128,128]{2,1,0:T(8,128)(2,1)S(1)} collective-permute-done((bf16[5,128,128]{2,1,0:T(8,128)(2,1)S(1)}, bf16[5,128,128]{2,1,0:T(8,128)(2,1)S(1)}, u32[]{:S(2)}, u32[]{:S(2)}) %collective-permute-start.4) | collective-permute-done | bytes 163872 | tf_op jit(solution)/shard_map/ppermute | solution.py:281
  29.5 1.5 term.4
  31.1 1.2 collective-permute-start.6
  32.5 5.3 %collective-permute-done.6.inter = bf16[5,128,128]{2,1,0:T(8,128)(2,1)S(1)} collective-permute-done((bf16[5,128,128]{2,1,0:T(8,128)(2,1)S(1)}, bf16[5,128,128]{2,1,0:T(8,128)(2,1)S(1)}, u32[]{:S(2)}, u32[]{:S(2)}) %collective-permute-start.6) | collective-permute-done | bytes 163872 | tf_op jit(solution)/shard_map/ppermute | solution.py:281
  37.8 1.5 update.4
  39.6 1.2 collective-permute-start.8
  40.8 5.5 %collective-permute-done.8.inter = bf16[5,128,128]{2,1,0:T(8,128)(2,1)S(1)} collective-permute-done((bf16[5,128,128]{2,1,0:T(8,128)(2,1)S(1)}, bf16[5,128,128]{2,1,0:T(8,128)(2,1)S(1)}, u32[]{:S(2)}, u32[]{:S(2)}) %collective-permute-start.8) | collective-permute-done | bytes 163872 | tf_op jit(solution)/shard_map/ppermute | solution.py:281
  46.3 2.3 %scaled.5 = (bf16[8,128,128]{2,1,0:T(8,128)(2,1)S(1)}, bf16[5,128,128]{2,1,0:T(8,128)(2,1)S(1)}, bf16[5,128,128]{2,1,0:T(8,128)(2,1)S(1)}) custom-call(s32[8,9]{1,0:T(8,128)S(1)} %fusion.1.index, s32[10]{0:T(128)S(1)} %pad_add_fusion.1.ints, f32[2]{0:T(128)S(1)} %pad_maximum_fusion.scal, bf16[8,128,128]{2,1,0:T(8,128)(2,1)S(1)} %get-tuple-element.46.own.rest_0_, ...), custom_call_target="tpu_custom_call" | custom-call | tf_op jit(solution)/shard_map/scaled/pallas_call | solution.py:321
  48.7 1.2 collective-permute-start.10
  50.1 5.3 %collective-permute-done.10.inter = bf16[5,128,128]{2,1,0:T(8,128)(2,1)S(1)} collective-permute-done((bf16[5,128,128]{2,1,0:T(8,128)(2,1)S(1)}, bf16[5,128,128]{2,1,0:T(8,128)(2,1)S(1)}, u32[]{:S(2)}, u32[]{:S(2)}) %collective-permute-start.10) | collective-permute-done | bytes 163872 | tf_op jit(solution)/shard_map/ppermute | solution.py:281
  55.4 1.5 term.5
  57.3 1.2 collective-permute-start.12
  58.5 5.5 %collective-permute-done.12.inter = bf16[5,128,128]{2,1,0:T(8,128)(2,1)S(1)} collective-permute-done((bf16[5,128,128]{2,1,0:T(8,128)(2,1)S(1)}, bf16[5,128,128]{2,1,0:T(8,128)(2,1)S(1)}, u32[]{:S(2)}, u32[]{:S(2)}) %collective-permute-start.12) | collective-permute-done | bytes 163872 | tf_op jit(solution)/shard_map/ppermute | solution.py:281
  63.9 1.5 update.5
  65.6 1.2 collective-permute-start.14
  66.9 5.3 %collective-permute-done.14.inter = bf16[5,128,128]{2,1,0:T(8,128)(2,1)S(1)} collective-permute-done((bf16[5,128,128]{2,1,0:T(8,128)(2,1)S(1)}, bf16[5,128,128]{2,1,0:T(8,128)(2,1)S(1)}, u32[]{:S(2)}, u32[]{:S(2)}) %collective-permute-start.14) | collective-permute-done | bytes 163872 | tf_op jit(solution)/shard_map/ppermute | solution.py:281
  72.2 2.3 %scaled.6 = (bf16[8,128,128]{2,1,0:T(8,128)(2,1)S(1)}, bf16[5,128,128]{2,1,0:T(8,128)(2,1)S(1)}, bf16[5,128,128]{2,1,0:T(8,128)(2,1)S(1)}) custom-call(s32[8,9]{1,0:T(8,128)S(1)} %fusion.1.index, s32[10]{0:T(128)S(1)} %pad_add_fusion.1.ints, f32[2]{0:T(128)S(1)} %pad_maximum_fusion.scal, bf16[8,128,128]{2,1,0:T(8,128)(2,1)S(1)} %get-tuple-element.55.own.rest_0_, ...), custom_call_target="tpu_custom_call" | custom-call | tf_op jit(solution)/shard_map/scaled/pallas_call | solution.py:321
  74.9 1.2 collective-permute-start.16
  76.1 5.5 %collective-permute-done.16.inter = bf16[5,128,128]{2,1,0:T(8,128)(2,1)S(1)} collective-permute-done((bf16[5,128,128]{2,1,0:T(8,128)(2,1)S(1)}, bf16[5,128,128]{2,1,0:T(8,128)(2,1)S(1)}, u32[]{:S(2)}, u32[]{:S(2)}) %collective-permute-start.16) | collective-permute-done | bytes 163872 | tf_op jit(solution)/shard_map/ppermute | solution.py:281
  81.6 1.5 term.6
  83.2 1.2 collective-permute-start.18
  84.5 5.3 %collective-permute-done.18.inter = bf16[5,128,128]{2,1,0:T(8,128)(2,1)S(1)} collective-permute-done((bf16[5,128,128]{2,1,0:T(8,128)(2,1)S(1)}, bf16[5,128,128]{2,1,0:T(8,128)(2,1)S(1)}, u32[]{:S(2)}, u32[]{:S(2)}) %collective-permute-start.18) | collective-permute-done | bytes 163872 | tf_op jit(solution)/shard_map/ppermute | solution.py:281
  89.9 1.5 update.6
  91.7 1.2 collective-permute-start.20
  92.9 5.5 %collective-permute-done.20.inter = bf16[5,128,128]{2,1,0:T(8,128)(2,1)S(1)} collective-permute-done((bf16[5,128,128]{2,1,0:T(8,128)(2,1)S(1)}, bf16[5,128,128]{2,1,0:T(8,128)(2,1)S(1)}, u32[]{:S(2)}, u32[]{:S(2)}) %collective-permute-start.20) | collective-permute-done | bytes 163872 | tf_op jit(solution)/shard_map/ppermute | solution.py:281
  98.4 2.3 %scaled.7 = (bf16[8,128,128]{2,1,0:T(8,128)(2,1)S(1)}, bf16[5,128,128]{2,1,0:T(8,128)(2,1)S(1)}, bf16[5,128,128]{2,1,0:T(8,128)(2,1)S(1)}) custom-call(s32[8,9]{1,0:T(8,128)S(1)} %fusion.1.index, s32[10]{0:T(128)S(1)} %pad_add_fusion.1.ints, f32[2]{0:T(128)S(1)} %pad_maximum_fusion.scal, bf16[8,128,128]{2,1,0:T(8,128)(2,1)S(1)} %get-tuple-element.64.own, ...), custom_call_target="tpu_custom_call" | custom-call | tf_op jit(solution)/shard_map/scaled/pallas_call | solution.py:321
  100.8 1.2 collective-permute-start.22
  102.1 5.3 %collective-permute-done.22.inter = bf16[5,128,128]{2,1,0:T(8,128)(2,1)S(1)} collective-permute-done((bf16[5,128,128]{2,1,0:T(8,128)(2,1)S(1)}, bf16[5,128,128]{2,1,0:T(8,128)(2,1)S(1)}, u32[]{:S(2)}, u32[]{:S(2)}) %collective-permute-start.22) | collective-permute-done | bytes 163872 | tf_op jit(solution)/shard_map/ppermute | solution.py:281
  107.5 1.5 term.7
  109.3 1.2 collective-permute-start.24
  110.5 5.5 %collective-permute-done.24.inter = bf16[5,128,128]{2,1,0:T(8,128)(2,1)S(1)} collective-permute-done((bf16[5,128,128]{2,1,0:T(8,128)(2,1)S(1)}, bf16[5,128,128]{2,1,0:T(8,128)(2,1)S(1)}, u32[]{:S(2)}, u32[]{:S(2)}) %collective-permute-start.24) | collective-permute-done | bytes 163872 | tf_op jit(solution)/shard_map/ppermute | solution.py:281
  116.0 1.7 %update.7 = (bf16[8,128,128]{2,1,0:T(8,128)(2,1)S(1)}, bf16[5,128,128]{2,1,0:T(8,128)(2,1)S(1)}, bf16[5,128,128]{2,1,0:T(8,128)(2,1)S(1)}) custom-call(s32[8,9]{1,0:T(8,128)S(1)} %fusion.1.index, s32[10]{0:T(128)S(1)} %pad_add_fusion.1.ints, bf16[8,128,128]{2,1,0:T(8,128)(2,1)S(1)} %get-tuple-element.70.own, ...), custom_call_target="tpu_custom_call" | custom-call | tf_op jit(solution)/shard_map/update/pallas_call | solution.py:321
  117.7 1.6 collective-permute-start.27
  120.6 5.3 %collective-permute-done.26.inter = bf16[5,128,128]{2,1,0:T(8,128)(2,1)S(1)} collective-permute-done((bf16[5,128,128]{2,1,0:T(8,128)(2,1)S(1)}, bf16[5,128,128]{2,1,0:T(8,128)(2,1)S(1)}, u32[]{:S(2)}, u32[]{:S(2)}) %collective-permute-start.26) | collective-permute-done | bytes 163872 | tf_op jit(solution)/shard_map/ppermute | solution.py:281
  126.0 2.6 %gram.1 = (f32[2,128,128]{2,1,0:T(8,128)S(1)}, f32[2,128,128]{2,1,0:T(8,128)S(1)}) custom-call(s32[8,9]{1,0:T(8,128)S(1)} %fusion.1.index, s32[10]{0:T(128)S(1)} %pad_add_fusion.1.ints, bf16[8,128,128]{2,1,0:T(8,128)(2,1)S(1)} %get-tuple-element.73.own.refs_4_, bf16[5,128,128]{2,1,0:T(8,128)(2,1)S(1)} %collective-permute-done.25.intra, ...), custom_call_target="tpu_custom_call" | custom-call | tf_op jit(solution)/shard_map/gram/pallas_call | solution.py:354
  128.9 1.1 collective-permute-done.28
  130.1 5.6 %collective-permute-done.29 = f32[2,128,128]{2,1,0:T(8,128)S(1)} collective-permute-done((f32[2,128,128]{2,1,0:T(8,128)S(1)}, f32[2,128,128]{2,1,0:T(8,128)S(1)}, u32[]{:S(2)}, u32[]{:S(2)}) %collective-permute-start.29) | collective-permute-done | bytes 131104 | tf_op jit(solution)/shard_map/ppermute | solution.py:373
  136.7 7.6 %collective-permute-done.30 = f32[2,128,128]{2,1,0:T(8,128)S(1)} collective-permute-done((f32[2,128,128]{2,1,0:T(8,128)S(1)}, f32[2,128,128]{2,1,0:T(8,128)S(1)}, u32[]{:S(2)}, u32[]{:S(2)}) %collective-permute-start.30) | collective-permute-done | bytes 131104 | tf_op jit(solution)/shard_map/ppermute | solution.py:373
  144.3 1.4 collective-permute-start.31
  145.8 4.0 %collective-permute-done.31.refs_1_ = f32[2,128,128]{2,1,0:T(8,128)S(1)} collective-permute-done((f32[2,128,128]{2,1,0:T(8,128)S(1)}, f32[2,128,128]{2,1,0:T(8,128)S(1)}, u32[]{:S(2)}, u32[]{:S(2)}) %collective-permute-start.31) | collective-permute-done | bytes 131104 | tf_op jit(solution)/shard_map/ppermute | solution.py:285
  149.8 1.3 collective-permute-done.33.refs_3_
  151.1 12.9 %finish.1 = (bf16[64,2048]{1,0:T(8,128)(2,1)}, f32[256,64]{1,0:T(8,128)S(1)}) custom-call(s32[3]{0:T(128)S(1)} %pad_add_fusion.ints, f32[2,128,128]{2,1,0:T(8,128)S(1)} %add.80.refs_0_, f32[2,128,128]{2,1,0:T(8,128)S(1)} %collective-permute-done.31.refs_1_, f32[2,128,128]{2,1,0:T(8,128)S(1)} %collective-permute-done.32.refs_2_, ...), custom_call_target="tpu_custom_call" | custom-call | tf_op jit(solution)/shard_map/finish/pallas_call | solution.py:380
  (65 shorter events, 9.4 us)
Async XLA Ops:
  0.6 1.0 copy-start
  1.7 6.8 %collective-permute-start = (bf16[8,64,128]{2,1,0:T(8,128)(2,1)S(1)}, bf16[8,64,128]{2,1,0:T(8,128)(2,1)S(1)}, u32[]{:S(2)}, u32[]{:S(2)}) collective-permute-start(bf16[8,64,128]{2,1,0:T(8,128)(2,1)S(1)} %get-tuple-element.85), channel_id=1, source_target_pairs={{0,1},{1,0},{2,3},{3,2},{4,5},{5,4},{6,7},{7,6},{8,9},{9,8},{10,11... | collective-permute-start | bytes 393224 | tf_op jit(solution)/shard_map/ppermute | solution.py:272
  4.3 4.2 %copy-start.3 = (s32[16,9]{1,0:T(8,128)S(1)}, s32[16,9]{1,0:T(8,128)}, u32[]{:S(2)}) copy-start(s32[16,9]{1,0:T(8,128)} %param.11) | copy-start | bytes 1732
  4.3 9.2 %copy-start.4 = (s32[16]{0:T(128)S(1)}, s32[16]{0:T(128)}, u32[]{:S(2)}) copy-start(s32[16]{0:T(128)} %param.13) | copy-start | bytes 196
  8.7 8.8 %collective-permute-start.2 = (bf16[5,128,128]{2,1,0:T(8,128)(2,1)S(1)}, bf16[5,128,128]{2,1,0:T(8,128)(2,1)S(1)}, u32[]{:S(2)}, u32[]{:S(2)}) collective-permute-start(bf16[5,128,128]{2,1,0:T(8,128)(2,1)S(1)} %get-tuple-element.82), channel_id=1, source_target_pairs={{1,4},{4,1},{3,6},{6,3},{5,8},{8,5},{7,10},{10,7},{9,12},{12,9},{1... | collective-permute-start | bytes 491528 | tf_op jit(solution)/shard_map/ppermute | solution.py:281
  13.5 4.1 %collective-permute-start.1 = (bf16[5,128,128]{2,1,0:T(8,128)(2,1)S(1)}, bf16[5,128,128]{2,1,0:T(8,128)(2,1)S(1)}, u32[]{:S(2)}, u32[]{:S(2)}) collective-permute-start(bf16[5,128,128]{2,1,0:T(8,128)(2,1)S(1)} %get-tuple-element.83), channel_id=1, source_target_pairs={{0,1},{1,0},{2,3},{3,2},{4,5},{5,4},{6,7},{7,6},{8,9},{9,8},{10,11... | collective-permute-start | bytes 491528 | tf_op jit(solution)/shard_map/ppermute | solution.py:272
  17.5 1.7 %copy-start.1 = (bf16[8,9,128,128]{3,2,1,0:T(8,128)(2,1)S(1)}, bf16[8,9,128,128]{3,2,1,0:T(8,128)(2,1)}, u32[]{:S(2)}) copy-start(bf16[8,9,128,128]{3,2,1,0:T(8,128)(2,1)} %get-tuple-element.87.ham.rest_1_) | copy-start | bytes 7077892
  21.5 2.6 %collective-permute-start.3 = (bf16[5,128,128]{2,1,0:T(8,128)(2,1)S(1)}, bf16[5,128,128]{2,1,0:T(8,128)(2,1)S(1)}, u32[]{:S(2)}, u32[]{:S(2)}) collective-permute-start(bf16[5,128,128]{2,1,0:T(8,128)(2,1)S(1)} %get-tuple-element.41), channel_id=1, source_target_pairs={{0,1},{1,0},{2,3},{3,2},{4,5},{5,4},{6,7},{7,6},{8,9},{9,8},{10,11... | collective-permute-start | bytes 491528 | tf_op jit(solution)/shard_map/ppermute | solution.py:272
  21.6 7.9 %collective-permute-start.4 = (bf16[5,128,128]{2,1,0:T(8,128)(2,1)S(1)}, bf16[5,128,128]{2,1,0:T(8,128)(2,1)S(1)}, u32[]{:S(2)}, u32[]{:S(2)}) collective-permute-start(bf16[5,128,128]{2,1,0:T(8,128)(2,1)S(1)} %get-tuple-element.42), channel_id=1, source_target_pairs={{1,4},{4,1},{3,6},{6,3},{5,8},{8,5},{7,10},{10,7},{9,12},{12,9},{1... | collective-permute-start | bytes 491528 | tf_op jit(solution)/shard_map/ppermute | solution.py:281
  29.5 16.8 %copy-start.2 = (bf16[8,9,128,128]{3,2,1,0:T(8,128)(2,1)S(1)}, bf16[8,9,128,128]{3,2,1,0:T(8,128)(2,1)}, u32[]{:S(2)}) copy-start(bf16[8,9,128,128]{3,2,1,0:T(8,128)(2,1)} %get-tuple-element.87.ham.rest_1_) | copy-start | bytes 7077892
  31.0 1.5 collective-permute-start.5
  31.1 6.7 %collective-permute-start.6 = (bf16[5,128,128]{2,1,0:T(8,128)(2,1)S(1)}, bf16[5,128,128]{2,1,0:T(8,128)(2,1)S(1)}, u32[]{:S(2)}, u32[]{:S(2)}) collective-permute-start(bf16[5,128,128]{2,1,0:T(8,128)(2,1)S(1)} %get-tuple-element.45), channel_id=1, source_target_pairs={{1,4},{4,1},{3,6},{6,3},{5,8},{8,5},{7,10},{10,7},{9,12},{12,9},{1... | collective-permute-start | bytes 491528 | tf_op jit(solution)/shard_map/ppermute | solution.py:281
  39.3 1.5 collective-permute-start.7
  39.6 6.7 %collective-permute-start.8 = (bf16[5,128,128]{2,1,0:T(8,128)(2,1)S(1)}, bf16[5,128,128]{2,1,0:T(8,128)(2,1)S(1)}, u32[]{:S(2)}, u32[]{:S(2)}) collective-permute-start(bf16[5,128,128]{2,1,0:T(8,128)(2,1)S(1)} %get-tuple-element.48), channel_id=1, source_target_pairs={{1,4},{4,1},{3,6},{6,3},{5,8},{8,5},{7,10},{10,7},{9,12},{12,9},{1... | collective-permute-start | bytes 491528 | tf_op jit(solution)/shard_map/ppermute | solution.py:281
  48.6 1.5 collective-permute-start.9
  48.7 6.7 %collective-permute-start.10 = (bf16[5,128,128]{2,1,0:T(8,128)(2,1)S(1)}, bf16[5,128,128]{2,1,0:T(8,128)(2,1)S(1)}, u32[]{:S(2)}, u32[]{:S(2)}) collective-permute-start(bf16[5,128,128]{2,1,0:T(8,128)(2,1)S(1)} %get-tuple-element.51), channel_id=1, source_target_pairs={{1,4},{4,1},{3,6},{6,3},{5,8},{8,5},{7,10},{10,7},{9,12},{12,9},{1... | collective-permute-start | bytes 491528 | tf_op jit(solution)/shard_map/ppermute | solution.py:281
  56.9 1.5 collective-permute-start.11
  57.3 6.7 %collective-permute-start.12 = (bf16[5,128,128]{2,1,0:T(8,128)(2,1)S(1)}, bf16[5,128,128]{2,1,0:T(8,128)(2,1)S(1)}, u32[]{:S(2)}, u32[]{:S(2)}) collective-permute-start(bf16[5,128,128]{2,1,0:T(8,128)(2,1)S(1)} %get-tuple-element.54), channel_id=1, source_target_pairs={{1,4},{4,1},{3,6},{6,3},{5,8},{8,5},{7,10},{10,7},{9,12},{12,9},{1... | collective-permute-start | bytes 491528 | tf_op jit(solution)/shard_map/ppermute | solution.py:281
  65.5 1.5 collective-permute-start.13
  65.6 6.7 %collective-permute-start.14 = (bf16[5,128,128]{2,1,0:T(8,128)(2,1)S(1)}, bf16[5,128,128]{2,1,0:T(8,128)(2,1)S(1)}, u32[]{:S(2)}, u32[]{:S(2)}) collective-permute-start(bf16[5,128,128]{2,1,0:T(8,128)(2,1)S(1)} %get-tuple-element.57), channel_id=1, source_target_pairs={{1,4},{4,1},{3,6},{6,3},{5,8},{8,5},{7,10},{10,7},{9,12},{12,9},{1... | collective-permute-start | bytes 491528 | tf_op jit(solution)/shard_map/ppermute | solution.py:281
  74.6 1.5 collective-permute-start.15
  74.9 6.7 %collective-permute-start.16 = (bf16[5,128,128]{2,1,0:T(8,128)(2,1)S(1)}, bf16[5,128,128]{2,1,0:T(8,128)(2,1)S(1)}, u32[]{:S(2)}, u32[]{:S(2)}) collective-permute-start(bf16[5,128,128]{2,1,0:T(8,128)(2,1)S(1)} %get-tuple-element.60), channel_id=1, source_target_pairs={{1,4},{4,1},{3,6},{6,3},{5,8},{8,5},{7,10},{10,7},{9,12},{12,9},{1... | collective-permute-start | bytes 491528 | tf_op jit(solution)/shard_map/ppermute | solution.py:281
  83.1 1.5 collective-permute-start.17
  83.2 6.7 %collective-permute-start.18 = (bf16[5,128,128]{2,1,0:T(8,128)(2,1)S(1)}, bf16[5,128,128]{2,1,0:T(8,128)(2,1)S(1)}, u32[]{:S(2)}, u32[]{:S(2)}) collective-permute-start(bf16[5,128,128]{2,1,0:T(8,128)(2,1)S(1)} %get-tuple-element.63), channel_id=1, source_target_pairs={{1,4},{4,1},{3,6},{6,3},{5,8},{8,5},{7,10},{10,7},{9,12},{12,9},{1... | collective-permute-start | bytes 491528 | tf_op jit(solution)/shard_map/ppermute | solution.py:281
  91.4 1.5 collective-permute-start.19
  91.7 6.7 %collective-permute-start.20 = (bf16[5,128,128]{2,1,0:T(8,128)(2,1)S(1)}, bf16[5,128,128]{2,1,0:T(8,128)(2,1)S(1)}, u32[]{:S(2)}, u32[]{:S(2)}) collective-permute-start(bf16[5,128,128]{2,1,0:T(8,128)(2,1)S(1)} %get-tuple-element.66), channel_id=1, source_target_pairs={{1,4},{4,1},{3,6},{6,3},{5,8},{8,5},{7,10},{10,7},{9,12},{12,9},{1... | collective-permute-start | bytes 491528 | tf_op jit(solution)/shard_map/ppermute | solution.py:281
  100.7 1.5 collective-permute-start.21
  100.8 6.7 %collective-permute-start.22 = (bf16[5,128,128]{2,1,0:T(8,128)(2,1)S(1)}, bf16[5,128,128]{2,1,0:T(8,128)(2,1)S(1)}, u32[]{:S(2)}, u32[]{:S(2)}) collective-permute-start(bf16[5,128,128]{2,1,0:T(8,128)(2,1)S(1)} %get-tuple-element.69), channel_id=1, source_target_pairs={{1,4},{4,1},{3,6},{6,3},{5,8},{8,5},{7,10},{10,7},{9,12},{12,9},{1... | collective-permute-start | bytes 491528 | tf_op jit(solution)/shard_map/ppermute | solution.py:281
  109.0 1.5 collective-permute-start.23
  109.3 6.7 %collective-permute-start.24 = (bf16[5,128,128]{2,1,0:T(8,128)(2,1)S(1)}, bf16[5,128,128]{2,1,0:T(8,128)(2,1)S(1)}, u32[]{:S(2)}, u32[]{:S(2)}) collective-permute-start(bf16[5,128,128]{2,1,0:T(8,128)(2,1)S(1)} %get-tuple-element.72), channel_id=1, source_target_pairs={{1,4},{4,1},{3,6},{6,3},{5,8},{8,5},{7,10},{10,7},{9,12},{12,9},{1... | collective-permute-start | bytes 491528 | tf_op jit(solution)/shard_map/ppermute | solution.py:281
  117.7 8.4 %collective-permute-start.27 = (bf16[8,128,128]{2,1,0:T(8,128)(2,1)S(1)}, bf16[8,128,128]{2,1,0:T(8,128)(2,1)S(1)}, u32[]{:S(2)}, u32[]{:S(2)}) collective-permute-start(bf16[8,128,128]{2,1,0:T(8,128)(2,1)S(1)} %get-tuple-element.73.own.refs_4_), channel_id=1, source_target_pairs={{2,0},{3,1},{0,2},{1,3},{6,4},{7,5},{4,6},{5,7},{10,8},{11,9},{8,1... | collective-permute-start | bytes 786440 | tf_op jit(solution)/shard_map/ppermute | solution.py:285
  119.2 1.4 collective-permute-start.25
  119.2 6.6 %collective-permute-start.26 = (bf16[5,128,128]{2,1,0:T(8,128)(2,1)S(1)}, bf16[5,128,128]{2,1,0:T(8,128)(2,1)S(1)}, u32[]{:S(2)}, u32[]{:S(2)}) collective-permute-start(bf16[5,128,128]{2,1,0:T(8,128)(2,1)S(1)} %get-tuple-element.75), channel_id=1, source_target_pairs={{1,4},{4,1},{3,6},{6,3},{5,8},{8,5},{7,10},{10,7},{9,12},{12,9},{1... | collective-permute-start | bytes 491528 | tf_op jit(solution)/shard_map/ppermute | solution.py:281
  128.6 1.4 collective-permute-start.28
  130.0 5.7 %collective-permute-start.29 = (f32[2,128,128]{2,1,0:T(8,128)S(1)}, f32[2,128,128]{2,1,0:T(8,128)S(1)}, u32[]{:S(2)}, u32[]{:S(2)}) collective-permute-start(f32[2,128,128]{2,1,0:T(8,128)S(1)} %add.78), channel_id=1, source_target_pairs={{0,4},{4,0},{8,12},{12,8},{1,5},{5,1},{9,13},{13,9},{2,6},{6,2},{1... | collective-permute-start | bytes 393224 | tf_op jit(solution)/shard_map/ppermute | solution.py:373
  135.7 8.6 %collective-permute-start.30 = (f32[2,128,128]{2,1,0:T(8,128)S(1)}, f32[2,128,128]{2,1,0:T(8,128)S(1)}, u32[]{:S(2)}, u32[]{:S(2)}) collective-permute-start(f32[2,128,128]{2,1,0:T(8,128)S(1)} %add.79), channel_id=1, source_target_pairs={{0,8},{4,12},{8,0},{12,4},{1,9},{5,13},{9,1},{13,5},{2,10},{6,14},... | collective-permute-start | bytes 393224 | tf_op jit(solution)/shard_map/ppermute | solution.py:373
  136.1 13.7 %collective-permute-start.34 = (bf16[8,128,128]{2,1,0:T(8,128)(2,1)S(1)}, bf16[8,128,128]{2,1,0:T(8,128)(2,1)S(1)}, u32[]{:S(2)}, u32[]{:S(2)}) collective-permute-start(bf16[8,128,128]{2,1,0:T(8,128)(2,1)S(1)} %get-tuple-element.73.own.refs_4_), channel_id=1, source_target_pairs={{0,1},{1,0},{2,3},{3,2},{4,5},{5,4},{6,7},{7,6},{8,9},{9,8},{10,11... | collective-permute-start | bytes 786440 | tf_op jit(solution)/shard_map/ppermute | solution.py:272
  136.2 13.7 %collective-permute-start.35 = (bf16[8,128,128]{2,1,0:T(8,128)(2,1)S(1)}, bf16[8,128,128]{2,1,0:T(8,128)(2,1)S(1)}, u32[]{:S(2)}, u32[]{:S(2)}) collective-permute-start(bf16[8,128,128]{2,1,0:T(8,128)(2,1)S(1)} %collective-permute-done.27.rest_0_.refs_5_), channel_id=1, source_target_pairs={{0,1},{1,0},{2,3},{3,2},{4,5},{5,4},{6,7},{7,6},{8,9},{9,8},{10,11... | collective-permute-start | bytes 786440 | tf_op jit(solution)/shard_map/ppermute | solution.py:272
  144.3 5.4 %collective-permute-start.31 = (f32[2,128,128]{2,1,0:T(8,128)S(1)}, f32[2,128,128]{2,1,0:T(8,128)S(1)}, u32[]{:S(2)}, u32[]{:S(2)}) collective-permute-start(f32[2,128,128]{2,1,0:T(8,128)S(1)} %add.80.refs_0_), channel_id=1, source_target_pairs={{2,0},{3,1},{0,2},{1,3},{6,4},{7,5},{4,6},{5,7},{10,8},{11,9},{8,1... | collective-permute-start | bytes 393224 | tf_op jit(solution)/shard_map/ppermute | solution.py:285
  145.8 4.1 %collective-permute-start.32 = (f32[2,128,128]{2,1,0:T(8,128)S(1)}, f32[2,128,128]{2,1,0:T(8,128)S(1)}, u32[]{:S(2)}, u32[]{:S(2)}) collective-permute-start(f32[2,128,128]{2,1,0:T(8,128)S(1)} %add.80.refs_0_), channel_id=1, source_target_pairs={{0,1},{1,0},{2,3},{3,2},{4,5},{5,4},{6,7},{7,6},{8,9},{9,8},{10,11... | collective-permute-start | bytes 393224 | tf_op jit(solution)/shard_map/ppermute | solution.py:272
  149.8 1.3 collective-permute-start.33
where the time goes:
time: 165 us
  waiting for transfers between devices  89.5 us (54%)
  Pallas kernels  36.8 us (22%)
  starting transfers between devices  27.3 us (17%)
  other arithmetic  6.13 us (4%)
  local copies, waits for them, and re-layouts  2.7 us (2%)
  between operations  2.24 us (1%)
    ppermute x13, waiting for transfers between devices, swap_chips(): return lax.ppermute(value, ('row', 'col'), pairs)  68.5 us
    pallas_call x12, Pallas kernels, step_call(): pl.pallas_call(kernel, name=name, out_shape=(state, end, end), in_specs=[...  21.4 us
    ppermute x13, starting transfers between devices, swap_chips(): return lax.ppermute(value, ('row', 'col'), pairs)  20.2 us
    ppermute x2, waiting for transfers between devices, local(): lax.ppermute(summed, 'row', [(r, r ^ bit) for r in range(num_rows)])  13.2 us
    pallas_call x1, Pallas kernels, local(): pl.pallas_call(functools.partial(finish_kernel, chips, 0.5 / (total_block...  12.9 us
    mul x1, other arithmetic, local(): own_half(correlation_offset) * sign  4.16 us
    ppermute x2, waiting for transfers between devices, from_chip(): return lax.ppermute(value, 'col', pairs)  4.15 us
    ppermute x19, starting transfers between devices, swap_cores(): return lax.ppermute(value, 'col', [(c, c ^ 1) for c in range(num_cols)])  3.69 us
  transfers between devices with their start and end apart: 36, of which 25 were waited for; matrix products, arithmetic and copies ran while one was open for 3% of the time, Pallas kernels for 0%

commit v1 on v0

v1 whole, which is shorter than its diff:
```python
import functools

import jax
import jax.numpy as jnp
from jax import lax
from jax.experimental import pallas as pl
from jax.experimental.pallas import tpu as pltpu
from jax.sharding import PartitionSpec as P

HALF_BAND = 5
DEGREE = 4
CORES = 2
PANEL = 32
GROUP = 8
DIAGONAL_ROWS = 16

BF16 = jnp.bfloat16
F32 = jnp.float32
NT = (((1,), (1,)), ((), ()))
TN = (((0,), (0,)), ((), ()))

SMEM = pl.BlockSpec(memory_space=pltpu.SMEM)
VMEM = pl.BlockSpec(memory_space=pltpu.VMEM)
HBM = pl.BlockSpec(memory_space=pltpu.HBM)


def vmem(shape, dtype):
    return pltpu.VMEM(shape, dtype)


def fill_ext(core, own, intra, inter, ext):
    half = own.shape[0]
    ext[HALF_BAND : HALF_BAND + half] = own[...]
    ext[pl.ds((half + HALF_BAND) * (1 - core), HALF_BAND)] = intra[...]
    ext[pl.ds((half + HALF_BAND) * core, HALF_BAND)] = inter[...]


def picked(table, ext, row):
    index, signs = table
    slots = index.shape[1]
    return jnp.concatenate(
        [ext[index[row, s]] * signs[row, s].astype(BF16) for s in range(slots)], axis=1
    )


def row_matrix(blocks, row):
    return jnp.concatenate([blocks[row, s] for s in range(blocks.shape[1])], axis=1)


def send_ends(core, full, intra_out, inter_out):
    spare = full.shape[0] - HALF_BAND
    intra_out[...] = full[pl.ds(spare * (1 - core), HALF_BAND)]
    inter_out[...] = full[pl.ds(spare * core, HALF_BAND)]


def image_of(table, ext, matrices, row):
    matrix = jnp.concatenate([row_matrix(blocks, row) for blocks in matrices], axis=0)
    return lax.dot_general(matrix, picked(table, ext, row), NT, preferred_element_type=F32)


def both_rows(table, ext, ham, ovl, row):
    orbs = ham.shape[2]
    image = image_of(table, ext, (ham, ovl), row)
    return image[:orbs].T, image[orbs:].T


def one_row(table, ext, ovl, row):
    return image_of(table, ext, (ovl,), row).T


def cut_kernel(ints, sizes, trial, keep, give):
    half, _, orbs = keep.shape
    core = ints[0]
    lane = lax.broadcasted_iota(jnp.int32, keep.shape[1:], 1)
    for out, which in ((give, 1 - core), (keep, core)):
        for row in range(half):
            at = which * half + row
            values = trial[:, pl.ds(pl.multiple_of(at * orbs, orbs), orbs)].astype(F32)
            out[row] = jnp.where(lane < sizes[at], values, 0.0).astype(BF16)


def load_kernel(total, ints, columns, phases, ham, ovl, ham_out, ovl_out, index, signs, sems):
    half, slots = index.shape
    first = ints[0] * half
    copies = []
    for row in range(half):
        for matrix, (source, target) in enumerate(((ham, ham_out), (ovl, ovl_out))):
            copies.append(
                pltpu.make_async_copy(
                    source.at[first + row], target.at[row], sems.at[matrix, row]
                )
            )
    for copy in copies:
        copy.start()
    start = ints[3] + first

    def fill(row, _):
        for slot in range(slots):
            away = columns[first + row, slot] - (start + row) + HALF_BAND
            away = jnp.where(away < 0, away + total, away)
            away = jnp.where(away >= total, away - total, away)
            index[row, slot] = row + away
            signs[row, slot] = (1 - 2 * phases[first + row, slot]).astype(F32)
        return 0

    lax.fori_loop(0, half, fill, 0)
    for copy in copies:
        copy.wait()


def scaled_kernel(
    ints, index, signs, shift, width, own, intra, inter, ham, ovl, out, intra_out, inter_out, ext
):
    core = ints[0]
    fill_ext(core, own, intra, inter, ext)
    inv = 1.0 / (jnp.zeros(own.shape[1:], F32) + width[0])
    for row in range(own.shape[0]):
        image_h, image_e = both_rows((index, signs), ext, ham, ovl, row)
        mine = own[row].astype(F32)
        out[row] = ((image_h - shift[0] * (mine + image_e)) * inv).astype(BF16)
    send_ends(core, out, intra_out, inter_out)


def term_kernel(ints, index, signs, own, intra, inter, ovl, out, intra_out, inter_out, ext):
    core = ints[0]
    fill_ext(core, own, intra, inter, ext)
    for row in range(own.shape[0]):
        out[row] = (-one_row((index, signs), ext, ovl, row)).astype(BF16)
    send_ends(core, out, intra_out, inter_out)


def update_kernel(first, ints, index, signs, sizes, own, intra, inter, scaled, *rest):
    if first:
        ovl, out, intra_out, inter_out, ext = rest
    else:
        previous, ovl, out, intra_out, inter_out, ext = rest
    core = ints[0]
    half = own.shape[0]
    fill_ext(core, own, intra, inter, ext)
    lane = lax.broadcasted_iota(jnp.int32, own.shape[1:], 1)
    for row in range(half):
        image = one_row((index, signs), ext, ovl, row)
        filtered = scaled[row].astype(F32) + own[row].astype(F32) - image
        if not first:
            filtered = 2.0 * filtered - previous[row].astype(F32)
        out[row] = jnp.where(lane < sizes[core * half + row], filtered, 0.0).astype(BF16)
    send_ends(core, out, intra_out, inter_out)


def images_kernel(ints, index, signs, own, intra, inter, ham, ovl, out, ext):
    core = ints[0]
    fill_ext(core, own, intra, inter, ext)
    half, _, orbs = own.shape
    for row in range(half):
        image_h, image_e = both_rows((index, signs), ext, ham, ovl, row)
        at = slice(row * orbs, (row + 1) * orbs)
        out[0, :, at] = (own[row].astype(F32) + image_e).astype(BF16)
        out[1, :, at] = image_h.astype(BF16)


def gram_kernel(chips, ints, index, signs, own, intra, inter, ham, ovl, ready, *rest):
    first, *others = rest[:chips]
    keep, send, ext, images, both = rest[chips:]
    images_kernel(ints, index, signs, own, intra, inter, ham, ovl, images, ext)
    core, chip = ints[0], ints[1]
    half, local_vecs, _ = own.shape
    vecs = CORES * local_vecs
    groups = [[first[row] for row in range(half)], [own[row] for row in range(half)]]
    for other in others:
        groups += [[other[g, row] for row in range(half)] for g in range(CORES)]
    flat = jnp.concatenate([jnp.concatenate(group, axis=1) for group in groups], axis=0)
    eye = lax.broadcasted_iota(jnp.int32, (vecs, vecs), 0) == lax.broadcasted_iota(
        jnp.int32, (vecs, vecs), 1
    )
    for matrix in range(2):
        mine = jnp.concatenate([ready[matrix], images[matrix]], axis=0)
        pair = lax.dot_general(mine, flat, NT, preferred_element_type=F32)
        for step in range(chips):
            where = pl.multiple_of(lax.rem(chip + step, chips) * vecs, vecs)
            block = pair[:, step * vecs : (step + 1) * vecs]
            both[matrix, pl.ds(where, vecs), :] = block.astype(BF16)
        diagonal = jnp.sum(jnp.where(eye, pair[:, :vecs], 0.0), axis=0, keepdims=True)
        both[matrix, chips * vecs :, :] = diagonal_parts(diagonal)
    keep[...] = both[core]
    send[...] = both[1 - core]


def diagonal_parts(diagonal):
    high, middle, low = (part.astype(F32) for part in split3(diagonal))
    rows = lax.broadcasted_iota(jnp.int32, (DIAGONAL_ROWS, diagonal.shape[1]), 0)
    parts = jnp.where(rows == 0, high, jnp.where(rows == 1, middle, jnp.where(rows == 2, low, 0.0)))
    return parts.astype(BF16)


def diagonal_of(payload):
    parts = payload[payload.shape[0] - DIAGONAL_ROWS :, :].astype(F32)
    return parts[0:1] + (parts[1:2] + parts[2:3])


def add_kernel(left, right, out):
    body = left.shape[0] - DIAGONAL_ROWS
    out[:body] = (left[:body, :].astype(F32) + right[:body, :].astype(F32)).astype(BF16)
    out[body:] = diagonal_parts(diagonal_of(left) + diagonal_of(right))


def split3(value):
    high = value.astype(BF16)
    rest = value - high.astype(F32)
    middle = rest.astype(BF16)
    low = (rest - middle.astype(F32)).astype(BF16)
    return high, middle, low


def reciprocal(value):
    guess = pl.reciprocal(value, approx=True)
    return guess * (2.0 - value * guess)


def panel_inverse(block):
    lane = lax.broadcasted_iota(jnp.int32, (PANEL, 128), 1)
    rows = lax.broadcasted_iota(jnp.int32, (PANEL, 128), 0)
    work = jnp.where(lane < PANEL, block, jnp.where(lax.rem(lane, PANEL) == rows, 1.0, 0.0))
    pieces = [work[g * GROUP : (g + 1) * GROUP] for g in range(PANEL // GROUP)]
    sub = lax.broadcasted_iota(jnp.int32, (GROUP, 128), 0)
    groups = PANEL // GROUP
    pivots = []
    for g in range(groups):
        columns = [
            [
                jnp.broadcast_to(pieces[v][:, g * GROUP + j : g * GROUP + j + 1], (GROUP, 128))
                for v in range(g, groups)
            ]
            for j in range(GROUP)
        ]
        pivot = jnp.ones((GROUP, 128), F32)
        for j in range(GROUP):
            at = jnp.broadcast_to(columns[j][0][j : j + 1], (GROUP, 128))
            pivot = jnp.where(sub == j, at, pivot)
            inv = reciprocal(at)
            factors = [c * inv for c in columns[j]]
            factors[0] = jnp.where(sub > j, factors[0], 0.0)
            for later in range(j + 1, GROUP):
                top = jnp.broadcast_to(columns[later][0][j : j + 1], (GROUP, 128))
                columns[later] = [c - f * top for c, f in zip(columns[later], factors)]
            top = jnp.broadcast_to(pieces[g][j : j + 1], (GROUP, 128))
            for v in range(g, groups):
                pieces[v] = pieces[v] - factors[v - g] * top
        pivots.append(pivot)
    pivot = jnp.concatenate(pivots, axis=0)
    root = lax.rsqrt(pivot)
    root = root * (1.5 - 0.5 * ((pivot * root) * root))
    return jnp.concatenate(pieces, axis=0) * root


def factor(work, inverse):
    size = work.shape[0]
    wide = lax.broadcasted_iota(jnp.int32, (PANEL, size), 1)
    tall = lax.broadcasted_iota(jnp.int32, (PANEL, size), 0)
    lane = lax.broadcasted_iota(jnp.int32, (PANEL, 128), 1)
    zero = jnp.zeros((PANEL, size), BF16)
    for start in range(0, size, PANEL):
        rows = work[start : start + PANEL, :]
        tile = start // 128 * 128
        block = work[start : start + PANEL, tile : tile + 128]
        if start % 128:
            block = pltpu.roll(block, 128 - start % 128, axis=1)
        t_high, t_mid, t_low = split3(panel_inverse(block))
        first = jnp.where(lane < 2 * PANEL, t_high, jnp.where(lane < 3 * PANEL, t_mid, t_low))
        second = jnp.where(lane < 2 * PANEL, t_high, jnp.where(lane < 3 * PANEL, t_mid, t_high))
        left = jnp.concatenate([first, second], axis=1)
        spread = jnp.where(lax.rem(wide, 128) < PANEL, jnp.zeros_like(left[:, :1]), jnp.ones_like(left[:, :1]))
        left = left * spread[:, : left.shape[1]]
        inside = (wide >= start) & (wide < start + PANEL)
        rows = jnp.where(inside, jnp.where(wide - start == tall, 1.0, 0.0), rows)
        r_high, r_mid, r_low = split3(rows)
        right = jnp.concatenate([zero, r_high, r_high, r_high, zero, r_mid, r_mid, r_low], axis=0)
        new = jnp.dot(left, right, preferred_element_type=F32)
        inverse[start : start + PANEL, :] = jnp.where(wide < start + PANEL, new, 0.0)
        after = start + PANEL
        if after < size:
            high, middle, low = split3(new)
            base = after // 128 * 128
            lhs = jnp.concatenate([high, high, middle, middle, high, low], axis=0)[:, base:]
            rhs = jnp.concatenate([high, middle, high, middle, low, high], axis=0)
            change = lax.dot_general(lhs, rhs, TN, preferred_element_type=F32)[after - base :]
            columns = lax.broadcasted_iota(jnp.int32, change.shape, 1)
            old = work[after:, :]
            work[after:, :] = jnp.where((columns >= start) & (columns < after), 0.0, old) - change


def finish_kernel(chips, scale, ints, *refs):
    mine, theirs = refs[:chips], refs[chips : 2 * chips]
    y_mine, y_theirs = refs[2 * chips : 3 * chips + 1], refs[3 * chips + 1 : 4 * chips + 1]
    basis, reduced, pair, work, inverse = refs[4 * chips + 1 :]
    core, chip, col = ints[0], ints[1], ints[2]
    half, local_vecs, orbs = y_mine[0].shape
    vecs = CORES * local_vecs
    eye = lax.broadcasted_iota(jnp.int32, (vecs, vecs), 0) == lax.broadcasted_iota(
        jnp.int32, (vecs, vecs), 1
    )
    for step in range(chips):
        which = lax.rem(chip + step, chips)
        rows = pl.ds(pl.multiple_of(which * vecs, vecs), vecs)
        for matrix, payload in ((core, mine[step]), (1 - core, theirs[step])):
            diagonal = diagonal_of(payload)
            for k in range(chips):
                block = payload[k * vecs : (k + 1) * vecs, :].astype(F32)
                block = jnp.where(eye & (which == k), diagonal, block)
                pair[matrix, rows, k * vecs : (k + 1) * vecs] = block
    work[...] = (pair[0] + pair[0].T) * scale
    factor(work, inverse)
    start = pl.multiple_of(col * local_vecs, local_vecs)
    own_rows = inverse[pl.ds(start, local_vecs), :]
    gram_h = (pair[1] + pair[1].T) * scale
    half_way = lax.dot_general(
        gram_h, own_rows, NT, precision=lax.Precision.HIGHEST, preferred_element_type=F32
    )
    reduced[...] = jnp.dot(
        inverse[...], half_way, precision=lax.Precision.HIGHEST, preferred_element_type=F32
    )
    rotation = own_rows.astype(BF16)
    turned = []
    for step in range(chips):
        which = lax.rem(chip + step, chips)
        part = rotation[:, :vecs]
        for k in range(1, chips):
            part = jnp.where(which == k, rotation[:, k * vecs : (k + 1) * vecs], part)
        turned.append(part)
    turned = jnp.concatenate(turned, axis=1)
    mine_groups = [y_mine[0], y_mine[1]]
    for other in y_mine[2:]:
        mine_groups += [other.at[g] for g in range(CORES)]
    their_groups = [other.at[g] for other in y_theirs for g in range(CORES)]
    for which, group in ((core, mine_groups), (1 - core, their_groups)):
        for row in range(half):
            everything = jnp.concatenate([vectors[row] for vectors in group], axis=0)
            result = jnp.dot(turned, everything, preferred_element_type=F32).astype(BF16)
            at = pl.multiple_of((which * half + row) * orbs, orbs)
            basis[:, pl.ds(at, orbs)] = result


def local(
    trial_vectors,
    hamiltonian_blocks,
    correlation_offset,
    block_columns,
    block_phases,
    block_sizes,
    shift,
    halfwidth,
):
    blocks_dev, slots = block_columns.shape
    orbs = hamiltonian_blocks.shape[2]
    num_rows, num_cols = lax.axis_size("row"), lax.axis_size("col")
    total_blocks = blocks_dev * num_rows
    half = blocks_dev // CORES
    chips = num_cols // CORES
    local_vecs = trial_vectors.shape[0]
    vecs = local_vecs * CORES
    size = local_vecs * num_cols
    row, col = lax.axis_index("row"), lax.axis_index("col")
    core, chip = lax.rem(col, CORES), lax.div(col, CORES)

    def swap_cores(value):
        return lax.ppermute(value, "col", [(c, c ^ 1) for c in range(num_cols)])

    def swap_chips(value):
        pairs = []
        for r in range(num_rows):
            for x in range(chips):
                upper = r * num_cols + x * CORES + 1
                lower = (r + 1) % num_rows * num_cols + x * CORES
                pairs += [(upper, lower), (lower, upper)]
        return lax.ppermute(value, ("row", "col"), pairs)

    def from_chip(value, step):
        pairs = [((c + step * CORES) % num_cols, c) for c in range(num_cols)]
        return lax.ppermute(value, "col", pairs)

    state = jax.ShapeDtypeStruct((half, local_vecs, orbs), BF16)
    end = jax.ShapeDtypeStruct((HALF_BAND, local_vecs, orbs), BF16)
    ext = pltpu.VMEM((half + 2 * HALF_BAND, local_vecs, orbs), BF16)
    params = pltpu.CompilerParams(vmem_limit_bytes=16 << 20)
    row_flops = 2 * half * slots * local_vecs * orbs * orbs

    def call(kernel, name, scalars, arrays, outs, scratch, flops):
        return pl.pallas_call(
            kernel,
            name=name,
            out_shape=outs,
            in_specs=[SMEM] * len(scalars) + [VMEM] * len(arrays),
            out_specs=(VMEM,) * len(outs),
            scratch_shapes=scratch,
            compiler_params=params,
            cost_estimate=pl.CostEstimate(
                flops=flops, bytes_accessed=flops // 128, transcendentals=0
            ),
        )(*scalars, *arrays)

    def step_call(kernel, name, scalars, arrays, flops):
        return call(kernel, name, scalars, arrays, (state, end, end), [ext], flops)

    def exchange(ends):
        inter = swap_chips(ends[1])
        return swap_cores(ends[0]), inter

    def scalars(value):
        return pltpu.with_memory_space_constraint(value, pltpu.SMEM)

    ints = scalars(jnp.stack([core, chip, col, row * blocks_dev]).astype(jnp.int32))
    block_sizes, shift, halfwidth = (scalars(x) for x in (block_sizes, shift, halfwidth))
    block_columns, block_phases = scalars(block_columns), scalars(block_phases)
    own, give = call(
        cut_kernel, "cut", (ints, block_sizes), (trial_vectors,), (state, state), [], row_flops
    )
    got = swap_cores(give)
    matrix = vmem((half, *hamiltonian_blocks.shape[1:]), BF16)
    ham, ovl, index, signs = pl.pallas_call(
        functools.partial(load_kernel, total_blocks),
        name="load",
        out_shape=(
            matrix,
            matrix,
            pltpu.SMEM((half, slots), jnp.int32),
            pltpu.SMEM((half, slots), F32),
        ),
        in_specs=[SMEM, SMEM, SMEM, HBM, HBM],
        out_specs=(VMEM, VMEM, SMEM, SMEM),
        scratch_shapes=[pltpu.SemaphoreType.DMA((2, half))],
        compiler_params=params,
        cost_estimate=pl.CostEstimate(
            flops=0, bytes_accessed=4 * hamiltonian_blocks.size, transcendentals=0
        ),
    )(
        ints,
        block_columns,
        block_phases,
        pltpu.with_memory_space_constraint(hamiltonian_blocks, pltpu.HBM),
        pltpu.with_memory_space_constraint(correlation_offset, pltpu.HBM),
    )
    got, ham, ovl = lax.optimization_barrier((got, ham, ovl))
    current = [jnp.where(core == 0, own, got), jnp.where(core == 0, got, own)]
    spare = half - HALF_BAND
    ends = [
        (
            lax.dynamic_slice_in_dim(value, spare * (1 - core), HALF_BAND, 0),
            lax.dynamic_slice_in_dim(value, spare * core, HALF_BAND, 0),
        )
        for value in current
    ]
    table = (ints, index, signs)
    scaled, term, previous = [None] * CORES, [None] * CORES, list(current)
    halo = [exchange(ends[g]) for g in range(CORES)]
    for degree in range(DEGREE):
        for g in range(CORES):
            scaled[g], *ends = step_call(
                scaled_kernel,
                "scaled",
                (*table, shift, halfwidth),
                (current[g], *halo[g], ham, ovl),
                2 * row_flops,
            )
            halo[g] = exchange(ends)
        for g in range(CORES):
            term[g], *ends = step_call(
                term_kernel, "term", table, (scaled[g], *halo[g], ovl), row_flops
            )
            halo[g] = exchange(ends)
        for g in range(CORES):
            first = degree == 0
            arrays = (term[g], *halo[g], scaled[g]) + (() if first else (previous[g],)) + (ovl,)
            updated, *ends = step_call(
                functools.partial(update_kernel, first),
                "update",
                (*table, block_sizes),
                arrays,
                row_flops,
            )
            halo[g] = exchange(ends)
            previous[g], current[g] = current[g], updated

    stacked = jnp.stack(current)
    y_others = [from_chip(stacked, step) for step in range(1, chips)]
    image = jax.ShapeDtypeStruct((2, local_vecs, half * orbs), BF16)
    (ready,) = call(
        images_kernel,
        "images",
        table,
        (current[0], *halo[0], ham, ovl),
        (image,),
        [ext],
        2 * row_flops,
    )
    payload = jax.ShapeDtypeStruct((size + DIAGONAL_ROWS, vecs), BF16)
    keep, send = call(
        functools.partial(gram_kernel, chips),
        "gram",
        table,
        (current[1], *halo[1], ham, ovl, ready, current[0], *y_others),
        (payload, payload),
        [ext, pltpu.VMEM(image.shape, BF16), pltpu.VMEM((2, *payload.shape), BF16)],
        3 * row_flops,
    )

    def add(left, right):
        return call(add_kernel, "add", (), (left, right), (payload,), [], row_flops // 8)[0]

    summed = add(keep, swap_cores(send))
    if num_rows & (num_rows - 1):
        every = lax.all_gather(summed, "row")
        summed = every[0]
        for r in range(1, num_rows):
            summed = add(summed, every[r])
    else:
        bit = 1
        while bit < num_rows:
            other = lax.ppermute(summed, "row", [(r, r ^ bit) for r in range(num_rows)])
            summed = add(summed, other)
            bit *= 2
    mine = [summed] + [from_chip(summed, step) for step in range(1, chips)]
    theirs = [swap_cores(value) for value in mine]
    y_theirs = [swap_cores(value) for value in (stacked, *y_others)]
    return call(
        functools.partial(finish_kernel, chips, 0.5 / (total_blocks * orbs)),
        "finish",
        (ints,),
        (*mine, *theirs, *current, *y_others, *y_theirs),
        (
            jax.ShapeDtypeStruct((local_vecs, blocks_dev * orbs), BF16),
            jax.ShapeDtypeStruct((size, local_vecs), F32),
        ),
        [
            pltpu.VMEM((2, size, size), F32),
            pltpu.VMEM((size, size), F32),
            pltpu.VMEM((size, size), F32),
        ],
        10 * row_flops,
    )


def solution(mesh):
    return jax.shard_map(
        local,
        mesh=mesh,
        in_specs=(
            P("col", ("pool", "row")),
            P(("pool", "row"), None, None, None),
            P(("pool", "row"), None, None, None),
            P(("pool", "row"), None),
            P(("pool", "row"), None),
            P(("pool", "row")),
            P("pool"),
            P("pool"),
        ),
        out_specs=(P("col", ("pool", "row")), P("pool", "col")),
        check_vma=False,
    )
```

time: 165 us -> 148 us (0.90)
  waiting for transfers between devices: 89.5 us -> 25.8 us
  starting transfers between devices: 27.3 us -> 55.7 us
  Pallas kernels: 36.8 us -> 60.4 us
  other arithmetic: 6.13 us -> 0.13 us
    ppermute x13 -> x26, waiting for transfers between devices: 68.5 us -> 10.7 us  [swap_chips(): return lax.ppermute(value, ('row', 'col'), pairs)]
    ppermute x13 -> x26, starting transfers between devices: 20.2 us -> 49.6 us  [swap_chips(): return lax.ppermute(value, ('row', 'col'), pairs)]
    pallas_call x14 -> x32, Pallas kernels: 36.8 us -> 60.4 us  [the longest x31 57.1 us: call(): pl.pallas_call(kernel, name=name, out_shape=outs, in_specs=[SMEM] * len(s...]
    ppermute x2, waiting for transfers between devices: 13.2 us -> 8.73 us  [local(): other = lax.ppermute(summed, 'row', [(r, r ^ bit) for r in range(num_rows)])]
    mul x1 -> x0, other arithmetic: 4.16 us -> none  [local(): own_half(correlation_offset) * sign]
    ppermute x19 -> x32, waiting for transfers between devices: 3.59 us -> 2.56 us  [swap_cores(): return lax.ppermute(value, 'col', [(c, c ^ 1) for c in range(num_cols)])]
    ppermute x19 -> x32, starting transfers between devices: 3.69 us -> 3.18 us  [swap_cores(): return lax.ppermute(value, 'col', [(c, c ^ 1) for c in range(num_cols)])]
  transfers between devices with their start and end apart: 36 -> 62, of which waited for: 25 -> 18; matrix products, arithmetic and copies ran while one was open for 3% -> 0% of each run, Pallas kernels for 0% -> 29%
where the time goes in v1:
time: 148 us
  Pallas kernels  60.4 us (41%)
  starting transfers between devices  55.7 us (38%)
  waiting for transfers between devices  25.8 us (17%)
  local copies, waits for them, and re-layouts  3.75 us (3%)
  between operations  2.49 us (2%)
    pallas_call x31, Pallas kernels, call(): pl.pallas_call(kernel, name=name, out_shape=outs, in_specs=[SMEM] * len(s...  57.1 us
    ppermute x26, starting transfers between devices, swap_chips(): return lax.ppermute(value, ('row', 'col'), pairs)  49.6 us
    ppermute x26, waiting for transfers between devices, swap_chips(): return lax.ppermute(value, ('row', 'col'), pairs)  10.7 us
    ppermute x2, waiting for transfers between devices, local(): other = lax.ppermute(summed, 'row', [(r, r ^ bit) for r in range(num_rows)])  8.73 us
    ppermute x2, waiting for transfers between devices, from_chip(): return lax.ppermute(value, 'col', pairs)  3.78 us
    pallas_call x1, Pallas kernels, local(): pl.pallas_call(functools.partial(load_kernel, total_blocks), name='load',...  3.24 us
    ppermute x32, starting transfers between devices, swap_cores(): return lax.ppermute(value, 'col', [(c, c ^ 1) for c in range(num_cols)])  3.18 us
    unnamed x10, local copies, waits for them, and re-layouts  3.01 us
  transfers between devices with their start and end apart: 62, of which 18 were waited for; matrix products, arithmetic and copies ran while one was open for 0% of the time, Pallas kernels for 29%

profile of v1, /device:TPU:0, one launch (start us, length us, event | category | flops | bytes accessed | tf_op | source)
XLA Modules:
  0.0 148.2 jit_solution(1716916155771261875)
XLA Ops:
  4.9 3.2 %load.1 = (bf16[8,9,128,128]{3,2,1,0:T(8,128)(2,1)S(1)}, bf16[8,9,128,128]{3,2,1,0:T(8,128)(2,1)S(1)}, s32[8,9]{1,0:T(8,128)S(4)}, f32[8,9]{1,0:T(8,128)S(4)}) custom-call(s32[4]{0:T(128)S(1)} %pad_add_fusion.ints, s32[16,9]{1,0:T(8,128)S(1)} %copy-done.2, s32[16,9]{1,0:T(8,128)S(1)} %copy-done.3, bf16[16,9,128,128]{3,2,1,0:T(8,128)(2,1)} %ham.1, ...), custom_call_target="tpu_custom_call" | custom-call | bytes 9437184 | tf_op jit(solution)/shard_map/load/pallas_call | solution.py:418
  8.3 4.7 %collective-permute-start.2 = (bf16[5,64,128]{2,1,0:T(8,128)(2,1)S(1)}, bf16[5,64,128]{2,1,0:T(8,128)(2,1)S(1)}, u32[]{:S(2)}, u32[]{:S(2)}) collective-permute-start(bf16[5,64,128]{2,1,0:T(8,128)(2,1)S(1)} %get-tuple-element.174), channel_id=1, source_target_pairs={{1,4},{4,1},{3,6},{6,3},{5,8},{8,5},{7,10},{10,7},{9,12},{12,9},{1... | collective-permute-start | bytes 245768 | tf_op jit(solution)/shard_map/ppermute | solution.py:374
  15.8 2.0 %scaled.8 = (bf16[8,64,128]{2,1,0:T(8,128)(2,1)S(1)}, bf16[5,64,128]{2,1,0:T(8,128)(2,1)S(1)}, bf16[5,64,128]{2,1,0:T(8,128)(2,1)S(1)}) custom-call(s32[4]{0:T(128)S(1)} %pad_add_fusion.ints, s32[8,9]{1,0:T(8,128)S(4)} %get-tuple-element.85.index, f32[8,9]{1,0:T(8,128)S(4)} %get-tuple-element.86.signs, f32[1]{0:T(128)S(6)} %copy.11.shift, f32[1]{0:T(128)S(6)} %copy.12.width, ...), custom_call_target="tpu_custom_call" | custom-call | flops 301989888 | bytes 2359296 | tf_op jit(solution)/shard_map/scaled/pallas_call | solution.py:387
  17.9 3.8 %collective-permute-start.4 = (bf16[5,64,128]{2,1,0:T(8,128)(2,1)S(1)}, bf16[5,64,128]{2,1,0:T(8,128)(2,1)S(1)}, u32[]{:S(2)}, u32[]{:S(2)}) collective-permute-start(bf16[5,64,128]{2,1,0:T(8,128)(2,1)S(1)} %get-tuple-element.96), channel_id=1, source_target_pairs={{1,4},{4,1},{3,6},{6,3},{5,8},{8,5},{7,10},{10,7},{9,12},{12,9},{1... | collective-permute-start | bytes 245768 | tf_op jit(solution)/shard_map/ppermute | solution.py:374
  21.7 2.0 %scaled.12 = (bf16[8,64,128]{2,1,0:T(8,128)(2,1)S(1)}, bf16[5,64,128]{2,1,0:T(8,128)(2,1)S(1)}, bf16[5,64,128]{2,1,0:T(8,128)(2,1)S(1)}) custom-call(s32[4]{0:T(128)S(1)} %pad_add_fusion.ints, s32[8,9]{1,0:T(8,128)S(4)} %get-tuple-element.85.index, f32[8,9]{1,0:T(8,128)S(4)} %get-tuple-element.86.signs, f32[1]{0:T(128)S(6)} %copy.11.shift, ...), custom_call_target="tpu_custom_call" | custom-call | flops 301989888 | bytes 2359296 | tf_op jit(solution)/shard_map/scaled/pallas_call | solution.py:387
  24.2 1.4 term.8
  25.8 3.2 %collective-permute-start.6 = (bf16[5,64,128]{2,1,0:T(8,128)(2,1)S(1)}, bf16[5,64,128]{2,1,0:T(8,128)(2,1)S(1)}, u32[]{:S(2)}, u32[]{:S(2)}) collective-permute-start(bf16[5,64,128]{2,1,0:T(8,128)(2,1)S(1)} %get-tuple-element.99), channel_id=1, source_target_pairs={{1,4},{4,1},{3,6},{6,3},{5,8},{8,5},{7,10},{10,7},{9,12},{12,9},{1... | collective-permute-start | bytes 245768 | tf_op jit(solution)/shard_map/ppermute | solution.py:374
  32.1 1.4 update.8
  33.6 2.7 %collective-permute-start.8 = (bf16[5,64,128]{2,1,0:T(8,128)(2,1)S(1)}, bf16[5,64,128]{2,1,0:T(8,128)(2,1)S(1)}, u32[]{:S(2)}, u32[]{:S(2)}) collective-permute-start(bf16[5,64,128]{2,1,0:T(8,128)(2,1)S(1)} %get-tuple-element.102), channel_id=1, source_target_pairs={{1,4},{4,1},{3,6},{6,3},{5,8},{8,5},{7,10},{10,7},{9,12},{12,9},{1... | collective-permute-start | bytes 245768 | tf_op jit(solution)/shard_map/ppermute | solution.py:374
  36.8 1.4 update.12
  39.9 2.0 %scaled.9 = (bf16[8,64,128]{2,1,0:T(8,128)(2,1)S(1)}, bf16[5,64,128]{2,1,0:T(8,128)(2,1)S(1)}, bf16[5,64,128]{2,1,0:T(8,128)(2,1)S(1)}) custom-call(s32[4]{0:T(128)S(1)} %pad_add_fusion.ints, s32[8,9]{1,0:T(8,128)S(4)} %get-tuple-element.85.index, f32[8,9]{1,0:T(8,128)S(4)} %get-tuple-element.86.signs, f32[1]{0:T(128)S(6)} %copy.11.shift, f32[1]{0:T(128)S(6)} %copy.12.width, ...), custom_call_target="tpu_custom_call" | custom-call | flops 301989888 | bytes 2359296 | tf_op jit(solution)/shard_map/scaled/pallas_call | solution.py:387
  42.0 2.1 %collective-permute-start.10 = (bf16[5,64,128]{2,1,0:T(8,128)(2,1)S(1)}, bf16[5,64,128]{2,1,0:T(8,128)(2,1)S(1)}, u32[]{:S(2)}, u32[]{:S(2)}) collective-permute-start(bf16[5,64,128]{2,1,0:T(8,128)(2,1)S(1)} %get-tuple-element.105), channel_id=1, source_target_pairs={{1,4},{4,1},{3,6},{6,3},{5,8},{8,5},{7,10},{10,7},{9,12},{12,9},{1... | collective-permute-start | bytes 245768 | tf_op jit(solution)/shard_map/ppermute | solution.py:374
  44.1 2.0 %scaled.13 = (bf16[8,64,128]{2,1,0:T(8,128)(2,1)S(1)}, bf16[5,64,128]{2,1,0:T(8,128)(2,1)S(1)}, bf16[5,64,128]{2,1,0:T(8,128)(2,1)S(1)}) custom-call(s32[4]{0:T(128)S(1)} %pad_add_fusion.ints, s32[8,9]{1,0:T(8,128)S(4)} %get-tuple-element.85.index, f32[8,9]{1,0:T(8,128)S(4)} %get-tuple-element.86.signs, f32[1]{0:T(128)S(6)} %copy.11.shift, ...), custom_call_target="tpu_custom_call" | custom-call | flops 301989888 | bytes 2359296 | tf_op jit(solution)/shard_map/scaled/pallas_call | solution.py:387
  46.2 1.5 %collective-permute-start.36 = (bf16[5,64,128]{2,1,0:T(8,128)(2,1)S(1)}, bf16[5,64,128]{2,1,0:T(8,128)(2,1)S(1)}, u32[]{:S(2)}, u32[]{:S(2)}) collective-permute-start(bf16[5,64,128]{2,1,0:T(8,128)(2,1)S(1)} %get-tuple-element.141), channel_id=1, source_target_pairs={{1,4},{4,1},{3,6},{6,3},{5,8},{8,5},{7,10},{10,7},{9,12},{12,9},{1... | collective-permute-start | bytes 245768 | tf_op jit(solution)/shard_map/ppermute | solution.py:374
  49.3 2.1 %collective-permute-start.12 = (bf16[5,64,128]{2,1,0:T(8,128)(2,1)S(1)}, bf16[5,64,128]{2,1,0:T(8,128)(2,1)S(1)}, u32[]{:S(2)}, u32[]{:S(2)}) collective-permute-start(bf16[5,64,128]{2,1,0:T(8,128)(2,1)S(1)} %get-tuple-element.108), channel_id=1, source_target_pairs={{1,4},{4,1},{3,6},{6,3},{5,8},{8,5},{7,10},{10,7},{9,12},{12,9},{1... | collective-permute-start | bytes 245768 | tf_op jit(solution)/shard_map/ppermute | solution.py:374
  53.5 1.5 %collective-permute-start.38 = (bf16[5,64,128]{2,1,0:T(8,128)(2,1)S(1)}, bf16[5,64,128]{2,1,0:T(8,128)(2,1)S(1)}, u32[]{:S(2)}, u32[]{:S(2)}) collective-permute-start(bf16[5,64,128]{2,1,0:T(8,128)(2,1)S(1)} %get-tuple-element.144), channel_id=1, source_target_pairs={{1,4},{4,1},{3,6},{6,3},{5,8},{8,5},{7,10},{10,7},{9,12},{12,9},{1... | collective-permute-start | bytes 245768 | tf_op jit(solution)/shard_map/ppermute | solution.py:374
  55.0 1.4 update.9
  56.7 2.1 %collective-permute-start.14 = (bf16[5,64,128]{2,1,0:T(8,128)(2,1)S(1)}, bf16[5,64,128]{2,1,0:T(8,128)(2,1)S(1)}, u32[]{:S(2)}, u32[]{:S(2)}) collective-permute-start(bf16[5,64,128]{2,1,0:T(8,128)(2,1)S(1)} %get-tuple-element.111), channel_id=1, source_target_pairs={{1,4},{4,1},{3,6},{6,3},{5,8},{8,5},{7,10},{10,7},{9,12},{12,9},{1... | collective-permute-start | bytes 245768 | tf_op jit(solution)/shard_map/ppermute | solution.py:374
  59.2 1.4 update.13
  60.7 1.5 %collective-permute-start.40 = (bf16[5,64,128]{2,1,0:T(8,128)(2,1)S(1)}, bf16[5,64,128]{2,1,0:T(8,128)(2,1)S(1)}, u32[]{:S(2)}, u32[]{:S(2)}) collective-permute-start(bf16[5,64,128]{2,1,0:T(8,128)(2,1)S(1)} %get-tuple-element.147), channel_id=1, source_target_pairs={{1,4},{4,1},{3,6},{6,3},{5,8},{8,5},{7,10},{10,7},{9,12},{12,9},{1... | collective-permute-start | bytes 245768 | tf_op jit(solution)/shard_map/ppermute | solution.py:374
  62.4 2.0 %scaled.10 = (bf16[8,64,128]{2,1,0:T(8,128)(2,1)S(1)}, bf16[5,64,128]{2,1,0:T(8,128)(2,1)S(1)}, bf16[5,64,128]{2,1,0:T(8,128)(2,1)S(1)}) custom-call(s32[4]{0:T(128)S(1)} %pad_add_fusion.ints, s32[8,9]{1,0:T(8,128)S(4)} %get-tuple-element.85.index, f32[8,9]{1,0:T(8,128)S(4)} %get-tuple-element.86.signs, f32[1]{0:T(128)S(6)} %copy.11.shift, ...), custom_call_target="tpu_custom_call" | custom-call | flops 301989888 | bytes 2359296 | tf_op jit(solution)/shard_map/scaled/pallas_call | solution.py:387
  64.6 2.1 %collective-permute-start.16 = (bf16[5,64,128]{2,1,0:T(8,128)(2,1)S(1)}, bf16[5,64,128]{2,1,0:T(8,128)(2,1)S(1)}, u32[]{:S(2)}, u32[]{:S(2)}) collective-permute-start(bf16[5,64,128]{2,1,0:T(8,128)(2,1)S(1)} %get-tuple-element.114), channel_id=1, source_target_pairs={{1,4},{4,1},{3,6},{6,3},{5,8},{8,5},{7,10},{10,7},{9,12},{12,9},{1... | collective-permute-start | bytes 245768 | tf_op jit(solution)/shard_map/ppermute | solution.py:374
  66.7 2.0 %scaled.14 = (bf16[8,64,128]{2,1,0:T(8,128)(2,1)S(1)}, bf16[5,64,128]{2,1,0:T(8,128)(2,1)S(1)}, bf16[5,64,128]{2,1,0:T(8,128)(2,1)S(1)}) custom-call(s32[4]{0:T(128)S(1)} %pad_add_fusion.ints, s32[8,9]{1,0:T(8,128)S(4)} %get-tuple-element.85.index, f32[8,9]{1,0:T(8,128)S(4)} %get-tuple-element.86.signs, f32[1]{0:T(128)S(6)} %copy.11.shift, ...), custom_call_target="tpu_custom_call" | custom-call | flops 301989888 | bytes 2359296 | tf_op jit(solution)/shard_map/scaled/pallas_call | solution.py:387
  68.8 1.6 %collective-permute-start.42 = (bf16[5,64,128]{2,1,0:T(8,128)(2,1)S(1)}, bf16[5,64,128]{2,1,0:T(8,128)(2,1)S(1)}, u32[]{:S(2)}, u32[]{:S(2)}) collective-permute-start(bf16[5,64,128]{2,1,0:T(8,128)(2,1)S(1)} %get-tuple-element.150), channel_id=1, source_target_pairs={{1,4},{4,1},{3,6},{6,3},{5,8},{8,5},{7,10},{10,7},{9,12},{12,9},{1... | collective-permute-start | bytes 245768 | tf_op jit(solution)/shard_map/ppermute | solution.py:374
  71.9 2.1 %collective-permute-start.18 = (bf16[5,64,128]{2,1,0:T(8,128)(2,1)S(1)}, bf16[5,64,128]{2,1,0:T(8,128)(2,1)S(1)}, u32[]{:S(2)}, u32[]{:S(2)}) collective-permute-start(bf16[5,64,128]{2,1,0:T(8,128)(2,1)S(1)} %get-tuple-element.117), channel_id=1, source_target_pairs={{1,4},{4,1},{3,6},{6,3},{5,8},{8,5},{7,10},{10,7},{9,12},{12,9},{1... | collective-permute-start | bytes 245768 | tf_op jit(solution)/shard_map/ppermute | solution.py:374
  76.0 1.6 %collective-permute-start.44 = (bf16[5,64,128]{2,1,0:T(8,128)(2,1)S(1)}, bf16[5,64,128]{2,1,0:T(8,128)(2,1)S(1)}, u32[]{:S(2)}, u32[]{:S(2)}) collective-permute-start(bf16[5,64,128]{2,1,0:T(8,128)(2,1)S(1)} %get-tuple-element.153), channel_id=1, source_target_pairs={{1,4},{4,1},{3,6},{6,3},{5,8},{8,5},{7,10},{10,7},{9,12},{12,9},{1... | collective-permute-start | bytes 245768 | tf_op jit(solution)/shard_map/ppermute | solution.py:374
  77.6 1.4 update.10
  79.1 2.1 %collective-permute-start.20 = (bf16[5,64,128]{2,1,0:T(8,128)(2,1)S(1)}, bf16[5,64,128]{2,1,0:T(8,128)(2,1)S(1)}, u32[]{:S(2)}, u32[]{:S(2)}) collective-permute-start(bf16[5,64,128]{2,1,0:T(8,128)(2,1)S(1)} %get-tuple-element.120), channel_id=1, source_target_pairs={{1,4},{4,1},{3,6},{6,3},{5,8},{8,5},{7,10},{10,7},{9,12},{12,9},{1... | collective-permute-start | bytes 245768 | tf_op jit(solution)/shard_map/ppermute | solution.py:374
  81.8 1.4 update.14
  83.3 1.6 %collective-permute-start.46 = (bf16[5,64,128]{2,1,0:T(8,128)(2,1)S(1)}, bf16[5,64,128]{2,1,0:T(8,128)(2,1)S(1)}, u32[]{:S(2)}, u32[]{:S(2)}) collective-permute-start(bf16[5,64,128]{2,1,0:T(8,128)(2,1)S(1)} %get-tuple-element.156), channel_id=1, source_target_pairs={{1,4},{4,1},{3,6},{6,3},{5,8},{8,5},{7,10},{10,7},{9,12},{12,9},{1... | collective-permute-start | bytes 245768 | tf_op jit(solution)/shard_map/ppermute | solution.py:374
  84.8 2.0 %scaled.11 = (bf16[8,64,128]{2,1,0:T(8,128)(2,1)S(1)}, bf16[5,64,128]{2,1,0:T(8,128)(2,1)S(1)}, bf16[5,64,128]{2,1,0:T(8,128)(2,1)S(1)}) custom-call(s32[4]{0:T(128)S(1)} %pad_add_fusion.ints, s32[8,9]{1,0:T(8,128)S(4)} %get-tuple-element.85.index, f32[8,9]{1,0:T(8,128)S(4)} %get-tuple-element.86.signs, f32[1]{0:T(128)S(6)} %copy.11.shift, ...), custom_call_target="tpu_custom_call" | custom-call | flops 301989888 | bytes 2359296 | tf_op jit(solution)/shard_map/scaled/pallas_call | solution.py:387
  86.9 2.1 %collective-permute-start.22 = (bf16[5,64,128]{2,1,0:T(8,128)(2,1)S(1)}, bf16[5,64,128]{2,1,0:T(8,128)(2,1)S(1)}, u32[]{:S(2)}, u32[]{:S(2)}) collective-permute-start(bf16[5,64,128]{2,1,0:T(8,128)(2,1)S(1)} %get-tuple-element.123), channel_id=1, source_target_pairs={{1,4},{4,1},{3,6},{6,3},{5,8},{8,5},{7,10},{10,7},{9,12},{12,9},{1... | collective-permute-start | bytes 245768 | tf_op jit(solution)/shard_map/ppermute | solution.py:374
  89.1 2.0 %scaled.15 = (bf16[8,64,128]{2,1,0:T(8,128)(2,1)S(1)}, bf16[5,64,128]{2,1,0:T(8,128)(2,1)S(1)}, bf16[5,64,128]{2,1,0:T(8,128)(2,1)S(1)}) custom-call(s32[4]{0:T(128)S(1)} %pad_add_fusion.ints, s32[8,9]{1,0:T(8,128)S(4)} %get-tuple-element.85.index, f32[8,9]{1,0:T(8,128)S(4)} %get-tuple-element.86.signs, f32[1]{0:T(128)S(6)} %copy.11.shift, ...), custom_call_target="tpu_custom_call" | custom-call | flops 301989888 | bytes 2359296 | tf_op jit(solution)/shard_map/scaled/pallas_call | solution.py:387
  91.2 1.6 %collective-permute-start.48 = (bf16[5,64,128]{2,1,0:T(8,128)(2,1)S(1)}, bf16[5,64,128]{2,1,0:T(8,128)(2,1)S(1)}, u32[]{:S(2)}, u32[]{:S(2)}) collective-permute-start(bf16[5,64,128]{2,1,0:T(8,128)(2,1)S(1)} %get-tuple-element.159), channel_id=1, source_target_pairs={{1,4},{4,1},{3,6},{6,3},{5,8},{8,5},{7,10},{10,7},{9,12},{12,9},{1... | collective-permute-start | bytes 245768 | tf_op jit(solution)/shard_map/ppermute | solution.py:374
  94.2 2.1 %collective-permute-start.24 = (bf16[5,64,128]{2,1,0:T(8,128)(2,1)S(1)}, bf16[5,64,128]{2,1,0:T(8,128)(2,1)S(1)}, u32[]{:S(2)}, u32[]{:S(2)}) collective-permute-start(bf16[5,64,128]{2,1,0:T(8,128)(2,1)S(1)} %get-tuple-element.126), channel_id=1, source_target_pairs={{1,4},{4,1},{3,6},{6,3},{5,8},{8,5},{7,10},{10,7},{9,12},{12,9},{1... | collective-permute-start | bytes 245768 | tf_op jit(solution)/shard_map/ppermute | solution.py:374
  98.4 1.6 %collective-permute-start.50 = (bf16[5,64,128]{2,1,0:T(8,128)(2,1)S(1)}, bf16[5,64,128]{2,1,0:T(8,128)(2,1)S(1)}, u32[]{:S(2)}, u32[]{:S(2)}) collective-permute-start(bf16[5,64,128]{2,1,0:T(8,128)(2,1)S(1)} %get-tuple-element.162), channel_id=1, source_target_pairs={{1,4},{4,1},{3,6},{6,3},{5,8},{8,5},{7,10},{10,7},{9,12},{12,9},{1... | collective-permute-start | bytes 245768 | tf_op jit(solution)/shard_map/ppermute | solution.py:374
  100.0 1.7 %update.11 = (bf16[8,64,128]{2,1,0:T(8,128)(2,1)S(1)}, bf16[5,64,128]{2,1,0:T(8,128)(2,1)S(1)}, bf16[5,64,128]{2,1,0:T(8,128)(2,1)S(1)}) custom-call(s32[4]{0:T(128)S(1)} %pad_add_fusion.ints, s32[8,9]{1,0:T(8,128)S(4)} %get-tuple-element.85.index, f32[8,9]{1,0:T(8,128)S(4)} %get-tuple-element.86.signs, s32[16]{0:T(128)S(1)} %copy-done.1, ...), custom_call_target="tpu_custom_call" | custom-call | flops 150994944 | bytes 1179648 | tf_op jit(solution)/shard_map/update/pallas_call | solution.py:387
  101.7 2.5 %collective-permute-done.50.inter = bf16[5,64,128]{2,1,0:T(8,128)(2,1)S(1)} collective-permute-done((bf16[5,64,128]{2,1,0:T(8,128)(2,1)S(1)}, bf16[5,64,128]{2,1,0:T(8,128)(2,1)S(1)}, u32[]{:S(2)}, u32[]{:S(2)}) %collective-permute-start.50) | collective-permute-done | bytes 81952 | tf_op jit(solution)/shard_map/ppermute | solution.py:374
  104.1 1.4 update.15
  105.6 1.6 %collective-permute-start.53 = (bf16[2,8,64,128]{3,2,1,0:T(8,128)(2,1)S(1)}, bf16[2,8,64,128]{3,2,1,0:T(8,128)(2,1)S(1)}, u32[]{:S(2)}, u32[]{:S(2)}) collective-permute-start(bf16[2,8,64,128]{3,2,1,0:T(8,128)(2,1)S(1)} %pad_maximum_fusion), channel_id=1, source_target_pairs={{2,0},{3,1},{0,2},{1,3},{6,4},{7,5},{4,6},{5,7},{10,8},{11,9},{8,1... | collective-permute-start | bytes 786440 | tf_op jit(solution)/shard_map/ppermute | solution.py:378
  108.4 2.3 %collective-permute-start.26 = (bf16[5,64,128]{2,1,0:T(8,128)(2,1)S(1)}, bf16[5,64,128]{2,1,0:T(8,128)(2,1)S(1)}, u32[]{:S(2)}, u32[]{:S(2)}) collective-permute-start(bf16[5,64,128]{2,1,0:T(8,128)(2,1)S(1)} %get-tuple-element.129), channel_id=1, source_target_pairs={{1,4},{4,1},{3,6},{6,3},{5,8},{8,5},{7,10},{10,7},{9,12},{12,9},{1... | collective-permute-start | bytes 245768 | tf_op jit(solution)/shard_map/ppermute | solution.py:374
  110.7 2.3 %collective-permute-done.52.inter = bf16[5,64,128]{2,1,0:T(8,128)(2,1)S(1)} collective-permute-done((bf16[5,64,128]{2,1,0:T(8,128)(2,1)S(1)}, bf16[5,64,128]{2,1,0:T(8,128)(2,1)S(1)}, u32[]{:S(2)}, u32[]{:S(2)}) %collective-permute-start.52) | collective-permute-done | bytes 81952 | tf_op jit(solution)/shard_map/ppermute | solution.py:374
  113.1 2.0 %images.1.ready = bf16[2,64,1024]{2,1,0:T(8,128)(2,1)S(1)} custom-call(s32[4]{0:T(128)S(1)} %pad_add_fusion.ints, s32[8,9]{1,0:T(8,128)S(4)} %get-tuple-element.85.index, f32[8,9]{1,0:T(8,128)S(4)} %get-tuple-element.86.signs, bf16[8,64,128]{2,1,0:T(8,128)(2,1)S(1)} %get-tuple-element.163.own.rest_0_.refs_4_, ...), custom_call_target="tpu_custom_call" | custom-call | flops 301989888 | bytes 2359296 | tf_op jit(solution)/shard_map/images/pallas_call | solution.py:387
  115.1 2.3 %gram.1 = (bf16[272,128]{1,0:T(8,128)(2,1)S(1)}, bf16[272,128]{1,0:T(8,128)(2,1)S(1)}) custom-call(s32[4]{0:T(128)S(1)} %pad_add_fusion.ints, s32[8,9]{1,0:T(8,128)S(4)} %get-tuple-element.85.index, f32[8,9]{1,0:T(8,128)S(4)} %get-tuple-element.86.signs, bf16[8,64,128]{2,1,0:T(8,128)(2,1)S(1)} %get-tuple-element.127.own.refs_5_, ...), custom_call_target="tpu_custom_call" | custom-call | flops 452984832 | bytes 3538944 | tf_op jit(solution)/shard_map/gram/pallas_call | solution.py:387
  119.4 3.7 %collective-permute-done.55.right = bf16[272,128]{1,0:T(8,128)(2,1)S(1)} collective-permute-done((bf16[272,128]{1,0:T(8,128)(2,1)S(1)}, bf16[272,128]{1,0:T(8,128)(2,1)S(1)}, u32[]{:S(2)}, u32[]{:S(2)}) %collective-permute-start.55) | collective-permute-done | bytes 69664 | tf_op jit(solution)/shard_map/ppermute | solution.py:517
  123.9 5.0 %collective-permute-done.56.right = bf16[272,128]{1,0:T(8,128)(2,1)S(1)} collective-permute-done((bf16[272,128]{1,0:T(8,128)(2,1)S(1)}, bf16[272,128]{1,0:T(8,128)(2,1)S(1)}, u32[]{:S(2)}, u32[]{:S(2)}) %collective-permute-start.56) | collective-permute-done | bytes 69664 | tf_op jit(solution)/shard_map/ppermute | solution.py:517
  129.5 3.8 %collective-permute-done.57.refs_1_ = bf16[272,128]{1,0:T(8,128)(2,1)S(1)} collective-permute-done((bf16[272,128]{1,0:T(8,128)(2,1)S(1)}, bf16[272,128]{1,0:T(8,128)(2,1)S(1)}, u32[]{:S(2)}, u32[]{:S(2)}) %collective-permute-start.57) | collective-permute-done | bytes 69664 | tf_op jit(solution)/shard_map/ppermute | solution.py:378
  134.5 12.9 %finish.1 = (bf16[64,2048]{1,0:T(8,128)(2,1)}, f32[256,64]{1,0:T(8,128)S(1)}) custom-call(s32[4]{0:T(128)S(1)} %pad_add_fusion.ints, bf16[272,128]{1,0:T(8,128)(2,1)S(1)} %add.21.refs_0_, bf16[272,128]{1,0:T(8,128)(2,1)S(1)} %collective-permute-done.57.refs_1_, bf16[272,128]{1,0:T(8,128)(2,1)S(1)} %collective-permute-done.58.refs_2_, ...), custom_call_target="tpu_custom_call" | custom-call | flops 1509949440 | bytes 11796480 | tf_op jit(solution)/shard_map/finish/pallas_call | solution.py:387
  (124 shorter events, 31.0 us)
Async XLA Ops:
  8.2 6.8 %collective-permute-start.1 = (bf16[5,64,128]{2,1,0:T(8,128)(2,1)S(1)}, bf16[5,64,128]{2,1,0:T(8,128)(2,1)S(1)}, u32[]{:S(2)}, u32[]{:S(2)}) collective-permute-start(bf16[5,64,128]{2,1,0:T(8,128)(2,1)S(1)} %get-tuple-element.175), channel_id=1, source_target_pairs={{0,1},{1,0},{2,3},{3,2},{4,5},{5,4},{6,7},{7,6},{8,9},{9,8},{10,11... | collective-permute-start | bytes 245768 | tf_op jit(solution)/shard_map/ppermute | solution.py:365
  8.3 7.5 %collective-permute-start.2 = (bf16[5,64,128]{2,1,0:T(8,128)(2,1)S(1)}, bf16[5,64,128]{2,1,0:T(8,128)(2,1)S(1)}, u32[]{:S(2)}, u32[]{:S(2)}) collective-permute-start(bf16[5,64,128]{2,1,0:T(8,128)(2,1)S(1)} %get-tuple-element.174), channel_id=1, source_target_pairs={{1,4},{4,1},{3,6},{6,3},{5,8},{8,5},{7,10},{10,7},{9,12},{12,9},{1... | collective-permute-start | bytes 245768 | tf_op jit(solution)/shard_map/ppermute | solution.py:374
  13.1 8.6 %collective-permute-start.27 = (bf16[5,64,128]{2,1,0:T(8,128)(2,1)S(1)}, bf16[5,64,128]{2,1,0:T(8,128)(2,1)S(1)}, u32[]{:S(2)}, u32[]{:S(2)}) collective-permute-start(bf16[5,64,128]{2,1,0:T(8,128)(2,1)S(1)} %get-tuple-element.173), channel_id=1, source_target_pairs={{0,1},{1,0},{2,3},{3,2},{4,5},{5,4},{6,7},{7,6},{8,9},{9,8},{10,11... | collective-permute-start | bytes 245768 | tf_op jit(solution)/shard_map/ppermute | solution.py:365
  13.1 8.5 %collective-permute-start.28 = (bf16[5,64,128]{2,1,0:T(8,128)(2,1)S(1)}, bf16[5,64,128]{2,1,0:T(8,128)(2,1)S(1)}, u32[]{:S(2)}, u32[]{:S(2)}) collective-permute-start(bf16[5,64,128]{2,1,0:T(8,128)(2,1)S(1)} %get-tuple-element.172), channel_id=1, source_target_pairs={{1,4},{4,1},{3,6},{6,3},{5,8},{8,5},{7,10},{10,7},{9,12},{12,9},{1... | collective-permute-start | bytes 245768 | tf_op jit(solution)/shard_map/ppermute | solution.py:374
  17.8 6.4 %collective-permute-start.3 = (bf16[5,64,128]{2,1,0:T(8,128)(2,1)S(1)}, bf16[5,64,128]{2,1,0:T(8,128)(2,1)S(1)}, u32[]{:S(2)}, u32[]{:S(2)}) collective-permute-start(bf16[5,64,128]{2,1,0:T(8,128)(2,1)S(1)} %get-tuple-element.95), channel_id=1, source_target_pairs={{0,1},{1,0},{2,3},{3,2},{4,5},{5,4},{6,7},{7,6},{8,9},{9,8},{10,11... | collective-permute-start | bytes 245768 | tf_op jit(solution)/shard_map/ppermute | solution.py:365
  17.9 6.3 %collective-permute-start.4 = (bf16[5,64,128]{2,1,0:T(8,128)(2,1)S(1)}, bf16[5,64,128]{2,1,0:T(8,128)(2,1)S(1)}, u32[]{:S(2)}, u32[]{:S(2)}) collective-permute-start(bf16[5,64,128]{2,1,0:T(8,128)(2,1)S(1)} %get-tuple-element.96), channel_id=1, source_target_pairs={{1,4},{4,1},{3,6},{6,3},{5,8},{8,5},{7,10},{10,7},{9,12},{12,9},{1... | collective-permute-start | bytes 245768 | tf_op jit(solution)/shard_map/ppermute | solution.py:374
  23.8 5.7 %collective-permute-start.30 = (bf16[5,64,128]{2,1,0:T(8,128)(2,1)S(1)}, bf16[5,64,128]{2,1,0:T(8,128)(2,1)S(1)}, u32[]{:S(2)}, u32[]{:S(2)}) collective-permute-start(bf16[5,64,128]{2,1,0:T(8,128)(2,1)S(1)} %get-tuple-element.132), channel_id=1, source_target_pairs={{1,4},{4,1},{3,6},{6,3},{5,8},{8,5},{7,10},{10,7},{9,12},{12,9},{1... | collective-permute-start | bytes 245768 | tf_op jit(solution)/shard_map/ppermute | solution.py:374
  25.7 6.1 %collective-permute-start.5 = (bf16[5,64,128]{2,1,0:T(8,128)(2,1)S(1)}, bf16[5,64,128]{2,1,0:T(8,128)(2,1)S(1)}, u32[]{:S(2)}, u32[]{:S(2)}) collective-permute-start(bf16[5,64,128]{2,1,0:T(8,128)(2,1)S(1)} %get-tuple-element.98), channel_id=1, source_target_pairs={{0,1},{1,0},{2,3},{3,2},{4,5},{5,4},{6,7},{7,6},{8,9},{9,8},{10,11... | collective-permute-start | bytes 245768 | tf_op jit(solution)/shard_map/ppermute | solution.py:365
  25.8 6.3 %collective-permute-start.6 = (bf16[5,64,128]{2,1,0:T(8,128)(2,1)S(1)}, bf16[5,64,128]{2,1,0:T(8,128)(2,1)S(1)}, u32[]{:S(2)}, u32[]{:S(2)}) collective-permute-start(bf16[5,64,128]{2,1,0:T(8,128)(2,1)S(1)} %get-tuple-element.99), channel_id=1, source_target_pairs={{1,4},{4,1},{3,6},{6,3},{5,8},{8,5},{7,10},{10,7},{9,12},{12,9},{1... | collective-permute-start | bytes 245768 | tf_op jit(solution)/shard_map/ppermute | solution.py:374
  31.0 5.7 %collective-permute-start.32 = (bf16[5,64,128]{2,1,0:T(8,128)(2,1)S(1)}, bf16[5,64,128]{2,1,0:T(8,128)(2,1)S(1)}, u32[]{:S(2)}, u32[]{:S(2)}) collective-permute-start(bf16[5,64,128]{2,1,0:T(8,128)(2,1)S(1)} %get-tuple-element.135), channel_id=1, source_target_pairs={{1,4},{4,1},{3,6},{6,3},{5,8},{8,5},{7,10},{10,7},{9,12},{12,9},{1... | collective-permute-start | bytes 245768 | tf_op jit(solution)/shard_map/ppermute | solution.py:374
  33.5 5.5 %collective-permute-start.7 = (bf16[5,64,128]{2,1,0:T(8,128)(2,1)S(1)}, bf16[5,64,128]{2,1,0:T(8,128)(2,1)S(1)}, u32[]{:S(2)}, u32[]{:S(2)}) collective-permute-start(bf16[5,64,128]{2,1,0:T(8,128)(2,1)S(1)} %get-tuple-element.101), channel_id=1, source_target_pairs={{0,1},{1,0},{2,3},{3,2},{4,5},{5,4},{6,7},{7,6},{8,9},{9,8},{10,11... | collective-permute-start | bytes 245768 | tf_op jit(solution)/shard_map/ppermute | solution.py:365
  33.6 6.3 %collective-permute-start.8 = (bf16[5,64,128]{2,1,0:T(8,128)(2,1)S(1)}, bf16[5,64,128]{2,1,0:T(8,128)(2,1)S(1)}, u32[]{:S(2)}, u32[]{:S(2)}) collective-permute-start(bf16[5,64,128]{2,1,0:T(8,128)(2,1)S(1)} %get-tuple-element.102), channel_id=1, source_target_pairs={{1,4},{4,1},{3,6},{6,3},{5,8},{8,5},{7,10},{10,7},{9,12},{12,9},{1... | collective-permute-start | bytes 245768 | tf_op jit(solution)/shard_map/ppermute | solution.py:374
  38.2 5.9 %collective-permute-start.33 = (bf16[5,64,128]{2,1,0:T(8,128)(2,1)S(1)}, bf16[5,64,128]{2,1,0:T(8,128)(2,1)S(1)}, u32[]{:S(2)}, u32[]{:S(2)}) collective-permute-start(bf16[5,64,128]{2,1,0:T(8,128)(2,1)S(1)} %get-tuple-element.137), channel_id=1, source_target_pairs={{0,1},{1,0},{2,3},{3,2},{4,5},{5,4},{6,7},{7,6},{8,9},{9,8},{10,11... | collective-permute-start | bytes 245768 | tf_op jit(solution)/shard_map/ppermute | solution.py:365
  38.3 5.8 %collective-permute-start.34 = (bf16[5,64,128]{2,1,0:T(8,128)(2,1)S(1)}, bf16[5,64,128]{2,1,0:T(8,128)(2,1)S(1)}, u32[]{:S(2)}, u32[]{:S(2)}) collective-permute-start(bf16[5,64,128]{2,1,0:T(8,128)(2,1)S(1)} %get-tuple-element.138), channel_id=1, source_target_pairs={{1,4},{4,1},{3,6},{6,3},{5,8},{8,5},{7,10},{10,7},{9,12},{12,9},{1... | collective-permute-start | bytes 245768 | tf_op jit(solution)/shard_map/ppermute | solution.py:374
  41.9 5.9 %collective-permute-start.9 = (bf16[5,64,128]{2,1,0:T(8,128)(2,1)S(1)}, bf16[5,64,128]{2,1,0:T(8,128)(2,1)S(1)}, u32[]{:S(2)}, u32[]{:S(2)}) collective-permute-start(bf16[5,64,128]{2,1,0:T(8,128)(2,1)S(1)} %get-tuple-element.104), channel_id=1, source_target_pairs={{0,1},{1,0},{2,3},{3,2},{4,5},{5,4},{6,7},{7,6},{8,9},{9,8},{10,11... | collective-permute-start | bytes 245768 | tf_op jit(solution)/shard_map/ppermute | solution.py:365
  42.0 5.8 %collective-permute-start.10 = (bf16[5,64,128]{2,1,0:T(8,128)(2,1)S(1)}, bf16[5,64,128]{2,1,0:T(8,128)(2,1)S(1)}, u32[]{:S(2)}, u32[]{:S(2)}) collective-permute-start(bf16[5,64,128]{2,1,0:T(8,128)(2,1)S(1)} %get-tuple-element.105), channel_id=1, source_target_pairs={{1,4},{4,1},{3,6},{6,3},{5,8},{8,5},{7,10},{10,7},{9,12},{12,9},{1... | collective-permute-start | bytes 245768 | tf_op jit(solution)/shard_map/ppermute | solution.py:374
  46.2 5.7 %collective-permute-start.36 = (bf16[5,64,128]{2,1,0:T(8,128)(2,1)S(1)}, bf16[5,64,128]{2,1,0:T(8,128)(2,1)S(1)}, u32[]{:S(2)}, u32[]{:S(2)}) collective-permute-start(bf16[5,64,128]{2,1,0:T(8,128)(2,1)S(1)} %get-tuple-element.141), channel_id=1, source_target_pairs={{1,4},{4,1},{3,6},{6,3},{5,8},{8,5},{7,10},{10,7},{9,12},{12,9},{1... | collective-permute-start | bytes 245768 | tf_op jit(solution)/shard_map/ppermute | solution.py:374
  49.2 5.8 %collective-permute-start.11 = (bf16[5,64,128]{2,1,0:T(8,128)(2,1)S(1)}, bf16[5,64,128]{2,1,0:T(8,128)(2,1)S(1)}, u32[]{:S(2)}, u32[]{:S(2)}) collective-permute-start(bf16[5,64,128]{2,1,0:T(8,128)(2,1)S(1)} %get-tuple-element.107), channel_id=1, source_target_pairs={{0,1},{1,0},{2,3},{3,2},{4,5},{5,4},{6,7},{7,6},{8,9},{9,8},{10,11... | collective-permute-start | bytes 245768 | tf_op jit(solution)/shard_map/ppermute | solution.py:365
  49.3 5.7 %collective-permute-start.12 = (bf16[5,64,128]{2,1,0:T(8,128)(2,1)S(1)}, bf16[5,64,128]{2,1,0:T(8,128)(2,1)S(1)}, u32[]{:S(2)}, u32[]{:S(2)}) collective-permute-start(bf16[5,64,128]{2,1,0:T(8,128)(2,1)S(1)} %get-tuple-element.108), channel_id=1, source_target_pairs={{1,4},{4,1},{3,6},{6,3},{5,8},{8,5},{7,10},{10,7},{9,12},{12,9},{1... | collective-permute-start | bytes 245768 | tf_op jit(solution)/shard_map/ppermute | solution.py:374
  53.4 5.5 %collective-permute-start.37 = (bf16[5,64,128]{2,1,0:T(8,128)(2,1)S(1)}, bf16[5,64,128]{2,1,0:T(8,128)(2,1)S(1)}, u32[]{:S(2)}, u32[]{:S(2)}) collective-permute-start(bf16[5,64,128]{2,1,0:T(8,128)(2,1)S(1)} %get-tuple-element.143), channel_id=1, source_target_pairs={{0,1},{1,0},{2,3},{3,2},{4,5},{5,4},{6,7},{7,6},{8,9},{9,8},{10,11... | collective-permute-start | bytes 245768 | tf_op jit(solution)/shard_map/ppermute | solution.py:365
  53.5 5.7 %collective-permute-start.38 = (bf16[5,64,128]{2,1,0:T(8,128)(2,1)S(1)}, bf16[5,64,128]{2,1,0:T(8,128)(2,1)S(1)}, u32[]{:S(2)}, u32[]{:S(2)}) collective-permute-start(bf16[5,64,128]{2,1,0:T(8,128)(2,1)S(1)} %get-tuple-element.144), channel_id=1, source_target_pairs={{1,4},{4,1},{3,6},{6,3},{5,8},{8,5},{7,10},{10,7},{9,12},{12,9},{1... | collective-permute-start | bytes 245768 | tf_op jit(solution)/shard_map/ppermute | solution.py:374
  56.5 5.8 %collective-permute-start.13 = (bf16[5,64,128]{2,1,0:T(8,128)(2,1)S(1)}, bf16[5,64,128]{2,1,0:T(8,128)(2,1)S(1)}, u32[]{:S(2)}, u32[]{:S(2)}) collective-permute-start(bf16[5,64,128]{2,1,0:T(8,128)(2,1)S(1)} %get-tuple-element.110), channel_id=1, source_target_pairs={{0,1},{1,0},{2,3},{3,2},{4,5},{5,4},{6,7},{7,6},{8,9},{9,8},{10,11... | collective-permute-start | bytes 245768 | tf_op jit(solution)/shard_map/ppermute | solution.py:365
  56.7 5.7 %collective-permute-start.14 = (bf16[5,64,128]{2,1,0:T(8,128)(2,1)S(1)}, bf16[5,64,128]{2,1,0:T(8,128)(2,1)S(1)}, u32[]{:S(2)}, u32[]{:S(2)}) collective-permute-start(bf16[5,64,128]{2,1,0:T(8,128)(2,1)S(1)} %get-tuple-element.111), channel_id=1, source_target_pairs={{1,4},{4,1},{3,6},{6,3},{5,8},{8,5},{7,10},{10,7},{9,12},{12,9},{1... | collective-permute-start | bytes 245768 | tf_op jit(solution)/shard_map/ppermute | solution.py:374
  60.6 6.1 %collective-permute-start.39 = (bf16[5,64,128]{2,1,0:T(8,128)(2,1)S(1)}, bf16[5,64,128]{2,1,0:T(8,128)(2,1)S(1)}, u32[]{:S(2)}, u32[]{:S(2)}) collective-permute-start(bf16[5,64,128]{2,1,0:T(8,128)(2,1)S(1)} %get-tuple-element.146), channel_id=1, source_target_pairs={{0,1},{1,0},{2,3},{3,2},{4,5},{5,4},{6,7},{7,6},{8,9},{9,8},{10,11... | collective-permute-start | bytes 245768 | tf_op jit(solution)/shard_map/ppermute | solution.py:365
  60.7 6.0 %collective-permute-start.40 = (bf16[5,64,128]{2,1,0:T(8,128)(2,1)S(1)}, bf16[5,64,128]{2,1,0:T(8,128)(2,1)S(1)}, u32[]{:S(2)}, u32[]{:S(2)}) collective-permute-start(bf16[5,64,128]{2,1,0:T(8,128)(2,1)S(1)} %get-tuple-element.147), channel_id=1, source_target_pairs={{1,4},{4,1},{3,6},{6,3},{5,8},{8,5},{7,10},{10,7},{9,12},{12,9},{1... | collective-permute-start | bytes 245768 | tf_op jit(solution)/shard_map/ppermute | solution.py:374
  64.5 5.9 %collective-permute-start.15 = (bf16[5,64,128]{2,1,0:T(8,128)(2,1)S(1)}, bf16[5,64,128]{2,1,0:T(8,128)(2,1)S(1)}, u32[]{:S(2)}, u32[]{:S(2)}) collective-permute-start(bf16[5,64,128]{2,1,0:T(8,128)(2,1)S(1)} %get-tuple-element.113), channel_id=1, source_target_pairs={{0,1},{1,0},{2,3},{3,2},{4,5},{5,4},{6,7},{7,6},{8,9},{9,8},{10,11... | collective-permute-start | bytes 245768 | tf_op jit(solution)/shard_map/ppermute | solution.py:365
  64.6 5.8 %collective-permute-start.16 = (bf16[5,64,128]{2,1,0:T(8,128)(2,1)S(1)}, bf16[5,64,128]{2,1,0:T(8,128)(2,1)S(1)}, u32[]{:S(2)}, u32[]{:S(2)}) collective-permute-start(bf16[5,64,128]{2,1,0:T(8,128)(2,1)S(1)} %get-tuple-element.114), channel_id=1, source_target_pairs={{1,4},{4,1},{3,6},{6,3},{5,8},{8,5},{7,10},{10,7},{9,12},{12,9},{1... | collective-permute-start | bytes 245768 | tf_op jit(solution)/shard_map/ppermute | solution.py:374
  68.8 5.7 %collective-permute-start.42 = (bf16[5,64,128]{2,1,0:T(8,128)(2,1)S(1)}, bf16[5,64,128]{2,1,0:T(8,128)(2,1)S(1)}, u32[]{:S(2)}, u32[]{:S(2)}) collective-permute-start(bf16[5,64,128]{2,1,0:T(8,128)(2,1)S(1)} %get-tuple-element.150), channel_id=1, source_target_pairs={{1,4},{4,1},{3,6},{6,3},{5,8},{8,5},{7,10},{10,7},{9,12},{12,9},{1... | collective-permute-start | bytes 245768 | tf_op jit(solution)/shard_map/ppermute | solution.py:374
  71.8 5.8 %collective-permute-start.17 = (bf16[5,64,128]{2,1,0:T(8,128)(2,1)S(1)}, bf16[5,64,128]{2,1,0:T(8,128)(2,1)S(1)}, u32[]{:S(2)}, u32[]{:S(2)}) collective-permute-start(bf16[5,64,128]{2,1,0:T(8,128)(2,1)S(1)} %get-tuple-element.116), channel_id=1, source_target_pairs={{0,1},{1,0},{2,3},{3,2},{4,5},{5,4},{6,7},{7,6},{8,9},{9,8},{10,11... | collective-permute-start | bytes 245768 | tf_op jit(solution)/shard_map/ppermute | solution.py:365
  71.9 5.7 %collective-permute-start.18 = (bf16[5,64,128]{2,1,0:T(8,128)(2,1)S(1)}, bf16[5,64,128]{2,1,0:T(8,128)(2,1)S(1)}, u32[]{:S(2)}, u32[]{:S(2)}) collective-permute-start(bf16[5,64,128]{2,1,0:T(8,128)(2,1)S(1)} %get-tuple-element.117), channel_id=1, source_target_pairs={{1,4},{4,1},{3,6},{6,3},{5,8},{8,5},{7,10},{10,7},{9,12},{12,9},{1... | collective-permute-start | bytes 245768 | tf_op jit(solution)/shard_map/ppermute | solution.py:374
  76.0 5.7 %collective-permute-start.44 = (bf16[5,64,128]{2,1,0:T(8,128)(2,1)S(1)}, bf16[5,64,128]{2,1,0:T(8,128)(2,1)S(1)}, u32[]{:S(2)}, u32[]{:S(2)}) collective-permute-start(bf16[5,64,128]{2,1,0:T(8,128)(2,1)S(1)} %get-tuple-element.153), channel_id=1, source_target_pairs={{1,4},{4,1},{3,6},{6,3},{5,8},{8,5},{7,10},{10,7},{9,12},{12,9},{1... | collective-permute-start | bytes 245768 | tf_op jit(solution)/shard_map/ppermute | solution.py:374
  79.0 5.8 %collective-permute-start.19 = (bf16[5,64,128]{2,1,0:T(8,128)(2,1)S(1)}, bf16[5,64,128]{2,1,0:T(8,128)(2,1)S(1)}, u32[]{:S(2)}, u32[]{:S(2)}) collective-permute-start(bf16[5,64,128]{2,1,0:T(8,128)(2,1)S(1)} %get-tuple-element.119), channel_id=1, source_target_pairs={{0,1},{1,0},{2,3},{3,2},{4,5},{5,4},{6,7},{7,6},{8,9},{9,8},{10,11... | collective-permute-start | bytes 245768 | tf_op jit(solution)/shard_map/ppermute | solution.py:365
  79.1 5.7 %collective-permute-start.20 = (bf16[5,64,128]{2,1,0:T(8,128)(2,1)S(1)}, bf16[5,64,128]{2,1,0:T(8,128)(2,1)S(1)}, u32[]{:S(2)}, u32[]{:S(2)}) collective-permute-start(bf16[5,64,128]{2,1,0:T(8,128)(2,1)S(1)} %get-tuple-element.120), channel_id=1, source_target_pairs={{1,4},{4,1},{3,6},{6,3},{5,8},{8,5},{7,10},{10,7},{9,12},{12,9},{1... | collective-permute-start | bytes 245768 | tf_op jit(solution)/shard_map/ppermute | solution.py:374
  83.2 5.9 %collective-permute-start.45 = (bf16[5,64,128]{2,1,0:T(8,128)(2,1)S(1)}, bf16[5,64,128]{2,1,0:T(8,128)(2,1)S(1)}, u32[]{:S(2)}, u32[]{:S(2)}) collective-permute-start(bf16[5,64,128]{2,1,0:T(8,128)(2,1)S(1)} %get-tuple-element.155), channel_id=1, source_target_pairs={{0,1},{1,0},{2,3},{3,2},{4,5},{5,4},{6,7},{7,6},{8,9},{9,8},{10,11... | collective-permute-start | bytes 245768 | tf_op jit(solution)/shard_map/ppermute | solution.py:365
  83.3 5.8 %collective-permute-start.46 = (bf16[5,64,128]{2,1,0:T(8,128)(2,1)S(1)}, bf16[5,64,128]{2,1,0:T(8,128)(2,1)S(1)}, u32[]{:S(2)}, u32[]{:S(2)}) collective-permute-start(bf16[5,64,128]{2,1,0:T(8,128)(2,1)S(1)} %get-tuple-element.156), channel_id=1, source_target_pairs={{1,4},{4,1},{3,6},{6,3},{5,8},{8,5},{7,10},{10,7},{9,12},{12,9},{1... | collective-permute-start | bytes 245768 | tf_op jit(solution)/shard_map/ppermute | solution.py:374
  86.9 5.9 %collective-permute-start.21 = (bf16[5,64,128]{2,1,0:T(8,128)(2,1)S(1)}, bf16[5,64,128]{2,1,0:T(8,128)(2,1)S(1)}, u32[]{:S(2)}, u32[]{:S(2)}) collective-permute-start(bf16[5,64,128]{2,1,0:T(8,128)(2,1)S(1)} %get-tuple-element.122), channel_id=1, source_target_pairs={{0,1},{1,0},{2,3},{3,2},{4,5},{5,4},{6,7},{7,6},{8,9},{9,8},{10,11... | collective-permute-start | bytes 245768 | tf_op jit(solution)/shard_map/ppermute | solution.py:365
  86.9 5.8 %collective-permute-start.22 = (bf16[5,64,128]{2,1,0:T(8,128)(2,1)S(1)}, bf16[5,64,128]{2,1,0:T(8,128)(2,1)S(1)}, u32[]{:S(2)}, u32[]{:S(2)}) collective-permute-start(bf16[5,64,128]{2,1,0:T(8,128)(2,1)S(1)} %get-tuple-element.123), channel_id=1, source_target_pairs={{1,4},{4,1},{3,6},{6,3},{5,8},{8,5},{7,10},{10,7},{9,12},{12,9},{1... | collective-permute-start | bytes 245768 | tf_op jit(solution)/shard_map/ppermute | solution.py:374
  91.2 5.7 %collective-permute-start.48 = (bf16[5,64,128]{2,1,0:T(8,128)(2,1)S(1)}, bf16[5,64,128]{2,1,0:T(8,128)(2,1)S(1)}, u32[]{:S(2)}, u32[]{:S(2)}) collective-permute-start(bf16[5,64,128]{2,1,0:T(8,128)(2,1)S(1)} %get-tuple-element.159), channel_id=1, source_target_pairs={{1,4},{4,1},{3,6},{6,3},{5,8},{8,5},{7,10},{10,7},{9,12},{12,9},{1... | collective-permute-start | bytes 245768 | tf_op jit(solution)/shard_map/ppermute | solution.py:374
  94.2 5.8 %collective-permute-start.23 = (bf16[5,64,128]{2,1,0:T(8,128)(2,1)S(1)}, bf16[5,64,128]{2,1,0:T(8,128)(2,1)S(1)}, u32[]{:S(2)}, u32[]{:S(2)}) collective-permute-start(bf16[5,64,128]{2,1,0:T(8,128)(2,1)S(1)} %get-tuple-element.125), channel_id=1, source_target_pairs={{0,1},{1,0},{2,3},{3,2},{4,5},{5,4},{6,7},{7,6},{8,9},{9,8},{10,11... | collective-permute-start | bytes 245768 | tf_op jit(solution)/shard_map/ppermute | solution.py:365
  94.2 5.7 %collective-permute-start.24 = (bf16[5,64,128]{2,1,0:T(8,128)(2,1)S(1)}, bf16[5,64,128]{2,1,0:T(8,128)(2,1)S(1)}, u32[]{:S(2)}, u32[]{:S(2)}) collective-permute-start(bf16[5,64,128]{2,1,0:T(8,128)(2,1)S(1)} %get-tuple-element.126), channel_id=1, source_target_pairs={{1,4},{4,1},{3,6},{6,3},{5,8},{8,5},{7,10},{10,7},{9,12},{12,9},{1... | collective-permute-start | bytes 245768 | tf_op jit(solution)/shard_map/ppermute | solution.py:374
  98.4 5.7 %collective-permute-start.50 = (bf16[5,64,128]{2,1,0:T(8,128)(2,1)S(1)}, bf16[5,64,128]{2,1,0:T(8,128)(2,1)S(1)}, u32[]{:S(2)}, u32[]{:S(2)}) collective-permute-start(bf16[5,64,128]{2,1,0:T(8,128)(2,1)S(1)} %get-tuple-element.162), channel_id=1, source_target_pairs={{1,4},{4,1},{3,6},{6,3},{5,8},{8,5},{7,10},{10,7},{9,12},{12,9},{1... | collective-permute-start | bytes 245768 | tf_op jit(solution)/shard_map/ppermute | solution.py:374
  105.6 9.5 %collective-permute-start.53 = (bf16[2,8,64,128]{3,2,1,0:T(8,128)(2,1)S(1)}, bf16[2,8,64,128]{3,2,1,0:T(8,128)(2,1)S(1)}, u32[]{:S(2)}, u32[]{:S(2)}) collective-permute-start(bf16[2,8,64,128]{3,2,1,0:T(8,128)(2,1)S(1)} %pad_maximum_fusion), channel_id=1, source_target_pairs={{2,0},{3,1},{0,2},{1,3},{6,4},{7,5},{4,6},{5,7},{10,8},{11,9},{8,1... | collective-permute-start | bytes 786440 | tf_op jit(solution)/shard_map/ppermute | solution.py:378
  107.2 5.9 %collective-permute-start.52 = (bf16[5,64,128]{2,1,0:T(8,128)(2,1)S(1)}, bf16[5,64,128]{2,1,0:T(8,128)(2,1)S(1)}, u32[]{:S(2)}, u32[]{:S(2)}) collective-permute-start(bf16[5,64,128]{2,1,0:T(8,128)(2,1)S(1)} %get-tuple-element.165), channel_id=1, source_target_pairs={{1,4},{4,1},{3,6},{6,3},{5,8},{8,5},{7,10},{10,7},{9,12},{12,9},{1... | collective-permute-start | bytes 245768 | tf_op jit(solution)/shard_map/ppermute | solution.py:374
  108.4 6.7 %collective-permute-start.25 = (bf16[5,64,128]{2,1,0:T(8,128)(2,1)S(1)}, bf16[5,64,128]{2,1,0:T(8,128)(2,1)S(1)}, u32[]{:S(2)}, u32[]{:S(2)}) collective-permute-start(bf16[5,64,128]{2,1,0:T(8,128)(2,1)S(1)} %get-tuple-element.128), channel_id=1, source_target_pairs={{0,1},{1,0},{2,3},{3,2},{4,5},{5,4},{6,7},{7,6},{8,9},{9,8},{10,11... | collective-permute-start | bytes 245768 | tf_op jit(solution)/shard_map/ppermute | solution.py:365
  108.4 6.7 %collective-permute-start.26 = (bf16[5,64,128]{2,1,0:T(8,128)(2,1)S(1)}, bf16[5,64,128]{2,1,0:T(8,128)(2,1)S(1)}, u32[]{:S(2)}, u32[]{:S(2)}) collective-permute-start(bf16[5,64,128]{2,1,0:T(8,128)(2,1)S(1)} %get-tuple-element.129), channel_id=1, source_target_pairs={{1,4},{4,1},{3,6},{6,3},{5,8},{8,5},{7,10},{10,7},{9,12},{12,9},{1... | collective-permute-start | bytes 245768 | tf_op jit(solution)/shard_map/ppermute | solution.py:374
  118.9 14.4 %collective-permute-start.60 = (bf16[2,8,64,128]{3,2,1,0:T(8,128)(2,1)S(1)}, bf16[2,8,64,128]{3,2,1,0:T(8,128)(2,1)S(1)}, u32[]{:S(2)}, u32[]{:S(2)}) collective-permute-start(bf16[2,8,64,128]{3,2,1,0:T(8,128)(2,1)S(1)} %pad_maximum_fusion), channel_id=1, source_target_pairs={{0,1},{1,0},{2,3},{3,2},{4,5},{5,4},{6,7},{7,6},{8,9},{9,8},{10,11... | collective-permute-start | bytes 786440 | tf_op jit(solution)/shard_map/ppermute | solution.py:365
  119.1 14.2 %collective-permute-start.61 = (bf16[2,8,64,128]{3,2,1,0:T(8,128)(2,1)S(1)}, bf16[2,8,64,128]{3,2,1,0:T(8,128)(2,1)S(1)}, u32[]{:S(2)}, u32[]{:S(2)}) collective-permute-start(bf16[2,8,64,128]{3,2,1,0:T(8,128)(2,1)S(1)} %collective-permute-done.53.rest_1_.refs_6_), channel_id=1, source_target_pairs={{0,1},{1,0},{2,3},{3,2},{4,5},{5,4},{6,7},{7,6},{8,9},{9,8},{10,11... | collective-permute-start | bytes 786440 | tf_op jit(solution)/shard_map/ppermute | solution.py:365
  123.2 5.7 %collective-permute-start.56 = (bf16[272,128]{1,0:T(8,128)(2,1)S(1)}, bf16[272,128]{1,0:T(8,128)(2,1)S(1)}, u32[]{:S(2)}, u32[]{:S(2)}) collective-permute-start(bf16[272,128]{1,0:T(8,128)(2,1)S(1)} %add.20.left), channel_id=1, source_target_pairs={{0,8},{4,12},{8,0},{12,4},{1,9},{5,13},{9,1},{13,5},{2,10},{6,14},... | collective-permute-start | bytes 208904 | tf_op jit(solution)/shard_map/ppermute | solution.py:517
  (19 other events, 76.0 us)

commit v2 on v1

--- a/solution.py
+++ b/solution.py
@@ -10,8 +10,9 @@
 HALF_BAND = 5
 DEGREE = 4
 CORES = 2
-PANEL = 32
-GROUP = 8
+PANEL = 64
+SLOWER = 24
+SUBLANES = 8
 DIAGONAL_ROWS = 16
 
 BF16 = jnp.bfloat16
@@ -68,60 +69,80 @@
     return image_of(table, ext, (ovl,), row).T
 
 
-def cut_kernel(ints, sizes, trial, keep, give):
+def cut_kernel(ints, sizes, trial, keep, give, sizes_here, trial_here, sems):
+    copies = [
+        pltpu.make_async_copy(sizes, sizes_here, sems.at[0]),
+        pltpu.make_async_copy(trial, trial_here, sems.at[1]),
+    ]
+    for copy in copies:
+        copy.start()
+    for copy in copies:
+        copy.wait()
     half, _, orbs = keep.shape
     core = ints[0]
     lane = lax.broadcasted_iota(jnp.int32, keep.shape[1:], 1)
     for out, which in ((give, 1 - core), (keep, core)):
         for row in range(half):
             at = which * half + row
-            values = trial[:, pl.ds(pl.multiple_of(at * orbs, orbs), orbs)].astype(F32)
-            out[row] = jnp.where(lane < sizes[at], values, 0.0).astype(BF16)
-
-
-def load_kernel(total, ints, columns, phases, ham, ovl, ham_out, ovl_out, index, signs, sems):
+            values = trial_here[:, pl.ds(pl.multiple_of(at * orbs, orbs), orbs)].astype(F32)
+            out[row] = jnp.where(lane < sizes_here[at], values, 0.0).astype(BF16)
+
+
+def load_kernel(total, ints, shift, width, columns, phases, sizes, ham, ovl, *rest):
+    ham_out, ovl_out, index, signs, place, scal, columns_here, phases_here, sizes_here = rest[:9]
+    sems, more_sems = rest[9:]
     half, slots = index.shape
     first = ints[0] * half
-    copies = []
-    for row in range(half):
-        for matrix, (source, target) in enumerate(((ham, ham_out), (ovl, ovl_out))):
-            copies.append(
-                pltpu.make_async_copy(
-                    source.at[first + row], target.at[row], sems.at[matrix, row]
-                )
-            )
-    for copy in copies:
+    small = [
+        pltpu.make_async_copy(source, target, more_sems.at[i])
+        for i, (source, target) in enumerate(
+            ((columns, columns_here), (phases, phases_here), (sizes, sizes_here))
+        )
+    ]
+    large = [
+        pltpu.make_async_copy(source.at[first + row], target.at[row], sems.at[matrix, row])
+        for row in range(half)
+        for matrix, (source, target) in enumerate(((ham, ham_out), (ovl, ovl_out)))
+    ]
+    for copy in small + large:
         copy.start()
+    scal[0] = shift[0]
+    scal[1] = width[0]
+    for i in range(3):
+        place[i] = ints[i]
+    for copy in small:
+        copy.wait()
     start = ints[3] + first
 
     def fill(row, _):
+        place[3 + row] = sizes_here[first + row]
         for slot in range(slots):
-            away = columns[first + row, slot] - (start + row) + HALF_BAND
+            away = columns_here[first + row, slot] - (start + row) + HALF_BAND
             away = jnp.where(away < 0, away + total, away)
             away = jnp.where(away >= total, away - total, away)
             index[row, slot] = row + away
-            signs[row, slot] = (1 - 2 * phases[first + row, slot]).astype(F32)
+            signs[row, slot] = (1 - 2 * phases_here[first + row, slot]).astype(F32)
         return 0
 
     lax.fori_loop(0, half, fill, 0)
-    for copy in copies:
+    for copy in large:
         copy.wait()
 
 
 def scaled_kernel(
-    ints, index, signs, shift, width, own, intra, inter, ham, ovl, out, intra_out, inter_out, ext
+    ints, index, signs, scal, own, inter, intra, ham, ovl, out, inter_out, intra_out, ext
 ):
     core = ints[0]
     fill_ext(core, own, intra, inter, ext)
-    inv = 1.0 / (jnp.zeros(own.shape[1:], F32) + width[0])
+    inv = 1.0 / (jnp.zeros(own.shape[1:], F32) + scal[1])
     for row in range(own.shape[0]):
         image_h, image_e = both_rows((index, signs), ext, ham, ovl, row)
         mine = own[row].astype(F32)
-        out[row] = ((image_h - shift[0] * (mine + image_e)) * inv).astype(BF16)
+        out[row] = ((image_h - scal[0] * (mine + image_e)) * inv).astype(BF16)
     send_ends(core, out, intra_out, inter_out)
 
 
-def term_kernel(ints, index, signs, own, intra, inter, ovl, out, intra_out, inter_out, ext):
+def term_kernel(ints, index, signs, own, inter, intra, ovl, out, inter_out, intra_out, ext):
     core = ints[0]
     fill_ext(core, own, intra, inter, ext)
     for row in range(own.shape[0]):
@@ -129,11 +150,11 @@
     send_ends(core, out, intra_out, inter_out)
 
 
-def update_kernel(first, ints, index, signs, sizes, own, intra, inter, scaled, *rest):
+def update_kernel(first, ints, index, signs, own, inter, intra, scaled, *rest):
     if first:
-        ovl, out, intra_out, inter_out, ext = rest
+        ovl, out, inter_out, intra_out, ext = rest
     else:
-        previous, ovl, out, intra_out, inter_out, ext = rest
+        previous, ovl, out, inter_out, intra_out, ext = rest
     core = ints[0]
     half = own.shape[0]
     fill_ext(core, own, intra, inter, ext)
@@ -143,11 +164,11 @@
         filtered = scaled[row].astype(F32) + own[row].astype(F32) - image
         if not first:
             filtered = 2.0 * filtered - previous[row].astype(F32)
-        out[row] = jnp.where(lane < sizes[core * half + row], filtered, 0.0).astype(BF16)
+        out[row] = jnp.where(lane < ints[3 + row], filtered, 0.0).astype(BF16)
     send_ends(core, out, intra_out, inter_out)
 
 
-def images_kernel(ints, index, signs, own, intra, inter, ham, ovl, out, ext):
+def images_kernel(ints, index, signs, own, inter, intra, ham, ovl, out, ext):
     core = ints[0]
     fill_ext(core, own, intra, inter, ext)
     half, _, orbs = own.shape
@@ -158,10 +179,10 @@
         out[1, :, at] = image_h.astype(BF16)
 
 
-def gram_kernel(chips, ints, index, signs, own, intra, inter, ham, ovl, ready, *rest):
+def gram_kernel(chips, ints, index, signs, own, inter, intra, ham, ovl, ready, *rest):
     first, *others = rest[:chips]
     keep, send, ext, images, both = rest[chips:]
-    images_kernel(ints, index, signs, own, intra, inter, ham, ovl, images, ext)
+    images_kernel(ints, index, signs, own, inter, intra, ham, ovl, images, ext)
     core, chip = ints[0], ints[1]
     half, local_vecs, _ = own.shape
     vecs = CORES * local_vecs
@@ -220,32 +241,40 @@
     lane = lax.broadcasted_iota(jnp.int32, (PANEL, 128), 1)
     rows = lax.broadcasted_iota(jnp.int32, (PANEL, 128), 0)
     work = jnp.where(lane < PANEL, block, jnp.where(lax.rem(lane, PANEL) == rows, 1.0, 0.0))
-    pieces = [work[g * GROUP : (g + 1) * GROUP] for g in range(PANEL // GROUP)]
-    sub = lax.broadcasted_iota(jnp.int32, (GROUP, 128), 0)
-    groups = PANEL // GROUP
-    pivots = []
-    for g in range(groups):
-        columns = [
-            [
-                jnp.broadcast_to(pieces[v][:, g * GROUP + j : g * GROUP + j + 1], (GROUP, 128))
-                for v in range(g, groups)
-            ]
-            for j in range(GROUP)
-        ]
-        pivot = jnp.ones((GROUP, 128), F32)
-        for j in range(GROUP):
-            at = jnp.broadcast_to(columns[j][0][j : j + 1], (GROUP, 128))
-            pivot = jnp.where(sub == j, at, pivot)
+    count = PANEL // SUBLANES
+    pieces = [work[v * SUBLANES : (v + 1) * SUBLANES] for v in range(count)]
+    sub = lax.broadcasted_iota(jnp.int32, (SUBLANES, 128), 0)
+
+    def spread(value, k):
+        return jnp.broadcast_to(value[k % SUBLANES : k % SUBLANES + 1], (SUBLANES, 128))
+
+    pivots = [jnp.ones((SUBLANES, 128), F32) for _ in range(count)]
+    for start, group in ((0, 8), (8, 8), (16, 8), (24, 8), (32, 16), (48, 16)):
+        columns = {
+            k: {
+                v: jnp.broadcast_to(pieces[v][:, k : k + 1], (SUBLANES, 128))
+                for v in range(start // SUBLANES, count)
+            }
+            for k in range(start, start + group)
+        }
+        at = spread(columns[start][start // SUBLANES], start)
+        for k in range(start, start + group):
+            here = k // SUBLANES
+            pivots[here] = jnp.where(sub == k % SUBLANES, at, pivots[here])
             inv = reciprocal(at)
-            factors = [c * inv for c in columns[j]]
-            factors[0] = jnp.where(sub > j, factors[0], 0.0)
-            for later in range(j + 1, GROUP):
-                top = jnp.broadcast_to(columns[later][0][j : j + 1], (GROUP, 128))
-                columns[later] = [c - f * top for c, f in zip(columns[later], factors)]
-            top = jnp.broadcast_to(pieces[g][j : j + 1], (GROUP, 128))
-            for v in range(g, groups):
-                pieces[v] = pieces[v] - factors[v - g] * top
-        pivots.append(pivot)
+            if k + 1 < start + group:
+                below = (k + 1) // SUBLANES
+                product = spread(columns[k][below], k + 1) * spread(columns[k + 1][here], k)
+                at = spread(columns[k + 1][below], k + 1) - product * inv
+            factors = {v: columns[k][v] * inv for v in range(here, count)}
+            factors[here] = jnp.where(sub > k % SUBLANES, factors[here], 0.0)
+            for later in range(k + 1, start + group):
+                top = spread(columns[later][here], k)
+                for v in range(here, count):
+                    columns[later][v] = columns[later][v] - factors[v] * top
+            top = spread(pieces[here], k)
+            for v in range(here, count):
+                pieces[v] = pieces[v] - factors[v] * top
     pivot = jnp.concatenate(pivots, axis=0)
     root = lax.rsqrt(pivot)
     root = root * (1.5 - 0.5 * ((pivot * root) * root))
@@ -264,16 +293,13 @@
         block = work[start : start + PANEL, tile : tile + 128]
         if start % 128:
             block = pltpu.roll(block, 128 - start % 128, axis=1)
-        t_high, t_mid, t_low = split3(panel_inverse(block))
-        first = jnp.where(lane < 2 * PANEL, t_high, jnp.where(lane < 3 * PANEL, t_mid, t_low))
-        second = jnp.where(lane < 2 * PANEL, t_high, jnp.where(lane < 3 * PANEL, t_mid, t_high))
-        left = jnp.concatenate([first, second], axis=1)
-        spread = jnp.where(lax.rem(wide, 128) < PANEL, jnp.zeros_like(left[:, :1]), jnp.ones_like(left[:, :1]))
-        left = left * spread[:, : left.shape[1]]
+        t_high, t_mid, t_low = split3(jnp.where(lane < PANEL, 0.0, panel_inverse(block)))
+        left = jnp.concatenate([t_high, t_mid, t_low, t_high, t_mid, t_high], axis=1)
         inside = (wide >= start) & (wide < start + PANEL)
         rows = jnp.where(inside, jnp.where(wide - start == tall, 1.0, 0.0), rows)
         r_high, r_mid, r_low = split3(rows)
-        right = jnp.concatenate([zero, r_high, r_high, r_high, zero, r_mid, r_mid, r_low], axis=0)
+        right = [part for r in (r_high, r_high, r_high, r_mid, r_mid, r_low) for part in (zero, r)]
+        right = jnp.concatenate(right, axis=0)
         new = jnp.dot(left, right, preferred_element_type=F32)
         inverse[start : start + PANEL, :] = jnp.where(wide < start + PANEL, new, 0.0)
         after = start + PANEL
@@ -312,11 +338,11 @@
     start = pl.multiple_of(col * local_vecs, local_vecs)
     own_rows = inverse[pl.ds(start, local_vecs), :]
     gram_h = (pair[1] + pair[1].T) * scale
-    half_way = lax.dot_general(
-        gram_h, own_rows, NT, precision=lax.Precision.HIGHEST, preferred_element_type=F32
-    )
-    reduced[...] = jnp.dot(
-        inverse[...], half_way, precision=lax.Precision.HIGHEST, preferred_element_type=F32
+    half_way = jnp.dot(
+        own_rows, gram_h, precision=lax.Precision.HIGHEST, preferred_element_type=F32
+    )
+    reduced[...] = lax.dot_general(
+        half_way, inverse[...], NT, precision=lax.Precision.HIGHEST, preferred_element_type=F32
     )
     rotation = own_rows.astype(BF16)
     turned = []
@@ -381,7 +407,7 @@
     end = jax.ShapeDtypeStruct((HALF_BAND, local_vecs, orbs), BF16)
     ext = pltpu.VMEM((half + 2 * HALF_BAND, local_vecs, orbs), BF16)
     params = pltpu.CompilerParams(vmem_limit_bytes=16 << 20)
-    row_flops = 2 * half * slots * local_vecs * orbs * orbs
+    row_flops = SLOWER * 2 * half * slots * local_vecs * orbs * orbs
 
     def call(kernel, name, scalars, arrays, outs, scratch, flops):
         return pl.pallas_call(
@@ -401,21 +427,33 @@
         return call(kernel, name, scalars, arrays, (state, end, end), [ext], flops)
 
     def exchange(ends):
-        inter = swap_chips(ends[1])
-        return swap_cores(ends[0]), inter
+        return swap_chips(ends[0]), swap_cores(ends[1])
 
     def scalars(value):
         return pltpu.with_memory_space_constraint(value, pltpu.SMEM)
 
     ints = scalars(jnp.stack([core, chip, col, row * blocks_dev]).astype(jnp.int32))
-    block_sizes, shift, halfwidth = (scalars(x) for x in (block_sizes, shift, halfwidth))
-    block_columns, block_phases = scalars(block_columns), scalars(block_phases)
-    own, give = call(
-        cut_kernel, "cut", (ints, block_sizes), (trial_vectors,), (state, state), [], row_flops
-    )
+    shift, halfwidth = scalars(shift), scalars(halfwidth)
+
+    def stays(value):
+        return pltpu.with_memory_space_constraint(value, pltpu.HBM)
+
+    own, give = pl.pallas_call(
+        cut_kernel,
+        name="cut",
+        out_shape=(state, state),
+        in_specs=[SMEM, HBM, HBM],
+        out_specs=(VMEM, VMEM),
+        scratch_shapes=[
+            pltpu.SMEM(block_sizes.shape, jnp.int32),
+            pltpu.VMEM(trial_vectors.shape, BF16),
+            pltpu.SemaphoreType.DMA((2,)),
+        ],
+        compiler_params=params,
+    )(ints, stays(block_sizes), stays(trial_vectors))
     got = swap_cores(give)
     matrix = vmem((half, *hamiltonian_blocks.shape[1:]), BF16)
-    ham, ovl, index, signs = pl.pallas_call(
+    ham, ovl, index, signs, place, scal = pl.pallas_call(
         functools.partial(load_kernel, total_blocks),
         name="load",
         out_shape=(
@@ -423,32 +461,42 @@
             matrix,
             pltpu.SMEM((half, slots), jnp.int32),
             pltpu.SMEM((half, slots), F32),
+            pltpu.SMEM((3 + half,), jnp.int32),
+            pltpu.SMEM((2,), F32),
         ),
-        in_specs=[SMEM, SMEM, SMEM, HBM, HBM],
-        out_specs=(VMEM, VMEM, SMEM, SMEM),
-        scratch_shapes=[pltpu.SemaphoreType.DMA((2, half))],
+        in_specs=[SMEM] * 3 + [HBM] * 5,
+        out_specs=(VMEM, VMEM, SMEM, SMEM, SMEM, SMEM),
+        scratch_shapes=[
+            pltpu.SMEM(block_columns.shape, jnp.int32),
+            pltpu.SMEM(block_phases.shape, jnp.int32),
+            pltpu.SMEM(block_sizes.shape, jnp.int32),
+            pltpu.SemaphoreType.DMA((2, half)),
+            pltpu.SemaphoreType.DMA((3,)),
+        ],
         compiler_params=params,
         cost_estimate=pl.CostEstimate(
             flops=0, bytes_accessed=4 * hamiltonian_blocks.size, transcendentals=0
         ),
     )(
         ints,
-        block_columns,
-        block_phases,
-        pltpu.with_memory_space_constraint(hamiltonian_blocks, pltpu.HBM),
-        pltpu.with_memory_space_constraint(correlation_offset, pltpu.HBM),
-    )
-    got, ham, ovl = lax.optimization_barrier((got, ham, ovl))
+        shift,
+        halfwidth,
+        stays(block_columns),
+        stays(block_phases),
+        stays(block_sizes),
+        stays(hamiltonian_blocks),
+        stays(correlation_offset),
+    )
     current = [jnp.where(core == 0, own, got), jnp.where(core == 0, got, own)]
     spare = half - HALF_BAND
     ends = [
         (
+            lax.dynamic_slice_in_dim(value, spare * core, HALF_BAND, 0),
             lax.dynamic_slice_in_dim(value, spare * (1 - core), HALF_BAND, 0),
-            lax.dynamic_slice_in_dim(value, spare * core, HALF_BAND, 0),
         )
         for value in current
     ]
-    table = (ints, index, signs)
+    table = (place, index, signs)
     scaled, term, previous = [None] * CORES, [None] * CORES, list(current)
     halo = [exchange(ends[g]) for g in range(CORES)]
     for degree in range(DEGREE):
@@ -456,7 +504,7 @@
             scaled[g], *ends = step_call(
                 scaled_kernel,
                 "scaled",
-                (*table, shift, halfwidth),
+                (*table, scal),
                 (current[g], *halo[g], ham, ovl),
                 2 * row_flops,
             )
@@ -472,7 +520,7 @@
             updated, *ends = step_call(
                 functools.partial(update_kernel, first),
                 "update",
-                (*table, block_sizes),
+                table,
                 arrays,
                 row_flops,
             )
@@ -520,14 +568,14 @@
     mine = [summed] + [from_chip(summed, step) for step in range(1, chips)]
     theirs = [swap_cores(value) for value in mine]
     y_theirs = [swap_cores(value) for value in (stacked, *y_others)]
-    return call(
+    basis, reduced = call(
         functools.partial(finish_kernel, chips, 0.5 / (total_blocks * orbs)),
         "finish",
-        (ints,),
+        (place,),
         (*mine, *theirs, *current, *y_others, *y_theirs),
         (
             jax.ShapeDtypeStruct((local_vecs, blocks_dev * orbs), BF16),
-            jax.ShapeDtypeStruct((size, local_vecs), F32),
+            jax.ShapeDtypeStruct((local_vecs, size), F32),
         ),
         [
             pltpu.VMEM((2, size, size), F32),
@@ -536,6 +584,7 @@
         ],
         10 * row_flops,
     )
+    return basis, reduced.T
 
 
 def solution(mesh):

time: 148 us -> 135 us (0.912)
  Pallas kernels: 60.4 us -> 44.1 us
  waiting for transfers between devices: 25.8 us -> 31 us
  local copies, waits for them, and re-layouts: 3.75 us -> 0.03 us
  starting transfers between devices: 55.7 us -> 57.7 us
    pallas_call x31 -> x30, Pallas kernels: 57.1 us -> 39.5 us  [call(): pl.pallas_call(kernel, name=name, out_shape=outs, in_specs=[SMEM] * len(s...]
    ppermute x26, waiting for transfers between devices: 10.7 us -> 17 us  [swap_chips(): return lax.ppermute(value, ('row', 'col'), pairs)]
    unnamed x10 -> x0, local copies, waits for them, and re-layouts: 3.01 us -> none
    ppermute x2, waiting for transfers between devices: 8.73 us -> 6.3 us  [local(): other = lax.ppermute(summed, 'row', [(r, r ^ bit) for r in range(num_rows)])]
    ppermute x2, starting transfers between devices: 0.72 us -> 2.84 us  [local(): other = lax.ppermute(summed, 'row', [(r, r ^ bit) for r in range(num_rows)])]
    pallas_call x0 -> x1, Pallas kernels: none -> 1.58 us  [local(): pl.pallas_call(cut_kernel, name='cut', out_shape=(state, state), in_specs...]
    ppermute x32, starting transfers between devices: 3.18 us -> 1.67 us  [swap_cores(): return lax.ppermute(value, 'col', [(c, c ^ 1) for c in range(num_cols)])]
  transfers between devices with their start and end apart: 62 -> 62, of which waited for: 18 -> 27; matrix products, arithmetic and copies ran while one was open for 0% -> 0% of each run, Pallas kernels for 29% -> 23%
where the time goes in v2:
time: 135 us
  starting transfers between devices  57.7 us (43%)
  Pallas kernels  44.1 us (33%)
  waiting for transfers between devices  31 us (23%)
  between operations  2.29 us (2%)
    ppermute x26, starting transfers between devices, swap_chips(): return lax.ppermute(value, ('row', 'col'), pairs)  50 us
    pallas_call x30, Pallas kernels, call(): pl.pallas_call(kernel, name=name, out_shape=outs, in_specs=[SMEM] * len(s...  39.5 us
    ppermute x26, waiting for transfers between devices, swap_chips(): return lax.ppermute(value, ('row', 'col'), pairs)  17 us
    ppermute x2, waiting for transfers between devices, local(): other = lax.ppermute(summed, 'row', [(r, r ^ bit) for r in range(num_rows)])  6.3 us
    ppermute x2, waiting for transfers between devices, from_chip(): return lax.ppermute(value, 'col', pairs)  5.12 us
    ppermute x2, starting transfers between devices, from_chip(): return lax.ppermute(value, 'col', pairs)  3.17 us
    pallas_call x1, Pallas kernels, local(): pl.pallas_call(functools.partial(load_kernel, total_blocks), name='load',...  3.01 us
    ppermute x2, starting transfers between devices, local(): other = lax.ppermute(summed, 'row', [(r, r ^ bit) for r in range(num_rows)])  2.84 us
  transfers between devices with their start and end apart: 62, of which 27 were waited for; matrix products, arithmetic and copies ran while one was open for 0% of the time, Pallas kernels for 23%

profile of v2, /device:TPU:0, one launch (start us, length us, event | category | flops | bytes accessed | tf_op | source)
XLA Modules:
  0.0 135.3 jit_solution(386875895479393575)
XLA Ops:
  0.7 1.6 %cut.1 = (bf16[8,64,128]{2,1,0:T(8,128)(2,1)S(1)}, bf16[8,64,128]{2,1,0:T(8,128)(2,1)S(1)}) custom-call(s32[4]{0:T(128)S(1)} %pad_add_fusion.ints, s32[16]{0:T(128)} %sizes.3, bf16[64,2048]{1,0:T(8,128)(2,1)} %trial.1), custom_call_target="tpu_custom_call" | custom-call | tf_op jit(solution)/shard_map/cut/pallas_call | solution.py:441
  4.1 3.0 %load.1 = (bf16[8,9,128,128]{3,2,1,0:T(8,128)(2,1)S(1)}, bf16[8,9,128,128]{3,2,1,0:T(8,128)(2,1)S(1)}, s32[8,9]{1,0:T(8,128)S(4)}, f32[8,9]{1,0:T(8,128)S(4)}, s32[11]{0:T(128)S(4)}, /*index=5*/f32[2]{0:T(128)S(4)}) custom-call(s32[4]{0:T(128)S(1)} %pad_add_fusion.ints, f32[1]{0:T(128)S(6)} %copy.10.shift, f32[1]{0:T(128)S(6)} %copy.11.width, ...), custom_call_target="tpu_custom_call" | custom-call | bytes 9437184 | tf_op jit(solution)/shard_map/load/pallas_call | solution.py:456
  7.2 4.8 %collective-permute-start.1 = (bf16[5,64,128]{2,1,0:T(8,128)(2,1)S(1)}, bf16[5,64,128]{2,1,0:T(8,128)(2,1)S(1)}, u32[]{:S(2)}, u32[]{:S(2)}) collective-permute-start(bf16[5,64,128]{2,1,0:T(8,128)(2,1)S(1)} %get-tuple-element.175), channel_id=1, source_target_pairs={{1,4},{4,1},{3,6},{6,3},{5,8},{8,5},{7,10},{10,7},{9,12},{12,9},{1... | collective-permute-start | bytes 245768 | tf_op jit(solution)/shard_map/ppermute | solution.py:400
  12.7 2.1 %collective-permute-done.1.inter = bf16[5,64,128]{2,1,0:T(8,128)(2,1)S(1)} collective-permute-done((bf16[5,64,128]{2,1,0:T(8,128)(2,1)S(1)}, bf16[5,64,128]{2,1,0:T(8,128)(2,1)S(1)}, u32[]{:S(2)}, u32[]{:S(2)}) %collective-permute-start.1) | collective-permute-done | bytes 81952 | tf_op jit(solution)/shard_map/ppermute | solution.py:400
  14.7 1.5 %scaled.8 = (bf16[8,64,128]{2,1,0:T(8,128)(2,1)S(1)}, bf16[5,64,128]{2,1,0:T(8,128)(2,1)S(1)}, bf16[5,64,128]{2,1,0:T(8,128)(2,1)S(1)}) custom-call(s32[11]{0:T(128)S(4)} %get-tuple-element.86.ints, s32[8,9]{1,0:T(8,128)S(4)} %get-tuple-element.87.index, f32[8,9]{1,0:T(8,128)S(4)} %get-tuple-element.88.signs, f32[2]{0:T(128)S(4)} %get-tuple-element.89.scal, ...), custom_call_target="tpu_custom_call" | custom-call | flops 7247757312 | bytes 56623104 | tf_op jit(solution)/shard_map/scaled/pallas_call | solution.py:413
  16.2 3.8 %collective-permute-start.3 = (bf16[5,64,128]{2,1,0:T(8,128)(2,1)S(1)}, bf16[5,64,128]{2,1,0:T(8,128)(2,1)S(1)}, u32[]{:S(2)}, u32[]{:S(2)}) collective-permute-start(bf16[5,64,128]{2,1,0:T(8,128)(2,1)S(1)} %get-tuple-element.95), channel_id=1, source_target_pairs={{1,4},{4,1},{3,6},{6,3},{5,8},{8,5},{7,10},{10,7},{9,12},{12,9},{1... | collective-permute-start | bytes 245768 | tf_op jit(solution)/shard_map/ppermute | solution.py:400
  20.0 1.5 %scaled.12 = (bf16[8,64,128]{2,1,0:T(8,128)(2,1)S(1)}, bf16[5,64,128]{2,1,0:T(8,128)(2,1)S(1)}, bf16[5,64,128]{2,1,0:T(8,128)(2,1)S(1)}) custom-call(s32[11]{0:T(128)S(4)} %get-tuple-element.86.ints, s32[8,9]{1,0:T(8,128)S(4)} %get-tuple-element.87.index, f32[8,9]{1,0:T(8,128)S(4)} %get-tuple-element.88.signs, f32[2]{0:T(128)S(4)} %get-tuple-element.89.scal, ...), custom_call_target="tpu_custom_call" | custom-call | flops 7247757312 | bytes 56623104 | tf_op jit(solution)/shard_map/scaled/pallas_call | solution.py:413
  23.1 3.6 %collective-permute-start.5 = (bf16[5,64,128]{2,1,0:T(8,128)(2,1)S(1)}, bf16[5,64,128]{2,1,0:T(8,128)(2,1)S(1)}, u32[]{:S(2)}, u32[]{:S(2)}) collective-permute-start(bf16[5,64,128]{2,1,0:T(8,128)(2,1)S(1)} %get-tuple-element.98), channel_id=1, source_target_pairs={{1,4},{4,1},{3,6},{6,3},{5,8},{8,5},{7,10},{10,7},{9,12},{12,9},{1... | collective-permute-start | bytes 245768 | tf_op jit(solution)/shard_map/ppermute | solution.py:400
  30.6 2.9 %collective-permute-start.7 = (bf16[5,64,128]{2,1,0:T(8,128)(2,1)S(1)}, bf16[5,64,128]{2,1,0:T(8,128)(2,1)S(1)}, u32[]{:S(2)}, u32[]{:S(2)}) collective-permute-start(bf16[5,64,128]{2,1,0:T(8,128)(2,1)S(1)} %get-tuple-element.101), channel_id=1, source_target_pairs={{1,4},{4,1},{3,6},{6,3},{5,8},{8,5},{7,10},{10,7},{9,12},{12,9},{1... | collective-permute-start | bytes 245768 | tf_op jit(solution)/shard_map/ppermute | solution.py:400
  34.0 0.9 update.12
  35.6 0.9 collective-permute-done.7.inter
  36.5 1.5 %scaled.9 = (bf16[8,64,128]{2,1,0:T(8,128)(2,1)S(1)}, bf16[5,64,128]{2,1,0:T(8,128)(2,1)S(1)}, bf16[5,64,128]{2,1,0:T(8,128)(2,1)S(1)}) custom-call(s32[11]{0:T(128)S(4)} %get-tuple-element.86.ints, s32[8,9]{1,0:T(8,128)S(4)} %get-tuple-element.87.index, f32[8,9]{1,0:T(8,128)S(4)} %get-tuple-element.88.signs, f32[2]{0:T(128)S(4)} %get-tuple-element.89.scal, ...), custom_call_target="tpu_custom_call" | custom-call | flops 7247757312 | bytes 56623104 | tf_op jit(solution)/shard_map/scaled/pallas_call | solution.py:413
  38.0 2.9 %collective-permute-start.9 = (bf16[5,64,128]{2,1,0:T(8,128)(2,1)S(1)}, bf16[5,64,128]{2,1,0:T(8,128)(2,1)S(1)}, u32[]{:S(2)}, u32[]{:S(2)}) collective-permute-start(bf16[5,64,128]{2,1,0:T(8,128)(2,1)S(1)} %get-tuple-element.104), channel_id=1, source_target_pairs={{1,4},{4,1},{3,6},{6,3},{5,8},{8,5},{7,10},{10,7},{9,12},{12,9},{1... | collective-permute-start | bytes 245768 | tf_op jit(solution)/shard_map/ppermute | solution.py:400
  40.9 1.5 %scaled.13 = (bf16[8,64,128]{2,1,0:T(8,128)(2,1)S(1)}, bf16[5,64,128]{2,1,0:T(8,128)(2,1)S(1)}, bf16[5,64,128]{2,1,0:T(8,128)(2,1)S(1)}) custom-call(s32[11]{0:T(128)S(4)} %get-tuple-element.86.ints, s32[8,9]{1,0:T(8,128)S(4)} %get-tuple-element.87.index, f32[8,9]{1,0:T(8,128)S(4)} %get-tuple-element.88.signs, f32[2]{0:T(128)S(4)} %get-tuple-element.89.scal, ...), custom_call_target="tpu_custom_call" | custom-call | flops 7247757312 | bytes 56623104 | tf_op jit(solution)/shard_map/scaled/pallas_call | solution.py:413
  44.7 2.9 %collective-permute-start.11 = (bf16[5,64,128]{2,1,0:T(8,128)(2,1)S(1)}, bf16[5,64,128]{2,1,0:T(8,128)(2,1)S(1)}, u32[]{:S(2)}, u32[]{:S(2)}) collective-permute-start(bf16[5,64,128]{2,1,0:T(8,128)(2,1)S(1)} %get-tuple-element.107), channel_id=1, source_target_pairs={{1,4},{4,1},{3,6},{6,3},{5,8},{8,5},{7,10},{10,7},{9,12},{12,9},{1... | collective-permute-start | bytes 245768 | tf_op jit(solution)/shard_map/ppermute | solution.py:400
  50.7 0.9 update.9
  51.6 2.8 %collective-permute-start.13 = (bf16[5,64,128]{2,1,0:T(8,128)(2,1)S(1)}, bf16[5,64,128]{2,1,0:T(8,128)(2,1)S(1)}, u32[]{:S(2)}, u32[]{:S(2)}) collective-permute-start(bf16[5,64,128]{2,1,0:T(8,128)(2,1)S(1)} %get-tuple-element.110), channel_id=1, source_target_pairs={{1,4},{4,1},{3,6},{6,3},{5,8},{8,5},{7,10},{10,7},{9,12},{12,9},{1... | collective-permute-start | bytes 245768 | tf_op jit(solution)/shard_map/ppermute | solution.py:400
  54.8 0.9 update.13
  57.3 1.5 %scaled.10 = (bf16[8,64,128]{2,1,0:T(8,128)(2,1)S(1)}, bf16[5,64,128]{2,1,0:T(8,128)(2,1)S(1)}, bf16[5,64,128]{2,1,0:T(8,128)(2,1)S(1)}) custom-call(s32[11]{0:T(128)S(4)} %get-tuple-element.86.ints, s32[8,9]{1,0:T(8,128)S(4)} %get-tuple-element.87.index, f32[8,9]{1,0:T(8,128)S(4)} %get-tuple-element.88.signs, f32[2]{0:T(128)S(4)} %get-tuple-element.89.scal, ...), custom_call_target="tpu_custom_call" | custom-call | flops 7247757312 | bytes 56623104 | tf_op jit(solution)/shard_map/scaled/pallas_call | solution.py:413
  58.8 2.9 %collective-permute-start.15 = (bf16[5,64,128]{2,1,0:T(8,128)(2,1)S(1)}, bf16[5,64,128]{2,1,0:T(8,128)(2,1)S(1)}, u32[]{:S(2)}, u32[]{:S(2)}) collective-permute-start(bf16[5,64,128]{2,1,0:T(8,128)(2,1)S(1)} %get-tuple-element.113), channel_id=1, source_target_pairs={{1,4},{4,1},{3,6},{6,3},{5,8},{8,5},{7,10},{10,7},{9,12},{12,9},{1... | collective-permute-start | bytes 245768 | tf_op jit(solution)/shard_map/ppermute | solution.py:400
  61.7 1.5 %scaled.14 = (bf16[8,64,128]{2,1,0:T(8,128)(2,1)S(1)}, bf16[5,64,128]{2,1,0:T(8,128)(2,1)S(1)}, bf16[5,64,128]{2,1,0:T(8,128)(2,1)S(1)}) custom-call(s32[11]{0:T(128)S(4)} %get-tuple-element.86.ints, s32[8,9]{1,0:T(8,128)S(4)} %get-tuple-element.87.index, f32[8,9]{1,0:T(8,128)S(4)} %get-tuple-element.88.signs, f32[2]{0:T(128)S(4)} %get-tuple-element.89.scal, ...), custom_call_target="tpu_custom_call" | custom-call | flops 7247757312 | bytes 56623104 | tf_op jit(solution)/shard_map/scaled/pallas_call | solution.py:413
  64.6 0.9 term.10
  65.5 3.0 %collective-permute-start.17 = (bf16[5,64,128]{2,1,0:T(8,128)(2,1)S(1)}, bf16[5,64,128]{2,1,0:T(8,128)(2,1)S(1)}, u32[]{:S(2)}, u32[]{:S(2)}) collective-permute-start(bf16[5,64,128]{2,1,0:T(8,128)(2,1)S(1)} %get-tuple-element.116), channel_id=1, source_target_pairs={{1,4},{4,1},{3,6},{6,3},{5,8},{8,5},{7,10},{10,7},{9,12},{12,9},{1... | collective-permute-start | bytes 245768 | tf_op jit(solution)/shard_map/ppermute | solution.py:400
  69.0 0.9 term.14
  71.5 0.9 update.10
  72.4 2.8 %collective-permute-start.19 = (bf16[5,64,128]{2,1,0:T(8,128)(2,1)S(1)}, bf16[5,64,128]{2,1,0:T(8,128)(2,1)S(1)}, u32[]{:S(2)}, u32[]{:S(2)}) collective-permute-start(bf16[5,64,128]{2,1,0:T(8,128)(2,1)S(1)} %get-tuple-element.119), channel_id=1, source_target_pairs={{1,4},{4,1},{3,6},{6,3},{5,8},{8,5},{7,10},{10,7},{9,12},{12,9},{1... | collective-permute-start | bytes 245768 | tf_op jit(solution)/shard_map/ppermute | solution.py:400
  75.7 0.9 update.14
  78.2 1.5 %scaled.11 = (bf16[8,64,128]{2,1,0:T(8,128)(2,1)S(1)}, bf16[5,64,128]{2,1,0:T(8,128)(2,1)S(1)}, bf16[5,64,128]{2,1,0:T(8,128)(2,1)S(1)}) custom-call(s32[11]{0:T(128)S(4)} %get-tuple-element.86.ints, s32[8,9]{1,0:T(8,128)S(4)} %get-tuple-element.87.index, f32[8,9]{1,0:T(8,128)S(4)} %get-tuple-element.88.signs, f32[2]{0:T(128)S(4)} %get-tuple-element.89.scal, ...), custom_call_target="tpu_custom_call" | custom-call | flops 7247757312 | bytes 56623104 | tf_op jit(solution)/shard_map/scaled/pallas_call | solution.py:413
  79.7 2.9 %collective-permute-start.21 = (bf16[5,64,128]{2,1,0:T(8,128)(2,1)S(1)}, bf16[5,64,128]{2,1,0:T(8,128)(2,1)S(1)}, u32[]{:S(2)}, u32[]{:S(2)}) collective-permute-start(bf16[5,64,128]{2,1,0:T(8,128)(2,1)S(1)} %get-tuple-element.122), channel_id=1, source_target_pairs={{1,4},{4,1},{3,6},{6,3},{5,8},{8,5},{7,10},{10,7},{9,12},{12,9},{1... | collective-permute-start | bytes 245768 | tf_op jit(solution)/shard_map/ppermute | solution.py:400
  82.6 1.5 %scaled.15 = (bf16[8,64,128]{2,1,0:T(8,128)(2,1)S(1)}, bf16[5,64,128]{2,1,0:T(8,128)(2,1)S(1)}, bf16[5,64,128]{2,1,0:T(8,128)(2,1)S(1)}) custom-call(s32[11]{0:T(128)S(4)} %get-tuple-element.86.ints, s32[8,9]{1,0:T(8,128)S(4)} %get-tuple-element.87.index, f32[8,9]{1,0:T(8,128)S(4)} %get-tuple-element.88.signs, f32[2]{0:T(128)S(4)} %get-tuple-element.89.scal, ...), custom_call_target="tpu_custom_call" | custom-call | flops 7247757312 | bytes 56623104 | tf_op jit(solution)/shard_map/scaled/pallas_call | solution.py:413
  86.3 3.0 %collective-permute-start.23 = (bf16[5,64,128]{2,1,0:T(8,128)(2,1)S(1)}, bf16[5,64,128]{2,1,0:T(8,128)(2,1)S(1)}, u32[]{:S(2)}, u32[]{:S(2)}) collective-permute-start(bf16[5,64,128]{2,1,0:T(8,128)(2,1)S(1)} %get-tuple-element.125), channel_id=1, source_target_pairs={{1,4},{4,1},{3,6},{6,3},{5,8},{8,5},{7,10},{10,7},{9,12},{12,9},{1... | collective-permute-start | bytes 245768 | tf_op jit(solution)/shard_map/ppermute | solution.py:400
  92.4 1.1 update.11
  93.5 2.8 %collective-permute-start.25 = (bf16[5,64,128]{2,1,0:T(8,128)(2,1)S(1)}, bf16[5,64,128]{2,1,0:T(8,128)(2,1)S(1)}, u32[]{:S(2)}, u32[]{:S(2)}) collective-permute-start(bf16[5,64,128]{2,1,0:T(8,128)(2,1)S(1)} %get-tuple-element.128), channel_id=1, source_target_pairs={{1,4},{4,1},{3,6},{6,3},{5,8},{8,5},{7,10},{10,7},{9,12},{12,9},{1... | collective-permute-start | bytes 245768 | tf_op jit(solution)/shard_map/ppermute | solution.py:400
  96.5 0.9 update.15
  98.2 1.6 %collective-permute-start.53 = (bf16[2,8,64,128]{3,2,1,0:T(8,128)(2,1)S(1)}, bf16[2,8,64,128]{3,2,1,0:T(8,128)(2,1)S(1)}, u32[]{:S(2)}, u32[]{:S(2)}) collective-permute-start(bf16[2,8,64,128]{3,2,1,0:T(8,128)(2,1)S(1)} %pad_maximum_fusion), channel_id=1, source_target_pairs={{2,0},{3,1},{0,2},{1,3},{6,4},{7,5},{4,6},{5,7},{10,8},{11,9},{8,1... | collective-permute-start | bytes 786440 | tf_op jit(solution)/shard_map/ppermute | solution.py:404
  99.8 3.3 %collective-permute-done.51.inter = bf16[5,64,128]{2,1,0:T(8,128)(2,1)S(1)} collective-permute-done((bf16[5,64,128]{2,1,0:T(8,128)(2,1)S(1)}, bf16[5,64,128]{2,1,0:T(8,128)(2,1)S(1)}, u32[]{:S(2)}, u32[]{:S(2)}) %collective-permute-start.51) | collective-permute-done | bytes 81952 | tf_op jit(solution)/shard_map/ppermute | solution.py:400
  103.2 1.5 %images.1.ready = bf16[2,64,1024]{2,1,0:T(8,128)(2,1)S(1)} custom-call(s32[11]{0:T(128)S(4)} %get-tuple-element.86.ints, s32[8,9]{1,0:T(8,128)S(4)} %get-tuple-element.87.index, f32[8,9]{1,0:T(8,128)S(4)} %get-tuple-element.88.signs, bf16[8,64,128]{2,1,0:T(8,128)(2,1)S(1)} %get-tuple-element.163.own.rest_0_.refs_4_, ...), custom_call_target="tpu_custom_call" | custom-call | flops 7247757312 | bytes 56623104 | tf_op jit(solution)/shard_map/images/pallas_call | solution.py:413
  104.7 2.3 %collective-permute-done.53.rest_1_.refs_6_ = bf16[2,8,64,128]{3,2,1,0:T(8,128)(2,1)S(1)} collective-permute-done((bf16[2,8,64,128]{3,2,1,0:T(8,128)(2,1)S(1)}, bf16[2,8,64,128]{3,2,1,0:T(8,128)(2,1)S(1)}, u32[]{:S(2)}, u32[]{:S(2)}) %collective-permute-start.53) | collective-permute-done | bytes 262176 | tf_op jit(solution)/shard_map/ppermute | solution.py:404
  107.0 1.7 %gram.1 = (bf16[272,128]{1,0:T(8,128)(2,1)S(1)}, bf16[272,128]{1,0:T(8,128)(2,1)S(1)}) custom-call(s32[11]{0:T(128)S(4)} %get-tuple-element.86.ints, s32[8,9]{1,0:T(8,128)S(4)} %get-tuple-element.87.index, f32[8,9]{1,0:T(8,128)S(4)} %get-tuple-element.88.signs, bf16[8,64,128]{2,1,0:T(8,128)(2,1)S(1)} %get-tuple-element.127.own.refs_5_, ...), custom_call_target="tpu_custom_call" | custom-call | flops 10871635968 | bytes 84934656 | tf_op jit(solution)/shard_map/gram/pallas_call | solution.py:413
  108.8 1.2 collective-permute-done.54.right
  110.1 1.3 collective-permute-start.55
  111.9 2.6 %collective-permute-done.55.right = bf16[272,128]{1,0:T(8,128)(2,1)S(1)} collective-permute-done((bf16[272,128]{1,0:T(8,128)(2,1)S(1)}, bf16[272,128]{1,0:T(8,128)(2,1)S(1)}, u32[]{:S(2)}, u32[]{:S(2)}) %collective-permute-start.55) | collective-permute-done | bytes 69664 | tf_op jit(solution)/shard_map/ppermute | solution.py:565
  114.5 1.5 %collective-permute-start.56 = (bf16[272,128]{1,0:T(8,128)(2,1)S(1)}, bf16[272,128]{1,0:T(8,128)(2,1)S(1)}, u32[]{:S(2)}, u32[]{:S(2)}) collective-permute-start(bf16[272,128]{1,0:T(8,128)(2,1)S(1)} %add.20.left), channel_id=1, source_target_pairs={{0,8},{4,12},{8,0},{12,4},{1,9},{5,13},{9,1},{13,5},{2,10},{6,14},... | collective-permute-start | bytes 208904 | tf_op jit(solution)/shard_map/ppermute | solution.py:565
  116.1 3.7 %collective-permute-done.56.right = bf16[272,128]{1,0:T(8,128)(2,1)S(1)} collective-permute-done((bf16[272,128]{1,0:T(8,128)(2,1)S(1)}, bf16[272,128]{1,0:T(8,128)(2,1)S(1)}, u32[]{:S(2)}, u32[]{:S(2)}) %collective-permute-start.56) | collective-permute-done | bytes 69664 | tf_op jit(solution)/shard_map/ppermute | solution.py:565
  119.8 1.6 %collective-permute-start.57 = (bf16[272,128]{1,0:T(8,128)(2,1)S(1)}, bf16[272,128]{1,0:T(8,128)(2,1)S(1)}, u32[]{:S(2)}, u32[]{:S(2)}) collective-permute-start(bf16[272,128]{1,0:T(8,128)(2,1)S(1)} %add.21.refs_0_), channel_id=1, source_target_pairs={{2,0},{3,1},{0,2},{1,3},{6,4},{7,5},{4,6},{5,7},{10,8},{11,9},{8,1... | collective-permute-start | bytes 208904 | tf_op jit(solution)/shard_map/ppermute | solution.py:404
  121.4 2.8 %collective-permute-done.57.refs_1_ = bf16[272,128]{1,0:T(8,128)(2,1)S(1)} collective-permute-done((bf16[272,128]{1,0:T(8,128)(2,1)S(1)}, bf16[272,128]{1,0:T(8,128)(2,1)S(1)}, u32[]{:S(2)}, u32[]{:S(2)}) %collective-permute-start.57) | collective-permute-done | bytes 69664 | tf_op jit(solution)/shard_map/ppermute | solution.py:404
  124.2 1.2 collective-permute-done.59.refs_3_
  125.5 9.8 %finish.1 = (bf16[64,2048]{1,0:T(8,128)(2,1)}, f32[64,256]{1,0:T(8,128)}) custom-call(s32[11]{0:T(128)S(4)} %get-tuple-element.86.ints, bf16[272,128]{1,0:T(8,128)(2,1)S(1)} %add.21.refs_0_, bf16[272,128]{1,0:T(8,128)(2,1)S(1)} %collective-permute-done.57.refs_1_, bf16[272,128]{1,0:T(8,128)(2,1)S(1)} %collective-permute-done.58.refs_2_, ...), custom_call_target="tpu_custom_call" | custom-call | flops 36238786560 | bytes 283115520 | tf_op jit(solution)/shard_map/finish/pallas_call | solution.py:413
  (113 shorter events, 28.1 us)
Async XLA Ops:
  2.3 4.8 %collective-permute-start = (bf16[8,64,128]{2,1,0:T(8,128)(2,1)S(1)}, bf16[8,64,128]{2,1,0:T(8,128)(2,1)S(1)}, u32[]{:S(2)}, u32[]{:S(2)}) collective-permute-start(bf16[8,64,128]{2,1,0:T(8,128)(2,1)S(1)} %get-tuple-element.90), channel_id=1, source_target_pairs={{0,1},{1,0},{2,3},{3,2},{4,5},{5,4},{6,7},{7,6},{8,9},{9,8},{10,11... | collective-permute-start | bytes 393224 | tf_op jit(solution)/shard_map/ppermute | solution.py:391
  7.2 7.5 %collective-permute-start.1 = (bf16[5,64,128]{2,1,0:T(8,128)(2,1)S(1)}, bf16[5,64,128]{2,1,0:T(8,128)(2,1)S(1)}, u32[]{:S(2)}, u32[]{:S(2)}) collective-permute-start(bf16[5,64,128]{2,1,0:T(8,128)(2,1)S(1)} %get-tuple-element.175), channel_id=1, source_target_pairs={{1,4},{4,1},{3,6},{6,3},{5,8},{8,5},{7,10},{10,7},{9,12},{12,9},{1... | collective-permute-start | bytes 245768 | tf_op jit(solution)/shard_map/ppermute | solution.py:400
  12.0 8.0 %collective-permute-start.27 = (bf16[5,64,128]{2,1,0:T(8,128)(2,1)S(1)}, bf16[5,64,128]{2,1,0:T(8,128)(2,1)S(1)}, u32[]{:S(2)}, u32[]{:S(2)}) collective-permute-start(bf16[5,64,128]{2,1,0:T(8,128)(2,1)S(1)} %get-tuple-element.173), channel_id=1, source_target_pairs={{1,4},{4,1},{3,6},{6,3},{5,8},{8,5},{7,10},{10,7},{9,12},{12,9},{1... | collective-permute-start | bytes 245768 | tf_op jit(solution)/shard_map/ppermute | solution.py:400
  12.6 7.4 %collective-permute-start.28 = (bf16[5,64,128]{2,1,0:T(8,128)(2,1)S(1)}, bf16[5,64,128]{2,1,0:T(8,128)(2,1)S(1)}, u32[]{:S(2)}, u32[]{:S(2)}) collective-permute-start(bf16[5,64,128]{2,1,0:T(8,128)(2,1)S(1)} %get-tuple-element.172), channel_id=1, source_target_pairs={{0,1},{1,0},{2,3},{3,2},{4,5},{5,4},{6,7},{7,6},{8,9},{9,8},{10,11... | collective-permute-start | bytes 245768 | tf_op jit(solution)/shard_map/ppermute | solution.py:391
  16.2 6.0 %collective-permute-start.3 = (bf16[5,64,128]{2,1,0:T(8,128)(2,1)S(1)}, bf16[5,64,128]{2,1,0:T(8,128)(2,1)S(1)}, u32[]{:S(2)}, u32[]{:S(2)}) collective-permute-start(bf16[5,64,128]{2,1,0:T(8,128)(2,1)S(1)} %get-tuple-element.95), channel_id=1, source_target_pairs={{1,4},{4,1},{3,6},{6,3},{5,8},{8,5},{7,10},{10,7},{9,12},{12,9},{1... | collective-permute-start | bytes 245768 | tf_op jit(solution)/shard_map/ppermute | solution.py:400
  21.5 5.8 %collective-permute-start.29 = (bf16[5,64,128]{2,1,0:T(8,128)(2,1)S(1)}, bf16[5,64,128]{2,1,0:T(8,128)(2,1)S(1)}, u32[]{:S(2)}, u32[]{:S(2)}) collective-permute-start(bf16[5,64,128]{2,1,0:T(8,128)(2,1)S(1)} %get-tuple-element.131), channel_id=1, source_target_pairs={{1,4},{4,1},{3,6},{6,3},{5,8},{8,5},{7,10},{10,7},{9,12},{12,9},{1... | collective-permute-start | bytes 245768 | tf_op jit(solution)/shard_map/ppermute | solution.py:400
  21.7 5.7 %collective-permute-start.30 = (bf16[5,64,128]{2,1,0:T(8,128)(2,1)S(1)}, bf16[5,64,128]{2,1,0:T(8,128)(2,1)S(1)}, u32[]{:S(2)}, u32[]{:S(2)}) collective-permute-start(bf16[5,64,128]{2,1,0:T(8,128)(2,1)S(1)} %get-tuple-element.132), channel_id=1, source_target_pairs={{0,1},{1,0},{2,3},{3,2},{4,5},{5,4},{6,7},{7,6},{8,9},{9,8},{10,11... | collective-permute-start | bytes 245768 | tf_op jit(solution)/shard_map/ppermute | solution.py:391
  23.1 6.6 %collective-permute-start.5 = (bf16[5,64,128]{2,1,0:T(8,128)(2,1)S(1)}, bf16[5,64,128]{2,1,0:T(8,128)(2,1)S(1)}, u32[]{:S(2)}, u32[]{:S(2)}) collective-permute-start(bf16[5,64,128]{2,1,0:T(8,128)(2,1)S(1)} %get-tuple-element.98), channel_id=1, source_target_pairs={{1,4},{4,1},{3,6},{6,3},{5,8},{8,5},{7,10},{10,7},{9,12},{12,9},{1... | collective-permute-start | bytes 245768 | tf_op jit(solution)/shard_map/ppermute | solution.py:400
  28.3 5.8 %collective-permute-start.31 = (bf16[5,64,128]{2,1,0:T(8,128)(2,1)S(1)}, bf16[5,64,128]{2,1,0:T(8,128)(2,1)S(1)}, u32[]{:S(2)}, u32[]{:S(2)}) collective-permute-start(bf16[5,64,128]{2,1,0:T(8,128)(2,1)S(1)} %get-tuple-element.134), channel_id=1, source_target_pairs={{1,4},{4,1},{3,6},{6,3},{5,8},{8,5},{7,10},{10,7},{9,12},{12,9},{1... | collective-permute-start | bytes 245768 | tf_op jit(solution)/shard_map/ppermute | solution.py:400
  28.9 5.1 %collective-permute-start.32 = (bf16[5,64,128]{2,1,0:T(8,128)(2,1)S(1)}, bf16[5,64,128]{2,1,0:T(8,128)(2,1)S(1)}, u32[]{:S(2)}, u32[]{:S(2)}) collective-permute-start(bf16[5,64,128]{2,1,0:T(8,128)(2,1)S(1)} %get-tuple-element.135), channel_id=1, source_target_pairs={{0,1},{1,0},{2,3},{3,2},{4,5},{5,4},{6,7},{7,6},{8,9},{9,8},{10,11... | collective-permute-start | bytes 245768 | tf_op jit(solution)/shard_map/ppermute | solution.py:391
  30.6 5.9 %collective-permute-start.7 = (bf16[5,64,128]{2,1,0:T(8,128)(2,1)S(1)}, bf16[5,64,128]{2,1,0:T(8,128)(2,1)S(1)}, u32[]{:S(2)}, u32[]{:S(2)}) collective-permute-start(bf16[5,64,128]{2,1,0:T(8,128)(2,1)S(1)} %get-tuple-element.101), channel_id=1, source_target_pairs={{1,4},{4,1},{3,6},{6,3},{5,8},{8,5},{7,10},{10,7},{9,12},{12,9},{1... | collective-permute-start | bytes 245768 | tf_op jit(solution)/shard_map/ppermute | solution.py:400
  34.9 6.0 %collective-permute-start.33 = (bf16[5,64,128]{2,1,0:T(8,128)(2,1)S(1)}, bf16[5,64,128]{2,1,0:T(8,128)(2,1)S(1)}, u32[]{:S(2)}, u32[]{:S(2)}) collective-permute-start(bf16[5,64,128]{2,1,0:T(8,128)(2,1)S(1)} %get-tuple-element.137), channel_id=1, source_target_pairs={{1,4},{4,1},{3,6},{6,3},{5,8},{8,5},{7,10},{10,7},{9,12},{12,9},{1... | collective-permute-start | bytes 245768 | tf_op jit(solution)/shard_map/ppermute | solution.py:400
  35.6 5.3 %collective-permute-start.34 = (bf16[5,64,128]{2,1,0:T(8,128)(2,1)S(1)}, bf16[5,64,128]{2,1,0:T(8,128)(2,1)S(1)}, u32[]{:S(2)}, u32[]{:S(2)}) collective-permute-start(bf16[5,64,128]{2,1,0:T(8,128)(2,1)S(1)} %get-tuple-element.138), channel_id=1, source_target_pairs={{0,1},{1,0},{2,3},{3,2},{4,5},{5,4},{6,7},{7,6},{8,9},{9,8},{10,11... | collective-permute-start | bytes 245768 | tf_op jit(solution)/shard_map/ppermute | solution.py:391
  38.0 5.8 %collective-permute-start.9 = (bf16[5,64,128]{2,1,0:T(8,128)(2,1)S(1)}, bf16[5,64,128]{2,1,0:T(8,128)(2,1)S(1)}, u32[]{:S(2)}, u32[]{:S(2)}) collective-permute-start(bf16[5,64,128]{2,1,0:T(8,128)(2,1)S(1)} %get-tuple-element.104), channel_id=1, source_target_pairs={{1,4},{4,1},{3,6},{6,3},{5,8},{8,5},{7,10},{10,7},{9,12},{12,9},{1... | collective-permute-start | bytes 245768 | tf_op jit(solution)/shard_map/ppermute | solution.py:400
  42.4 5.8 %collective-permute-start.35 = (bf16[5,64,128]{2,1,0:T(8,128)(2,1)S(1)}, bf16[5,64,128]{2,1,0:T(8,128)(2,1)S(1)}, u32[]{:S(2)}, u32[]{:S(2)}) collective-permute-start(bf16[5,64,128]{2,1,0:T(8,128)(2,1)S(1)} %get-tuple-element.140), channel_id=1, source_target_pairs={{1,4},{4,1},{3,6},{6,3},{5,8},{8,5},{7,10},{10,7},{9,12},{12,9},{1... | collective-permute-start | bytes 245768 | tf_op jit(solution)/shard_map/ppermute | solution.py:400
  43.2 4.9 %collective-permute-start.36 = (bf16[5,64,128]{2,1,0:T(8,128)(2,1)S(1)}, bf16[5,64,128]{2,1,0:T(8,128)(2,1)S(1)}, u32[]{:S(2)}, u32[]{:S(2)}) collective-permute-start(bf16[5,64,128]{2,1,0:T(8,128)(2,1)S(1)} %get-tuple-element.141), channel_id=1, source_target_pairs={{0,1},{1,0},{2,3},{3,2},{4,5},{5,4},{6,7},{7,6},{8,9},{9,8},{10,11... | collective-permute-start | bytes 245768 | tf_op jit(solution)/shard_map/ppermute | solution.py:391
  44.7 6.0 %collective-permute-start.11 = (bf16[5,64,128]{2,1,0:T(8,128)(2,1)S(1)}, bf16[5,64,128]{2,1,0:T(8,128)(2,1)S(1)}, u32[]{:S(2)}, u32[]{:S(2)}) collective-permute-start(bf16[5,64,128]{2,1,0:T(8,128)(2,1)S(1)} %get-tuple-element.107), channel_id=1, source_target_pairs={{1,4},{4,1},{3,6},{6,3},{5,8},{8,5},{7,10},{10,7},{9,12},{12,9},{1... | collective-permute-start | bytes 245768 | tf_op jit(solution)/shard_map/ppermute | solution.py:400
  47.6 3.1 %collective-permute-start.12 = (bf16[5,64,128]{2,1,0:T(8,128)(2,1)S(1)}, bf16[5,64,128]{2,1,0:T(8,128)(2,1)S(1)}, u32[]{:S(2)}, u32[]{:S(2)}) collective-permute-start(bf16[5,64,128]{2,1,0:T(8,128)(2,1)S(1)} %get-tuple-element.108), channel_id=1, source_target_pairs={{0,1},{1,0},{2,3},{3,2},{4,5},{5,4},{6,7},{7,6},{8,9},{9,8},{10,11... | collective-permute-start | bytes 245768 | tf_op jit(solution)/shard_map/ppermute | solution.py:391
  49.0 5.8 %collective-permute-start.37 = (bf16[5,64,128]{2,1,0:T(8,128)(2,1)S(1)}, bf16[5,64,128]{2,1,0:T(8,128)(2,1)S(1)}, u32[]{:S(2)}, u32[]{:S(2)}) collective-permute-start(bf16[5,64,128]{2,1,0:T(8,128)(2,1)S(1)} %get-tuple-element.143), channel_id=1, source_target_pairs={{1,4},{4,1},{3,6},{6,3},{5,8},{8,5},{7,10},{10,7},{9,12},{12,9},{1... | collective-permute-start | bytes 245768 | tf_op jit(solution)/shard_map/ppermute | solution.py:400
  49.9 4.9 %collective-permute-start.38 = (bf16[5,64,128]{2,1,0:T(8,128)(2,1)S(1)}, bf16[5,64,128]{2,1,0:T(8,128)(2,1)S(1)}, u32[]{:S(2)}, u32[]{:S(2)}) collective-permute-start(bf16[5,64,128]{2,1,0:T(8,128)(2,1)S(1)} %get-tuple-element.144), channel_id=1, source_target_pairs={{0,1},{1,0},{2,3},{3,2},{4,5},{5,4},{6,7},{7,6},{8,9},{9,8},{10,11... | collective-permute-start | bytes 245768 | tf_op jit(solution)/shard_map/ppermute | solution.py:391
  51.6 5.8 %collective-permute-start.13 = (bf16[5,64,128]{2,1,0:T(8,128)(2,1)S(1)}, bf16[5,64,128]{2,1,0:T(8,128)(2,1)S(1)}, u32[]{:S(2)}, u32[]{:S(2)}) collective-permute-start(bf16[5,64,128]{2,1,0:T(8,128)(2,1)S(1)} %get-tuple-element.110), channel_id=1, source_target_pairs={{1,4},{4,1},{3,6},{6,3},{5,8},{8,5},{7,10},{10,7},{9,12},{12,9},{1... | collective-permute-start | bytes 245768 | tf_op jit(solution)/shard_map/ppermute | solution.py:400
  55.7 6.0 %collective-permute-start.39 = (bf16[5,64,128]{2,1,0:T(8,128)(2,1)S(1)}, bf16[5,64,128]{2,1,0:T(8,128)(2,1)S(1)}, u32[]{:S(2)}, u32[]{:S(2)}) collective-permute-start(bf16[5,64,128]{2,1,0:T(8,128)(2,1)S(1)} %get-tuple-element.146), channel_id=1, source_target_pairs={{1,4},{4,1},{3,6},{6,3},{5,8},{8,5},{7,10},{10,7},{9,12},{12,9},{1... | collective-permute-start | bytes 245768 | tf_op jit(solution)/shard_map/ppermute | solution.py:400
  56.6 5.2 %collective-permute-start.40 = (bf16[5,64,128]{2,1,0:T(8,128)(2,1)S(1)}, bf16[5,64,128]{2,1,0:T(8,128)(2,1)S(1)}, u32[]{:S(2)}, u32[]{:S(2)}) collective-permute-start(bf16[5,64,128]{2,1,0:T(8,128)(2,1)S(1)} %get-tuple-element.147), channel_id=1, source_target_pairs={{0,1},{1,0},{2,3},{3,2},{4,5},{5,4},{6,7},{7,6},{8,9},{9,8},{10,11... | collective-permute-start | bytes 245768 | tf_op jit(solution)/shard_map/ppermute | solution.py:391
  58.8 5.8 %collective-permute-start.15 = (bf16[5,64,128]{2,1,0:T(8,128)(2,1)S(1)}, bf16[5,64,128]{2,1,0:T(8,128)(2,1)S(1)}, u32[]{:S(2)}, u32[]{:S(2)}) collective-permute-start(bf16[5,64,128]{2,1,0:T(8,128)(2,1)S(1)} %get-tuple-element.113), channel_id=1, source_target_pairs={{1,4},{4,1},{3,6},{6,3},{5,8},{8,5},{7,10},{10,7},{9,12},{12,9},{1... | collective-permute-start | bytes 245768 | tf_op jit(solution)/shard_map/ppermute | solution.py:400
  63.2 5.8 %collective-permute-start.41 = (bf16[5,64,128]{2,1,0:T(8,128)(2,1)S(1)}, bf16[5,64,128]{2,1,0:T(8,128)(2,1)S(1)}, u32[]{:S(2)}, u32[]{:S(2)}) collective-permute-start(bf16[5,64,128]{2,1,0:T(8,128)(2,1)S(1)} %get-tuple-element.149), channel_id=1, source_target_pairs={{1,4},{4,1},{3,6},{6,3},{5,8},{8,5},{7,10},{10,7},{9,12},{12,9},{1... | collective-permute-start | bytes 245768 | tf_op jit(solution)/shard_map/ppermute | solution.py:400
  64.0 5.0 %collective-permute-start.42 = (bf16[5,64,128]{2,1,0:T(8,128)(2,1)S(1)}, bf16[5,64,128]{2,1,0:T(8,128)(2,1)S(1)}, u32[]{:S(2)}, u32[]{:S(2)}) collective-permute-start(bf16[5,64,128]{2,1,0:T(8,128)(2,1)S(1)} %get-tuple-element.150), channel_id=1, source_target_pairs={{0,1},{1,0},{2,3},{3,2},{4,5},{5,4},{6,7},{7,6},{8,9},{9,8},{10,11... | collective-permute-start | bytes 245768 | tf_op jit(solution)/shard_map/ppermute | solution.py:391
  65.5 6.1 %collective-permute-start.17 = (bf16[5,64,128]{2,1,0:T(8,128)(2,1)S(1)}, bf16[5,64,128]{2,1,0:T(8,128)(2,1)S(1)}, u32[]{:S(2)}, u32[]{:S(2)}) collective-permute-start(bf16[5,64,128]{2,1,0:T(8,128)(2,1)S(1)} %get-tuple-element.116), channel_id=1, source_target_pairs={{1,4},{4,1},{3,6},{6,3},{5,8},{8,5},{7,10},{10,7},{9,12},{12,9},{1... | collective-permute-start | bytes 245768 | tf_op jit(solution)/shard_map/ppermute | solution.py:400
  69.9 5.8 %collective-permute-start.43 = (bf16[5,64,128]{2,1,0:T(8,128)(2,1)S(1)}, bf16[5,64,128]{2,1,0:T(8,128)(2,1)S(1)}, u32[]{:S(2)}, u32[]{:S(2)}) collective-permute-start(bf16[5,64,128]{2,1,0:T(8,128)(2,1)S(1)} %get-tuple-element.152), channel_id=1, source_target_pairs={{1,4},{4,1},{3,6},{6,3},{5,8},{8,5},{7,10},{10,7},{9,12},{12,9},{1... | collective-permute-start | bytes 245768 | tf_op jit(solution)/shard_map/ppermute | solution.py:400
  70.7 5.0 %collective-permute-start.44 = (bf16[5,64,128]{2,1,0:T(8,128)(2,1)S(1)}, bf16[5,64,128]{2,1,0:T(8,128)(2,1)S(1)}, u32[]{:S(2)}, u32[]{:S(2)}) collective-permute-start(bf16[5,64,128]{2,1,0:T(8,128)(2,1)S(1)} %get-tuple-element.153), channel_id=1, source_target_pairs={{0,1},{1,0},{2,3},{3,2},{4,5},{5,4},{6,7},{7,6},{8,9},{9,8},{10,11... | collective-permute-start | bytes 245768 | tf_op jit(solution)/shard_map/ppermute | solution.py:391
  72.4 5.8 %collective-permute-start.19 = (bf16[5,64,128]{2,1,0:T(8,128)(2,1)S(1)}, bf16[5,64,128]{2,1,0:T(8,128)(2,1)S(1)}, u32[]{:S(2)}, u32[]{:S(2)}) collective-permute-start(bf16[5,64,128]{2,1,0:T(8,128)(2,1)S(1)} %get-tuple-element.119), channel_id=1, source_target_pairs={{1,4},{4,1},{3,6},{6,3},{5,8},{8,5},{7,10},{10,7},{9,12},{12,9},{1... | collective-permute-start | bytes 245768 | tf_op jit(solution)/shard_map/ppermute | solution.py:400
  76.6 6.0 %collective-permute-start.45 = (bf16[5,64,128]{2,1,0:T(8,128)(2,1)S(1)}, bf16[5,64,128]{2,1,0:T(8,128)(2,1)S(1)}, u32[]{:S(2)}, u32[]{:S(2)}) collective-permute-start(bf16[5,64,128]{2,1,0:T(8,128)(2,1)S(1)} %get-tuple-element.155), channel_id=1, source_target_pairs={{1,4},{4,1},{3,6},{6,3},{5,8},{8,5},{7,10},{10,7},{9,12},{12,9},{1... | collective-permute-start | bytes 245768 | tf_op jit(solution)/shard_map/ppermute | solution.py:400
  77.4 5.3 %collective-permute-start.46 = (bf16[5,64,128]{2,1,0:T(8,128)(2,1)S(1)}, bf16[5,64,128]{2,1,0:T(8,128)(2,1)S(1)}, u32[]{:S(2)}, u32[]{:S(2)}) collective-permute-start(bf16[5,64,128]{2,1,0:T(8,128)(2,1)S(1)} %get-tuple-element.156), channel_id=1, source_target_pairs={{0,1},{1,0},{2,3},{3,2},{4,5},{5,4},{6,7},{7,6},{8,9},{9,8},{10,11... | collective-permute-start | bytes 245768 | tf_op jit(solution)/shard_map/ppermute | solution.py:391
  79.7 5.8 %collective-permute-start.21 = (bf16[5,64,128]{2,1,0:T(8,128)(2,1)S(1)}, bf16[5,64,128]{2,1,0:T(8,128)(2,1)S(1)}, u32[]{:S(2)}, u32[]{:S(2)}) collective-permute-start(bf16[5,64,128]{2,1,0:T(8,128)(2,1)S(1)} %get-tuple-element.122), channel_id=1, source_target_pairs={{1,4},{4,1},{3,6},{6,3},{5,8},{8,5},{7,10},{10,7},{9,12},{12,9},{1... | collective-permute-start | bytes 245768 | tf_op jit(solution)/shard_map/ppermute | solution.py:400
  84.1 5.8 %collective-permute-start.47 = (bf16[5,64,128]{2,1,0:T(8,128)(2,1)S(1)}, bf16[5,64,128]{2,1,0:T(8,128)(2,1)S(1)}, u32[]{:S(2)}, u32[]{:S(2)}) collective-permute-start(bf16[5,64,128]{2,1,0:T(8,128)(2,1)S(1)} %get-tuple-element.158), channel_id=1, source_target_pairs={{1,4},{4,1},{3,6},{6,3},{5,8},{8,5},{7,10},{10,7},{9,12},{12,9},{1... | collective-permute-start | bytes 245768 | tf_op jit(solution)/shard_map/ppermute | solution.py:400
  84.9 5.0 %collective-permute-start.48 = (bf16[5,64,128]{2,1,0:T(8,128)(2,1)S(1)}, bf16[5,64,128]{2,1,0:T(8,128)(2,1)S(1)}, u32[]{:S(2)}, u32[]{:S(2)}) collective-permute-start(bf16[5,64,128]{2,1,0:T(8,128)(2,1)S(1)} %get-tuple-element.159), channel_id=1, source_target_pairs={{0,1},{1,0},{2,3},{3,2},{4,5},{5,4},{6,7},{7,6},{8,9},{9,8},{10,11... | collective-permute-start | bytes 245768 | tf_op jit(solution)/shard_map/ppermute | solution.py:391
  86.3 6.1 %collective-permute-start.23 = (bf16[5,64,128]{2,1,0:T(8,128)(2,1)S(1)}, bf16[5,64,128]{2,1,0:T(8,128)(2,1)S(1)}, u32[]{:S(2)}, u32[]{:S(2)}) collective-permute-start(bf16[5,64,128]{2,1,0:T(8,128)(2,1)S(1)} %get-tuple-element.125), channel_id=1, source_target_pairs={{1,4},{4,1},{3,6},{6,3},{5,8},{8,5},{7,10},{10,7},{9,12},{12,9},{1... | collective-permute-start | bytes 245768 | tf_op jit(solution)/shard_map/ppermute | solution.py:400
  90.8 5.7 %collective-permute-start.49 = (bf16[5,64,128]{2,1,0:T(8,128)(2,1)S(1)}, bf16[5,64,128]{2,1,0:T(8,128)(2,1)S(1)}, u32[]{:S(2)}, u32[]{:S(2)}) collective-permute-start(bf16[5,64,128]{2,1,0:T(8,128)(2,1)S(1)} %get-tuple-element.161), channel_id=1, source_target_pairs={{1,4},{4,1},{3,6},{6,3},{5,8},{8,5},{7,10},{10,7},{9,12},{12,9},{1... | collective-permute-start | bytes 245768 | tf_op jit(solution)/shard_map/ppermute | solution.py:400
  91.5 5.0 %collective-permute-start.50 = (bf16[5,64,128]{2,1,0:T(8,128)(2,1)S(1)}, bf16[5,64,128]{2,1,0:T(8,128)(2,1)S(1)}, u32[]{:S(2)}, u32[]{:S(2)}) collective-permute-start(bf16[5,64,128]{2,1,0:T(8,128)(2,1)S(1)} %get-tuple-element.162), channel_id=1, source_target_pairs={{0,1},{1,0},{2,3},{3,2},{4,5},{5,4},{6,7},{7,6},{8,9},{9,8},{10,11... | collective-permute-start | bytes 245768 | tf_op jit(solution)/shard_map/ppermute | solution.py:391
  93.5 11.1 %collective-permute-start.25 = (bf16[5,64,128]{2,1,0:T(8,128)(2,1)S(1)}, bf16[5,64,128]{2,1,0:T(8,128)(2,1)S(1)}, u32[]{:S(2)}, u32[]{:S(2)}) collective-permute-start(bf16[5,64,128]{2,1,0:T(8,128)(2,1)S(1)} %get-tuple-element.128), channel_id=1, source_target_pairs={{1,4},{4,1},{3,6},{6,3},{5,8},{8,5},{7,10},{10,7},{9,12},{12,9},{1... | collective-permute-start | bytes 245768 | tf_op jit(solution)/shard_map/ppermute | solution.py:400
  96.3 8.3 %collective-permute-start.26 = (bf16[5,64,128]{2,1,0:T(8,128)(2,1)S(1)}, bf16[5,64,128]{2,1,0:T(8,128)(2,1)S(1)}, u32[]{:S(2)}, u32[]{:S(2)}) collective-permute-start(bf16[5,64,128]{2,1,0:T(8,128)(2,1)S(1)} %get-tuple-element.129), channel_id=1, source_target_pairs={{0,1},{1,0},{2,3},{3,2},{4,5},{5,4},{6,7},{7,6},{8,9},{9,8},{10,11... | collective-permute-start | bytes 245768 | tf_op jit(solution)/shard_map/ppermute | solution.py:391
  97.4 5.7 %collective-permute-start.51 = (bf16[5,64,128]{2,1,0:T(8,128)(2,1)S(1)}, bf16[5,64,128]{2,1,0:T(8,128)(2,1)S(1)}, u32[]{:S(2)}, u32[]{:S(2)}) collective-permute-start(bf16[5,64,128]{2,1,0:T(8,128)(2,1)S(1)} %get-tuple-element.164), channel_id=1, source_target_pairs={{1,4},{4,1},{3,6},{6,3},{5,8},{8,5},{7,10},{10,7},{9,12},{12,9},{1... | collective-permute-start | bytes 245768 | tf_op jit(solution)/shard_map/ppermute | solution.py:400
  98.2 5.0 %collective-permute-start.52 = (bf16[5,64,128]{2,1,0:T(8,128)(2,1)S(1)}, bf16[5,64,128]{2,1,0:T(8,128)(2,1)S(1)}, u32[]{:S(2)}, u32[]{:S(2)}) collective-permute-start(bf16[5,64,128]{2,1,0:T(8,128)(2,1)S(1)} %get-tuple-element.165), channel_id=1, source_target_pairs={{0,1},{1,0},{2,3},{3,2},{4,5},{5,4},{6,7},{7,6},{8,9},{9,8},{10,11... | collective-permute-start | bytes 245768 | tf_op jit(solution)/shard_map/ppermute | solution.py:391
  98.2 8.8 %collective-permute-start.53 = (bf16[2,8,64,128]{3,2,1,0:T(8,128)(2,1)S(1)}, bf16[2,8,64,128]{3,2,1,0:T(8,128)(2,1)S(1)}, u32[]{:S(2)}, u32[]{:S(2)}) collective-permute-start(bf16[2,8,64,128]{3,2,1,0:T(8,128)(2,1)S(1)} %pad_maximum_fusion), channel_id=1, source_target_pairs={{2,0},{3,1},{0,2},{1,3},{6,4},{7,5},{4,6},{5,7},{10,8},{11,9},{8,1... | collective-permute-start | bytes 786440 | tf_op jit(solution)/shard_map/ppermute | solution.py:404
  110.1 4.4 %collective-permute-start.55 = (bf16[272,128]{1,0:T(8,128)(2,1)S(1)}, bf16[272,128]{1,0:T(8,128)(2,1)S(1)}, u32[]{:S(2)}, u32[]{:S(2)}) collective-permute-start(bf16[272,128]{1,0:T(8,128)(2,1)S(1)} %add.19.left), channel_id=1, source_target_pairs={{0,4},{4,0},{8,12},{12,8},{1,5},{5,1},{9,13},{13,9},{2,6},{6,2},{1... | collective-permute-start | bytes 208904 | tf_op jit(solution)/shard_map/ppermute | solution.py:565
  111.4 12.8 %collective-permute-start.60 = (bf16[2,8,64,128]{3,2,1,0:T(8,128)(2,1)S(1)}, bf16[2,8,64,128]{3,2,1,0:T(8,128)(2,1)S(1)}, u32[]{:S(2)}, u32[]{:S(2)}) collective-permute-start(bf16[2,8,64,128]{3,2,1,0:T(8,128)(2,1)S(1)} %pad_maximum_fusion), channel_id=1, source_target_pairs={{0,1},{1,0},{2,3},{3,2},{4,5},{5,4},{6,7},{7,6},{8,9},{9,8},{10,11... | collective-permute-start | bytes 786440 | tf_op jit(solution)/shard_map/ppermute | solution.py:391
  111.4 12.8 %collective-permute-start.61 = (bf16[2,8,64,128]{3,2,1,0:T(8,128)(2,1)S(1)}, bf16[2,8,64,128]{3,2,1,0:T(8,128)(2,1)S(1)}, u32[]{:S(2)}, u32[]{:S(2)}) collective-permute-start(bf16[2,8,64,128]{3,2,1,0:T(8,128)(2,1)S(1)} %collective-permute-done.53.rest_1_.refs_6_), channel_id=1, source_target_pairs={{0,1},{1,0},{2,3},{3,2},{4,5},{5,4},{6,7},{7,6},{8,9},{9,8},{10,11... | collective-permute-start | bytes 786440 | tf_op jit(solution)/shard_map/ppermute | solution.py:391
  114.5 5.3 %collective-permute-start.56 = (bf16[272,128]{1,0:T(8,128)(2,1)S(1)}, bf16[272,128]{1,0:T(8,128)(2,1)S(1)}, u32[]{:S(2)}, u32[]{:S(2)}) collective-permute-start(bf16[272,128]{1,0:T(8,128)(2,1)S(1)} %add.20.left), channel_id=1, source_target_pairs={{0,8},{4,12},{8,0},{12,4},{1,9},{5,13},{9,1},{13,5},{2,10},{6,14},... | collective-permute-start | bytes 208904 | tf_op jit(solution)/shard_map/ppermute | solution.py:565
  119.8 4.4 %collective-permute-start.57 = (bf16[272,128]{1,0:T(8,128)(2,1)S(1)}, bf16[272,128]{1,0:T(8,128)(2,1)S(1)}, u32[]{:S(2)}, u32[]{:S(2)}) collective-permute-start(bf16[272,128]{1,0:T(8,128)(2,1)S(1)} %add.21.refs_0_), channel_id=1, source_target_pairs={{2,0},{3,1},{0,2},{1,3},{6,4},{7,5},{4,6},{5,7},{10,8},{11,9},{8,1... | collective-permute-start | bytes 208904 | tf_op jit(solution)/shard_map/ppermute | solution.py:404
  (14 other events, 37.1 us)

commit v3 on v2

--- a/solution.py
+++ b/solution.py
@@ -10,7 +10,7 @@
 HALF_BAND = 5
 DEGREE = 4
 CORES = 2
-PANEL = 64
+PANEL = 32
 SLOWER = 24
 SUBLANES = 8
 DIAGONAL_ROWS = 16
@@ -180,15 +180,15 @@
 
 
 def gram_kernel(chips, ints, index, signs, own, inter, intra, ham, ovl, ready, *rest):
-    first, *others = rest[:chips]
-    keep, send, ext, images, both = rest[chips:]
+    count = CORES * chips - 1
+    first, *others = rest[:count]
+    keep, send, ext, images, both = rest[count:]
     images_kernel(ints, index, signs, own, inter, intra, ham, ovl, images, ext)
     core, chip = ints[0], ints[1]
     half, local_vecs, _ = own.shape
     vecs = CORES * local_vecs
     groups = [[first[row] for row in range(half)], [own[row] for row in range(half)]]
-    for other in others:
-        groups += [[other[g, row] for row in range(half)] for g in range(CORES)]
+    groups += [[other[row] for row in range(half)] for other in others]
     flat = jnp.concatenate([jnp.concatenate(group, axis=1) for group in groups], axis=0)
     eye = lax.broadcasted_iota(jnp.int32, (vecs, vecs), 0) == lax.broadcasted_iota(
         jnp.int32, (vecs, vecs), 1
@@ -249,7 +249,7 @@
         return jnp.broadcast_to(value[k % SUBLANES : k % SUBLANES + 1], (SUBLANES, 128))
 
     pivots = [jnp.ones((SUBLANES, 128), F32) for _ in range(count)]
-    for start, group in ((0, 8), (8, 8), (16, 8), (24, 8), (32, 16), (48, 16)):
+    for start, group in ((0, 16), (16, 16)):
         columns = {
             k: {
                 v: jnp.broadcast_to(pieces[v][:, k : k + 1], (SUBLANES, 128))
@@ -294,12 +294,13 @@
         if start % 128:
             block = pltpu.roll(block, 128 - start % 128, axis=1)
         t_high, t_mid, t_low = split3(jnp.where(lane < PANEL, 0.0, panel_inverse(block)))
-        left = jnp.concatenate([t_high, t_mid, t_low, t_high, t_mid, t_high], axis=1)
+        first = jnp.where(lane < 2 * PANEL, t_high, jnp.where(lane < 3 * PANEL, t_mid, t_low))
+        second = jnp.where(lane < 2 * PANEL, t_high, jnp.where(lane < 3 * PANEL, t_mid, t_high))
+        left = jnp.concatenate([first, second], axis=1)
         inside = (wide >= start) & (wide < start + PANEL)
         rows = jnp.where(inside, jnp.where(wide - start == tall, 1.0, 0.0), rows)
         r_high, r_mid, r_low = split3(rows)
-        right = [part for r in (r_high, r_high, r_high, r_mid, r_mid, r_low) for part in (zero, r)]
-        right = jnp.concatenate(right, axis=0)
+        right = jnp.concatenate([zero, r_high, r_high, r_high, zero, r_mid, r_mid, r_low], axis=0)
         new = jnp.dot(left, right, preferred_element_type=F32)
         inverse[start : start + PANEL, :] = jnp.where(wide < start + PANEL, new, 0.0)
         after = start + PANEL
@@ -316,8 +317,9 @@
 
 def finish_kernel(chips, scale, ints, *refs):
     mine, theirs = refs[:chips], refs[chips : 2 * chips]
-    y_mine, y_theirs = refs[2 * chips : 3 * chips + 1], refs[3 * chips + 1 : 4 * chips + 1]
-    basis, reduced, pair, work, inverse = refs[4 * chips + 1 :]
+    y_mine = refs[2 * chips : (2 + CORES) * chips]
+    y_theirs = refs[(2 + CORES) * chips : (2 + 2 * CORES) * chips]
+    basis, reduced, pair, work, inverse = refs[(2 + 2 * CORES) * chips :]
     core, chip, col = ints[0], ints[1], ints[2]
     half, local_vecs, orbs = y_mine[0].shape
     vecs = CORES * local_vecs
@@ -353,11 +355,7 @@
             part = jnp.where(which == k, rotation[:, k * vecs : (k + 1) * vecs], part)
         turned.append(part)
     turned = jnp.concatenate(turned, axis=1)
-    mine_groups = [y_mine[0], y_mine[1]]
-    for other in y_mine[2:]:
-        mine_groups += [other.at[g] for g in range(CORES)]
-    their_groups = [other.at[g] for other in y_theirs for g in range(CORES)]
-    for which, group in ((core, mine_groups), (1 - core, their_groups)):
+    for which, group in ((core, y_mine), (1 - core, y_theirs)):
         for row in range(half):
             everything = jnp.concatenate([vectors[row] for vectors in group], axis=0)
             result = jnp.dot(turned, everything, preferred_element_type=F32).astype(BF16)
@@ -451,7 +449,7 @@
         ],
         compiler_params=params,
     )(ints, stays(block_sizes), stays(trial_vectors))
-    got = swap_cores(give)
+    got, ints = lax.optimization_barrier((swap_cores(give), ints))
     matrix = vmem((half, *hamiltonian_blocks.shape[1:]), BF16)
     ham, ovl, index, signs, place, scal = pl.pallas_call(
         functools.partial(load_kernel, total_blocks),
@@ -501,6 +499,8 @@
     halo = [exchange(ends[g]) for g in range(CORES)]
     for degree in range(DEGREE):
         for g in range(CORES):
+            if g > 0:
+                current[g], scaled[0] = lax.optimization_barrier((current[g], scaled[0]))
             scaled[g], *ends = step_call(
                 scaled_kernel,
                 "scaled",
@@ -527,8 +527,7 @@
             halo[g] = exchange(ends)
             previous[g], current[g] = current[g], updated
 
-    stacked = jnp.stack(current)
-    y_others = [from_chip(stacked, step) for step in range(1, chips)]
+    y_others = [from_chip(value, step) for step in range(1, chips) for value in current]
     image = jax.ShapeDtypeStruct((2, local_vecs, half * orbs), BF16)
     (ready,) = call(
         images_kernel,
@@ -567,7 +566,7 @@
             bit *= 2
     mine = [summed] + [from_chip(summed, step) for step in range(1, chips)]
     theirs = [swap_cores(value) for value in mine]
-    y_theirs = [swap_cores(value) for value in (stacked, *y_others)]
+    y_theirs = [swap_cores(value) for value in (*current, *y_others)]
     basis, reduced = call(
         functools.partial(finish_kernel, chips, 0.5 / (total_blocks * orbs)),
         "finish",

time: 135 us -> 133 us (0.985)
  waiting for transfers between devices: 31 us -> 27.7 us
    ppermute x26, waiting for transfers between devices: 17 us -> 12.8 us  [swap_chips(): return lax.ppermute(value, ('row', 'col'), pairs)]
    ppermute x2 -> x3, starting transfers between devices: 3.17 us -> 4.15 us  [from_chip(): return lax.ppermute(value, 'col', pairs)]
    ppermute x2 -> x3, waiting for transfers between devices: 5.12 us -> 5.53 us  [from_chip(): return lax.ppermute(value, 'col', pairs)]
  transfers between devices with their start and end apart: 62 -> 65, of which waited for: 27 -> 27; matrix products, arithmetic and copies ran while one was open for 0% -> 0% of each run, Pallas kernels for 23% -> 23%
where the time goes in v3:
time: 133 us
  starting transfers between devices  58.3 us (44%)
  Pallas kernels  44.1 us (33%)
  waiting for transfers between devices  27.7 us (21%)
  between operations  2.3 us (2%)
    ppermute x26, starting transfers between devices, swap_chips(): return lax.ppermute(value, ('row', 'col'), pairs)  49.4 us
    pallas_call x30, Pallas kernels, call(): pl.pallas_call(kernel, name=name, out_shape=outs, in_specs=[SMEM] * len(s...  39.5 us
    ppermute x26, waiting for transfers between devices, swap_chips(): return lax.ppermute(value, ('row', 'col'), pairs)  12.8 us
    ppermute x2, waiting for transfers between devices, local(): other = lax.ppermute(summed, 'row', [(r, r ^ bit) for r in range(num_rows)])  6.83 us
    ppermute x3, waiting for transfers between devices, from_chip(): return lax.ppermute(value, 'col', pairs)  5.53 us
    ppermute x3, starting transfers between devices, from_chip(): return lax.ppermute(value, 'col', pairs)  4.15 us
    pallas_call x1, Pallas kernels, local(): pl.pallas_call(functools.partial(load_kernel, total_blocks), name='load',...  3.01 us
    ppermute x2, starting transfers between devices, local(): other = lax.ppermute(summed, 'row', [(r, r ^ bit) for r in range(num_rows)])  2.82 us
  transfers between devices with their start and end apart: 65, of which 27 were waited for; matrix products, arithmetic and copies ran while one was open for 0% of the time, Pallas kernels for 23%

profile of v3, /device:TPU:0, one launch (start us, length us, event | category | flops | bytes accessed | tf_op | source)
XLA Modules:
  0.0 132.6 jit_solution(17159570123204962554)
XLA Ops:
  0.7 1.6 %cut.1 = (bf16[8,64,128]{2,1,0:T(8,128)(2,1)S(1)}, bf16[8,64,128]{2,1,0:T(8,128)(2,1)S(1)}) custom-call(s32[4]{0:T(128)S(1)} %pad_add_fusion.ints, s32[16]{0:T(128)} %sizes.3, bf16[64,2048]{1,0:T(8,128)(2,1)} %trial.1), custom_call_target="tpu_custom_call" | custom-call | tf_op jit(solution)/shard_map/cut/pallas_call | solution.py:439
  4.3 4.7 %collective-permute-start.1 = (bf16[5,64,128]{2,1,0:T(8,128)(2,1)S(1)}, bf16[5,64,128]{2,1,0:T(8,128)(2,1)S(1)}, u32[]{:S(2)}, u32[]{:S(2)}) collective-permute-start(bf16[5,64,128]{2,1,0:T(8,128)(2,1)S(1)} %get-tuple-element.195), channel_id=1, source_target_pairs={{1,4},{4,1},{3,6},{6,3},{5,8},{8,5},{7,10},{10,7},{9,12},{12,9},{1... | collective-permute-start | bytes 245768 | tf_op jit(solution)/shard_map/ppermute | solution.py:398
  9.7 3.0 %load.1 = (bf16[8,9,128,128]{3,2,1,0:T(8,128)(2,1)S(1)}, bf16[8,9,128,128]{3,2,1,0:T(8,128)(2,1)S(1)}, s32[8,9]{1,0:T(8,128)S(4)}, f32[8,9]{1,0:T(8,128)S(4)}, s32[11]{0:T(128)S(4)}, /*index=5*/f32[2]{0:T(128)S(4)}) custom-call(s32[4]{0:T(128)S(1)} %pad_add_fusion.ints, f32[1]{0:T(128)S(6)} %copy.10.shift, f32[1]{0:T(128)S(6)} %copy.11.width, ...), custom_call_target="tpu_custom_call" | custom-call | bytes 9437184 | tf_op jit(solution)/shard_map/load/pallas_call | solution.py:454
  12.7 1.5 %scaled.8 = (bf16[8,64,128]{2,1,0:T(8,128)(2,1)S(1)}, bf16[5,64,128]{2,1,0:T(8,128)(2,1)S(1)}, bf16[5,64,128]{2,1,0:T(8,128)(2,1)S(1)}) custom-call(s32[11]{0:T(128)S(4)} %get-tuple-element.98.ints, s32[8,9]{1,0:T(8,128)S(4)} %get-tuple-element.99.index, f32[8,9]{1,0:T(8,128)S(4)} %get-tuple-element.100.signs, f32[2]{0:T(128)S(4)} %get-tuple-element.101.scal, ...), custom_call_target="tpu_custom_call" | custom-call | flops 7247757312 | bytes 56623104 | tf_op jit(solution)/shard_map/scaled/pallas_call | solution.py:411
  14.2 3.1 %collective-permute-start.9 = (bf16[5,64,128]{2,1,0:T(8,128)(2,1)S(1)}, bf16[5,64,128]{2,1,0:T(8,128)(2,1)S(1)}, u32[]{:S(2)}, u32[]{:S(2)}) collective-permute-start(bf16[5,64,128]{2,1,0:T(8,128)(2,1)S(1)} %get-tuple-element.116), channel_id=1, source_target_pairs={{1,4},{4,1},{3,6},{6,3},{5,8},{8,5},{7,10},{10,7},{9,12},{12,9},{1... | collective-permute-start | bytes 245768 | tf_op jit(solution)/shard_map/ppermute | solution.py:398
  17.4 1.5 %scaled.9 = (bf16[8,64,128]{2,1,0:T(8,128)(2,1)S(1)}, bf16[5,64,128]{2,1,0:T(8,128)(2,1)S(1)}, bf16[5,64,128]{2,1,0:T(8,128)(2,1)S(1)}) custom-call(s32[11]{0:T(128)S(4)} %get-tuple-element.98.ints, s32[8,9]{1,0:T(8,128)S(4)} %get-tuple-element.99.index, f32[8,9]{1,0:T(8,128)S(4)} %get-tuple-element.100.signs, f32[2]{0:T(128)S(4)} %get-tuple-element.101.scal, ...), custom_call_target="tpu_custom_call" | custom-call | flops 7247757312 | bytes 56623104 | tf_op jit(solution)/shard_map/scaled/pallas_call | solution.py:411
  20.9 3.3 %collective-permute-start.11 = (bf16[5,64,128]{2,1,0:T(8,128)(2,1)S(1)}, bf16[5,64,128]{2,1,0:T(8,128)(2,1)S(1)}, u32[]{:S(2)}, u32[]{:S(2)}) collective-permute-start(bf16[5,64,128]{2,1,0:T(8,128)(2,1)S(1)} %get-tuple-element.119), channel_id=1, source_target_pairs={{1,4},{4,1},{3,6},{6,3},{5,8},{8,5},{7,10},{10,7},{9,12},{12,9},{1... | collective-permute-start | bytes 245768 | tf_op jit(solution)/shard_map/ppermute | solution.py:398
  28.0 2.9 %collective-permute-start.13 = (bf16[5,64,128]{2,1,0:T(8,128)(2,1)S(1)}, bf16[5,64,128]{2,1,0:T(8,128)(2,1)S(1)}, u32[]{:S(2)}, u32[]{:S(2)}) collective-permute-start(bf16[5,64,128]{2,1,0:T(8,128)(2,1)S(1)} %get-tuple-element.122), channel_id=1, source_target_pairs={{1,4},{4,1},{3,6},{6,3},{5,8},{8,5},{7,10},{10,7},{9,12},{12,9},{1... | collective-permute-start | bytes 245768 | tf_op jit(solution)/shard_map/ppermute | solution.py:398
  31.3 0.9 update.8
  33.8 1.5 %scaled.10 = (bf16[8,64,128]{2,1,0:T(8,128)(2,1)S(1)}, bf16[5,64,128]{2,1,0:T(8,128)(2,1)S(1)}, bf16[5,64,128]{2,1,0:T(8,128)(2,1)S(1)}) custom-call(s32[11]{0:T(128)S(4)} %get-tuple-element.98.ints, s32[8,9]{1,0:T(8,128)S(4)} %get-tuple-element.99.index, f32[8,9]{1,0:T(8,128)S(4)} %get-tuple-element.100.signs, f32[2]{0:T(128)S(4)} %get-tuple-element.101.scal, ...), custom_call_target="tpu_custom_call" | custom-call | flops 7247757312 | bytes 56623104 | tf_op jit(solution)/shard_map/scaled/pallas_call | solution.py:411
  35.3 3.0 %collective-permute-start.21 = (bf16[5,64,128]{2,1,0:T(8,128)(2,1)S(1)}, bf16[5,64,128]{2,1,0:T(8,128)(2,1)S(1)}, u32[]{:S(2)}, u32[]{:S(2)}) collective-permute-start(bf16[5,64,128]{2,1,0:T(8,128)(2,1)S(1)} %get-tuple-element.136), channel_id=1, source_target_pairs={{1,4},{4,1},{3,6},{6,3},{5,8},{8,5},{7,10},{10,7},{9,12},{12,9},{1... | collective-permute-start | bytes 245768 | tf_op jit(solution)/shard_map/ppermute | solution.py:398
  38.4 1.5 %scaled.11 = (bf16[8,64,128]{2,1,0:T(8,128)(2,1)S(1)}, bf16[5,64,128]{2,1,0:T(8,128)(2,1)S(1)}, bf16[5,64,128]{2,1,0:T(8,128)(2,1)S(1)}) custom-call(s32[11]{0:T(128)S(4)} %get-tuple-element.98.ints, s32[8,9]{1,0:T(8,128)S(4)} %get-tuple-element.99.index, f32[8,9]{1,0:T(8,128)S(4)} %get-tuple-element.100.signs, f32[2]{0:T(128)S(4)} %get-tuple-element.101.scal, ...), custom_call_target="tpu_custom_call" | custom-call | flops 7247757312 | bytes 56623104 | tf_op jit(solution)/shard_map/scaled/pallas_call | solution.py:411
  41.1 0.9 term.11
  42.0 3.1 %collective-permute-start.23 = (bf16[5,64,128]{2,1,0:T(8,128)(2,1)S(1)}, bf16[5,64,128]{2,1,0:T(8,128)(2,1)S(1)}, u32[]{:S(2)}, u32[]{:S(2)}) collective-permute-start(bf16[5,64,128]{2,1,0:T(8,128)(2,1)S(1)} %get-tuple-element.139), channel_id=1, source_target_pairs={{1,4},{4,1},{3,6},{6,3},{5,8},{8,5},{7,10},{10,7},{9,12},{12,9},{1... | collective-permute-start | bytes 245768 | tf_op jit(solution)/shard_map/ppermute | solution.py:398
  47.3 0.9 collective-permute-done.23.inter
  48.1 0.9 update.11
  49.0 2.8 %collective-permute-start.25 = (bf16[5,64,128]{2,1,0:T(8,128)(2,1)S(1)}, bf16[5,64,128]{2,1,0:T(8,128)(2,1)S(1)}, u32[]{:S(2)}, u32[]{:S(2)}) collective-permute-start(bf16[5,64,128]{2,1,0:T(8,128)(2,1)S(1)} %get-tuple-element.142), channel_id=1, source_target_pairs={{1,4},{4,1},{3,6},{6,3},{5,8},{8,5},{7,10},{10,7},{9,12},{12,9},{1... | collective-permute-start | bytes 245768 | tf_op jit(solution)/shard_map/ppermute | solution.py:398
  52.3 1.1 update.10
  54.8 1.5 %scaled.12 = (bf16[8,64,128]{2,1,0:T(8,128)(2,1)S(1)}, bf16[5,64,128]{2,1,0:T(8,128)(2,1)S(1)}, bf16[5,64,128]{2,1,0:T(8,128)(2,1)S(1)}) custom-call(s32[11]{0:T(128)S(4)} %get-tuple-element.98.ints, s32[8,9]{1,0:T(8,128)S(4)} %get-tuple-element.99.index, f32[8,9]{1,0:T(8,128)S(4)} %get-tuple-element.100.signs, f32[2]{0:T(128)S(4)} %get-tuple-element.101.scal, ...), custom_call_target="tpu_custom_call" | custom-call | flops 7247757312 | bytes 56623104 | tf_op jit(solution)/shard_map/scaled/pallas_call | solution.py:411
  56.3 2.9 %collective-permute-start.33 = (bf16[5,64,128]{2,1,0:T(8,128)(2,1)S(1)}, bf16[5,64,128]{2,1,0:T(8,128)(2,1)S(1)}, u32[]{:S(2)}, u32[]{:S(2)}) collective-permute-start(bf16[5,64,128]{2,1,0:T(8,128)(2,1)S(1)} %get-tuple-element.156), channel_id=1, source_target_pairs={{1,4},{4,1},{3,6},{6,3},{5,8},{8,5},{7,10},{10,7},{9,12},{12,9},{1... | collective-permute-start | bytes 245768 | tf_op jit(solution)/shard_map/ppermute | solution.py:398
  59.2 1.5 %scaled.13 = (bf16[8,64,128]{2,1,0:T(8,128)(2,1)S(1)}, bf16[5,64,128]{2,1,0:T(8,128)(2,1)S(1)}, bf16[5,64,128]{2,1,0:T(8,128)(2,1)S(1)}) custom-call(s32[11]{0:T(128)S(4)} %get-tuple-element.98.ints, s32[8,9]{1,0:T(8,128)S(4)} %get-tuple-element.99.index, f32[8,9]{1,0:T(8,128)S(4)} %get-tuple-element.100.signs, f32[2]{0:T(128)S(4)} %get-tuple-element.101.scal, ...), custom_call_target="tpu_custom_call" | custom-call | flops 7247757312 | bytes 56623104 | tf_op jit(solution)/shard_map/scaled/pallas_call | solution.py:411
  63.2 2.7 %collective-permute-start.35 = (bf16[5,64,128]{2,1,0:T(8,128)(2,1)S(1)}, bf16[5,64,128]{2,1,0:T(8,128)(2,1)S(1)}, u32[]{:S(2)}, u32[]{:S(2)}) collective-permute-start(bf16[5,64,128]{2,1,0:T(8,128)(2,1)S(1)} %get-tuple-element.159), channel_id=1, source_target_pairs={{1,4},{4,1},{3,6},{6,3},{5,8},{8,5},{7,10},{10,7},{9,12},{12,9},{1... | collective-permute-start | bytes 245768 | tf_op jit(solution)/shard_map/ppermute | solution.py:398
  69.0 0.9 update.13
  69.9 2.8 %collective-permute-start.37 = (bf16[5,64,128]{2,1,0:T(8,128)(2,1)S(1)}, bf16[5,64,128]{2,1,0:T(8,128)(2,1)S(1)}, u32[]{:S(2)}, u32[]{:S(2)}) collective-permute-start(bf16[5,64,128]{2,1,0:T(8,128)(2,1)S(1)} %get-tuple-element.162), channel_id=1, source_target_pairs={{1,4},{4,1},{3,6},{6,3},{5,8},{8,5},{7,10},{10,7},{9,12},{12,9},{1... | collective-permute-start | bytes 245768 | tf_op jit(solution)/shard_map/ppermute | solution.py:398
  73.2 0.9 update.12
  75.7 1.5 %scaled.14 = (bf16[8,64,128]{2,1,0:T(8,128)(2,1)S(1)}, bf16[5,64,128]{2,1,0:T(8,128)(2,1)S(1)}, bf16[5,64,128]{2,1,0:T(8,128)(2,1)S(1)}) custom-call(s32[11]{0:T(128)S(4)} %get-tuple-element.98.ints, s32[8,9]{1,0:T(8,128)S(4)} %get-tuple-element.99.index, f32[8,9]{1,0:T(8,128)S(4)} %get-tuple-element.100.signs, f32[2]{0:T(128)S(4)} %get-tuple-element.101.scal, ...), custom_call_target="tpu_custom_call" | custom-call | flops 7247757312 | bytes 56623104 | tf_op jit(solution)/shard_map/scaled/pallas_call | solution.py:411
  77.2 2.9 %collective-permute-start.47 = (bf16[5,64,128]{2,1,0:T(8,128)(2,1)S(1)}, bf16[5,64,128]{2,1,0:T(8,128)(2,1)S(1)}, u32[]{:S(2)}, u32[]{:S(2)}) collective-permute-start(bf16[5,64,128]{2,1,0:T(8,128)(2,1)S(1)} %get-tuple-element.178), channel_id=1, source_target_pairs={{1,4},{4,1},{3,6},{6,3},{5,8},{8,5},{7,10},{10,7},{9,12},{12,9},{1... | collective-permute-start | bytes 245768 | tf_op jit(solution)/shard_map/ppermute | solution.py:398
  80.1 1.5 %scaled.15 = (bf16[8,64,128]{2,1,0:T(8,128)(2,1)S(1)}, bf16[5,64,128]{2,1,0:T(8,128)(2,1)S(1)}, bf16[5,64,128]{2,1,0:T(8,128)(2,1)S(1)}) custom-call(s32[11]{0:T(128)S(4)} %get-tuple-element.98.ints, s32[8,9]{1,0:T(8,128)S(4)} %get-tuple-element.99.index, f32[8,9]{1,0:T(8,128)S(4)} %get-tuple-element.100.signs, f32[2]{0:T(128)S(4)} %get-tuple-element.101.scal, ...), custom_call_target="tpu_custom_call" | custom-call | flops 7247757312 | bytes 56623104 | tf_op jit(solution)/shard_map/scaled/pallas_call | solution.py:411
  83.8 3.0 %collective-permute-start.49 = (bf16[5,64,128]{2,1,0:T(8,128)(2,1)S(1)}, bf16[5,64,128]{2,1,0:T(8,128)(2,1)S(1)}, u32[]{:S(2)}, u32[]{:S(2)}) collective-permute-start(bf16[5,64,128]{2,1,0:T(8,128)(2,1)S(1)} %get-tuple-element.181), channel_id=1, source_target_pairs={{1,4},{4,1},{3,6},{6,3},{5,8},{8,5},{7,10},{10,7},{9,12},{12,9},{1... | collective-permute-start | bytes 245768 | tf_op jit(solution)/shard_map/ppermute | solution.py:398
  87.4 0.9 term.14
  89.9 1.1 update.15
  91.0 2.8 %collective-permute-start.51 = (bf16[5,64,128]{2,1,0:T(8,128)(2,1)S(1)}, bf16[5,64,128]{2,1,0:T(8,128)(2,1)S(1)}, u32[]{:S(2)}, u32[]{:S(2)}) collective-permute-start(bf16[5,64,128]{2,1,0:T(8,128)(2,1)S(1)} %get-tuple-element.184), channel_id=1, source_target_pairs={{1,4},{4,1},{3,6},{6,3},{5,8},{8,5},{7,10},{10,7},{9,12},{12,9},{1... | collective-permute-start | bytes 245768 | tf_op jit(solution)/shard_map/ppermute | solution.py:398
  94.0 0.9 update.14
  95.7 1.5 %collective-permute-start.53 = (bf16[8,64,128]{2,1,0:T(8,128)(2,1)S(1)}, bf16[8,64,128]{2,1,0:T(8,128)(2,1)S(1)}, u32[]{:S(2)}, u32[]{:S(2)}) collective-permute-start(bf16[8,64,128]{2,1,0:T(8,128)(2,1)S(1)} %get-tuple-element.183.own.rest_0_.refs_4_), channel_id=1, source_target_pairs={{2,0},{3,1},{0,2},{1,3},{6,4},{7,5},{4,6},{5,7},{10,8},{11,9},{8,1... | collective-permute-start | bytes 393224 | tf_op jit(solution)/shard_map/ppermute | solution.py:402
  97.2 1.1 collective-permute-start.54
  98.3 1.5 %images.1.ready = bf16[2,64,1024]{2,1,0:T(8,128)(2,1)S(1)} custom-call(s32[11]{0:T(128)S(4)} %get-tuple-element.98.ints, s32[8,9]{1,0:T(8,128)S(4)} %get-tuple-element.99.index, f32[8,9]{1,0:T(8,128)S(4)} %get-tuple-element.100.signs, bf16[8,64,128]{2,1,0:T(8,128)(2,1)S(1)} %get-tuple-element.183.own.rest_0_.refs_4_, ...), custom_call_target="tpu_custom_call" | custom-call | flops 7247757312 | bytes 56623104 | tf_op jit(solution)/shard_map/images/pallas_call | solution.py:411
  100.6 1.3 %collective-permute-done.53.rest_1_.refs_6_ = bf16[8,64,128]{2,1,0:T(8,128)(2,1)S(1)} collective-permute-done((bf16[8,64,128]{2,1,0:T(8,128)(2,1)S(1)}, bf16[8,64,128]{2,1,0:T(8,128)(2,1)S(1)}, u32[]{:S(2)}, u32[]{:S(2)}) %collective-permute-start.53) | collective-permute-done | bytes 131104 | tf_op jit(solution)/shard_map/ppermute | solution.py:402
  102.0 2.4 %collective-permute-done.54.rest_2_.refs_7_ = bf16[8,64,128]{2,1,0:T(8,128)(2,1)S(1)} collective-permute-done((bf16[8,64,128]{2,1,0:T(8,128)(2,1)S(1)}, bf16[8,64,128]{2,1,0:T(8,128)(2,1)S(1)}, u32[]{:S(2)}, u32[]{:S(2)}) %collective-permute-start.54) | collective-permute-done | bytes 131104 | tf_op jit(solution)/shard_map/ppermute | solution.py:402
  104.4 1.7 %gram.1 = (bf16[272,128]{1,0:T(8,128)(2,1)S(1)}, bf16[272,128]{1,0:T(8,128)(2,1)S(1)}) custom-call(s32[11]{0:T(128)S(4)} %get-tuple-element.98.ints, s32[8,9]{1,0:T(8,128)S(4)} %get-tuple-element.99.index, f32[8,9]{1,0:T(8,128)S(4)} %get-tuple-element.100.signs, bf16[8,64,128]{2,1,0:T(8,128)(2,1)S(1)} %get-tuple-element.174.own.refs_5_, ...), custom_call_target="tpu_custom_call" | custom-call | flops 10871635968 | bytes 84934656 | tf_op jit(solution)/shard_map/gram/pallas_call | solution.py:411
  106.2 1.2 collective-permute-done.55.right
  107.5 1.3 collective-permute-start.56
  108.8 3.1 %collective-permute-done.56.right = bf16[272,128]{1,0:T(8,128)(2,1)S(1)} collective-permute-done((bf16[272,128]{1,0:T(8,128)(2,1)S(1)}, bf16[272,128]{1,0:T(8,128)(2,1)S(1)}, u32[]{:S(2)}, u32[]{:S(2)}) %collective-permute-start.56) | collective-permute-done | bytes 69664 | tf_op jit(solution)/shard_map/ppermute | solution.py:564
  111.9 1.5 %collective-permute-start.57 = (bf16[272,128]{1,0:T(8,128)(2,1)S(1)}, bf16[272,128]{1,0:T(8,128)(2,1)S(1)}, u32[]{:S(2)}, u32[]{:S(2)}) collective-permute-start(bf16[272,128]{1,0:T(8,128)(2,1)S(1)} %add.20.left), channel_id=1, source_target_pairs={{0,8},{4,12},{8,0},{12,4},{1,9},{5,13},{9,1},{13,5},{2,10},{6,14},... | collective-permute-start | bytes 208904 | tf_op jit(solution)/shard_map/ppermute | solution.py:564
  113.5 3.7 %collective-permute-done.57.right = bf16[272,128]{1,0:T(8,128)(2,1)S(1)} collective-permute-done((bf16[272,128]{1,0:T(8,128)(2,1)S(1)}, bf16[272,128]{1,0:T(8,128)(2,1)S(1)}, u32[]{:S(2)}, u32[]{:S(2)}) %collective-permute-start.57) | collective-permute-done | bytes 69664 | tf_op jit(solution)/shard_map/ppermute | solution.py:564
  117.2 1.6 %collective-permute-start.58 = (bf16[272,128]{1,0:T(8,128)(2,1)S(1)}, bf16[272,128]{1,0:T(8,128)(2,1)S(1)}, u32[]{:S(2)}, u32[]{:S(2)}) collective-permute-start(bf16[272,128]{1,0:T(8,128)(2,1)S(1)} %add.21.refs_0_), channel_id=1, source_target_pairs={{2,0},{3,1},{0,2},{1,3},{6,4},{7,5},{4,6},{5,7},{10,8},{11,9},{8,1... | collective-permute-start | bytes 208904 | tf_op jit(solution)/shard_map/ppermute | solution.py:402
  119.8 1.8 %collective-permute-done.58.refs_1_ = bf16[272,128]{1,0:T(8,128)(2,1)S(1)} collective-permute-done((bf16[272,128]{1,0:T(8,128)(2,1)S(1)}, bf16[272,128]{1,0:T(8,128)(2,1)S(1)}, u32[]{:S(2)}, u32[]{:S(2)}) %collective-permute-start.58) | collective-permute-done | bytes 69664 | tf_op jit(solution)/shard_map/ppermute | solution.py:402
  121.6 1.2 collective-permute-done.60.refs_3_
  122.9 9.7 %finish.1 = (bf16[64,2048]{1,0:T(8,128)(2,1)}, f32[64,256]{1,0:T(8,128)}) custom-call(s32[11]{0:T(128)S(4)} %get-tuple-element.98.ints, bf16[272,128]{1,0:T(8,128)(2,1)S(1)} %add.21.refs_0_, bf16[272,128]{1,0:T(8,128)(2,1)S(1)} %collective-permute-done.58.refs_1_, bf16[272,128]{1,0:T(8,128)(2,1)S(1)} %collective-permute-done.59.refs_2_, ...), custom_call_target="tpu_custom_call" | custom-call | flops 36238786560 | bytes 283115520 | tf_op jit(solution)/shard_map/finish/pallas_call | solution.py:411
  (118 shorter events, 29.6 us)
Async XLA Ops:
  4.2 8.5 %collective-permute-start.2 = (bf16[5,64,128]{2,1,0:T(8,128)(2,1)S(1)}, bf16[5,64,128]{2,1,0:T(8,128)(2,1)S(1)}, u32[]{:S(2)}, u32[]{:S(2)}) collective-permute-start(bf16[5,64,128]{2,1,0:T(8,128)(2,1)S(1)} %get-tuple-element.194), channel_id=1, source_target_pairs={{0,1},{1,0},{2,3},{3,2},{4,5},{5,4},{6,7},{7,6},{8,9},{9,8},{10,11... | collective-permute-start | bytes 245768 | tf_op jit(solution)/shard_map/ppermute | solution.py:389
  4.3 8.4 %collective-permute-start.1 = (bf16[5,64,128]{2,1,0:T(8,128)(2,1)S(1)}, bf16[5,64,128]{2,1,0:T(8,128)(2,1)S(1)}, u32[]{:S(2)}, u32[]{:S(2)}) collective-permute-start(bf16[5,64,128]{2,1,0:T(8,128)(2,1)S(1)} %get-tuple-element.195), channel_id=1, source_target_pairs={{1,4},{4,1},{3,6},{6,3},{5,8},{8,5},{7,10},{10,7},{9,12},{12,9},{1... | collective-permute-start | bytes 245768 | tf_op jit(solution)/shard_map/ppermute | solution.py:398
  9.1 8.3 %collective-permute-start.4 = (bf16[5,64,128]{2,1,0:T(8,128)(2,1)S(1)}, bf16[5,64,128]{2,1,0:T(8,128)(2,1)S(1)}, u32[]{:S(2)}, u32[]{:S(2)}) collective-permute-start(bf16[5,64,128]{2,1,0:T(8,128)(2,1)S(1)} %get-tuple-element.192), channel_id=1, source_target_pairs={{0,1},{1,0},{2,3},{3,2},{4,5},{5,4},{6,7},{7,6},{8,9},{9,8},{10,11... | collective-permute-start | bytes 245768 | tf_op jit(solution)/shard_map/ppermute | solution.py:389
  9.1 8.2 %collective-permute-start.3 = (bf16[5,64,128]{2,1,0:T(8,128)(2,1)S(1)}, bf16[5,64,128]{2,1,0:T(8,128)(2,1)S(1)}, u32[]{:S(2)}, u32[]{:S(2)}) collective-permute-start(bf16[5,64,128]{2,1,0:T(8,128)(2,1)S(1)} %get-tuple-element.193), channel_id=1, source_target_pairs={{1,4},{4,1},{3,6},{6,3},{5,8},{8,5},{7,10},{10,7},{9,12},{12,9},{1... | collective-permute-start | bytes 245768 | tf_op jit(solution)/shard_map/ppermute | solution.py:398
  14.2 5.7 %collective-permute-start.9 = (bf16[5,64,128]{2,1,0:T(8,128)(2,1)S(1)}, bf16[5,64,128]{2,1,0:T(8,128)(2,1)S(1)}, u32[]{:S(2)}, u32[]{:S(2)}) collective-permute-start(bf16[5,64,128]{2,1,0:T(8,128)(2,1)S(1)} %get-tuple-element.116), channel_id=1, source_target_pairs={{1,4},{4,1},{3,6},{6,3},{5,8},{8,5},{7,10},{10,7},{9,12},{12,9},{1... | collective-permute-start | bytes 245768 | tf_op jit(solution)/shard_map/ppermute | solution.py:398
  18.9 5.8 %collective-permute-start.5 = (bf16[5,64,128]{2,1,0:T(8,128)(2,1)S(1)}, bf16[5,64,128]{2,1,0:T(8,128)(2,1)S(1)}, u32[]{:S(2)}, u32[]{:S(2)}) collective-permute-start(bf16[5,64,128]{2,1,0:T(8,128)(2,1)S(1)} %get-tuple-element.109), channel_id=1, source_target_pairs={{1,4},{4,1},{3,6},{6,3},{5,8},{8,5},{7,10},{10,7},{9,12},{12,9},{1... | collective-permute-start | bytes 245768 | tf_op jit(solution)/shard_map/ppermute | solution.py:398
  19.4 5.2 %collective-permute-start.6 = (bf16[5,64,128]{2,1,0:T(8,128)(2,1)S(1)}, bf16[5,64,128]{2,1,0:T(8,128)(2,1)S(1)}, u32[]{:S(2)}, u32[]{:S(2)}) collective-permute-start(bf16[5,64,128]{2,1,0:T(8,128)(2,1)S(1)} %get-tuple-element.110), channel_id=1, source_target_pairs={{0,1},{1,0},{2,3},{3,2},{4,5},{5,4},{6,7},{7,6},{8,9},{9,8},{10,11... | collective-permute-start | bytes 245768 | tf_op jit(solution)/shard_map/ppermute | solution.py:389
  20.9 6.3 %collective-permute-start.11 = (bf16[5,64,128]{2,1,0:T(8,128)(2,1)S(1)}, bf16[5,64,128]{2,1,0:T(8,128)(2,1)S(1)}, u32[]{:S(2)}, u32[]{:S(2)}) collective-permute-start(bf16[5,64,128]{2,1,0:T(8,128)(2,1)S(1)} %get-tuple-element.119), channel_id=1, source_target_pairs={{1,4},{4,1},{3,6},{6,3},{5,8},{8,5},{7,10},{10,7},{9,12},{12,9},{1... | collective-permute-start | bytes 245768 | tf_op jit(solution)/shard_map/ppermute | solution.py:398
  25.5 5.8 %collective-permute-start.7 = (bf16[5,64,128]{2,1,0:T(8,128)(2,1)S(1)}, bf16[5,64,128]{2,1,0:T(8,128)(2,1)S(1)}, u32[]{:S(2)}, u32[]{:S(2)}) collective-permute-start(bf16[5,64,128]{2,1,0:T(8,128)(2,1)S(1)} %get-tuple-element.112), channel_id=1, source_target_pairs={{1,4},{4,1},{3,6},{6,3},{5,8},{8,5},{7,10},{10,7},{9,12},{12,9},{1... | collective-permute-start | bytes 245768 | tf_op jit(solution)/shard_map/ppermute | solution.py:398
  26.3 5.1 %collective-permute-start.8 = (bf16[5,64,128]{2,1,0:T(8,128)(2,1)S(1)}, bf16[5,64,128]{2,1,0:T(8,128)(2,1)S(1)}, u32[]{:S(2)}, u32[]{:S(2)}) collective-permute-start(bf16[5,64,128]{2,1,0:T(8,128)(2,1)S(1)} %get-tuple-element.113), channel_id=1, source_target_pairs={{0,1},{1,0},{2,3},{3,2},{4,5},{5,4},{6,7},{7,6},{8,9},{9,8},{10,11... | collective-permute-start | bytes 245768 | tf_op jit(solution)/shard_map/ppermute | solution.py:389
  28.0 5.8 %collective-permute-start.13 = (bf16[5,64,128]{2,1,0:T(8,128)(2,1)S(1)}, bf16[5,64,128]{2,1,0:T(8,128)(2,1)S(1)}, u32[]{:S(2)}, u32[]{:S(2)}) collective-permute-start(bf16[5,64,128]{2,1,0:T(8,128)(2,1)S(1)} %get-tuple-element.122), channel_id=1, source_target_pairs={{1,4},{4,1},{3,6},{6,3},{5,8},{8,5},{7,10},{10,7},{9,12},{12,9},{1... | collective-permute-start | bytes 245768 | tf_op jit(solution)/shard_map/ppermute | solution.py:398
  32.2 6.1 %collective-permute-start.15 = (bf16[5,64,128]{2,1,0:T(8,128)(2,1)S(1)}, bf16[5,64,128]{2,1,0:T(8,128)(2,1)S(1)}, u32[]{:S(2)}, u32[]{:S(2)}) collective-permute-start(bf16[5,64,128]{2,1,0:T(8,128)(2,1)S(1)} %get-tuple-element.126), channel_id=1, source_target_pairs={{1,4},{4,1},{3,6},{6,3},{5,8},{8,5},{7,10},{10,7},{9,12},{12,9},{1... | collective-permute-start | bytes 245768 | tf_op jit(solution)/shard_map/ppermute | solution.py:398
  32.9 5.4 %collective-permute-start.16 = (bf16[5,64,128]{2,1,0:T(8,128)(2,1)S(1)}, bf16[5,64,128]{2,1,0:T(8,128)(2,1)S(1)}, u32[]{:S(2)}, u32[]{:S(2)}) collective-permute-start(bf16[5,64,128]{2,1,0:T(8,128)(2,1)S(1)} %get-tuple-element.127), channel_id=1, source_target_pairs={{0,1},{1,0},{2,3},{3,2},{4,5},{5,4},{6,7},{7,6},{8,9},{9,8},{10,11... | collective-permute-start | bytes 245768 | tf_op jit(solution)/shard_map/ppermute | solution.py:389
  35.3 5.8 %collective-permute-start.21 = (bf16[5,64,128]{2,1,0:T(8,128)(2,1)S(1)}, bf16[5,64,128]{2,1,0:T(8,128)(2,1)S(1)}, u32[]{:S(2)}, u32[]{:S(2)}) collective-permute-start(bf16[5,64,128]{2,1,0:T(8,128)(2,1)S(1)} %get-tuple-element.136), channel_id=1, source_target_pairs={{1,4},{4,1},{3,6},{6,3},{5,8},{8,5},{7,10},{10,7},{9,12},{12,9},{1... | collective-permute-start | bytes 245768 | tf_op jit(solution)/shard_map/ppermute | solution.py:398
  39.9 5.8 %collective-permute-start.17 = (bf16[5,64,128]{2,1,0:T(8,128)(2,1)S(1)}, bf16[5,64,128]{2,1,0:T(8,128)(2,1)S(1)}, u32[]{:S(2)}, u32[]{:S(2)}) collective-permute-start(bf16[5,64,128]{2,1,0:T(8,128)(2,1)S(1)} %get-tuple-element.129), channel_id=1, source_target_pairs={{1,4},{4,1},{3,6},{6,3},{5,8},{8,5},{7,10},{10,7},{9,12},{12,9},{1... | collective-permute-start | bytes 245768 | tf_op jit(solution)/shard_map/ppermute | solution.py:398
  40.5 5.1 %collective-permute-start.18 = (bf16[5,64,128]{2,1,0:T(8,128)(2,1)S(1)}, bf16[5,64,128]{2,1,0:T(8,128)(2,1)S(1)}, u32[]{:S(2)}, u32[]{:S(2)}) collective-permute-start(bf16[5,64,128]{2,1,0:T(8,128)(2,1)S(1)} %get-tuple-element.130), channel_id=1, source_target_pairs={{0,1},{1,0},{2,3},{3,2},{4,5},{5,4},{6,7},{7,6},{8,9},{9,8},{10,11... | collective-permute-start | bytes 245768 | tf_op jit(solution)/shard_map/ppermute | solution.py:389
  42.0 6.2 %collective-permute-start.23 = (bf16[5,64,128]{2,1,0:T(8,128)(2,1)S(1)}, bf16[5,64,128]{2,1,0:T(8,128)(2,1)S(1)}, u32[]{:S(2)}, u32[]{:S(2)}) collective-permute-start(bf16[5,64,128]{2,1,0:T(8,128)(2,1)S(1)} %get-tuple-element.139), channel_id=1, source_target_pairs={{1,4},{4,1},{3,6},{6,3},{5,8},{8,5},{7,10},{10,7},{9,12},{12,9},{1... | collective-permute-start | bytes 245768 | tf_op jit(solution)/shard_map/ppermute | solution.py:398
  46.5 5.8 %collective-permute-start.19 = (bf16[5,64,128]{2,1,0:T(8,128)(2,1)S(1)}, bf16[5,64,128]{2,1,0:T(8,128)(2,1)S(1)}, u32[]{:S(2)}, u32[]{:S(2)}) collective-permute-start(bf16[5,64,128]{2,1,0:T(8,128)(2,1)S(1)} %get-tuple-element.132), channel_id=1, source_target_pairs={{1,4},{4,1},{3,6},{6,3},{5,8},{8,5},{7,10},{10,7},{9,12},{12,9},{1... | collective-permute-start | bytes 245768 | tf_op jit(solution)/shard_map/ppermute | solution.py:398
  47.3 5.1 %collective-permute-start.20 = (bf16[5,64,128]{2,1,0:T(8,128)(2,1)S(1)}, bf16[5,64,128]{2,1,0:T(8,128)(2,1)S(1)}, u32[]{:S(2)}, u32[]{:S(2)}) collective-permute-start(bf16[5,64,128]{2,1,0:T(8,128)(2,1)S(1)} %get-tuple-element.133), channel_id=1, source_target_pairs={{0,1},{1,0},{2,3},{3,2},{4,5},{5,4},{6,7},{7,6},{8,9},{9,8},{10,11... | collective-permute-start | bytes 245768 | tf_op jit(solution)/shard_map/ppermute | solution.py:389
  49.0 5.8 %collective-permute-start.25 = (bf16[5,64,128]{2,1,0:T(8,128)(2,1)S(1)}, bf16[5,64,128]{2,1,0:T(8,128)(2,1)S(1)}, u32[]{:S(2)}, u32[]{:S(2)}) collective-permute-start(bf16[5,64,128]{2,1,0:T(8,128)(2,1)S(1)} %get-tuple-element.142), channel_id=1, source_target_pairs={{1,4},{4,1},{3,6},{6,3},{5,8},{8,5},{7,10},{10,7},{9,12},{12,9},{1... | collective-permute-start | bytes 245768 | tf_op jit(solution)/shard_map/ppermute | solution.py:398
  53.4 5.8 %collective-permute-start.27 = (bf16[5,64,128]{2,1,0:T(8,128)(2,1)S(1)}, bf16[5,64,128]{2,1,0:T(8,128)(2,1)S(1)}, u32[]{:S(2)}, u32[]{:S(2)}) collective-permute-start(bf16[5,64,128]{2,1,0:T(8,128)(2,1)S(1)} %get-tuple-element.146), channel_id=1, source_target_pairs={{1,4},{4,1},{3,6},{6,3},{5,8},{8,5},{7,10},{10,7},{9,12},{12,9},{1... | collective-permute-start | bytes 245768 | tf_op jit(solution)/shard_map/ppermute | solution.py:398
  54.1 5.1 %collective-permute-start.28 = (bf16[5,64,128]{2,1,0:T(8,128)(2,1)S(1)}, bf16[5,64,128]{2,1,0:T(8,128)(2,1)S(1)}, u32[]{:S(2)}, u32[]{:S(2)}) collective-permute-start(bf16[5,64,128]{2,1,0:T(8,128)(2,1)S(1)} %get-tuple-element.147), channel_id=1, source_target_pairs={{0,1},{1,0},{2,3},{3,2},{4,5},{5,4},{6,7},{7,6},{8,9},{9,8},{10,11... | collective-permute-start | bytes 245768 | tf_op jit(solution)/shard_map/ppermute | solution.py:389
  56.3 6.0 %collective-permute-start.33 = (bf16[5,64,128]{2,1,0:T(8,128)(2,1)S(1)}, bf16[5,64,128]{2,1,0:T(8,128)(2,1)S(1)}, u32[]{:S(2)}, u32[]{:S(2)}) collective-permute-start(bf16[5,64,128]{2,1,0:T(8,128)(2,1)S(1)} %get-tuple-element.156), channel_id=1, source_target_pairs={{1,4},{4,1},{3,6},{6,3},{5,8},{8,5},{7,10},{10,7},{9,12},{12,9},{1... | collective-permute-start | bytes 245768 | tf_op jit(solution)/shard_map/ppermute | solution.py:398
  60.7 5.8 %collective-permute-start.29 = (bf16[5,64,128]{2,1,0:T(8,128)(2,1)S(1)}, bf16[5,64,128]{2,1,0:T(8,128)(2,1)S(1)}, u32[]{:S(2)}, u32[]{:S(2)}) collective-permute-start(bf16[5,64,128]{2,1,0:T(8,128)(2,1)S(1)} %get-tuple-element.149), channel_id=1, source_target_pairs={{1,4},{4,1},{3,6},{6,3},{5,8},{8,5},{7,10},{10,7},{9,12},{12,9},{1... | collective-permute-start | bytes 245768 | tf_op jit(solution)/shard_map/ppermute | solution.py:398
  61.5 5.0 %collective-permute-start.30 = (bf16[5,64,128]{2,1,0:T(8,128)(2,1)S(1)}, bf16[5,64,128]{2,1,0:T(8,128)(2,1)S(1)}, u32[]{:S(2)}, u32[]{:S(2)}) collective-permute-start(bf16[5,64,128]{2,1,0:T(8,128)(2,1)S(1)} %get-tuple-element.150), channel_id=1, source_target_pairs={{0,1},{1,0},{2,3},{3,2},{4,5},{5,4},{6,7},{7,6},{8,9},{9,8},{10,11... | collective-permute-start | bytes 245768 | tf_op jit(solution)/shard_map/ppermute | solution.py:389
  63.2 5.8 %collective-permute-start.35 = (bf16[5,64,128]{2,1,0:T(8,128)(2,1)S(1)}, bf16[5,64,128]{2,1,0:T(8,128)(2,1)S(1)}, u32[]{:S(2)}, u32[]{:S(2)}) collective-permute-start(bf16[5,64,128]{2,1,0:T(8,128)(2,1)S(1)} %get-tuple-element.159), channel_id=1, source_target_pairs={{1,4},{4,1},{3,6},{6,3},{5,8},{8,5},{7,10},{10,7},{9,12},{12,9},{1... | collective-permute-start | bytes 245768 | tf_op jit(solution)/shard_map/ppermute | solution.py:398
  65.9 3.1 %collective-permute-start.36 = (bf16[5,64,128]{2,1,0:T(8,128)(2,1)S(1)}, bf16[5,64,128]{2,1,0:T(8,128)(2,1)S(1)}, u32[]{:S(2)}, u32[]{:S(2)}) collective-permute-start(bf16[5,64,128]{2,1,0:T(8,128)(2,1)S(1)} %get-tuple-element.160), channel_id=1, source_target_pairs={{0,1},{1,0},{2,3},{3,2},{4,5},{5,4},{6,7},{7,6},{8,9},{9,8},{10,11... | collective-permute-start | bytes 245768 | tf_op jit(solution)/shard_map/ppermute | solution.py:389
  67.4 5.8 %collective-permute-start.31 = (bf16[5,64,128]{2,1,0:T(8,128)(2,1)S(1)}, bf16[5,64,128]{2,1,0:T(8,128)(2,1)S(1)}, u32[]{:S(2)}, u32[]{:S(2)}) collective-permute-start(bf16[5,64,128]{2,1,0:T(8,128)(2,1)S(1)} %get-tuple-element.152), channel_id=1, source_target_pairs={{1,4},{4,1},{3,6},{6,3},{5,8},{8,5},{7,10},{10,7},{9,12},{12,9},{1... | collective-permute-start | bytes 245768 | tf_op jit(solution)/shard_map/ppermute | solution.py:398
  68.1 5.0 %collective-permute-start.32 = (bf16[5,64,128]{2,1,0:T(8,128)(2,1)S(1)}, bf16[5,64,128]{2,1,0:T(8,128)(2,1)S(1)}, u32[]{:S(2)}, u32[]{:S(2)}) collective-permute-start(bf16[5,64,128]{2,1,0:T(8,128)(2,1)S(1)} %get-tuple-element.153), channel_id=1, source_target_pairs={{0,1},{1,0},{2,3},{3,2},{4,5},{5,4},{6,7},{7,6},{8,9},{9,8},{10,11... | collective-permute-start | bytes 245768 | tf_op jit(solution)/shard_map/ppermute | solution.py:389
  69.9 5.8 %collective-permute-start.37 = (bf16[5,64,128]{2,1,0:T(8,128)(2,1)S(1)}, bf16[5,64,128]{2,1,0:T(8,128)(2,1)S(1)}, u32[]{:S(2)}, u32[]{:S(2)}) collective-permute-start(bf16[5,64,128]{2,1,0:T(8,128)(2,1)S(1)} %get-tuple-element.162), channel_id=1, source_target_pairs={{1,4},{4,1},{3,6},{6,3},{5,8},{8,5},{7,10},{10,7},{9,12},{12,9},{1... | collective-permute-start | bytes 245768 | tf_op jit(solution)/shard_map/ppermute | solution.py:398
  74.1 6.0 %collective-permute-start.39 = (bf16[5,64,128]{2,1,0:T(8,128)(2,1)S(1)}, bf16[5,64,128]{2,1,0:T(8,128)(2,1)S(1)}, u32[]{:S(2)}, u32[]{:S(2)}) collective-permute-start(bf16[5,64,128]{2,1,0:T(8,128)(2,1)S(1)} %get-tuple-element.166), channel_id=1, source_target_pairs={{1,4},{4,1},{3,6},{6,3},{5,8},{8,5},{7,10},{10,7},{9,12},{12,9},{1... | collective-permute-start | bytes 245768 | tf_op jit(solution)/shard_map/ppermute | solution.py:398
  74.8 5.3 %collective-permute-start.40 = (bf16[5,64,128]{2,1,0:T(8,128)(2,1)S(1)}, bf16[5,64,128]{2,1,0:T(8,128)(2,1)S(1)}, u32[]{:S(2)}, u32[]{:S(2)}) collective-permute-start(bf16[5,64,128]{2,1,0:T(8,128)(2,1)S(1)} %get-tuple-element.167), channel_id=1, source_target_pairs={{0,1},{1,0},{2,3},{3,2},{4,5},{5,4},{6,7},{7,6},{8,9},{9,8},{10,11... | collective-permute-start | bytes 245768 | tf_op jit(solution)/shard_map/ppermute | solution.py:389
  77.2 5.8 %collective-permute-start.47 = (bf16[5,64,128]{2,1,0:T(8,128)(2,1)S(1)}, bf16[5,64,128]{2,1,0:T(8,128)(2,1)S(1)}, u32[]{:S(2)}, u32[]{:S(2)}) collective-permute-start(bf16[5,64,128]{2,1,0:T(8,128)(2,1)S(1)} %get-tuple-element.178), channel_id=1, source_target_pairs={{1,4},{4,1},{3,6},{6,3},{5,8},{8,5},{7,10},{10,7},{9,12},{12,9},{1... | collective-permute-start | bytes 245768 | tf_op jit(solution)/shard_map/ppermute | solution.py:398
  81.6 5.8 %collective-permute-start.41 = (bf16[5,64,128]{2,1,0:T(8,128)(2,1)S(1)}, bf16[5,64,128]{2,1,0:T(8,128)(2,1)S(1)}, u32[]{:S(2)}, u32[]{:S(2)}) collective-permute-start(bf16[5,64,128]{2,1,0:T(8,128)(2,1)S(1)} %get-tuple-element.169), channel_id=1, source_target_pairs={{1,4},{4,1},{3,6},{6,3},{5,8},{8,5},{7,10},{10,7},{9,12},{12,9},{1... | collective-permute-start | bytes 245768 | tf_op jit(solution)/shard_map/ppermute | solution.py:398
  82.3 5.0 %collective-permute-start.42 = (bf16[5,64,128]{2,1,0:T(8,128)(2,1)S(1)}, bf16[5,64,128]{2,1,0:T(8,128)(2,1)S(1)}, u32[]{:S(2)}, u32[]{:S(2)}) collective-permute-start(bf16[5,64,128]{2,1,0:T(8,128)(2,1)S(1)} %get-tuple-element.170), channel_id=1, source_target_pairs={{0,1},{1,0},{2,3},{3,2},{4,5},{5,4},{6,7},{7,6},{8,9},{9,8},{10,11... | collective-permute-start | bytes 245768 | tf_op jit(solution)/shard_map/ppermute | solution.py:389
  83.8 6.1 %collective-permute-start.49 = (bf16[5,64,128]{2,1,0:T(8,128)(2,1)S(1)}, bf16[5,64,128]{2,1,0:T(8,128)(2,1)S(1)}, u32[]{:S(2)}, u32[]{:S(2)}) collective-permute-start(bf16[5,64,128]{2,1,0:T(8,128)(2,1)S(1)} %get-tuple-element.181), channel_id=1, source_target_pairs={{1,4},{4,1},{3,6},{6,3},{5,8},{8,5},{7,10},{10,7},{9,12},{12,9},{1... | collective-permute-start | bytes 245768 | tf_op jit(solution)/shard_map/ppermute | solution.py:398
  88.3 5.7 %collective-permute-start.43 = (bf16[5,64,128]{2,1,0:T(8,128)(2,1)S(1)}, bf16[5,64,128]{2,1,0:T(8,128)(2,1)S(1)}, u32[]{:S(2)}, u32[]{:S(2)}) collective-permute-start(bf16[5,64,128]{2,1,0:T(8,128)(2,1)S(1)} %get-tuple-element.172), channel_id=1, source_target_pairs={{1,4},{4,1},{3,6},{6,3},{5,8},{8,5},{7,10},{10,7},{9,12},{12,9},{1... | collective-permute-start | bytes 245768 | tf_op jit(solution)/shard_map/ppermute | solution.py:398
  89.0 5.0 %collective-permute-start.44 = (bf16[5,64,128]{2,1,0:T(8,128)(2,1)S(1)}, bf16[5,64,128]{2,1,0:T(8,128)(2,1)S(1)}, u32[]{:S(2)}, u32[]{:S(2)}) collective-permute-start(bf16[5,64,128]{2,1,0:T(8,128)(2,1)S(1)} %get-tuple-element.173), channel_id=1, source_target_pairs={{0,1},{1,0},{2,3},{3,2},{4,5},{5,4},{6,7},{7,6},{8,9},{9,8},{10,11... | collective-permute-start | bytes 245768 | tf_op jit(solution)/shard_map/ppermute | solution.py:389
  91.0 6.2 %collective-permute-start.51 = (bf16[5,64,128]{2,1,0:T(8,128)(2,1)S(1)}, bf16[5,64,128]{2,1,0:T(8,128)(2,1)S(1)}, u32[]{:S(2)}, u32[]{:S(2)}) collective-permute-start(bf16[5,64,128]{2,1,0:T(8,128)(2,1)S(1)} %get-tuple-element.184), channel_id=1, source_target_pairs={{1,4},{4,1},{3,6},{6,3},{5,8},{8,5},{7,10},{10,7},{9,12},{12,9},{1... | collective-permute-start | bytes 245768 | tf_op jit(solution)/shard_map/ppermute | solution.py:398
  93.8 4.5 %collective-permute-start.52 = (bf16[5,64,128]{2,1,0:T(8,128)(2,1)S(1)}, bf16[5,64,128]{2,1,0:T(8,128)(2,1)S(1)}, u32[]{:S(2)}, u32[]{:S(2)}) collective-permute-start(bf16[5,64,128]{2,1,0:T(8,128)(2,1)S(1)} %get-tuple-element.185), channel_id=1, source_target_pairs={{0,1},{1,0},{2,3},{3,2},{4,5},{5,4},{6,7},{7,6},{8,9},{9,8},{10,11... | collective-permute-start | bytes 245768 | tf_op jit(solution)/shard_map/ppermute | solution.py:389
  94.9 5.7 %collective-permute-start.45 = (bf16[5,64,128]{2,1,0:T(8,128)(2,1)S(1)}, bf16[5,64,128]{2,1,0:T(8,128)(2,1)S(1)}, u32[]{:S(2)}, u32[]{:S(2)}) collective-permute-start(bf16[5,64,128]{2,1,0:T(8,128)(2,1)S(1)} %get-tuple-element.175), channel_id=1, source_target_pairs={{1,4},{4,1},{3,6},{6,3},{5,8},{8,5},{7,10},{10,7},{9,12},{12,9},{1... | collective-permute-start | bytes 245768 | tf_op jit(solution)/shard_map/ppermute | solution.py:398
  95.7 5.0 %collective-permute-start.46 = (bf16[5,64,128]{2,1,0:T(8,128)(2,1)S(1)}, bf16[5,64,128]{2,1,0:T(8,128)(2,1)S(1)}, u32[]{:S(2)}, u32[]{:S(2)}) collective-permute-start(bf16[5,64,128]{2,1,0:T(8,128)(2,1)S(1)} %get-tuple-element.176), channel_id=1, source_target_pairs={{0,1},{1,0},{2,3},{3,2},{4,5},{5,4},{6,7},{7,6},{8,9},{9,8},{10,11... | collective-permute-start | bytes 245768 | tf_op jit(solution)/shard_map/ppermute | solution.py:389
  95.7 6.3 %collective-permute-start.53 = (bf16[8,64,128]{2,1,0:T(8,128)(2,1)S(1)}, bf16[8,64,128]{2,1,0:T(8,128)(2,1)S(1)}, u32[]{:S(2)}, u32[]{:S(2)}) collective-permute-start(bf16[8,64,128]{2,1,0:T(8,128)(2,1)S(1)} %get-tuple-element.183.own.rest_0_.refs_4_), channel_id=1, source_target_pairs={{2,0},{3,1},{0,2},{1,3},{6,4},{7,5},{4,6},{5,7},{10,8},{11,9},{8,1... | collective-permute-start | bytes 393224 | tf_op jit(solution)/shard_map/ppermute | solution.py:402
  97.2 7.2 %collective-permute-start.54 = (bf16[8,64,128]{2,1,0:T(8,128)(2,1)S(1)}, bf16[8,64,128]{2,1,0:T(8,128)(2,1)S(1)}, u32[]{:S(2)}, u32[]{:S(2)}) collective-permute-start(bf16[8,64,128]{2,1,0:T(8,128)(2,1)S(1)} %get-tuple-element.174.own.refs_5_), channel_id=1, source_target_pairs={{2,0},{3,1},{0,2},{1,3},{6,4},{7,5},{4,6},{5,7},{10,8},{11,9},{8,1... | collective-permute-start | bytes 393224 | tf_op jit(solution)/shard_map/ppermute | solution.py:402
  107.5 4.4 %collective-permute-start.56 = (bf16[272,128]{1,0:T(8,128)(2,1)S(1)}, bf16[272,128]{1,0:T(8,128)(2,1)S(1)}, u32[]{:S(2)}, u32[]{:S(2)}) collective-permute-start(bf16[272,128]{1,0:T(8,128)(2,1)S(1)} %add.19.left), channel_id=1, source_target_pairs={{0,4},{4,0},{8,12},{12,8},{1,5},{5,1},{9,13},{13,9},{2,6},{6,2},{1... | collective-permute-start | bytes 208904 | tf_op jit(solution)/shard_map/ppermute | solution.py:564
  111.9 5.3 %collective-permute-start.57 = (bf16[272,128]{1,0:T(8,128)(2,1)S(1)}, bf16[272,128]{1,0:T(8,128)(2,1)S(1)}, u32[]{:S(2)}, u32[]{:S(2)}) collective-permute-start(bf16[272,128]{1,0:T(8,128)(2,1)S(1)} %add.20.left), channel_id=1, source_target_pairs={{0,8},{4,12},{8,0},{12,4},{1,9},{5,13},{9,1},{13,5},{2,10},{6,14},... | collective-permute-start | bytes 208904 | tf_op jit(solution)/shard_map/ppermute | solution.py:564
  113.5 5.9 %collective-permute-start.61 = (bf16[8,64,128]{2,1,0:T(8,128)(2,1)S(1)}, bf16[8,64,128]{2,1,0:T(8,128)(2,1)S(1)}, u32[]{:S(2)}, u32[]{:S(2)}) collective-permute-start(bf16[8,64,128]{2,1,0:T(8,128)(2,1)S(1)} %get-tuple-element.183.own.rest_0_.refs_4_), channel_id=1, source_target_pairs={{0,1},{1,0},{2,3},{3,2},{4,5},{5,4},{6,7},{7,6},{8,9},{9,8},{10,11... | collective-permute-start | bytes 393224 | tf_op jit(solution)/shard_map/ppermute | solution.py:389
  117.2 4.4 %collective-permute-start.58 = (bf16[272,128]{1,0:T(8,128)(2,1)S(1)}, bf16[272,128]{1,0:T(8,128)(2,1)S(1)}, u32[]{:S(2)}, u32[]{:S(2)}) collective-permute-start(bf16[272,128]{1,0:T(8,128)(2,1)S(1)} %add.21.refs_0_), channel_id=1, source_target_pairs={{2,0},{3,1},{0,2},{1,3},{6,4},{7,5},{4,6},{5,7},{10,8},{11,9},{8,1... | collective-permute-start | bytes 208904 | tf_op jit(solution)/shard_map/ppermute | solution.py:402
  (17 other events, 43.7 us)

commit v4 on v3

--- a/solution.py
+++ b/solution.py
@@ -69,23 +69,28 @@
     return image_of(table, ext, (ovl,), row).T
 
 
-def cut_kernel(ints, sizes, trial, keep, give, sizes_here, trial_here, sems):
+def cut_kernel(ints, sizes, trial, own, near, give, far, across, sizes_here, here, masked, sems):
     copies = [
         pltpu.make_async_copy(sizes, sizes_here, sems.at[0]),
-        pltpu.make_async_copy(trial, trial_here, sems.at[1]),
+        pltpu.make_async_copy(trial, here, sems.at[1]),
     ]
     for copy in copies:
         copy.start()
     for copy in copies:
         copy.wait()
-    half, _, orbs = keep.shape
+    half, _, orbs = own.shape
     core = ints[0]
-    lane = lax.broadcasted_iota(jnp.int32, keep.shape[1:], 1)
-    for out, which in ((give, 1 - core), (keep, core)):
-        for row in range(half):
-            at = which * half + row
-            values = trial_here[:, pl.ds(pl.multiple_of(at * orbs, orbs), orbs)].astype(F32)
-            out[row] = jnp.where(lane < sizes_here[at], values, 0.0).astype(BF16)
+    lane = lax.broadcasted_iota(jnp.int32, own.shape[1:], 1)
+    for row in range(2 * half):
+        values = here[:, row * orbs : (row + 1) * orbs].astype(F32)
+        masked[row] = jnp.where(lane < sizes_here[row], values, 0.0).astype(BF16)
+    spare = half - HALF_BAND
+    last = 2 * half - HALF_BAND
+    own[...] = masked[pl.ds(half * core, half)]
+    near[...] = masked[pl.ds(half - HALF_BAND * core, HALF_BAND)]
+    give[...] = masked[pl.ds(spare * (1 - core), half + HALF_BAND)]
+    far[...] = masked[pl.ds(last * (1 - core), HALF_BAND)]
+    across[...] = masked[pl.ds(last * core, HALF_BAND)]
 
 
 def load_kernel(total, ints, shift, width, columns, phases, sizes, ham, ovl, *rest):
@@ -168,7 +173,8 @@
     send_ends(core, out, intra_out, inter_out)
 
 
-def images_kernel(ints, index, signs, own, inter, intra, ham, ovl, out, ext):
+def images_kernel(ints, index, signs, own, inter, intra, ham, ovl, y_other, out, ext):
+    del y_other
     core = ints[0]
     fill_ext(core, own, intra, inter, ext)
     half, _, orbs = own.shape
@@ -179,22 +185,20 @@
         out[1, :, at] = image_h.astype(BF16)
 
 
-def gram_kernel(chips, ints, index, signs, own, inter, intra, ham, ovl, ready, *rest):
-    count = CORES * chips - 1
-    first, *others = rest[:count]
-    keep, send, ext, images, both = rest[count:]
-    images_kernel(ints, index, signs, own, inter, intra, ham, ovl, images, ext)
+def gram_kernel(chips, ints, *refs):
+    images, groups = refs[:CORES], refs[CORES : CORES + CORES * chips]
+    keep, send, both = refs[CORES + CORES * chips :]
     core, chip = ints[0], ints[1]
-    half, local_vecs, _ = own.shape
+    half, local_vecs, _ = groups[0].shape
     vecs = CORES * local_vecs
-    groups = [[first[row] for row in range(half)], [own[row] for row in range(half)]]
-    groups += [[other[row] for row in range(half)] for other in others]
-    flat = jnp.concatenate([jnp.concatenate(group, axis=1) for group in groups], axis=0)
+    flat = jnp.concatenate(
+        [jnp.concatenate([group[row] for row in range(half)], axis=1) for group in groups], axis=0
+    )
     eye = lax.broadcasted_iota(jnp.int32, (vecs, vecs), 0) == lax.broadcasted_iota(
         jnp.int32, (vecs, vecs), 1
     )
     for matrix in range(2):
-        mine = jnp.concatenate([ready[matrix], images[matrix]], axis=0)
+        mine = jnp.concatenate([image[matrix] for image in images], axis=0)
         pair = lax.dot_general(mine, flat, NT, preferred_element_type=F32)
         for step in range(chips):
             where = pl.multiple_of(lax.rem(chip + step, chips) * vecs, vecs)
@@ -230,11 +234,6 @@
     middle = rest.astype(BF16)
     low = (rest - middle.astype(F32)).astype(BF16)
     return high, middle, low
-
-
-def reciprocal(value):
-    guess = pl.reciprocal(value, approx=True)
-    return guess * (2.0 - value * guess)
 
 
 def panel_inverse(block):
@@ -261,11 +260,13 @@
         for k in range(start, start + group):
             here = k // SUBLANES
             pivots[here] = jnp.where(sub == k % SUBLANES, at, pivots[here])
-            inv = reciprocal(at)
+            guess = pl.reciprocal(at, approx=True)
+            correction = 2.0 - at * guess
+            inv = guess * correction
             if k + 1 < start + group:
                 below = (k + 1) // SUBLANES
                 product = spread(columns[k][below], k + 1) * spread(columns[k + 1][here], k)
-                at = spread(columns[k + 1][below], k + 1) - product * inv
+                at = spread(columns[k + 1][below], k + 1) - (product * guess) * correction
             factors = {v: columns[k][v] * inv for v in range(here, count)}
             factors[here] = jnp.where(sub > k % SUBLANES, factors[here], 0.0)
             for later in range(k + 1, start + group):
@@ -397,6 +398,14 @@
                 pairs += [(upper, lower), (lower, upper)]
         return lax.ppermute(value, ("row", "col"), pairs)
 
+    def next_chips(value):
+        pairs = []
+        for r in range(num_rows):
+            for c in range(num_cols):
+                to = (r + 1 if c % CORES == 0 else r - 1) % num_rows
+                pairs.append((r * num_cols + c, to * num_cols + c))
+        return lax.ppermute(value, ("row", "col"), pairs)
+
     def from_chip(value, step):
         pairs = [((c + step * CORES) % num_cols, c) for c in range(num_cols)]
         return lax.ppermute(value, "col", pairs)
@@ -436,20 +445,23 @@
     def stays(value):
         return pltpu.with_memory_space_constraint(value, pltpu.HBM)
 
-    own, give = pl.pallas_call(
+    more = jax.ShapeDtypeStruct((half + HALF_BAND, local_vecs, orbs), BF16)
+    own, near, give, far, across = pl.pallas_call(
         cut_kernel,
         name="cut",
-        out_shape=(state, state),
+        out_shape=(state, end, more, end, end),
         in_specs=[SMEM, HBM, HBM],
-        out_specs=(VMEM, VMEM),
+        out_specs=(VMEM,) * 5,
         scratch_shapes=[
             pltpu.SMEM(block_sizes.shape, jnp.int32),
             pltpu.VMEM(trial_vectors.shape, BF16),
+            pltpu.VMEM((blocks_dev, local_vecs, orbs), BF16),
             pltpu.SemaphoreType.DMA((2,)),
         ],
         compiler_params=params,
     )(ints, stays(block_sizes), stays(trial_vectors))
-    got, ints = lax.optimization_barrier((swap_cores(give), ints))
+    far, across = next_chips(far), swap_chips(across)
+    got = swap_cores(give)
     matrix = vmem((half, *hamiltonian_blocks.shape[1:]), BF16)
     ham, ovl, index, signs, place, scal = pl.pallas_call(
         functools.partial(load_kernel, total_blocks),
@@ -485,18 +497,16 @@
         stays(hamiltonian_blocks),
         stays(correlation_offset),
     )
-    current = [jnp.where(core == 0, own, got), jnp.where(core == 0, got, own)]
-    spare = half - HALF_BAND
-    ends = [
-        (
-            lax.dynamic_slice_in_dim(value, spare * core, HALF_BAND, 0),
-            lax.dynamic_slice_in_dim(value, spare * (1 - core), HALF_BAND, 0),
-        )
-        for value in current
-    ]
+    got_own = lax.dynamic_slice_in_dim(got, HALF_BAND * core, half, 0)
+    got_near = lax.dynamic_slice_in_dim(got, half * (1 - core), HALF_BAND, 0)
+
+    def by_group(mine, other):
+        return [jnp.where(core == 0, mine, other), jnp.where(core == 0, other, mine)]
+
+    current = by_group(own, got_own)
+    halo = list(zip(by_group(far, across), by_group(near, got_near)))
     table = (place, index, signs)
     scaled, term, previous = [None] * CORES, [None] * CORES, list(current)
-    halo = [exchange(ends[g]) for g in range(CORES)]
     for degree in range(DEGREE):
         for g in range(CORES):
             if g > 0:
@@ -529,24 +539,28 @@
 
     y_others = [from_chip(value, step) for step in range(1, chips) for value in current]
     image = jax.ShapeDtypeStruct((2, local_vecs, half * orbs), BF16)
-    (ready,) = call(
-        images_kernel,
-        "images",
-        table,
-        (current[0], *halo[0], ham, ovl),
-        (image,),
-        [ext],
-        2 * row_flops,
-    )
+    images = []
+    for g, vectors in enumerate(current):
+        if g > 0:
+            vectors, images[0] = lax.optimization_barrier((vectors, images[0]))
+        images += call(
+            images_kernel,
+            "images",
+            table,
+            (vectors, *halo[g], ham, ovl, y_others[0]),
+            (image,),
+            [ext],
+            2 * row_flops,
+        )
     payload = jax.ShapeDtypeStruct((size + DIAGONAL_ROWS, vecs), BF16)
     keep, send = call(
         functools.partial(gram_kernel, chips),
         "gram",
-        table,
-        (current[1], *halo[1], ham, ovl, ready, current[0], *y_others),
+        (place,),
+        (*images, *current, *y_others),
         (payload, payload),
-        [ext, pltpu.VMEM(image.shape, BF16), pltpu.VMEM((2, *payload.shape), BF16)],
-        3 * row_flops,
+        [pltpu.VMEM((2, *payload.shape), BF16)],
+        row_flops,
     )
 
     def add(left, right):

time: 133 us -> 129 us (0.970)
  waiting for transfers between devices: 27.7 us -> 21.6 us
  starting transfers between devices: 58.3 us -> 60.4 us
    ppermute x26 -> x25, waiting for transfers between devices: 12.8 us -> 7.37 us  [swap_chips(): return lax.ppermute(value, ('row', 'col'), pairs)]
    ppermute x0 -> x1, starting transfers between devices: none -> 3.08 us  [next_chips(): return lax.ppermute(value, ('row', 'col'), pairs)]
    ppermute x3, waiting for transfers between devices: 5.53 us -> 2.86 us  [from_chip(): return lax.ppermute(value, 'col', pairs)]
    ppermute x2, waiting for transfers between devices: 6.83 us -> 8.86 us  [local(): other = lax.ppermute(summed, 'row', [(r, r ^ bit) for r in range(num_rows)])]
    ppermute x2, starting transfers between devices: 2.82 us -> 1.43 us  [local(): other = lax.ppermute(summed, 'row', [(r, r ^ bit) for r in range(num_rows)])]
    ppermute x26 -> x25, starting transfers between devices: 49.4 us -> 50.4 us  [swap_chips(): return lax.ppermute(value, ('row', 'col'), pairs)]
    pallas_call x30 -> x31, Pallas kernels: 39.5 us -> 39.3 us  [call(): pl.pallas_call(kernel, name=name, out_shape=outs, in_specs=[SMEM] * len(s...]
  transfers between devices with their start and end apart: 65 -> 63, of which waited for: 27 -> 21; matrix products, arithmetic and copies ran while one was open for 0% -> 0% of each run, Pallas kernels for 23% -> 24%
where the time goes in v4:
time: 129 us; the launch traced here: 128 us
  starting transfers between devices  60.4 us (47%)
  Pallas kernels  43.9 us (34%)
  waiting for transfers between devices  21.6 us (17%)
  between operations  2.31 us (2%)
    ppermute x25, starting transfers between devices, swap_chips(): return lax.ppermute(value, ('row', 'col'), pairs)  50.4 us
    pallas_call x31, Pallas kernels, call(): pl.pallas_call(kernel, name=name, out_shape=outs, in_specs=[SMEM] * len(s...  39.3 us
    ppermute x2, waiting for transfers between devices, local(): other = lax.ppermute(summed, 'row', [(r, r ^ bit) for r in range(num_rows)])  8.86 us
    ppermute x25, waiting for transfers between devices, swap_chips(): return lax.ppermute(value, ('row', 'col'), pairs)  7.37 us
    ppermute x3, starting transfers between devices, from_chip(): return lax.ppermute(value, 'col', pairs)  4.2 us
    ppermute x1, starting transfers between devices, next_chips(): return lax.ppermute(value, ('row', 'col'), pairs)  3.08 us
    pallas_call x1, Pallas kernels, local(): pl.pallas_call(functools.partial(load_kernel, total_blocks), name='load',...  3.01 us
    ppermute x3, waiting for transfers between devices, from_chip(): return lax.ppermute(value, 'col', pairs)  2.86 us
  transfers between devices with their start and end apart: 63, of which 21 were waited for; matrix products, arithmetic and copies ran while one was open for 0% of the time, Pallas kernels for 24%

profile of v4, /device:TPU:0, one launch (start us, length us, event | category | flops | bytes accessed | tf_op | source)
XLA Modules:
  0.0 128.4 jit_solution(11030268568827026307)
XLA Ops:
  0.7 1.6 %cut.1 = (bf16[8,64,128]{2,1,0:T(8,128)(2,1)S(1)}, bf16[5,64,128]{2,1,0:T(8,128)(2,1)S(1)}, bf16[13,64,128]{2,1,0:T(8,128)(2,1)S(1)}, bf16[5,64,128]{2,1,0:T(8,128)(2,1)S(1)}, bf16[5,64,128]{2,1,0:T(8,128)(2,1)S(1)}) custom-call(s32[4]{0:T(128)S(1)} %pad_add_fusion.ints, s32[16]{0:T(128)} %sizes.3, bf16[64,2048]{1,0:T(8,128)(2,1)} %trial.1), custom_call_target="tpu_custom_call" | custom-call | tf_op jit(solution)/shard_map/cut/pallas_call | solution.py:449
  2.3 3.1 %collective-permute-start.1 = (bf16[5,64,128]{2,1,0:T(8,128)(2,1)S(1)}, bf16[5,64,128]{2,1,0:T(8,128)(2,1)S(1)}, u32[]{:S(2)}, u32[]{:S(2)}) collective-permute-start(bf16[5,64,128]{2,1,0:T(8,128)(2,1)S(1)} %get-tuple-element.105), channel_id=1, source_target_pairs={{0,4},{1,13},{2,6},{3,15},{4,8},{5,1},{6,10},{7,3},{8,12},{9,5},{1... | collective-permute-start | bytes 245768 | tf_op jit(solution)/shard_map/ppermute | solution.py:407
  5.4 1.6 %collective-permute-start.2 = (bf16[5,64,128]{2,1,0:T(8,128)(2,1)S(1)}, bf16[5,64,128]{2,1,0:T(8,128)(2,1)S(1)}, u32[]{:S(2)}, u32[]{:S(2)}) collective-permute-start(bf16[5,64,128]{2,1,0:T(8,128)(2,1)S(1)} %get-tuple-element.106), channel_id=1, source_target_pairs={{1,4},{4,1},{3,6},{6,3},{5,8},{8,5},{7,10},{10,7},{9,12},{12,9},{1... | collective-permute-start | bytes 245768 | tf_op jit(solution)/shard_map/ppermute | solution.py:399
  8.4 3.0 %load.1 = (bf16[8,9,128,128]{3,2,1,0:T(8,128)(2,1)S(1)}, bf16[8,9,128,128]{3,2,1,0:T(8,128)(2,1)S(1)}, s32[8,9]{1,0:T(8,128)S(4)}, f32[8,9]{1,0:T(8,128)S(4)}, s32[11]{0:T(128)S(4)}, /*index=5*/f32[2]{0:T(128)S(4)}) custom-call(s32[4]{0:T(128)S(1)} %pad_add_fusion.ints, f32[1]{0:T(128)S(6)} %copy.10.shift, f32[1]{0:T(128)S(6)} %copy.11.width, ...), custom_call_target="tpu_custom_call" | custom-call | bytes 9437184 | tf_op jit(solution)/shard_map/load/pallas_call | solution.py:466
  12.0 1.5 %scaled.8 = (bf16[8,64,128]{2,1,0:T(8,128)(2,1)S(1)}, bf16[5,64,128]{2,1,0:T(8,128)(2,1)S(1)}, bf16[5,64,128]{2,1,0:T(8,128)(2,1)S(1)}) custom-call(s32[11]{0:T(128)S(4)} %get-tuple-element.99.ints, s32[8,9]{1,0:T(8,128)S(4)} %get-tuple-element.100.index, f32[8,9]{1,0:T(8,128)S(4)} %get-tuple-element.101.signs, f32[2]{0:T(128)S(4)} %get-tuple-element.102.scal, ...), custom_call_target="tpu_custom_call" | custom-call | flops 7247757312 | bytes 56623104 | tf_op jit(solution)/shard_map/scaled/pallas_call | solution.py:420
  13.5 1.7 %collective-permute-start.7 = (bf16[5,64,128]{2,1,0:T(8,128)(2,1)S(1)}, bf16[5,64,128]{2,1,0:T(8,128)(2,1)S(1)}, u32[]{:S(2)}, u32[]{:S(2)}) collective-permute-start(bf16[5,64,128]{2,1,0:T(8,128)(2,1)S(1)} %get-tuple-element.120), channel_id=1, source_target_pairs={{1,4},{4,1},{3,6},{6,3},{5,8},{8,5},{7,10},{10,7},{9,12},{12,9},{1... | collective-permute-start | bytes 245768 | tf_op jit(solution)/shard_map/ppermute | solution.py:399
  15.2 1.5 %scaled.9 = (bf16[8,64,128]{2,1,0:T(8,128)(2,1)S(1)}, bf16[5,64,128]{2,1,0:T(8,128)(2,1)S(1)}, bf16[5,64,128]{2,1,0:T(8,128)(2,1)S(1)}) custom-call(s32[11]{0:T(128)S(4)} %get-tuple-element.99.ints, s32[8,9]{1,0:T(8,128)S(4)} %get-tuple-element.100.index, f32[8,9]{1,0:T(8,128)S(4)} %get-tuple-element.101.signs, f32[2]{0:T(128)S(4)} %get-tuple-element.102.scal, ...), custom_call_target="tpu_custom_call" | custom-call | flops 7247757312 | bytes 56623104 | tf_op jit(solution)/shard_map/scaled/pallas_call | solution.py:420
  16.7 1.9 %collective-permute-start.3 = (bf16[5,64,128]{2,1,0:T(8,128)(2,1)S(1)}, bf16[5,64,128]{2,1,0:T(8,128)(2,1)S(1)}, u32[]{:S(2)}, u32[]{:S(2)}) collective-permute-start(bf16[5,64,128]{2,1,0:T(8,128)(2,1)S(1)} %get-tuple-element.113), channel_id=1, source_target_pairs={{1,4},{4,1},{3,6},{6,3},{5,8},{8,5},{7,10},{10,7},{9,12},{12,9},{1... | collective-permute-start | bytes 245768 | tf_op jit(solution)/shard_map/ppermute | solution.py:399
  20.2 1.6 %collective-permute-start.9 = (bf16[5,64,128]{2,1,0:T(8,128)(2,1)S(1)}, bf16[5,64,128]{2,1,0:T(8,128)(2,1)S(1)}, u32[]{:S(2)}, u32[]{:S(2)}) collective-permute-start(bf16[5,64,128]{2,1,0:T(8,128)(2,1)S(1)} %get-tuple-element.123), channel_id=1, source_target_pairs={{1,4},{4,1},{3,6},{6,3},{5,8},{8,5},{7,10},{10,7},{9,12},{12,9},{1... | collective-permute-start | bytes 245768 | tf_op jit(solution)/shard_map/ppermute | solution.py:399
  23.5 1.9 %collective-permute-start.5 = (bf16[5,64,128]{2,1,0:T(8,128)(2,1)S(1)}, bf16[5,64,128]{2,1,0:T(8,128)(2,1)S(1)}, u32[]{:S(2)}, u32[]{:S(2)}) collective-permute-start(bf16[5,64,128]{2,1,0:T(8,128)(2,1)S(1)} %get-tuple-element.116), channel_id=1, source_target_pairs={{1,4},{4,1},{3,6},{6,3},{5,8},{8,5},{7,10},{10,7},{9,12},{12,9},{1... | collective-permute-start | bytes 245768 | tf_op jit(solution)/shard_map/ppermute | solution.py:399
  26.8 1.8 %collective-permute-start.11 = (bf16[5,64,128]{2,1,0:T(8,128)(2,1)S(1)}, bf16[5,64,128]{2,1,0:T(8,128)(2,1)S(1)}, u32[]{:S(2)}, u32[]{:S(2)}) collective-permute-start(bf16[5,64,128]{2,1,0:T(8,128)(2,1)S(1)} %get-tuple-element.126), channel_id=1, source_target_pairs={{1,4},{4,1},{3,6},{6,3},{5,8},{8,5},{7,10},{10,7},{9,12},{12,9},{1... | collective-permute-start | bytes 245768 | tf_op jit(solution)/shard_map/ppermute | solution.py:399
  30.1 2.0 %collective-permute-start.13 = (bf16[5,64,128]{2,1,0:T(8,128)(2,1)S(1)}, bf16[5,64,128]{2,1,0:T(8,128)(2,1)S(1)}, u32[]{:S(2)}, u32[]{:S(2)}) collective-permute-start(bf16[5,64,128]{2,1,0:T(8,128)(2,1)S(1)} %get-tuple-element.130), channel_id=1, source_target_pairs={{1,4},{4,1},{3,6},{6,3},{5,8},{8,5},{7,10},{10,7},{9,12},{12,9},{1... | collective-permute-start | bytes 245768 | tf_op jit(solution)/shard_map/ppermute | solution.py:399
  32.5 1.5 %scaled.10 = (bf16[8,64,128]{2,1,0:T(8,128)(2,1)S(1)}, bf16[5,64,128]{2,1,0:T(8,128)(2,1)S(1)}, bf16[5,64,128]{2,1,0:T(8,128)(2,1)S(1)}) custom-call(s32[11]{0:T(128)S(4)} %get-tuple-element.99.ints, s32[8,9]{1,0:T(8,128)S(4)} %get-tuple-element.100.index, f32[8,9]{1,0:T(8,128)S(4)} %get-tuple-element.101.signs, f32[2]{0:T(128)S(4)} %get-tuple-element.102.scal, ...), custom_call_target="tpu_custom_call" | custom-call | flops 7247757312 | bytes 56623104 | tf_op jit(solution)/shard_map/scaled/pallas_call | solution.py:420
  34.0 2.0 %collective-permute-start.19 = (bf16[5,64,128]{2,1,0:T(8,128)(2,1)S(1)}, bf16[5,64,128]{2,1,0:T(8,128)(2,1)S(1)}, u32[]{:S(2)}, u32[]{:S(2)}) collective-permute-start(bf16[5,64,128]{2,1,0:T(8,128)(2,1)S(1)} %get-tuple-element.140), channel_id=1, source_target_pairs={{1,4},{4,1},{3,6},{6,3},{5,8},{8,5},{7,10},{10,7},{9,12},{12,9},{1... | collective-permute-start | bytes 245768 | tf_op jit(solution)/shard_map/ppermute | solution.py:399
  36.0 1.5 %scaled.11 = (bf16[8,64,128]{2,1,0:T(8,128)(2,1)S(1)}, bf16[5,64,128]{2,1,0:T(8,128)(2,1)S(1)}, bf16[5,64,128]{2,1,0:T(8,128)(2,1)S(1)}) custom-call(s32[11]{0:T(128)S(4)} %get-tuple-element.99.ints, s32[8,9]{1,0:T(8,128)S(4)} %get-tuple-element.100.index, f32[8,9]{1,0:T(8,128)S(4)} %get-tuple-element.101.signs, f32[2]{0:T(128)S(4)} %get-tuple-element.102.scal, ...), custom_call_target="tpu_custom_call" | custom-call | flops 7247757312 | bytes 56623104 | tf_op jit(solution)/shard_map/scaled/pallas_call | solution.py:420
  37.5 1.9 %collective-permute-start.15 = (bf16[5,64,128]{2,1,0:T(8,128)(2,1)S(1)}, bf16[5,64,128]{2,1,0:T(8,128)(2,1)S(1)}, u32[]{:S(2)}, u32[]{:S(2)}) collective-permute-start(bf16[5,64,128]{2,1,0:T(8,128)(2,1)S(1)} %get-tuple-element.133), channel_id=1, source_target_pairs={{1,4},{4,1},{3,6},{6,3},{5,8},{8,5},{7,10},{10,7},{9,12},{12,9},{1... | collective-permute-start | bytes 245768 | tf_op jit(solution)/shard_map/ppermute | solution.py:399
  40.6 2.0 %collective-permute-start.21 = (bf16[5,64,128]{2,1,0:T(8,128)(2,1)S(1)}, bf16[5,64,128]{2,1,0:T(8,128)(2,1)S(1)}, u32[]{:S(2)}, u32[]{:S(2)}) collective-permute-start(bf16[5,64,128]{2,1,0:T(8,128)(2,1)S(1)} %get-tuple-element.143), channel_id=1, source_target_pairs={{1,4},{4,1},{3,6},{6,3},{5,8},{8,5},{7,10},{10,7},{9,12},{12,9},{1... | collective-permute-start | bytes 245768 | tf_op jit(solution)/shard_map/ppermute | solution.py:399
  44.1 2.0 %collective-permute-start.17 = (bf16[5,64,128]{2,1,0:T(8,128)(2,1)S(1)}, bf16[5,64,128]{2,1,0:T(8,128)(2,1)S(1)}, u32[]{:S(2)}, u32[]{:S(2)}) collective-permute-start(bf16[5,64,128]{2,1,0:T(8,128)(2,1)S(1)} %get-tuple-element.136), channel_id=1, source_target_pairs={{1,4},{4,1},{3,6},{6,3},{5,8},{8,5},{7,10},{10,7},{9,12},{12,9},{1... | collective-permute-start | bytes 245768 | tf_op jit(solution)/shard_map/ppermute | solution.py:399
  47.2 2.2 %collective-permute-start.23 = (bf16[5,64,128]{2,1,0:T(8,128)(2,1)S(1)}, bf16[5,64,128]{2,1,0:T(8,128)(2,1)S(1)}, u32[]{:S(2)}, u32[]{:S(2)}) collective-permute-start(bf16[5,64,128]{2,1,0:T(8,128)(2,1)S(1)} %get-tuple-element.146), channel_id=1, source_target_pairs={{1,4},{4,1},{3,6},{6,3},{5,8},{8,5},{7,10},{10,7},{9,12},{12,9},{1... | collective-permute-start | bytes 245768 | tf_op jit(solution)/shard_map/ppermute | solution.py:399
  49.8 1.1 update.10
  50.9 2.2 %collective-permute-start.25 = (bf16[5,64,128]{2,1,0:T(8,128)(2,1)S(1)}, bf16[5,64,128]{2,1,0:T(8,128)(2,1)S(1)}, u32[]{:S(2)}, u32[]{:S(2)}) collective-permute-start(bf16[5,64,128]{2,1,0:T(8,128)(2,1)S(1)} %get-tuple-element.150), channel_id=1, source_target_pairs={{1,4},{4,1},{3,6},{6,3},{5,8},{8,5},{7,10},{10,7},{9,12},{12,9},{1... | collective-permute-start | bytes 245768 | tf_op jit(solution)/shard_map/ppermute | solution.py:399
  53.1 1.5 %scaled.12 = (bf16[8,64,128]{2,1,0:T(8,128)(2,1)S(1)}, bf16[5,64,128]{2,1,0:T(8,128)(2,1)S(1)}, bf16[5,64,128]{2,1,0:T(8,128)(2,1)S(1)}) custom-call(s32[11]{0:T(128)S(4)} %get-tuple-element.99.ints, s32[8,9]{1,0:T(8,128)S(4)} %get-tuple-element.100.index, f32[8,9]{1,0:T(8,128)S(4)} %get-tuple-element.101.signs, f32[2]{0:T(128)S(4)} %get-tuple-element.102.scal, ...), custom_call_target="tpu_custom_call" | custom-call | flops 7247757312 | bytes 56623104 | tf_op jit(solution)/shard_map/scaled/pallas_call | solution.py:420
  54.6 2.1 %collective-permute-start.31 = (bf16[5,64,128]{2,1,0:T(8,128)(2,1)S(1)}, bf16[5,64,128]{2,1,0:T(8,128)(2,1)S(1)}, u32[]{:S(2)}, u32[]{:S(2)}) collective-permute-start(bf16[5,64,128]{2,1,0:T(8,128)(2,1)S(1)} %get-tuple-element.160), channel_id=1, source_target_pairs={{1,4},{4,1},{3,6},{6,3},{5,8},{8,5},{7,10},{10,7},{9,12},{12,9},{1... | collective-permute-start | bytes 245768 | tf_op jit(solution)/shard_map/ppermute | solution.py:399
  56.7 1.5 %scaled.13 = (bf16[8,64,128]{2,1,0:T(8,128)(2,1)S(1)}, bf16[5,64,128]{2,1,0:T(8,128)(2,1)S(1)}, bf16[5,64,128]{2,1,0:T(8,128)(2,1)S(1)}) custom-call(s32[11]{0:T(128)S(4)} %get-tuple-element.99.ints, s32[8,9]{1,0:T(8,128)S(4)} %get-tuple-element.100.index, f32[8,9]{1,0:T(8,128)S(4)} %get-tuple-element.101.signs, f32[2]{0:T(128)S(4)} %get-tuple-element.102.scal, ...), custom_call_target="tpu_custom_call" | custom-call | flops 7247757312 | bytes 56623104 | tf_op jit(solution)/shard_map/scaled/pallas_call | solution.py:420
  58.2 2.2 %collective-permute-start.27 = (bf16[5,64,128]{2,1,0:T(8,128)(2,1)S(1)}, bf16[5,64,128]{2,1,0:T(8,128)(2,1)S(1)}, u32[]{:S(2)}, u32[]{:S(2)}) collective-permute-start(bf16[5,64,128]{2,1,0:T(8,128)(2,1)S(1)} %get-tuple-element.153), channel_id=1, source_target_pairs={{1,4},{4,1},{3,6},{6,3},{5,8},{8,5},{7,10},{10,7},{9,12},{12,9},{1... | collective-permute-start | bytes 245768 | tf_op jit(solution)/shard_map/ppermute | solution.py:399
  61.3 2.1 %collective-permute-start.33 = (bf16[5,64,128]{2,1,0:T(8,128)(2,1)S(1)}, bf16[5,64,128]{2,1,0:T(8,128)(2,1)S(1)}, u32[]{:S(2)}, u32[]{:S(2)}) collective-permute-start(bf16[5,64,128]{2,1,0:T(8,128)(2,1)S(1)} %get-tuple-element.163), channel_id=1, source_target_pairs={{1,4},{4,1},{3,6},{6,3},{5,8},{8,5},{7,10},{10,7},{9,12},{12,9},{1... | collective-permute-start | bytes 245768 | tf_op jit(solution)/shard_map/ppermute | solution.py:399
  64.8 2.3 %collective-permute-start.29 = (bf16[5,64,128]{2,1,0:T(8,128)(2,1)S(1)}, bf16[5,64,128]{2,1,0:T(8,128)(2,1)S(1)}, u32[]{:S(2)}, u32[]{:S(2)}) collective-permute-start(bf16[5,64,128]{2,1,0:T(8,128)(2,1)S(1)} %get-tuple-element.156), channel_id=1, source_target_pairs={{1,4},{4,1},{3,6},{6,3},{5,8},{8,5},{7,10},{10,7},{9,12},{12,9},{1... | collective-permute-start | bytes 245768 | tf_op jit(solution)/shard_map/ppermute | solution.py:399
  68.1 2.1 %collective-permute-start.35 = (bf16[5,64,128]{2,1,0:T(8,128)(2,1)S(1)}, bf16[5,64,128]{2,1,0:T(8,128)(2,1)S(1)}, u32[]{:S(2)}, u32[]{:S(2)}) collective-permute-start(bf16[5,64,128]{2,1,0:T(8,128)(2,1)S(1)} %get-tuple-element.166), channel_id=1, source_target_pairs={{1,4},{4,1},{3,6},{6,3},{5,8},{8,5},{7,10},{10,7},{9,12},{12,9},{1... | collective-permute-start | bytes 245768 | tf_op jit(solution)/shard_map/ppermute | solution.py:399
  71.4 2.5 %collective-permute-start.37 = (bf16[5,64,128]{2,1,0:T(8,128)(2,1)S(1)}, bf16[5,64,128]{2,1,0:T(8,128)(2,1)S(1)}, u32[]{:S(2)}, u32[]{:S(2)}) collective-permute-start(bf16[5,64,128]{2,1,0:T(8,128)(2,1)S(1)} %get-tuple-element.170), channel_id=1, source_target_pairs={{1,4},{4,1},{3,6},{6,3},{5,8},{8,5},{7,10},{10,7},{9,12},{12,9},{1... | collective-permute-start | bytes 245768 | tf_op jit(solution)/shard_map/ppermute | solution.py:399
  74.0 1.5 %scaled.14 = (bf16[8,64,128]{2,1,0:T(8,128)(2,1)S(1)}, bf16[5,64,128]{2,1,0:T(8,128)(2,1)S(1)}, bf16[5,64,128]{2,1,0:T(8,128)(2,1)S(1)}) custom-call(s32[11]{0:T(128)S(4)} %get-tuple-element.99.ints, s32[8,9]{1,0:T(8,128)S(4)} %get-tuple-element.100.index, f32[8,9]{1,0:T(8,128)S(4)} %get-tuple-element.101.signs, f32[2]{0:T(128)S(4)} %get-tuple-element.102.scal, ...), custom_call_target="tpu_custom_call" | custom-call | flops 7247757312 | bytes 56623104 | tf_op jit(solution)/shard_map/scaled/pallas_call | solution.py:420
  75.5 2.0 %collective-permute-start.43 = (bf16[5,64,128]{2,1,0:T(8,128)(2,1)S(1)}, bf16[5,64,128]{2,1,0:T(8,128)(2,1)S(1)}, u32[]{:S(2)}, u32[]{:S(2)}) collective-permute-start(bf16[5,64,128]{2,1,0:T(8,128)(2,1)S(1)} %get-tuple-element.180), channel_id=1, source_target_pairs={{1,4},{4,1},{3,6},{6,3},{5,8},{8,5},{7,10},{10,7},{9,12},{12,9},{1... | collective-permute-start | bytes 245768 | tf_op jit(solution)/shard_map/ppermute | solution.py:399
  77.5 1.5 %scaled.15 = (bf16[8,64,128]{2,1,0:T(8,128)(2,1)S(1)}, bf16[5,64,128]{2,1,0:T(8,128)(2,1)S(1)}, bf16[5,64,128]{2,1,0:T(8,128)(2,1)S(1)}) custom-call(s32[11]{0:T(128)S(4)} %get-tuple-element.99.ints, s32[8,9]{1,0:T(8,128)S(4)} %get-tuple-element.100.index, f32[8,9]{1,0:T(8,128)S(4)} %get-tuple-element.101.signs, f32[2]{0:T(128)S(4)} %get-tuple-element.102.scal, ...), custom_call_target="tpu_custom_call" | custom-call | flops 7247757312 | bytes 56623104 | tf_op jit(solution)/shard_map/scaled/pallas_call | solution.py:420
  79.0 2.3 %collective-permute-start.39 = (bf16[5,64,128]{2,1,0:T(8,128)(2,1)S(1)}, bf16[5,64,128]{2,1,0:T(8,128)(2,1)S(1)}, u32[]{:S(2)}, u32[]{:S(2)}) collective-permute-start(bf16[5,64,128]{2,1,0:T(8,128)(2,1)S(1)} %get-tuple-element.173), channel_id=1, source_target_pairs={{1,4},{4,1},{3,6},{6,3},{5,8},{8,5},{7,10},{10,7},{9,12},{12,9},{1... | collective-permute-start | bytes 245768 | tf_op jit(solution)/shard_map/ppermute | solution.py:399
  82.2 1.9 %collective-permute-start.45 = (bf16[5,64,128]{2,1,0:T(8,128)(2,1)S(1)}, bf16[5,64,128]{2,1,0:T(8,128)(2,1)S(1)}, u32[]{:S(2)}, u32[]{:S(2)}) collective-permute-start(bf16[5,64,128]{2,1,0:T(8,128)(2,1)S(1)} %get-tuple-element.183), channel_id=1, source_target_pairs={{1,4},{4,1},{3,6},{6,3},{5,8},{8,5},{7,10},{10,7},{9,12},{12,9},{1... | collective-permute-start | bytes 245768 | tf_op jit(solution)/shard_map/ppermute | solution.py:399
  85.6 2.5 %collective-permute-start.41 = (bf16[5,64,128]{2,1,0:T(8,128)(2,1)S(1)}, bf16[5,64,128]{2,1,0:T(8,128)(2,1)S(1)}, u32[]{:S(2)}, u32[]{:S(2)}) collective-permute-start(bf16[5,64,128]{2,1,0:T(8,128)(2,1)S(1)} %get-tuple-element.176), channel_id=1, source_target_pairs={{1,4},{4,1},{3,6},{6,3},{5,8},{8,5},{7,10},{10,7},{9,12},{12,9},{1... | collective-permute-start | bytes 245768 | tf_op jit(solution)/shard_map/ppermute | solution.py:399
  89.2 1.9 %collective-permute-start.47 = (bf16[5,64,128]{2,1,0:T(8,128)(2,1)S(1)}, bf16[5,64,128]{2,1,0:T(8,128)(2,1)S(1)}, u32[]{:S(2)}, u32[]{:S(2)}) collective-permute-start(bf16[5,64,128]{2,1,0:T(8,128)(2,1)S(1)} %get-tuple-element.186), channel_id=1, source_target_pairs={{1,4},{4,1},{3,6},{6,3},{5,8},{8,5},{7,10},{10,7},{9,12},{12,9},{1... | collective-permute-start | bytes 245768 | tf_op jit(solution)/shard_map/ppermute | solution.py:399
  91.1 1.5 %collective-permute-start.49 = (bf16[8,64,128]{2,1,0:T(8,128)(2,1)S(1)}, bf16[8,64,128]{2,1,0:T(8,128)(2,1)S(1)}, u32[]{:S(2)}, u32[]{:S(2)}) collective-permute-start(bf16[8,64,128]{2,1,0:T(8,128)(2,1)S(1)} %get-tuple-element.185.own.refs_2_.refs_4_), channel_id=1, source_target_pairs={{2,0},{3,1},{0,2},{1,3},{6,4},{7,5},{4,6},{5,7},{10,8},{11,9},{8,1... | collective-permute-start | bytes 393224 | tf_op jit(solution)/shard_map/ppermute | solution.py:411
  93.5 1.5 %collective-permute-start.50 = (bf16[5,64,128]{2,1,0:T(8,128)(2,1)S(1)}, bf16[5,64,128]{2,1,0:T(8,128)(2,1)S(1)}, u32[]{:S(2)}, u32[]{:S(2)}) collective-permute-start(bf16[5,64,128]{2,1,0:T(8,128)(2,1)S(1)} %get-tuple-element.190), channel_id=1, source_target_pairs={{1,4},{4,1},{3,6},{6,3},{5,8},{8,5},{7,10},{10,7},{9,12},{12,9},{1... | collective-permute-start | bytes 245768 | tf_op jit(solution)/shard_map/ppermute | solution.py:399
  95.0 1.4 %collective-permute-start.52 = (bf16[8,64,128]{2,1,0:T(8,128)(2,1)S(1)}, bf16[8,64,128]{2,1,0:T(8,128)(2,1)S(1)}, u32[]{:S(2)}, u32[]{:S(2)}) collective-permute-start(bf16[8,64,128]{2,1,0:T(8,128)(2,1)S(1)} %get-tuple-element.189.own.refs_3_.refs_5_), channel_id=1, source_target_pairs={{2,0},{3,1},{0,2},{1,3},{6,4},{7,5},{4,6},{5,7},{10,8},{11,9},{8,1... | collective-permute-start | bytes 393224 | tf_op jit(solution)/shard_map/ppermute | solution.py:411
  97.0 1.5 %images.2.refs_0_ = bf16[2,64,1024]{2,1,0:T(8,128)(2,1)S(1)} custom-call(s32[11]{0:T(128)S(4)} %get-tuple-element.99.ints, s32[8,9]{1,0:T(8,128)S(4)} %get-tuple-element.100.index, f32[8,9]{1,0:T(8,128)S(4)} %get-tuple-element.101.signs, bf16[8,64,128]{2,1,0:T(8,128)(2,1)S(1)} %get-tuple-element.185.own.refs_2_.refs_4_, ...), custom_call_target="tpu_custom_call" | custom-call | flops 7247757312 | bytes 56623104 | tf_op jit(solution)/shard_map/images/pallas_call | solution.py:420
  99.2 1.5 %images.3.refs_1_ = bf16[2,64,1024]{2,1,0:T(8,128)(2,1)S(1)} custom-call(s32[11]{0:T(128)S(4)} %get-tuple-element.99.ints, s32[8,9]{1,0:T(8,128)S(4)} %get-tuple-element.100.index, f32[8,9]{1,0:T(8,128)S(4)} %get-tuple-element.101.signs, bf16[8,64,128]{2,1,0:T(8,128)(2,1)S(1)} %get-tuple-element.189.own.refs_3_.refs_5_, ...), custom_call_target="tpu_custom_call" | custom-call | flops 7247757312 | bytes 56623104 | tf_op jit(solution)/shard_map/images/pallas_call | solution.py:420
  101.4 1.2 collective-permute-done.53.right
  103.2 3.8 %collective-permute-done.54.right = bf16[272,128]{1,0:T(8,128)(2,1)S(1)} collective-permute-done((bf16[272,128]{1,0:T(8,128)(2,1)S(1)}, bf16[272,128]{1,0:T(8,128)(2,1)S(1)}, u32[]{:S(2)}, u32[]{:S(2)}) %collective-permute-start.54) | collective-permute-done | bytes 69664 | tf_op jit(solution)/shard_map/ppermute | solution.py:578
  108.0 5.0 %collective-permute-done.55.right = bf16[272,128]{1,0:T(8,128)(2,1)S(1)} collective-permute-done((bf16[272,128]{1,0:T(8,128)(2,1)S(1)}, bf16[272,128]{1,0:T(8,128)(2,1)S(1)}, u32[]{:S(2)}, u32[]{:S(2)}) %collective-permute-start.55) | collective-permute-done | bytes 69664 | tf_op jit(solution)/shard_map/ppermute | solution.py:578
  113.1 1.2 collective-permute-start.56
  115.3 2.1 %collective-permute-done.56.refs_1_ = bf16[272,128]{1,0:T(8,128)(2,1)S(1)} collective-permute-done((bf16[272,128]{1,0:T(8,128)(2,1)S(1)}, bf16[272,128]{1,0:T(8,128)(2,1)S(1)}, u32[]{:S(2)}, u32[]{:S(2)}) %collective-permute-start.56) | collective-permute-done | bytes 69664 | tf_op jit(solution)/shard_map/ppermute | solution.py:411
  117.5 1.2 collective-permute-done.58.refs_3_
  118.7 9.6 %finish.1 = (bf16[64,2048]{1,0:T(8,128)(2,1)}, f32[64,256]{1,0:T(8,128)}) custom-call(s32[11]{0:T(128)S(4)} %get-tuple-element.99.ints, bf16[272,128]{1,0:T(8,128)(2,1)S(1)} %add.19.refs_0_, bf16[272,128]{1,0:T(8,128)(2,1)S(1)} %collective-permute-done.56.refs_1_, bf16[272,128]{1,0:T(8,128)(2,1)S(1)} %collective-permute-done.57.refs_2_, ...), custom_call_target="tpu_custom_call" | custom-call | flops 36238786560 | bytes 283115520 | tf_op jit(solution)/shard_map/finish/pallas_call | solution.py:420
  (115 shorter events, 24.8 us)
Async XLA Ops:
  2.3 9.1 %collective-permute-start.1 = (bf16[5,64,128]{2,1,0:T(8,128)(2,1)S(1)}, bf16[5,64,128]{2,1,0:T(8,128)(2,1)S(1)}, u32[]{:S(2)}, u32[]{:S(2)}) collective-permute-start(bf16[5,64,128]{2,1,0:T(8,128)(2,1)S(1)} %get-tuple-element.105), channel_id=1, source_target_pairs={{0,4},{1,13},{2,6},{3,15},{4,8},{5,1},{6,10},{7,3},{8,12},{9,5},{1... | collective-permute-start | bytes 245768 | tf_op jit(solution)/shard_map/ppermute | solution.py:407
  5.4 6.5 %collective-permute-start.2 = (bf16[5,64,128]{2,1,0:T(8,128)(2,1)S(1)}, bf16[5,64,128]{2,1,0:T(8,128)(2,1)S(1)}, u32[]{:S(2)}, u32[]{:S(2)}) collective-permute-start(bf16[5,64,128]{2,1,0:T(8,128)(2,1)S(1)} %get-tuple-element.106), channel_id=1, source_target_pairs={{1,4},{4,1},{3,6},{6,3},{5,8},{8,5},{7,10},{10,7},{9,12},{12,9},{1... | collective-permute-start | bytes 245768 | tf_op jit(solution)/shard_map/ppermute | solution.py:399
  7.0 4.9 %collective-permute-start = (bf16[13,64,128]{2,1,0:T(8,128)(2,1)S(1)}, bf16[13,64,128]{2,1,0:T(8,128)(2,1)S(1)}, u32[]{:S(2)}, u32[]{:S(2)}) collective-permute-start(bf16[13,64,128]{2,1,0:T(8,128)(2,1)S(1)} %get-tuple-element.103), channel_id=1, source_target_pairs={{0,1},{1,0},{2,3},{3,2},{4,5},{5,4},{6,7},{7,6},{8,9},{9,8},{10,11... | collective-permute-start | bytes 638984 | tf_op jit(solution)/shard_map/ppermute | solution.py:390
  13.5 5.8 %collective-permute-start.7 = (bf16[5,64,128]{2,1,0:T(8,128)(2,1)S(1)}, bf16[5,64,128]{2,1,0:T(8,128)(2,1)S(1)}, u32[]{:S(2)}, u32[]{:S(2)}) collective-permute-start(bf16[5,64,128]{2,1,0:T(8,128)(2,1)S(1)} %get-tuple-element.120), channel_id=1, source_target_pairs={{1,4},{4,1},{3,6},{6,3},{5,8},{8,5},{7,10},{10,7},{9,12},{12,9},{1... | collective-permute-start | bytes 245768 | tf_op jit(solution)/shard_map/ppermute | solution.py:399
  15.2 4.1 %collective-permute-start.8 = (bf16[5,64,128]{2,1,0:T(8,128)(2,1)S(1)}, bf16[5,64,128]{2,1,0:T(8,128)(2,1)S(1)}, u32[]{:S(2)}, u32[]{:S(2)}) collective-permute-start(bf16[5,64,128]{2,1,0:T(8,128)(2,1)S(1)} %get-tuple-element.121), channel_id=1, source_target_pairs={{0,1},{1,0},{2,3},{3,2},{4,5},{5,4},{6,7},{7,6},{8,9},{9,8},{10,11... | collective-permute-start | bytes 245768 | tf_op jit(solution)/shard_map/ppermute | solution.py:390
  16.7 5.9 %collective-permute-start.3 = (bf16[5,64,128]{2,1,0:T(8,128)(2,1)S(1)}, bf16[5,64,128]{2,1,0:T(8,128)(2,1)S(1)}, u32[]{:S(2)}, u32[]{:S(2)}) collective-permute-start(bf16[5,64,128]{2,1,0:T(8,128)(2,1)S(1)} %get-tuple-element.113), channel_id=1, source_target_pairs={{1,4},{4,1},{3,6},{6,3},{5,8},{8,5},{7,10},{10,7},{9,12},{12,9},{1... | collective-permute-start | bytes 245768 | tf_op jit(solution)/shard_map/ppermute | solution.py:399
  18.6 4.0 %collective-permute-start.4 = (bf16[5,64,128]{2,1,0:T(8,128)(2,1)S(1)}, bf16[5,64,128]{2,1,0:T(8,128)(2,1)S(1)}, u32[]{:S(2)}, u32[]{:S(2)}) collective-permute-start(bf16[5,64,128]{2,1,0:T(8,128)(2,1)S(1)} %get-tuple-element.114), channel_id=1, source_target_pairs={{0,1},{1,0},{2,3},{3,2},{4,5},{5,4},{6,7},{7,6},{8,9},{9,8},{10,11... | collective-permute-start | bytes 245768 | tf_op jit(solution)/shard_map/ppermute | solution.py:390
  20.2 5.7 %collective-permute-start.9 = (bf16[5,64,128]{2,1,0:T(8,128)(2,1)S(1)}, bf16[5,64,128]{2,1,0:T(8,128)(2,1)S(1)}, u32[]{:S(2)}, u32[]{:S(2)}) collective-permute-start(bf16[5,64,128]{2,1,0:T(8,128)(2,1)S(1)} %get-tuple-element.123), channel_id=1, source_target_pairs={{1,4},{4,1},{3,6},{6,3},{5,8},{8,5},{7,10},{10,7},{9,12},{12,9},{1... | collective-permute-start | bytes 245768 | tf_op jit(solution)/shard_map/ppermute | solution.py:399
  21.8 4.1 %collective-permute-start.10 = (bf16[5,64,128]{2,1,0:T(8,128)(2,1)S(1)}, bf16[5,64,128]{2,1,0:T(8,128)(2,1)S(1)}, u32[]{:S(2)}, u32[]{:S(2)}) collective-permute-start(bf16[5,64,128]{2,1,0:T(8,128)(2,1)S(1)} %get-tuple-element.124), channel_id=1, source_target_pairs={{0,1},{1,0},{2,3},{3,2},{4,5},{5,4},{6,7},{7,6},{8,9},{9,8},{10,11... | collective-permute-start | bytes 245768 | tf_op jit(solution)/shard_map/ppermute | solution.py:390
  23.5 5.8 %collective-permute-start.5 = (bf16[5,64,128]{2,1,0:T(8,128)(2,1)S(1)}, bf16[5,64,128]{2,1,0:T(8,128)(2,1)S(1)}, u32[]{:S(2)}, u32[]{:S(2)}) collective-permute-start(bf16[5,64,128]{2,1,0:T(8,128)(2,1)S(1)} %get-tuple-element.116), channel_id=1, source_target_pairs={{1,4},{4,1},{3,6},{6,3},{5,8},{8,5},{7,10},{10,7},{9,12},{12,9},{1... | collective-permute-start | bytes 245768 | tf_op jit(solution)/shard_map/ppermute | solution.py:399
  25.4 3.8 %collective-permute-start.6 = (bf16[5,64,128]{2,1,0:T(8,128)(2,1)S(1)}, bf16[5,64,128]{2,1,0:T(8,128)(2,1)S(1)}, u32[]{:S(2)}, u32[]{:S(2)}) collective-permute-start(bf16[5,64,128]{2,1,0:T(8,128)(2,1)S(1)} %get-tuple-element.117), channel_id=1, source_target_pairs={{0,1},{1,0},{2,3},{3,2},{4,5},{5,4},{6,7},{7,6},{8,9},{9,8},{10,11... | collective-permute-start | bytes 245768 | tf_op jit(solution)/shard_map/ppermute | solution.py:390
  26.8 5.7 %collective-permute-start.11 = (bf16[5,64,128]{2,1,0:T(8,128)(2,1)S(1)}, bf16[5,64,128]{2,1,0:T(8,128)(2,1)S(1)}, u32[]{:S(2)}, u32[]{:S(2)}) collective-permute-start(bf16[5,64,128]{2,1,0:T(8,128)(2,1)S(1)} %get-tuple-element.126), channel_id=1, source_target_pairs={{1,4},{4,1},{3,6},{6,3},{5,8},{8,5},{7,10},{10,7},{9,12},{12,9},{1... | collective-permute-start | bytes 245768 | tf_op jit(solution)/shard_map/ppermute | solution.py:399
  28.6 3.9 %collective-permute-start.12 = (bf16[5,64,128]{2,1,0:T(8,128)(2,1)S(1)}, bf16[5,64,128]{2,1,0:T(8,128)(2,1)S(1)}, u32[]{:S(2)}, u32[]{:S(2)}) collective-permute-start(bf16[5,64,128]{2,1,0:T(8,128)(2,1)S(1)} %get-tuple-element.127), channel_id=1, source_target_pairs={{0,1},{1,0},{2,3},{3,2},{4,5},{5,4},{6,7},{7,6},{8,9},{9,8},{10,11... | collective-permute-start | bytes 245768 | tf_op jit(solution)/shard_map/ppermute | solution.py:390
  30.1 5.9 %collective-permute-start.13 = (bf16[5,64,128]{2,1,0:T(8,128)(2,1)S(1)}, bf16[5,64,128]{2,1,0:T(8,128)(2,1)S(1)}, u32[]{:S(2)}, u32[]{:S(2)}) collective-permute-start(bf16[5,64,128]{2,1,0:T(8,128)(2,1)S(1)} %get-tuple-element.130), channel_id=1, source_target_pairs={{1,4},{4,1},{3,6},{6,3},{5,8},{8,5},{7,10},{10,7},{9,12},{12,9},{1... | collective-permute-start | bytes 245768 | tf_op jit(solution)/shard_map/ppermute | solution.py:399
  32.1 3.9 %collective-permute-start.14 = (bf16[5,64,128]{2,1,0:T(8,128)(2,1)S(1)}, bf16[5,64,128]{2,1,0:T(8,128)(2,1)S(1)}, u32[]{:S(2)}, u32[]{:S(2)}) collective-permute-start(bf16[5,64,128]{2,1,0:T(8,128)(2,1)S(1)} %get-tuple-element.131), channel_id=1, source_target_pairs={{0,1},{1,0},{2,3},{3,2},{4,5},{5,4},{6,7},{7,6},{8,9},{9,8},{10,11... | collective-permute-start | bytes 245768 | tf_op jit(solution)/shard_map/ppermute | solution.py:390
  34.0 5.7 %collective-permute-start.19 = (bf16[5,64,128]{2,1,0:T(8,128)(2,1)S(1)}, bf16[5,64,128]{2,1,0:T(8,128)(2,1)S(1)}, u32[]{:S(2)}, u32[]{:S(2)}) collective-permute-start(bf16[5,64,128]{2,1,0:T(8,128)(2,1)S(1)} %get-tuple-element.140), channel_id=1, source_target_pairs={{1,4},{4,1},{3,6},{6,3},{5,8},{8,5},{7,10},{10,7},{9,12},{12,9},{1... | collective-permute-start | bytes 245768 | tf_op jit(solution)/shard_map/ppermute | solution.py:399
  36.0 3.8 %collective-permute-start.20 = (bf16[5,64,128]{2,1,0:T(8,128)(2,1)S(1)}, bf16[5,64,128]{2,1,0:T(8,128)(2,1)S(1)}, u32[]{:S(2)}, u32[]{:S(2)}) collective-permute-start(bf16[5,64,128]{2,1,0:T(8,128)(2,1)S(1)} %get-tuple-element.141), channel_id=1, source_target_pairs={{0,1},{1,0},{2,3},{3,2},{4,5},{5,4},{6,7},{7,6},{8,9},{9,8},{10,11... | collective-permute-start | bytes 245768 | tf_op jit(solution)/shard_map/ppermute | solution.py:390
  37.5 5.7 %collective-permute-start.15 = (bf16[5,64,128]{2,1,0:T(8,128)(2,1)S(1)}, bf16[5,64,128]{2,1,0:T(8,128)(2,1)S(1)}, u32[]{:S(2)}, u32[]{:S(2)}) collective-permute-start(bf16[5,64,128]{2,1,0:T(8,128)(2,1)S(1)} %get-tuple-element.133), channel_id=1, source_target_pairs={{1,4},{4,1},{3,6},{6,3},{5,8},{8,5},{7,10},{10,7},{9,12},{12,9},{1... | collective-permute-start | bytes 245768 | tf_op jit(solution)/shard_map/ppermute | solution.py:399
  39.4 3.8 %collective-permute-start.16 = (bf16[5,64,128]{2,1,0:T(8,128)(2,1)S(1)}, bf16[5,64,128]{2,1,0:T(8,128)(2,1)S(1)}, u32[]{:S(2)}, u32[]{:S(2)}) collective-permute-start(bf16[5,64,128]{2,1,0:T(8,128)(2,1)S(1)} %get-tuple-element.134), channel_id=1, source_target_pairs={{0,1},{1,0},{2,3},{3,2},{4,5},{5,4},{6,7},{7,6},{8,9},{9,8},{10,11... | collective-permute-start | bytes 245768 | tf_op jit(solution)/shard_map/ppermute | solution.py:390
  40.6 5.7 %collective-permute-start.21 = (bf16[5,64,128]{2,1,0:T(8,128)(2,1)S(1)}, bf16[5,64,128]{2,1,0:T(8,128)(2,1)S(1)}, u32[]{:S(2)}, u32[]{:S(2)}) collective-permute-start(bf16[5,64,128]{2,1,0:T(8,128)(2,1)S(1)} %get-tuple-element.143), channel_id=1, source_target_pairs={{1,4},{4,1},{3,6},{6,3},{5,8},{8,5},{7,10},{10,7},{9,12},{12,9},{1... | collective-permute-start | bytes 245768 | tf_op jit(solution)/shard_map/ppermute | solution.py:399
  44.1 5.7 %collective-permute-start.17 = (bf16[5,64,128]{2,1,0:T(8,128)(2,1)S(1)}, bf16[5,64,128]{2,1,0:T(8,128)(2,1)S(1)}, u32[]{:S(2)}, u32[]{:S(2)}) collective-permute-start(bf16[5,64,128]{2,1,0:T(8,128)(2,1)S(1)} %get-tuple-element.136), channel_id=1, source_target_pairs={{1,4},{4,1},{3,6},{6,3},{5,8},{8,5},{7,10},{10,7},{9,12},{12,9},{1... | collective-permute-start | bytes 245768 | tf_op jit(solution)/shard_map/ppermute | solution.py:399
  47.2 5.9 %collective-permute-start.23 = (bf16[5,64,128]{2,1,0:T(8,128)(2,1)S(1)}, bf16[5,64,128]{2,1,0:T(8,128)(2,1)S(1)}, u32[]{:S(2)}, u32[]{:S(2)}) collective-permute-start(bf16[5,64,128]{2,1,0:T(8,128)(2,1)S(1)} %get-tuple-element.146), channel_id=1, source_target_pairs={{1,4},{4,1},{3,6},{6,3},{5,8},{8,5},{7,10},{10,7},{9,12},{12,9},{1... | collective-permute-start | bytes 245768 | tf_op jit(solution)/shard_map/ppermute | solution.py:399
  50.9 5.8 %collective-permute-start.25 = (bf16[5,64,128]{2,1,0:T(8,128)(2,1)S(1)}, bf16[5,64,128]{2,1,0:T(8,128)(2,1)S(1)}, u32[]{:S(2)}, u32[]{:S(2)}) collective-permute-start(bf16[5,64,128]{2,1,0:T(8,128)(2,1)S(1)} %get-tuple-element.150), channel_id=1, source_target_pairs={{1,4},{4,1},{3,6},{6,3},{5,8},{8,5},{7,10},{10,7},{9,12},{12,9},{1... | collective-permute-start | bytes 245768 | tf_op jit(solution)/shard_map/ppermute | solution.py:399
  54.6 5.8 %collective-permute-start.31 = (bf16[5,64,128]{2,1,0:T(8,128)(2,1)S(1)}, bf16[5,64,128]{2,1,0:T(8,128)(2,1)S(1)}, u32[]{:S(2)}, u32[]{:S(2)}) collective-permute-start(bf16[5,64,128]{2,1,0:T(8,128)(2,1)S(1)} %get-tuple-element.160), channel_id=1, source_target_pairs={{1,4},{4,1},{3,6},{6,3},{5,8},{8,5},{7,10},{10,7},{9,12},{12,9},{1... | collective-permute-start | bytes 245768 | tf_op jit(solution)/shard_map/ppermute | solution.py:399
  58.2 5.7 %collective-permute-start.27 = (bf16[5,64,128]{2,1,0:T(8,128)(2,1)S(1)}, bf16[5,64,128]{2,1,0:T(8,128)(2,1)S(1)}, u32[]{:S(2)}, u32[]{:S(2)}) collective-permute-start(bf16[5,64,128]{2,1,0:T(8,128)(2,1)S(1)} %get-tuple-element.153), channel_id=1, source_target_pairs={{1,4},{4,1},{3,6},{6,3},{5,8},{8,5},{7,10},{10,7},{9,12},{12,9},{1... | collective-permute-start | bytes 245768 | tf_op jit(solution)/shard_map/ppermute | solution.py:399
  61.3 5.9 %collective-permute-start.33 = (bf16[5,64,128]{2,1,0:T(8,128)(2,1)S(1)}, bf16[5,64,128]{2,1,0:T(8,128)(2,1)S(1)}, u32[]{:S(2)}, u32[]{:S(2)}) collective-permute-start(bf16[5,64,128]{2,1,0:T(8,128)(2,1)S(1)} %get-tuple-element.163), channel_id=1, source_target_pairs={{1,4},{4,1},{3,6},{6,3},{5,8},{8,5},{7,10},{10,7},{9,12},{12,9},{1... | collective-permute-start | bytes 245768 | tf_op jit(solution)/shard_map/ppermute | solution.py:399
  63.3 3.8 %collective-permute-start.34 = (bf16[5,64,128]{2,1,0:T(8,128)(2,1)S(1)}, bf16[5,64,128]{2,1,0:T(8,128)(2,1)S(1)}, u32[]{:S(2)}, u32[]{:S(2)}) collective-permute-start(bf16[5,64,128]{2,1,0:T(8,128)(2,1)S(1)} %get-tuple-element.164), channel_id=1, source_target_pairs={{0,1},{1,0},{2,3},{3,2},{4,5},{5,4},{6,7},{7,6},{8,9},{9,8},{10,11... | collective-permute-start | bytes 245768 | tf_op jit(solution)/shard_map/ppermute | solution.py:390
  64.8 5.7 %collective-permute-start.29 = (bf16[5,64,128]{2,1,0:T(8,128)(2,1)S(1)}, bf16[5,64,128]{2,1,0:T(8,128)(2,1)S(1)}, u32[]{:S(2)}, u32[]{:S(2)}) collective-permute-start(bf16[5,64,128]{2,1,0:T(8,128)(2,1)S(1)} %get-tuple-element.156), channel_id=1, source_target_pairs={{1,4},{4,1},{3,6},{6,3},{5,8},{8,5},{7,10},{10,7},{9,12},{12,9},{1... | collective-permute-start | bytes 245768 | tf_op jit(solution)/shard_map/ppermute | solution.py:399
  68.1 5.9 %collective-permute-start.35 = (bf16[5,64,128]{2,1,0:T(8,128)(2,1)S(1)}, bf16[5,64,128]{2,1,0:T(8,128)(2,1)S(1)}, u32[]{:S(2)}, u32[]{:S(2)}) collective-permute-start(bf16[5,64,128]{2,1,0:T(8,128)(2,1)S(1)} %get-tuple-element.166), channel_id=1, source_target_pairs={{1,4},{4,1},{3,6},{6,3},{5,8},{8,5},{7,10},{10,7},{9,12},{12,9},{1... | collective-permute-start | bytes 245768 | tf_op jit(solution)/shard_map/ppermute | solution.py:399
  70.1 3.8 %collective-permute-start.36 = (bf16[5,64,128]{2,1,0:T(8,128)(2,1)S(1)}, bf16[5,64,128]{2,1,0:T(8,128)(2,1)S(1)}, u32[]{:S(2)}, u32[]{:S(2)}) collective-permute-start(bf16[5,64,128]{2,1,0:T(8,128)(2,1)S(1)} %get-tuple-element.167), channel_id=1, source_target_pairs={{0,1},{1,0},{2,3},{3,2},{4,5},{5,4},{6,7},{7,6},{8,9},{9,8},{10,11... | collective-permute-start | bytes 245768 | tf_op jit(solution)/shard_map/ppermute | solution.py:390
  71.4 6.1 %collective-permute-start.37 = (bf16[5,64,128]{2,1,0:T(8,128)(2,1)S(1)}, bf16[5,64,128]{2,1,0:T(8,128)(2,1)S(1)}, u32[]{:S(2)}, u32[]{:S(2)}) collective-permute-start(bf16[5,64,128]{2,1,0:T(8,128)(2,1)S(1)} %get-tuple-element.170), channel_id=1, source_target_pairs={{1,4},{4,1},{3,6},{6,3},{5,8},{8,5},{7,10},{10,7},{9,12},{12,9},{1... | collective-permute-start | bytes 245768 | tf_op jit(solution)/shard_map/ppermute | solution.py:399
  75.5 5.9 %collective-permute-start.43 = (bf16[5,64,128]{2,1,0:T(8,128)(2,1)S(1)}, bf16[5,64,128]{2,1,0:T(8,128)(2,1)S(1)}, u32[]{:S(2)}, u32[]{:S(2)}) collective-permute-start(bf16[5,64,128]{2,1,0:T(8,128)(2,1)S(1)} %get-tuple-element.180), channel_id=1, source_target_pairs={{1,4},{4,1},{3,6},{6,3},{5,8},{8,5},{7,10},{10,7},{9,12},{12,9},{1... | collective-permute-start | bytes 245768 | tf_op jit(solution)/shard_map/ppermute | solution.py:399
  77.5 3.8 %collective-permute-start.44 = (bf16[5,64,128]{2,1,0:T(8,128)(2,1)S(1)}, bf16[5,64,128]{2,1,0:T(8,128)(2,1)S(1)}, u32[]{:S(2)}, u32[]{:S(2)}) collective-permute-start(bf16[5,64,128]{2,1,0:T(8,128)(2,1)S(1)} %get-tuple-element.181), channel_id=1, source_target_pairs={{0,1},{1,0},{2,3},{3,2},{4,5},{5,4},{6,7},{7,6},{8,9},{9,8},{10,11... | collective-permute-start | bytes 245768 | tf_op jit(solution)/shard_map/ppermute | solution.py:390
  79.0 5.7 %collective-permute-start.39 = (bf16[5,64,128]{2,1,0:T(8,128)(2,1)S(1)}, bf16[5,64,128]{2,1,0:T(8,128)(2,1)S(1)}, u32[]{:S(2)}, u32[]{:S(2)}) collective-permute-start(bf16[5,64,128]{2,1,0:T(8,128)(2,1)S(1)} %get-tuple-element.173), channel_id=1, source_target_pairs={{1,4},{4,1},{3,6},{6,3},{5,8},{8,5},{7,10},{10,7},{9,12},{12,9},{1... | collective-permute-start | bytes 245768 | tf_op jit(solution)/shard_map/ppermute | solution.py:399
  82.2 5.9 %collective-permute-start.45 = (bf16[5,64,128]{2,1,0:T(8,128)(2,1)S(1)}, bf16[5,64,128]{2,1,0:T(8,128)(2,1)S(1)}, u32[]{:S(2)}, u32[]{:S(2)}) collective-permute-start(bf16[5,64,128]{2,1,0:T(8,128)(2,1)S(1)} %get-tuple-element.183), channel_id=1, source_target_pairs={{1,4},{4,1},{3,6},{6,3},{5,8},{8,5},{7,10},{10,7},{9,12},{12,9},{1... | collective-permute-start | bytes 245768 | tf_op jit(solution)/shard_map/ppermute | solution.py:399
  84.1 4.0 %collective-permute-start.46 = (bf16[5,64,128]{2,1,0:T(8,128)(2,1)S(1)}, bf16[5,64,128]{2,1,0:T(8,128)(2,1)S(1)}, u32[]{:S(2)}, u32[]{:S(2)}) collective-permute-start(bf16[5,64,128]{2,1,0:T(8,128)(2,1)S(1)} %get-tuple-element.184), channel_id=1, source_target_pairs={{0,1},{1,0},{2,3},{3,2},{4,5},{5,4},{6,7},{7,6},{8,9},{9,8},{10,11... | collective-permute-start | bytes 245768 | tf_op jit(solution)/shard_map/ppermute | solution.py:390
  85.6 7.0 %collective-permute-start.41 = (bf16[5,64,128]{2,1,0:T(8,128)(2,1)S(1)}, bf16[5,64,128]{2,1,0:T(8,128)(2,1)S(1)}, u32[]{:S(2)}, u32[]{:S(2)}) collective-permute-start(bf16[5,64,128]{2,1,0:T(8,128)(2,1)S(1)} %get-tuple-element.176), channel_id=1, source_target_pairs={{1,4},{4,1},{3,6},{6,3},{5,8},{8,5},{7,10},{10,7},{9,12},{12,9},{1... | collective-permute-start | bytes 245768 | tf_op jit(solution)/shard_map/ppermute | solution.py:399
  88.1 4.5 %collective-permute-start.42 = (bf16[5,64,128]{2,1,0:T(8,128)(2,1)S(1)}, bf16[5,64,128]{2,1,0:T(8,128)(2,1)S(1)}, u32[]{:S(2)}, u32[]{:S(2)}) collective-permute-start(bf16[5,64,128]{2,1,0:T(8,128)(2,1)S(1)} %get-tuple-element.177), channel_id=1, source_target_pairs={{0,1},{1,0},{2,3},{3,2},{4,5},{5,4},{6,7},{7,6},{8,9},{9,8},{10,11... | collective-permute-start | bytes 245768 | tf_op jit(solution)/shard_map/ppermute | solution.py:390
  89.2 5.8 %collective-permute-start.47 = (bf16[5,64,128]{2,1,0:T(8,128)(2,1)S(1)}, bf16[5,64,128]{2,1,0:T(8,128)(2,1)S(1)}, u32[]{:S(2)}, u32[]{:S(2)}) collective-permute-start(bf16[5,64,128]{2,1,0:T(8,128)(2,1)S(1)} %get-tuple-element.186), channel_id=1, source_target_pairs={{1,4},{4,1},{3,6},{6,3},{5,8},{8,5},{7,10},{10,7},{9,12},{12,9},{1... | collective-permute-start | bytes 245768 | tf_op jit(solution)/shard_map/ppermute | solution.py:399
  91.1 5.3 %collective-permute-start.48 = (bf16[5,64,128]{2,1,0:T(8,128)(2,1)S(1)}, bf16[5,64,128]{2,1,0:T(8,128)(2,1)S(1)}, u32[]{:S(2)}, u32[]{:S(2)}) collective-permute-start(bf16[5,64,128]{2,1,0:T(8,128)(2,1)S(1)} %get-tuple-element.187), channel_id=1, source_target_pairs={{0,1},{1,0},{2,3},{3,2},{4,5},{5,4},{6,7},{7,6},{8,9},{9,8},{10,11... | collective-permute-start | bytes 245768 | tf_op jit(solution)/shard_map/ppermute | solution.py:390
  91.1 5.9 %collective-permute-start.49 = (bf16[8,64,128]{2,1,0:T(8,128)(2,1)S(1)}, bf16[8,64,128]{2,1,0:T(8,128)(2,1)S(1)}, u32[]{:S(2)}, u32[]{:S(2)}) collective-permute-start(bf16[8,64,128]{2,1,0:T(8,128)(2,1)S(1)} %get-tuple-element.185.own.refs_2_.refs_4_), channel_id=1, source_target_pairs={{2,0},{3,1},{0,2},{1,3},{6,4},{7,5},{4,6},{5,7},{10,8},{11,9},{8,1... | collective-permute-start | bytes 393224 | tf_op jit(solution)/shard_map/ppermute | solution.py:411
  93.5 5.7 %collective-permute-start.50 = (bf16[5,64,128]{2,1,0:T(8,128)(2,1)S(1)}, bf16[5,64,128]{2,1,0:T(8,128)(2,1)S(1)}, u32[]{:S(2)}, u32[]{:S(2)}) collective-permute-start(bf16[5,64,128]{2,1,0:T(8,128)(2,1)S(1)} %get-tuple-element.190), channel_id=1, source_target_pairs={{1,4},{4,1},{3,6},{6,3},{5,8},{8,5},{7,10},{10,7},{9,12},{12,9},{1... | collective-permute-start | bytes 245768 | tf_op jit(solution)/shard_map/ppermute | solution.py:399
  94.9 4.3 %collective-permute-start.51 = (bf16[5,64,128]{2,1,0:T(8,128)(2,1)S(1)}, bf16[5,64,128]{2,1,0:T(8,128)(2,1)S(1)}, u32[]{:S(2)}, u32[]{:S(2)}) collective-permute-start(bf16[5,64,128]{2,1,0:T(8,128)(2,1)S(1)} %get-tuple-element.191), channel_id=1, source_target_pairs={{0,1},{1,0},{2,3},{3,2},{4,5},{5,4},{6,7},{7,6},{8,9},{9,8},{10,11... | collective-permute-start | bytes 245768 | tf_op jit(solution)/shard_map/ppermute | solution.py:390
  95.0 5.9 %collective-permute-start.52 = (bf16[8,64,128]{2,1,0:T(8,128)(2,1)S(1)}, bf16[8,64,128]{2,1,0:T(8,128)(2,1)S(1)}, u32[]{:S(2)}, u32[]{:S(2)}) collective-permute-start(bf16[8,64,128]{2,1,0:T(8,128)(2,1)S(1)} %get-tuple-element.189.own.refs_3_.refs_5_), channel_id=1, source_target_pairs={{2,0},{3,1},{0,2},{1,3},{6,4},{7,5},{4,6},{5,7},{10,8},{11,9},{8,1... | collective-permute-start | bytes 393224 | tf_op jit(solution)/shard_map/ppermute | solution.py:411
  102.7 4.4 %collective-permute-start.54 = (bf16[272,128]{1,0:T(8,128)(2,1)S(1)}, bf16[272,128]{1,0:T(8,128)(2,1)S(1)}, u32[]{:S(2)}, u32[]{:S(2)}) collective-permute-start(bf16[272,128]{1,0:T(8,128)(2,1)S(1)} %add.17.left), channel_id=1, source_target_pairs={{0,4},{4,0},{8,12},{12,8},{1,5},{5,1},{9,13},{13,9},{2,6},{6,2},{1... | collective-permute-start | bytes 208904 | tf_op jit(solution)/shard_map/ppermute | solution.py:578
  107.1 5.9 %collective-permute-start.55 = (bf16[272,128]{1,0:T(8,128)(2,1)S(1)}, bf16[272,128]{1,0:T(8,128)(2,1)S(1)}, u32[]{:S(2)}, u32[]{:S(2)}) collective-permute-start(bf16[272,128]{1,0:T(8,128)(2,1)S(1)} %add.18.left), channel_id=1, source_target_pairs={{0,8},{4,12},{8,0},{12,4},{1,9},{5,13},{9,1},{13,5},{2,10},{6,14},... | collective-permute-start | bytes 208904 | tf_op jit(solution)/shard_map/ppermute | solution.py:578
  108.0 6.8 %collective-permute-start.59 = (bf16[8,64,128]{2,1,0:T(8,128)(2,1)S(1)}, bf16[8,64,128]{2,1,0:T(8,128)(2,1)S(1)}, u32[]{:S(2)}, u32[]{:S(2)}) collective-permute-start(bf16[8,64,128]{2,1,0:T(8,128)(2,1)S(1)} %get-tuple-element.185.own.refs_2_.refs_4_), channel_id=1, source_target_pairs={{0,1},{1,0},{2,3},{3,2},{4,5},{5,4},{6,7},{7,6},{8,9},{9,8},{10,11... | collective-permute-start | bytes 393224 | tf_op jit(solution)/shard_map/ppermute | solution.py:390
  113.1 4.4 %collective-permute-start.56 = (bf16[272,128]{1,0:T(8,128)(2,1)S(1)}, bf16[272,128]{1,0:T(8,128)(2,1)S(1)}, u32[]{:S(2)}, u32[]{:S(2)}) collective-permute-start(bf16[272,128]{1,0:T(8,128)(2,1)S(1)} %add.19.refs_0_), channel_id=1, source_target_pairs={{2,0},{3,1},{0,2},{1,3},{6,4},{7,5},{4,6},{5,7},{10,8},{11,9},{8,1... | collective-permute-start | bytes 208904 | tf_op jit(solution)/shard_map/ppermute | solution.py:411
  (15 other events, 46.4 us)

commit v5 on v4

--- a/solution.py
+++ b/solution.py
@@ -14,6 +14,7 @@
 SLOWER = 24
 SUBLANES = 8
 DIAGONAL_ROWS = 16
+DEVICE_ROW = 3
 
 BF16 = jnp.bfloat16
 F32 = jnp.float32
@@ -115,12 +116,13 @@
     scal[1] = width[0]
     for i in range(3):
         place[i] = ints[i]
+    place[DEVICE_ROW] = ints[4]
     for copy in small:
         copy.wait()
     start = ints[3] + first
 
     def fill(row, _):
-        place[3 + row] = sizes_here[first + row]
+        place[4 + row] = sizes_here[first + row]
         for slot in range(slots):
             away = columns_here[first + row, slot] - (start + row) + HALF_BAND
             away = jnp.where(away < 0, away + total, away)
@@ -169,7 +171,7 @@
         filtered = scaled[row].astype(F32) + own[row].astype(F32) - image
         if not first:
             filtered = 2.0 * filtered - previous[row].astype(F32)
-        out[row] = jnp.where(lane < ints[3 + row], filtered, 0.0).astype(BF16)
+        out[row] = jnp.where(lane < ints[4 + row], filtered, 0.0).astype(BF16)
     send_ends(core, out, intra_out, inter_out)
 
 
@@ -226,6 +228,21 @@
     body = left.shape[0] - DIAGONAL_ROWS
     out[:body] = (left[:body, :].astype(F32) + right[:body, :].astype(F32)).astype(BF16)
     out[body:] = diagonal_parts(diagonal_of(left) + diagonal_of(right))
+
+
+def sum_kernel(ints, *refs):
+    *payloads, out, held = refs
+    count = len(payloads)
+    for step, payload in enumerate(payloads):
+        held[lax.rem(ints[DEVICE_ROW] + count - step, count)] = payload[...]
+    body = out.shape[0] - DIAGONAL_ROWS
+    total = held[0, :body, :].astype(F32)
+    diagonal = diagonal_of(held.at[0])
+    for r in range(1, count):
+        total = total + held[r, :body, :].astype(F32)
+        diagonal = diagonal + diagonal_of(held.at[r])
+    out[:body] = total.astype(BF16)
+    out[body:] = diagonal_parts(diagonal)
 
 
 def split3(value):
@@ -439,7 +456,7 @@
     def scalars(value):
         return pltpu.with_memory_space_constraint(value, pltpu.SMEM)
 
-    ints = scalars(jnp.stack([core, chip, col, row * blocks_dev]).astype(jnp.int32))
+    ints = scalars(jnp.stack([core, chip, col, row * blocks_dev, row]).astype(jnp.int32))
     shift, halfwidth = scalars(shift), scalars(halfwidth)
 
     def stays(value):
@@ -471,7 +488,7 @@
             matrix,
             pltpu.SMEM((half, slots), jnp.int32),
             pltpu.SMEM((half, slots), F32),
-            pltpu.SMEM((3 + half,), jnp.int32),
+            pltpu.SMEM((4 + half,), jnp.int32),
             pltpu.SMEM((2,), F32),
         ),
         in_specs=[SMEM] * 3 + [HBM] * 5,
@@ -567,7 +584,21 @@
         return call(add_kernel, "add", (), (left, right), (payload,), [], row_flops // 8)[0]
 
     summed = add(keep, swap_cores(send))
-    if num_rows & (num_rows - 1):
+    if num_rows <= 4:
+        others = [
+            lax.ppermute(summed, "row", [(r, (r + step) % num_rows) for r in range(num_rows)])
+            for step in range(1, num_rows)
+        ]
+        (summed,) = call(
+            sum_kernel,
+            "sum",
+            (place,),
+            (summed, *others),
+            (payload,),
+            [pltpu.VMEM((num_rows, *payload.shape), BF16)],
+            row_flops // 8,
+        )
+    elif num_rows & (num_rows - 1):
         every = lax.all_gather(summed, "row")
         summed = every[0]
         for r in range(1, num_rows):

time: 129 us -> 128 us (level)
  waiting for transfers between devices: 21.6 us -> 19 us
  starting transfers between devices: 60.4 us -> 62 us
    ppermute x2 -> x3, waiting for transfers between devices: 8.86 us -> 6.44 us  [local(): lax.ppermute(summed, 'row', [(r, (r + step) % num_rows) for r in range(nu...]
    ppermute x2 -> x3, starting transfers between devices: 1.43 us -> 2.92 us  [local(): lax.ppermute(summed, 'row', [(r, (r + step) % num_rows) for r in range(nu...]
    pallas_call x31 -> x30, Pallas kernels: 39.3 us -> 39.3 us  [call(): pl.pallas_call(kernel, name=name, out_shape=outs, in_specs=[SMEM] * len(s...]
  transfers between devices with their start and end apart: 63 -> 64, of which waited for: 21 -> 21; matrix products, arithmetic and copies ran while one was open for 0% -> 0% of each run, Pallas kernels for 24% -> 24%
where the time goes in v5:
time: 128 us; the launch traced here: 127 us
  starting transfers between devices  62 us (48%)
  Pallas kernels  43.9 us (34%)
  waiting for transfers between devices  19 us (15%)
  between operations  2.31 us (2%)
    ppermute x25, starting transfers between devices, swap_chips(): return lax.ppermute(value, ('row', 'col'), pairs)  50.4 us
    pallas_call x30, Pallas kernels, call(): pl.pallas_call(kernel, name=name, out_shape=outs, in_specs=[SMEM] * len(s...  39.3 us
    ppermute x25, waiting for transfers between devices, swap_chips(): return lax.ppermute(value, ('row', 'col'), pairs)  7.38 us
    ppermute x3, waiting for transfers between devices, local(): lax.ppermute(summed, 'row', [(r, (r + step) % num_rows) for r in range(nu...  6.44 us
    ppermute x3, starting transfers between devices, from_chip(): return lax.ppermute(value, 'col', pairs)  4.41 us
    ppermute x1, starting transfers between devices, next_chips(): return lax.ppermute(value, ('row', 'col'), pairs)  3.08 us
    pallas_call x1, Pallas kernels, local(): pl.pallas_call(functools.partial(load_kernel, total_blocks), name='load',...  3.01 us
    ppermute x3, starting transfers between devices, local(): lax.ppermute(summed, 'row', [(r, (r + step) % num_rows) for r in range(nu...  2.92 us
  transfers between devices with their start and end apart: 64, of which 21 were waited for; matrix products, arithmetic and copies ran while one was open for 0% of the time, Pallas kernels for 24%

profile of v5, /device:TPU:0, one launch (start us, length us, event | category | flops | bytes accessed | tf_op | source)
XLA Modules:
  0.0 127.4 jit_solution(17754917565146954987)
XLA Ops:
  0.7 1.6 %cut.1 = (bf16[8,64,128]{2,1,0:T(8,128)(2,1)S(1)}, bf16[5,64,128]{2,1,0:T(8,128)(2,1)S(1)}, bf16[13,64,128]{2,1,0:T(8,128)(2,1)S(1)}, bf16[5,64,128]{2,1,0:T(8,128)(2,1)S(1)}, bf16[5,64,128]{2,1,0:T(8,128)(2,1)S(1)}) custom-call(s32[5]{0:T(128)S(1)} %stack.23.ints, s32[16]{0:T(128)} %sizes.3, bf16[64,2048]{1,0:T(8,128)(2,1)} %trial.1), custom_call_target="tpu_custom_call" | custom-call | tf_op jit(solution)/shard_map/cut/pallas_call | solution.py:466
  2.3 3.1 %collective-permute-start.1 = (bf16[5,64,128]{2,1,0:T(8,128)(2,1)S(1)}, bf16[5,64,128]{2,1,0:T(8,128)(2,1)S(1)}, u32[]{:S(2)}, u32[]{:S(2)}) collective-permute-start(bf16[5,64,128]{2,1,0:T(8,128)(2,1)S(1)} %get-tuple-element.105), channel_id=1, source_target_pairs={{0,4},{1,13},{2,6},{3,15},{4,8},{5,1},{6,10},{7,3},{8,12},{9,5},{1... | collective-permute-start | bytes 245768 | tf_op jit(solution)/shard_map/ppermute | solution.py:424
  5.4 1.6 %collective-permute-start.2 = (bf16[5,64,128]{2,1,0:T(8,128)(2,1)S(1)}, bf16[5,64,128]{2,1,0:T(8,128)(2,1)S(1)}, u32[]{:S(2)}, u32[]{:S(2)}) collective-permute-start(bf16[5,64,128]{2,1,0:T(8,128)(2,1)S(1)} %get-tuple-element.106), channel_id=1, source_target_pairs={{1,4},{4,1},{3,6},{6,3},{5,8},{8,5},{7,10},{10,7},{9,12},{12,9},{1... | collective-permute-start | bytes 245768 | tf_op jit(solution)/shard_map/ppermute | solution.py:416
  8.4 3.0 %load.1 = (bf16[8,9,128,128]{3,2,1,0:T(8,128)(2,1)S(1)}, bf16[8,9,128,128]{3,2,1,0:T(8,128)(2,1)S(1)}, s32[8,9]{1,0:T(8,128)S(4)}, f32[8,9]{1,0:T(8,128)S(4)}, s32[12]{0:T(128)S(4)}, /*index=5*/f32[2]{0:T(128)S(4)}) custom-call(s32[5]{0:T(128)S(1)} %stack.23.ints, f32[1]{0:T(128)S(6)} %copy.10.shift, f32[1]{0:T(128)S(6)} %copy.11.width, s32[16,9]{1,0:T(8,128)} %columns.1, ...), custom_call_target="tpu_custom_call" | custom-call | bytes 9437184 | tf_op jit(solution)/shard_map/load/pallas_call | solution.py:483
  12.0 1.5 %scaled.8 = (bf16[8,64,128]{2,1,0:T(8,128)(2,1)S(1)}, bf16[5,64,128]{2,1,0:T(8,128)(2,1)S(1)}, bf16[5,64,128]{2,1,0:T(8,128)(2,1)S(1)}) custom-call(s32[12]{0:T(128)S(4)} %get-tuple-element.99.ints, s32[8,9]{1,0:T(8,128)S(4)} %get-tuple-element.100.index, f32[8,9]{1,0:T(8,128)S(4)} %get-tuple-element.101.signs, f32[2]{0:T(128)S(4)} %get-tuple-element.102.scal, ...), custom_call_target="tpu_custom_call" | custom-call | flops 7247757312 | bytes 56623104 | tf_op jit(solution)/shard_map/scaled/pallas_call | solution.py:437
  13.5 1.7 %collective-permute-start.7 = (bf16[5,64,128]{2,1,0:T(8,128)(2,1)S(1)}, bf16[5,64,128]{2,1,0:T(8,128)(2,1)S(1)}, u32[]{:S(2)}, u32[]{:S(2)}) collective-permute-start(bf16[5,64,128]{2,1,0:T(8,128)(2,1)S(1)} %get-tuple-element.120), channel_id=1, source_target_pairs={{1,4},{4,1},{3,6},{6,3},{5,8},{8,5},{7,10},{10,7},{9,12},{12,9},{1... | collective-permute-start | bytes 245768 | tf_op jit(solution)/shard_map/ppermute | solution.py:416
  15.2 1.5 %scaled.9 = (bf16[8,64,128]{2,1,0:T(8,128)(2,1)S(1)}, bf16[5,64,128]{2,1,0:T(8,128)(2,1)S(1)}, bf16[5,64,128]{2,1,0:T(8,128)(2,1)S(1)}) custom-call(s32[12]{0:T(128)S(4)} %get-tuple-element.99.ints, s32[8,9]{1,0:T(8,128)S(4)} %get-tuple-element.100.index, f32[8,9]{1,0:T(8,128)S(4)} %get-tuple-element.101.signs, f32[2]{0:T(128)S(4)} %get-tuple-element.102.scal, ...), custom_call_target="tpu_custom_call" | custom-call | flops 7247757312 | bytes 56623104 | tf_op jit(solution)/shard_map/scaled/pallas_call | solution.py:437
  16.7 1.9 %collective-permute-start.3 = (bf16[5,64,128]{2,1,0:T(8,128)(2,1)S(1)}, bf16[5,64,128]{2,1,0:T(8,128)(2,1)S(1)}, u32[]{:S(2)}, u32[]{:S(2)}) collective-permute-start(bf16[5,64,128]{2,1,0:T(8,128)(2,1)S(1)} %get-tuple-element.113), channel_id=1, source_target_pairs={{1,4},{4,1},{3,6},{6,3},{5,8},{8,5},{7,10},{10,7},{9,12},{12,9},{1... | collective-permute-start | bytes 245768 | tf_op jit(solution)/shard_map/ppermute | solution.py:416
  20.2 1.6 %collective-permute-start.9 = (bf16[5,64,128]{2,1,0:T(8,128)(2,1)S(1)}, bf16[5,64,128]{2,1,0:T(8,128)(2,1)S(1)}, u32[]{:S(2)}, u32[]{:S(2)}) collective-permute-start(bf16[5,64,128]{2,1,0:T(8,128)(2,1)S(1)} %get-tuple-element.123), channel_id=1, source_target_pairs={{1,4},{4,1},{3,6},{6,3},{5,8},{8,5},{7,10},{10,7},{9,12},{12,9},{1... | collective-permute-start | bytes 245768 | tf_op jit(solution)/shard_map/ppermute | solution.py:416
  23.5 1.9 %collective-permute-start.5 = (bf16[5,64,128]{2,1,0:T(8,128)(2,1)S(1)}, bf16[5,64,128]{2,1,0:T(8,128)(2,1)S(1)}, u32[]{:S(2)}, u32[]{:S(2)}) collective-permute-start(bf16[5,64,128]{2,1,0:T(8,128)(2,1)S(1)} %get-tuple-element.116), channel_id=1, source_target_pairs={{1,4},{4,1},{3,6},{6,3},{5,8},{8,5},{7,10},{10,7},{9,12},{12,9},{1... | collective-permute-start | bytes 245768 | tf_op jit(solution)/shard_map/ppermute | solution.py:416
  26.8 1.8 %collective-permute-start.11 = (bf16[5,64,128]{2,1,0:T(8,128)(2,1)S(1)}, bf16[5,64,128]{2,1,0:T(8,128)(2,1)S(1)}, u32[]{:S(2)}, u32[]{:S(2)}) collective-permute-start(bf16[5,64,128]{2,1,0:T(8,128)(2,1)S(1)} %get-tuple-element.126), channel_id=1, source_target_pairs={{1,4},{4,1},{3,6},{6,3},{5,8},{8,5},{7,10},{10,7},{9,12},{12,9},{1... | collective-permute-start | bytes 245768 | tf_op jit(solution)/shard_map/ppermute | solution.py:416
  30.1 2.0 %collective-permute-start.13 = (bf16[5,64,128]{2,1,0:T(8,128)(2,1)S(1)}, bf16[5,64,128]{2,1,0:T(8,128)(2,1)S(1)}, u32[]{:S(2)}, u32[]{:S(2)}) collective-permute-start(bf16[5,64,128]{2,1,0:T(8,128)(2,1)S(1)} %get-tuple-element.130), channel_id=1, source_target_pairs={{1,4},{4,1},{3,6},{6,3},{5,8},{8,5},{7,10},{10,7},{9,12},{12,9},{1... | collective-permute-start | bytes 245768 | tf_op jit(solution)/shard_map/ppermute | solution.py:416
  32.5 1.5 %scaled.10 = (bf16[8,64,128]{2,1,0:T(8,128)(2,1)S(1)}, bf16[5,64,128]{2,1,0:T(8,128)(2,1)S(1)}, bf16[5,64,128]{2,1,0:T(8,128)(2,1)S(1)}) custom-call(s32[12]{0:T(128)S(4)} %get-tuple-element.99.ints, s32[8,9]{1,0:T(8,128)S(4)} %get-tuple-element.100.index, f32[8,9]{1,0:T(8,128)S(4)} %get-tuple-element.101.signs, f32[2]{0:T(128)S(4)} %get-tuple-element.102.scal, ...), custom_call_target="tpu_custom_call" | custom-call | flops 7247757312 | bytes 56623104 | tf_op jit(solution)/shard_map/scaled/pallas_call | solution.py:437
  34.0 2.0 %collective-permute-start.19 = (bf16[5,64,128]{2,1,0:T(8,128)(2,1)S(1)}, bf16[5,64,128]{2,1,0:T(8,128)(2,1)S(1)}, u32[]{:S(2)}, u32[]{:S(2)}) collective-permute-start(bf16[5,64,128]{2,1,0:T(8,128)(2,1)S(1)} %get-tuple-element.140), channel_id=1, source_target_pairs={{1,4},{4,1},{3,6},{6,3},{5,8},{8,5},{7,10},{10,7},{9,12},{12,9},{1... | collective-permute-start | bytes 245768 | tf_op jit(solution)/shard_map/ppermute | solution.py:416
  36.0 1.5 %scaled.11 = (bf16[8,64,128]{2,1,0:T(8,128)(2,1)S(1)}, bf16[5,64,128]{2,1,0:T(8,128)(2,1)S(1)}, bf16[5,64,128]{2,1,0:T(8,128)(2,1)S(1)}) custom-call(s32[12]{0:T(128)S(4)} %get-tuple-element.99.ints, s32[8,9]{1,0:T(8,128)S(4)} %get-tuple-element.100.index, f32[8,9]{1,0:T(8,128)S(4)} %get-tuple-element.101.signs, f32[2]{0:T(128)S(4)} %get-tuple-element.102.scal, ...), custom_call_target="tpu_custom_call" | custom-call | flops 7247757312 | bytes 56623104 | tf_op jit(solution)/shard_map/scaled/pallas_call | solution.py:437
  37.5 1.9 %collective-permute-start.15 = (bf16[5,64,128]{2,1,0:T(8,128)(2,1)S(1)}, bf16[5,64,128]{2,1,0:T(8,128)(2,1)S(1)}, u32[]{:S(2)}, u32[]{:S(2)}) collective-permute-start(bf16[5,64,128]{2,1,0:T(8,128)(2,1)S(1)} %get-tuple-element.133), channel_id=1, source_target_pairs={{1,4},{4,1},{3,6},{6,3},{5,8},{8,5},{7,10},{10,7},{9,12},{12,9},{1... | collective-permute-start | bytes 245768 | tf_op jit(solution)/shard_map/ppermute | solution.py:416
  40.6 2.0 %collective-permute-start.21 = (bf16[5,64,128]{2,1,0:T(8,128)(2,1)S(1)}, bf16[5,64,128]{2,1,0:T(8,128)(2,1)S(1)}, u32[]{:S(2)}, u32[]{:S(2)}) collective-permute-start(bf16[5,64,128]{2,1,0:T(8,128)(2,1)S(1)} %get-tuple-element.143), channel_id=1, source_target_pairs={{1,4},{4,1},{3,6},{6,3},{5,8},{8,5},{7,10},{10,7},{9,12},{12,9},{1... | collective-permute-start | bytes 245768 | tf_op jit(solution)/shard_map/ppermute | solution.py:416
  44.1 2.0 %collective-permute-start.17 = (bf16[5,64,128]{2,1,0:T(8,128)(2,1)S(1)}, bf16[5,64,128]{2,1,0:T(8,128)(2,1)S(1)}, u32[]{:S(2)}, u32[]{:S(2)}) collective-permute-start(bf16[5,64,128]{2,1,0:T(8,128)(2,1)S(1)} %get-tuple-element.136), channel_id=1, source_target_pairs={{1,4},{4,1},{3,6},{6,3},{5,8},{8,5},{7,10},{10,7},{9,12},{12,9},{1... | collective-permute-start | bytes 245768 | tf_op jit(solution)/shard_map/ppermute | solution.py:416
  47.2 2.2 %collective-permute-start.23 = (bf16[5,64,128]{2,1,0:T(8,128)(2,1)S(1)}, bf16[5,64,128]{2,1,0:T(8,128)(2,1)S(1)}, u32[]{:S(2)}, u32[]{:S(2)}) collective-permute-start(bf16[5,64,128]{2,1,0:T(8,128)(2,1)S(1)} %get-tuple-element.146), channel_id=1, source_target_pairs={{1,4},{4,1},{3,6},{6,3},{5,8},{8,5},{7,10},{10,7},{9,12},{12,9},{1... | collective-permute-start | bytes 245768 | tf_op jit(solution)/shard_map/ppermute | solution.py:416
  50.9 2.2 %collective-permute-start.25 = (bf16[5,64,128]{2,1,0:T(8,128)(2,1)S(1)}, bf16[5,64,128]{2,1,0:T(8,128)(2,1)S(1)}, u32[]{:S(2)}, u32[]{:S(2)}) collective-permute-start(bf16[5,64,128]{2,1,0:T(8,128)(2,1)S(1)} %get-tuple-element.150), channel_id=1, source_target_pairs={{1,4},{4,1},{3,6},{6,3},{5,8},{8,5},{7,10},{10,7},{9,12},{12,9},{1... | collective-permute-start | bytes 245768 | tf_op jit(solution)/shard_map/ppermute | solution.py:416
  53.1 1.5 %scaled.12 = (bf16[8,64,128]{2,1,0:T(8,128)(2,1)S(1)}, bf16[5,64,128]{2,1,0:T(8,128)(2,1)S(1)}, bf16[5,64,128]{2,1,0:T(8,128)(2,1)S(1)}) custom-call(s32[12]{0:T(128)S(4)} %get-tuple-element.99.ints, s32[8,9]{1,0:T(8,128)S(4)} %get-tuple-element.100.index, f32[8,9]{1,0:T(8,128)S(4)} %get-tuple-element.101.signs, f32[2]{0:T(128)S(4)} %get-tuple-element.102.scal, ...), custom_call_target="tpu_custom_call" | custom-call | flops 7247757312 | bytes 56623104 | tf_op jit(solution)/shard_map/scaled/pallas_call | solution.py:437
  54.6 2.2 %collective-permute-start.31 = (bf16[5,64,128]{2,1,0:T(8,128)(2,1)S(1)}, bf16[5,64,128]{2,1,0:T(8,128)(2,1)S(1)}, u32[]{:S(2)}, u32[]{:S(2)}) collective-permute-start(bf16[5,64,128]{2,1,0:T(8,128)(2,1)S(1)} %get-tuple-element.160), channel_id=1, source_target_pairs={{1,4},{4,1},{3,6},{6,3},{5,8},{8,5},{7,10},{10,7},{9,12},{12,9},{1... | collective-permute-start | bytes 245768 | tf_op jit(solution)/shard_map/ppermute | solution.py:416
  56.8 1.5 %scaled.13 = (bf16[8,64,128]{2,1,0:T(8,128)(2,1)S(1)}, bf16[5,64,128]{2,1,0:T(8,128)(2,1)S(1)}, bf16[5,64,128]{2,1,0:T(8,128)(2,1)S(1)}) custom-call(s32[12]{0:T(128)S(4)} %get-tuple-element.99.ints, s32[8,9]{1,0:T(8,128)S(4)} %get-tuple-element.100.index, f32[8,9]{1,0:T(8,128)S(4)} %get-tuple-element.101.signs, f32[2]{0:T(128)S(4)} %get-tuple-element.102.scal, ...), custom_call_target="tpu_custom_call" | custom-call | flops 7247757312 | bytes 56623104 | tf_op jit(solution)/shard_map/scaled/pallas_call | solution.py:437
  58.3 2.1 %collective-permute-start.27 = (bf16[5,64,128]{2,1,0:T(8,128)(2,1)S(1)}, bf16[5,64,128]{2,1,0:T(8,128)(2,1)S(1)}, u32[]{:S(2)}, u32[]{:S(2)}) collective-permute-start(bf16[5,64,128]{2,1,0:T(8,128)(2,1)S(1)} %get-tuple-element.153), channel_id=1, source_target_pairs={{1,4},{4,1},{3,6},{6,3},{5,8},{8,5},{7,10},{10,7},{9,12},{12,9},{1... | collective-permute-start | bytes 245768 | tf_op jit(solution)/shard_map/ppermute | solution.py:416
  61.3 2.2 %collective-permute-start.33 = (bf16[5,64,128]{2,1,0:T(8,128)(2,1)S(1)}, bf16[5,64,128]{2,1,0:T(8,128)(2,1)S(1)}, u32[]{:S(2)}, u32[]{:S(2)}) collective-permute-start(bf16[5,64,128]{2,1,0:T(8,128)(2,1)S(1)} %get-tuple-element.163), channel_id=1, source_target_pairs={{1,4},{4,1},{3,6},{6,3},{5,8},{8,5},{7,10},{10,7},{9,12},{12,9},{1... | collective-permute-start | bytes 245768 | tf_op jit(solution)/shard_map/ppermute | solution.py:416
  64.9 2.3 %collective-permute-start.29 = (bf16[5,64,128]{2,1,0:T(8,128)(2,1)S(1)}, bf16[5,64,128]{2,1,0:T(8,128)(2,1)S(1)}, u32[]{:S(2)}, u32[]{:S(2)}) collective-permute-start(bf16[5,64,128]{2,1,0:T(8,128)(2,1)S(1)} %get-tuple-element.156), channel_id=1, source_target_pairs={{1,4},{4,1},{3,6},{6,3},{5,8},{8,5},{7,10},{10,7},{9,12},{12,9},{1... | collective-permute-start | bytes 245768 | tf_op jit(solution)/shard_map/ppermute | solution.py:416
  68.0 2.2 %collective-permute-start.35 = (bf16[5,64,128]{2,1,0:T(8,128)(2,1)S(1)}, bf16[5,64,128]{2,1,0:T(8,128)(2,1)S(1)}, u32[]{:S(2)}, u32[]{:S(2)}) collective-permute-start(bf16[5,64,128]{2,1,0:T(8,128)(2,1)S(1)} %get-tuple-element.166), channel_id=1, source_target_pairs={{1,4},{4,1},{3,6},{6,3},{5,8},{8,5},{7,10},{10,7},{9,12},{12,9},{1... | collective-permute-start | bytes 245768 | tf_op jit(solution)/shard_map/ppermute | solution.py:416
  71.5 2.4 %collective-permute-start.37 = (bf16[5,64,128]{2,1,0:T(8,128)(2,1)S(1)}, bf16[5,64,128]{2,1,0:T(8,128)(2,1)S(1)}, u32[]{:S(2)}, u32[]{:S(2)}) collective-permute-start(bf16[5,64,128]{2,1,0:T(8,128)(2,1)S(1)} %get-tuple-element.170), channel_id=1, source_target_pairs={{1,4},{4,1},{3,6},{6,3},{5,8},{8,5},{7,10},{10,7},{9,12},{12,9},{1... | collective-permute-start | bytes 245768 | tf_op jit(solution)/shard_map/ppermute | solution.py:416
  73.9 1.5 %scaled.14 = (bf16[8,64,128]{2,1,0:T(8,128)(2,1)S(1)}, bf16[5,64,128]{2,1,0:T(8,128)(2,1)S(1)}, bf16[5,64,128]{2,1,0:T(8,128)(2,1)S(1)}) custom-call(s32[12]{0:T(128)S(4)} %get-tuple-element.99.ints, s32[8,9]{1,0:T(8,128)S(4)} %get-tuple-element.100.index, f32[8,9]{1,0:T(8,128)S(4)} %get-tuple-element.101.signs, f32[2]{0:T(128)S(4)} %get-tuple-element.102.scal, ...), custom_call_target="tpu_custom_call" | custom-call | flops 7247757312 | bytes 56623104 | tf_op jit(solution)/shard_map/scaled/pallas_call | solution.py:437
  75.4 2.1 %collective-permute-start.43 = (bf16[5,64,128]{2,1,0:T(8,128)(2,1)S(1)}, bf16[5,64,128]{2,1,0:T(8,128)(2,1)S(1)}, u32[]{:S(2)}, u32[]{:S(2)}) collective-permute-start(bf16[5,64,128]{2,1,0:T(8,128)(2,1)S(1)} %get-tuple-element.180), channel_id=1, source_target_pairs={{1,4},{4,1},{3,6},{6,3},{5,8},{8,5},{7,10},{10,7},{9,12},{12,9},{1... | collective-permute-start | bytes 245768 | tf_op jit(solution)/shard_map/ppermute | solution.py:416
  77.6 1.5 %scaled.15 = (bf16[8,64,128]{2,1,0:T(8,128)(2,1)S(1)}, bf16[5,64,128]{2,1,0:T(8,128)(2,1)S(1)}, bf16[5,64,128]{2,1,0:T(8,128)(2,1)S(1)}) custom-call(s32[12]{0:T(128)S(4)} %get-tuple-element.99.ints, s32[8,9]{1,0:T(8,128)S(4)} %get-tuple-element.100.index, f32[8,9]{1,0:T(8,128)S(4)} %get-tuple-element.101.signs, f32[2]{0:T(128)S(4)} %get-tuple-element.102.scal, ...), custom_call_target="tpu_custom_call" | custom-call | flops 7247757312 | bytes 56623104 | tf_op jit(solution)/shard_map/scaled/pallas_call | solution.py:437
  79.1 2.2 %collective-permute-start.39 = (bf16[5,64,128]{2,1,0:T(8,128)(2,1)S(1)}, bf16[5,64,128]{2,1,0:T(8,128)(2,1)S(1)}, u32[]{:S(2)}, u32[]{:S(2)}) collective-permute-start(bf16[5,64,128]{2,1,0:T(8,128)(2,1)S(1)} %get-tuple-element.173), channel_id=1, source_target_pairs={{1,4},{4,1},{3,6},{6,3},{5,8},{8,5},{7,10},{10,7},{9,12},{12,9},{1... | collective-permute-start | bytes 245768 | tf_op jit(solution)/shard_map/ppermute | solution.py:416
  82.2 2.1 %collective-permute-start.45 = (bf16[5,64,128]{2,1,0:T(8,128)(2,1)S(1)}, bf16[5,64,128]{2,1,0:T(8,128)(2,1)S(1)}, u32[]{:S(2)}, u32[]{:S(2)}) collective-permute-start(bf16[5,64,128]{2,1,0:T(8,128)(2,1)S(1)} %get-tuple-element.183), channel_id=1, source_target_pairs={{1,4},{4,1},{3,6},{6,3},{5,8},{8,5},{7,10},{10,7},{9,12},{12,9},{1... | collective-permute-start | bytes 245768 | tf_op jit(solution)/shard_map/ppermute | solution.py:416
  85.7 2.4 %collective-permute-start.41 = (bf16[5,64,128]{2,1,0:T(8,128)(2,1)S(1)}, bf16[5,64,128]{2,1,0:T(8,128)(2,1)S(1)}, u32[]{:S(2)}, u32[]{:S(2)}) collective-permute-start(bf16[5,64,128]{2,1,0:T(8,128)(2,1)S(1)} %get-tuple-element.176), channel_id=1, source_target_pairs={{1,4},{4,1},{3,6},{6,3},{5,8},{8,5},{7,10},{10,7},{9,12},{12,9},{1... | collective-permute-start | bytes 245768 | tf_op jit(solution)/shard_map/ppermute | solution.py:416
  89.1 2.1 %collective-permute-start.47 = (bf16[5,64,128]{2,1,0:T(8,128)(2,1)S(1)}, bf16[5,64,128]{2,1,0:T(8,128)(2,1)S(1)}, u32[]{:S(2)}, u32[]{:S(2)}) collective-permute-start(bf16[5,64,128]{2,1,0:T(8,128)(2,1)S(1)} %get-tuple-element.186), channel_id=1, source_target_pairs={{1,4},{4,1},{3,6},{6,3},{5,8},{8,5},{7,10},{10,7},{9,12},{12,9},{1... | collective-permute-start | bytes 245768 | tf_op jit(solution)/shard_map/ppermute | solution.py:416
  91.2 1.5 %collective-permute-start.49 = (bf16[8,64,128]{2,1,0:T(8,128)(2,1)S(1)}, bf16[8,64,128]{2,1,0:T(8,128)(2,1)S(1)}, u32[]{:S(2)}, u32[]{:S(2)}) collective-permute-start(bf16[8,64,128]{2,1,0:T(8,128)(2,1)S(1)} %get-tuple-element.185.own.refs_2_.refs_4_), channel_id=1, source_target_pairs={{2,0},{3,1},{0,2},{1,3},{6,4},{7,5},{4,6},{5,7},{10,8},{11,9},{8,1... | collective-permute-start | bytes 393224 | tf_op jit(solution)/shard_map/ppermute | solution.py:428
  93.6 1.4 %collective-permute-start.50 = (bf16[5,64,128]{2,1,0:T(8,128)(2,1)S(1)}, bf16[5,64,128]{2,1,0:T(8,128)(2,1)S(1)}, u32[]{:S(2)}, u32[]{:S(2)}) collective-permute-start(bf16[5,64,128]{2,1,0:T(8,128)(2,1)S(1)} %get-tuple-element.190), channel_id=1, source_target_pairs={{1,4},{4,1},{3,6},{6,3},{5,8},{8,5},{7,10},{10,7},{9,12},{12,9},{1... | collective-permute-start | bytes 245768 | tf_op jit(solution)/shard_map/ppermute | solution.py:416
  94.9 1.4 %collective-permute-start.52 = (bf16[8,64,128]{2,1,0:T(8,128)(2,1)S(1)}, bf16[8,64,128]{2,1,0:T(8,128)(2,1)S(1)}, u32[]{:S(2)}, u32[]{:S(2)}) collective-permute-start(bf16[8,64,128]{2,1,0:T(8,128)(2,1)S(1)} %get-tuple-element.189.own.refs_3_.refs_5_), channel_id=1, source_target_pairs={{2,0},{3,1},{0,2},{1,3},{6,4},{7,5},{4,6},{5,7},{10,8},{11,9},{8,1... | collective-permute-start | bytes 393224 | tf_op jit(solution)/shard_map/ppermute | solution.py:428
  97.1 1.5 %images.2.refs_0_ = bf16[2,64,1024]{2,1,0:T(8,128)(2,1)S(1)} custom-call(s32[12]{0:T(128)S(4)} %get-tuple-element.99.ints, s32[8,9]{1,0:T(8,128)S(4)} %get-tuple-element.100.index, f32[8,9]{1,0:T(8,128)S(4)} %get-tuple-element.101.signs, bf16[8,64,128]{2,1,0:T(8,128)(2,1)S(1)} %get-tuple-element.185.own.refs_2_.refs_4_, ...), custom_call_target="tpu_custom_call" | custom-call | flops 7247757312 | bytes 56623104 | tf_op jit(solution)/shard_map/images/pallas_call | solution.py:437
  99.3 1.5 %images.3.refs_1_ = bf16[2,64,1024]{2,1,0:T(8,128)(2,1)S(1)} custom-call(s32[12]{0:T(128)S(4)} %get-tuple-element.99.ints, s32[8,9]{1,0:T(8,128)S(4)} %get-tuple-element.100.index, f32[8,9]{1,0:T(8,128)S(4)} %get-tuple-element.101.signs, bf16[8,64,128]{2,1,0:T(8,128)(2,1)S(1)} %get-tuple-element.189.own.refs_3_.refs_5_, ...), custom_call_target="tpu_custom_call" | custom-call | flops 7247757312 | bytes 56623104 | tf_op jit(solution)/shard_map/images/pallas_call | solution.py:437
  101.4 1.2 collective-permute-done.53.right
  102.7 2.2 %collective-permute-start.56 = (bf16[272,128]{1,0:T(8,128)(2,1)S(1)}, bf16[272,128]{1,0:T(8,128)(2,1)S(1)}, u32[]{:S(2)}, u32[]{:S(2)}) collective-permute-start(bf16[272,128]{1,0:T(8,128)(2,1)S(1)} %add.9.refs_0_), channel_id=1, source_target_pairs={{0,12},{4,0},{8,4},{12,8},{1,13},{5,1},{9,5},{13,9},{2,14},{6,2},{... | collective-permute-start | bytes 208904 | tf_op jit(solution)/shard_map/ppermute | solution.py:589
  105.6 1.9 %collective-permute-done.56.refs_3_ = bf16[272,128]{1,0:T(8,128)(2,1)S(1)} collective-permute-done((bf16[272,128]{1,0:T(8,128)(2,1)S(1)}, bf16[272,128]{1,0:T(8,128)(2,1)S(1)}, u32[]{:S(2)}, u32[]{:S(2)}) %collective-permute-start.56) | collective-permute-done | bytes 69664 | tf_op jit(solution)/shard_map/ppermute | solution.py:589
  107.5 4.6 %collective-permute-done.55.refs_2_ = bf16[272,128]{1,0:T(8,128)(2,1)S(1)} collective-permute-done((bf16[272,128]{1,0:T(8,128)(2,1)S(1)}, bf16[272,128]{1,0:T(8,128)(2,1)S(1)}, u32[]{:S(2)}, u32[]{:S(2)}) %collective-permute-start.55) | collective-permute-done | bytes 69664 | tf_op jit(solution)/shard_map/ppermute | solution.py:589
  112.1 1.5 %collective-permute-start.57 = (bf16[272,128]{1,0:T(8,128)(2,1)S(1)}, bf16[272,128]{1,0:T(8,128)(2,1)S(1)}, u32[]{:S(2)}, u32[]{:S(2)}) collective-permute-start(bf16[272,128]{1,0:T(8,128)(2,1)S(1)} %sum.1.refs_0_), channel_id=1, source_target_pairs={{2,0},{3,1},{0,2},{1,3},{6,4},{7,5},{4,6},{5,7},{10,8},{11,9},{8,1... | collective-permute-start | bytes 208904 | tf_op jit(solution)/shard_map/ppermute | solution.py:428
  114.6 1.9 %collective-permute-done.57.refs_1_ = bf16[272,128]{1,0:T(8,128)(2,1)S(1)} collective-permute-done((bf16[272,128]{1,0:T(8,128)(2,1)S(1)}, bf16[272,128]{1,0:T(8,128)(2,1)S(1)}, u32[]{:S(2)}, u32[]{:S(2)}) %collective-permute-start.57) | collective-permute-done | bytes 69664 | tf_op jit(solution)/shard_map/ppermute | solution.py:428
  116.5 1.2 collective-permute-done.59.refs_3_
  117.8 9.6 %finish.1 = (bf16[64,2048]{1,0:T(8,128)(2,1)}, f32[64,256]{1,0:T(8,128)}) custom-call(s32[12]{0:T(128)S(4)} %get-tuple-element.99.ints, bf16[272,128]{1,0:T(8,128)(2,1)S(1)} %sum.1.refs_0_, bf16[272,128]{1,0:T(8,128)(2,1)S(1)} %collective-permute-done.57.refs_1_, bf16[272,128]{1,0:T(8,128)(2,1)S(1)} %collective-permute-done.58.refs_2_, ...), custom_call_target="tpu_custom_call" | custom-call | flops 36238786560 | bytes 283115520 | tf_op jit(solution)/shard_map/finish/pallas_call | solution.py:437
  (116 shorter events, 25.2 us)
Async XLA Ops:
  2.3 9.1 %collective-permute-start.1 = (bf16[5,64,128]{2,1,0:T(8,128)(2,1)S(1)}, bf16[5,64,128]{2,1,0:T(8,128)(2,1)S(1)}, u32[]{:S(2)}, u32[]{:S(2)}) collective-permute-start(bf16[5,64,128]{2,1,0:T(8,128)(2,1)S(1)} %get-tuple-element.105), channel_id=1, source_target_pairs={{0,4},{1,13},{2,6},{3,15},{4,8},{5,1},{6,10},{7,3},{8,12},{9,5},{1... | collective-permute-start | bytes 245768 | tf_op jit(solution)/shard_map/ppermute | solution.py:424
  5.4 6.5 %collective-permute-start.2 = (bf16[5,64,128]{2,1,0:T(8,128)(2,1)S(1)}, bf16[5,64,128]{2,1,0:T(8,128)(2,1)S(1)}, u32[]{:S(2)}, u32[]{:S(2)}) collective-permute-start(bf16[5,64,128]{2,1,0:T(8,128)(2,1)S(1)} %get-tuple-element.106), channel_id=1, source_target_pairs={{1,4},{4,1},{3,6},{6,3},{5,8},{8,5},{7,10},{10,7},{9,12},{12,9},{1... | collective-permute-start | bytes 245768 | tf_op jit(solution)/shard_map/ppermute | solution.py:416
  7.0 4.9 %collective-permute-start = (bf16[13,64,128]{2,1,0:T(8,128)(2,1)S(1)}, bf16[13,64,128]{2,1,0:T(8,128)(2,1)S(1)}, u32[]{:S(2)}, u32[]{:S(2)}) collective-permute-start(bf16[13,64,128]{2,1,0:T(8,128)(2,1)S(1)} %get-tuple-element.103), channel_id=1, source_target_pairs={{0,1},{1,0},{2,3},{3,2},{4,5},{5,4},{6,7},{7,6},{8,9},{9,8},{10,11... | collective-permute-start | bytes 638984 | tf_op jit(solution)/shard_map/ppermute | solution.py:407
  13.5 5.8 %collective-permute-start.7 = (bf16[5,64,128]{2,1,0:T(8,128)(2,1)S(1)}, bf16[5,64,128]{2,1,0:T(8,128)(2,1)S(1)}, u32[]{:S(2)}, u32[]{:S(2)}) collective-permute-start(bf16[5,64,128]{2,1,0:T(8,128)(2,1)S(1)} %get-tuple-element.120), channel_id=1, source_target_pairs={{1,4},{4,1},{3,6},{6,3},{5,8},{8,5},{7,10},{10,7},{9,12},{12,9},{1... | collective-permute-start | bytes 245768 | tf_op jit(solution)/shard_map/ppermute | solution.py:416
  15.2 4.1 %collective-permute-start.8 = (bf16[5,64,128]{2,1,0:T(8,128)(2,1)S(1)}, bf16[5,64,128]{2,1,0:T(8,128)(2,1)S(1)}, u32[]{:S(2)}, u32[]{:S(2)}) collective-permute-start(bf16[5,64,128]{2,1,0:T(8,128)(2,1)S(1)} %get-tuple-element.121), channel_id=1, source_target_pairs={{0,1},{1,0},{2,3},{3,2},{4,5},{5,4},{6,7},{7,6},{8,9},{9,8},{10,11... | collective-permute-start | bytes 245768 | tf_op jit(solution)/shard_map/ppermute | solution.py:407
  16.7 5.9 %collective-permute-start.3 = (bf16[5,64,128]{2,1,0:T(8,128)(2,1)S(1)}, bf16[5,64,128]{2,1,0:T(8,128)(2,1)S(1)}, u32[]{:S(2)}, u32[]{:S(2)}) collective-permute-start(bf16[5,64,128]{2,1,0:T(8,128)(2,1)S(1)} %get-tuple-element.113), channel_id=1, source_target_pairs={{1,4},{4,1},{3,6},{6,3},{5,8},{8,5},{7,10},{10,7},{9,12},{12,9},{1... | collective-permute-start | bytes 245768 | tf_op jit(solution)/shard_map/ppermute | solution.py:416
  18.6 4.0 %collective-permute-start.4 = (bf16[5,64,128]{2,1,0:T(8,128)(2,1)S(1)}, bf16[5,64,128]{2,1,0:T(8,128)(2,1)S(1)}, u32[]{:S(2)}, u32[]{:S(2)}) collective-permute-start(bf16[5,64,128]{2,1,0:T(8,128)(2,1)S(1)} %get-tuple-element.114), channel_id=1, source_target_pairs={{0,1},{1,0},{2,3},{3,2},{4,5},{5,4},{6,7},{7,6},{8,9},{9,8},{10,11... | collective-permute-start | bytes 245768 | tf_op jit(solution)/shard_map/ppermute | solution.py:407
  20.2 5.7 %collective-permute-start.9 = (bf16[5,64,128]{2,1,0:T(8,128)(2,1)S(1)}, bf16[5,64,128]{2,1,0:T(8,128)(2,1)S(1)}, u32[]{:S(2)}, u32[]{:S(2)}) collective-permute-start(bf16[5,64,128]{2,1,0:T(8,128)(2,1)S(1)} %get-tuple-element.123), channel_id=1, source_target_pairs={{1,4},{4,1},{3,6},{6,3},{5,8},{8,5},{7,10},{10,7},{9,12},{12,9},{1... | collective-permute-start | bytes 245768 | tf_op jit(solution)/shard_map/ppermute | solution.py:416
  21.8 4.1 %collective-permute-start.10 = (bf16[5,64,128]{2,1,0:T(8,128)(2,1)S(1)}, bf16[5,64,128]{2,1,0:T(8,128)(2,1)S(1)}, u32[]{:S(2)}, u32[]{:S(2)}) collective-permute-start(bf16[5,64,128]{2,1,0:T(8,128)(2,1)S(1)} %get-tuple-element.124), channel_id=1, source_target_pairs={{0,1},{1,0},{2,3},{3,2},{4,5},{5,4},{6,7},{7,6},{8,9},{9,8},{10,11... | collective-permute-start | bytes 245768 | tf_op jit(solution)/shard_map/ppermute | solution.py:407
  23.5 5.8 %collective-permute-start.5 = (bf16[5,64,128]{2,1,0:T(8,128)(2,1)S(1)}, bf16[5,64,128]{2,1,0:T(8,128)(2,1)S(1)}, u32[]{:S(2)}, u32[]{:S(2)}) collective-permute-start(bf16[5,64,128]{2,1,0:T(8,128)(2,1)S(1)} %get-tuple-element.116), channel_id=1, source_target_pairs={{1,4},{4,1},{3,6},{6,3},{5,8},{8,5},{7,10},{10,7},{9,12},{12,9},{1... | collective-permute-start | bytes 245768 | tf_op jit(solution)/shard_map/ppermute | solution.py:416
  25.4 3.9 %collective-permute-start.6 = (bf16[5,64,128]{2,1,0:T(8,128)(2,1)S(1)}, bf16[5,64,128]{2,1,0:T(8,128)(2,1)S(1)}, u32[]{:S(2)}, u32[]{:S(2)}) collective-permute-start(bf16[5,64,128]{2,1,0:T(8,128)(2,1)S(1)} %get-tuple-element.117), channel_id=1, source_target_pairs={{0,1},{1,0},{2,3},{3,2},{4,5},{5,4},{6,7},{7,6},{8,9},{9,8},{10,11... | collective-permute-start | bytes 245768 | tf_op jit(solution)/shard_map/ppermute | solution.py:407
  26.8 5.7 %collective-permute-start.11 = (bf16[5,64,128]{2,1,0:T(8,128)(2,1)S(1)}, bf16[5,64,128]{2,1,0:T(8,128)(2,1)S(1)}, u32[]{:S(2)}, u32[]{:S(2)}) collective-permute-start(bf16[5,64,128]{2,1,0:T(8,128)(2,1)S(1)} %get-tuple-element.126), channel_id=1, source_target_pairs={{1,4},{4,1},{3,6},{6,3},{5,8},{8,5},{7,10},{10,7},{9,12},{12,9},{1... | collective-permute-start | bytes 245768 | tf_op jit(solution)/shard_map/ppermute | solution.py:416
  28.6 3.9 %collective-permute-start.12 = (bf16[5,64,128]{2,1,0:T(8,128)(2,1)S(1)}, bf16[5,64,128]{2,1,0:T(8,128)(2,1)S(1)}, u32[]{:S(2)}, u32[]{:S(2)}) collective-permute-start(bf16[5,64,128]{2,1,0:T(8,128)(2,1)S(1)} %get-tuple-element.127), channel_id=1, source_target_pairs={{0,1},{1,0},{2,3},{3,2},{4,5},{5,4},{6,7},{7,6},{8,9},{9,8},{10,11... | collective-permute-start | bytes 245768 | tf_op jit(solution)/shard_map/ppermute | solution.py:407
  30.1 5.9 %collective-permute-start.13 = (bf16[5,64,128]{2,1,0:T(8,128)(2,1)S(1)}, bf16[5,64,128]{2,1,0:T(8,128)(2,1)S(1)}, u32[]{:S(2)}, u32[]{:S(2)}) collective-permute-start(bf16[5,64,128]{2,1,0:T(8,128)(2,1)S(1)} %get-tuple-element.130), channel_id=1, source_target_pairs={{1,4},{4,1},{3,6},{6,3},{5,8},{8,5},{7,10},{10,7},{9,12},{12,9},{1... | collective-permute-start | bytes 245768 | tf_op jit(solution)/shard_map/ppermute | solution.py:416
  32.1 3.9 %collective-permute-start.14 = (bf16[5,64,128]{2,1,0:T(8,128)(2,1)S(1)}, bf16[5,64,128]{2,1,0:T(8,128)(2,1)S(1)}, u32[]{:S(2)}, u32[]{:S(2)}) collective-permute-start(bf16[5,64,128]{2,1,0:T(8,128)(2,1)S(1)} %get-tuple-element.131), channel_id=1, source_target_pairs={{0,1},{1,0},{2,3},{3,2},{4,5},{5,4},{6,7},{7,6},{8,9},{9,8},{10,11... | collective-permute-start | bytes 245768 | tf_op jit(solution)/shard_map/ppermute | solution.py:407
  34.0 5.7 %collective-permute-start.19 = (bf16[5,64,128]{2,1,0:T(8,128)(2,1)S(1)}, bf16[5,64,128]{2,1,0:T(8,128)(2,1)S(1)}, u32[]{:S(2)}, u32[]{:S(2)}) collective-permute-start(bf16[5,64,128]{2,1,0:T(8,128)(2,1)S(1)} %get-tuple-element.140), channel_id=1, source_target_pairs={{1,4},{4,1},{3,6},{6,3},{5,8},{8,5},{7,10},{10,7},{9,12},{12,9},{1... | collective-permute-start | bytes 245768 | tf_op jit(solution)/shard_map/ppermute | solution.py:416
  36.0 3.8 %collective-permute-start.20 = (bf16[5,64,128]{2,1,0:T(8,128)(2,1)S(1)}, bf16[5,64,128]{2,1,0:T(8,128)(2,1)S(1)}, u32[]{:S(2)}, u32[]{:S(2)}) collective-permute-start(bf16[5,64,128]{2,1,0:T(8,128)(2,1)S(1)} %get-tuple-element.141), channel_id=1, source_target_pairs={{0,1},{1,0},{2,3},{3,2},{4,5},{5,4},{6,7},{7,6},{8,9},{9,8},{10,11... | collective-permute-start | bytes 245768 | tf_op jit(solution)/shard_map/ppermute | solution.py:407
  37.5 5.7 %collective-permute-start.15 = (bf16[5,64,128]{2,1,0:T(8,128)(2,1)S(1)}, bf16[5,64,128]{2,1,0:T(8,128)(2,1)S(1)}, u32[]{:S(2)}, u32[]{:S(2)}) collective-permute-start(bf16[5,64,128]{2,1,0:T(8,128)(2,1)S(1)} %get-tuple-element.133), channel_id=1, source_target_pairs={{1,4},{4,1},{3,6},{6,3},{5,8},{8,5},{7,10},{10,7},{9,12},{12,9},{1... | collective-permute-start | bytes 245768 | tf_op jit(solution)/shard_map/ppermute | solution.py:416
  39.4 3.8 %collective-permute-start.16 = (bf16[5,64,128]{2,1,0:T(8,128)(2,1)S(1)}, bf16[5,64,128]{2,1,0:T(8,128)(2,1)S(1)}, u32[]{:S(2)}, u32[]{:S(2)}) collective-permute-start(bf16[5,64,128]{2,1,0:T(8,128)(2,1)S(1)} %get-tuple-element.134), channel_id=1, source_target_pairs={{0,1},{1,0},{2,3},{3,2},{4,5},{5,4},{6,7},{7,6},{8,9},{9,8},{10,11... | collective-permute-start | bytes 245768 | tf_op jit(solution)/shard_map/ppermute | solution.py:407
  40.6 5.7 %collective-permute-start.21 = (bf16[5,64,128]{2,1,0:T(8,128)(2,1)S(1)}, bf16[5,64,128]{2,1,0:T(8,128)(2,1)S(1)}, u32[]{:S(2)}, u32[]{:S(2)}) collective-permute-start(bf16[5,64,128]{2,1,0:T(8,128)(2,1)S(1)} %get-tuple-element.143), channel_id=1, source_target_pairs={{1,4},{4,1},{3,6},{6,3},{5,8},{8,5},{7,10},{10,7},{9,12},{12,9},{1... | collective-permute-start | bytes 245768 | tf_op jit(solution)/shard_map/ppermute | solution.py:416
  44.1 5.7 %collective-permute-start.17 = (bf16[5,64,128]{2,1,0:T(8,128)(2,1)S(1)}, bf16[5,64,128]{2,1,0:T(8,128)(2,1)S(1)}, u32[]{:S(2)}, u32[]{:S(2)}) collective-permute-start(bf16[5,64,128]{2,1,0:T(8,128)(2,1)S(1)} %get-tuple-element.136), channel_id=1, source_target_pairs={{1,4},{4,1},{3,6},{6,3},{5,8},{8,5},{7,10},{10,7},{9,12},{12,9},{1... | collective-permute-start | bytes 245768 | tf_op jit(solution)/shard_map/ppermute | solution.py:416
  47.2 5.8 %collective-permute-start.23 = (bf16[5,64,128]{2,1,0:T(8,128)(2,1)S(1)}, bf16[5,64,128]{2,1,0:T(8,128)(2,1)S(1)}, u32[]{:S(2)}, u32[]{:S(2)}) collective-permute-start(bf16[5,64,128]{2,1,0:T(8,128)(2,1)S(1)} %get-tuple-element.146), channel_id=1, source_target_pairs={{1,4},{4,1},{3,6},{6,3},{5,8},{8,5},{7,10},{10,7},{9,12},{12,9},{1... | collective-permute-start | bytes 245768 | tf_op jit(solution)/shard_map/ppermute | solution.py:416
  50.9 5.9 %collective-permute-start.25 = (bf16[5,64,128]{2,1,0:T(8,128)(2,1)S(1)}, bf16[5,64,128]{2,1,0:T(8,128)(2,1)S(1)}, u32[]{:S(2)}, u32[]{:S(2)}) collective-permute-start(bf16[5,64,128]{2,1,0:T(8,128)(2,1)S(1)} %get-tuple-element.150), channel_id=1, source_target_pairs={{1,4},{4,1},{3,6},{6,3},{5,8},{8,5},{7,10},{10,7},{9,12},{12,9},{1... | collective-permute-start | bytes 245768 | tf_op jit(solution)/shard_map/ppermute | solution.py:416
  54.6 5.8 %collective-permute-start.31 = (bf16[5,64,128]{2,1,0:T(8,128)(2,1)S(1)}, bf16[5,64,128]{2,1,0:T(8,128)(2,1)S(1)}, u32[]{:S(2)}, u32[]{:S(2)}) collective-permute-start(bf16[5,64,128]{2,1,0:T(8,128)(2,1)S(1)} %get-tuple-element.160), channel_id=1, source_target_pairs={{1,4},{4,1},{3,6},{6,3},{5,8},{8,5},{7,10},{10,7},{9,12},{12,9},{1... | collective-permute-start | bytes 245768 | tf_op jit(solution)/shard_map/ppermute | solution.py:416
  58.3 5.7 %collective-permute-start.27 = (bf16[5,64,128]{2,1,0:T(8,128)(2,1)S(1)}, bf16[5,64,128]{2,1,0:T(8,128)(2,1)S(1)}, u32[]{:S(2)}, u32[]{:S(2)}) collective-permute-start(bf16[5,64,128]{2,1,0:T(8,128)(2,1)S(1)} %get-tuple-element.153), channel_id=1, source_target_pairs={{1,4},{4,1},{3,6},{6,3},{5,8},{8,5},{7,10},{10,7},{9,12},{12,9},{1... | collective-permute-start | bytes 245768 | tf_op jit(solution)/shard_map/ppermute | solution.py:416
  61.3 5.9 %collective-permute-start.33 = (bf16[5,64,128]{2,1,0:T(8,128)(2,1)S(1)}, bf16[5,64,128]{2,1,0:T(8,128)(2,1)S(1)}, u32[]{:S(2)}, u32[]{:S(2)}) collective-permute-start(bf16[5,64,128]{2,1,0:T(8,128)(2,1)S(1)} %get-tuple-element.163), channel_id=1, source_target_pairs={{1,4},{4,1},{3,6},{6,3},{5,8},{8,5},{7,10},{10,7},{9,12},{12,9},{1... | collective-permute-start | bytes 245768 | tf_op jit(solution)/shard_map/ppermute | solution.py:416
  63.4 3.7 %collective-permute-start.34 = (bf16[5,64,128]{2,1,0:T(8,128)(2,1)S(1)}, bf16[5,64,128]{2,1,0:T(8,128)(2,1)S(1)}, u32[]{:S(2)}, u32[]{:S(2)}) collective-permute-start(bf16[5,64,128]{2,1,0:T(8,128)(2,1)S(1)} %get-tuple-element.164), channel_id=1, source_target_pairs={{0,1},{1,0},{2,3},{3,2},{4,5},{5,4},{6,7},{7,6},{8,9},{9,8},{10,11... | collective-permute-start | bytes 245768 | tf_op jit(solution)/shard_map/ppermute | solution.py:407
  64.9 5.7 %collective-permute-start.29 = (bf16[5,64,128]{2,1,0:T(8,128)(2,1)S(1)}, bf16[5,64,128]{2,1,0:T(8,128)(2,1)S(1)}, u32[]{:S(2)}, u32[]{:S(2)}) collective-permute-start(bf16[5,64,128]{2,1,0:T(8,128)(2,1)S(1)} %get-tuple-element.156), channel_id=1, source_target_pairs={{1,4},{4,1},{3,6},{6,3},{5,8},{8,5},{7,10},{10,7},{9,12},{12,9},{1... | collective-permute-start | bytes 245768 | tf_op jit(solution)/shard_map/ppermute | solution.py:416
  68.0 5.9 %collective-permute-start.35 = (bf16[5,64,128]{2,1,0:T(8,128)(2,1)S(1)}, bf16[5,64,128]{2,1,0:T(8,128)(2,1)S(1)}, u32[]{:S(2)}, u32[]{:S(2)}) collective-permute-start(bf16[5,64,128]{2,1,0:T(8,128)(2,1)S(1)} %get-tuple-element.166), channel_id=1, source_target_pairs={{1,4},{4,1},{3,6},{6,3},{5,8},{8,5},{7,10},{10,7},{9,12},{12,9},{1... | collective-permute-start | bytes 245768 | tf_op jit(solution)/shard_map/ppermute | solution.py:416
  70.2 3.7 %collective-permute-start.36 = (bf16[5,64,128]{2,1,0:T(8,128)(2,1)S(1)}, bf16[5,64,128]{2,1,0:T(8,128)(2,1)S(1)}, u32[]{:S(2)}, u32[]{:S(2)}) collective-permute-start(bf16[5,64,128]{2,1,0:T(8,128)(2,1)S(1)} %get-tuple-element.167), channel_id=1, source_target_pairs={{0,1},{1,0},{2,3},{3,2},{4,5},{5,4},{6,7},{7,6},{8,9},{9,8},{10,11... | collective-permute-start | bytes 245768 | tf_op jit(solution)/shard_map/ppermute | solution.py:407
  71.5 6.1 %collective-permute-start.37 = (bf16[5,64,128]{2,1,0:T(8,128)(2,1)S(1)}, bf16[5,64,128]{2,1,0:T(8,128)(2,1)S(1)}, u32[]{:S(2)}, u32[]{:S(2)}) collective-permute-start(bf16[5,64,128]{2,1,0:T(8,128)(2,1)S(1)} %get-tuple-element.170), channel_id=1, source_target_pairs={{1,4},{4,1},{3,6},{6,3},{5,8},{8,5},{7,10},{10,7},{9,12},{12,9},{1... | collective-permute-start | bytes 245768 | tf_op jit(solution)/shard_map/ppermute | solution.py:416
  75.4 5.8 %collective-permute-start.43 = (bf16[5,64,128]{2,1,0:T(8,128)(2,1)S(1)}, bf16[5,64,128]{2,1,0:T(8,128)(2,1)S(1)}, u32[]{:S(2)}, u32[]{:S(2)}) collective-permute-start(bf16[5,64,128]{2,1,0:T(8,128)(2,1)S(1)} %get-tuple-element.180), channel_id=1, source_target_pairs={{1,4},{4,1},{3,6},{6,3},{5,8},{8,5},{7,10},{10,7},{9,12},{12,9},{1... | collective-permute-start | bytes 245768 | tf_op jit(solution)/shard_map/ppermute | solution.py:416
  79.1 5.7 %collective-permute-start.39 = (bf16[5,64,128]{2,1,0:T(8,128)(2,1)S(1)}, bf16[5,64,128]{2,1,0:T(8,128)(2,1)S(1)}, u32[]{:S(2)}, u32[]{:S(2)}) collective-permute-start(bf16[5,64,128]{2,1,0:T(8,128)(2,1)S(1)} %get-tuple-element.173), channel_id=1, source_target_pairs={{1,4},{4,1},{3,6},{6,3},{5,8},{8,5},{7,10},{10,7},{9,12},{12,9},{1... | collective-permute-start | bytes 245768 | tf_op jit(solution)/shard_map/ppermute | solution.py:416
  82.2 5.9 %collective-permute-start.45 = (bf16[5,64,128]{2,1,0:T(8,128)(2,1)S(1)}, bf16[5,64,128]{2,1,0:T(8,128)(2,1)S(1)}, u32[]{:S(2)}, u32[]{:S(2)}) collective-permute-start(bf16[5,64,128]{2,1,0:T(8,128)(2,1)S(1)} %get-tuple-element.183), channel_id=1, source_target_pairs={{1,4},{4,1},{3,6},{6,3},{5,8},{8,5},{7,10},{10,7},{9,12},{12,9},{1... | collective-permute-start | bytes 245768 | tf_op jit(solution)/shard_map/ppermute | solution.py:416
  84.2 3.8 %collective-permute-start.46 = (bf16[5,64,128]{2,1,0:T(8,128)(2,1)S(1)}, bf16[5,64,128]{2,1,0:T(8,128)(2,1)S(1)}, u32[]{:S(2)}, u32[]{:S(2)}) collective-permute-start(bf16[5,64,128]{2,1,0:T(8,128)(2,1)S(1)} %get-tuple-element.184), channel_id=1, source_target_pairs={{0,1},{1,0},{2,3},{3,2},{4,5},{5,4},{6,7},{7,6},{8,9},{9,8},{10,11... | collective-permute-start | bytes 245768 | tf_op jit(solution)/shard_map/ppermute | solution.py:407
  85.7 7.0 %collective-permute-start.41 = (bf16[5,64,128]{2,1,0:T(8,128)(2,1)S(1)}, bf16[5,64,128]{2,1,0:T(8,128)(2,1)S(1)}, u32[]{:S(2)}, u32[]{:S(2)}) collective-permute-start(bf16[5,64,128]{2,1,0:T(8,128)(2,1)S(1)} %get-tuple-element.176), channel_id=1, source_target_pairs={{1,4},{4,1},{3,6},{6,3},{5,8},{8,5},{7,10},{10,7},{9,12},{12,9},{1... | collective-permute-start | bytes 245768 | tf_op jit(solution)/shard_map/ppermute | solution.py:416
  88.0 4.6 %collective-permute-start.42 = (bf16[5,64,128]{2,1,0:T(8,128)(2,1)S(1)}, bf16[5,64,128]{2,1,0:T(8,128)(2,1)S(1)}, u32[]{:S(2)}, u32[]{:S(2)}) collective-permute-start(bf16[5,64,128]{2,1,0:T(8,128)(2,1)S(1)} %get-tuple-element.177), channel_id=1, source_target_pairs={{0,1},{1,0},{2,3},{3,2},{4,5},{5,4},{6,7},{7,6},{8,9},{9,8},{10,11... | collective-permute-start | bytes 245768 | tf_op jit(solution)/shard_map/ppermute | solution.py:407
  89.1 5.8 %collective-permute-start.47 = (bf16[5,64,128]{2,1,0:T(8,128)(2,1)S(1)}, bf16[5,64,128]{2,1,0:T(8,128)(2,1)S(1)}, u32[]{:S(2)}, u32[]{:S(2)}) collective-permute-start(bf16[5,64,128]{2,1,0:T(8,128)(2,1)S(1)} %get-tuple-element.186), channel_id=1, source_target_pairs={{1,4},{4,1},{3,6},{6,3},{5,8},{8,5},{7,10},{10,7},{9,12},{12,9},{1... | collective-permute-start | bytes 245768 | tf_op jit(solution)/shard_map/ppermute | solution.py:416
  91.2 5.2 %collective-permute-start.48 = (bf16[5,64,128]{2,1,0:T(8,128)(2,1)S(1)}, bf16[5,64,128]{2,1,0:T(8,128)(2,1)S(1)}, u32[]{:S(2)}, u32[]{:S(2)}) collective-permute-start(bf16[5,64,128]{2,1,0:T(8,128)(2,1)S(1)} %get-tuple-element.187), channel_id=1, source_target_pairs={{0,1},{1,0},{2,3},{3,2},{4,5},{5,4},{6,7},{7,6},{8,9},{9,8},{10,11... | collective-permute-start | bytes 245768 | tf_op jit(solution)/shard_map/ppermute | solution.py:407
  91.2 5.9 %collective-permute-start.49 = (bf16[8,64,128]{2,1,0:T(8,128)(2,1)S(1)}, bf16[8,64,128]{2,1,0:T(8,128)(2,1)S(1)}, u32[]{:S(2)}, u32[]{:S(2)}) collective-permute-start(bf16[8,64,128]{2,1,0:T(8,128)(2,1)S(1)} %get-tuple-element.185.own.refs_2_.refs_4_), channel_id=1, source_target_pairs={{2,0},{3,1},{0,2},{1,3},{6,4},{7,5},{4,6},{5,7},{10,8},{11,9},{8,1... | collective-permute-start | bytes 393224 | tf_op jit(solution)/shard_map/ppermute | solution.py:428
  93.6 5.7 %collective-permute-start.50 = (bf16[5,64,128]{2,1,0:T(8,128)(2,1)S(1)}, bf16[5,64,128]{2,1,0:T(8,128)(2,1)S(1)}, u32[]{:S(2)}, u32[]{:S(2)}) collective-permute-start(bf16[5,64,128]{2,1,0:T(8,128)(2,1)S(1)} %get-tuple-element.190), channel_id=1, source_target_pairs={{1,4},{4,1},{3,6},{6,3},{5,8},{8,5},{7,10},{10,7},{9,12},{12,9},{1... | collective-permute-start | bytes 245768 | tf_op jit(solution)/shard_map/ppermute | solution.py:416
  94.9 4.4 %collective-permute-start.51 = (bf16[5,64,128]{2,1,0:T(8,128)(2,1)S(1)}, bf16[5,64,128]{2,1,0:T(8,128)(2,1)S(1)}, u32[]{:S(2)}, u32[]{:S(2)}) collective-permute-start(bf16[5,64,128]{2,1,0:T(8,128)(2,1)S(1)} %get-tuple-element.191), channel_id=1, source_target_pairs={{0,1},{1,0},{2,3},{3,2},{4,5},{5,4},{6,7},{7,6},{8,9},{9,8},{10,11... | collective-permute-start | bytes 245768 | tf_op jit(solution)/shard_map/ppermute | solution.py:407
  94.9 5.9 %collective-permute-start.52 = (bf16[8,64,128]{2,1,0:T(8,128)(2,1)S(1)}, bf16[8,64,128]{2,1,0:T(8,128)(2,1)S(1)}, u32[]{:S(2)}, u32[]{:S(2)}) collective-permute-start(bf16[8,64,128]{2,1,0:T(8,128)(2,1)S(1)} %get-tuple-element.189.own.refs_3_.refs_5_), channel_id=1, source_target_pairs={{2,0},{3,1},{0,2},{1,3},{6,4},{7,5},{4,6},{5,7},{10,8},{11,9},{8,1... | collective-permute-start | bytes 393224 | tf_op jit(solution)/shard_map/ppermute | solution.py:428
  102.7 4.8 %collective-permute-start.56 = (bf16[272,128]{1,0:T(8,128)(2,1)S(1)}, bf16[272,128]{1,0:T(8,128)(2,1)S(1)}, u32[]{:S(2)}, u32[]{:S(2)}) collective-permute-start(bf16[272,128]{1,0:T(8,128)(2,1)S(1)} %add.9.refs_0_), channel_id=1, source_target_pairs={{0,12},{4,0},{8,4},{12,8},{1,13},{5,1},{9,5},{13,9},{2,14},{6,2},{... | collective-permute-start | bytes 208904 | tf_op jit(solution)/shard_map/ppermute | solution.py:589
  104.9 7.2 %collective-permute-start.55 = (bf16[272,128]{1,0:T(8,128)(2,1)S(1)}, bf16[272,128]{1,0:T(8,128)(2,1)S(1)}, u32[]{:S(2)}, u32[]{:S(2)}) collective-permute-start(bf16[272,128]{1,0:T(8,128)(2,1)S(1)} %add.9.refs_0_), channel_id=1, source_target_pairs={{0,8},{4,12},{8,0},{12,4},{1,9},{5,13},{9,1},{13,5},{2,10},{6,14},... | collective-permute-start | bytes 208904 | tf_op jit(solution)/shard_map/ppermute | solution.py:589
  104.9 7.2 %collective-permute-start.54 = (bf16[272,128]{1,0:T(8,128)(2,1)S(1)}, bf16[272,128]{1,0:T(8,128)(2,1)S(1)}, u32[]{:S(2)}, u32[]{:S(2)}) collective-permute-start(bf16[272,128]{1,0:T(8,128)(2,1)S(1)} %add.9.refs_0_), channel_id=1, source_target_pairs={{0,4},{4,8},{8,12},{12,0},{1,5},{5,9},{9,13},{13,1},{2,6},{6,10},{... | collective-permute-start | bytes 208904 | tf_op jit(solution)/shard_map/ppermute | solution.py:589
  105.6 8.5 %collective-permute-start.60 = (bf16[8,64,128]{2,1,0:T(8,128)(2,1)S(1)}, bf16[8,64,128]{2,1,0:T(8,128)(2,1)S(1)}, u32[]{:S(2)}, u32[]{:S(2)}) collective-permute-start(bf16[8,64,128]{2,1,0:T(8,128)(2,1)S(1)} %get-tuple-element.185.own.refs_2_.refs_4_), channel_id=1, source_target_pairs={{0,1},{1,0},{2,3},{3,2},{4,5},{5,4},{6,7},{7,6},{8,9},{9,8},{10,11... | collective-permute-start | bytes 393224 | tf_op jit(solution)/shard_map/ppermute | solution.py:407
  112.1 4.4 %collective-permute-start.57 = (bf16[272,128]{1,0:T(8,128)(2,1)S(1)}, bf16[272,128]{1,0:T(8,128)(2,1)S(1)}, u32[]{:S(2)}, u32[]{:S(2)}) collective-permute-start(bf16[272,128]{1,0:T(8,128)(2,1)S(1)} %sum.1.refs_0_), channel_id=1, source_target_pairs={{2,0},{3,1},{0,2},{1,3},{6,4},{7,5},{4,6},{5,7},{10,8},{11,9},{8,1... | collective-permute-start | bytes 208904 | tf_op jit(solution)/shard_map/ppermute | solution.py:428
  (16 other events, 49.6 us)

commit v6 on v5

--- a/solution.py
+++ b/solution.py
@@ -202,14 +202,41 @@
     for matrix in range(2):
         mine = jnp.concatenate([image[matrix] for image in images], axis=0)
         pair = lax.dot_general(mine, flat, NT, preferred_element_type=F32)
-        for step in range(chips):
-            where = pl.multiple_of(lax.rem(chip + step, chips) * vecs, vecs)
+        both[matrix, : vecs // 2, :] = packed(pair[:, :vecs]).astype(BF16)
+        for step in range(1, chips):
             block = pair[:, step * vecs : (step + 1) * vecs]
-            both[matrix, pl.ds(where, vecs), :] = block.astype(BF16)
+            both[matrix, (2 * step - 1) * vecs // 2 : (2 * step + 1) * vecs // 2, :] = block.astype(BF16)
         diagonal = jnp.sum(jnp.where(eye, pair[:, :vecs], 0.0), axis=0, keepdims=True)
-        both[matrix, chips * vecs :, :] = diagonal_parts(diagonal)
+        both[matrix, (2 * chips - 1) * vecs // 2 :, :] = diagonal_parts(diagonal)
     keep[...] = both[core]
     send[...] = both[1 - core]
+
+
+def packed(block):
+    half = block.shape[0] // 2
+    block = 0.5 * (block + block.T)
+    top, bottom = block[:half], block[half:]
+    bottom = jnp.concatenate([bottom[:, half:], bottom[:, :half]], axis=1)
+    row = lax.broadcasted_iota(jnp.int32, top.shape, 0)
+    lane = lax.broadcasted_iota(jnp.int32, top.shape, 1)
+    return jnp.where((lane < half) & (lane > row), bottom, top)
+
+
+def unpacked(block):
+    half = block.shape[0]
+    turned = block.T
+    row = lax.broadcasted_iota(jnp.int32, (half, half), 0)
+    lane = lax.broadcasted_iota(jnp.int32, (half, half), 1)
+    square, beside = block[:, :half], block[:, half:]
+    first = jnp.where(lane < row, square, turned[:half])
+    last = jnp.where(lane > row, square, turned[:half])
+    return jnp.concatenate(
+        [
+            jnp.concatenate([first, beside], axis=1),
+            jnp.concatenate([turned[half:], last], axis=1),
+        ],
+        axis=0,
+    )
 
 
 def diagonal_parts(diagonal):
@@ -348,10 +375,14 @@
         which = lax.rem(chip + step, chips)
         rows = pl.ds(pl.multiple_of(which * vecs, vecs), vecs)
         for matrix, payload in ((core, mine[step]), (1 - core, theirs[step])):
-            diagonal = diagonal_of(payload)
+            own_block = unpacked(payload[: vecs // 2, :].astype(F32))
+            own_block = jnp.where(eye, diagonal_of(payload), own_block)
             for k in range(chips):
-                block = payload[k * vecs : (k + 1) * vecs, :].astype(F32)
-                block = jnp.where(eye & (which == k), diagonal, block)
+                block = own_block
+                for away in range(1, chips):
+                    at = (2 * away - 1) * vecs // 2
+                    other = payload[at : at + vecs, :].astype(F32)
+                    block = jnp.where(lax.rem(which + away, chips) == k, other, block)
                 pair[matrix, rows, k * vecs : (k + 1) * vecs] = block
     work[...] = (pair[0] + pair[0].T) * scale
     factor(work, inverse)
@@ -569,7 +600,7 @@
             [ext],
             2 * row_flops,
         )
-    payload = jax.ShapeDtypeStruct((size + DIAGONAL_ROWS, vecs), BF16)
+    payload = jax.ShapeDtypeStruct((size - vecs // 2 + DIAGONAL_ROWS, vecs), BF16)
     keep, send = call(
         functools.partial(gram_kernel, chips),
         "gram",

time: 128 us -> 127 us (level)
    ppermute x3, waiting for transfers between devices: 6.44 us -> 4.87 us  [local(): lax.ppermute(summed, 'row', [(r, (r + step) % num_rows) for r in range(nu...]
where the time goes in v6:
time: 127 us
  starting transfers between devices  61.7 us (49%)
  Pallas kernels  44.2 us (35%)
  waiting for transfers between devices  18.2 us (14%)
  between operations  2.31 us (2%)
    ppermute x25, starting transfers between devices, swap_chips(): return lax.ppermute(value, ('row', 'col'), pairs)  50.4 us
    pallas_call x30, Pallas kernels, call(): pl.pallas_call(kernel, name=name, out_shape=outs, in_specs=[SMEM] * len(s...  39.6 us
    ppermute x25, waiting for transfers between devices, swap_chips(): return lax.ppermute(value, ('row', 'col'), pairs)  7.44 us
    ppermute x3, waiting for transfers between devices, local(): lax.ppermute(summed, 'row', [(r, (r + step) % num_rows) for r in range(nu...  4.87 us
    ppermute x3, starting transfers between devices, from_chip(): return lax.ppermute(value, 'col', pairs)  4.42 us
    ppermute x3, waiting for transfers between devices, from_chip(): return lax.ppermute(value, 'col', pairs)  3.37 us
    ppermute x1, starting transfers between devices, next_chips(): return lax.ppermute(value, ('row', 'col'), pairs)  3.08 us
    pallas_call x1, Pallas kernels, local(): pl.pallas_call(functools.partial(load_kernel, total_blocks), name='load',...  3.01 us
  transfers between devices with their start and end apart: 64, of which 21 were waited for; matrix products, arithmetic and copies ran while one was open for 0% of the time, Pallas kernels for 24%

profile of v6, /device:TPU:0, one launch (start us, length us, event | category | flops | bytes accessed | tf_op | source)
XLA Modules:
  0.0 126.6 jit_solution(13808072754867474656)
XLA Ops:
  0.7 1.6 %cut.1 = (bf16[8,64,128]{2,1,0:T(8,128)(2,1)S(1)}, bf16[5,64,128]{2,1,0:T(8,128)(2,1)S(1)}, bf16[13,64,128]{2,1,0:T(8,128)(2,1)S(1)}, bf16[5,64,128]{2,1,0:T(8,128)(2,1)S(1)}, bf16[5,64,128]{2,1,0:T(8,128)(2,1)S(1)}) custom-call(s32[5]{0:T(128)S(1)} %stack.23.ints, s32[16]{0:T(128)} %sizes.3, bf16[64,2048]{1,0:T(8,128)(2,1)} %trial.1), custom_call_target="tpu_custom_call" | custom-call | tf_op jit(solution)/shard_map/cut/pallas_call | solution.py:497
  2.3 3.1 %collective-permute-start.1 = (bf16[5,64,128]{2,1,0:T(8,128)(2,1)S(1)}, bf16[5,64,128]{2,1,0:T(8,128)(2,1)S(1)}, u32[]{:S(2)}, u32[]{:S(2)}) collective-permute-start(bf16[5,64,128]{2,1,0:T(8,128)(2,1)S(1)} %get-tuple-element.105), channel_id=1, source_target_pairs={{0,4},{1,13},{2,6},{3,15},{4,8},{5,1},{6,10},{7,3},{8,12},{9,5},{1... | collective-permute-start | bytes 245768 | tf_op jit(solution)/shard_map/ppermute | solution.py:455
  5.4 1.6 %collective-permute-start.2 = (bf16[5,64,128]{2,1,0:T(8,128)(2,1)S(1)}, bf16[5,64,128]{2,1,0:T(8,128)(2,1)S(1)}, u32[]{:S(2)}, u32[]{:S(2)}) collective-permute-start(bf16[5,64,128]{2,1,0:T(8,128)(2,1)S(1)} %get-tuple-element.106), channel_id=1, source_target_pairs={{1,4},{4,1},{3,6},{6,3},{5,8},{8,5},{7,10},{10,7},{9,12},{12,9},{1... | collective-permute-start | bytes 245768 | tf_op jit(solution)/shard_map/ppermute | solution.py:447
  8.4 3.0 %load.1 = (bf16[8,9,128,128]{3,2,1,0:T(8,128)(2,1)S(1)}, bf16[8,9,128,128]{3,2,1,0:T(8,128)(2,1)S(1)}, s32[8,9]{1,0:T(8,128)S(4)}, f32[8,9]{1,0:T(8,128)S(4)}, s32[12]{0:T(128)S(4)}, /*index=5*/f32[2]{0:T(128)S(4)}) custom-call(s32[5]{0:T(128)S(1)} %stack.23.ints, f32[1]{0:T(128)S(6)} %copy.10.shift, f32[1]{0:T(128)S(6)} %copy.11.width, s32[16,9]{1,0:T(8,128)} %columns.1, ...), custom_call_target="tpu_custom_call" | custom-call | bytes 9437184 | tf_op jit(solution)/shard_map/load/pallas_call | solution.py:514
  12.0 1.5 %scaled.8 = (bf16[8,64,128]{2,1,0:T(8,128)(2,1)S(1)}, bf16[5,64,128]{2,1,0:T(8,128)(2,1)S(1)}, bf16[5,64,128]{2,1,0:T(8,128)(2,1)S(1)}) custom-call(s32[12]{0:T(128)S(4)} %get-tuple-element.99.ints, s32[8,9]{1,0:T(8,128)S(4)} %get-tuple-element.100.index, f32[8,9]{1,0:T(8,128)S(4)} %get-tuple-element.101.signs, f32[2]{0:T(128)S(4)} %get-tuple-element.102.scal, ...), custom_call_target="tpu_custom_call" | custom-call | flops 7247757312 | bytes 56623104 | tf_op jit(solution)/shard_map/scaled/pallas_call | solution.py:468
  13.5 1.7 %collective-permute-start.7 = (bf16[5,64,128]{2,1,0:T(8,128)(2,1)S(1)}, bf16[5,64,128]{2,1,0:T(8,128)(2,1)S(1)}, u32[]{:S(2)}, u32[]{:S(2)}) collective-permute-start(bf16[5,64,128]{2,1,0:T(8,128)(2,1)S(1)} %get-tuple-element.120), channel_id=1, source_target_pairs={{1,4},{4,1},{3,6},{6,3},{5,8},{8,5},{7,10},{10,7},{9,12},{12,9},{1... | collective-permute-start | bytes 245768 | tf_op jit(solution)/shard_map/ppermute | solution.py:447
  15.2 1.5 %scaled.9 = (bf16[8,64,128]{2,1,0:T(8,128)(2,1)S(1)}, bf16[5,64,128]{2,1,0:T(8,128)(2,1)S(1)}, bf16[5,64,128]{2,1,0:T(8,128)(2,1)S(1)}) custom-call(s32[12]{0:T(128)S(4)} %get-tuple-element.99.ints, s32[8,9]{1,0:T(8,128)S(4)} %get-tuple-element.100.index, f32[8,9]{1,0:T(8,128)S(4)} %get-tuple-element.101.signs, f32[2]{0:T(128)S(4)} %get-tuple-element.102.scal, ...), custom_call_target="tpu_custom_call" | custom-call | flops 7247757312 | bytes 56623104 | tf_op jit(solution)/shard_map/scaled/pallas_call | solution.py:468
  16.7 1.9 %collective-permute-start.3 = (bf16[5,64,128]{2,1,0:T(8,128)(2,1)S(1)}, bf16[5,64,128]{2,1,0:T(8,128)(2,1)S(1)}, u32[]{:S(2)}, u32[]{:S(2)}) collective-permute-start(bf16[5,64,128]{2,1,0:T(8,128)(2,1)S(1)} %get-tuple-element.113), channel_id=1, source_target_pairs={{1,4},{4,1},{3,6},{6,3},{5,8},{8,5},{7,10},{10,7},{9,12},{12,9},{1... | collective-permute-start | bytes 245768 | tf_op jit(solution)/shard_map/ppermute | solution.py:447
  20.2 1.6 %collective-permute-start.9 = (bf16[5,64,128]{2,1,0:T(8,128)(2,1)S(1)}, bf16[5,64,128]{2,1,0:T(8,128)(2,1)S(1)}, u32[]{:S(2)}, u32[]{:S(2)}) collective-permute-start(bf16[5,64,128]{2,1,0:T(8,128)(2,1)S(1)} %get-tuple-element.123), channel_id=1, source_target_pairs={{1,4},{4,1},{3,6},{6,3},{5,8},{8,5},{7,10},{10,7},{9,12},{12,9},{1... | collective-permute-start | bytes 245768 | tf_op jit(solution)/shard_map/ppermute | solution.py:447
  23.5 1.9 %collective-permute-start.5 = (bf16[5,64,128]{2,1,0:T(8,128)(2,1)S(1)}, bf16[5,64,128]{2,1,0:T(8,128)(2,1)S(1)}, u32[]{:S(2)}, u32[]{:S(2)}) collective-permute-start(bf16[5,64,128]{2,1,0:T(8,128)(2,1)S(1)} %get-tuple-element.116), channel_id=1, source_target_pairs={{1,4},{4,1},{3,6},{6,3},{5,8},{8,5},{7,10},{10,7},{9,12},{12,9},{1... | collective-permute-start | bytes 245768 | tf_op jit(solution)/shard_map/ppermute | solution.py:447
  26.8 1.8 %collective-permute-start.11 = (bf16[5,64,128]{2,1,0:T(8,128)(2,1)S(1)}, bf16[5,64,128]{2,1,0:T(8,128)(2,1)S(1)}, u32[]{:S(2)}, u32[]{:S(2)}) collective-permute-start(bf16[5,64,128]{2,1,0:T(8,128)(2,1)S(1)} %get-tuple-element.126), channel_id=1, source_target_pairs={{1,4},{4,1},{3,6},{6,3},{5,8},{8,5},{7,10},{10,7},{9,12},{12,9},{1... | collective-permute-start | bytes 245768 | tf_op jit(solution)/shard_map/ppermute | solution.py:447
  30.1 2.0 %collective-permute-start.13 = (bf16[5,64,128]{2,1,0:T(8,128)(2,1)S(1)}, bf16[5,64,128]{2,1,0:T(8,128)(2,1)S(1)}, u32[]{:S(2)}, u32[]{:S(2)}) collective-permute-start(bf16[5,64,128]{2,1,0:T(8,128)(2,1)S(1)} %get-tuple-element.130), channel_id=1, source_target_pairs={{1,4},{4,1},{3,6},{6,3},{5,8},{8,5},{7,10},{10,7},{9,12},{12,9},{1... | collective-permute-start | bytes 245768 | tf_op jit(solution)/shard_map/ppermute | solution.py:447
  32.5 1.5 %scaled.10 = (bf16[8,64,128]{2,1,0:T(8,128)(2,1)S(1)}, bf16[5,64,128]{2,1,0:T(8,128)(2,1)S(1)}, bf16[5,64,128]{2,1,0:T(8,128)(2,1)S(1)}) custom-call(s32[12]{0:T(128)S(4)} %get-tuple-element.99.ints, s32[8,9]{1,0:T(8,128)S(4)} %get-tuple-element.100.index, f32[8,9]{1,0:T(8,128)S(4)} %get-tuple-element.101.signs, f32[2]{0:T(128)S(4)} %get-tuple-element.102.scal, ...), custom_call_target="tpu_custom_call" | custom-call | flops 7247757312 | bytes 56623104 | tf_op jit(solution)/shard_map/scaled/pallas_call | solution.py:468
  34.0 2.0 %collective-permute-start.19 = (bf16[5,64,128]{2,1,0:T(8,128)(2,1)S(1)}, bf16[5,64,128]{2,1,0:T(8,128)(2,1)S(1)}, u32[]{:S(2)}, u32[]{:S(2)}) collective-permute-start(bf16[5,64,128]{2,1,0:T(8,128)(2,1)S(1)} %get-tuple-element.140), channel_id=1, source_target_pairs={{1,4},{4,1},{3,6},{6,3},{5,8},{8,5},{7,10},{10,7},{9,12},{12,9},{1... | collective-permute-start | bytes 245768 | tf_op jit(solution)/shard_map/ppermute | solution.py:447
  36.0 1.5 %scaled.11 = (bf16[8,64,128]{2,1,0:T(8,128)(2,1)S(1)}, bf16[5,64,128]{2,1,0:T(8,128)(2,1)S(1)}, bf16[5,64,128]{2,1,0:T(8,128)(2,1)S(1)}) custom-call(s32[12]{0:T(128)S(4)} %get-tuple-element.99.ints, s32[8,9]{1,0:T(8,128)S(4)} %get-tuple-element.100.index, f32[8,9]{1,0:T(8,128)S(4)} %get-tuple-element.101.signs, f32[2]{0:T(128)S(4)} %get-tuple-element.102.scal, ...), custom_call_target="tpu_custom_call" | custom-call | flops 7247757312 | bytes 56623104 | tf_op jit(solution)/shard_map/scaled/pallas_call | solution.py:468
  37.5 1.9 %collective-permute-start.15 = (bf16[5,64,128]{2,1,0:T(8,128)(2,1)S(1)}, bf16[5,64,128]{2,1,0:T(8,128)(2,1)S(1)}, u32[]{:S(2)}, u32[]{:S(2)}) collective-permute-start(bf16[5,64,128]{2,1,0:T(8,128)(2,1)S(1)} %get-tuple-element.133), channel_id=1, source_target_pairs={{1,4},{4,1},{3,6},{6,3},{5,8},{8,5},{7,10},{10,7},{9,12},{12,9},{1... | collective-permute-start | bytes 245768 | tf_op jit(solution)/shard_map/ppermute | solution.py:447
  40.6 2.0 %collective-permute-start.21 = (bf16[5,64,128]{2,1,0:T(8,128)(2,1)S(1)}, bf16[5,64,128]{2,1,0:T(8,128)(2,1)S(1)}, u32[]{:S(2)}, u32[]{:S(2)}) collective-permute-start(bf16[5,64,128]{2,1,0:T(8,128)(2,1)S(1)} %get-tuple-element.143), channel_id=1, source_target_pairs={{1,4},{4,1},{3,6},{6,3},{5,8},{8,5},{7,10},{10,7},{9,12},{12,9},{1... | collective-permute-start | bytes 245768 | tf_op jit(solution)/shard_map/ppermute | solution.py:447
  44.1 2.0 %collective-permute-start.17 = (bf16[5,64,128]{2,1,0:T(8,128)(2,1)S(1)}, bf16[5,64,128]{2,1,0:T(8,128)(2,1)S(1)}, u32[]{:S(2)}, u32[]{:S(2)}) collective-permute-start(bf16[5,64,128]{2,1,0:T(8,128)(2,1)S(1)} %get-tuple-element.136), channel_id=1, source_target_pairs={{1,4},{4,1},{3,6},{6,3},{5,8},{8,5},{7,10},{10,7},{9,12},{12,9},{1... | collective-permute-start | bytes 245768 | tf_op jit(solution)/shard_map/ppermute | solution.py:447
  47.2 2.2 %collective-permute-start.23 = (bf16[5,64,128]{2,1,0:T(8,128)(2,1)S(1)}, bf16[5,64,128]{2,1,0:T(8,128)(2,1)S(1)}, u32[]{:S(2)}, u32[]{:S(2)}) collective-permute-start(bf16[5,64,128]{2,1,0:T(8,128)(2,1)S(1)} %get-tuple-element.146), channel_id=1, source_target_pairs={{1,4},{4,1},{3,6},{6,3},{5,8},{8,5},{7,10},{10,7},{9,12},{12,9},{1... | collective-permute-start | bytes 245768 | tf_op jit(solution)/shard_map/ppermute | solution.py:447
  50.9 2.2 %collective-permute-start.25 = (bf16[5,64,128]{2,1,0:T(8,128)(2,1)S(1)}, bf16[5,64,128]{2,1,0:T(8,128)(2,1)S(1)}, u32[]{:S(2)}, u32[]{:S(2)}) collective-permute-start(bf16[5,64,128]{2,1,0:T(8,128)(2,1)S(1)} %get-tuple-element.150), channel_id=1, source_target_pairs={{1,4},{4,1},{3,6},{6,3},{5,8},{8,5},{7,10},{10,7},{9,12},{12,9},{1... | collective-permute-start | bytes 245768 | tf_op jit(solution)/shard_map/ppermute | solution.py:447
  53.1 1.5 %scaled.12 = (bf16[8,64,128]{2,1,0:T(8,128)(2,1)S(1)}, bf16[5,64,128]{2,1,0:T(8,128)(2,1)S(1)}, bf16[5,64,128]{2,1,0:T(8,128)(2,1)S(1)}) custom-call(s32[12]{0:T(128)S(4)} %get-tuple-element.99.ints, s32[8,9]{1,0:T(8,128)S(4)} %get-tuple-element.100.index, f32[8,9]{1,0:T(8,128)S(4)} %get-tuple-element.101.signs, f32[2]{0:T(128)S(4)} %get-tuple-element.102.scal, ...), custom_call_target="tpu_custom_call" | custom-call | flops 7247757312 | bytes 56623104 | tf_op jit(solution)/shard_map/scaled/pallas_call | solution.py:468
  54.6 2.1 %collective-permute-start.31 = (bf16[5,64,128]{2,1,0:T(8,128)(2,1)S(1)}, bf16[5,64,128]{2,1,0:T(8,128)(2,1)S(1)}, u32[]{:S(2)}, u32[]{:S(2)}) collective-permute-start(bf16[5,64,128]{2,1,0:T(8,128)(2,1)S(1)} %get-tuple-element.160), channel_id=1, source_target_pairs={{1,4},{4,1},{3,6},{6,3},{5,8},{8,5},{7,10},{10,7},{9,12},{12,9},{1... | collective-permute-start | bytes 245768 | tf_op jit(solution)/shard_map/ppermute | solution.py:447
  56.7 1.5 %scaled.13 = (bf16[8,64,128]{2,1,0:T(8,128)(2,1)S(1)}, bf16[5,64,128]{2,1,0:T(8,128)(2,1)S(1)}, bf16[5,64,128]{2,1,0:T(8,128)(2,1)S(1)}) custom-call(s32[12]{0:T(128)S(4)} %get-tuple-element.99.ints, s32[8,9]{1,0:T(8,128)S(4)} %get-tuple-element.100.index, f32[8,9]{1,0:T(8,128)S(4)} %get-tuple-element.101.signs, f32[2]{0:T(128)S(4)} %get-tuple-element.102.scal, ...), custom_call_target="tpu_custom_call" | custom-call | flops 7247757312 | bytes 56623104 | tf_op jit(solution)/shard_map/scaled/pallas_call | solution.py:468
  58.2 2.2 %collective-permute-start.27 = (bf16[5,64,128]{2,1,0:T(8,128)(2,1)S(1)}, bf16[5,64,128]{2,1,0:T(8,128)(2,1)S(1)}, u32[]{:S(2)}, u32[]{:S(2)}) collective-permute-start(bf16[5,64,128]{2,1,0:T(8,128)(2,1)S(1)} %get-tuple-element.153), channel_id=1, source_target_pairs={{1,4},{4,1},{3,6},{6,3},{5,8},{8,5},{7,10},{10,7},{9,12},{12,9},{1... | collective-permute-start | bytes 245768 | tf_op jit(solution)/shard_map/ppermute | solution.py:447
  61.3 2.1 %collective-permute-start.33 = (bf16[5,64,128]{2,1,0:T(8,128)(2,1)S(1)}, bf16[5,64,128]{2,1,0:T(8,128)(2,1)S(1)}, u32[]{:S(2)}, u32[]{:S(2)}) collective-permute-start(bf16[5,64,128]{2,1,0:T(8,128)(2,1)S(1)} %get-tuple-element.163), channel_id=1, source_target_pairs={{1,4},{4,1},{3,6},{6,3},{5,8},{8,5},{7,10},{10,7},{9,12},{12,9},{1... | collective-permute-start | bytes 245768 | tf_op jit(solution)/shard_map/ppermute | solution.py:447
  64.8 2.3 %collective-permute-start.29 = (bf16[5,64,128]{2,1,0:T(8,128)(2,1)S(1)}, bf16[5,64,128]{2,1,0:T(8,128)(2,1)S(1)}, u32[]{:S(2)}, u32[]{:S(2)}) collective-permute-start(bf16[5,64,128]{2,1,0:T(8,128)(2,1)S(1)} %get-tuple-element.156), channel_id=1, source_target_pairs={{1,4},{4,1},{3,6},{6,3},{5,8},{8,5},{7,10},{10,7},{9,12},{12,9},{1... | collective-permute-start | bytes 245768 | tf_op jit(solution)/shard_map/ppermute | solution.py:447
  68.1 2.1 %collective-permute-start.35 = (bf16[5,64,128]{2,1,0:T(8,128)(2,1)S(1)}, bf16[5,64,128]{2,1,0:T(8,128)(2,1)S(1)}, u32[]{:S(2)}, u32[]{:S(2)}) collective-permute-start(bf16[5,64,128]{2,1,0:T(8,128)(2,1)S(1)} %get-tuple-element.166), channel_id=1, source_target_pairs={{1,4},{4,1},{3,6},{6,3},{5,8},{8,5},{7,10},{10,7},{9,12},{12,9},{1... | collective-permute-start | bytes 245768 | tf_op jit(solution)/shard_map/ppermute | solution.py:447
  71.4 2.5 %collective-permute-start.37 = (bf16[5,64,128]{2,1,0:T(8,128)(2,1)S(1)}, bf16[5,64,128]{2,1,0:T(8,128)(2,1)S(1)}, u32[]{:S(2)}, u32[]{:S(2)}) collective-permute-start(bf16[5,64,128]{2,1,0:T(8,128)(2,1)S(1)} %get-tuple-element.170), channel_id=1, source_target_pairs={{1,4},{4,1},{3,6},{6,3},{5,8},{8,5},{7,10},{10,7},{9,12},{12,9},{1... | collective-permute-start | bytes 245768 | tf_op jit(solution)/shard_map/ppermute | solution.py:447
  74.0 1.5 %scaled.14 = (bf16[8,64,128]{2,1,0:T(8,128)(2,1)S(1)}, bf16[5,64,128]{2,1,0:T(8,128)(2,1)S(1)}, bf16[5,64,128]{2,1,0:T(8,128)(2,1)S(1)}) custom-call(s32[12]{0:T(128)S(4)} %get-tuple-element.99.ints, s32[8,9]{1,0:T(8,128)S(4)} %get-tuple-element.100.index, f32[8,9]{1,0:T(8,128)S(4)} %get-tuple-element.101.signs, f32[2]{0:T(128)S(4)} %get-tuple-element.102.scal, ...), custom_call_target="tpu_custom_call" | custom-call | flops 7247757312 | bytes 56623104 | tf_op jit(solution)/shard_map/scaled/pallas_call | solution.py:468
  75.5 2.0 %collective-permute-start.43 = (bf16[5,64,128]{2,1,0:T(8,128)(2,1)S(1)}, bf16[5,64,128]{2,1,0:T(8,128)(2,1)S(1)}, u32[]{:S(2)}, u32[]{:S(2)}) collective-permute-start(bf16[5,64,128]{2,1,0:T(8,128)(2,1)S(1)} %get-tuple-element.180), channel_id=1, source_target_pairs={{1,4},{4,1},{3,6},{6,3},{5,8},{8,5},{7,10},{10,7},{9,12},{12,9},{1... | collective-permute-start | bytes 245768 | tf_op jit(solution)/shard_map/ppermute | solution.py:447
  77.5 1.5 %scaled.15 = (bf16[8,64,128]{2,1,0:T(8,128)(2,1)S(1)}, bf16[5,64,128]{2,1,0:T(8,128)(2,1)S(1)}, bf16[5,64,128]{2,1,0:T(8,128)(2,1)S(1)}) custom-call(s32[12]{0:T(128)S(4)} %get-tuple-element.99.ints, s32[8,9]{1,0:T(8,128)S(4)} %get-tuple-element.100.index, f32[8,9]{1,0:T(8,128)S(4)} %get-tuple-element.101.signs, f32[2]{0:T(128)S(4)} %get-tuple-element.102.scal, ...), custom_call_target="tpu_custom_call" | custom-call | flops 7247757312 | bytes 56623104 | tf_op jit(solution)/shard_map/scaled/pallas_call | solution.py:468
  79.0 2.3 %collective-permute-start.39 = (bf16[5,64,128]{2,1,0:T(8,128)(2,1)S(1)}, bf16[5,64,128]{2,1,0:T(8,128)(2,1)S(1)}, u32[]{:S(2)}, u32[]{:S(2)}) collective-permute-start(bf16[5,64,128]{2,1,0:T(8,128)(2,1)S(1)} %get-tuple-element.173), channel_id=1, source_target_pairs={{1,4},{4,1},{3,6},{6,3},{5,8},{8,5},{7,10},{10,7},{9,12},{12,9},{1... | collective-permute-start | bytes 245768 | tf_op jit(solution)/shard_map/ppermute | solution.py:447
  82.2 2.0 %collective-permute-start.45 = (bf16[5,64,128]{2,1,0:T(8,128)(2,1)S(1)}, bf16[5,64,128]{2,1,0:T(8,128)(2,1)S(1)}, u32[]{:S(2)}, u32[]{:S(2)}) collective-permute-start(bf16[5,64,128]{2,1,0:T(8,128)(2,1)S(1)} %get-tuple-element.183), channel_id=1, source_target_pairs={{1,4},{4,1},{3,6},{6,3},{5,8},{8,5},{7,10},{10,7},{9,12},{12,9},{1... | collective-permute-start | bytes 245768 | tf_op jit(solution)/shard_map/ppermute | solution.py:447
  85.6 2.5 %collective-permute-start.41 = (bf16[5,64,128]{2,1,0:T(8,128)(2,1)S(1)}, bf16[5,64,128]{2,1,0:T(8,128)(2,1)S(1)}, u32[]{:S(2)}, u32[]{:S(2)}) collective-permute-start(bf16[5,64,128]{2,1,0:T(8,128)(2,1)S(1)} %get-tuple-element.176), channel_id=1, source_target_pairs={{1,4},{4,1},{3,6},{6,3},{5,8},{8,5},{7,10},{10,7},{9,12},{12,9},{1... | collective-permute-start | bytes 245768 | tf_op jit(solution)/shard_map/ppermute | solution.py:447
  88.1 1.1 update.15
  89.2 1.9 %collective-permute-start.47 = (bf16[5,64,128]{2,1,0:T(8,128)(2,1)S(1)}, bf16[5,64,128]{2,1,0:T(8,128)(2,1)S(1)}, u32[]{:S(2)}, u32[]{:S(2)}) collective-permute-start(bf16[5,64,128]{2,1,0:T(8,128)(2,1)S(1)} %get-tuple-element.186), channel_id=1, source_target_pairs={{1,4},{4,1},{3,6},{6,3},{5,8},{8,5},{7,10},{10,7},{9,12},{12,9},{1... | collective-permute-start | bytes 245768 | tf_op jit(solution)/shard_map/ppermute | solution.py:447
  91.1 1.5 %collective-permute-start.49 = (bf16[8,64,128]{2,1,0:T(8,128)(2,1)S(1)}, bf16[8,64,128]{2,1,0:T(8,128)(2,1)S(1)}, u32[]{:S(2)}, u32[]{:S(2)}) collective-permute-start(bf16[8,64,128]{2,1,0:T(8,128)(2,1)S(1)} %get-tuple-element.185.own.refs_2_.refs_4_), channel_id=1, source_target_pairs={{2,0},{3,1},{0,2},{1,3},{6,4},{7,5},{4,6},{5,7},{10,8},{11,9},{8,1... | collective-permute-start | bytes 393224 | tf_op jit(solution)/shard_map/ppermute | solution.py:459
  93.5 1.5 %collective-permute-start.50 = (bf16[5,64,128]{2,1,0:T(8,128)(2,1)S(1)}, bf16[5,64,128]{2,1,0:T(8,128)(2,1)S(1)}, u32[]{:S(2)}, u32[]{:S(2)}) collective-permute-start(bf16[5,64,128]{2,1,0:T(8,128)(2,1)S(1)} %get-tuple-element.190), channel_id=1, source_target_pairs={{1,4},{4,1},{3,6},{6,3},{5,8},{8,5},{7,10},{10,7},{9,12},{12,9},{1... | collective-permute-start | bytes 245768 | tf_op jit(solution)/shard_map/ppermute | solution.py:447
  94.9 1.4 %collective-permute-start.52 = (bf16[8,64,128]{2,1,0:T(8,128)(2,1)S(1)}, bf16[8,64,128]{2,1,0:T(8,128)(2,1)S(1)}, u32[]{:S(2)}, u32[]{:S(2)}) collective-permute-start(bf16[8,64,128]{2,1,0:T(8,128)(2,1)S(1)} %get-tuple-element.189.own.refs_3_.refs_5_), channel_id=1, source_target_pairs={{2,0},{3,1},{0,2},{1,3},{6,4},{7,5},{4,6},{5,7},{10,8},{11,9},{8,1... | collective-permute-start | bytes 393224 | tf_op jit(solution)/shard_map/ppermute | solution.py:459
  97.0 1.5 %images.2.refs_0_ = bf16[2,64,1024]{2,1,0:T(8,128)(2,1)S(1)} custom-call(s32[12]{0:T(128)S(4)} %get-tuple-element.99.ints, s32[8,9]{1,0:T(8,128)S(4)} %get-tuple-element.100.index, f32[8,9]{1,0:T(8,128)S(4)} %get-tuple-element.101.signs, bf16[8,64,128]{2,1,0:T(8,128)(2,1)S(1)} %get-tuple-element.185.own.refs_2_.refs_4_, ...), custom_call_target="tpu_custom_call" | custom-call | flops 7247757312 | bytes 56623104 | tf_op jit(solution)/shard_map/images/pallas_call | solution.py:468
  99.2 1.5 %images.3.refs_1_ = bf16[2,64,1024]{2,1,0:T(8,128)(2,1)S(1)} custom-call(s32[12]{0:T(128)S(4)} %get-tuple-element.99.ints, s32[8,9]{1,0:T(8,128)S(4)} %get-tuple-element.100.index, f32[8,9]{1,0:T(8,128)S(4)} %get-tuple-element.101.signs, bf16[8,64,128]{2,1,0:T(8,128)(2,1)S(1)} %get-tuple-element.189.own.refs_3_.refs_5_, ...), custom_call_target="tpu_custom_call" | custom-call | flops 7247757312 | bytes 56623104 | tf_op jit(solution)/shard_map/images/pallas_call | solution.py:468
  101.6 1.2 collective-permute-done.53.right
  102.8 2.1 %collective-permute-start.56 = (bf16[208,128]{1,0:T(8,128)(2,1)S(1)}, bf16[208,128]{1,0:T(8,128)(2,1)S(1)}, u32[]{:S(2)}, u32[]{:S(2)}) collective-permute-start(bf16[208,128]{1,0:T(8,128)(2,1)S(1)} %add.9.refs_0_), channel_id=1, source_target_pairs={{0,12},{4,0},{8,4},{12,8},{1,13},{5,1},{9,5},{13,9},{2,14},{6,2},{... | collective-permute-start | bytes 159752 | tf_op jit(solution)/shard_map/ppermute | solution.py:620
  107.1 4.0 %collective-permute-done.55.refs_2_ = bf16[208,128]{1,0:T(8,128)(2,1)S(1)} collective-permute-done((bf16[208,128]{1,0:T(8,128)(2,1)S(1)}, bf16[208,128]{1,0:T(8,128)(2,1)S(1)}, u32[]{:S(2)}, u32[]{:S(2)}) %collective-permute-start.55) | collective-permute-done | bytes 53280 | tf_op jit(solution)/shard_map/ppermute | solution.py:620
  111.2 1.5 %collective-permute-start.57 = (bf16[208,128]{1,0:T(8,128)(2,1)S(1)}, bf16[208,128]{1,0:T(8,128)(2,1)S(1)}, u32[]{:S(2)}, u32[]{:S(2)}) collective-permute-start(bf16[208,128]{1,0:T(8,128)(2,1)S(1)} %sum.1.refs_0_), channel_id=1, source_target_pairs={{2,0},{3,1},{0,2},{1,3},{6,4},{7,5},{4,6},{5,7},{10,8},{11,9},{8,1... | collective-permute-start | bytes 159752 | tf_op jit(solution)/shard_map/ppermute | solution.py:459
  112.9 2.6 %collective-permute-done.57.refs_1_ = bf16[208,128]{1,0:T(8,128)(2,1)S(1)} collective-permute-done((bf16[208,128]{1,0:T(8,128)(2,1)S(1)}, bf16[208,128]{1,0:T(8,128)(2,1)S(1)}, u32[]{:S(2)}, u32[]{:S(2)}) %collective-permute-start.57) | collective-permute-done | bytes 53280 | tf_op jit(solution)/shard_map/ppermute | solution.py:459
  115.5 1.2 collective-permute-done.59.refs_3_
  116.7 9.8 %finish.1 = (bf16[64,2048]{1,0:T(8,128)(2,1)}, f32[64,256]{1,0:T(8,128)}) custom-call(s32[12]{0:T(128)S(4)} %get-tuple-element.99.ints, bf16[208,128]{1,0:T(8,128)(2,1)S(1)} %sum.1.refs_0_, bf16[208,128]{1,0:T(8,128)(2,1)S(1)} %collective-permute-done.57.refs_1_, bf16[208,128]{1,0:T(8,128)(2,1)S(1)} %collective-permute-done.58.refs_2_, ...), custom_call_target="tpu_custom_call" | custom-call | flops 36238786560 | bytes 283115520 | tf_op jit(solution)/shard_map/finish/pallas_call | solution.py:468
  (116 shorter events, 25.0 us)
Async XLA Ops:
  2.3 9.1 %collective-permute-start.1 = (bf16[5,64,128]{2,1,0:T(8,128)(2,1)S(1)}, bf16[5,64,128]{2,1,0:T(8,128)(2,1)S(1)}, u32[]{:S(2)}, u32[]{:S(2)}) collective-permute-start(bf16[5,64,128]{2,1,0:T(8,128)(2,1)S(1)} %get-tuple-element.105), channel_id=1, source_target_pairs={{0,4},{1,13},{2,6},{3,15},{4,8},{5,1},{6,10},{7,3},{8,12},{9,5},{1... | collective-permute-start | bytes 245768 | tf_op jit(solution)/shard_map/ppermute | solution.py:455
  5.4 6.5 %collective-permute-start.2 = (bf16[5,64,128]{2,1,0:T(8,128)(2,1)S(1)}, bf16[5,64,128]{2,1,0:T(8,128)(2,1)S(1)}, u32[]{:S(2)}, u32[]{:S(2)}) collective-permute-start(bf16[5,64,128]{2,1,0:T(8,128)(2,1)S(1)} %get-tuple-element.106), channel_id=1, source_target_pairs={{1,4},{4,1},{3,6},{6,3},{5,8},{8,5},{7,10},{10,7},{9,12},{12,9},{1... | collective-permute-start | bytes 245768 | tf_op jit(solution)/shard_map/ppermute | solution.py:447
  7.0 4.9 %collective-permute-start = (bf16[13,64,128]{2,1,0:T(8,128)(2,1)S(1)}, bf16[13,64,128]{2,1,0:T(8,128)(2,1)S(1)}, u32[]{:S(2)}, u32[]{:S(2)}) collective-permute-start(bf16[13,64,128]{2,1,0:T(8,128)(2,1)S(1)} %get-tuple-element.103), channel_id=1, source_target_pairs={{0,1},{1,0},{2,3},{3,2},{4,5},{5,4},{6,7},{7,6},{8,9},{9,8},{10,11... | collective-permute-start | bytes 638984 | tf_op jit(solution)/shard_map/ppermute | solution.py:438
  13.5 5.8 %collective-permute-start.7 = (bf16[5,64,128]{2,1,0:T(8,128)(2,1)S(1)}, bf16[5,64,128]{2,1,0:T(8,128)(2,1)S(1)}, u32[]{:S(2)}, u32[]{:S(2)}) collective-permute-start(bf16[5,64,128]{2,1,0:T(8,128)(2,1)S(1)} %get-tuple-element.120), channel_id=1, source_target_pairs={{1,4},{4,1},{3,6},{6,3},{5,8},{8,5},{7,10},{10,7},{9,12},{12,9},{1... | collective-permute-start | bytes 245768 | tf_op jit(solution)/shard_map/ppermute | solution.py:447
  15.2 4.1 %collective-permute-start.8 = (bf16[5,64,128]{2,1,0:T(8,128)(2,1)S(1)}, bf16[5,64,128]{2,1,0:T(8,128)(2,1)S(1)}, u32[]{:S(2)}, u32[]{:S(2)}) collective-permute-start(bf16[5,64,128]{2,1,0:T(8,128)(2,1)S(1)} %get-tuple-element.121), channel_id=1, source_target_pairs={{0,1},{1,0},{2,3},{3,2},{4,5},{5,4},{6,7},{7,6},{8,9},{9,8},{10,11... | collective-permute-start | bytes 245768 | tf_op jit(solution)/shard_map/ppermute | solution.py:438
  16.7 5.9 %collective-permute-start.3 = (bf16[5,64,128]{2,1,0:T(8,128)(2,1)S(1)}, bf16[5,64,128]{2,1,0:T(8,128)(2,1)S(1)}, u32[]{:S(2)}, u32[]{:S(2)}) collective-permute-start(bf16[5,64,128]{2,1,0:T(8,128)(2,1)S(1)} %get-tuple-element.113), channel_id=1, source_target_pairs={{1,4},{4,1},{3,6},{6,3},{5,8},{8,5},{7,10},{10,7},{9,12},{12,9},{1... | collective-permute-start | bytes 245768 | tf_op jit(solution)/shard_map/ppermute | solution.py:447
  18.6 4.0 %collective-permute-start.4 = (bf16[5,64,128]{2,1,0:T(8,128)(2,1)S(1)}, bf16[5,64,128]{2,1,0:T(8,128)(2,1)S(1)}, u32[]{:S(2)}, u32[]{:S(2)}) collective-permute-start(bf16[5,64,128]{2,1,0:T(8,128)(2,1)S(1)} %get-tuple-element.114), channel_id=1, source_target_pairs={{0,1},{1,0},{2,3},{3,2},{4,5},{5,4},{6,7},{7,6},{8,9},{9,8},{10,11... | collective-permute-start | bytes 245768 | tf_op jit(solution)/shard_map/ppermute | solution.py:438
  20.2 5.7 %collective-permute-start.9 = (bf16[5,64,128]{2,1,0:T(8,128)(2,1)S(1)}, bf16[5,64,128]{2,1,0:T(8,128)(2,1)S(1)}, u32[]{:S(2)}, u32[]{:S(2)}) collective-permute-start(bf16[5,64,128]{2,1,0:T(8,128)(2,1)S(1)} %get-tuple-element.123), channel_id=1, source_target_pairs={{1,4},{4,1},{3,6},{6,3},{5,8},{8,5},{7,10},{10,7},{9,12},{12,9},{1... | collective-permute-start | bytes 245768 | tf_op jit(solution)/shard_map/ppermute | solution.py:447
  21.8 4.1 %collective-permute-start.10 = (bf16[5,64,128]{2,1,0:T(8,128)(2,1)S(1)}, bf16[5,64,128]{2,1,0:T(8,128)(2,1)S(1)}, u32[]{:S(2)}, u32[]{:S(2)}) collective-permute-start(bf16[5,64,128]{2,1,0:T(8,128)(2,1)S(1)} %get-tuple-element.124), channel_id=1, source_target_pairs={{0,1},{1,0},{2,3},{3,2},{4,5},{5,4},{6,7},{7,6},{8,9},{9,8},{10,11... | collective-permute-start | bytes 245768 | tf_op jit(solution)/shard_map/ppermute | solution.py:438
  23.5 5.8 %collective-permute-start.5 = (bf16[5,64,128]{2,1,0:T(8,128)(2,1)S(1)}, bf16[5,64,128]{2,1,0:T(8,128)(2,1)S(1)}, u32[]{:S(2)}, u32[]{:S(2)}) collective-permute-start(bf16[5,64,128]{2,1,0:T(8,128)(2,1)S(1)} %get-tuple-element.116), channel_id=1, source_target_pairs={{1,4},{4,1},{3,6},{6,3},{5,8},{8,5},{7,10},{10,7},{9,12},{12,9},{1... | collective-permute-start | bytes 245768 | tf_op jit(solution)/shard_map/ppermute | solution.py:447
  25.4 3.9 %collective-permute-start.6 = (bf16[5,64,128]{2,1,0:T(8,128)(2,1)S(1)}, bf16[5,64,128]{2,1,0:T(8,128)(2,1)S(1)}, u32[]{:S(2)}, u32[]{:S(2)}) collective-permute-start(bf16[5,64,128]{2,1,0:T(8,128)(2,1)S(1)} %get-tuple-element.117), channel_id=1, source_target_pairs={{0,1},{1,0},{2,3},{3,2},{4,5},{5,4},{6,7},{7,6},{8,9},{9,8},{10,11... | collective-permute-start | bytes 245768 | tf_op jit(solution)/shard_map/ppermute | solution.py:438
  26.8 5.7 %collective-permute-start.11 = (bf16[5,64,128]{2,1,0:T(8,128)(2,1)S(1)}, bf16[5,64,128]{2,1,0:T(8,128)(2,1)S(1)}, u32[]{:S(2)}, u32[]{:S(2)}) collective-permute-start(bf16[5,64,128]{2,1,0:T(8,128)(2,1)S(1)} %get-tuple-element.126), channel_id=1, source_target_pairs={{1,4},{4,1},{3,6},{6,3},{5,8},{8,5},{7,10},{10,7},{9,12},{12,9},{1... | collective-permute-start | bytes 245768 | tf_op jit(solution)/shard_map/ppermute | solution.py:447
  28.6 3.9 %collective-permute-start.12 = (bf16[5,64,128]{2,1,0:T(8,128)(2,1)S(1)}, bf16[5,64,128]{2,1,0:T(8,128)(2,1)S(1)}, u32[]{:S(2)}, u32[]{:S(2)}) collective-permute-start(bf16[5,64,128]{2,1,0:T(8,128)(2,1)S(1)} %get-tuple-element.127), channel_id=1, source_target_pairs={{0,1},{1,0},{2,3},{3,2},{4,5},{5,4},{6,7},{7,6},{8,9},{9,8},{10,11... | collective-permute-start | bytes 245768 | tf_op jit(solution)/shard_map/ppermute | solution.py:438
  30.1 5.9 %collective-permute-start.13 = (bf16[5,64,128]{2,1,0:T(8,128)(2,1)S(1)}, bf16[5,64,128]{2,1,0:T(8,128)(2,1)S(1)}, u32[]{:S(2)}, u32[]{:S(2)}) collective-permute-start(bf16[5,64,128]{2,1,0:T(8,128)(2,1)S(1)} %get-tuple-element.130), channel_id=1, source_target_pairs={{1,4},{4,1},{3,6},{6,3},{5,8},{8,5},{7,10},{10,7},{9,12},{12,9},{1... | collective-permute-start | bytes 245768 | tf_op jit(solution)/shard_map/ppermute | solution.py:447
  32.1 3.9 %collective-permute-start.14 = (bf16[5,64,128]{2,1,0:T(8,128)(2,1)S(1)}, bf16[5,64,128]{2,1,0:T(8,128)(2,1)S(1)}, u32[]{:S(2)}, u32[]{:S(2)}) collective-permute-start(bf16[5,64,128]{2,1,0:T(8,128)(2,1)S(1)} %get-tuple-element.131), channel_id=1, source_target_pairs={{0,1},{1,0},{2,3},{3,2},{4,5},{5,4},{6,7},{7,6},{8,9},{9,8},{10,11... | collective-permute-start | bytes 245768 | tf_op jit(solution)/shard_map/ppermute | solution.py:438
  34.0 5.7 %collective-permute-start.19 = (bf16[5,64,128]{2,1,0:T(8,128)(2,1)S(1)}, bf16[5,64,128]{2,1,0:T(8,128)(2,1)S(1)}, u32[]{:S(2)}, u32[]{:S(2)}) collective-permute-start(bf16[5,64,128]{2,1,0:T(8,128)(2,1)S(1)} %get-tuple-element.140), channel_id=1, source_target_pairs={{1,4},{4,1},{3,6},{6,3},{5,8},{8,5},{7,10},{10,7},{9,12},{12,9},{1... | collective-permute-start | bytes 245768 | tf_op jit(solution)/shard_map/ppermute | solution.py:447
  37.5 5.7 %collective-permute-start.15 = (bf16[5,64,128]{2,1,0:T(8,128)(2,1)S(1)}, bf16[5,64,128]{2,1,0:T(8,128)(2,1)S(1)}, u32[]{:S(2)}, u32[]{:S(2)}) collective-permute-start(bf16[5,64,128]{2,1,0:T(8,128)(2,1)S(1)} %get-tuple-element.133), channel_id=1, source_target_pairs={{1,4},{4,1},{3,6},{6,3},{5,8},{8,5},{7,10},{10,7},{9,12},{12,9},{1... | collective-permute-start | bytes 245768 | tf_op jit(solution)/shard_map/ppermute | solution.py:447
  39.4 3.9 %collective-permute-start.16 = (bf16[5,64,128]{2,1,0:T(8,128)(2,1)S(1)}, bf16[5,64,128]{2,1,0:T(8,128)(2,1)S(1)}, u32[]{:S(2)}, u32[]{:S(2)}) collective-permute-start(bf16[5,64,128]{2,1,0:T(8,128)(2,1)S(1)} %get-tuple-element.134), channel_id=1, source_target_pairs={{0,1},{1,0},{2,3},{3,2},{4,5},{5,4},{6,7},{7,6},{8,9},{9,8},{10,11... | collective-permute-start | bytes 245768 | tf_op jit(solution)/shard_map/ppermute | solution.py:438
  40.6 5.7 %collective-permute-start.21 = (bf16[5,64,128]{2,1,0:T(8,128)(2,1)S(1)}, bf16[5,64,128]{2,1,0:T(8,128)(2,1)S(1)}, u32[]{:S(2)}, u32[]{:S(2)}) collective-permute-start(bf16[5,64,128]{2,1,0:T(8,128)(2,1)S(1)} %get-tuple-element.143), channel_id=1, source_target_pairs={{1,4},{4,1},{3,6},{6,3},{5,8},{8,5},{7,10},{10,7},{9,12},{12,9},{1... | collective-permute-start | bytes 245768 | tf_op jit(solution)/shard_map/ppermute | solution.py:447
  44.1 5.7 %collective-permute-start.17 = (bf16[5,64,128]{2,1,0:T(8,128)(2,1)S(1)}, bf16[5,64,128]{2,1,0:T(8,128)(2,1)S(1)}, u32[]{:S(2)}, u32[]{:S(2)}) collective-permute-start(bf16[5,64,128]{2,1,0:T(8,128)(2,1)S(1)} %get-tuple-element.136), channel_id=1, source_target_pairs={{1,4},{4,1},{3,6},{6,3},{5,8},{8,5},{7,10},{10,7},{9,12},{12,9},{1... | collective-permute-start | bytes 245768 | tf_op jit(solution)/shard_map/ppermute | solution.py:447
  47.2 5.9 %collective-permute-start.23 = (bf16[5,64,128]{2,1,0:T(8,128)(2,1)S(1)}, bf16[5,64,128]{2,1,0:T(8,128)(2,1)S(1)}, u32[]{:S(2)}, u32[]{:S(2)}) collective-permute-start(bf16[5,64,128]{2,1,0:T(8,128)(2,1)S(1)} %get-tuple-element.146), channel_id=1, source_target_pairs={{1,4},{4,1},{3,6},{6,3},{5,8},{8,5},{7,10},{10,7},{9,12},{12,9},{1... | collective-permute-start | bytes 245768 | tf_op jit(solution)/shard_map/ppermute | solution.py:447
  50.9 5.8 %collective-permute-start.25 = (bf16[5,64,128]{2,1,0:T(8,128)(2,1)S(1)}, bf16[5,64,128]{2,1,0:T(8,128)(2,1)S(1)}, u32[]{:S(2)}, u32[]{:S(2)}) collective-permute-start(bf16[5,64,128]{2,1,0:T(8,128)(2,1)S(1)} %get-tuple-element.150), channel_id=1, source_target_pairs={{1,4},{4,1},{3,6},{6,3},{5,8},{8,5},{7,10},{10,7},{9,12},{12,9},{1... | collective-permute-start | bytes 245768 | tf_op jit(solution)/shard_map/ppermute | solution.py:447
  54.6 5.8 %collective-permute-start.31 = (bf16[5,64,128]{2,1,0:T(8,128)(2,1)S(1)}, bf16[5,64,128]{2,1,0:T(8,128)(2,1)S(1)}, u32[]{:S(2)}, u32[]{:S(2)}) collective-permute-start(bf16[5,64,128]{2,1,0:T(8,128)(2,1)S(1)} %get-tuple-element.160), channel_id=1, source_target_pairs={{1,4},{4,1},{3,6},{6,3},{5,8},{8,5},{7,10},{10,7},{9,12},{12,9},{1... | collective-permute-start | bytes 245768 | tf_op jit(solution)/shard_map/ppermute | solution.py:447
  58.2 5.7 %collective-permute-start.27 = (bf16[5,64,128]{2,1,0:T(8,128)(2,1)S(1)}, bf16[5,64,128]{2,1,0:T(8,128)(2,1)S(1)}, u32[]{:S(2)}, u32[]{:S(2)}) collective-permute-start(bf16[5,64,128]{2,1,0:T(8,128)(2,1)S(1)} %get-tuple-element.153), channel_id=1, source_target_pairs={{1,4},{4,1},{3,6},{6,3},{5,8},{8,5},{7,10},{10,7},{9,12},{12,9},{1... | collective-permute-start | bytes 245768 | tf_op jit(solution)/shard_map/ppermute | solution.py:447
  61.3 5.9 %collective-permute-start.33 = (bf16[5,64,128]{2,1,0:T(8,128)(2,1)S(1)}, bf16[5,64,128]{2,1,0:T(8,128)(2,1)S(1)}, u32[]{:S(2)}, u32[]{:S(2)}) collective-permute-start(bf16[5,64,128]{2,1,0:T(8,128)(2,1)S(1)} %get-tuple-element.163), channel_id=1, source_target_pairs={{1,4},{4,1},{3,6},{6,3},{5,8},{8,5},{7,10},{10,7},{9,12},{12,9},{1... | collective-permute-start | bytes 245768 | tf_op jit(solution)/shard_map/ppermute | solution.py:447
  64.8 5.7 %collective-permute-start.29 = (bf16[5,64,128]{2,1,0:T(8,128)(2,1)S(1)}, bf16[5,64,128]{2,1,0:T(8,128)(2,1)S(1)}, u32[]{:S(2)}, u32[]{:S(2)}) collective-permute-start(bf16[5,64,128]{2,1,0:T(8,128)(2,1)S(1)} %get-tuple-element.156), channel_id=1, source_target_pairs={{1,4},{4,1},{3,6},{6,3},{5,8},{8,5},{7,10},{10,7},{9,12},{12,9},{1... | collective-permute-start | bytes 245768 | tf_op jit(solution)/shard_map/ppermute | solution.py:447
  68.1 5.9 %collective-permute-start.35 = (bf16[5,64,128]{2,1,0:T(8,128)(2,1)S(1)}, bf16[5,64,128]{2,1,0:T(8,128)(2,1)S(1)}, u32[]{:S(2)}, u32[]{:S(2)}) collective-permute-start(bf16[5,64,128]{2,1,0:T(8,128)(2,1)S(1)} %get-tuple-element.166), channel_id=1, source_target_pairs={{1,4},{4,1},{3,6},{6,3},{5,8},{8,5},{7,10},{10,7},{9,12},{12,9},{1... | collective-permute-start | bytes 245768 | tf_op jit(solution)/shard_map/ppermute | solution.py:447
  71.4 6.1 %collective-permute-start.37 = (bf16[5,64,128]{2,1,0:T(8,128)(2,1)S(1)}, bf16[5,64,128]{2,1,0:T(8,128)(2,1)S(1)}, u32[]{:S(2)}, u32[]{:S(2)}) collective-permute-start(bf16[5,64,128]{2,1,0:T(8,128)(2,1)S(1)} %get-tuple-element.170), channel_id=1, source_target_pairs={{1,4},{4,1},{3,6},{6,3},{5,8},{8,5},{7,10},{10,7},{9,12},{12,9},{1... | collective-permute-start | bytes 245768 | tf_op jit(solution)/shard_map/ppermute | solution.py:447
  75.5 5.9 %collective-permute-start.43 = (bf16[5,64,128]{2,1,0:T(8,128)(2,1)S(1)}, bf16[5,64,128]{2,1,0:T(8,128)(2,1)S(1)}, u32[]{:S(2)}, u32[]{:S(2)}) collective-permute-start(bf16[5,64,128]{2,1,0:T(8,128)(2,1)S(1)} %get-tuple-element.180), channel_id=1, source_target_pairs={{1,4},{4,1},{3,6},{6,3},{5,8},{8,5},{7,10},{10,7},{9,12},{12,9},{1... | collective-permute-start | bytes 245768 | tf_op jit(solution)/shard_map/ppermute | solution.py:447
  79.0 5.7 %collective-permute-start.39 = (bf16[5,64,128]{2,1,0:T(8,128)(2,1)S(1)}, bf16[5,64,128]{2,1,0:T(8,128)(2,1)S(1)}, u32[]{:S(2)}, u32[]{:S(2)}) collective-permute-start(bf16[5,64,128]{2,1,0:T(8,128)(2,1)S(1)} %get-tuple-element.173), channel_id=1, source_target_pairs={{1,4},{4,1},{3,6},{6,3},{5,8},{8,5},{7,10},{10,7},{9,12},{12,9},{1... | collective-permute-start | bytes 245768 | tf_op jit(solution)/shard_map/ppermute | solution.py:447
  82.2 5.9 %collective-permute-start.45 = (bf16[5,64,128]{2,1,0:T(8,128)(2,1)S(1)}, bf16[5,64,128]{2,1,0:T(8,128)(2,1)S(1)}, u32[]{:S(2)}, u32[]{:S(2)}) collective-permute-start(bf16[5,64,128]{2,1,0:T(8,128)(2,1)S(1)} %get-tuple-element.183), channel_id=1, source_target_pairs={{1,4},{4,1},{3,6},{6,3},{5,8},{8,5},{7,10},{10,7},{9,12},{12,9},{1... | collective-permute-start | bytes 245768 | tf_op jit(solution)/shard_map/ppermute | solution.py:447
  84.1 3.9 %collective-permute-start.46 = (bf16[5,64,128]{2,1,0:T(8,128)(2,1)S(1)}, bf16[5,64,128]{2,1,0:T(8,128)(2,1)S(1)}, u32[]{:S(2)}, u32[]{:S(2)}) collective-permute-start(bf16[5,64,128]{2,1,0:T(8,128)(2,1)S(1)} %get-tuple-element.184), channel_id=1, source_target_pairs={{0,1},{1,0},{2,3},{3,2},{4,5},{5,4},{6,7},{7,6},{8,9},{9,8},{10,11... | collective-permute-start | bytes 245768 | tf_op jit(solution)/shard_map/ppermute | solution.py:438
  85.6 7.0 %collective-permute-start.41 = (bf16[5,64,128]{2,1,0:T(8,128)(2,1)S(1)}, bf16[5,64,128]{2,1,0:T(8,128)(2,1)S(1)}, u32[]{:S(2)}, u32[]{:S(2)}) collective-permute-start(bf16[5,64,128]{2,1,0:T(8,128)(2,1)S(1)} %get-tuple-element.176), channel_id=1, source_target_pairs={{1,4},{4,1},{3,6},{6,3},{5,8},{8,5},{7,10},{10,7},{9,12},{12,9},{1... | collective-permute-start | bytes 245768 | tf_op jit(solution)/shard_map/ppermute | solution.py:447
  88.1 4.5 %collective-permute-start.42 = (bf16[5,64,128]{2,1,0:T(8,128)(2,1)S(1)}, bf16[5,64,128]{2,1,0:T(8,128)(2,1)S(1)}, u32[]{:S(2)}, u32[]{:S(2)}) collective-permute-start(bf16[5,64,128]{2,1,0:T(8,128)(2,1)S(1)} %get-tuple-element.177), channel_id=1, source_target_pairs={{0,1},{1,0},{2,3},{3,2},{4,5},{5,4},{6,7},{7,6},{8,9},{9,8},{10,11... | collective-permute-start | bytes 245768 | tf_op jit(solution)/shard_map/ppermute | solution.py:438
  89.2 5.8 %collective-permute-start.47 = (bf16[5,64,128]{2,1,0:T(8,128)(2,1)S(1)}, bf16[5,64,128]{2,1,0:T(8,128)(2,1)S(1)}, u32[]{:S(2)}, u32[]{:S(2)}) collective-permute-start(bf16[5,64,128]{2,1,0:T(8,128)(2,1)S(1)} %get-tuple-element.186), channel_id=1, source_target_pairs={{1,4},{4,1},{3,6},{6,3},{5,8},{8,5},{7,10},{10,7},{9,12},{12,9},{1... | collective-permute-start | bytes 245768 | tf_op jit(solution)/shard_map/ppermute | solution.py:447
  91.1 5.3 %collective-permute-start.48 = (bf16[5,64,128]{2,1,0:T(8,128)(2,1)S(1)}, bf16[5,64,128]{2,1,0:T(8,128)(2,1)S(1)}, u32[]{:S(2)}, u32[]{:S(2)}) collective-permute-start(bf16[5,64,128]{2,1,0:T(8,128)(2,1)S(1)} %get-tuple-element.187), channel_id=1, source_target_pairs={{0,1},{1,0},{2,3},{3,2},{4,5},{5,4},{6,7},{7,6},{8,9},{9,8},{10,11... | collective-permute-start | bytes 245768 | tf_op jit(solution)/shard_map/ppermute | solution.py:438
  91.1 5.9 %collective-permute-start.49 = (bf16[8,64,128]{2,1,0:T(8,128)(2,1)S(1)}, bf16[8,64,128]{2,1,0:T(8,128)(2,1)S(1)}, u32[]{:S(2)}, u32[]{:S(2)}) collective-permute-start(bf16[8,64,128]{2,1,0:T(8,128)(2,1)S(1)} %get-tuple-element.185.own.refs_2_.refs_4_), channel_id=1, source_target_pairs={{2,0},{3,1},{0,2},{1,3},{6,4},{7,5},{4,6},{5,7},{10,8},{11,9},{8,1... | collective-permute-start | bytes 393224 | tf_op jit(solution)/shard_map/ppermute | solution.py:459
  93.5 5.7 %collective-permute-start.50 = (bf16[5,64,128]{2,1,0:T(8,128)(2,1)S(1)}, bf16[5,64,128]{2,1,0:T(8,128)(2,1)S(1)}, u32[]{:S(2)}, u32[]{:S(2)}) collective-permute-start(bf16[5,64,128]{2,1,0:T(8,128)(2,1)S(1)} %get-tuple-element.190), channel_id=1, source_target_pairs={{1,4},{4,1},{3,6},{6,3},{5,8},{8,5},{7,10},{10,7},{9,12},{12,9},{1... | collective-permute-start | bytes 245768 | tf_op jit(solution)/shard_map/ppermute | solution.py:447
  94.9 4.2 %collective-permute-start.51 = (bf16[5,64,128]{2,1,0:T(8,128)(2,1)S(1)}, bf16[5,64,128]{2,1,0:T(8,128)(2,1)S(1)}, u32[]{:S(2)}, u32[]{:S(2)}) collective-permute-start(bf16[5,64,128]{2,1,0:T(8,128)(2,1)S(1)} %get-tuple-element.191), channel_id=1, source_target_pairs={{0,1},{1,0},{2,3},{3,2},{4,5},{5,4},{6,7},{7,6},{8,9},{9,8},{10,11... | collective-permute-start | bytes 245768 | tf_op jit(solution)/shard_map/ppermute | solution.py:438
  94.9 5.9 %collective-permute-start.52 = (bf16[8,64,128]{2,1,0:T(8,128)(2,1)S(1)}, bf16[8,64,128]{2,1,0:T(8,128)(2,1)S(1)}, u32[]{:S(2)}, u32[]{:S(2)}) collective-permute-start(bf16[8,64,128]{2,1,0:T(8,128)(2,1)S(1)} %get-tuple-element.189.own.refs_3_.refs_5_), channel_id=1, source_target_pairs={{2,0},{3,1},{0,2},{1,3},{6,4},{7,5},{4,6},{5,7},{10,8},{11,9},{8,1... | collective-permute-start | bytes 393224 | tf_op jit(solution)/shard_map/ppermute | solution.py:459
  102.8 4.3 %collective-permute-start.56 = (bf16[208,128]{1,0:T(8,128)(2,1)S(1)}, bf16[208,128]{1,0:T(8,128)(2,1)S(1)}, u32[]{:S(2)}, u32[]{:S(2)}) collective-permute-start(bf16[208,128]{1,0:T(8,128)(2,1)S(1)} %add.9.refs_0_), channel_id=1, source_target_pairs={{0,12},{4,0},{8,4},{12,8},{1,13},{5,1},{9,5},{13,9},{2,14},{6,2},{... | collective-permute-start | bytes 159752 | tf_op jit(solution)/shard_map/ppermute | solution.py:620
  104.9 6.2 %collective-permute-start.55 = (bf16[208,128]{1,0:T(8,128)(2,1)S(1)}, bf16[208,128]{1,0:T(8,128)(2,1)S(1)}, u32[]{:S(2)}, u32[]{:S(2)}) collective-permute-start(bf16[208,128]{1,0:T(8,128)(2,1)S(1)} %add.9.refs_0_), channel_id=1, source_target_pairs={{0,8},{4,12},{8,0},{12,4},{1,9},{5,13},{9,1},{13,5},{2,10},{6,14},... | collective-permute-start | bytes 159752 | tf_op jit(solution)/shard_map/ppermute | solution.py:620
  104.9 6.2 %collective-permute-start.54 = (bf16[208,128]{1,0:T(8,128)(2,1)S(1)}, bf16[208,128]{1,0:T(8,128)(2,1)S(1)}, u32[]{:S(2)}, u32[]{:S(2)}) collective-permute-start(bf16[208,128]{1,0:T(8,128)(2,1)S(1)} %add.9.refs_0_), channel_id=1, source_target_pairs={{0,4},{4,8},{8,12},{12,0},{1,5},{5,9},{9,13},{13,1},{2,6},{6,10},{... | collective-permute-start | bytes 159752 | tf_op jit(solution)/shard_map/ppermute | solution.py:620
  105.7 6.9 %collective-permute-start.60 = (bf16[8,64,128]{2,1,0:T(8,128)(2,1)S(1)}, bf16[8,64,128]{2,1,0:T(8,128)(2,1)S(1)}, u32[]{:S(2)}, u32[]{:S(2)}) collective-permute-start(bf16[8,64,128]{2,1,0:T(8,128)(2,1)S(1)} %get-tuple-element.185.own.refs_2_.refs_4_), channel_id=1, source_target_pairs={{0,1},{1,0},{2,3},{3,2},{4,5},{5,4},{6,7},{7,6},{8,9},{9,8},{10,11... | collective-permute-start | bytes 393224 | tf_op jit(solution)/shard_map/ppermute | solution.py:438
  105.8 9.8 %collective-permute-start.61 = (bf16[8,64,128]{2,1,0:T(8,128)(2,1)S(1)}, bf16[8,64,128]{2,1,0:T(8,128)(2,1)S(1)}, u32[]{:S(2)}, u32[]{:S(2)}) collective-permute-start(bf16[8,64,128]{2,1,0:T(8,128)(2,1)S(1)} %get-tuple-element.189.own.refs_3_.refs_5_), channel_id=1, source_target_pairs={{0,1},{1,0},{2,3},{3,2},{4,5},{5,4},{6,7},{7,6},{8,9},{9,8},{10,11... | collective-permute-start | bytes 393224 | tf_op jit(solution)/shard_map/ppermute | solution.py:438
  107.1 8.4 %collective-permute-start.62 = (bf16[8,64,128]{2,1,0:T(8,128)(2,1)S(1)}, bf16[8,64,128]{2,1,0:T(8,128)(2,1)S(1)}, u32[]{:S(2)}, u32[]{:S(2)}) collective-permute-start(bf16[8,64,128]{2,1,0:T(8,128)(2,1)S(1)} %collective-permute-done.49.y_other.refs_4_.refs_6_), channel_id=1, source_target_pairs={{0,1},{1,0},{2,3},{3,2},{4,5},{5,4},{6,7},{7,6},{8,9},{9,8},{10,11... | collective-permute-start | bytes 393224 | tf_op jit(solution)/shard_map/ppermute | solution.py:438
  111.1 4.4 %collective-permute-start.63 = (bf16[8,64,128]{2,1,0:T(8,128)(2,1)S(1)}, bf16[8,64,128]{2,1,0:T(8,128)(2,1)S(1)}, u32[]{:S(2)}, u32[]{:S(2)}) collective-permute-start(bf16[8,64,128]{2,1,0:T(8,128)(2,1)S(1)} %collective-permute-done.52.refs_5_.refs_7_), channel_id=1, source_target_pairs={{0,1},{1,0},{2,3},{3,2},{4,5},{5,4},{6,7},{7,6},{8,9},{9,8},{10,11... | collective-permute-start | bytes 393224 | tf_op jit(solution)/shard_map/ppermute | solution.py:438
  111.2 4.3 %collective-permute-start.57 = (bf16[208,128]{1,0:T(8,128)(2,1)S(1)}, bf16[208,128]{1,0:T(8,128)(2,1)S(1)}, u32[]{:S(2)}, u32[]{:S(2)}) collective-permute-start(bf16[208,128]{1,0:T(8,128)(2,1)S(1)} %sum.1.refs_0_), channel_id=1, source_target_pairs={{2,0},{3,1},{0,2},{1,3},{6,4},{7,5},{4,6},{5,7},{10,8},{11,9},{8,1... | collective-permute-start | bytes 159752 | tf_op jit(solution)/shard_map/ppermute | solution.py:459
  (16 other events, 53.0 us)

commit v7 on v6

--- a/solution.py
+++ b/solution.py
@@ -261,7 +261,7 @@
     *payloads, out, held = refs
     count = len(payloads)
     for step, payload in enumerate(payloads):
-        held[lax.rem(ints[DEVICE_ROW] + count - step, count)] = payload[...]
+        held[lax.bitwise_xor(ints[DEVICE_ROW], jnp.int32(step))] = payload[...]
     body = out.shape[0] - DIAGONAL_ROWS
     total = held[0, :body, :].astype(F32)
     diagonal = diagonal_of(held.at[0])
@@ -280,6 +280,14 @@
     return high, middle, low
 
 
+def three_terms(left, right, axis):
+    (high, middle, _), (other, little, _) = split3(left), split3(right)
+    return (
+        jnp.concatenate([high, high, middle], axis=1),
+        jnp.concatenate([other, little, other], axis=axis),
+    )
+
+
 def panel_inverse(block):
     lane = lax.broadcasted_iota(jnp.int32, (PANEL, 128), 1)
     rows = lax.broadcasted_iota(jnp.int32, (PANEL, 128), 0)
@@ -292,7 +300,7 @@
         return jnp.broadcast_to(value[k % SUBLANES : k % SUBLANES + 1], (SUBLANES, 128))
 
     pivots = [jnp.ones((SUBLANES, 128), F32) for _ in range(count)]
-    for start, group in ((0, 16), (16, 16)):
+    for start, group in ((0, 8), (8, 8), (16, 16)):
         columns = {
             k: {
                 v: jnp.broadcast_to(pieces[v][:, k : k + 1], (SUBLANES, 128))
@@ -389,11 +397,9 @@
     start = pl.multiple_of(col * local_vecs, local_vecs)
     own_rows = inverse[pl.ds(start, local_vecs), :]
     gram_h = (pair[1] + pair[1].T) * scale
-    half_way = jnp.dot(
-        own_rows, gram_h, precision=lax.Precision.HIGHEST, preferred_element_type=F32
-    )
+    half_way = jnp.dot(*three_terms(own_rows, gram_h, 0), preferred_element_type=F32)
     reduced[...] = lax.dot_general(
-        half_way, inverse[...], NT, precision=lax.Precision.HIGHEST, preferred_element_type=F32
+        *three_terms(half_way, inverse[...], 1), NT, preferred_element_type=F32
     )
     rotation = own_rows.astype(BF16)
     turned = []
@@ -615,9 +621,9 @@
         return call(add_kernel, "add", (), (left, right), (payload,), [], row_flops // 8)[0]
 
     summed = add(keep, swap_cores(send))
-    if num_rows <= 4:
+    if num_rows in (2, 4):
         others = [
-            lax.ppermute(summed, "row", [(r, (r + step) % num_rows) for r in range(num_rows)])
+            lax.ppermute(summed, "row", [(r, r ^ step) for r in range(num_rows)])
             for step in range(1, num_rows)
         ]
         (summed,) = call(

time: 127 us -> 127 us (level)
  waiting for transfers between devices: 18.2 us -> 16.3 us
  starting transfers between devices: 61.7 us -> 63.3 us
    ppermute x3, waiting for transfers between devices: 4.87 us -> 3.07 us  [local(): lax.ppermute(summed, 'row', [(r, r ^ step) for r in range(num_rows)])]
    ppermute x3, starting transfers between devices: 2.93 us -> 4.45 us  [local(): lax.ppermute(summed, 'row', [(r, r ^ step) for r in range(num_rows)])]
where the time goes in v7:
time: 127 us; the launch traced here: 126 us
  starting transfers between devices  63.3 us (50%)
  Pallas kernels  44.4 us (35%)
  waiting for transfers between devices  16.3 us (13%)
  between operations  2.31 us (2%)
    ppermute x25, starting transfers between devices, swap_chips(): return lax.ppermute(value, ('row', 'col'), pairs)  50.5 us
    pallas_call x30, Pallas kernels, call(): pl.pallas_call(kernel, name=name, out_shape=outs, in_specs=[SMEM] * len(s...  39.8 us
    ppermute x25, waiting for transfers between devices, swap_chips(): return lax.ppermute(value, ('row', 'col'), pairs)  7.35 us
    ppermute x3, starting transfers between devices, local(): lax.ppermute(summed, 'row', [(r, r ^ step) for r in range(num_rows)])  4.45 us
    ppermute x3, starting transfers between devices, from_chip(): return lax.ppermute(value, 'col', pairs)  4.39 us
    ppermute x3, waiting for transfers between devices, from_chip(): return lax.ppermute(value, 'col', pairs)  3.4 us
    ppermute x1, starting transfers between devices, next_chips(): return lax.ppermute(value, ('row', 'col'), pairs)  3.08 us
    ppermute x3, waiting for transfers between devices, local(): lax.ppermute(summed, 'row', [(r, r ^ step) for r in range(num_rows)])  3.07 us
  transfers between devices with their start and end apart: 64, of which 21 were waited for; matrix products, arithmetic and copies ran while one was open for 0% of the time, Pallas kernels for 24%

profile of v7, /device:TPU:0, one launch (start us, length us, event | category | flops | bytes accessed | tf_op | source)
XLA Modules:
  0.0 126.5 jit_solution(15078422734123565905)
XLA Ops:
  0.7 1.6 %cut.1 = (bf16[8,64,128]{2,1,0:T(8,128)(2,1)S(1)}, bf16[5,64,128]{2,1,0:T(8,128)(2,1)S(1)}, bf16[13,64,128]{2,1,0:T(8,128)(2,1)S(1)}, bf16[5,64,128]{2,1,0:T(8,128)(2,1)S(1)}, bf16[5,64,128]{2,1,0:T(8,128)(2,1)S(1)}) custom-call(s32[5]{0:T(128)S(1)} %stack.23.ints, s32[16]{0:T(128)} %sizes.3, bf16[64,2048]{1,0:T(8,128)(2,1)} %trial.1), custom_call_target="tpu_custom_call" | custom-call | tf_op jit(solution)/shard_map/cut/pallas_call | solution.py:503
  2.3 3.1 %collective-permute-start.1 = (bf16[5,64,128]{2,1,0:T(8,128)(2,1)S(1)}, bf16[5,64,128]{2,1,0:T(8,128)(2,1)S(1)}, u32[]{:S(2)}, u32[]{:S(2)}) collective-permute-start(bf16[5,64,128]{2,1,0:T(8,128)(2,1)S(1)} %get-tuple-element.105), channel_id=1, source_target_pairs={{0,4},{1,13},{2,6},{3,15},{4,8},{5,1},{6,10},{7,3},{8,12},{9,5},{1... | collective-permute-start | bytes 245768 | tf_op jit(solution)/shard_map/ppermute | solution.py:461
  5.4 1.6 %collective-permute-start.2 = (bf16[5,64,128]{2,1,0:T(8,128)(2,1)S(1)}, bf16[5,64,128]{2,1,0:T(8,128)(2,1)S(1)}, u32[]{:S(2)}, u32[]{:S(2)}) collective-permute-start(bf16[5,64,128]{2,1,0:T(8,128)(2,1)S(1)} %get-tuple-element.106), channel_id=1, source_target_pairs={{1,4},{4,1},{3,6},{6,3},{5,8},{8,5},{7,10},{10,7},{9,12},{12,9},{1... | collective-permute-start | bytes 245768 | tf_op jit(solution)/shard_map/ppermute | solution.py:453
  8.4 3.0 %load.1 = (bf16[8,9,128,128]{3,2,1,0:T(8,128)(2,1)S(1)}, bf16[8,9,128,128]{3,2,1,0:T(8,128)(2,1)S(1)}, s32[8,9]{1,0:T(8,128)S(4)}, f32[8,9]{1,0:T(8,128)S(4)}, s32[12]{0:T(128)S(4)}, /*index=5*/f32[2]{0:T(128)S(4)}) custom-call(s32[5]{0:T(128)S(1)} %stack.23.ints, f32[1]{0:T(128)S(6)} %copy.10.shift, f32[1]{0:T(128)S(6)} %copy.11.width, s32[16,9]{1,0:T(8,128)} %columns.1, ...), custom_call_target="tpu_custom_call" | custom-call | bytes 9437184 | tf_op jit(solution)/shard_map/load/pallas_call | solution.py:520
  12.0 1.5 %scaled.8 = (bf16[8,64,128]{2,1,0:T(8,128)(2,1)S(1)}, bf16[5,64,128]{2,1,0:T(8,128)(2,1)S(1)}, bf16[5,64,128]{2,1,0:T(8,128)(2,1)S(1)}) custom-call(s32[12]{0:T(128)S(4)} %get-tuple-element.99.ints, s32[8,9]{1,0:T(8,128)S(4)} %get-tuple-element.100.index, f32[8,9]{1,0:T(8,128)S(4)} %get-tuple-element.101.signs, f32[2]{0:T(128)S(4)} %get-tuple-element.102.scal, ...), custom_call_target="tpu_custom_call" | custom-call | flops 7247757312 | bytes 56623104 | tf_op jit(solution)/shard_map/scaled/pallas_call | solution.py:474
  13.5 1.7 %collective-permute-start.7 = (bf16[5,64,128]{2,1,0:T(8,128)(2,1)S(1)}, bf16[5,64,128]{2,1,0:T(8,128)(2,1)S(1)}, u32[]{:S(2)}, u32[]{:S(2)}) collective-permute-start(bf16[5,64,128]{2,1,0:T(8,128)(2,1)S(1)} %get-tuple-element.120), channel_id=1, source_target_pairs={{1,4},{4,1},{3,6},{6,3},{5,8},{8,5},{7,10},{10,7},{9,12},{12,9},{1... | collective-permute-start | bytes 245768 | tf_op jit(solution)/shard_map/ppermute | solution.py:453
  15.2 1.5 %scaled.9 = (bf16[8,64,128]{2,1,0:T(8,128)(2,1)S(1)}, bf16[5,64,128]{2,1,0:T(8,128)(2,1)S(1)}, bf16[5,64,128]{2,1,0:T(8,128)(2,1)S(1)}) custom-call(s32[12]{0:T(128)S(4)} %get-tuple-element.99.ints, s32[8,9]{1,0:T(8,128)S(4)} %get-tuple-element.100.index, f32[8,9]{1,0:T(8,128)S(4)} %get-tuple-element.101.signs, f32[2]{0:T(128)S(4)} %get-tuple-element.102.scal, ...), custom_call_target="tpu_custom_call" | custom-call | flops 7247757312 | bytes 56623104 | tf_op jit(solution)/shard_map/scaled/pallas_call | solution.py:474
  16.7 1.9 %collective-permute-start.3 = (bf16[5,64,128]{2,1,0:T(8,128)(2,1)S(1)}, bf16[5,64,128]{2,1,0:T(8,128)(2,1)S(1)}, u32[]{:S(2)}, u32[]{:S(2)}) collective-permute-start(bf16[5,64,128]{2,1,0:T(8,128)(2,1)S(1)} %get-tuple-element.113), channel_id=1, source_target_pairs={{1,4},{4,1},{3,6},{6,3},{5,8},{8,5},{7,10},{10,7},{9,12},{12,9},{1... | collective-permute-start | bytes 245768 | tf_op jit(solution)/shard_map/ppermute | solution.py:453
  20.2 1.6 %collective-permute-start.9 = (bf16[5,64,128]{2,1,0:T(8,128)(2,1)S(1)}, bf16[5,64,128]{2,1,0:T(8,128)(2,1)S(1)}, u32[]{:S(2)}, u32[]{:S(2)}) collective-permute-start(bf16[5,64,128]{2,1,0:T(8,128)(2,1)S(1)} %get-tuple-element.123), channel_id=1, source_target_pairs={{1,4},{4,1},{3,6},{6,3},{5,8},{8,5},{7,10},{10,7},{9,12},{12,9},{1... | collective-permute-start | bytes 245768 | tf_op jit(solution)/shard_map/ppermute | solution.py:453
  23.5 1.9 %collective-permute-start.5 = (bf16[5,64,128]{2,1,0:T(8,128)(2,1)S(1)}, bf16[5,64,128]{2,1,0:T(8,128)(2,1)S(1)}, u32[]{:S(2)}, u32[]{:S(2)}) collective-permute-start(bf16[5,64,128]{2,1,0:T(8,128)(2,1)S(1)} %get-tuple-element.116), channel_id=1, source_target_pairs={{1,4},{4,1},{3,6},{6,3},{5,8},{8,5},{7,10},{10,7},{9,12},{12,9},{1... | collective-permute-start | bytes 245768 | tf_op jit(solution)/shard_map/ppermute | solution.py:453
  26.8 1.8 %collective-permute-start.11 = (bf16[5,64,128]{2,1,0:T(8,128)(2,1)S(1)}, bf16[5,64,128]{2,1,0:T(8,128)(2,1)S(1)}, u32[]{:S(2)}, u32[]{:S(2)}) collective-permute-start(bf16[5,64,128]{2,1,0:T(8,128)(2,1)S(1)} %get-tuple-element.126), channel_id=1, source_target_pairs={{1,4},{4,1},{3,6},{6,3},{5,8},{8,5},{7,10},{10,7},{9,12},{12,9},{1... | collective-permute-start | bytes 245768 | tf_op jit(solution)/shard_map/ppermute | solution.py:453
  30.1 2.0 %collective-permute-start.13 = (bf16[5,64,128]{2,1,0:T(8,128)(2,1)S(1)}, bf16[5,64,128]{2,1,0:T(8,128)(2,1)S(1)}, u32[]{:S(2)}, u32[]{:S(2)}) collective-permute-start(bf16[5,64,128]{2,1,0:T(8,128)(2,1)S(1)} %get-tuple-element.130), channel_id=1, source_target_pairs={{1,4},{4,1},{3,6},{6,3},{5,8},{8,5},{7,10},{10,7},{9,12},{12,9},{1... | collective-permute-start | bytes 245768 | tf_op jit(solution)/shard_map/ppermute | solution.py:453
  32.5 1.5 %scaled.10 = (bf16[8,64,128]{2,1,0:T(8,128)(2,1)S(1)}, bf16[5,64,128]{2,1,0:T(8,128)(2,1)S(1)}, bf16[5,64,128]{2,1,0:T(8,128)(2,1)S(1)}) custom-call(s32[12]{0:T(128)S(4)} %get-tuple-element.99.ints, s32[8,9]{1,0:T(8,128)S(4)} %get-tuple-element.100.index, f32[8,9]{1,0:T(8,128)S(4)} %get-tuple-element.101.signs, f32[2]{0:T(128)S(4)} %get-tuple-element.102.scal, ...), custom_call_target="tpu_custom_call" | custom-call | flops 7247757312 | bytes 56623104 | tf_op jit(solution)/shard_map/scaled/pallas_call | solution.py:474
  34.0 2.0 %collective-permute-start.19 = (bf16[5,64,128]{2,1,0:T(8,128)(2,1)S(1)}, bf16[5,64,128]{2,1,0:T(8,128)(2,1)S(1)}, u32[]{:S(2)}, u32[]{:S(2)}) collective-permute-start(bf16[5,64,128]{2,1,0:T(8,128)(2,1)S(1)} %get-tuple-element.140), channel_id=1, source_target_pairs={{1,4},{4,1},{3,6},{6,3},{5,8},{8,5},{7,10},{10,7},{9,12},{12,9},{1... | collective-permute-start | bytes 245768 | tf_op jit(solution)/shard_map/ppermute | solution.py:453
  36.0 1.5 %scaled.11 = (bf16[8,64,128]{2,1,0:T(8,128)(2,1)S(1)}, bf16[5,64,128]{2,1,0:T(8,128)(2,1)S(1)}, bf16[5,64,128]{2,1,0:T(8,128)(2,1)S(1)}) custom-call(s32[12]{0:T(128)S(4)} %get-tuple-element.99.ints, s32[8,9]{1,0:T(8,128)S(4)} %get-tuple-element.100.index, f32[8,9]{1,0:T(8,128)S(4)} %get-tuple-element.101.signs, f32[2]{0:T(128)S(4)} %get-tuple-element.102.scal, ...), custom_call_target="tpu_custom_call" | custom-call | flops 7247757312 | bytes 56623104 | tf_op jit(solution)/shard_map/scaled/pallas_call | solution.py:474
  37.5 1.9 %collective-permute-start.15 = (bf16[5,64,128]{2,1,0:T(8,128)(2,1)S(1)}, bf16[5,64,128]{2,1,0:T(8,128)(2,1)S(1)}, u32[]{:S(2)}, u32[]{:S(2)}) collective-permute-start(bf16[5,64,128]{2,1,0:T(8,128)(2,1)S(1)} %get-tuple-element.133), channel_id=1, source_target_pairs={{1,4},{4,1},{3,6},{6,3},{5,8},{8,5},{7,10},{10,7},{9,12},{12,9},{1... | collective-permute-start | bytes 245768 | tf_op jit(solution)/shard_map/ppermute | solution.py:453
  40.6 2.0 %collective-permute-start.21 = (bf16[5,64,128]{2,1,0:T(8,128)(2,1)S(1)}, bf16[5,64,128]{2,1,0:T(8,128)(2,1)S(1)}, u32[]{:S(2)}, u32[]{:S(2)}) collective-permute-start(bf16[5,64,128]{2,1,0:T(8,128)(2,1)S(1)} %get-tuple-element.143), channel_id=1, source_target_pairs={{1,4},{4,1},{3,6},{6,3},{5,8},{8,5},{7,10},{10,7},{9,12},{12,9},{1... | collective-permute-start | bytes 245768 | tf_op jit(solution)/shard_map/ppermute | solution.py:453
  44.1 2.0 %collective-permute-start.17 = (bf16[5,64,128]{2,1,0:T(8,128)(2,1)S(1)}, bf16[5,64,128]{2,1,0:T(8,128)(2,1)S(1)}, u32[]{:S(2)}, u32[]{:S(2)}) collective-permute-start(bf16[5,64,128]{2,1,0:T(8,128)(2,1)S(1)} %get-tuple-element.136), channel_id=1, source_target_pairs={{1,4},{4,1},{3,6},{6,3},{5,8},{8,5},{7,10},{10,7},{9,12},{12,9},{1... | collective-permute-start | bytes 245768 | tf_op jit(solution)/shard_map/ppermute | solution.py:453
  47.2 2.2 %collective-permute-start.23 = (bf16[5,64,128]{2,1,0:T(8,128)(2,1)S(1)}, bf16[5,64,128]{2,1,0:T(8,128)(2,1)S(1)}, u32[]{:S(2)}, u32[]{:S(2)}) collective-permute-start(bf16[5,64,128]{2,1,0:T(8,128)(2,1)S(1)} %get-tuple-element.146), channel_id=1, source_target_pairs={{1,4},{4,1},{3,6},{6,3},{5,8},{8,5},{7,10},{10,7},{9,12},{12,9},{1... | collective-permute-start | bytes 245768 | tf_op jit(solution)/shard_map/ppermute | solution.py:453
  50.9 2.2 %collective-permute-start.25 = (bf16[5,64,128]{2,1,0:T(8,128)(2,1)S(1)}, bf16[5,64,128]{2,1,0:T(8,128)(2,1)S(1)}, u32[]{:S(2)}, u32[]{:S(2)}) collective-permute-start(bf16[5,64,128]{2,1,0:T(8,128)(2,1)S(1)} %get-tuple-element.150), channel_id=1, source_target_pairs={{1,4},{4,1},{3,6},{6,3},{5,8},{8,5},{7,10},{10,7},{9,12},{12,9},{1... | collective-permute-start | bytes 245768 | tf_op jit(solution)/shard_map/ppermute | solution.py:453
  53.1 1.5 %scaled.12 = (bf16[8,64,128]{2,1,0:T(8,128)(2,1)S(1)}, bf16[5,64,128]{2,1,0:T(8,128)(2,1)S(1)}, bf16[5,64,128]{2,1,0:T(8,128)(2,1)S(1)}) custom-call(s32[12]{0:T(128)S(4)} %get-tuple-element.99.ints, s32[8,9]{1,0:T(8,128)S(4)} %get-tuple-element.100.index, f32[8,9]{1,0:T(8,128)S(4)} %get-tuple-element.101.signs, f32[2]{0:T(128)S(4)} %get-tuple-element.102.scal, ...), custom_call_target="tpu_custom_call" | custom-call | flops 7247757312 | bytes 56623104 | tf_op jit(solution)/shard_map/scaled/pallas_call | solution.py:474
  54.6 2.1 %collective-permute-start.31 = (bf16[5,64,128]{2,1,0:T(8,128)(2,1)S(1)}, bf16[5,64,128]{2,1,0:T(8,128)(2,1)S(1)}, u32[]{:S(2)}, u32[]{:S(2)}) collective-permute-start(bf16[5,64,128]{2,1,0:T(8,128)(2,1)S(1)} %get-tuple-element.160), channel_id=1, source_target_pairs={{1,4},{4,1},{3,6},{6,3},{5,8},{8,5},{7,10},{10,7},{9,12},{12,9},{1... | collective-permute-start | bytes 245768 | tf_op jit(solution)/shard_map/ppermute | solution.py:453
  56.7 1.5 %scaled.13 = (bf16[8,64,128]{2,1,0:T(8,128)(2,1)S(1)}, bf16[5,64,128]{2,1,0:T(8,128)(2,1)S(1)}, bf16[5,64,128]{2,1,0:T(8,128)(2,1)S(1)}) custom-call(s32[12]{0:T(128)S(4)} %get-tuple-element.99.ints, s32[8,9]{1,0:T(8,128)S(4)} %get-tuple-element.100.index, f32[8,9]{1,0:T(8,128)S(4)} %get-tuple-element.101.signs, f32[2]{0:T(128)S(4)} %get-tuple-element.102.scal, ...), custom_call_target="tpu_custom_call" | custom-call | flops 7247757312 | bytes 56623104 | tf_op jit(solution)/shard_map/scaled/pallas_call | solution.py:474
  58.2 2.2 %collective-permute-start.27 = (bf16[5,64,128]{2,1,0:T(8,128)(2,1)S(1)}, bf16[5,64,128]{2,1,0:T(8,128)(2,1)S(1)}, u32[]{:S(2)}, u32[]{:S(2)}) collective-permute-start(bf16[5,64,128]{2,1,0:T(8,128)(2,1)S(1)} %get-tuple-element.153), channel_id=1, source_target_pairs={{1,4},{4,1},{3,6},{6,3},{5,8},{8,5},{7,10},{10,7},{9,12},{12,9},{1... | collective-permute-start | bytes 245768 | tf_op jit(solution)/shard_map/ppermute | solution.py:453
  61.3 2.1 %collective-permute-start.33 = (bf16[5,64,128]{2,1,0:T(8,128)(2,1)S(1)}, bf16[5,64,128]{2,1,0:T(8,128)(2,1)S(1)}, u32[]{:S(2)}, u32[]{:S(2)}) collective-permute-start(bf16[5,64,128]{2,1,0:T(8,128)(2,1)S(1)} %get-tuple-element.163), channel_id=1, source_target_pairs={{1,4},{4,1},{3,6},{6,3},{5,8},{8,5},{7,10},{10,7},{9,12},{12,9},{1... | collective-permute-start | bytes 245768 | tf_op jit(solution)/shard_map/ppermute | solution.py:453
  64.8 2.3 %collective-permute-start.29 = (bf16[5,64,128]{2,1,0:T(8,128)(2,1)S(1)}, bf16[5,64,128]{2,1,0:T(8,128)(2,1)S(1)}, u32[]{:S(2)}, u32[]{:S(2)}) collective-permute-start(bf16[5,64,128]{2,1,0:T(8,128)(2,1)S(1)} %get-tuple-element.156), channel_id=1, source_target_pairs={{1,4},{4,1},{3,6},{6,3},{5,8},{8,5},{7,10},{10,7},{9,12},{12,9},{1... | collective-permute-start | bytes 245768 | tf_op jit(solution)/shard_map/ppermute | solution.py:453
  68.0 2.1 %collective-permute-start.35 = (bf16[5,64,128]{2,1,0:T(8,128)(2,1)S(1)}, bf16[5,64,128]{2,1,0:T(8,128)(2,1)S(1)}, u32[]{:S(2)}, u32[]{:S(2)}) collective-permute-start(bf16[5,64,128]{2,1,0:T(8,128)(2,1)S(1)} %get-tuple-element.166), channel_id=1, source_target_pairs={{1,4},{4,1},{3,6},{6,3},{5,8},{8,5},{7,10},{10,7},{9,12},{12,9},{1... | collective-permute-start | bytes 245768 | tf_op jit(solution)/shard_map/ppermute | solution.py:453
  71.4 2.5 %collective-permute-start.37 = (bf16[5,64,128]{2,1,0:T(8,128)(2,1)S(1)}, bf16[5,64,128]{2,1,0:T(8,128)(2,1)S(1)}, u32[]{:S(2)}, u32[]{:S(2)}) collective-permute-start(bf16[5,64,128]{2,1,0:T(8,128)(2,1)S(1)} %get-tuple-element.170), channel_id=1, source_target_pairs={{1,4},{4,1},{3,6},{6,3},{5,8},{8,5},{7,10},{10,7},{9,12},{12,9},{1... | collective-permute-start | bytes 245768 | tf_op jit(solution)/shard_map/ppermute | solution.py:453
  73.9 1.5 %scaled.14 = (bf16[8,64,128]{2,1,0:T(8,128)(2,1)S(1)}, bf16[5,64,128]{2,1,0:T(8,128)(2,1)S(1)}, bf16[5,64,128]{2,1,0:T(8,128)(2,1)S(1)}) custom-call(s32[12]{0:T(128)S(4)} %get-tuple-element.99.ints, s32[8,9]{1,0:T(8,128)S(4)} %get-tuple-element.100.index, f32[8,9]{1,0:T(8,128)S(4)} %get-tuple-element.101.signs, f32[2]{0:T(128)S(4)} %get-tuple-element.102.scal, ...), custom_call_target="tpu_custom_call" | custom-call | flops 7247757312 | bytes 56623104 | tf_op jit(solution)/shard_map/scaled/pallas_call | solution.py:474
  75.4 2.1 %collective-permute-start.43 = (bf16[5,64,128]{2,1,0:T(8,128)(2,1)S(1)}, bf16[5,64,128]{2,1,0:T(8,128)(2,1)S(1)}, u32[]{:S(2)}, u32[]{:S(2)}) collective-permute-start(bf16[5,64,128]{2,1,0:T(8,128)(2,1)S(1)} %get-tuple-element.180), channel_id=1, source_target_pairs={{1,4},{4,1},{3,6},{6,3},{5,8},{8,5},{7,10},{10,7},{9,12},{12,9},{1... | collective-permute-start | bytes 245768 | tf_op jit(solution)/shard_map/ppermute | solution.py:453
  77.5 1.5 %scaled.15 = (bf16[8,64,128]{2,1,0:T(8,128)(2,1)S(1)}, bf16[5,64,128]{2,1,0:T(8,128)(2,1)S(1)}, bf16[5,64,128]{2,1,0:T(8,128)(2,1)S(1)}) custom-call(s32[12]{0:T(128)S(4)} %get-tuple-element.99.ints, s32[8,9]{1,0:T(8,128)S(4)} %get-tuple-element.100.index, f32[8,9]{1,0:T(8,128)S(4)} %get-tuple-element.101.signs, f32[2]{0:T(128)S(4)} %get-tuple-element.102.scal, ...), custom_call_target="tpu_custom_call" | custom-call | flops 7247757312 | bytes 56623104 | tf_op jit(solution)/shard_map/scaled/pallas_call | solution.py:474
  79.0 2.3 %collective-permute-start.39 = (bf16[5,64,128]{2,1,0:T(8,128)(2,1)S(1)}, bf16[5,64,128]{2,1,0:T(8,128)(2,1)S(1)}, u32[]{:S(2)}, u32[]{:S(2)}) collective-permute-start(bf16[5,64,128]{2,1,0:T(8,128)(2,1)S(1)} %get-tuple-element.173), channel_id=1, source_target_pairs={{1,4},{4,1},{3,6},{6,3},{5,8},{8,5},{7,10},{10,7},{9,12},{12,9},{1... | collective-permute-start | bytes 245768 | tf_op jit(solution)/shard_map/ppermute | solution.py:453
  82.2 2.0 %collective-permute-start.45 = (bf16[5,64,128]{2,1,0:T(8,128)(2,1)S(1)}, bf16[5,64,128]{2,1,0:T(8,128)(2,1)S(1)}, u32[]{:S(2)}, u32[]{:S(2)}) collective-permute-start(bf16[5,64,128]{2,1,0:T(8,128)(2,1)S(1)} %get-tuple-element.183), channel_id=1, source_target_pairs={{1,4},{4,1},{3,6},{6,3},{5,8},{8,5},{7,10},{10,7},{9,12},{12,9},{1... | collective-permute-start | bytes 245768 | tf_op jit(solution)/shard_map/ppermute | solution.py:453
  85.6 2.5 %collective-permute-start.41 = (bf16[5,64,128]{2,1,0:T(8,128)(2,1)S(1)}, bf16[5,64,128]{2,1,0:T(8,128)(2,1)S(1)}, u32[]{:S(2)}, u32[]{:S(2)}) collective-permute-start(bf16[5,64,128]{2,1,0:T(8,128)(2,1)S(1)} %get-tuple-element.176), channel_id=1, source_target_pairs={{1,4},{4,1},{3,6},{6,3},{5,8},{8,5},{7,10},{10,7},{9,12},{12,9},{1... | collective-permute-start | bytes 245768 | tf_op jit(solution)/shard_map/ppermute | solution.py:453
  89.1 2.0 %collective-permute-start.47 = (bf16[5,64,128]{2,1,0:T(8,128)(2,1)S(1)}, bf16[5,64,128]{2,1,0:T(8,128)(2,1)S(1)}, u32[]{:S(2)}, u32[]{:S(2)}) collective-permute-start(bf16[5,64,128]{2,1,0:T(8,128)(2,1)S(1)} %get-tuple-element.186), channel_id=1, source_target_pairs={{1,4},{4,1},{3,6},{6,3},{5,8},{8,5},{7,10},{10,7},{9,12},{12,9},{1... | collective-permute-start | bytes 245768 | tf_op jit(solution)/shard_map/ppermute | solution.py:453
  91.1 1.5 %collective-permute-start.49 = (bf16[8,64,128]{2,1,0:T(8,128)(2,1)S(1)}, bf16[8,64,128]{2,1,0:T(8,128)(2,1)S(1)}, u32[]{:S(2)}, u32[]{:S(2)}) collective-permute-start(bf16[8,64,128]{2,1,0:T(8,128)(2,1)S(1)} %get-tuple-element.185.own.refs_2_.refs_4_), channel_id=1, source_target_pairs={{2,0},{3,1},{0,2},{1,3},{6,4},{7,5},{4,6},{5,7},{10,8},{11,9},{8,1... | collective-permute-start | bytes 393224 | tf_op jit(solution)/shard_map/ppermute | solution.py:465
  93.4 1.5 %collective-permute-start.50 = (bf16[5,64,128]{2,1,0:T(8,128)(2,1)S(1)}, bf16[5,64,128]{2,1,0:T(8,128)(2,1)S(1)}, u32[]{:S(2)}, u32[]{:S(2)}) collective-permute-start(bf16[5,64,128]{2,1,0:T(8,128)(2,1)S(1)} %get-tuple-element.190), channel_id=1, source_target_pairs={{1,4},{4,1},{3,6},{6,3},{5,8},{8,5},{7,10},{10,7},{9,12},{12,9},{1... | collective-permute-start | bytes 245768 | tf_op jit(solution)/shard_map/ppermute | solution.py:453
  95.0 1.4 %collective-permute-start.52 = (bf16[8,64,128]{2,1,0:T(8,128)(2,1)S(1)}, bf16[8,64,128]{2,1,0:T(8,128)(2,1)S(1)}, u32[]{:S(2)}, u32[]{:S(2)}) collective-permute-start(bf16[8,64,128]{2,1,0:T(8,128)(2,1)S(1)} %get-tuple-element.189.own.refs_3_.refs_5_), channel_id=1, source_target_pairs={{2,0},{3,1},{0,2},{1,3},{6,4},{7,5},{4,6},{5,7},{10,8},{11,9},{8,1... | collective-permute-start | bytes 393224 | tf_op jit(solution)/shard_map/ppermute | solution.py:465
  97.0 1.5 %images.2.refs_0_ = bf16[2,64,1024]{2,1,0:T(8,128)(2,1)S(1)} custom-call(s32[12]{0:T(128)S(4)} %get-tuple-element.99.ints, s32[8,9]{1,0:T(8,128)S(4)} %get-tuple-element.100.index, f32[8,9]{1,0:T(8,128)S(4)} %get-tuple-element.101.signs, bf16[8,64,128]{2,1,0:T(8,128)(2,1)S(1)} %get-tuple-element.185.own.refs_2_.refs_4_, ...), custom_call_target="tpu_custom_call" | custom-call | flops 7247757312 | bytes 56623104 | tf_op jit(solution)/shard_map/images/pallas_call | solution.py:474
  99.2 1.5 %images.3.refs_1_ = bf16[2,64,1024]{2,1,0:T(8,128)(2,1)S(1)} custom-call(s32[12]{0:T(128)S(4)} %get-tuple-element.99.ints, s32[8,9]{1,0:T(8,128)S(4)} %get-tuple-element.100.index, f32[8,9]{1,0:T(8,128)S(4)} %get-tuple-element.101.signs, bf16[8,64,128]{2,1,0:T(8,128)(2,1)S(1)} %get-tuple-element.189.own.refs_3_.refs_5_, ...), custom_call_target="tpu_custom_call" | custom-call | flops 7247757312 | bytes 56623104 | tf_op jit(solution)/shard_map/images/pallas_call | solution.py:474
  101.6 1.2 collective-permute-done.53.right
  102.8 2.0 %collective-permute-start.56 = (bf16[208,128]{1,0:T(8,128)(2,1)S(1)}, bf16[208,128]{1,0:T(8,128)(2,1)S(1)}, u32[]{:S(2)}, u32[]{:S(2)}) collective-permute-start(bf16[208,128]{1,0:T(8,128)(2,1)S(1)} %add.9.refs_0_), channel_id=1, source_target_pairs={{0,12},{4,8},{8,4},{12,0},{1,13},{5,9},{9,5},{13,1},{2,14},{6,10},... | collective-permute-start | bytes 159752 | tf_op jit(solution)/shard_map/ppermute | solution.py:626
  104.9 2.4 %collective-permute-start.54 = (bf16[208,128]{1,0:T(8,128)(2,1)S(1)}, bf16[208,128]{1,0:T(8,128)(2,1)S(1)}, u32[]{:S(2)}, u32[]{:S(2)}) collective-permute-start(bf16[208,128]{1,0:T(8,128)(2,1)S(1)} %add.9.refs_0_), channel_id=1, source_target_pairs={{0,4},{4,0},{8,12},{12,8},{1,5},{5,1},{9,13},{13,9},{2,6},{6,2},{1... | collective-permute-start | bytes 159752 | tf_op jit(solution)/shard_map/ppermute | solution.py:626
  107.8 1.5 %collective-permute-done.56.refs_3_ = bf16[208,128]{1,0:T(8,128)(2,1)S(1)} collective-permute-done((bf16[208,128]{1,0:T(8,128)(2,1)S(1)}, bf16[208,128]{1,0:T(8,128)(2,1)S(1)}, u32[]{:S(2)}, u32[]{:S(2)}) %collective-permute-start.56) | collective-permute-done | bytes 53280 | tf_op jit(solution)/shard_map/ppermute | solution.py:626
  109.3 1.6 %collective-permute-done.55.refs_2_ = bf16[208,128]{1,0:T(8,128)(2,1)S(1)} collective-permute-done((bf16[208,128]{1,0:T(8,128)(2,1)S(1)}, bf16[208,128]{1,0:T(8,128)(2,1)S(1)}, u32[]{:S(2)}, u32[]{:S(2)}) %collective-permute-start.55) | collective-permute-done | bytes 53280 | tf_op jit(solution)/shard_map/ppermute | solution.py:626
  111.0 1.5 %collective-permute-start.57 = (bf16[208,128]{1,0:T(8,128)(2,1)S(1)}, bf16[208,128]{1,0:T(8,128)(2,1)S(1)}, u32[]{:S(2)}, u32[]{:S(2)}) collective-permute-start(bf16[208,128]{1,0:T(8,128)(2,1)S(1)} %sum.1.refs_0_), channel_id=1, source_target_pairs={{2,0},{3,1},{0,2},{1,3},{6,4},{7,5},{4,6},{5,7},{10,8},{11,9},{8,1... | collective-permute-start | bytes 159752 | tf_op jit(solution)/shard_map/ppermute | solution.py:465
  112.7 2.6 %collective-permute-done.57.refs_1_ = bf16[208,128]{1,0:T(8,128)(2,1)S(1)} collective-permute-done((bf16[208,128]{1,0:T(8,128)(2,1)S(1)}, bf16[208,128]{1,0:T(8,128)(2,1)S(1)}, u32[]{:S(2)}, u32[]{:S(2)}) %collective-permute-start.57) | collective-permute-done | bytes 53280 | tf_op jit(solution)/shard_map/ppermute | solution.py:465
  116.5 10.0 %finish.1 = (bf16[64,2048]{1,0:T(8,128)(2,1)}, f32[64,256]{1,0:T(8,128)}) custom-call(s32[12]{0:T(128)S(4)} %get-tuple-element.99.ints, bf16[208,128]{1,0:T(8,128)(2,1)S(1)} %sum.1.refs_0_, bf16[208,128]{1,0:T(8,128)(2,1)S(1)} %collective-permute-done.57.refs_1_, bf16[208,128]{1,0:T(8,128)(2,1)S(1)} %collective-permute-done.58.refs_2_, ...), custom_call_target="tpu_custom_call" | custom-call | flops 36238786560 | bytes 283115520 | tf_op jit(solution)/shard_map/finish/pallas_call | solution.py:474
  (116 shorter events, 25.5 us)
Async XLA Ops:
  2.3 9.1 %collective-permute-start.1 = (bf16[5,64,128]{2,1,0:T(8,128)(2,1)S(1)}, bf16[5,64,128]{2,1,0:T(8,128)(2,1)S(1)}, u32[]{:S(2)}, u32[]{:S(2)}) collective-permute-start(bf16[5,64,128]{2,1,0:T(8,128)(2,1)S(1)} %get-tuple-element.105), channel_id=1, source_target_pairs={{0,4},{1,13},{2,6},{3,15},{4,8},{5,1},{6,10},{7,3},{8,12},{9,5},{1... | collective-permute-start | bytes 245768 | tf_op jit(solution)/shard_map/ppermute | solution.py:461
  5.4 6.5 %collective-permute-start.2 = (bf16[5,64,128]{2,1,0:T(8,128)(2,1)S(1)}, bf16[5,64,128]{2,1,0:T(8,128)(2,1)S(1)}, u32[]{:S(2)}, u32[]{:S(2)}) collective-permute-start(bf16[5,64,128]{2,1,0:T(8,128)(2,1)S(1)} %get-tuple-element.106), channel_id=1, source_target_pairs={{1,4},{4,1},{3,6},{6,3},{5,8},{8,5},{7,10},{10,7},{9,12},{12,9},{1... | collective-permute-start | bytes 245768 | tf_op jit(solution)/shard_map/ppermute | solution.py:453
  7.0 4.9 %collective-permute-start = (bf16[13,64,128]{2,1,0:T(8,128)(2,1)S(1)}, bf16[13,64,128]{2,1,0:T(8,128)(2,1)S(1)}, u32[]{:S(2)}, u32[]{:S(2)}) collective-permute-start(bf16[13,64,128]{2,1,0:T(8,128)(2,1)S(1)} %get-tuple-element.103), channel_id=1, source_target_pairs={{0,1},{1,0},{2,3},{3,2},{4,5},{5,4},{6,7},{7,6},{8,9},{9,8},{10,11... | collective-permute-start | bytes 638984 | tf_op jit(solution)/shard_map/ppermute | solution.py:444
  13.5 5.8 %collective-permute-start.7 = (bf16[5,64,128]{2,1,0:T(8,128)(2,1)S(1)}, bf16[5,64,128]{2,1,0:T(8,128)(2,1)S(1)}, u32[]{:S(2)}, u32[]{:S(2)}) collective-permute-start(bf16[5,64,128]{2,1,0:T(8,128)(2,1)S(1)} %get-tuple-element.120), channel_id=1, source_target_pairs={{1,4},{4,1},{3,6},{6,3},{5,8},{8,5},{7,10},{10,7},{9,12},{12,9},{1... | collective-permute-start | bytes 245768 | tf_op jit(solution)/shard_map/ppermute | solution.py:453
  15.2 4.1 %collective-permute-start.8 = (bf16[5,64,128]{2,1,0:T(8,128)(2,1)S(1)}, bf16[5,64,128]{2,1,0:T(8,128)(2,1)S(1)}, u32[]{:S(2)}, u32[]{:S(2)}) collective-permute-start(bf16[5,64,128]{2,1,0:T(8,128)(2,1)S(1)} %get-tuple-element.121), channel_id=1, source_target_pairs={{0,1},{1,0},{2,3},{3,2},{4,5},{5,4},{6,7},{7,6},{8,9},{9,8},{10,11... | collective-permute-start | bytes 245768 | tf_op jit(solution)/shard_map/ppermute | solution.py:444
  16.7 5.9 %collective-permute-start.3 = (bf16[5,64,128]{2,1,0:T(8,128)(2,1)S(1)}, bf16[5,64,128]{2,1,0:T(8,128)(2,1)S(1)}, u32[]{:S(2)}, u32[]{:S(2)}) collective-permute-start(bf16[5,64,128]{2,1,0:T(8,128)(2,1)S(1)} %get-tuple-element.113), channel_id=1, source_target_pairs={{1,4},{4,1},{3,6},{6,3},{5,8},{8,5},{7,10},{10,7},{9,12},{12,9},{1... | collective-permute-start | bytes 245768 | tf_op jit(solution)/shard_map/ppermute | solution.py:453
  18.6 4.0 %collective-permute-start.4 = (bf16[5,64,128]{2,1,0:T(8,128)(2,1)S(1)}, bf16[5,64,128]{2,1,0:T(8,128)(2,1)S(1)}, u32[]{:S(2)}, u32[]{:S(2)}) collective-permute-start(bf16[5,64,128]{2,1,0:T(8,128)(2,1)S(1)} %get-tuple-element.114), channel_id=1, source_target_pairs={{0,1},{1,0},{2,3},{3,2},{4,5},{5,4},{6,7},{7,6},{8,9},{9,8},{10,11... | collective-permute-start | bytes 245768 | tf_op jit(solution)/shard_map/ppermute | solution.py:444
  20.2 5.7 %collective-permute-start.9 = (bf16[5,64,128]{2,1,0:T(8,128)(2,1)S(1)}, bf16[5,64,128]{2,1,0:T(8,128)(2,1)S(1)}, u32[]{:S(2)}, u32[]{:S(2)}) collective-permute-start(bf16[5,64,128]{2,1,0:T(8,128)(2,1)S(1)} %get-tuple-element.123), channel_id=1, source_target_pairs={{1,4},{4,1},{3,6},{6,3},{5,8},{8,5},{7,10},{10,7},{9,12},{12,9},{1... | collective-permute-start | bytes 245768 | tf_op jit(solution)/shard_map/ppermute | solution.py:453
  21.8 4.1 %collective-permute-start.10 = (bf16[5,64,128]{2,1,0:T(8,128)(2,1)S(1)}, bf16[5,64,128]{2,1,0:T(8,128)(2,1)S(1)}, u32[]{:S(2)}, u32[]{:S(2)}) collective-permute-start(bf16[5,64,128]{2,1,0:T(8,128)(2,1)S(1)} %get-tuple-element.124), channel_id=1, source_target_pairs={{0,1},{1,0},{2,3},{3,2},{4,5},{5,4},{6,7},{7,6},{8,9},{9,8},{10,11... | collective-permute-start | bytes 245768 | tf_op jit(solution)/shard_map/ppermute | solution.py:444
  23.5 5.8 %collective-permute-start.5 = (bf16[5,64,128]{2,1,0:T(8,128)(2,1)S(1)}, bf16[5,64,128]{2,1,0:T(8,128)(2,1)S(1)}, u32[]{:S(2)}, u32[]{:S(2)}) collective-permute-start(bf16[5,64,128]{2,1,0:T(8,128)(2,1)S(1)} %get-tuple-element.116), channel_id=1, source_target_pairs={{1,4},{4,1},{3,6},{6,3},{5,8},{8,5},{7,10},{10,7},{9,12},{12,9},{1... | collective-permute-start | bytes 245768 | tf_op jit(solution)/shard_map/ppermute | solution.py:453
  25.4 3.9 %collective-permute-start.6 = (bf16[5,64,128]{2,1,0:T(8,128)(2,1)S(1)}, bf16[5,64,128]{2,1,0:T(8,128)(2,1)S(1)}, u32[]{:S(2)}, u32[]{:S(2)}) collective-permute-start(bf16[5,64,128]{2,1,0:T(8,128)(2,1)S(1)} %get-tuple-element.117), channel_id=1, source_target_pairs={{0,1},{1,0},{2,3},{3,2},{4,5},{5,4},{6,7},{7,6},{8,9},{9,8},{10,11... | collective-permute-start | bytes 245768 | tf_op jit(solution)/shard_map/ppermute | solution.py:444
  26.8 5.7 %collective-permute-start.11 = (bf16[5,64,128]{2,1,0:T(8,128)(2,1)S(1)}, bf16[5,64,128]{2,1,0:T(8,128)(2,1)S(1)}, u32[]{:S(2)}, u32[]{:S(2)}) collective-permute-start(bf16[5,64,128]{2,1,0:T(8,128)(2,1)S(1)} %get-tuple-element.126), channel_id=1, source_target_pairs={{1,4},{4,1},{3,6},{6,3},{5,8},{8,5},{7,10},{10,7},{9,12},{12,9},{1... | collective-permute-start | bytes 245768 | tf_op jit(solution)/shard_map/ppermute | solution.py:453
  28.6 3.9 %collective-permute-start.12 = (bf16[5,64,128]{2,1,0:T(8,128)(2,1)S(1)}, bf16[5,64,128]{2,1,0:T(8,128)(2,1)S(1)}, u32[]{:S(2)}, u32[]{:S(2)}) collective-permute-start(bf16[5,64,128]{2,1,0:T(8,128)(2,1)S(1)} %get-tuple-element.127), channel_id=1, source_target_pairs={{0,1},{1,0},{2,3},{3,2},{4,5},{5,4},{6,7},{7,6},{8,9},{9,8},{10,11... | collective-permute-start | bytes 245768 | tf_op jit(solution)/shard_map/ppermute | solution.py:444
  30.1 5.9 %collective-permute-start.13 = (bf16[5,64,128]{2,1,0:T(8,128)(2,1)S(1)}, bf16[5,64,128]{2,1,0:T(8,128)(2,1)S(1)}, u32[]{:S(2)}, u32[]{:S(2)}) collective-permute-start(bf16[5,64,128]{2,1,0:T(8,128)(2,1)S(1)} %get-tuple-element.130), channel_id=1, source_target_pairs={{1,4},{4,1},{3,6},{6,3},{5,8},{8,5},{7,10},{10,7},{9,12},{12,9},{1... | collective-permute-start | bytes 245768 | tf_op jit(solution)/shard_map/ppermute | solution.py:453
  32.1 3.9 %collective-permute-start.14 = (bf16[5,64,128]{2,1,0:T(8,128)(2,1)S(1)}, bf16[5,64,128]{2,1,0:T(8,128)(2,1)S(1)}, u32[]{:S(2)}, u32[]{:S(2)}) collective-permute-start(bf16[5,64,128]{2,1,0:T(8,128)(2,1)S(1)} %get-tuple-element.131), channel_id=1, source_target_pairs={{0,1},{1,0},{2,3},{3,2},{4,5},{5,4},{6,7},{7,6},{8,9},{9,8},{10,11... | collective-permute-start | bytes 245768 | tf_op jit(solution)/shard_map/ppermute | solution.py:444
  34.0 5.7 %collective-permute-start.19 = (bf16[5,64,128]{2,1,0:T(8,128)(2,1)S(1)}, bf16[5,64,128]{2,1,0:T(8,128)(2,1)S(1)}, u32[]{:S(2)}, u32[]{:S(2)}) collective-permute-start(bf16[5,64,128]{2,1,0:T(8,128)(2,1)S(1)} %get-tuple-element.140), channel_id=1, source_target_pairs={{1,4},{4,1},{3,6},{6,3},{5,8},{8,5},{7,10},{10,7},{9,12},{12,9},{1... | collective-permute-start | bytes 245768 | tf_op jit(solution)/shard_map/ppermute | solution.py:453
  37.5 5.7 %collective-permute-start.15 = (bf16[5,64,128]{2,1,0:T(8,128)(2,1)S(1)}, bf16[5,64,128]{2,1,0:T(8,128)(2,1)S(1)}, u32[]{:S(2)}, u32[]{:S(2)}) collective-permute-start(bf16[5,64,128]{2,1,0:T(8,128)(2,1)S(1)} %get-tuple-element.133), channel_id=1, source_target_pairs={{1,4},{4,1},{3,6},{6,3},{5,8},{8,5},{7,10},{10,7},{9,12},{12,9},{1... | collective-permute-start | bytes 245768 | tf_op jit(solution)/shard_map/ppermute | solution.py:453
  39.4 3.9 %collective-permute-start.16 = (bf16[5,64,128]{2,1,0:T(8,128)(2,1)S(1)}, bf16[5,64,128]{2,1,0:T(8,128)(2,1)S(1)}, u32[]{:S(2)}, u32[]{:S(2)}) collective-permute-start(bf16[5,64,128]{2,1,0:T(8,128)(2,1)S(1)} %get-tuple-element.134), channel_id=1, source_target_pairs={{0,1},{1,0},{2,3},{3,2},{4,5},{5,4},{6,7},{7,6},{8,9},{9,8},{10,11... | collective-permute-start | bytes 245768 | tf_op jit(solution)/shard_map/ppermute | solution.py:444
  40.6 5.7 %collective-permute-start.21 = (bf16[5,64,128]{2,1,0:T(8,128)(2,1)S(1)}, bf16[5,64,128]{2,1,0:T(8,128)(2,1)S(1)}, u32[]{:S(2)}, u32[]{:S(2)}) collective-permute-start(bf16[5,64,128]{2,1,0:T(8,128)(2,1)S(1)} %get-tuple-element.143), channel_id=1, source_target_pairs={{1,4},{4,1},{3,6},{6,3},{5,8},{8,5},{7,10},{10,7},{9,12},{12,9},{1... | collective-permute-start | bytes 245768 | tf_op jit(solution)/shard_map/ppermute | solution.py:453
  44.1 5.7 %collective-permute-start.17 = (bf16[5,64,128]{2,1,0:T(8,128)(2,1)S(1)}, bf16[5,64,128]{2,1,0:T(8,128)(2,1)S(1)}, u32[]{:S(2)}, u32[]{:S(2)}) collective-permute-start(bf16[5,64,128]{2,1,0:T(8,128)(2,1)S(1)} %get-tuple-element.136), channel_id=1, source_target_pairs={{1,4},{4,1},{3,6},{6,3},{5,8},{8,5},{7,10},{10,7},{9,12},{12,9},{1... | collective-permute-start | bytes 245768 | tf_op jit(solution)/shard_map/ppermute | solution.py:453
  47.2 5.9 %collective-permute-start.23 = (bf16[5,64,128]{2,1,0:T(8,128)(2,1)S(1)}, bf16[5,64,128]{2,1,0:T(8,128)(2,1)S(1)}, u32[]{:S(2)}, u32[]{:S(2)}) collective-permute-start(bf16[5,64,128]{2,1,0:T(8,128)(2,1)S(1)} %get-tuple-element.146), channel_id=1, source_target_pairs={{1,4},{4,1},{3,6},{6,3},{5,8},{8,5},{7,10},{10,7},{9,12},{12,9},{1... | collective-permute-start | bytes 245768 | tf_op jit(solution)/shard_map/ppermute | solution.py:453
  50.9 5.8 %collective-permute-start.25 = (bf16[5,64,128]{2,1,0:T(8,128)(2,1)S(1)}, bf16[5,64,128]{2,1,0:T(8,128)(2,1)S(1)}, u32[]{:S(2)}, u32[]{:S(2)}) collective-permute-start(bf16[5,64,128]{2,1,0:T(8,128)(2,1)S(1)} %get-tuple-element.150), channel_id=1, source_target_pairs={{1,4},{4,1},{3,6},{6,3},{5,8},{8,5},{7,10},{10,7},{9,12},{12,9},{1... | collective-permute-start | bytes 245768 | tf_op jit(solution)/shard_map/ppermute | solution.py:453
  54.6 5.8 %collective-permute-start.31 = (bf16[5,64,128]{2,1,0:T(8,128)(2,1)S(1)}, bf16[5,64,128]{2,1,0:T(8,128)(2,1)S(1)}, u32[]{:S(2)}, u32[]{:S(2)}) collective-permute-start(bf16[5,64,128]{2,1,0:T(8,128)(2,1)S(1)} %get-tuple-element.160), channel_id=1, source_target_pairs={{1,4},{4,1},{3,6},{6,3},{5,8},{8,5},{7,10},{10,7},{9,12},{12,9},{1... | collective-permute-start | bytes 245768 | tf_op jit(solution)/shard_map/ppermute | solution.py:453
  58.2 5.7 %collective-permute-start.27 = (bf16[5,64,128]{2,1,0:T(8,128)(2,1)S(1)}, bf16[5,64,128]{2,1,0:T(8,128)(2,1)S(1)}, u32[]{:S(2)}, u32[]{:S(2)}) collective-permute-start(bf16[5,64,128]{2,1,0:T(8,128)(2,1)S(1)} %get-tuple-element.153), channel_id=1, source_target_pairs={{1,4},{4,1},{3,6},{6,3},{5,8},{8,5},{7,10},{10,7},{9,12},{12,9},{1... | collective-permute-start | bytes 245768 | tf_op jit(solution)/shard_map/ppermute | solution.py:453
  61.3 5.9 %collective-permute-start.33 = (bf16[5,64,128]{2,1,0:T(8,128)(2,1)S(1)}, bf16[5,64,128]{2,1,0:T(8,128)(2,1)S(1)}, u32[]{:S(2)}, u32[]{:S(2)}) collective-permute-start(bf16[5,64,128]{2,1,0:T(8,128)(2,1)S(1)} %get-tuple-element.163), channel_id=1, source_target_pairs={{1,4},{4,1},{3,6},{6,3},{5,8},{8,5},{7,10},{10,7},{9,12},{12,9},{1... | collective-permute-start | bytes 245768 | tf_op jit(solution)/shard_map/ppermute | solution.py:453
  64.8 5.7 %collective-permute-start.29 = (bf16[5,64,128]{2,1,0:T(8,128)(2,1)S(1)}, bf16[5,64,128]{2,1,0:T(8,128)(2,1)S(1)}, u32[]{:S(2)}, u32[]{:S(2)}) collective-permute-start(bf16[5,64,128]{2,1,0:T(8,128)(2,1)S(1)} %get-tuple-element.156), channel_id=1, source_target_pairs={{1,4},{4,1},{3,6},{6,3},{5,8},{8,5},{7,10},{10,7},{9,12},{12,9},{1... | collective-permute-start | bytes 245768 | tf_op jit(solution)/shard_map/ppermute | solution.py:453
  68.0 5.9 %collective-permute-start.35 = (bf16[5,64,128]{2,1,0:T(8,128)(2,1)S(1)}, bf16[5,64,128]{2,1,0:T(8,128)(2,1)S(1)}, u32[]{:S(2)}, u32[]{:S(2)}) collective-permute-start(bf16[5,64,128]{2,1,0:T(8,128)(2,1)S(1)} %get-tuple-element.166), channel_id=1, source_target_pairs={{1,4},{4,1},{3,6},{6,3},{5,8},{8,5},{7,10},{10,7},{9,12},{12,9},{1... | collective-permute-start | bytes 245768 | tf_op jit(solution)/shard_map/ppermute | solution.py:453
  71.4 6.1 %collective-permute-start.37 = (bf16[5,64,128]{2,1,0:T(8,128)(2,1)S(1)}, bf16[5,64,128]{2,1,0:T(8,128)(2,1)S(1)}, u32[]{:S(2)}, u32[]{:S(2)}) collective-permute-start(bf16[5,64,128]{2,1,0:T(8,128)(2,1)S(1)} %get-tuple-element.170), channel_id=1, source_target_pairs={{1,4},{4,1},{3,6},{6,3},{5,8},{8,5},{7,10},{10,7},{9,12},{12,9},{1... | collective-permute-start | bytes 245768 | tf_op jit(solution)/shard_map/ppermute | solution.py:453
  75.4 5.9 %collective-permute-start.43 = (bf16[5,64,128]{2,1,0:T(8,128)(2,1)S(1)}, bf16[5,64,128]{2,1,0:T(8,128)(2,1)S(1)}, u32[]{:S(2)}, u32[]{:S(2)}) collective-permute-start(bf16[5,64,128]{2,1,0:T(8,128)(2,1)S(1)} %get-tuple-element.180), channel_id=1, source_target_pairs={{1,4},{4,1},{3,6},{6,3},{5,8},{8,5},{7,10},{10,7},{9,12},{12,9},{1... | collective-permute-start | bytes 245768 | tf_op jit(solution)/shard_map/ppermute | solution.py:453
  79.0 5.7 %collective-permute-start.39 = (bf16[5,64,128]{2,1,0:T(8,128)(2,1)S(1)}, bf16[5,64,128]{2,1,0:T(8,128)(2,1)S(1)}, u32[]{:S(2)}, u32[]{:S(2)}) collective-permute-start(bf16[5,64,128]{2,1,0:T(8,128)(2,1)S(1)} %get-tuple-element.173), channel_id=1, source_target_pairs={{1,4},{4,1},{3,6},{6,3},{5,8},{8,5},{7,10},{10,7},{9,12},{12,9},{1... | collective-permute-start | bytes 245768 | tf_op jit(solution)/shard_map/ppermute | solution.py:453
  82.2 5.9 %collective-permute-start.45 = (bf16[5,64,128]{2,1,0:T(8,128)(2,1)S(1)}, bf16[5,64,128]{2,1,0:T(8,128)(2,1)S(1)}, u32[]{:S(2)}, u32[]{:S(2)}) collective-permute-start(bf16[5,64,128]{2,1,0:T(8,128)(2,1)S(1)} %get-tuple-element.183), channel_id=1, source_target_pairs={{1,4},{4,1},{3,6},{6,3},{5,8},{8,5},{7,10},{10,7},{9,12},{12,9},{1... | collective-permute-start | bytes 245768 | tf_op jit(solution)/shard_map/ppermute | solution.py:453
  84.2 3.9 %collective-permute-start.46 = (bf16[5,64,128]{2,1,0:T(8,128)(2,1)S(1)}, bf16[5,64,128]{2,1,0:T(8,128)(2,1)S(1)}, u32[]{:S(2)}, u32[]{:S(2)}) collective-permute-start(bf16[5,64,128]{2,1,0:T(8,128)(2,1)S(1)} %get-tuple-element.184), channel_id=1, source_target_pairs={{0,1},{1,0},{2,3},{3,2},{4,5},{5,4},{6,7},{7,6},{8,9},{9,8},{10,11... | collective-permute-start | bytes 245768 | tf_op jit(solution)/shard_map/ppermute | solution.py:444
  85.6 7.0 %collective-permute-start.41 = (bf16[5,64,128]{2,1,0:T(8,128)(2,1)S(1)}, bf16[5,64,128]{2,1,0:T(8,128)(2,1)S(1)}, u32[]{:S(2)}, u32[]{:S(2)}) collective-permute-start(bf16[5,64,128]{2,1,0:T(8,128)(2,1)S(1)} %get-tuple-element.176), channel_id=1, source_target_pairs={{1,4},{4,1},{3,6},{6,3},{5,8},{8,5},{7,10},{10,7},{9,12},{12,9},{1... | collective-permute-start | bytes 245768 | tf_op jit(solution)/shard_map/ppermute | solution.py:453
  88.1 4.5 %collective-permute-start.42 = (bf16[5,64,128]{2,1,0:T(8,128)(2,1)S(1)}, bf16[5,64,128]{2,1,0:T(8,128)(2,1)S(1)}, u32[]{:S(2)}, u32[]{:S(2)}) collective-permute-start(bf16[5,64,128]{2,1,0:T(8,128)(2,1)S(1)} %get-tuple-element.177), channel_id=1, source_target_pairs={{0,1},{1,0},{2,3},{3,2},{4,5},{5,4},{6,7},{7,6},{8,9},{9,8},{10,11... | collective-permute-start | bytes 245768 | tf_op jit(solution)/shard_map/ppermute | solution.py:444
  89.1 5.8 %collective-permute-start.47 = (bf16[5,64,128]{2,1,0:T(8,128)(2,1)S(1)}, bf16[5,64,128]{2,1,0:T(8,128)(2,1)S(1)}, u32[]{:S(2)}, u32[]{:S(2)}) collective-permute-start(bf16[5,64,128]{2,1,0:T(8,128)(2,1)S(1)} %get-tuple-element.186), channel_id=1, source_target_pairs={{1,4},{4,1},{3,6},{6,3},{5,8},{8,5},{7,10},{10,7},{9,12},{12,9},{1... | collective-permute-start | bytes 245768 | tf_op jit(solution)/shard_map/ppermute | solution.py:453
  91.1 5.3 %collective-permute-start.48 = (bf16[5,64,128]{2,1,0:T(8,128)(2,1)S(1)}, bf16[5,64,128]{2,1,0:T(8,128)(2,1)S(1)}, u32[]{:S(2)}, u32[]{:S(2)}) collective-permute-start(bf16[5,64,128]{2,1,0:T(8,128)(2,1)S(1)} %get-tuple-element.187), channel_id=1, source_target_pairs={{0,1},{1,0},{2,3},{3,2},{4,5},{5,4},{6,7},{7,6},{8,9},{9,8},{10,11... | collective-permute-start | bytes 245768 | tf_op jit(solution)/shard_map/ppermute | solution.py:444
  91.1 5.9 %collective-permute-start.49 = (bf16[8,64,128]{2,1,0:T(8,128)(2,1)S(1)}, bf16[8,64,128]{2,1,0:T(8,128)(2,1)S(1)}, u32[]{:S(2)}, u32[]{:S(2)}) collective-permute-start(bf16[8,64,128]{2,1,0:T(8,128)(2,1)S(1)} %get-tuple-element.185.own.refs_2_.refs_4_), channel_id=1, source_target_pairs={{2,0},{3,1},{0,2},{1,3},{6,4},{7,5},{4,6},{5,7},{10,8},{11,9},{8,1... | collective-permute-start | bytes 393224 | tf_op jit(solution)/shard_map/ppermute | solution.py:465
  93.4 5.7 %collective-permute-start.50 = (bf16[5,64,128]{2,1,0:T(8,128)(2,1)S(1)}, bf16[5,64,128]{2,1,0:T(8,128)(2,1)S(1)}, u32[]{:S(2)}, u32[]{:S(2)}) collective-permute-start(bf16[5,64,128]{2,1,0:T(8,128)(2,1)S(1)} %get-tuple-element.190), channel_id=1, source_target_pairs={{1,4},{4,1},{3,6},{6,3},{5,8},{8,5},{7,10},{10,7},{9,12},{12,9},{1... | collective-permute-start | bytes 245768 | tf_op jit(solution)/shard_map/ppermute | solution.py:453
  95.0 4.2 %collective-permute-start.51 = (bf16[5,64,128]{2,1,0:T(8,128)(2,1)S(1)}, bf16[5,64,128]{2,1,0:T(8,128)(2,1)S(1)}, u32[]{:S(2)}, u32[]{:S(2)}) collective-permute-start(bf16[5,64,128]{2,1,0:T(8,128)(2,1)S(1)} %get-tuple-element.191), channel_id=1, source_target_pairs={{0,1},{1,0},{2,3},{3,2},{4,5},{5,4},{6,7},{7,6},{8,9},{9,8},{10,11... | collective-permute-start | bytes 245768 | tf_op jit(solution)/shard_map/ppermute | solution.py:444
  95.0 5.9 %collective-permute-start.52 = (bf16[8,64,128]{2,1,0:T(8,128)(2,1)S(1)}, bf16[8,64,128]{2,1,0:T(8,128)(2,1)S(1)}, u32[]{:S(2)}, u32[]{:S(2)}) collective-permute-start(bf16[8,64,128]{2,1,0:T(8,128)(2,1)S(1)} %get-tuple-element.189.own.refs_3_.refs_5_), channel_id=1, source_target_pairs={{2,0},{3,1},{0,2},{1,3},{6,4},{7,5},{4,6},{5,7},{10,8},{11,9},{8,1... | collective-permute-start | bytes 393224 | tf_op jit(solution)/shard_map/ppermute | solution.py:465
  102.8 6.4 %collective-permute-start.56 = (bf16[208,128]{1,0:T(8,128)(2,1)S(1)}, bf16[208,128]{1,0:T(8,128)(2,1)S(1)}, u32[]{:S(2)}, u32[]{:S(2)}) collective-permute-start(bf16[208,128]{1,0:T(8,128)(2,1)S(1)} %add.9.refs_0_), channel_id=1, source_target_pairs={{0,12},{4,8},{8,4},{12,0},{1,13},{5,9},{9,5},{13,1},{2,14},{6,10},... | collective-permute-start | bytes 159752 | tf_op jit(solution)/shard_map/ppermute | solution.py:626
  104.9 6.0 %collective-permute-start.55 = (bf16[208,128]{1,0:T(8,128)(2,1)S(1)}, bf16[208,128]{1,0:T(8,128)(2,1)S(1)}, u32[]{:S(2)}, u32[]{:S(2)}) collective-permute-start(bf16[208,128]{1,0:T(8,128)(2,1)S(1)} %add.9.refs_0_), channel_id=1, source_target_pairs={{0,8},{4,12},{8,0},{12,4},{1,9},{5,13},{9,1},{13,5},{2,10},{6,14},... | collective-permute-start | bytes 159752 | tf_op jit(solution)/shard_map/ppermute | solution.py:626
  104.9 6.0 %collective-permute-start.54 = (bf16[208,128]{1,0:T(8,128)(2,1)S(1)}, bf16[208,128]{1,0:T(8,128)(2,1)S(1)}, u32[]{:S(2)}, u32[]{:S(2)}) collective-permute-start(bf16[208,128]{1,0:T(8,128)(2,1)S(1)} %add.9.refs_0_), channel_id=1, source_target_pairs={{0,4},{4,0},{8,12},{12,8},{1,5},{5,1},{9,13},{13,9},{2,6},{6,2},{1... | collective-permute-start | bytes 159752 | tf_op jit(solution)/shard_map/ppermute | solution.py:626
  107.3 5.2 %collective-permute-start.60 = (bf16[8,64,128]{2,1,0:T(8,128)(2,1)S(1)}, bf16[8,64,128]{2,1,0:T(8,128)(2,1)S(1)}, u32[]{:S(2)}, u32[]{:S(2)}) collective-permute-start(bf16[8,64,128]{2,1,0:T(8,128)(2,1)S(1)} %get-tuple-element.185.own.refs_2_.refs_4_), channel_id=1, source_target_pairs={{0,1},{1,0},{2,3},{3,2},{4,5},{5,4},{6,7},{7,6},{8,9},{9,8},{10,11... | collective-permute-start | bytes 393224 | tf_op jit(solution)/shard_map/ppermute | solution.py:444
  107.3 8.0 %collective-permute-start.61 = (bf16[8,64,128]{2,1,0:T(8,128)(2,1)S(1)}, bf16[8,64,128]{2,1,0:T(8,128)(2,1)S(1)}, u32[]{:S(2)}, u32[]{:S(2)}) collective-permute-start(bf16[8,64,128]{2,1,0:T(8,128)(2,1)S(1)} %get-tuple-element.189.own.refs_3_.refs_5_), channel_id=1, source_target_pairs={{0,1},{1,0},{2,3},{3,2},{4,5},{5,4},{6,7},{7,6},{8,9},{9,8},{10,11... | collective-permute-start | bytes 393224 | tf_op jit(solution)/shard_map/ppermute | solution.py:444
  109.3 6.0 %collective-permute-start.62 = (bf16[8,64,128]{2,1,0:T(8,128)(2,1)S(1)}, bf16[8,64,128]{2,1,0:T(8,128)(2,1)S(1)}, u32[]{:S(2)}, u32[]{:S(2)}) collective-permute-start(bf16[8,64,128]{2,1,0:T(8,128)(2,1)S(1)} %collective-permute-done.49.y_other.refs_4_.refs_6_), channel_id=1, source_target_pairs={{0,1},{1,0},{2,3},{3,2},{4,5},{5,4},{6,7},{7,6},{8,9},{9,8},{10,11... | collective-permute-start | bytes 393224 | tf_op jit(solution)/shard_map/ppermute | solution.py:444
  110.9 4.4 %collective-permute-start.63 = (bf16[8,64,128]{2,1,0:T(8,128)(2,1)S(1)}, bf16[8,64,128]{2,1,0:T(8,128)(2,1)S(1)}, u32[]{:S(2)}, u32[]{:S(2)}) collective-permute-start(bf16[8,64,128]{2,1,0:T(8,128)(2,1)S(1)} %collective-permute-done.52.refs_5_.refs_7_), channel_id=1, source_target_pairs={{0,1},{1,0},{2,3},{3,2},{4,5},{5,4},{6,7},{7,6},{8,9},{9,8},{10,11... | collective-permute-start | bytes 393224 | tf_op jit(solution)/shard_map/ppermute | solution.py:444
  111.0 4.3 %collective-permute-start.57 = (bf16[208,128]{1,0:T(8,128)(2,1)S(1)}, bf16[208,128]{1,0:T(8,128)(2,1)S(1)}, u32[]{:S(2)}, u32[]{:S(2)}) collective-permute-start(bf16[208,128]{1,0:T(8,128)(2,1)S(1)} %sum.1.refs_0_), channel_id=1, source_target_pairs={{2,0},{3,1},{0,2},{1,3},{6,4},{7,5},{4,6},{5,7},{10,8},{11,9},{8,1... | collective-permute-start | bytes 159752 | tf_op jit(solution)/shard_map/ppermute | solution.py:465
  (16 other events, 52.9 us)

commit v8 on v7

--- a/solution.py
+++ b/solution.py
@@ -300,7 +300,7 @@
         return jnp.broadcast_to(value[k % SUBLANES : k % SUBLANES + 1], (SUBLANES, 128))
 
     pivots = [jnp.ones((SUBLANES, 128), F32) for _ in range(count)]
-    for start, group in ((0, 8), (8, 8), (16, 16)):
+    for start, group in ((0, 16), (16, 16)):
         columns = {
             k: {
                 v: jnp.broadcast_to(pieces[v][:, k : k + 1], (SUBLANES, 128))
@@ -368,6 +368,30 @@
             work[after:, :] = jnp.where((columns >= start) & (columns < after), 0.0, old) - change
 
 
+def six_terms(left, right):
+    (high, middle, low), (other, little, least) = split3(left), split3(right)
+    return jnp.dot(
+        jnp.concatenate([high, high, middle, middle, high, low], axis=1),
+        jnp.concatenate([other, little, other, little, least, other], axis=0),
+        preferred_element_type=F32,
+    )
+
+
+def factor_halves(gram, work, inverse):
+    half = gram.shape[0] // 2
+    first, last = slice(0, half), slice(half, 2 * half)
+    work[0] = gram[first, first]
+    factor(work.at[0], inverse.at[first, first])
+    beside = six_terms(inverse[first, first], gram[first, last])
+    turned = beside.T
+    work[1] = gram[last, last] - six_terms(turned, beside)
+    factor(work.at[1], inverse.at[last, last])
+    inverse[last, first] = -six_terms(
+        inverse[last, last], six_terms(turned, inverse[first, first])
+    )
+    inverse[first, last] = jnp.zeros((half, half), F32)
+
+
 def finish_kernel(chips, scale, ints, *refs):
     mine, theirs = refs[:chips], refs[chips : 2 * chips]
     y_mine = refs[2 * chips : (2 + CORES) * chips]
@@ -392,8 +416,7 @@
                     other = payload[at : at + vecs, :].astype(F32)
                     block = jnp.where(lax.rem(which + away, chips) == k, other, block)
                 pair[matrix, rows, k * vecs : (k + 1) * vecs] = block
-    work[...] = (pair[0] + pair[0].T) * scale
-    factor(work, inverse)
+    factor_halves((pair[0] + pair[0].T) * scale, work, inverse)
     start = pl.multiple_of(col * local_vecs, local_vecs)
     own_rows = inverse[pl.ds(start, local_vecs), :]
     gram_h = (pair[1] + pair[1].T) * scale
@@ -660,7 +683,7 @@
         ),
         [
             pltpu.VMEM((2, size, size), F32),
-            pltpu.VMEM((size, size), F32),
+            pltpu.VMEM((2, size // 2, size // 2), F32),
             pltpu.VMEM((size, size), F32),
         ],
         10 * row_flops,

time: 127 us -> 127 us (level)
  transfers between devices with their start and end apart: 64 -> 64, of which waited for: 21 -> 20; matrix products, arithmetic and copies ran while one was open for 0% -> 0% of each run, Pallas kernels for 24% -> 24%
where the time goes in v8:
time: 127 us; the launch traced here: 126 us
  starting transfers between devices  63.1 us (50%)
  Pallas kernels  44.3 us (35%)
  waiting for transfers between devices  16.5 us (13%)
  between operations  2.32 us (2%)
    ppermute x25, starting transfers between devices, swap_chips(): return lax.ppermute(value, ('row', 'col'), pairs)  50.2 us
    pallas_call x30, Pallas kernels, call(): pl.pallas_call(kernel, name=name, out_shape=outs, in_specs=[SMEM] * len(s...  39.7 us
    ppermute x25, waiting for transfers between devices, swap_chips(): return lax.ppermute(value, ('row', 'col'), pairs)  7.56 us
    ppermute x3, starting transfers between devices, local(): lax.ppermute(summed, 'row', [(r, r ^ step) for r in range(num_rows)])  4.45 us
    ppermute x3, starting transfers between devices, from_chip(): return lax.ppermute(value, 'col', pairs)  4.45 us
    ppermute x3, waiting for transfers between devices, from_chip(): return lax.ppermute(value, 'col', pairs)  3.38 us
    ppermute x1, starting transfers between devices, next_chips(): return lax.ppermute(value, ('row', 'col'), pairs)  3.08 us
    ppermute x3, waiting for transfers between devices, local(): lax.ppermute(summed, 'row', [(r, r ^ step) for r in range(num_rows)])  3.07 us
  transfers between devices with their start and end apart: 64, of which 20 were waited for; matrix products, arithmetic and copies ran while one was open for 0% of the time, Pallas kernels for 24%

profile of v8, /device:TPU:0, one launch (start us, length us, event | category | flops | bytes accessed | tf_op | source)
XLA Modules:
  0.0 126.4 jit_solution(3791303372283950729)
XLA Ops:
  0.7 1.6 %cut.1 = (bf16[8,64,128]{2,1,0:T(8,128)(2,1)S(1)}, bf16[5,64,128]{2,1,0:T(8,128)(2,1)S(1)}, bf16[13,64,128]{2,1,0:T(8,128)(2,1)S(1)}, bf16[5,64,128]{2,1,0:T(8,128)(2,1)S(1)}, bf16[5,64,128]{2,1,0:T(8,128)(2,1)S(1)}) custom-call(s32[5]{0:T(128)S(1)} %stack.23.ints, s32[16]{0:T(128)} %sizes.3, bf16[64,2048]{1,0:T(8,128)(2,1)} %trial.1), custom_call_target="tpu_custom_call" | custom-call | tf_op jit(solution)/shard_map/cut/pallas_call | solution.py:526
  2.3 3.1 %collective-permute-start.1 = (bf16[5,64,128]{2,1,0:T(8,128)(2,1)S(1)}, bf16[5,64,128]{2,1,0:T(8,128)(2,1)S(1)}, u32[]{:S(2)}, u32[]{:S(2)}) collective-permute-start(bf16[5,64,128]{2,1,0:T(8,128)(2,1)S(1)} %get-tuple-element.105), channel_id=1, source_target_pairs={{0,4},{1,13},{2,6},{3,15},{4,8},{5,1},{6,10},{7,3},{8,12},{9,5},{1... | collective-permute-start | bytes 245768 | tf_op jit(solution)/shard_map/ppermute | solution.py:484
  5.4 1.6 %collective-permute-start.2 = (bf16[5,64,128]{2,1,0:T(8,128)(2,1)S(1)}, bf16[5,64,128]{2,1,0:T(8,128)(2,1)S(1)}, u32[]{:S(2)}, u32[]{:S(2)}) collective-permute-start(bf16[5,64,128]{2,1,0:T(8,128)(2,1)S(1)} %get-tuple-element.106), channel_id=1, source_target_pairs={{1,4},{4,1},{3,6},{6,3},{5,8},{8,5},{7,10},{10,7},{9,12},{12,9},{1... | collective-permute-start | bytes 245768 | tf_op jit(solution)/shard_map/ppermute | solution.py:476
  8.4 3.0 %load.1 = (bf16[8,9,128,128]{3,2,1,0:T(8,128)(2,1)S(1)}, bf16[8,9,128,128]{3,2,1,0:T(8,128)(2,1)S(1)}, s32[8,9]{1,0:T(8,128)S(4)}, f32[8,9]{1,0:T(8,128)S(4)}, s32[12]{0:T(128)S(4)}, /*index=5*/f32[2]{0:T(128)S(4)}) custom-call(s32[5]{0:T(128)S(1)} %stack.23.ints, f32[1]{0:T(128)S(6)} %copy.10.shift, f32[1]{0:T(128)S(6)} %copy.11.width, s32[16,9]{1,0:T(8,128)} %columns.1, ...), custom_call_target="tpu_custom_call" | custom-call | bytes 9437184 | tf_op jit(solution)/shard_map/load/pallas_call | solution.py:543
  12.0 1.5 %scaled.8 = (bf16[8,64,128]{2,1,0:T(8,128)(2,1)S(1)}, bf16[5,64,128]{2,1,0:T(8,128)(2,1)S(1)}, bf16[5,64,128]{2,1,0:T(8,128)(2,1)S(1)}) custom-call(s32[12]{0:T(128)S(4)} %get-tuple-element.99.ints, s32[8,9]{1,0:T(8,128)S(4)} %get-tuple-element.100.index, f32[8,9]{1,0:T(8,128)S(4)} %get-tuple-element.101.signs, f32[2]{0:T(128)S(4)} %get-tuple-element.102.scal, ...), custom_call_target="tpu_custom_call" | custom-call | flops 7247757312 | bytes 56623104 | tf_op jit(solution)/shard_map/scaled/pallas_call | solution.py:497
  13.5 1.7 %collective-permute-start.7 = (bf16[5,64,128]{2,1,0:T(8,128)(2,1)S(1)}, bf16[5,64,128]{2,1,0:T(8,128)(2,1)S(1)}, u32[]{:S(2)}, u32[]{:S(2)}) collective-permute-start(bf16[5,64,128]{2,1,0:T(8,128)(2,1)S(1)} %get-tuple-element.120), channel_id=1, source_target_pairs={{1,4},{4,1},{3,6},{6,3},{5,8},{8,5},{7,10},{10,7},{9,12},{12,9},{1... | collective-permute-start | bytes 245768 | tf_op jit(solution)/shard_map/ppermute | solution.py:476
  15.2 1.5 %scaled.9 = (bf16[8,64,128]{2,1,0:T(8,128)(2,1)S(1)}, bf16[5,64,128]{2,1,0:T(8,128)(2,1)S(1)}, bf16[5,64,128]{2,1,0:T(8,128)(2,1)S(1)}) custom-call(s32[12]{0:T(128)S(4)} %get-tuple-element.99.ints, s32[8,9]{1,0:T(8,128)S(4)} %get-tuple-element.100.index, f32[8,9]{1,0:T(8,128)S(4)} %get-tuple-element.101.signs, f32[2]{0:T(128)S(4)} %get-tuple-element.102.scal, ...), custom_call_target="tpu_custom_call" | custom-call | flops 7247757312 | bytes 56623104 | tf_op jit(solution)/shard_map/scaled/pallas_call | solution.py:497
  16.7 1.9 %collective-permute-start.3 = (bf16[5,64,128]{2,1,0:T(8,128)(2,1)S(1)}, bf16[5,64,128]{2,1,0:T(8,128)(2,1)S(1)}, u32[]{:S(2)}, u32[]{:S(2)}) collective-permute-start(bf16[5,64,128]{2,1,0:T(8,128)(2,1)S(1)} %get-tuple-element.113), channel_id=1, source_target_pairs={{1,4},{4,1},{3,6},{6,3},{5,8},{8,5},{7,10},{10,7},{9,12},{12,9},{1... | collective-permute-start | bytes 245768 | tf_op jit(solution)/shard_map/ppermute | solution.py:476
  20.2 1.6 %collective-permute-start.9 = (bf16[5,64,128]{2,1,0:T(8,128)(2,1)S(1)}, bf16[5,64,128]{2,1,0:T(8,128)(2,1)S(1)}, u32[]{:S(2)}, u32[]{:S(2)}) collective-permute-start(bf16[5,64,128]{2,1,0:T(8,128)(2,1)S(1)} %get-tuple-element.123), channel_id=1, source_target_pairs={{1,4},{4,1},{3,6},{6,3},{5,8},{8,5},{7,10},{10,7},{9,12},{12,9},{1... | collective-permute-start | bytes 245768 | tf_op jit(solution)/shard_map/ppermute | solution.py:476
  23.5 1.9 %collective-permute-start.5 = (bf16[5,64,128]{2,1,0:T(8,128)(2,1)S(1)}, bf16[5,64,128]{2,1,0:T(8,128)(2,1)S(1)}, u32[]{:S(2)}, u32[]{:S(2)}) collective-permute-start(bf16[5,64,128]{2,1,0:T(8,128)(2,1)S(1)} %get-tuple-element.116), channel_id=1, source_target_pairs={{1,4},{4,1},{3,6},{6,3},{5,8},{8,5},{7,10},{10,7},{9,12},{12,9},{1... | collective-permute-start | bytes 245768 | tf_op jit(solution)/shard_map/ppermute | solution.py:476
  26.8 1.8 %collective-permute-start.11 = (bf16[5,64,128]{2,1,0:T(8,128)(2,1)S(1)}, bf16[5,64,128]{2,1,0:T(8,128)(2,1)S(1)}, u32[]{:S(2)}, u32[]{:S(2)}) collective-permute-start(bf16[5,64,128]{2,1,0:T(8,128)(2,1)S(1)} %get-tuple-element.126), channel_id=1, source_target_pairs={{1,4},{4,1},{3,6},{6,3},{5,8},{8,5},{7,10},{10,7},{9,12},{12,9},{1... | collective-permute-start | bytes 245768 | tf_op jit(solution)/shard_map/ppermute | solution.py:476
  30.1 2.0 %collective-permute-start.13 = (bf16[5,64,128]{2,1,0:T(8,128)(2,1)S(1)}, bf16[5,64,128]{2,1,0:T(8,128)(2,1)S(1)}, u32[]{:S(2)}, u32[]{:S(2)}) collective-permute-start(bf16[5,64,128]{2,1,0:T(8,128)(2,1)S(1)} %get-tuple-element.130), channel_id=1, source_target_pairs={{1,4},{4,1},{3,6},{6,3},{5,8},{8,5},{7,10},{10,7},{9,12},{12,9},{1... | collective-permute-start | bytes 245768 | tf_op jit(solution)/shard_map/ppermute | solution.py:476
  32.5 1.5 %scaled.10 = (bf16[8,64,128]{2,1,0:T(8,128)(2,1)S(1)}, bf16[5,64,128]{2,1,0:T(8,128)(2,1)S(1)}, bf16[5,64,128]{2,1,0:T(8,128)(2,1)S(1)}) custom-call(s32[12]{0:T(128)S(4)} %get-tuple-element.99.ints, s32[8,9]{1,0:T(8,128)S(4)} %get-tuple-element.100.index, f32[8,9]{1,0:T(8,128)S(4)} %get-tuple-element.101.signs, f32[2]{0:T(128)S(4)} %get-tuple-element.102.scal, ...), custom_call_target="tpu_custom_call" | custom-call | flops 7247757312 | bytes 56623104 | tf_op jit(solution)/shard_map/scaled/pallas_call | solution.py:497
  34.0 2.0 %collective-permute-start.19 = (bf16[5,64,128]{2,1,0:T(8,128)(2,1)S(1)}, bf16[5,64,128]{2,1,0:T(8,128)(2,1)S(1)}, u32[]{:S(2)}, u32[]{:S(2)}) collective-permute-start(bf16[5,64,128]{2,1,0:T(8,128)(2,1)S(1)} %get-tuple-element.140), channel_id=1, source_target_pairs={{1,4},{4,1},{3,6},{6,3},{5,8},{8,5},{7,10},{10,7},{9,12},{12,9},{1... | collective-permute-start | bytes 245768 | tf_op jit(solution)/shard_map/ppermute | solution.py:476
  36.0 1.5 %scaled.11 = (bf16[8,64,128]{2,1,0:T(8,128)(2,1)S(1)}, bf16[5,64,128]{2,1,0:T(8,128)(2,1)S(1)}, bf16[5,64,128]{2,1,0:T(8,128)(2,1)S(1)}) custom-call(s32[12]{0:T(128)S(4)} %get-tuple-element.99.ints, s32[8,9]{1,0:T(8,128)S(4)} %get-tuple-element.100.index, f32[8,9]{1,0:T(8,128)S(4)} %get-tuple-element.101.signs, f32[2]{0:T(128)S(4)} %get-tuple-element.102.scal, ...), custom_call_target="tpu_custom_call" | custom-call | flops 7247757312 | bytes 56623104 | tf_op jit(solution)/shard_map/scaled/pallas_call | solution.py:497
  37.5 1.9 %collective-permute-start.15 = (bf16[5,64,128]{2,1,0:T(8,128)(2,1)S(1)}, bf16[5,64,128]{2,1,0:T(8,128)(2,1)S(1)}, u32[]{:S(2)}, u32[]{:S(2)}) collective-permute-start(bf16[5,64,128]{2,1,0:T(8,128)(2,1)S(1)} %get-tuple-element.133), channel_id=1, source_target_pairs={{1,4},{4,1},{3,6},{6,3},{5,8},{8,5},{7,10},{10,7},{9,12},{12,9},{1... | collective-permute-start | bytes 245768 | tf_op jit(solution)/shard_map/ppermute | solution.py:476
  40.6 2.0 %collective-permute-start.21 = (bf16[5,64,128]{2,1,0:T(8,128)(2,1)S(1)}, bf16[5,64,128]{2,1,0:T(8,128)(2,1)S(1)}, u32[]{:S(2)}, u32[]{:S(2)}) collective-permute-start(bf16[5,64,128]{2,1,0:T(8,128)(2,1)S(1)} %get-tuple-element.143), channel_id=1, source_target_pairs={{1,4},{4,1},{3,6},{6,3},{5,8},{8,5},{7,10},{10,7},{9,12},{12,9},{1... | collective-permute-start | bytes 245768 | tf_op jit(solution)/shard_map/ppermute | solution.py:476
  44.1 2.0 %collective-permute-start.17 = (bf16[5,64,128]{2,1,0:T(8,128)(2,1)S(1)}, bf16[5,64,128]{2,1,0:T(8,128)(2,1)S(1)}, u32[]{:S(2)}, u32[]{:S(2)}) collective-permute-start(bf16[5,64,128]{2,1,0:T(8,128)(2,1)S(1)} %get-tuple-element.136), channel_id=1, source_target_pairs={{1,4},{4,1},{3,6},{6,3},{5,8},{8,5},{7,10},{10,7},{9,12},{12,9},{1... | collective-permute-start | bytes 245768 | tf_op jit(solution)/shard_map/ppermute | solution.py:476
  47.2 2.2 %collective-permute-start.23 = (bf16[5,64,128]{2,1,0:T(8,128)(2,1)S(1)}, bf16[5,64,128]{2,1,0:T(8,128)(2,1)S(1)}, u32[]{:S(2)}, u32[]{:S(2)}) collective-permute-start(bf16[5,64,128]{2,1,0:T(8,128)(2,1)S(1)} %get-tuple-element.146), channel_id=1, source_target_pairs={{1,4},{4,1},{3,6},{6,3},{5,8},{8,5},{7,10},{10,7},{9,12},{12,9},{1... | collective-permute-start | bytes 245768 | tf_op jit(solution)/shard_map/ppermute | solution.py:476
  50.9 2.2 %collective-permute-start.25 = (bf16[5,64,128]{2,1,0:T(8,128)(2,1)S(1)}, bf16[5,64,128]{2,1,0:T(8,128)(2,1)S(1)}, u32[]{:S(2)}, u32[]{:S(2)}) collective-permute-start(bf16[5,64,128]{2,1,0:T(8,128)(2,1)S(1)} %get-tuple-element.150), channel_id=1, source_target_pairs={{1,4},{4,1},{3,6},{6,3},{5,8},{8,5},{7,10},{10,7},{9,12},{12,9},{1... | collective-permute-start | bytes 245768 | tf_op jit(solution)/shard_map/ppermute | solution.py:476
  53.1 1.5 %scaled.12 = (bf16[8,64,128]{2,1,0:T(8,128)(2,1)S(1)}, bf16[5,64,128]{2,1,0:T(8,128)(2,1)S(1)}, bf16[5,64,128]{2,1,0:T(8,128)(2,1)S(1)}) custom-call(s32[12]{0:T(128)S(4)} %get-tuple-element.99.ints, s32[8,9]{1,0:T(8,128)S(4)} %get-tuple-element.100.index, f32[8,9]{1,0:T(8,128)S(4)} %get-tuple-element.101.signs, f32[2]{0:T(128)S(4)} %get-tuple-element.102.scal, ...), custom_call_target="tpu_custom_call" | custom-call | flops 7247757312 | bytes 56623104 | tf_op jit(solution)/shard_map/scaled/pallas_call | solution.py:497
  54.6 2.1 %collective-permute-start.31 = (bf16[5,64,128]{2,1,0:T(8,128)(2,1)S(1)}, bf16[5,64,128]{2,1,0:T(8,128)(2,1)S(1)}, u32[]{:S(2)}, u32[]{:S(2)}) collective-permute-start(bf16[5,64,128]{2,1,0:T(8,128)(2,1)S(1)} %get-tuple-element.160), channel_id=1, source_target_pairs={{1,4},{4,1},{3,6},{6,3},{5,8},{8,5},{7,10},{10,7},{9,12},{12,9},{1... | collective-permute-start | bytes 245768 | tf_op jit(solution)/shard_map/ppermute | solution.py:476
  56.7 1.5 %scaled.13 = (bf16[8,64,128]{2,1,0:T(8,128)(2,1)S(1)}, bf16[5,64,128]{2,1,0:T(8,128)(2,1)S(1)}, bf16[5,64,128]{2,1,0:T(8,128)(2,1)S(1)}) custom-call(s32[12]{0:T(128)S(4)} %get-tuple-element.99.ints, s32[8,9]{1,0:T(8,128)S(4)} %get-tuple-element.100.index, f32[8,9]{1,0:T(8,128)S(4)} %get-tuple-element.101.signs, f32[2]{0:T(128)S(4)} %get-tuple-element.102.scal, ...), custom_call_target="tpu_custom_call" | custom-call | flops 7247757312 | bytes 56623104 | tf_op jit(solution)/shard_map/scaled/pallas_call | solution.py:497
  58.2 2.2 %collective-permute-start.27 = (bf16[5,64,128]{2,1,0:T(8,128)(2,1)S(1)}, bf16[5,64,128]{2,1,0:T(8,128)(2,1)S(1)}, u32[]{:S(2)}, u32[]{:S(2)}) collective-permute-start(bf16[5,64,128]{2,1,0:T(8,128)(2,1)S(1)} %get-tuple-element.153), channel_id=1, source_target_pairs={{1,4},{4,1},{3,6},{6,3},{5,8},{8,5},{7,10},{10,7},{9,12},{12,9},{1... | collective-permute-start | bytes 245768 | tf_op jit(solution)/shard_map/ppermute | solution.py:476
  61.3 2.1 %collective-permute-start.33 = (bf16[5,64,128]{2,1,0:T(8,128)(2,1)S(1)}, bf16[5,64,128]{2,1,0:T(8,128)(2,1)S(1)}, u32[]{:S(2)}, u32[]{:S(2)}) collective-permute-start(bf16[5,64,128]{2,1,0:T(8,128)(2,1)S(1)} %get-tuple-element.163), channel_id=1, source_target_pairs={{1,4},{4,1},{3,6},{6,3},{5,8},{8,5},{7,10},{10,7},{9,12},{12,9},{1... | collective-permute-start | bytes 245768 | tf_op jit(solution)/shard_map/ppermute | solution.py:476
  64.8 2.3 %collective-permute-start.29 = (bf16[5,64,128]{2,1,0:T(8,128)(2,1)S(1)}, bf16[5,64,128]{2,1,0:T(8,128)(2,1)S(1)}, u32[]{:S(2)}, u32[]{:S(2)}) collective-permute-start(bf16[5,64,128]{2,1,0:T(8,128)(2,1)S(1)} %get-tuple-element.156), channel_id=1, source_target_pairs={{1,4},{4,1},{3,6},{6,3},{5,8},{8,5},{7,10},{10,7},{9,12},{12,9},{1... | collective-permute-start | bytes 245768 | tf_op jit(solution)/shard_map/ppermute | solution.py:476
  68.1 2.1 %collective-permute-start.35 = (bf16[5,64,128]{2,1,0:T(8,128)(2,1)S(1)}, bf16[5,64,128]{2,1,0:T(8,128)(2,1)S(1)}, u32[]{:S(2)}, u32[]{:S(2)}) collective-permute-start(bf16[5,64,128]{2,1,0:T(8,128)(2,1)S(1)} %get-tuple-element.166), channel_id=1, source_target_pairs={{1,4},{4,1},{3,6},{6,3},{5,8},{8,5},{7,10},{10,7},{9,12},{12,9},{1... | collective-permute-start | bytes 245768 | tf_op jit(solution)/shard_map/ppermute | solution.py:476
  71.4 2.5 %collective-permute-start.37 = (bf16[5,64,128]{2,1,0:T(8,128)(2,1)S(1)}, bf16[5,64,128]{2,1,0:T(8,128)(2,1)S(1)}, u32[]{:S(2)}, u32[]{:S(2)}) collective-permute-start(bf16[5,64,128]{2,1,0:T(8,128)(2,1)S(1)} %get-tuple-element.170), channel_id=1, source_target_pairs={{1,4},{4,1},{3,6},{6,3},{5,8},{8,5},{7,10},{10,7},{9,12},{12,9},{1... | collective-permute-start | bytes 245768 | tf_op jit(solution)/shard_map/ppermute | solution.py:476
  74.0 1.5 %scaled.14 = (bf16[8,64,128]{2,1,0:T(8,128)(2,1)S(1)}, bf16[5,64,128]{2,1,0:T(8,128)(2,1)S(1)}, bf16[5,64,128]{2,1,0:T(8,128)(2,1)S(1)}) custom-call(s32[12]{0:T(128)S(4)} %get-tuple-element.99.ints, s32[8,9]{1,0:T(8,128)S(4)} %get-tuple-element.100.index, f32[8,9]{1,0:T(8,128)S(4)} %get-tuple-element.101.signs, f32[2]{0:T(128)S(4)} %get-tuple-element.102.scal, ...), custom_call_target="tpu_custom_call" | custom-call | flops 7247757312 | bytes 56623104 | tf_op jit(solution)/shard_map/scaled/pallas_call | solution.py:497
  75.4 2.0 %collective-permute-start.43 = (bf16[5,64,128]{2,1,0:T(8,128)(2,1)S(1)}, bf16[5,64,128]{2,1,0:T(8,128)(2,1)S(1)}, u32[]{:S(2)}, u32[]{:S(2)}) collective-permute-start(bf16[5,64,128]{2,1,0:T(8,128)(2,1)S(1)} %get-tuple-element.180), channel_id=1, source_target_pairs={{1,4},{4,1},{3,6},{6,3},{5,8},{8,5},{7,10},{10,7},{9,12},{12,9},{1... | collective-permute-start | bytes 245768 | tf_op jit(solution)/shard_map/ppermute | solution.py:476
  77.5 1.5 %scaled.15 = (bf16[8,64,128]{2,1,0:T(8,128)(2,1)S(1)}, bf16[5,64,128]{2,1,0:T(8,128)(2,1)S(1)}, bf16[5,64,128]{2,1,0:T(8,128)(2,1)S(1)}) custom-call(s32[12]{0:T(128)S(4)} %get-tuple-element.99.ints, s32[8,9]{1,0:T(8,128)S(4)} %get-tuple-element.100.index, f32[8,9]{1,0:T(8,128)S(4)} %get-tuple-element.101.signs, f32[2]{0:T(128)S(4)} %get-tuple-element.102.scal, ...), custom_call_target="tpu_custom_call" | custom-call | flops 7247757312 | bytes 56623104 | tf_op jit(solution)/shard_map/scaled/pallas_call | solution.py:497
  79.0 2.3 %collective-permute-start.39 = (bf16[5,64,128]{2,1,0:T(8,128)(2,1)S(1)}, bf16[5,64,128]{2,1,0:T(8,128)(2,1)S(1)}, u32[]{:S(2)}, u32[]{:S(2)}) collective-permute-start(bf16[5,64,128]{2,1,0:T(8,128)(2,1)S(1)} %get-tuple-element.173), channel_id=1, source_target_pairs={{1,4},{4,1},{3,6},{6,3},{5,8},{8,5},{7,10},{10,7},{9,12},{12,9},{1... | collective-permute-start | bytes 245768 | tf_op jit(solution)/shard_map/ppermute | solution.py:476
  82.2 2.0 %collective-permute-start.45 = (bf16[5,64,128]{2,1,0:T(8,128)(2,1)S(1)}, bf16[5,64,128]{2,1,0:T(8,128)(2,1)S(1)}, u32[]{:S(2)}, u32[]{:S(2)}) collective-permute-start(bf16[5,64,128]{2,1,0:T(8,128)(2,1)S(1)} %get-tuple-element.183), channel_id=1, source_target_pairs={{1,4},{4,1},{3,6},{6,3},{5,8},{8,5},{7,10},{10,7},{9,12},{12,9},{1... | collective-permute-start | bytes 245768 | tf_op jit(solution)/shard_map/ppermute | solution.py:476
  85.6 2.5 %collective-permute-start.41 = (bf16[5,64,128]{2,1,0:T(8,128)(2,1)S(1)}, bf16[5,64,128]{2,1,0:T(8,128)(2,1)S(1)}, u32[]{:S(2)}, u32[]{:S(2)}) collective-permute-start(bf16[5,64,128]{2,1,0:T(8,128)(2,1)S(1)} %get-tuple-element.176), channel_id=1, source_target_pairs={{1,4},{4,1},{3,6},{6,3},{5,8},{8,5},{7,10},{10,7},{9,12},{12,9},{1... | collective-permute-start | bytes 245768 | tf_op jit(solution)/shard_map/ppermute | solution.py:476
  89.2 1.9 %collective-permute-start.47 = (bf16[5,64,128]{2,1,0:T(8,128)(2,1)S(1)}, bf16[5,64,128]{2,1,0:T(8,128)(2,1)S(1)}, u32[]{:S(2)}, u32[]{:S(2)}) collective-permute-start(bf16[5,64,128]{2,1,0:T(8,128)(2,1)S(1)} %get-tuple-element.186), channel_id=1, source_target_pairs={{1,4},{4,1},{3,6},{6,3},{5,8},{8,5},{7,10},{10,7},{9,12},{12,9},{1... | collective-permute-start | bytes 245768 | tf_op jit(solution)/shard_map/ppermute | solution.py:476
  91.1 1.6 %collective-permute-start.49 = (bf16[8,64,128]{2,1,0:T(8,128)(2,1)S(1)}, bf16[8,64,128]{2,1,0:T(8,128)(2,1)S(1)}, u32[]{:S(2)}, u32[]{:S(2)}) collective-permute-start(bf16[8,64,128]{2,1,0:T(8,128)(2,1)S(1)} %get-tuple-element.185.own.refs_2_.refs_4_), channel_id=1, source_target_pairs={{2,0},{3,1},{0,2},{1,3},{6,4},{7,5},{4,6},{5,7},{10,8},{11,9},{8,1... | collective-permute-start | bytes 393224 | tf_op jit(solution)/shard_map/ppermute | solution.py:488
  93.6 1.2 collective-permute-start.50
  94.9 1.4 %collective-permute-start.52 = (bf16[8,64,128]{2,1,0:T(8,128)(2,1)S(1)}, bf16[8,64,128]{2,1,0:T(8,128)(2,1)S(1)}, u32[]{:S(2)}, u32[]{:S(2)}) collective-permute-start(bf16[8,64,128]{2,1,0:T(8,128)(2,1)S(1)} %get-tuple-element.189.own.refs_3_.refs_5_), channel_id=1, source_target_pairs={{2,0},{3,1},{0,2},{1,3},{6,4},{7,5},{4,6},{5,7},{10,8},{11,9},{8,1... | collective-permute-start | bytes 393224 | tf_op jit(solution)/shard_map/ppermute | solution.py:488
  97.0 1.5 %images.2.refs_0_ = bf16[2,64,1024]{2,1,0:T(8,128)(2,1)S(1)} custom-call(s32[12]{0:T(128)S(4)} %get-tuple-element.99.ints, s32[8,9]{1,0:T(8,128)S(4)} %get-tuple-element.100.index, f32[8,9]{1,0:T(8,128)S(4)} %get-tuple-element.101.signs, bf16[8,64,128]{2,1,0:T(8,128)(2,1)S(1)} %get-tuple-element.185.own.refs_2_.refs_4_, ...), custom_call_target="tpu_custom_call" | custom-call | flops 7247757312 | bytes 56623104 | tf_op jit(solution)/shard_map/images/pallas_call | solution.py:497
  99.4 1.5 %images.3.refs_1_ = bf16[2,64,1024]{2,1,0:T(8,128)(2,1)S(1)} custom-call(s32[12]{0:T(128)S(4)} %get-tuple-element.99.ints, s32[8,9]{1,0:T(8,128)S(4)} %get-tuple-element.100.index, f32[8,9]{1,0:T(8,128)S(4)} %get-tuple-element.101.signs, bf16[8,64,128]{2,1,0:T(8,128)(2,1)S(1)} %get-tuple-element.189.own.refs_3_.refs_5_, ...), custom_call_target="tpu_custom_call" | custom-call | flops 7247757312 | bytes 56623104 | tf_op jit(solution)/shard_map/images/pallas_call | solution.py:497
  101.5 1.2 collective-permute-done.53.right
  102.8 2.3 %collective-permute-start.56 = (bf16[208,128]{1,0:T(8,128)(2,1)S(1)}, bf16[208,128]{1,0:T(8,128)(2,1)S(1)}, u32[]{:S(2)}, u32[]{:S(2)}) collective-permute-start(bf16[208,128]{1,0:T(8,128)(2,1)S(1)} %add.9.refs_0_), channel_id=1, source_target_pairs={{0,12},{4,8},{8,4},{12,0},{1,13},{5,9},{9,5},{13,1},{2,14},{6,10},... | collective-permute-start | bytes 159752 | tf_op jit(solution)/shard_map/ppermute | solution.py:649
  105.1 2.2 %collective-permute-start.54 = (bf16[208,128]{1,0:T(8,128)(2,1)S(1)}, bf16[208,128]{1,0:T(8,128)(2,1)S(1)}, u32[]{:S(2)}, u32[]{:S(2)}) collective-permute-start(bf16[208,128]{1,0:T(8,128)(2,1)S(1)} %add.9.refs_0_), channel_id=1, source_target_pairs={{0,4},{4,0},{8,12},{12,8},{1,5},{5,1},{9,13},{13,9},{2,6},{6,2},{1... | collective-permute-start | bytes 159752 | tf_op jit(solution)/shard_map/ppermute | solution.py:649
  107.8 1.5 %collective-permute-done.56.refs_3_ = bf16[208,128]{1,0:T(8,128)(2,1)S(1)} collective-permute-done((bf16[208,128]{1,0:T(8,128)(2,1)S(1)}, bf16[208,128]{1,0:T(8,128)(2,1)S(1)}, u32[]{:S(2)}, u32[]{:S(2)}) %collective-permute-start.56) | collective-permute-done | bytes 53280 | tf_op jit(solution)/shard_map/ppermute | solution.py:649
  109.2 1.6 %collective-permute-done.55.refs_2_ = bf16[208,128]{1,0:T(8,128)(2,1)S(1)} collective-permute-done((bf16[208,128]{1,0:T(8,128)(2,1)S(1)}, bf16[208,128]{1,0:T(8,128)(2,1)S(1)}, u32[]{:S(2)}, u32[]{:S(2)}) %collective-permute-start.55) | collective-permute-done | bytes 53280 | tf_op jit(solution)/shard_map/ppermute | solution.py:649
  110.9 1.4 %collective-permute-start.57 = (bf16[208,128]{1,0:T(8,128)(2,1)S(1)}, bf16[208,128]{1,0:T(8,128)(2,1)S(1)}, u32[]{:S(2)}, u32[]{:S(2)}) collective-permute-start(bf16[208,128]{1,0:T(8,128)(2,1)S(1)} %sum.1.refs_0_), channel_id=1, source_target_pairs={{2,0},{3,1},{0,2},{1,3},{6,4},{7,5},{4,6},{5,7},{10,8},{11,9},{8,1... | collective-permute-start | bytes 159752 | tf_op jit(solution)/shard_map/ppermute | solution.py:488
  112.5 2.7 %collective-permute-done.57.refs_1_ = bf16[208,128]{1,0:T(8,128)(2,1)S(1)} collective-permute-done((bf16[208,128]{1,0:T(8,128)(2,1)S(1)}, bf16[208,128]{1,0:T(8,128)(2,1)S(1)}, u32[]{:S(2)}, u32[]{:S(2)}) %collective-permute-start.57) | collective-permute-done | bytes 53280 | tf_op jit(solution)/shard_map/ppermute | solution.py:488
  116.5 10.0 %finish.1 = (bf16[64,2048]{1,0:T(8,128)(2,1)}, f32[64,256]{1,0:T(8,128)}) custom-call(s32[12]{0:T(128)S(4)} %get-tuple-element.99.ints, bf16[208,128]{1,0:T(8,128)(2,1)S(1)} %sum.1.refs_0_, bf16[208,128]{1,0:T(8,128)(2,1)S(1)} %collective-permute-done.57.refs_1_, bf16[208,128]{1,0:T(8,128)(2,1)S(1)} %collective-permute-done.58.refs_2_, ...), custom_call_target="tpu_custom_call" | custom-call | flops 36238786560 | bytes 283115520 | tf_op jit(solution)/shard_map/finish/pallas_call | solution.py:497
  (116 shorter events, 25.6 us)
Async XLA Ops:
  2.3 9.1 %collective-permute-start.1 = (bf16[5,64,128]{2,1,0:T(8,128)(2,1)S(1)}, bf16[5,64,128]{2,1,0:T(8,128)(2,1)S(1)}, u32[]{:S(2)}, u32[]{:S(2)}) collective-permute-start(bf16[5,64,128]{2,1,0:T(8,128)(2,1)S(1)} %get-tuple-element.105), channel_id=1, source_target_pairs={{0,4},{1,13},{2,6},{3,15},{4,8},{5,1},{6,10},{7,3},{8,12},{9,5},{1... | collective-permute-start | bytes 245768 | tf_op jit(solution)/shard_map/ppermute | solution.py:484
  5.4 6.5 %collective-permute-start.2 = (bf16[5,64,128]{2,1,0:T(8,128)(2,1)S(1)}, bf16[5,64,128]{2,1,0:T(8,128)(2,1)S(1)}, u32[]{:S(2)}, u32[]{:S(2)}) collective-permute-start(bf16[5,64,128]{2,1,0:T(8,128)(2,1)S(1)} %get-tuple-element.106), channel_id=1, source_target_pairs={{1,4},{4,1},{3,6},{6,3},{5,8},{8,5},{7,10},{10,7},{9,12},{12,9},{1... | collective-permute-start | bytes 245768 | tf_op jit(solution)/shard_map/ppermute | solution.py:476
  7.0 4.9 %collective-permute-start = (bf16[13,64,128]{2,1,0:T(8,128)(2,1)S(1)}, bf16[13,64,128]{2,1,0:T(8,128)(2,1)S(1)}, u32[]{:S(2)}, u32[]{:S(2)}) collective-permute-start(bf16[13,64,128]{2,1,0:T(8,128)(2,1)S(1)} %get-tuple-element.103), channel_id=1, source_target_pairs={{0,1},{1,0},{2,3},{3,2},{4,5},{5,4},{6,7},{7,6},{8,9},{9,8},{10,11... | collective-permute-start | bytes 638984 | tf_op jit(solution)/shard_map/ppermute | solution.py:467
  13.5 5.8 %collective-permute-start.7 = (bf16[5,64,128]{2,1,0:T(8,128)(2,1)S(1)}, bf16[5,64,128]{2,1,0:T(8,128)(2,1)S(1)}, u32[]{:S(2)}, u32[]{:S(2)}) collective-permute-start(bf16[5,64,128]{2,1,0:T(8,128)(2,1)S(1)} %get-tuple-element.120), channel_id=1, source_target_pairs={{1,4},{4,1},{3,6},{6,3},{5,8},{8,5},{7,10},{10,7},{9,12},{12,9},{1... | collective-permute-start | bytes 245768 | tf_op jit(solution)/shard_map/ppermute | solution.py:476
  15.2 4.1 %collective-permute-start.8 = (bf16[5,64,128]{2,1,0:T(8,128)(2,1)S(1)}, bf16[5,64,128]{2,1,0:T(8,128)(2,1)S(1)}, u32[]{:S(2)}, u32[]{:S(2)}) collective-permute-start(bf16[5,64,128]{2,1,0:T(8,128)(2,1)S(1)} %get-tuple-element.121), channel_id=1, source_target_pairs={{0,1},{1,0},{2,3},{3,2},{4,5},{5,4},{6,7},{7,6},{8,9},{9,8},{10,11... | collective-permute-start | bytes 245768 | tf_op jit(solution)/shard_map/ppermute | solution.py:467
  16.7 5.9 %collective-permute-start.3 = (bf16[5,64,128]{2,1,0:T(8,128)(2,1)S(1)}, bf16[5,64,128]{2,1,0:T(8,128)(2,1)S(1)}, u32[]{:S(2)}, u32[]{:S(2)}) collective-permute-start(bf16[5,64,128]{2,1,0:T(8,128)(2,1)S(1)} %get-tuple-element.113), channel_id=1, source_target_pairs={{1,4},{4,1},{3,6},{6,3},{5,8},{8,5},{7,10},{10,7},{9,12},{12,9},{1... | collective-permute-start | bytes 245768 | tf_op jit(solution)/shard_map/ppermute | solution.py:476
  18.6 4.0 %collective-permute-start.4 = (bf16[5,64,128]{2,1,0:T(8,128)(2,1)S(1)}, bf16[5,64,128]{2,1,0:T(8,128)(2,1)S(1)}, u32[]{:S(2)}, u32[]{:S(2)}) collective-permute-start(bf16[5,64,128]{2,1,0:T(8,128)(2,1)S(1)} %get-tuple-element.114), channel_id=1, source_target_pairs={{0,1},{1,0},{2,3},{3,2},{4,5},{5,4},{6,7},{7,6},{8,9},{9,8},{10,11... | collective-permute-start | bytes 245768 | tf_op jit(solution)/shard_map/ppermute | solution.py:467
  20.2 5.7 %collective-permute-start.9 = (bf16[5,64,128]{2,1,0:T(8,128)(2,1)S(1)}, bf16[5,64,128]{2,1,0:T(8,128)(2,1)S(1)}, u32[]{:S(2)}, u32[]{:S(2)}) collective-permute-start(bf16[5,64,128]{2,1,0:T(8,128)(2,1)S(1)} %get-tuple-element.123), channel_id=1, source_target_pairs={{1,4},{4,1},{3,6},{6,3},{5,8},{8,5},{7,10},{10,7},{9,12},{12,9},{1... | collective-permute-start | bytes 245768 | tf_op jit(solution)/shard_map/ppermute | solution.py:476
  21.8 4.1 %collective-permute-start.10 = (bf16[5,64,128]{2,1,0:T(8,128)(2,1)S(1)}, bf16[5,64,128]{2,1,0:T(8,128)(2,1)S(1)}, u32[]{:S(2)}, u32[]{:S(2)}) collective-permute-start(bf16[5,64,128]{2,1,0:T(8,128)(2,1)S(1)} %get-tuple-element.124), channel_id=1, source_target_pairs={{0,1},{1,0},{2,3},{3,2},{4,5},{5,4},{6,7},{7,6},{8,9},{9,8},{10,11... | collective-permute-start | bytes 245768 | tf_op jit(solution)/shard_map/ppermute | solution.py:467
  23.5 5.8 %collective-permute-start.5 = (bf16[5,64,128]{2,1,0:T(8,128)(2,1)S(1)}, bf16[5,64,128]{2,1,0:T(8,128)(2,1)S(1)}, u32[]{:S(2)}, u32[]{:S(2)}) collective-permute-start(bf16[5,64,128]{2,1,0:T(8,128)(2,1)S(1)} %get-tuple-element.116), channel_id=1, source_target_pairs={{1,4},{4,1},{3,6},{6,3},{5,8},{8,5},{7,10},{10,7},{9,12},{12,9},{1... | collective-permute-start | bytes 245768 | tf_op jit(solution)/shard_map/ppermute | solution.py:476
  25.4 3.9 %collective-permute-start.6 = (bf16[5,64,128]{2,1,0:T(8,128)(2,1)S(1)}, bf16[5,64,128]{2,1,0:T(8,128)(2,1)S(1)}, u32[]{:S(2)}, u32[]{:S(2)}) collective-permute-start(bf16[5,64,128]{2,1,0:T(8,128)(2,1)S(1)} %get-tuple-element.117), channel_id=1, source_target_pairs={{0,1},{1,0},{2,3},{3,2},{4,5},{5,4},{6,7},{7,6},{8,9},{9,8},{10,11... | collective-permute-start | bytes 245768 | tf_op jit(solution)/shard_map/ppermute | solution.py:467
  26.8 5.7 %collective-permute-start.11 = (bf16[5,64,128]{2,1,0:T(8,128)(2,1)S(1)}, bf16[5,64,128]{2,1,0:T(8,128)(2,1)S(1)}, u32[]{:S(2)}, u32[]{:S(2)}) collective-permute-start(bf16[5,64,128]{2,1,0:T(8,128)(2,1)S(1)} %get-tuple-element.126), channel_id=1, source_target_pairs={{1,4},{4,1},{3,6},{6,3},{5,8},{8,5},{7,10},{10,7},{9,12},{12,9},{1... | collective-permute-start | bytes 245768 | tf_op jit(solution)/shard_map/ppermute | solution.py:476
  28.6 3.9 %collective-permute-start.12 = (bf16[5,64,128]{2,1,0:T(8,128)(2,1)S(1)}, bf16[5,64,128]{2,1,0:T(8,128)(2,1)S(1)}, u32[]{:S(2)}, u32[]{:S(2)}) collective-permute-start(bf16[5,64,128]{2,1,0:T(8,128)(2,1)S(1)} %get-tuple-element.127), channel_id=1, source_target_pairs={{0,1},{1,0},{2,3},{3,2},{4,5},{5,4},{6,7},{7,6},{8,9},{9,8},{10,11... | collective-permute-start | bytes 245768 | tf_op jit(solution)/shard_map/ppermute | solution.py:467
  30.1 5.9 %collective-permute-start.13 = (bf16[5,64,128]{2,1,0:T(8,128)(2,1)S(1)}, bf16[5,64,128]{2,1,0:T(8,128)(2,1)S(1)}, u32[]{:S(2)}, u32[]{:S(2)}) collective-permute-start(bf16[5,64,128]{2,1,0:T(8,128)(2,1)S(1)} %get-tuple-element.130), channel_id=1, source_target_pairs={{1,4},{4,1},{3,6},{6,3},{5,8},{8,5},{7,10},{10,7},{9,12},{12,9},{1... | collective-permute-start | bytes 245768 | tf_op jit(solution)/shard_map/ppermute | solution.py:476
  32.1 3.9 %collective-permute-start.14 = (bf16[5,64,128]{2,1,0:T(8,128)(2,1)S(1)}, bf16[5,64,128]{2,1,0:T(8,128)(2,1)S(1)}, u32[]{:S(2)}, u32[]{:S(2)}) collective-permute-start(bf16[5,64,128]{2,1,0:T(8,128)(2,1)S(1)} %get-tuple-element.131), channel_id=1, source_target_pairs={{0,1},{1,0},{2,3},{3,2},{4,5},{5,4},{6,7},{7,6},{8,9},{9,8},{10,11... | collective-permute-start | bytes 245768 | tf_op jit(solution)/shard_map/ppermute | solution.py:467
  34.0 5.7 %collective-permute-start.19 = (bf16[5,64,128]{2,1,0:T(8,128)(2,1)S(1)}, bf16[5,64,128]{2,1,0:T(8,128)(2,1)S(1)}, u32[]{:S(2)}, u32[]{:S(2)}) collective-permute-start(bf16[5,64,128]{2,1,0:T(8,128)(2,1)S(1)} %get-tuple-element.140), channel_id=1, source_target_pairs={{1,4},{4,1},{3,6},{6,3},{5,8},{8,5},{7,10},{10,7},{9,12},{12,9},{1... | collective-permute-start | bytes 245768 | tf_op jit(solution)/shard_map/ppermute | solution.py:476
  37.5 5.7 %collective-permute-start.15 = (bf16[5,64,128]{2,1,0:T(8,128)(2,1)S(1)}, bf16[5,64,128]{2,1,0:T(8,128)(2,1)S(1)}, u32[]{:S(2)}, u32[]{:S(2)}) collective-permute-start(bf16[5,64,128]{2,1,0:T(8,128)(2,1)S(1)} %get-tuple-element.133), channel_id=1, source_target_pairs={{1,4},{4,1},{3,6},{6,3},{5,8},{8,5},{7,10},{10,7},{9,12},{12,9},{1... | collective-permute-start | bytes 245768 | tf_op jit(solution)/shard_map/ppermute | solution.py:476
  39.4 3.8 %collective-permute-start.16 = (bf16[5,64,128]{2,1,0:T(8,128)(2,1)S(1)}, bf16[5,64,128]{2,1,0:T(8,128)(2,1)S(1)}, u32[]{:S(2)}, u32[]{:S(2)}) collective-permute-start(bf16[5,64,128]{2,1,0:T(8,128)(2,1)S(1)} %get-tuple-element.134), channel_id=1, source_target_pairs={{0,1},{1,0},{2,3},{3,2},{4,5},{5,4},{6,7},{7,6},{8,9},{9,8},{10,11... | collective-permute-start | bytes 245768 | tf_op jit(solution)/shard_map/ppermute | solution.py:467
  40.6 5.7 %collective-permute-start.21 = (bf16[5,64,128]{2,1,0:T(8,128)(2,1)S(1)}, bf16[5,64,128]{2,1,0:T(8,128)(2,1)S(1)}, u32[]{:S(2)}, u32[]{:S(2)}) collective-permute-start(bf16[5,64,128]{2,1,0:T(8,128)(2,1)S(1)} %get-tuple-element.143), channel_id=1, source_target_pairs={{1,4},{4,1},{3,6},{6,3},{5,8},{8,5},{7,10},{10,7},{9,12},{12,9},{1... | collective-permute-start | bytes 245768 | tf_op jit(solution)/shard_map/ppermute | solution.py:476
  44.1 5.7 %collective-permute-start.17 = (bf16[5,64,128]{2,1,0:T(8,128)(2,1)S(1)}, bf16[5,64,128]{2,1,0:T(8,128)(2,1)S(1)}, u32[]{:S(2)}, u32[]{:S(2)}) collective-permute-start(bf16[5,64,128]{2,1,0:T(8,128)(2,1)S(1)} %get-tuple-element.136), channel_id=1, source_target_pairs={{1,4},{4,1},{3,6},{6,3},{5,8},{8,5},{7,10},{10,7},{9,12},{12,9},{1... | collective-permute-start | bytes 245768 | tf_op jit(solution)/shard_map/ppermute | solution.py:476
  47.2 5.9 %collective-permute-start.23 = (bf16[5,64,128]{2,1,0:T(8,128)(2,1)S(1)}, bf16[5,64,128]{2,1,0:T(8,128)(2,1)S(1)}, u32[]{:S(2)}, u32[]{:S(2)}) collective-permute-start(bf16[5,64,128]{2,1,0:T(8,128)(2,1)S(1)} %get-tuple-element.146), channel_id=1, source_target_pairs={{1,4},{4,1},{3,6},{6,3},{5,8},{8,5},{7,10},{10,7},{9,12},{12,9},{1... | collective-permute-start | bytes 245768 | tf_op jit(solution)/shard_map/ppermute | solution.py:476
  50.9 5.8 %collective-permute-start.25 = (bf16[5,64,128]{2,1,0:T(8,128)(2,1)S(1)}, bf16[5,64,128]{2,1,0:T(8,128)(2,1)S(1)}, u32[]{:S(2)}, u32[]{:S(2)}) collective-permute-start(bf16[5,64,128]{2,1,0:T(8,128)(2,1)S(1)} %get-tuple-element.150), channel_id=1, source_target_pairs={{1,4},{4,1},{3,6},{6,3},{5,8},{8,5},{7,10},{10,7},{9,12},{12,9},{1... | collective-permute-start | bytes 245768 | tf_op jit(solution)/shard_map/ppermute | solution.py:476
  54.6 5.8 %collective-permute-start.31 = (bf16[5,64,128]{2,1,0:T(8,128)(2,1)S(1)}, bf16[5,64,128]{2,1,0:T(8,128)(2,1)S(1)}, u32[]{:S(2)}, u32[]{:S(2)}) collective-permute-start(bf16[5,64,128]{2,1,0:T(8,128)(2,1)S(1)} %get-tuple-element.160), channel_id=1, source_target_pairs={{1,4},{4,1},{3,6},{6,3},{5,8},{8,5},{7,10},{10,7},{9,12},{12,9},{1... | collective-permute-start | bytes 245768 | tf_op jit(solution)/shard_map/ppermute | solution.py:476
  58.2 5.7 %collective-permute-start.27 = (bf16[5,64,128]{2,1,0:T(8,128)(2,1)S(1)}, bf16[5,64,128]{2,1,0:T(8,128)(2,1)S(1)}, u32[]{:S(2)}, u32[]{:S(2)}) collective-permute-start(bf16[5,64,128]{2,1,0:T(8,128)(2,1)S(1)} %get-tuple-element.153), channel_id=1, source_target_pairs={{1,4},{4,1},{3,6},{6,3},{5,8},{8,5},{7,10},{10,7},{9,12},{12,9},{1... | collective-permute-start | bytes 245768 | tf_op jit(solution)/shard_map/ppermute | solution.py:476
  61.3 5.9 %collective-permute-start.33 = (bf16[5,64,128]{2,1,0:T(8,128)(2,1)S(1)}, bf16[5,64,128]{2,1,0:T(8,128)(2,1)S(1)}, u32[]{:S(2)}, u32[]{:S(2)}) collective-permute-start(bf16[5,64,128]{2,1,0:T(8,128)(2,1)S(1)} %get-tuple-element.163), channel_id=1, source_target_pairs={{1,4},{4,1},{3,6},{6,3},{5,8},{8,5},{7,10},{10,7},{9,12},{12,9},{1... | collective-permute-start | bytes 245768 | tf_op jit(solution)/shard_map/ppermute | solution.py:476
  64.8 5.7 %collective-permute-start.29 = (bf16[5,64,128]{2,1,0:T(8,128)(2,1)S(1)}, bf16[5,64,128]{2,1,0:T(8,128)(2,1)S(1)}, u32[]{:S(2)}, u32[]{:S(2)}) collective-permute-start(bf16[5,64,128]{2,1,0:T(8,128)(2,1)S(1)} %get-tuple-element.156), channel_id=1, source_target_pairs={{1,4},{4,1},{3,6},{6,3},{5,8},{8,5},{7,10},{10,7},{9,12},{12,9},{1... | collective-permute-start | bytes 245768 | tf_op jit(solution)/shard_map/ppermute | solution.py:476
  68.1 5.9 %collective-permute-start.35 = (bf16[5,64,128]{2,1,0:T(8,128)(2,1)S(1)}, bf16[5,64,128]{2,1,0:T(8,128)(2,1)S(1)}, u32[]{:S(2)}, u32[]{:S(2)}) collective-permute-start(bf16[5,64,128]{2,1,0:T(8,128)(2,1)S(1)} %get-tuple-element.166), channel_id=1, source_target_pairs={{1,4},{4,1},{3,6},{6,3},{5,8},{8,5},{7,10},{10,7},{9,12},{12,9},{1... | collective-permute-start | bytes 245768 | tf_op jit(solution)/shard_map/ppermute | solution.py:476
  71.4 6.1 %collective-permute-start.37 = (bf16[5,64,128]{2,1,0:T(8,128)(2,1)S(1)}, bf16[5,64,128]{2,1,0:T(8,128)(2,1)S(1)}, u32[]{:S(2)}, u32[]{:S(2)}) collective-permute-start(bf16[5,64,128]{2,1,0:T(8,128)(2,1)S(1)} %get-tuple-element.170), channel_id=1, source_target_pairs={{1,4},{4,1},{3,6},{6,3},{5,8},{8,5},{7,10},{10,7},{9,12},{12,9},{1... | collective-permute-start | bytes 245768 | tf_op jit(solution)/shard_map/ppermute | solution.py:476
  75.4 5.9 %collective-permute-start.43 = (bf16[5,64,128]{2,1,0:T(8,128)(2,1)S(1)}, bf16[5,64,128]{2,1,0:T(8,128)(2,1)S(1)}, u32[]{:S(2)}, u32[]{:S(2)}) collective-permute-start(bf16[5,64,128]{2,1,0:T(8,128)(2,1)S(1)} %get-tuple-element.180), channel_id=1, source_target_pairs={{1,4},{4,1},{3,6},{6,3},{5,8},{8,5},{7,10},{10,7},{9,12},{12,9},{1... | collective-permute-start | bytes 245768 | tf_op jit(solution)/shard_map/ppermute | solution.py:476
  79.0 5.7 %collective-permute-start.39 = (bf16[5,64,128]{2,1,0:T(8,128)(2,1)S(1)}, bf16[5,64,128]{2,1,0:T(8,128)(2,1)S(1)}, u32[]{:S(2)}, u32[]{:S(2)}) collective-permute-start(bf16[5,64,128]{2,1,0:T(8,128)(2,1)S(1)} %get-tuple-element.173), channel_id=1, source_target_pairs={{1,4},{4,1},{3,6},{6,3},{5,8},{8,5},{7,10},{10,7},{9,12},{12,9},{1... | collective-permute-start | bytes 245768 | tf_op jit(solution)/shard_map/ppermute | solution.py:476
  82.2 5.9 %collective-permute-start.45 = (bf16[5,64,128]{2,1,0:T(8,128)(2,1)S(1)}, bf16[5,64,128]{2,1,0:T(8,128)(2,1)S(1)}, u32[]{:S(2)}, u32[]{:S(2)}) collective-permute-start(bf16[5,64,128]{2,1,0:T(8,128)(2,1)S(1)} %get-tuple-element.183), channel_id=1, source_target_pairs={{1,4},{4,1},{3,6},{6,3},{5,8},{8,5},{7,10},{10,7},{9,12},{12,9},{1... | collective-permute-start | bytes 245768 | tf_op jit(solution)/shard_map/ppermute | solution.py:476
  84.1 3.9 %collective-permute-start.46 = (bf16[5,64,128]{2,1,0:T(8,128)(2,1)S(1)}, bf16[5,64,128]{2,1,0:T(8,128)(2,1)S(1)}, u32[]{:S(2)}, u32[]{:S(2)}) collective-permute-start(bf16[5,64,128]{2,1,0:T(8,128)(2,1)S(1)} %get-tuple-element.184), channel_id=1, source_target_pairs={{0,1},{1,0},{2,3},{3,2},{4,5},{5,4},{6,7},{7,6},{8,9},{9,8},{10,11... | collective-permute-start | bytes 245768 | tf_op jit(solution)/shard_map/ppermute | solution.py:467
  85.6 7.2 %collective-permute-start.41 = (bf16[5,64,128]{2,1,0:T(8,128)(2,1)S(1)}, bf16[5,64,128]{2,1,0:T(8,128)(2,1)S(1)}, u32[]{:S(2)}, u32[]{:S(2)}) collective-permute-start(bf16[5,64,128]{2,1,0:T(8,128)(2,1)S(1)} %get-tuple-element.176), channel_id=1, source_target_pairs={{1,4},{4,1},{3,6},{6,3},{5,8},{8,5},{7,10},{10,7},{9,12},{12,9},{1... | collective-permute-start | bytes 245768 | tf_op jit(solution)/shard_map/ppermute | solution.py:476
  88.1 4.7 %collective-permute-start.42 = (bf16[5,64,128]{2,1,0:T(8,128)(2,1)S(1)}, bf16[5,64,128]{2,1,0:T(8,128)(2,1)S(1)}, u32[]{:S(2)}, u32[]{:S(2)}) collective-permute-start(bf16[5,64,128]{2,1,0:T(8,128)(2,1)S(1)} %get-tuple-element.177), channel_id=1, source_target_pairs={{0,1},{1,0},{2,3},{3,2},{4,5},{5,4},{6,7},{7,6},{8,9},{9,8},{10,11... | collective-permute-start | bytes 245768 | tf_op jit(solution)/shard_map/ppermute | solution.py:467
  89.2 5.7 %collective-permute-start.47 = (bf16[5,64,128]{2,1,0:T(8,128)(2,1)S(1)}, bf16[5,64,128]{2,1,0:T(8,128)(2,1)S(1)}, u32[]{:S(2)}, u32[]{:S(2)}) collective-permute-start(bf16[5,64,128]{2,1,0:T(8,128)(2,1)S(1)} %get-tuple-element.186), channel_id=1, source_target_pairs={{1,4},{4,1},{3,6},{6,3},{5,8},{8,5},{7,10},{10,7},{9,12},{12,9},{1... | collective-permute-start | bytes 245768 | tf_op jit(solution)/shard_map/ppermute | solution.py:476
  91.1 5.2 %collective-permute-start.48 = (bf16[5,64,128]{2,1,0:T(8,128)(2,1)S(1)}, bf16[5,64,128]{2,1,0:T(8,128)(2,1)S(1)}, u32[]{:S(2)}, u32[]{:S(2)}) collective-permute-start(bf16[5,64,128]{2,1,0:T(8,128)(2,1)S(1)} %get-tuple-element.187), channel_id=1, source_target_pairs={{0,1},{1,0},{2,3},{3,2},{4,5},{5,4},{6,7},{7,6},{8,9},{9,8},{10,11... | collective-permute-start | bytes 245768 | tf_op jit(solution)/shard_map/ppermute | solution.py:467
  91.1 5.9 %collective-permute-start.49 = (bf16[8,64,128]{2,1,0:T(8,128)(2,1)S(1)}, bf16[8,64,128]{2,1,0:T(8,128)(2,1)S(1)}, u32[]{:S(2)}, u32[]{:S(2)}) collective-permute-start(bf16[8,64,128]{2,1,0:T(8,128)(2,1)S(1)} %get-tuple-element.185.own.refs_2_.refs_4_), channel_id=1, source_target_pairs={{2,0},{3,1},{0,2},{1,3},{6,4},{7,5},{4,6},{5,7},{10,8},{11,9},{8,1... | collective-permute-start | bytes 393224 | tf_op jit(solution)/shard_map/ppermute | solution.py:488
  93.6 5.7 %collective-permute-start.50 = (bf16[5,64,128]{2,1,0:T(8,128)(2,1)S(1)}, bf16[5,64,128]{2,1,0:T(8,128)(2,1)S(1)}, u32[]{:S(2)}, u32[]{:S(2)}) collective-permute-start(bf16[5,64,128]{2,1,0:T(8,128)(2,1)S(1)} %get-tuple-element.190), channel_id=1, source_target_pairs={{1,4},{4,1},{3,6},{6,3},{5,8},{8,5},{7,10},{10,7},{9,12},{12,9},{1... | collective-permute-start | bytes 245768 | tf_op jit(solution)/shard_map/ppermute | solution.py:476
  94.9 4.5 %collective-permute-start.51 = (bf16[5,64,128]{2,1,0:T(8,128)(2,1)S(1)}, bf16[5,64,128]{2,1,0:T(8,128)(2,1)S(1)}, u32[]{:S(2)}, u32[]{:S(2)}) collective-permute-start(bf16[5,64,128]{2,1,0:T(8,128)(2,1)S(1)} %get-tuple-element.191), channel_id=1, source_target_pairs={{0,1},{1,0},{2,3},{3,2},{4,5},{5,4},{6,7},{7,6},{8,9},{9,8},{10,11... | collective-permute-start | bytes 245768 | tf_op jit(solution)/shard_map/ppermute | solution.py:467
  94.9 6.0 %collective-permute-start.52 = (bf16[8,64,128]{2,1,0:T(8,128)(2,1)S(1)}, bf16[8,64,128]{2,1,0:T(8,128)(2,1)S(1)}, u32[]{:S(2)}, u32[]{:S(2)}) collective-permute-start(bf16[8,64,128]{2,1,0:T(8,128)(2,1)S(1)} %get-tuple-element.189.own.refs_3_.refs_5_), channel_id=1, source_target_pairs={{2,0},{3,1},{0,2},{1,3},{6,4},{7,5},{4,6},{5,7},{10,8},{11,9},{8,1... | collective-permute-start | bytes 393224 | tf_op jit(solution)/shard_map/ppermute | solution.py:488
  102.8 6.4 %collective-permute-start.56 = (bf16[208,128]{1,0:T(8,128)(2,1)S(1)}, bf16[208,128]{1,0:T(8,128)(2,1)S(1)}, u32[]{:S(2)}, u32[]{:S(2)}) collective-permute-start(bf16[208,128]{1,0:T(8,128)(2,1)S(1)} %add.9.refs_0_), channel_id=1, source_target_pairs={{0,12},{4,8},{8,4},{12,0},{1,13},{5,9},{9,5},{13,1},{2,14},{6,10},... | collective-permute-start | bytes 159752 | tf_op jit(solution)/shard_map/ppermute | solution.py:649
  105.1 5.8 %collective-permute-start.55 = (bf16[208,128]{1,0:T(8,128)(2,1)S(1)}, bf16[208,128]{1,0:T(8,128)(2,1)S(1)}, u32[]{:S(2)}, u32[]{:S(2)}) collective-permute-start(bf16[208,128]{1,0:T(8,128)(2,1)S(1)} %add.9.refs_0_), channel_id=1, source_target_pairs={{0,8},{4,12},{8,0},{12,4},{1,9},{5,13},{9,1},{13,5},{2,10},{6,14},... | collective-permute-start | bytes 159752 | tf_op jit(solution)/shard_map/ppermute | solution.py:649
  105.1 5.8 %collective-permute-start.54 = (bf16[208,128]{1,0:T(8,128)(2,1)S(1)}, bf16[208,128]{1,0:T(8,128)(2,1)S(1)}, u32[]{:S(2)}, u32[]{:S(2)}) collective-permute-start(bf16[208,128]{1,0:T(8,128)(2,1)S(1)} %add.9.refs_0_), channel_id=1, source_target_pairs={{0,4},{4,0},{8,12},{12,8},{1,5},{5,1},{9,13},{13,9},{2,6},{6,2},{1... | collective-permute-start | bytes 159752 | tf_op jit(solution)/shard_map/ppermute | solution.py:649
  107.3 5.1 %collective-permute-start.60 = (bf16[8,64,128]{2,1,0:T(8,128)(2,1)S(1)}, bf16[8,64,128]{2,1,0:T(8,128)(2,1)S(1)}, u32[]{:S(2)}, u32[]{:S(2)}) collective-permute-start(bf16[8,64,128]{2,1,0:T(8,128)(2,1)S(1)} %get-tuple-element.185.own.refs_2_.refs_4_), channel_id=1, source_target_pairs={{0,1},{1,0},{2,3},{3,2},{4,5},{5,4},{6,7},{7,6},{8,9},{9,8},{10,11... | collective-permute-start | bytes 393224 | tf_op jit(solution)/shard_map/ppermute | solution.py:467
  107.3 8.0 %collective-permute-start.61 = (bf16[8,64,128]{2,1,0:T(8,128)(2,1)S(1)}, bf16[8,64,128]{2,1,0:T(8,128)(2,1)S(1)}, u32[]{:S(2)}, u32[]{:S(2)}) collective-permute-start(bf16[8,64,128]{2,1,0:T(8,128)(2,1)S(1)} %get-tuple-element.189.own.refs_3_.refs_5_), channel_id=1, source_target_pairs={{0,1},{1,0},{2,3},{3,2},{4,5},{5,4},{6,7},{7,6},{8,9},{9,8},{10,11... | collective-permute-start | bytes 393224 | tf_op jit(solution)/shard_map/ppermute | solution.py:467
  109.2 6.0 %collective-permute-start.62 = (bf16[8,64,128]{2,1,0:T(8,128)(2,1)S(1)}, bf16[8,64,128]{2,1,0:T(8,128)(2,1)S(1)}, u32[]{:S(2)}, u32[]{:S(2)}) collective-permute-start(bf16[8,64,128]{2,1,0:T(8,128)(2,1)S(1)} %collective-permute-done.49.y_other.refs_4_.refs_6_), channel_id=1, source_target_pairs={{0,1},{1,0},{2,3},{3,2},{4,5},{5,4},{6,7},{7,6},{8,9},{9,8},{10,11... | collective-permute-start | bytes 393224 | tf_op jit(solution)/shard_map/ppermute | solution.py:467
  110.8 4.4 %collective-permute-start.63 = (bf16[8,64,128]{2,1,0:T(8,128)(2,1)S(1)}, bf16[8,64,128]{2,1,0:T(8,128)(2,1)S(1)}, u32[]{:S(2)}, u32[]{:S(2)}) collective-permute-start(bf16[8,64,128]{2,1,0:T(8,128)(2,1)S(1)} %collective-permute-done.52.refs_5_.refs_7_), channel_id=1, source_target_pairs={{0,1},{1,0},{2,3},{3,2},{4,5},{5,4},{6,7},{7,6},{8,9},{9,8},{10,11... | collective-permute-start | bytes 393224 | tf_op jit(solution)/shard_map/ppermute | solution.py:467
  110.9 4.3 %collective-permute-start.57 = (bf16[208,128]{1,0:T(8,128)(2,1)S(1)}, bf16[208,128]{1,0:T(8,128)(2,1)S(1)}, u32[]{:S(2)}, u32[]{:S(2)}) collective-permute-start(bf16[208,128]{1,0:T(8,128)(2,1)S(1)} %sum.1.refs_0_), channel_id=1, source_target_pairs={{2,0},{3,1},{0,2},{1,3},{6,4},{7,5},{4,6},{5,7},{10,8},{11,9},{8,1... | collective-permute-start | bytes 159752 | tf_op jit(solution)/shard_map/ppermute | solution.py:488
  (16 other events, 53.0 us)

commit v9 on v8

--- a/solution.py
+++ b/solution.py
@@ -136,24 +136,41 @@
         copy.wait()
 
 
+def for_rows(count, step):
+    def pair(i, carry):
+        step(2 * i)
+        step(2 * i + 1)
+        return carry
+
+    lax.fori_loop(0, count // 2, pair, 0)
+    if count % 2:
+        step(count - 1)
+
+
 def scaled_kernel(
     ints, index, signs, scal, own, inter, intra, ham, ovl, out, inter_out, intra_out, ext
 ):
     core = ints[0]
     fill_ext(core, own, intra, inter, ext)
     inv = 1.0 / (jnp.zeros(own.shape[1:], F32) + scal[1])
-    for row in range(own.shape[0]):
+
+    def step(row):
         image_h, image_e = both_rows((index, signs), ext, ham, ovl, row)
         mine = own[row].astype(F32)
         out[row] = ((image_h - scal[0] * (mine + image_e)) * inv).astype(BF16)
+
+    for_rows(own.shape[0], step)
     send_ends(core, out, intra_out, inter_out)
 
 
 def term_kernel(ints, index, signs, own, inter, intra, ovl, out, inter_out, intra_out, ext):
     core = ints[0]
     fill_ext(core, own, intra, inter, ext)
-    for row in range(own.shape[0]):
+
+    def step(row):
         out[row] = (-one_row((index, signs), ext, ovl, row)).astype(BF16)
+
+    for_rows(own.shape[0], step)
     send_ends(core, out, intra_out, inter_out)
 
 
@@ -166,12 +183,15 @@
     half = own.shape[0]
     fill_ext(core, own, intra, inter, ext)
     lane = lax.broadcasted_iota(jnp.int32, own.shape[1:], 1)
-    for row in range(half):
+
+    def step(row):
         image = one_row((index, signs), ext, ovl, row)
         filtered = scaled[row].astype(F32) + own[row].astype(F32) - image
         if not first:
             filtered = 2.0 * filtered - previous[row].astype(F32)
         out[row] = jnp.where(lane < ints[4 + row], filtered, 0.0).astype(BF16)
+
+    for_rows(half, step)
     send_ends(core, out, intra_out, inter_out)
 
 
@@ -336,36 +356,36 @@
 
 def factor(work, inverse):
     size = work.shape[0]
-    wide = lax.broadcasted_iota(jnp.int32, (PANEL, size), 1)
+    lane = lax.broadcasted_iota(jnp.int32, (PANEL, size), 1)
     tall = lax.broadcasted_iota(jnp.int32, (PANEL, size), 0)
-    lane = lax.broadcasted_iota(jnp.int32, (PANEL, 128), 1)
+    all_rows = lax.broadcasted_iota(jnp.int32, (size, size), 0)
+    columns = lax.broadcasted_iota(jnp.int32, (size, size), 1)
     zero = jnp.zeros((PANEL, size), BF16)
-    for start in range(0, size, PANEL):
-        rows = work[start : start + PANEL, :]
-        tile = start // 128 * 128
-        block = work[start : start + PANEL, tile : tile + 128]
-        if start % 128:
-            block = pltpu.roll(block, 128 - start % 128, axis=1)
+
+    def panel(i, carry):
+        start = pl.multiple_of(i * PANEL, PANEL)
+        after = start + PANEL
+        rows = work[pl.ds(start, PANEL), :]
+        block = pltpu.roll(rows, lax.rem(size - start, size), axis=1)
         t_high, t_mid, t_low = split3(jnp.where(lane < PANEL, 0.0, panel_inverse(block)))
         first = jnp.where(lane < 2 * PANEL, t_high, jnp.where(lane < 3 * PANEL, t_mid, t_low))
         second = jnp.where(lane < 2 * PANEL, t_high, jnp.where(lane < 3 * PANEL, t_mid, t_high))
         left = jnp.concatenate([first, second], axis=1)
-        inside = (wide >= start) & (wide < start + PANEL)
-        rows = jnp.where(inside, jnp.where(wide - start == tall, 1.0, 0.0), rows)
+        inside = (lane >= start) & (lane < after)
+        rows = jnp.where(inside, jnp.where(lane - start == tall, 1.0, 0.0), rows)
         r_high, r_mid, r_low = split3(rows)
         right = jnp.concatenate([zero, r_high, r_high, r_high, zero, r_mid, r_mid, r_low], axis=0)
         new = jnp.dot(left, right, preferred_element_type=F32)
-        inverse[start : start + PANEL, :] = jnp.where(wide < start + PANEL, new, 0.0)
-        after = start + PANEL
-        if after < size:
-            high, middle, low = split3(new)
-            base = after // 128 * 128
-            lhs = jnp.concatenate([high, high, middle, middle, high, low], axis=0)[:, base:]
-            rhs = jnp.concatenate([high, middle, high, middle, low, high], axis=0)
-            change = lax.dot_general(lhs, rhs, TN, preferred_element_type=F32)[after - base :]
-            columns = lax.broadcasted_iota(jnp.int32, change.shape, 1)
-            old = work[after:, :]
-            work[after:, :] = jnp.where((columns >= start) & (columns < after), 0.0, old) - change
+        inverse[pl.ds(start, PANEL), :] = jnp.where(lane < after, new, 0.0)
+        high, middle, low = split3(new)
+        lhs = jnp.concatenate([high, high, middle, middle, high, low], axis=0)
+        rhs = jnp.concatenate([high, middle, high, middle, low, high], axis=0)
+        change = lax.dot_general(lhs, rhs, TN, preferred_element_type=F32)
+        old = jnp.where((columns >= start) & (columns < after), 0.0, work[...])
+        work[...] = jnp.where(all_rows < after, 0.0, old - change)
+        return carry
+
+    lax.fori_loop(0, size // PANEL, panel, 0)
 
 
 def six_terms(left, right):

time: 127 us -> 137 us (1.079)
  Pallas kernels: 44.3 us -> 62.3 us
  starting transfers between devices: 63.1 us -> 56.7 us
  waiting for transfers between devices: 16.5 us -> 15 us
    pallas_call x30, Pallas kernels: 39.7 us -> 57.7 us  [call(): pl.pallas_call(kernel, name=name, out_shape=outs, in_specs=[SMEM] * len(s...]
    ppermute x25, starting transfers between devices: 50.2 us -> 45.3 us  [swap_chips(): return lax.ppermute(value, ('row', 'col'), pairs)]
    ppermute x25, waiting for transfers between devices: 7.56 us -> 5.45 us  [swap_chips(): return lax.ppermute(value, ('row', 'col'), pairs)]
    ppermute x3, starting transfers between devices: 4.45 us -> 2.93 us  [from_chip(): return lax.ppermute(value, 'col', pairs)]
  transfers between devices with their start and end apart: 64 -> 64, of which waited for: 20 -> 16; matrix products, arithmetic and copies ran while one was open for 0% -> 0% of each run, Pallas kernels for 24% -> 34%
where the time goes in v9:
time: 137 us; the launch traced here: 136 us
  Pallas kernels  62.3 us (45%)
  starting transfers between devices  56.7 us (41%)
  waiting for transfers between devices  15 us (11%)
  between operations  2.31 us (2%)
    pallas_call x30, Pallas kernels, call(): pl.pallas_call(kernel, name=name, out_shape=outs, in_specs=[SMEM] * len(s...  57.7 us
    ppermute x25, starting transfers between devices, swap_chips(): return lax.ppermute(value, ('row', 'col'), pairs)  45.3 us
    ppermute x25, waiting for transfers between devices, swap_chips(): return lax.ppermute(value, ('row', 'col'), pairs)  5.45 us
    ppermute x3, starting transfers between devices, local(): lax.ppermute(summed, 'row', [(r, r ^ step) for r in range(num_rows)])  4.45 us
    ppermute x3, waiting for transfers between devices, from_chip(): return lax.ppermute(value, 'col', pairs)  3.96 us
    ppermute x1, starting transfers between devices, next_chips(): return lax.ppermute(value, ('row', 'col'), pairs)  3.08 us
    ppermute x3, waiting for transfers between devices, local(): lax.ppermute(summed, 'row', [(r, r ^ step) for r in range(num_rows)])  3.07 us
    pallas_call x1, Pallas kernels, local(): pl.pallas_call(functools.partial(load_kernel, total_blocks), name='load',...  3.01 us
  transfers between devices with their start and end apart: 64, of which 16 were waited for; matrix products, arithmetic and copies ran while one was open for 0% of the time, Pallas kernels for 34%

profile of v9, /device:TPU:0, one launch (start us, length us, event | category | flops | bytes accessed | tf_op | source)
XLA Modules:
  0.0 136.5 jit_solution(8303908660026201669)
XLA Ops:
  0.7 1.6 %cut.1 = (bf16[8,64,128]{2,1,0:T(8,128)(2,1)S(1)}, bf16[5,64,128]{2,1,0:T(8,128)(2,1)S(1)}, bf16[13,64,128]{2,1,0:T(8,128)(2,1)S(1)}, bf16[5,64,128]{2,1,0:T(8,128)(2,1)S(1)}, bf16[5,64,128]{2,1,0:T(8,128)(2,1)S(1)}) custom-call(s32[5]{0:T(128)S(1)} %stack.23.ints, s32[16]{0:T(128)} %sizes.3, bf16[64,2048]{1,0:T(8,128)(2,1)} %trial.1), custom_call_target="tpu_custom_call" | custom-call | tf_op jit(solution)/shard_map/cut/pallas_call | solution.py:546
  2.3 3.1 %collective-permute-start.1 = (bf16[5,64,128]{2,1,0:T(8,128)(2,1)S(1)}, bf16[5,64,128]{2,1,0:T(8,128)(2,1)S(1)}, u32[]{:S(2)}, u32[]{:S(2)}) collective-permute-start(bf16[5,64,128]{2,1,0:T(8,128)(2,1)S(1)} %get-tuple-element.105), channel_id=1, source_target_pairs={{0,4},{1,13},{2,6},{3,15},{4,8},{5,1},{6,10},{7,3},{8,12},{9,5},{1... | collective-permute-start | bytes 245768 | tf_op jit(solution)/shard_map/ppermute | solution.py:504
  5.4 1.6 %collective-permute-start.2 = (bf16[5,64,128]{2,1,0:T(8,128)(2,1)S(1)}, bf16[5,64,128]{2,1,0:T(8,128)(2,1)S(1)}, u32[]{:S(2)}, u32[]{:S(2)}) collective-permute-start(bf16[5,64,128]{2,1,0:T(8,128)(2,1)S(1)} %get-tuple-element.106), channel_id=1, source_target_pairs={{1,4},{4,1},{3,6},{6,3},{5,8},{8,5},{7,10},{10,7},{9,12},{12,9},{1... | collective-permute-start | bytes 245768 | tf_op jit(solution)/shard_map/ppermute | solution.py:496
  8.4 3.0 %load.1 = (bf16[8,9,128,128]{3,2,1,0:T(8,128)(2,1)S(1)}, bf16[8,9,128,128]{3,2,1,0:T(8,128)(2,1)S(1)}, s32[8,9]{1,0:T(8,128)S(4)}, f32[8,9]{1,0:T(8,128)S(4)}, s32[12]{0:T(128)S(4)}, /*index=5*/f32[2]{0:T(128)S(4)}) custom-call(s32[5]{0:T(128)S(1)} %stack.23.ints, f32[1]{0:T(128)S(6)} %copy.10.shift, f32[1]{0:T(128)S(6)} %copy.11.width, s32[16,9]{1,0:T(8,128)} %columns.1, ...), custom_call_target="tpu_custom_call" | custom-call | bytes 9437184 | tf_op jit(solution)/shard_map/load/pallas_call | solution.py:563
  12.0 2.2 %scaled.8 = (bf16[8,64,128]{2,1,0:T(8,128)(2,1)S(1)}, bf16[5,64,128]{2,1,0:T(8,128)(2,1)S(1)}, bf16[5,64,128]{2,1,0:T(8,128)(2,1)S(1)}) custom-call(s32[12]{0:T(128)S(4)} %get-tuple-element.99.ints, s32[8,9]{1,0:T(8,128)S(4)} %get-tuple-element.100.index, f32[8,9]{1,0:T(8,128)S(4)} %get-tuple-element.101.signs, f32[2]{0:T(128)S(4)} %get-tuple-element.102.scal, ...), custom_call_target="tpu_custom_call" | custom-call | flops 7247757312 | bytes 56623104 | tf_op jit(solution)/shard_map/scaled/pallas_call | solution.py:517
  14.2 1.8 %collective-permute-start.7 = (bf16[5,64,128]{2,1,0:T(8,128)(2,1)S(1)}, bf16[5,64,128]{2,1,0:T(8,128)(2,1)S(1)}, u32[]{:S(2)}, u32[]{:S(2)}) collective-permute-start(bf16[5,64,128]{2,1,0:T(8,128)(2,1)S(1)} %get-tuple-element.120), channel_id=1, source_target_pairs={{1,4},{4,1},{3,6},{6,3},{5,8},{8,5},{7,10},{10,7},{9,12},{12,9},{1... | collective-permute-start | bytes 245768 | tf_op jit(solution)/shard_map/ppermute | solution.py:496
  15.9 2.2 %scaled.9 = (bf16[8,64,128]{2,1,0:T(8,128)(2,1)S(1)}, bf16[5,64,128]{2,1,0:T(8,128)(2,1)S(1)}, bf16[5,64,128]{2,1,0:T(8,128)(2,1)S(1)}) custom-call(s32[12]{0:T(128)S(4)} %get-tuple-element.99.ints, s32[8,9]{1,0:T(8,128)S(4)} %get-tuple-element.100.index, f32[8,9]{1,0:T(8,128)S(4)} %get-tuple-element.101.signs, f32[2]{0:T(128)S(4)} %get-tuple-element.102.scal, ...), custom_call_target="tpu_custom_call" | custom-call | flops 7247757312 | bytes 56623104 | tf_op jit(solution)/shard_map/scaled/pallas_call | solution.py:517
  18.1 1.9 %collective-permute-start.3 = (bf16[5,64,128]{2,1,0:T(8,128)(2,1)S(1)}, bf16[5,64,128]{2,1,0:T(8,128)(2,1)S(1)}, u32[]{:S(2)}, u32[]{:S(2)}) collective-permute-start(bf16[5,64,128]{2,1,0:T(8,128)(2,1)S(1)} %get-tuple-element.113), channel_id=1, source_target_pairs={{1,4},{4,1},{3,6},{6,3},{5,8},{8,5},{7,10},{10,7},{9,12},{12,9},{1... | collective-permute-start | bytes 245768 | tf_op jit(solution)/shard_map/ppermute | solution.py:496
  21.6 1.8 %collective-permute-start.9 = (bf16[5,64,128]{2,1,0:T(8,128)(2,1)S(1)}, bf16[5,64,128]{2,1,0:T(8,128)(2,1)S(1)}, u32[]{:S(2)}, u32[]{:S(2)}) collective-permute-start(bf16[5,64,128]{2,1,0:T(8,128)(2,1)S(1)} %get-tuple-element.123), channel_id=1, source_target_pairs={{1,4},{4,1},{3,6},{6,3},{5,8},{8,5},{7,10},{10,7},{9,12},{12,9},{1... | collective-permute-start | bytes 245768 | tf_op jit(solution)/shard_map/ppermute | solution.py:496
  25.6 1.8 %collective-permute-start.5 = (bf16[5,64,128]{2,1,0:T(8,128)(2,1)S(1)}, bf16[5,64,128]{2,1,0:T(8,128)(2,1)S(1)}, u32[]{:S(2)}, u32[]{:S(2)}) collective-permute-start(bf16[5,64,128]{2,1,0:T(8,128)(2,1)S(1)} %get-tuple-element.116), channel_id=1, source_target_pairs={{1,4},{4,1},{3,6},{6,3},{5,8},{8,5},{7,10},{10,7},{9,12},{12,9},{1... | collective-permute-start | bytes 245768 | tf_op jit(solution)/shard_map/ppermute | solution.py:496
  27.4 1.6 %update.9 = (bf16[8,64,128]{2,1,0:T(8,128)(2,1)S(1)}, bf16[5,64,128]{2,1,0:T(8,128)(2,1)S(1)}, bf16[5,64,128]{2,1,0:T(8,128)(2,1)S(1)}) custom-call(s32[12]{0:T(128)S(4)} %get-tuple-element.99.ints, s32[8,9]{1,0:T(8,128)S(4)} %get-tuple-element.100.index, f32[8,9]{1,0:T(8,128)S(4)} %get-tuple-element.101.signs, ...), custom_call_target="tpu_custom_call" | custom-call | flops 3623878656 | bytes 28311552 | tf_op jit(solution)/shard_map/update/pallas_call | solution.py:517
  29.0 1.9 %collective-permute-start.11 = (bf16[5,64,128]{2,1,0:T(8,128)(2,1)S(1)}, bf16[5,64,128]{2,1,0:T(8,128)(2,1)S(1)}, u32[]{:S(2)}, u32[]{:S(2)}) collective-permute-start(bf16[5,64,128]{2,1,0:T(8,128)(2,1)S(1)} %get-tuple-element.126), channel_id=1, source_target_pairs={{1,4},{4,1},{3,6},{6,3},{5,8},{8,5},{7,10},{10,7},{9,12},{12,9},{1... | collective-permute-start | bytes 245768 | tf_op jit(solution)/shard_map/ppermute | solution.py:496
  31.3 1.6 %update.8 = (bf16[8,64,128]{2,1,0:T(8,128)(2,1)S(1)}, bf16[5,64,128]{2,1,0:T(8,128)(2,1)S(1)}, bf16[5,64,128]{2,1,0:T(8,128)(2,1)S(1)}) custom-call(s32[12]{0:T(128)S(4)} %get-tuple-element.99.ints, s32[8,9]{1,0:T(8,128)S(4)} %get-tuple-element.100.index, f32[8,9]{1,0:T(8,128)S(4)} %get-tuple-element.101.signs, ...), custom_call_target="tpu_custom_call" | custom-call | flops 3623878656 | bytes 28311552 | tf_op jit(solution)/shard_map/update/pallas_call | solution.py:517
  32.9 1.8 %collective-permute-start.13 = (bf16[5,64,128]{2,1,0:T(8,128)(2,1)S(1)}, bf16[5,64,128]{2,1,0:T(8,128)(2,1)S(1)}, u32[]{:S(2)}, u32[]{:S(2)}) collective-permute-start(bf16[5,64,128]{2,1,0:T(8,128)(2,1)S(1)} %get-tuple-element.130), channel_id=1, source_target_pairs={{1,4},{4,1},{3,6},{6,3},{5,8},{8,5},{7,10},{10,7},{9,12},{12,9},{1... | collective-permute-start | bytes 245768 | tf_op jit(solution)/shard_map/ppermute | solution.py:496
  34.7 2.2 %scaled.10 = (bf16[8,64,128]{2,1,0:T(8,128)(2,1)S(1)}, bf16[5,64,128]{2,1,0:T(8,128)(2,1)S(1)}, bf16[5,64,128]{2,1,0:T(8,128)(2,1)S(1)}) custom-call(s32[12]{0:T(128)S(4)} %get-tuple-element.99.ints, s32[8,9]{1,0:T(8,128)S(4)} %get-tuple-element.100.index, f32[8,9]{1,0:T(8,128)S(4)} %get-tuple-element.101.signs, f32[2]{0:T(128)S(4)} %get-tuple-element.102.scal, ...), custom_call_target="tpu_custom_call" | custom-call | flops 7247757312 | bytes 56623104 | tf_op jit(solution)/shard_map/scaled/pallas_call | solution.py:517
  36.9 1.9 %collective-permute-start.19 = (bf16[5,64,128]{2,1,0:T(8,128)(2,1)S(1)}, bf16[5,64,128]{2,1,0:T(8,128)(2,1)S(1)}, u32[]{:S(2)}, u32[]{:S(2)}) collective-permute-start(bf16[5,64,128]{2,1,0:T(8,128)(2,1)S(1)} %get-tuple-element.140), channel_id=1, source_target_pairs={{1,4},{4,1},{3,6},{6,3},{5,8},{8,5},{7,10},{10,7},{9,12},{12,9},{1... | collective-permute-start | bytes 245768 | tf_op jit(solution)/shard_map/ppermute | solution.py:496
  38.8 2.2 %scaled.11 = (bf16[8,64,128]{2,1,0:T(8,128)(2,1)S(1)}, bf16[5,64,128]{2,1,0:T(8,128)(2,1)S(1)}, bf16[5,64,128]{2,1,0:T(8,128)(2,1)S(1)}) custom-call(s32[12]{0:T(128)S(4)} %get-tuple-element.99.ints, s32[8,9]{1,0:T(8,128)S(4)} %get-tuple-element.100.index, f32[8,9]{1,0:T(8,128)S(4)} %get-tuple-element.101.signs, f32[2]{0:T(128)S(4)} %get-tuple-element.102.scal, ...), custom_call_target="tpu_custom_call" | custom-call | flops 7247757312 | bytes 56623104 | tf_op jit(solution)/shard_map/scaled/pallas_call | solution.py:517
  41.0 1.8 %collective-permute-start.15 = (bf16[5,64,128]{2,1,0:T(8,128)(2,1)S(1)}, bf16[5,64,128]{2,1,0:T(8,128)(2,1)S(1)}, u32[]{:S(2)}, u32[]{:S(2)}) collective-permute-start(bf16[5,64,128]{2,1,0:T(8,128)(2,1)S(1)} %get-tuple-element.133), channel_id=1, source_target_pairs={{1,4},{4,1},{3,6},{6,3},{5,8},{8,5},{7,10},{10,7},{9,12},{12,9},{1... | collective-permute-start | bytes 245768 | tf_op jit(solution)/shard_map/ppermute | solution.py:496
  44.4 1.9 %collective-permute-start.21 = (bf16[5,64,128]{2,1,0:T(8,128)(2,1)S(1)}, bf16[5,64,128]{2,1,0:T(8,128)(2,1)S(1)}, u32[]{:S(2)}, u32[]{:S(2)}) collective-permute-start(bf16[5,64,128]{2,1,0:T(8,128)(2,1)S(1)} %get-tuple-element.143), channel_id=1, source_target_pairs={{1,4},{4,1},{3,6},{6,3},{5,8},{8,5},{7,10},{10,7},{9,12},{12,9},{1... | collective-permute-start | bytes 245768 | tf_op jit(solution)/shard_map/ppermute | solution.py:496
  48.3 1.8 %collective-permute-start.17 = (bf16[5,64,128]{2,1,0:T(8,128)(2,1)S(1)}, bf16[5,64,128]{2,1,0:T(8,128)(2,1)S(1)}, u32[]{:S(2)}, u32[]{:S(2)}) collective-permute-start(bf16[5,64,128]{2,1,0:T(8,128)(2,1)S(1)} %get-tuple-element.136), channel_id=1, source_target_pairs={{1,4},{4,1},{3,6},{6,3},{5,8},{8,5},{7,10},{10,7},{9,12},{12,9},{1... | collective-permute-start | bytes 245768 | tf_op jit(solution)/shard_map/ppermute | solution.py:496
  50.1 1.6 %update.11 = (bf16[8,64,128]{2,1,0:T(8,128)(2,1)S(1)}, bf16[5,64,128]{2,1,0:T(8,128)(2,1)S(1)}, bf16[5,64,128]{2,1,0:T(8,128)(2,1)S(1)}) custom-call(s32[12]{0:T(128)S(4)} %get-tuple-element.99.ints, s32[8,9]{1,0:T(8,128)S(4)} %get-tuple-element.100.index, f32[8,9]{1,0:T(8,128)S(4)} %get-tuple-element.101.signs, ...), custom_call_target="tpu_custom_call" | custom-call | flops 3623878656 | bytes 28311552 | tf_op jit(solution)/shard_map/update/pallas_call | solution.py:517
  51.7 1.9 %collective-permute-start.23 = (bf16[5,64,128]{2,1,0:T(8,128)(2,1)S(1)}, bf16[5,64,128]{2,1,0:T(8,128)(2,1)S(1)}, u32[]{:S(2)}, u32[]{:S(2)}) collective-permute-start(bf16[5,64,128]{2,1,0:T(8,128)(2,1)S(1)} %get-tuple-element.146), channel_id=1, source_target_pairs={{1,4},{4,1},{3,6},{6,3},{5,8},{8,5},{7,10},{10,7},{9,12},{12,9},{1... | collective-permute-start | bytes 245768 | tf_op jit(solution)/shard_map/ppermute | solution.py:496
  54.1 1.6 %update.10 = (bf16[8,64,128]{2,1,0:T(8,128)(2,1)S(1)}, bf16[5,64,128]{2,1,0:T(8,128)(2,1)S(1)}, bf16[5,64,128]{2,1,0:T(8,128)(2,1)S(1)}) custom-call(s32[12]{0:T(128)S(4)} %get-tuple-element.99.ints, s32[8,9]{1,0:T(8,128)S(4)} %get-tuple-element.100.index, f32[8,9]{1,0:T(8,128)S(4)} %get-tuple-element.101.signs, ...), custom_call_target="tpu_custom_call" | custom-call | flops 3623878656 | bytes 28311552 | tf_op jit(solution)/shard_map/update/pallas_call | solution.py:517
  55.7 1.8 %collective-permute-start.25 = (bf16[5,64,128]{2,1,0:T(8,128)(2,1)S(1)}, bf16[5,64,128]{2,1,0:T(8,128)(2,1)S(1)}, u32[]{:S(2)}, u32[]{:S(2)}) collective-permute-start(bf16[5,64,128]{2,1,0:T(8,128)(2,1)S(1)} %get-tuple-element.150), channel_id=1, source_target_pairs={{1,4},{4,1},{3,6},{6,3},{5,8},{8,5},{7,10},{10,7},{9,12},{12,9},{1... | collective-permute-start | bytes 245768 | tf_op jit(solution)/shard_map/ppermute | solution.py:496
  57.5 2.2 %scaled.12 = (bf16[8,64,128]{2,1,0:T(8,128)(2,1)S(1)}, bf16[5,64,128]{2,1,0:T(8,128)(2,1)S(1)}, bf16[5,64,128]{2,1,0:T(8,128)(2,1)S(1)}) custom-call(s32[12]{0:T(128)S(4)} %get-tuple-element.99.ints, s32[8,9]{1,0:T(8,128)S(4)} %get-tuple-element.100.index, f32[8,9]{1,0:T(8,128)S(4)} %get-tuple-element.101.signs, f32[2]{0:T(128)S(4)} %get-tuple-element.102.scal, ...), custom_call_target="tpu_custom_call" | custom-call | flops 7247757312 | bytes 56623104 | tf_op jit(solution)/shard_map/scaled/pallas_call | solution.py:517
  59.7 1.9 %collective-permute-start.31 = (bf16[5,64,128]{2,1,0:T(8,128)(2,1)S(1)}, bf16[5,64,128]{2,1,0:T(8,128)(2,1)S(1)}, u32[]{:S(2)}, u32[]{:S(2)}) collective-permute-start(bf16[5,64,128]{2,1,0:T(8,128)(2,1)S(1)} %get-tuple-element.160), channel_id=1, source_target_pairs={{1,4},{4,1},{3,6},{6,3},{5,8},{8,5},{7,10},{10,7},{9,12},{12,9},{1... | collective-permute-start | bytes 245768 | tf_op jit(solution)/shard_map/ppermute | solution.py:496
  61.6 2.2 %scaled.13 = (bf16[8,64,128]{2,1,0:T(8,128)(2,1)S(1)}, bf16[5,64,128]{2,1,0:T(8,128)(2,1)S(1)}, bf16[5,64,128]{2,1,0:T(8,128)(2,1)S(1)}) custom-call(s32[12]{0:T(128)S(4)} %get-tuple-element.99.ints, s32[8,9]{1,0:T(8,128)S(4)} %get-tuple-element.100.index, f32[8,9]{1,0:T(8,128)S(4)} %get-tuple-element.101.signs, f32[2]{0:T(128)S(4)} %get-tuple-element.102.scal, ...), custom_call_target="tpu_custom_call" | custom-call | flops 7247757312 | bytes 56623104 | tf_op jit(solution)/shard_map/scaled/pallas_call | solution.py:517
  63.8 1.8 %collective-permute-start.27 = (bf16[5,64,128]{2,1,0:T(8,128)(2,1)S(1)}, bf16[5,64,128]{2,1,0:T(8,128)(2,1)S(1)}, u32[]{:S(2)}, u32[]{:S(2)}) collective-permute-start(bf16[5,64,128]{2,1,0:T(8,128)(2,1)S(1)} %get-tuple-element.153), channel_id=1, source_target_pairs={{1,4},{4,1},{3,6},{6,3},{5,8},{8,5},{7,10},{10,7},{9,12},{12,9},{1... | collective-permute-start | bytes 245768 | tf_op jit(solution)/shard_map/ppermute | solution.py:496
  67.1 1.9 %collective-permute-start.33 = (bf16[5,64,128]{2,1,0:T(8,128)(2,1)S(1)}, bf16[5,64,128]{2,1,0:T(8,128)(2,1)S(1)}, u32[]{:S(2)}, u32[]{:S(2)}) collective-permute-start(bf16[5,64,128]{2,1,0:T(8,128)(2,1)S(1)} %get-tuple-element.163), channel_id=1, source_target_pairs={{1,4},{4,1},{3,6},{6,3},{5,8},{8,5},{7,10},{10,7},{9,12},{12,9},{1... | collective-permute-start | bytes 245768 | tf_op jit(solution)/shard_map/ppermute | solution.py:496
  71.1 1.8 %collective-permute-start.29 = (bf16[5,64,128]{2,1,0:T(8,128)(2,1)S(1)}, bf16[5,64,128]{2,1,0:T(8,128)(2,1)S(1)}, u32[]{:S(2)}, u32[]{:S(2)}) collective-permute-start(bf16[5,64,128]{2,1,0:T(8,128)(2,1)S(1)} %get-tuple-element.156), channel_id=1, source_target_pairs={{1,4},{4,1},{3,6},{6,3},{5,8},{8,5},{7,10},{10,7},{9,12},{12,9},{1... | collective-permute-start | bytes 245768 | tf_op jit(solution)/shard_map/ppermute | solution.py:496
  72.9 1.6 %update.13 = (bf16[8,64,128]{2,1,0:T(8,128)(2,1)S(1)}, bf16[5,64,128]{2,1,0:T(8,128)(2,1)S(1)}, bf16[5,64,128]{2,1,0:T(8,128)(2,1)S(1)}) custom-call(s32[12]{0:T(128)S(4)} %get-tuple-element.99.ints, s32[8,9]{1,0:T(8,128)S(4)} %get-tuple-element.100.index, f32[8,9]{1,0:T(8,128)S(4)} %get-tuple-element.101.signs, ...), custom_call_target="tpu_custom_call" | custom-call | flops 3623878656 | bytes 28311552 | tf_op jit(solution)/shard_map/update/pallas_call | solution.py:517
  74.5 1.9 %collective-permute-start.35 = (bf16[5,64,128]{2,1,0:T(8,128)(2,1)S(1)}, bf16[5,64,128]{2,1,0:T(8,128)(2,1)S(1)}, u32[]{:S(2)}, u32[]{:S(2)}) collective-permute-start(bf16[5,64,128]{2,1,0:T(8,128)(2,1)S(1)} %get-tuple-element.166), channel_id=1, source_target_pairs={{1,4},{4,1},{3,6},{6,3},{5,8},{8,5},{7,10},{10,7},{9,12},{12,9},{1... | collective-permute-start | bytes 245768 | tf_op jit(solution)/shard_map/ppermute | solution.py:496
  76.8 1.6 %update.12 = (bf16[8,64,128]{2,1,0:T(8,128)(2,1)S(1)}, bf16[5,64,128]{2,1,0:T(8,128)(2,1)S(1)}, bf16[5,64,128]{2,1,0:T(8,128)(2,1)S(1)}) custom-call(s32[12]{0:T(128)S(4)} %get-tuple-element.99.ints, s32[8,9]{1,0:T(8,128)S(4)} %get-tuple-element.100.index, f32[8,9]{1,0:T(8,128)S(4)} %get-tuple-element.101.signs, ...), custom_call_target="tpu_custom_call" | custom-call | flops 3623878656 | bytes 28311552 | tf_op jit(solution)/shard_map/update/pallas_call | solution.py:517
  78.4 1.8 %collective-permute-start.37 = (bf16[5,64,128]{2,1,0:T(8,128)(2,1)S(1)}, bf16[5,64,128]{2,1,0:T(8,128)(2,1)S(1)}, u32[]{:S(2)}, u32[]{:S(2)}) collective-permute-start(bf16[5,64,128]{2,1,0:T(8,128)(2,1)S(1)} %get-tuple-element.170), channel_id=1, source_target_pairs={{1,4},{4,1},{3,6},{6,3},{5,8},{8,5},{7,10},{10,7},{9,12},{12,9},{1... | collective-permute-start | bytes 245768 | tf_op jit(solution)/shard_map/ppermute | solution.py:496
  80.2 2.2 %scaled.14 = (bf16[8,64,128]{2,1,0:T(8,128)(2,1)S(1)}, bf16[5,64,128]{2,1,0:T(8,128)(2,1)S(1)}, bf16[5,64,128]{2,1,0:T(8,128)(2,1)S(1)}) custom-call(s32[12]{0:T(128)S(4)} %get-tuple-element.99.ints, s32[8,9]{1,0:T(8,128)S(4)} %get-tuple-element.100.index, f32[8,9]{1,0:T(8,128)S(4)} %get-tuple-element.101.signs, f32[2]{0:T(128)S(4)} %get-tuple-element.102.scal, ...), custom_call_target="tpu_custom_call" | custom-call | flops 7247757312 | bytes 56623104 | tf_op jit(solution)/shard_map/scaled/pallas_call | solution.py:517
  82.4 1.9 %collective-permute-start.43 = (bf16[5,64,128]{2,1,0:T(8,128)(2,1)S(1)}, bf16[5,64,128]{2,1,0:T(8,128)(2,1)S(1)}, u32[]{:S(2)}, u32[]{:S(2)}) collective-permute-start(bf16[5,64,128]{2,1,0:T(8,128)(2,1)S(1)} %get-tuple-element.180), channel_id=1, source_target_pairs={{1,4},{4,1},{3,6},{6,3},{5,8},{8,5},{7,10},{10,7},{9,12},{12,9},{1... | collective-permute-start | bytes 245768 | tf_op jit(solution)/shard_map/ppermute | solution.py:496
  84.3 2.2 %scaled.15 = (bf16[8,64,128]{2,1,0:T(8,128)(2,1)S(1)}, bf16[5,64,128]{2,1,0:T(8,128)(2,1)S(1)}, bf16[5,64,128]{2,1,0:T(8,128)(2,1)S(1)}) custom-call(s32[12]{0:T(128)S(4)} %get-tuple-element.99.ints, s32[8,9]{1,0:T(8,128)S(4)} %get-tuple-element.100.index, f32[8,9]{1,0:T(8,128)S(4)} %get-tuple-element.101.signs, f32[2]{0:T(128)S(4)} %get-tuple-element.102.scal, ...), custom_call_target="tpu_custom_call" | custom-call | flops 7247757312 | bytes 56623104 | tf_op jit(solution)/shard_map/scaled/pallas_call | solution.py:517
  86.5 1.8 %collective-permute-start.39 = (bf16[5,64,128]{2,1,0:T(8,128)(2,1)S(1)}, bf16[5,64,128]{2,1,0:T(8,128)(2,1)S(1)}, u32[]{:S(2)}, u32[]{:S(2)}) collective-permute-start(bf16[5,64,128]{2,1,0:T(8,128)(2,1)S(1)} %get-tuple-element.173), channel_id=1, source_target_pairs={{1,4},{4,1},{3,6},{6,3},{5,8},{8,5},{7,10},{10,7},{9,12},{12,9},{1... | collective-permute-start | bytes 245768 | tf_op jit(solution)/shard_map/ppermute | solution.py:496
  89.9 1.9 %collective-permute-start.45 = (bf16[5,64,128]{2,1,0:T(8,128)(2,1)S(1)}, bf16[5,64,128]{2,1,0:T(8,128)(2,1)S(1)}, u32[]{:S(2)}, u32[]{:S(2)}) collective-permute-start(bf16[5,64,128]{2,1,0:T(8,128)(2,1)S(1)} %get-tuple-element.183), channel_id=1, source_target_pairs={{1,4},{4,1},{3,6},{6,3},{5,8},{8,5},{7,10},{10,7},{9,12},{12,9},{1... | collective-permute-start | bytes 245768 | tf_op jit(solution)/shard_map/ppermute | solution.py:496
  93.8 1.8 %collective-permute-start.41 = (bf16[5,64,128]{2,1,0:T(8,128)(2,1)S(1)}, bf16[5,64,128]{2,1,0:T(8,128)(2,1)S(1)}, u32[]{:S(2)}, u32[]{:S(2)}) collective-permute-start(bf16[5,64,128]{2,1,0:T(8,128)(2,1)S(1)} %get-tuple-element.176), channel_id=1, source_target_pairs={{1,4},{4,1},{3,6},{6,3},{5,8},{8,5},{7,10},{10,7},{9,12},{12,9},{1... | collective-permute-start | bytes 245768 | tf_op jit(solution)/shard_map/ppermute | solution.py:496
  95.6 1.6 %update.15 = (bf16[8,64,128]{2,1,0:T(8,128)(2,1)S(1)}, bf16[5,64,128]{2,1,0:T(8,128)(2,1)S(1)}, bf16[5,64,128]{2,1,0:T(8,128)(2,1)S(1)}) custom-call(s32[12]{0:T(128)S(4)} %get-tuple-element.99.ints, s32[8,9]{1,0:T(8,128)S(4)} %get-tuple-element.100.index, f32[8,9]{1,0:T(8,128)S(4)} %get-tuple-element.101.signs, ...), custom_call_target="tpu_custom_call" | custom-call | flops 3623878656 | bytes 28311552 | tf_op jit(solution)/shard_map/update/pallas_call | solution.py:517
  97.2 1.8 %collective-permute-start.47 = (bf16[5,64,128]{2,1,0:T(8,128)(2,1)S(1)}, bf16[5,64,128]{2,1,0:T(8,128)(2,1)S(1)}, u32[]{:S(2)}, u32[]{:S(2)}) collective-permute-start(bf16[5,64,128]{2,1,0:T(8,128)(2,1)S(1)} %get-tuple-element.186), channel_id=1, source_target_pairs={{1,4},{4,1},{3,6},{6,3},{5,8},{8,5},{7,10},{10,7},{9,12},{12,9},{1... | collective-permute-start | bytes 245768 | tf_op jit(solution)/shard_map/ppermute | solution.py:496
  100.6 1.8 %update.14 = (bf16[8,64,128]{2,1,0:T(8,128)(2,1)S(1)}, bf16[5,64,128]{2,1,0:T(8,128)(2,1)S(1)}, bf16[5,64,128]{2,1,0:T(8,128)(2,1)S(1)}) custom-call(s32[12]{0:T(128)S(4)} %get-tuple-element.99.ints, s32[8,9]{1,0:T(8,128)S(4)} %get-tuple-element.100.index, f32[8,9]{1,0:T(8,128)S(4)} %get-tuple-element.101.signs, ...), custom_call_target="tpu_custom_call" | custom-call | flops 3623878656 | bytes 28311552 | tf_op jit(solution)/shard_map/update/pallas_call | solution.py:517
  106.5 1.6 %collective-permute-done.50.inter = bf16[5,64,128]{2,1,0:T(8,128)(2,1)S(1)} collective-permute-done((bf16[5,64,128]{2,1,0:T(8,128)(2,1)S(1)}, bf16[5,64,128]{2,1,0:T(8,128)(2,1)S(1)}, u32[]{:S(2)}, u32[]{:S(2)}) %collective-permute-start.50) | collective-permute-done | bytes 81952 | tf_op jit(solution)/shard_map/ppermute | solution.py:496
  111.8 2.0 %collective-permute-start.56 = (bf16[208,128]{1,0:T(8,128)(2,1)S(1)}, bf16[208,128]{1,0:T(8,128)(2,1)S(1)}, u32[]{:S(2)}, u32[]{:S(2)}) collective-permute-start(bf16[208,128]{1,0:T(8,128)(2,1)S(1)} %add.9.refs_0_), channel_id=1, source_target_pairs={{0,12},{4,8},{8,4},{12,0},{1,13},{5,9},{9,5},{13,1},{2,14},{6,10},... | collective-permute-start | bytes 159752 | tf_op jit(solution)/shard_map/ppermute | solution.py:669
  113.8 2.5 %collective-permute-start.54 = (bf16[208,128]{1,0:T(8,128)(2,1)S(1)}, bf16[208,128]{1,0:T(8,128)(2,1)S(1)}, u32[]{:S(2)}, u32[]{:S(2)}) collective-permute-start(bf16[208,128]{1,0:T(8,128)(2,1)S(1)} %add.9.refs_0_), channel_id=1, source_target_pairs={{0,4},{4,0},{8,12},{12,8},{1,5},{5,1},{9,13},{13,9},{2,6},{6,2},{1... | collective-permute-start | bytes 159752 | tf_op jit(solution)/shard_map/ppermute | solution.py:669
  120.9 3.3 %collective-permute-done.57.refs_1_ = bf16[208,128]{1,0:T(8,128)(2,1)S(1)} collective-permute-done((bf16[208,128]{1,0:T(8,128)(2,1)S(1)}, bf16[208,128]{1,0:T(8,128)(2,1)S(1)}, u32[]{:S(2)}, u32[]{:S(2)}) %collective-permute-start.57) | collective-permute-done | bytes 53280 | tf_op jit(solution)/shard_map/ppermute | solution.py:508
  125.5 11.0 %finish.1 = (bf16[64,2048]{1,0:T(8,128)(2,1)}, f32[64,256]{1,0:T(8,128)}) custom-call(s32[12]{0:T(128)S(4)} %get-tuple-element.99.ints, bf16[208,128]{1,0:T(8,128)(2,1)S(1)} %sum.1.refs_0_, bf16[208,128]{1,0:T(8,128)(2,1)S(1)} %collective-permute-done.57.refs_1_, bf16[208,128]{1,0:T(8,128)(2,1)S(1)} %collective-permute-done.58.refs_2_, ...), custom_call_target="tpu_custom_call" | custom-call | flops 36238786560 | bytes 283115520 | tf_op jit(solution)/shard_map/finish/pallas_call | solution.py:517
  (116 shorter events, 31.9 us)
Async XLA Ops:
  2.3 9.1 %collective-permute-start.1 = (bf16[5,64,128]{2,1,0:T(8,128)(2,1)S(1)}, bf16[5,64,128]{2,1,0:T(8,128)(2,1)S(1)}, u32[]{:S(2)}, u32[]{:S(2)}) collective-permute-start(bf16[5,64,128]{2,1,0:T(8,128)(2,1)S(1)} %get-tuple-element.105), channel_id=1, source_target_pairs={{0,4},{1,13},{2,6},{3,15},{4,8},{5,1},{6,10},{7,3},{8,12},{9,5},{1... | collective-permute-start | bytes 245768 | tf_op jit(solution)/shard_map/ppermute | solution.py:504
  5.4 6.5 %collective-permute-start.2 = (bf16[5,64,128]{2,1,0:T(8,128)(2,1)S(1)}, bf16[5,64,128]{2,1,0:T(8,128)(2,1)S(1)}, u32[]{:S(2)}, u32[]{:S(2)}) collective-permute-start(bf16[5,64,128]{2,1,0:T(8,128)(2,1)S(1)} %get-tuple-element.106), channel_id=1, source_target_pairs={{1,4},{4,1},{3,6},{6,3},{5,8},{8,5},{7,10},{10,7},{9,12},{12,9},{1... | collective-permute-start | bytes 245768 | tf_op jit(solution)/shard_map/ppermute | solution.py:496
  7.0 4.9 %collective-permute-start = (bf16[13,64,128]{2,1,0:T(8,128)(2,1)S(1)}, bf16[13,64,128]{2,1,0:T(8,128)(2,1)S(1)}, u32[]{:S(2)}, u32[]{:S(2)}) collective-permute-start(bf16[13,64,128]{2,1,0:T(8,128)(2,1)S(1)} %get-tuple-element.103), channel_id=1, source_target_pairs={{0,1},{1,0},{2,3},{3,2},{4,5},{5,4},{6,7},{7,6},{8,9},{9,8},{10,11... | collective-permute-start | bytes 638984 | tf_op jit(solution)/shard_map/ppermute | solution.py:487
  14.2 5.9 %collective-permute-start.7 = (bf16[5,64,128]{2,1,0:T(8,128)(2,1)S(1)}, bf16[5,64,128]{2,1,0:T(8,128)(2,1)S(1)}, u32[]{:S(2)}, u32[]{:S(2)}) collective-permute-start(bf16[5,64,128]{2,1,0:T(8,128)(2,1)S(1)} %get-tuple-element.120), channel_id=1, source_target_pairs={{1,4},{4,1},{3,6},{6,3},{5,8},{8,5},{7,10},{10,7},{9,12},{12,9},{1... | collective-permute-start | bytes 245768 | tf_op jit(solution)/shard_map/ppermute | solution.py:496
  15.9 4.1 %collective-permute-start.8 = (bf16[5,64,128]{2,1,0:T(8,128)(2,1)S(1)}, bf16[5,64,128]{2,1,0:T(8,128)(2,1)S(1)}, u32[]{:S(2)}, u32[]{:S(2)}) collective-permute-start(bf16[5,64,128]{2,1,0:T(8,128)(2,1)S(1)} %get-tuple-element.121), channel_id=1, source_target_pairs={{0,1},{1,0},{2,3},{3,2},{4,5},{5,4},{6,7},{7,6},{8,9},{9,8},{10,11... | collective-permute-start | bytes 245768 | tf_op jit(solution)/shard_map/ppermute | solution.py:487
  18.1 5.9 %collective-permute-start.3 = (bf16[5,64,128]{2,1,0:T(8,128)(2,1)S(1)}, bf16[5,64,128]{2,1,0:T(8,128)(2,1)S(1)}, u32[]{:S(2)}, u32[]{:S(2)}) collective-permute-start(bf16[5,64,128]{2,1,0:T(8,128)(2,1)S(1)} %get-tuple-element.113), channel_id=1, source_target_pairs={{1,4},{4,1},{3,6},{6,3},{5,8},{8,5},{7,10},{10,7},{9,12},{12,9},{1... | collective-permute-start | bytes 245768 | tf_op jit(solution)/shard_map/ppermute | solution.py:496
  20.0 4.0 %collective-permute-start.4 = (bf16[5,64,128]{2,1,0:T(8,128)(2,1)S(1)}, bf16[5,64,128]{2,1,0:T(8,128)(2,1)S(1)}, u32[]{:S(2)}, u32[]{:S(2)}) collective-permute-start(bf16[5,64,128]{2,1,0:T(8,128)(2,1)S(1)} %get-tuple-element.114), channel_id=1, source_target_pairs={{0,1},{1,0},{2,3},{3,2},{4,5},{5,4},{6,7},{7,6},{8,9},{9,8},{10,11... | collective-permute-start | bytes 245768 | tf_op jit(solution)/shard_map/ppermute | solution.py:487
  21.6 5.7 %collective-permute-start.9 = (bf16[5,64,128]{2,1,0:T(8,128)(2,1)S(1)}, bf16[5,64,128]{2,1,0:T(8,128)(2,1)S(1)}, u32[]{:S(2)}, u32[]{:S(2)}) collective-permute-start(bf16[5,64,128]{2,1,0:T(8,128)(2,1)S(1)} %get-tuple-element.123), channel_id=1, source_target_pairs={{1,4},{4,1},{3,6},{6,3},{5,8},{8,5},{7,10},{10,7},{9,12},{12,9},{1... | collective-permute-start | bytes 245768 | tf_op jit(solution)/shard_map/ppermute | solution.py:496
  23.4 4.0 %collective-permute-start.10 = (bf16[5,64,128]{2,1,0:T(8,128)(2,1)S(1)}, bf16[5,64,128]{2,1,0:T(8,128)(2,1)S(1)}, u32[]{:S(2)}, u32[]{:S(2)}) collective-permute-start(bf16[5,64,128]{2,1,0:T(8,128)(2,1)S(1)} %get-tuple-element.124), channel_id=1, source_target_pairs={{0,1},{1,0},{2,3},{3,2},{4,5},{5,4},{6,7},{7,6},{8,9},{9,8},{10,11... | collective-permute-start | bytes 245768 | tf_op jit(solution)/shard_map/ppermute | solution.py:487
  25.6 5.7 %collective-permute-start.5 = (bf16[5,64,128]{2,1,0:T(8,128)(2,1)S(1)}, bf16[5,64,128]{2,1,0:T(8,128)(2,1)S(1)}, u32[]{:S(2)}, u32[]{:S(2)}) collective-permute-start(bf16[5,64,128]{2,1,0:T(8,128)(2,1)S(1)} %get-tuple-element.116), channel_id=1, source_target_pairs={{1,4},{4,1},{3,6},{6,3},{5,8},{8,5},{7,10},{10,7},{9,12},{12,9},{1... | collective-permute-start | bytes 245768 | tf_op jit(solution)/shard_map/ppermute | solution.py:496
  29.0 5.7 %collective-permute-start.11 = (bf16[5,64,128]{2,1,0:T(8,128)(2,1)S(1)}, bf16[5,64,128]{2,1,0:T(8,128)(2,1)S(1)}, u32[]{:S(2)}, u32[]{:S(2)}) collective-permute-start(bf16[5,64,128]{2,1,0:T(8,128)(2,1)S(1)} %get-tuple-element.126), channel_id=1, source_target_pairs={{1,4},{4,1},{3,6},{6,3},{5,8},{8,5},{7,10},{10,7},{9,12},{12,9},{1... | collective-permute-start | bytes 245768 | tf_op jit(solution)/shard_map/ppermute | solution.py:496
  32.9 5.9 %collective-permute-start.13 = (bf16[5,64,128]{2,1,0:T(8,128)(2,1)S(1)}, bf16[5,64,128]{2,1,0:T(8,128)(2,1)S(1)}, u32[]{:S(2)}, u32[]{:S(2)}) collective-permute-start(bf16[5,64,128]{2,1,0:T(8,128)(2,1)S(1)} %get-tuple-element.130), channel_id=1, source_target_pairs={{1,4},{4,1},{3,6},{6,3},{5,8},{8,5},{7,10},{10,7},{9,12},{12,9},{1... | collective-permute-start | bytes 245768 | tf_op jit(solution)/shard_map/ppermute | solution.py:496
  34.7 4.1 %collective-permute-start.14 = (bf16[5,64,128]{2,1,0:T(8,128)(2,1)S(1)}, bf16[5,64,128]{2,1,0:T(8,128)(2,1)S(1)}, u32[]{:S(2)}, u32[]{:S(2)}) collective-permute-start(bf16[5,64,128]{2,1,0:T(8,128)(2,1)S(1)} %get-tuple-element.131), channel_id=1, source_target_pairs={{0,1},{1,0},{2,3},{3,2},{4,5},{5,4},{6,7},{7,6},{8,9},{9,8},{10,11... | collective-permute-start | bytes 245768 | tf_op jit(solution)/shard_map/ppermute | solution.py:487
  36.9 5.9 %collective-permute-start.19 = (bf16[5,64,128]{2,1,0:T(8,128)(2,1)S(1)}, bf16[5,64,128]{2,1,0:T(8,128)(2,1)S(1)}, u32[]{:S(2)}, u32[]{:S(2)}) collective-permute-start(bf16[5,64,128]{2,1,0:T(8,128)(2,1)S(1)} %get-tuple-element.140), channel_id=1, source_target_pairs={{1,4},{4,1},{3,6},{6,3},{5,8},{8,5},{7,10},{10,7},{9,12},{12,9},{1... | collective-permute-start | bytes 245768 | tf_op jit(solution)/shard_map/ppermute | solution.py:496
  41.0 5.7 %collective-permute-start.15 = (bf16[5,64,128]{2,1,0:T(8,128)(2,1)S(1)}, bf16[5,64,128]{2,1,0:T(8,128)(2,1)S(1)}, u32[]{:S(2)}, u32[]{:S(2)}) collective-permute-start(bf16[5,64,128]{2,1,0:T(8,128)(2,1)S(1)} %get-tuple-element.133), channel_id=1, source_target_pairs={{1,4},{4,1},{3,6},{6,3},{5,8},{8,5},{7,10},{10,7},{9,12},{12,9},{1... | collective-permute-start | bytes 245768 | tf_op jit(solution)/shard_map/ppermute | solution.py:496
  44.4 5.7 %collective-permute-start.21 = (bf16[5,64,128]{2,1,0:T(8,128)(2,1)S(1)}, bf16[5,64,128]{2,1,0:T(8,128)(2,1)S(1)}, u32[]{:S(2)}, u32[]{:S(2)}) collective-permute-start(bf16[5,64,128]{2,1,0:T(8,128)(2,1)S(1)} %get-tuple-element.143), channel_id=1, source_target_pairs={{1,4},{4,1},{3,6},{6,3},{5,8},{8,5},{7,10},{10,7},{9,12},{12,9},{1... | collective-permute-start | bytes 245768 | tf_op jit(solution)/shard_map/ppermute | solution.py:496
  48.3 5.7 %collective-permute-start.17 = (bf16[5,64,128]{2,1,0:T(8,128)(2,1)S(1)}, bf16[5,64,128]{2,1,0:T(8,128)(2,1)S(1)}, u32[]{:S(2)}, u32[]{:S(2)}) collective-permute-start(bf16[5,64,128]{2,1,0:T(8,128)(2,1)S(1)} %get-tuple-element.136), channel_id=1, source_target_pairs={{1,4},{4,1},{3,6},{6,3},{5,8},{8,5},{7,10},{10,7},{9,12},{12,9},{1... | collective-permute-start | bytes 245768 | tf_op jit(solution)/shard_map/ppermute | solution.py:496
  51.7 5.7 %collective-permute-start.23 = (bf16[5,64,128]{2,1,0:T(8,128)(2,1)S(1)}, bf16[5,64,128]{2,1,0:T(8,128)(2,1)S(1)}, u32[]{:S(2)}, u32[]{:S(2)}) collective-permute-start(bf16[5,64,128]{2,1,0:T(8,128)(2,1)S(1)} %get-tuple-element.146), channel_id=1, source_target_pairs={{1,4},{4,1},{3,6},{6,3},{5,8},{8,5},{7,10},{10,7},{9,12},{12,9},{1... | collective-permute-start | bytes 245768 | tf_op jit(solution)/shard_map/ppermute | solution.py:496
  55.7 5.9 %collective-permute-start.25 = (bf16[5,64,128]{2,1,0:T(8,128)(2,1)S(1)}, bf16[5,64,128]{2,1,0:T(8,128)(2,1)S(1)}, u32[]{:S(2)}, u32[]{:S(2)}) collective-permute-start(bf16[5,64,128]{2,1,0:T(8,128)(2,1)S(1)} %get-tuple-element.150), channel_id=1, source_target_pairs={{1,4},{4,1},{3,6},{6,3},{5,8},{8,5},{7,10},{10,7},{9,12},{12,9},{1... | collective-permute-start | bytes 245768 | tf_op jit(solution)/shard_map/ppermute | solution.py:496
  57.4 4.1 %collective-permute-start.26 = (bf16[5,64,128]{2,1,0:T(8,128)(2,1)S(1)}, bf16[5,64,128]{2,1,0:T(8,128)(2,1)S(1)}, u32[]{:S(2)}, u32[]{:S(2)}) collective-permute-start(bf16[5,64,128]{2,1,0:T(8,128)(2,1)S(1)} %get-tuple-element.151), channel_id=1, source_target_pairs={{0,1},{1,0},{2,3},{3,2},{4,5},{5,4},{6,7},{7,6},{8,9},{9,8},{10,11... | collective-permute-start | bytes 245768 | tf_op jit(solution)/shard_map/ppermute | solution.py:487
  59.7 5.9 %collective-permute-start.31 = (bf16[5,64,128]{2,1,0:T(8,128)(2,1)S(1)}, bf16[5,64,128]{2,1,0:T(8,128)(2,1)S(1)}, u32[]{:S(2)}, u32[]{:S(2)}) collective-permute-start(bf16[5,64,128]{2,1,0:T(8,128)(2,1)S(1)} %get-tuple-element.160), channel_id=1, source_target_pairs={{1,4},{4,1},{3,6},{6,3},{5,8},{8,5},{7,10},{10,7},{9,12},{12,9},{1... | collective-permute-start | bytes 245768 | tf_op jit(solution)/shard_map/ppermute | solution.py:496
  61.5 4.0 %collective-permute-start.32 = (bf16[5,64,128]{2,1,0:T(8,128)(2,1)S(1)}, bf16[5,64,128]{2,1,0:T(8,128)(2,1)S(1)}, u32[]{:S(2)}, u32[]{:S(2)}) collective-permute-start(bf16[5,64,128]{2,1,0:T(8,128)(2,1)S(1)} %get-tuple-element.161), channel_id=1, source_target_pairs={{0,1},{1,0},{2,3},{3,2},{4,5},{5,4},{6,7},{7,6},{8,9},{9,8},{10,11... | collective-permute-start | bytes 245768 | tf_op jit(solution)/shard_map/ppermute | solution.py:487
  63.8 5.7 %collective-permute-start.27 = (bf16[5,64,128]{2,1,0:T(8,128)(2,1)S(1)}, bf16[5,64,128]{2,1,0:T(8,128)(2,1)S(1)}, u32[]{:S(2)}, u32[]{:S(2)}) collective-permute-start(bf16[5,64,128]{2,1,0:T(8,128)(2,1)S(1)} %get-tuple-element.153), channel_id=1, source_target_pairs={{1,4},{4,1},{3,6},{6,3},{5,8},{8,5},{7,10},{10,7},{9,12},{12,9},{1... | collective-permute-start | bytes 245768 | tf_op jit(solution)/shard_map/ppermute | solution.py:496
  67.1 5.7 %collective-permute-start.33 = (bf16[5,64,128]{2,1,0:T(8,128)(2,1)S(1)}, bf16[5,64,128]{2,1,0:T(8,128)(2,1)S(1)}, u32[]{:S(2)}, u32[]{:S(2)}) collective-permute-start(bf16[5,64,128]{2,1,0:T(8,128)(2,1)S(1)} %get-tuple-element.163), channel_id=1, source_target_pairs={{1,4},{4,1},{3,6},{6,3},{5,8},{8,5},{7,10},{10,7},{9,12},{12,9},{1... | collective-permute-start | bytes 245768 | tf_op jit(solution)/shard_map/ppermute | solution.py:496
  71.1 5.7 %collective-permute-start.29 = (bf16[5,64,128]{2,1,0:T(8,128)(2,1)S(1)}, bf16[5,64,128]{2,1,0:T(8,128)(2,1)S(1)}, u32[]{:S(2)}, u32[]{:S(2)}) collective-permute-start(bf16[5,64,128]{2,1,0:T(8,128)(2,1)S(1)} %get-tuple-element.156), channel_id=1, source_target_pairs={{1,4},{4,1},{3,6},{6,3},{5,8},{8,5},{7,10},{10,7},{9,12},{12,9},{1... | collective-permute-start | bytes 245768 | tf_op jit(solution)/shard_map/ppermute | solution.py:496
  74.5 5.7 %collective-permute-start.35 = (bf16[5,64,128]{2,1,0:T(8,128)(2,1)S(1)}, bf16[5,64,128]{2,1,0:T(8,128)(2,1)S(1)}, u32[]{:S(2)}, u32[]{:S(2)}) collective-permute-start(bf16[5,64,128]{2,1,0:T(8,128)(2,1)S(1)} %get-tuple-element.166), channel_id=1, source_target_pairs={{1,4},{4,1},{3,6},{6,3},{5,8},{8,5},{7,10},{10,7},{9,12},{12,9},{1... | collective-permute-start | bytes 245768 | tf_op jit(solution)/shard_map/ppermute | solution.py:496
  78.4 5.9 %collective-permute-start.37 = (bf16[5,64,128]{2,1,0:T(8,128)(2,1)S(1)}, bf16[5,64,128]{2,1,0:T(8,128)(2,1)S(1)}, u32[]{:S(2)}, u32[]{:S(2)}) collective-permute-start(bf16[5,64,128]{2,1,0:T(8,128)(2,1)S(1)} %get-tuple-element.170), channel_id=1, source_target_pairs={{1,4},{4,1},{3,6},{6,3},{5,8},{8,5},{7,10},{10,7},{9,12},{12,9},{1... | collective-permute-start | bytes 245768 | tf_op jit(solution)/shard_map/ppermute | solution.py:496
  80.2 4.1 %collective-permute-start.38 = (bf16[5,64,128]{2,1,0:T(8,128)(2,1)S(1)}, bf16[5,64,128]{2,1,0:T(8,128)(2,1)S(1)}, u32[]{:S(2)}, u32[]{:S(2)}) collective-permute-start(bf16[5,64,128]{2,1,0:T(8,128)(2,1)S(1)} %get-tuple-element.171), channel_id=1, source_target_pairs={{0,1},{1,0},{2,3},{3,2},{4,5},{5,4},{6,7},{7,6},{8,9},{9,8},{10,11... | collective-permute-start | bytes 245768 | tf_op jit(solution)/shard_map/ppermute | solution.py:487
  82.4 5.9 %collective-permute-start.43 = (bf16[5,64,128]{2,1,0:T(8,128)(2,1)S(1)}, bf16[5,64,128]{2,1,0:T(8,128)(2,1)S(1)}, u32[]{:S(2)}, u32[]{:S(2)}) collective-permute-start(bf16[5,64,128]{2,1,0:T(8,128)(2,1)S(1)} %get-tuple-element.180), channel_id=1, source_target_pairs={{1,4},{4,1},{3,6},{6,3},{5,8},{8,5},{7,10},{10,7},{9,12},{12,9},{1... | collective-permute-start | bytes 245768 | tf_op jit(solution)/shard_map/ppermute | solution.py:496
  84.3 4.0 %collective-permute-start.44 = (bf16[5,64,128]{2,1,0:T(8,128)(2,1)S(1)}, bf16[5,64,128]{2,1,0:T(8,128)(2,1)S(1)}, u32[]{:S(2)}, u32[]{:S(2)}) collective-permute-start(bf16[5,64,128]{2,1,0:T(8,128)(2,1)S(1)} %get-tuple-element.181), channel_id=1, source_target_pairs={{0,1},{1,0},{2,3},{3,2},{4,5},{5,4},{6,7},{7,6},{8,9},{9,8},{10,11... | collective-permute-start | bytes 245768 | tf_op jit(solution)/shard_map/ppermute | solution.py:487
  86.5 5.7 %collective-permute-start.39 = (bf16[5,64,128]{2,1,0:T(8,128)(2,1)S(1)}, bf16[5,64,128]{2,1,0:T(8,128)(2,1)S(1)}, u32[]{:S(2)}, u32[]{:S(2)}) collective-permute-start(bf16[5,64,128]{2,1,0:T(8,128)(2,1)S(1)} %get-tuple-element.173), channel_id=1, source_target_pairs={{1,4},{4,1},{3,6},{6,3},{5,8},{8,5},{7,10},{10,7},{9,12},{12,9},{1... | collective-permute-start | bytes 245768 | tf_op jit(solution)/shard_map/ppermute | solution.py:496
  89.9 5.7 %collective-permute-start.45 = (bf16[5,64,128]{2,1,0:T(8,128)(2,1)S(1)}, bf16[5,64,128]{2,1,0:T(8,128)(2,1)S(1)}, u32[]{:S(2)}, u32[]{:S(2)}) collective-permute-start(bf16[5,64,128]{2,1,0:T(8,128)(2,1)S(1)} %get-tuple-element.183), channel_id=1, source_target_pairs={{1,4},{4,1},{3,6},{6,3},{5,8},{8,5},{7,10},{10,7},{9,12},{12,9},{1... | collective-permute-start | bytes 245768 | tf_op jit(solution)/shard_map/ppermute | solution.py:496
  93.8 6.8 %collective-permute-start.41 = (bf16[5,64,128]{2,1,0:T(8,128)(2,1)S(1)}, bf16[5,64,128]{2,1,0:T(8,128)(2,1)S(1)}, u32[]{:S(2)}, u32[]{:S(2)}) collective-permute-start(bf16[5,64,128]{2,1,0:T(8,128)(2,1)S(1)} %get-tuple-element.176), channel_id=1, source_target_pairs={{1,4},{4,1},{3,6},{6,3},{5,8},{8,5},{7,10},{10,7},{9,12},{12,9},{1... | collective-permute-start | bytes 245768 | tf_op jit(solution)/shard_map/ppermute | solution.py:496
  95.6 5.0 %collective-permute-start.42 = (bf16[5,64,128]{2,1,0:T(8,128)(2,1)S(1)}, bf16[5,64,128]{2,1,0:T(8,128)(2,1)S(1)}, u32[]{:S(2)}, u32[]{:S(2)}) collective-permute-start(bf16[5,64,128]{2,1,0:T(8,128)(2,1)S(1)} %get-tuple-element.177), channel_id=1, source_target_pairs={{0,1},{1,0},{2,3},{3,2},{4,5},{5,4},{6,7},{7,6},{8,9},{9,8},{10,11... | collective-permute-start | bytes 245768 | tf_op jit(solution)/shard_map/ppermute | solution.py:487
  97.2 6.7 %collective-permute-start.47 = (bf16[5,64,128]{2,1,0:T(8,128)(2,1)S(1)}, bf16[5,64,128]{2,1,0:T(8,128)(2,1)S(1)}, u32[]{:S(2)}, u32[]{:S(2)}) collective-permute-start(bf16[5,64,128]{2,1,0:T(8,128)(2,1)S(1)} %get-tuple-element.186), channel_id=1, source_target_pairs={{1,4},{4,1},{3,6},{6,3},{5,8},{8,5},{7,10},{10,7},{9,12},{12,9},{1... | collective-permute-start | bytes 245768 | tf_op jit(solution)/shard_map/ppermute | solution.py:496
  99.1 5.6 %collective-permute-start.48 = (bf16[5,64,128]{2,1,0:T(8,128)(2,1)S(1)}, bf16[5,64,128]{2,1,0:T(8,128)(2,1)S(1)}, u32[]{:S(2)}, u32[]{:S(2)}) collective-permute-start(bf16[5,64,128]{2,1,0:T(8,128)(2,1)S(1)} %get-tuple-element.187), channel_id=1, source_target_pairs={{0,1},{1,0},{2,3},{3,2},{4,5},{5,4},{6,7},{7,6},{8,9},{9,8},{10,11... | collective-permute-start | bytes 245768 | tf_op jit(solution)/shard_map/ppermute | solution.py:487
  99.1 5.9 %collective-permute-start.49 = (bf16[8,64,128]{2,1,0:T(8,128)(2,1)S(1)}, bf16[8,64,128]{2,1,0:T(8,128)(2,1)S(1)}, u32[]{:S(2)}, u32[]{:S(2)}) collective-permute-start(bf16[8,64,128]{2,1,0:T(8,128)(2,1)S(1)} %get-tuple-element.185.own.refs_2_.refs_4_), channel_id=1, source_target_pairs={{2,0},{3,1},{0,2},{1,3},{6,4},{7,5},{4,6},{5,7},{10,8},{11,9},{8,1... | collective-permute-start | bytes 393224 | tf_op jit(solution)/shard_map/ppermute | solution.py:508
  102.4 5.7 %collective-permute-start.50 = (bf16[5,64,128]{2,1,0:T(8,128)(2,1)S(1)}, bf16[5,64,128]{2,1,0:T(8,128)(2,1)S(1)}, u32[]{:S(2)}, u32[]{:S(2)}) collective-permute-start(bf16[5,64,128]{2,1,0:T(8,128)(2,1)S(1)} %get-tuple-element.190), channel_id=1, source_target_pairs={{1,4},{4,1},{3,6},{6,3},{5,8},{8,5},{7,10},{10,7},{9,12},{12,9},{1... | collective-permute-start | bytes 245768 | tf_op jit(solution)/shard_map/ppermute | solution.py:496
  103.9 4.2 %collective-permute-start.51 = (bf16[5,64,128]{2,1,0:T(8,128)(2,1)S(1)}, bf16[5,64,128]{2,1,0:T(8,128)(2,1)S(1)}, u32[]{:S(2)}, u32[]{:S(2)}) collective-permute-start(bf16[5,64,128]{2,1,0:T(8,128)(2,1)S(1)} %get-tuple-element.191), channel_id=1, source_target_pairs={{0,1},{1,0},{2,3},{3,2},{4,5},{5,4},{6,7},{7,6},{8,9},{9,8},{10,11... | collective-permute-start | bytes 245768 | tf_op jit(solution)/shard_map/ppermute | solution.py:487
  104.0 5.9 %collective-permute-start.52 = (bf16[8,64,128]{2,1,0:T(8,128)(2,1)S(1)}, bf16[8,64,128]{2,1,0:T(8,128)(2,1)S(1)}, u32[]{:S(2)}, u32[]{:S(2)}) collective-permute-start(bf16[8,64,128]{2,1,0:T(8,128)(2,1)S(1)} %get-tuple-element.189.own.refs_3_.refs_5_), channel_id=1, source_target_pairs={{2,0},{3,1},{0,2},{1,3},{6,4},{7,5},{4,6},{5,7},{10,8},{11,9},{8,1... | collective-permute-start | bytes 393224 | tf_op jit(solution)/shard_map/ppermute | solution.py:508
  111.8 6.4 %collective-permute-start.56 = (bf16[208,128]{1,0:T(8,128)(2,1)S(1)}, bf16[208,128]{1,0:T(8,128)(2,1)S(1)}, u32[]{:S(2)}, u32[]{:S(2)}) collective-permute-start(bf16[208,128]{1,0:T(8,128)(2,1)S(1)} %add.9.refs_0_), channel_id=1, source_target_pairs={{0,12},{4,8},{8,4},{12,0},{1,13},{5,9},{9,5},{13,1},{2,14},{6,10},... | collective-permute-start | bytes 159752 | tf_op jit(solution)/shard_map/ppermute | solution.py:669
  113.8 6.1 %collective-permute-start.55 = (bf16[208,128]{1,0:T(8,128)(2,1)S(1)}, bf16[208,128]{1,0:T(8,128)(2,1)S(1)}, u32[]{:S(2)}, u32[]{:S(2)}) collective-permute-start(bf16[208,128]{1,0:T(8,128)(2,1)S(1)} %add.9.refs_0_), channel_id=1, source_target_pairs={{0,8},{4,12},{8,0},{12,4},{1,9},{5,13},{9,1},{13,5},{2,10},{6,14},... | collective-permute-start | bytes 159752 | tf_op jit(solution)/shard_map/ppermute | solution.py:669
  113.8 6.1 %collective-permute-start.54 = (bf16[208,128]{1,0:T(8,128)(2,1)S(1)}, bf16[208,128]{1,0:T(8,128)(2,1)S(1)}, u32[]{:S(2)}, u32[]{:S(2)}) collective-permute-start(bf16[208,128]{1,0:T(8,128)(2,1)S(1)} %add.9.refs_0_), channel_id=1, source_target_pairs={{0,4},{4,0},{8,12},{12,8},{1,5},{5,1},{9,13},{13,9},{2,6},{6,2},{1... | collective-permute-start | bytes 159752 | tf_op jit(solution)/shard_map/ppermute | solution.py:669
  116.3 4.4 %collective-permute-start.60 = (bf16[8,64,128]{2,1,0:T(8,128)(2,1)S(1)}, bf16[8,64,128]{2,1,0:T(8,128)(2,1)S(1)}, u32[]{:S(2)}, u32[]{:S(2)}) collective-permute-start(bf16[8,64,128]{2,1,0:T(8,128)(2,1)S(1)} %get-tuple-element.185.own.refs_2_.refs_4_), channel_id=1, source_target_pairs={{0,1},{1,0},{2,3},{3,2},{4,5},{5,4},{6,7},{7,6},{8,9},{9,8},{10,11... | collective-permute-start | bytes 393224 | tf_op jit(solution)/shard_map/ppermute | solution.py:487
  116.3 8.0 %collective-permute-start.61 = (bf16[8,64,128]{2,1,0:T(8,128)(2,1)S(1)}, bf16[8,64,128]{2,1,0:T(8,128)(2,1)S(1)}, u32[]{:S(2)}, u32[]{:S(2)}) collective-permute-start(bf16[8,64,128]{2,1,0:T(8,128)(2,1)S(1)} %get-tuple-element.189.own.refs_3_.refs_5_), channel_id=1, source_target_pairs={{0,1},{1,0},{2,3},{3,2},{4,5},{5,4},{6,7},{7,6},{8,9},{9,8},{10,11... | collective-permute-start | bytes 393224 | tf_op jit(solution)/shard_map/ppermute | solution.py:487
  118.3 6.0 %collective-permute-start.62 = (bf16[8,64,128]{2,1,0:T(8,128)(2,1)S(1)}, bf16[8,64,128]{2,1,0:T(8,128)(2,1)S(1)}, u32[]{:S(2)}, u32[]{:S(2)}) collective-permute-start(bf16[8,64,128]{2,1,0:T(8,128)(2,1)S(1)} %collective-permute-done.49.y_other.refs_4_.refs_6_), channel_id=1, source_target_pairs={{0,1},{1,0},{2,3},{3,2},{4,5},{5,4},{6,7},{7,6},{8,9},{9,8},{10,11... | collective-permute-start | bytes 393224 | tf_op jit(solution)/shard_map/ppermute | solution.py:487
  119.9 4.4 %collective-permute-start.63 = (bf16[8,64,128]{2,1,0:T(8,128)(2,1)S(1)}, bf16[8,64,128]{2,1,0:T(8,128)(2,1)S(1)}, u32[]{:S(2)}, u32[]{:S(2)}) collective-permute-start(bf16[8,64,128]{2,1,0:T(8,128)(2,1)S(1)} %collective-permute-done.52.refs_5_.refs_7_), channel_id=1, source_target_pairs={{0,1},{1,0},{2,3},{3,2},{4,5},{5,4},{6,7},{7,6},{8,9},{9,8},{10,11... | collective-permute-start | bytes 393224 | tf_op jit(solution)/shard_map/ppermute | solution.py:487
  119.9 4.3 %collective-permute-start.57 = (bf16[208,128]{1,0:T(8,128)(2,1)S(1)}, bf16[208,128]{1,0:T(8,128)(2,1)S(1)}, u32[]{:S(2)}, u32[]{:S(2)}) collective-permute-start(bf16[208,128]{1,0:T(8,128)(2,1)S(1)} %sum.1.refs_0_), channel_id=1, source_target_pairs={{2,0},{3,1},{0,2},{1,3},{6,4},{7,5},{4,6},{5,7},{10,8},{11,9},{8,1... | collective-permute-start | bytes 159752 | tf_op jit(solution)/shard_map/ppermute | solution.py:508
  (16 other events, 56.8 us)

commit v10 on v7

--- a/solution.py
+++ b/solution.py
@@ -143,9 +143,10 @@
     fill_ext(core, own, intra, inter, ext)
     inv = 1.0 / (jnp.zeros(own.shape[1:], F32) + scal[1])
     for row in range(own.shape[0]):
-        image_h, image_e = both_rows((index, signs), ext, ham, ovl, row)
-        mine = own[row].astype(F32)
-        out[row] = ((image_h - scal[0] * (mine + image_e)) * inv).astype(BF16)
+        image = image_of((index, signs), ext, (ham, ovl), row)
+        orbs = ham.shape[2]
+        image = (image[:orbs] - scal[0] * image[orbs:]).T
+        out[row] = ((image - scal[0] * own[row].astype(F32)) * inv).astype(BF16)
     send_ends(core, out, intra_out, inter_out)
 
 
@@ -153,7 +154,7 @@
     core = ints[0]
     fill_ext(core, own, intra, inter, ext)
     for row in range(own.shape[0]):
-        out[row] = (-one_row((index, signs), ext, ovl, row)).astype(BF16)
+        out[row] = (-image_of((index, signs), ext, (ovl,), row)).astype(BF16).T
     send_ends(core, out, intra_out, inter_out)
 
 

time: 127 us -> 127 us (level)
  no operation moved by 1% of the time
where the time goes in v10:
time: 127 us
  starting transfers between devices  64.2 us (51%)
  Pallas kernels  43.8 us (34%)
  waiting for transfers between devices  16 us (13%)
  between operations  2.31 us (2%)
    ppermute x25, starting transfers between devices, swap_chips(): return lax.ppermute(value, ('row', 'col'), pairs)  51.2 us
    pallas_call x30, Pallas kernels, call(): pl.pallas_call(kernel, name=name, out_shape=outs, in_specs=[SMEM] * len(s...  39.2 us
    ppermute x25, waiting for transfers between devices, swap_chips(): return lax.ppermute(value, ('row', 'col'), pairs)  7.45 us
    ppermute x3, starting transfers between devices, from_chip(): return lax.ppermute(value, 'col', pairs)  4.6 us
    ppermute x3, starting transfers between devices, local(): lax.ppermute(summed, 'row', [(r, r ^ step) for r in range(num_rows)])  4.45 us
    ppermute x1, starting transfers between devices, next_chips(): return lax.ppermute(value, ('row', 'col'), pairs)  3.08 us
    ppermute x3, waiting for transfers between devices, local(): lax.ppermute(summed, 'row', [(r, r ^ step) for r in range(num_rows)])  3.07 us
    pallas_call x1, Pallas kernels, local(): pl.pallas_call(functools.partial(load_kernel, total_blocks), name='load',...  3.01 us
  transfers between devices with their start and end apart: 64, of which 21 were waited for; matrix products, arithmetic and copies ran while one was open for 0% of the time, Pallas kernels for 24%

profile of v10, /device:TPU:0, one launch (start us, length us, event | category | flops | bytes accessed | tf_op | source)
XLA Modules:
  0.0 126.5 jit_solution(7225336914356848703)
XLA Ops:
  0.7 1.6 %cut.1 = (bf16[8,64,128]{2,1,0:T(8,128)(2,1)S(1)}, bf16[5,64,128]{2,1,0:T(8,128)(2,1)S(1)}, bf16[13,64,128]{2,1,0:T(8,128)(2,1)S(1)}, bf16[5,64,128]{2,1,0:T(8,128)(2,1)S(1)}, bf16[5,64,128]{2,1,0:T(8,128)(2,1)S(1)}) custom-call(s32[5]{0:T(128)S(1)} %stack.23.ints, s32[16]{0:T(128)} %sizes.3, bf16[64,2048]{1,0:T(8,128)(2,1)} %trial.1), custom_call_target="tpu_custom_call" | custom-call | tf_op jit(solution)/shard_map/cut/pallas_call | solution.py:504
  2.3 3.1 %collective-permute-start.1 = (bf16[5,64,128]{2,1,0:T(8,128)(2,1)S(1)}, bf16[5,64,128]{2,1,0:T(8,128)(2,1)S(1)}, u32[]{:S(2)}, u32[]{:S(2)}) collective-permute-start(bf16[5,64,128]{2,1,0:T(8,128)(2,1)S(1)} %get-tuple-element.105), channel_id=1, source_target_pairs={{0,4},{1,13},{2,6},{3,15},{4,8},{5,1},{6,10},{7,3},{8,12},{9,5},{1... | collective-permute-start | bytes 245768 | tf_op jit(solution)/shard_map/ppermute | solution.py:462
  5.4 1.6 %collective-permute-start.2 = (bf16[5,64,128]{2,1,0:T(8,128)(2,1)S(1)}, bf16[5,64,128]{2,1,0:T(8,128)(2,1)S(1)}, u32[]{:S(2)}, u32[]{:S(2)}) collective-permute-start(bf16[5,64,128]{2,1,0:T(8,128)(2,1)S(1)} %get-tuple-element.106), channel_id=1, source_target_pairs={{1,4},{4,1},{3,6},{6,3},{5,8},{8,5},{7,10},{10,7},{9,12},{12,9},{1... | collective-permute-start | bytes 245768 | tf_op jit(solution)/shard_map/ppermute | solution.py:454
  8.4 3.0 %load.1 = (bf16[8,9,128,128]{3,2,1,0:T(8,128)(2,1)S(1)}, bf16[8,9,128,128]{3,2,1,0:T(8,128)(2,1)S(1)}, s32[8,9]{1,0:T(8,128)S(4)}, f32[8,9]{1,0:T(8,128)S(4)}, s32[12]{0:T(128)S(4)}, /*index=5*/f32[2]{0:T(128)S(4)}) custom-call(s32[5]{0:T(128)S(1)} %stack.23.ints, f32[1]{0:T(128)S(6)} %copy.10.shift, f32[1]{0:T(128)S(6)} %copy.11.width, s32[16,9]{1,0:T(8,128)} %columns.1, ...), custom_call_target="tpu_custom_call" | custom-call | bytes 9437184 | tf_op jit(solution)/shard_map/load/pallas_call | solution.py:521
  12.0 1.5 %scaled.8 = (bf16[8,64,128]{2,1,0:T(8,128)(2,1)S(1)}, bf16[5,64,128]{2,1,0:T(8,128)(2,1)S(1)}, bf16[5,64,128]{2,1,0:T(8,128)(2,1)S(1)}) custom-call(s32[12]{0:T(128)S(4)} %get-tuple-element.99.ints, s32[8,9]{1,0:T(8,128)S(4)} %get-tuple-element.100.index, f32[8,9]{1,0:T(8,128)S(4)} %get-tuple-element.101.signs, f32[2]{0:T(128)S(4)} %get-tuple-element.102.scal, ...), custom_call_target="tpu_custom_call" | custom-call | flops 7247757312 | bytes 56623104 | tf_op jit(solution)/shard_map/scaled/pallas_call | solution.py:475
  13.5 1.7 %collective-permute-start.7 = (bf16[5,64,128]{2,1,0:T(8,128)(2,1)S(1)}, bf16[5,64,128]{2,1,0:T(8,128)(2,1)S(1)}, u32[]{:S(2)}, u32[]{:S(2)}) collective-permute-start(bf16[5,64,128]{2,1,0:T(8,128)(2,1)S(1)} %get-tuple-element.120), channel_id=1, source_target_pairs={{1,4},{4,1},{3,6},{6,3},{5,8},{8,5},{7,10},{10,7},{9,12},{12,9},{1... | collective-permute-start | bytes 245768 | tf_op jit(solution)/shard_map/ppermute | solution.py:454
  15.2 1.5 %scaled.9 = (bf16[8,64,128]{2,1,0:T(8,128)(2,1)S(1)}, bf16[5,64,128]{2,1,0:T(8,128)(2,1)S(1)}, bf16[5,64,128]{2,1,0:T(8,128)(2,1)S(1)}) custom-call(s32[12]{0:T(128)S(4)} %get-tuple-element.99.ints, s32[8,9]{1,0:T(8,128)S(4)} %get-tuple-element.100.index, f32[8,9]{1,0:T(8,128)S(4)} %get-tuple-element.101.signs, f32[2]{0:T(128)S(4)} %get-tuple-element.102.scal, ...), custom_call_target="tpu_custom_call" | custom-call | flops 7247757312 | bytes 56623104 | tf_op jit(solution)/shard_map/scaled/pallas_call | solution.py:475
  16.7 1.9 %collective-permute-start.3 = (bf16[5,64,128]{2,1,0:T(8,128)(2,1)S(1)}, bf16[5,64,128]{2,1,0:T(8,128)(2,1)S(1)}, u32[]{:S(2)}, u32[]{:S(2)}) collective-permute-start(bf16[5,64,128]{2,1,0:T(8,128)(2,1)S(1)} %get-tuple-element.113), channel_id=1, source_target_pairs={{1,4},{4,1},{3,6},{6,3},{5,8},{8,5},{7,10},{10,7},{9,12},{12,9},{1... | collective-permute-start | bytes 245768 | tf_op jit(solution)/shard_map/ppermute | solution.py:454
  20.2 1.6 %collective-permute-start.9 = (bf16[5,64,128]{2,1,0:T(8,128)(2,1)S(1)}, bf16[5,64,128]{2,1,0:T(8,128)(2,1)S(1)}, u32[]{:S(2)}, u32[]{:S(2)}) collective-permute-start(bf16[5,64,128]{2,1,0:T(8,128)(2,1)S(1)} %get-tuple-element.123), channel_id=1, source_target_pairs={{1,4},{4,1},{3,6},{6,3},{5,8},{8,5},{7,10},{10,7},{9,12},{12,9},{1... | collective-permute-start | bytes 245768 | tf_op jit(solution)/shard_map/ppermute | solution.py:454
  23.5 1.9 %collective-permute-start.5 = (bf16[5,64,128]{2,1,0:T(8,128)(2,1)S(1)}, bf16[5,64,128]{2,1,0:T(8,128)(2,1)S(1)}, u32[]{:S(2)}, u32[]{:S(2)}) collective-permute-start(bf16[5,64,128]{2,1,0:T(8,128)(2,1)S(1)} %get-tuple-element.116), channel_id=1, source_target_pairs={{1,4},{4,1},{3,6},{6,3},{5,8},{8,5},{7,10},{10,7},{9,12},{12,9},{1... | collective-permute-start | bytes 245768 | tf_op jit(solution)/shard_map/ppermute | solution.py:454
  26.8 1.8 %collective-permute-start.11 = (bf16[5,64,128]{2,1,0:T(8,128)(2,1)S(1)}, bf16[5,64,128]{2,1,0:T(8,128)(2,1)S(1)}, u32[]{:S(2)}, u32[]{:S(2)}) collective-permute-start(bf16[5,64,128]{2,1,0:T(8,128)(2,1)S(1)} %get-tuple-element.126), channel_id=1, source_target_pairs={{1,4},{4,1},{3,6},{6,3},{5,8},{8,5},{7,10},{10,7},{9,12},{12,9},{1... | collective-permute-start | bytes 245768 | tf_op jit(solution)/shard_map/ppermute | solution.py:454
  30.1 2.1 %collective-permute-start.13 = (bf16[5,64,128]{2,1,0:T(8,128)(2,1)S(1)}, bf16[5,64,128]{2,1,0:T(8,128)(2,1)S(1)}, u32[]{:S(2)}, u32[]{:S(2)}) collective-permute-start(bf16[5,64,128]{2,1,0:T(8,128)(2,1)S(1)} %get-tuple-element.130), channel_id=1, source_target_pairs={{1,4},{4,1},{3,6},{6,3},{5,8},{8,5},{7,10},{10,7},{9,12},{12,9},{1... | collective-permute-start | bytes 245768 | tf_op jit(solution)/shard_map/ppermute | solution.py:454
  32.5 1.5 %scaled.10 = (bf16[8,64,128]{2,1,0:T(8,128)(2,1)S(1)}, bf16[5,64,128]{2,1,0:T(8,128)(2,1)S(1)}, bf16[5,64,128]{2,1,0:T(8,128)(2,1)S(1)}) custom-call(s32[12]{0:T(128)S(4)} %get-tuple-element.99.ints, s32[8,9]{1,0:T(8,128)S(4)} %get-tuple-element.100.index, f32[8,9]{1,0:T(8,128)S(4)} %get-tuple-element.101.signs, f32[2]{0:T(128)S(4)} %get-tuple-element.102.scal, ...), custom_call_target="tpu_custom_call" | custom-call | flops 7247757312 | bytes 56623104 | tf_op jit(solution)/shard_map/scaled/pallas_call | solution.py:475
  34.0 2.0 %collective-permute-start.19 = (bf16[5,64,128]{2,1,0:T(8,128)(2,1)S(1)}, bf16[5,64,128]{2,1,0:T(8,128)(2,1)S(1)}, u32[]{:S(2)}, u32[]{:S(2)}) collective-permute-start(bf16[5,64,128]{2,1,0:T(8,128)(2,1)S(1)} %get-tuple-element.140), channel_id=1, source_target_pairs={{1,4},{4,1},{3,6},{6,3},{5,8},{8,5},{7,10},{10,7},{9,12},{12,9},{1... | collective-permute-start | bytes 245768 | tf_op jit(solution)/shard_map/ppermute | solution.py:454
  36.0 1.5 %scaled.11 = (bf16[8,64,128]{2,1,0:T(8,128)(2,1)S(1)}, bf16[5,64,128]{2,1,0:T(8,128)(2,1)S(1)}, bf16[5,64,128]{2,1,0:T(8,128)(2,1)S(1)}) custom-call(s32[12]{0:T(128)S(4)} %get-tuple-element.99.ints, s32[8,9]{1,0:T(8,128)S(4)} %get-tuple-element.100.index, f32[8,9]{1,0:T(8,128)S(4)} %get-tuple-element.101.signs, f32[2]{0:T(128)S(4)} %get-tuple-element.102.scal, ...), custom_call_target="tpu_custom_call" | custom-call | flops 7247757312 | bytes 56623104 | tf_op jit(solution)/shard_map/scaled/pallas_call | solution.py:475
  37.5 1.9 %collective-permute-start.15 = (bf16[5,64,128]{2,1,0:T(8,128)(2,1)S(1)}, bf16[5,64,128]{2,1,0:T(8,128)(2,1)S(1)}, u32[]{:S(2)}, u32[]{:S(2)}) collective-permute-start(bf16[5,64,128]{2,1,0:T(8,128)(2,1)S(1)} %get-tuple-element.133), channel_id=1, source_target_pairs={{1,4},{4,1},{3,6},{6,3},{5,8},{8,5},{7,10},{10,7},{9,12},{12,9},{1... | collective-permute-start | bytes 245768 | tf_op jit(solution)/shard_map/ppermute | solution.py:454
  40.6 2.0 %collective-permute-start.21 = (bf16[5,64,128]{2,1,0:T(8,128)(2,1)S(1)}, bf16[5,64,128]{2,1,0:T(8,128)(2,1)S(1)}, u32[]{:S(2)}, u32[]{:S(2)}) collective-permute-start(bf16[5,64,128]{2,1,0:T(8,128)(2,1)S(1)} %get-tuple-element.143), channel_id=1, source_target_pairs={{1,4},{4,1},{3,6},{6,3},{5,8},{8,5},{7,10},{10,7},{9,12},{12,9},{1... | collective-permute-start | bytes 245768 | tf_op jit(solution)/shard_map/ppermute | solution.py:454
  44.1 2.1 %collective-permute-start.17 = (bf16[5,64,128]{2,1,0:T(8,128)(2,1)S(1)}, bf16[5,64,128]{2,1,0:T(8,128)(2,1)S(1)}, u32[]{:S(2)}, u32[]{:S(2)}) collective-permute-start(bf16[5,64,128]{2,1,0:T(8,128)(2,1)S(1)} %get-tuple-element.136), channel_id=1, source_target_pairs={{1,4},{4,1},{3,6},{6,3},{5,8},{8,5},{7,10},{10,7},{9,12},{12,9},{1... | collective-permute-start | bytes 245768 | tf_op jit(solution)/shard_map/ppermute | solution.py:454
  47.2 2.2 %collective-permute-start.23 = (bf16[5,64,128]{2,1,0:T(8,128)(2,1)S(1)}, bf16[5,64,128]{2,1,0:T(8,128)(2,1)S(1)}, u32[]{:S(2)}, u32[]{:S(2)}) collective-permute-start(bf16[5,64,128]{2,1,0:T(8,128)(2,1)S(1)} %get-tuple-element.146), channel_id=1, source_target_pairs={{1,4},{4,1},{3,6},{6,3},{5,8},{8,5},{7,10},{10,7},{9,12},{12,9},{1... | collective-permute-start | bytes 245768 | tf_op jit(solution)/shard_map/ppermute | solution.py:454
  50.7 2.4 %collective-permute-start.25 = (bf16[5,64,128]{2,1,0:T(8,128)(2,1)S(1)}, bf16[5,64,128]{2,1,0:T(8,128)(2,1)S(1)}, u32[]{:S(2)}, u32[]{:S(2)}) collective-permute-start(bf16[5,64,128]{2,1,0:T(8,128)(2,1)S(1)} %get-tuple-element.150), channel_id=1, source_target_pairs={{1,4},{4,1},{3,6},{6,3},{5,8},{8,5},{7,10},{10,7},{9,12},{12,9},{1... | collective-permute-start | bytes 245768 | tf_op jit(solution)/shard_map/ppermute | solution.py:454
  53.1 1.5 %scaled.12 = (bf16[8,64,128]{2,1,0:T(8,128)(2,1)S(1)}, bf16[5,64,128]{2,1,0:T(8,128)(2,1)S(1)}, bf16[5,64,128]{2,1,0:T(8,128)(2,1)S(1)}) custom-call(s32[12]{0:T(128)S(4)} %get-tuple-element.99.ints, s32[8,9]{1,0:T(8,128)S(4)} %get-tuple-element.100.index, f32[8,9]{1,0:T(8,128)S(4)} %get-tuple-element.101.signs, f32[2]{0:T(128)S(4)} %get-tuple-element.102.scal, ...), custom_call_target="tpu_custom_call" | custom-call | flops 7247757312 | bytes 56623104 | tf_op jit(solution)/shard_map/scaled/pallas_call | solution.py:475
  54.6 2.2 %collective-permute-start.31 = (bf16[5,64,128]{2,1,0:T(8,128)(2,1)S(1)}, bf16[5,64,128]{2,1,0:T(8,128)(2,1)S(1)}, u32[]{:S(2)}, u32[]{:S(2)}) collective-permute-start(bf16[5,64,128]{2,1,0:T(8,128)(2,1)S(1)} %get-tuple-element.160), channel_id=1, source_target_pairs={{1,4},{4,1},{3,6},{6,3},{5,8},{8,5},{7,10},{10,7},{9,12},{12,9},{1... | collective-permute-start | bytes 245768 | tf_op jit(solution)/shard_map/ppermute | solution.py:454
  56.8 1.5 %scaled.13 = (bf16[8,64,128]{2,1,0:T(8,128)(2,1)S(1)}, bf16[5,64,128]{2,1,0:T(8,128)(2,1)S(1)}, bf16[5,64,128]{2,1,0:T(8,128)(2,1)S(1)}) custom-call(s32[12]{0:T(128)S(4)} %get-tuple-element.99.ints, s32[8,9]{1,0:T(8,128)S(4)} %get-tuple-element.100.index, f32[8,9]{1,0:T(8,128)S(4)} %get-tuple-element.101.signs, f32[2]{0:T(128)S(4)} %get-tuple-element.102.scal, ...), custom_call_target="tpu_custom_call" | custom-call | flops 7247757312 | bytes 56623104 | tf_op jit(solution)/shard_map/scaled/pallas_call | solution.py:475
  58.3 2.1 %collective-permute-start.27 = (bf16[5,64,128]{2,1,0:T(8,128)(2,1)S(1)}, bf16[5,64,128]{2,1,0:T(8,128)(2,1)S(1)}, u32[]{:S(2)}, u32[]{:S(2)}) collective-permute-start(bf16[5,64,128]{2,1,0:T(8,128)(2,1)S(1)} %get-tuple-element.153), channel_id=1, source_target_pairs={{1,4},{4,1},{3,6},{6,3},{5,8},{8,5},{7,10},{10,7},{9,12},{12,9},{1... | collective-permute-start | bytes 245768 | tf_op jit(solution)/shard_map/ppermute | solution.py:454
  61.3 2.1 %collective-permute-start.33 = (bf16[5,64,128]{2,1,0:T(8,128)(2,1)S(1)}, bf16[5,64,128]{2,1,0:T(8,128)(2,1)S(1)}, u32[]{:S(2)}, u32[]{:S(2)}) collective-permute-start(bf16[5,64,128]{2,1,0:T(8,128)(2,1)S(1)} %get-tuple-element.163), channel_id=1, source_target_pairs={{1,4},{4,1},{3,6},{6,3},{5,8},{8,5},{7,10},{10,7},{9,12},{12,9},{1... | collective-permute-start | bytes 245768 | tf_op jit(solution)/shard_map/ppermute | solution.py:454
  64.9 2.3 %collective-permute-start.29 = (bf16[5,64,128]{2,1,0:T(8,128)(2,1)S(1)}, bf16[5,64,128]{2,1,0:T(8,128)(2,1)S(1)}, u32[]{:S(2)}, u32[]{:S(2)}) collective-permute-start(bf16[5,64,128]{2,1,0:T(8,128)(2,1)S(1)} %get-tuple-element.156), channel_id=1, source_target_pairs={{1,4},{4,1},{3,6},{6,3},{5,8},{8,5},{7,10},{10,7},{9,12},{12,9},{1... | collective-permute-start | bytes 245768 | tf_op jit(solution)/shard_map/ppermute | solution.py:454
  68.0 2.1 %collective-permute-start.35 = (bf16[5,64,128]{2,1,0:T(8,128)(2,1)S(1)}, bf16[5,64,128]{2,1,0:T(8,128)(2,1)S(1)}, u32[]{:S(2)}, u32[]{:S(2)}) collective-permute-start(bf16[5,64,128]{2,1,0:T(8,128)(2,1)S(1)} %get-tuple-element.166), channel_id=1, source_target_pairs={{1,4},{4,1},{3,6},{6,3},{5,8},{8,5},{7,10},{10,7},{9,12},{12,9},{1... | collective-permute-start | bytes 245768 | tf_op jit(solution)/shard_map/ppermute | solution.py:454
  71.5 2.4 %collective-permute-start.37 = (bf16[5,64,128]{2,1,0:T(8,128)(2,1)S(1)}, bf16[5,64,128]{2,1,0:T(8,128)(2,1)S(1)}, u32[]{:S(2)}, u32[]{:S(2)}) collective-permute-start(bf16[5,64,128]{2,1,0:T(8,128)(2,1)S(1)} %get-tuple-element.170), channel_id=1, source_target_pairs={{1,4},{4,1},{3,6},{6,3},{5,8},{8,5},{7,10},{10,7},{9,12},{12,9},{1... | collective-permute-start | bytes 245768 | tf_op jit(solution)/shard_map/ppermute | solution.py:454
  73.9 1.5 %scaled.14 = (bf16[8,64,128]{2,1,0:T(8,128)(2,1)S(1)}, bf16[5,64,128]{2,1,0:T(8,128)(2,1)S(1)}, bf16[5,64,128]{2,1,0:T(8,128)(2,1)S(1)}) custom-call(s32[12]{0:T(128)S(4)} %get-tuple-element.99.ints, s32[8,9]{1,0:T(8,128)S(4)} %get-tuple-element.100.index, f32[8,9]{1,0:T(8,128)S(4)} %get-tuple-element.101.signs, f32[2]{0:T(128)S(4)} %get-tuple-element.102.scal, ...), custom_call_target="tpu_custom_call" | custom-call | flops 7247757312 | bytes 56623104 | tf_op jit(solution)/shard_map/scaled/pallas_call | solution.py:475
  75.4 2.1 %collective-permute-start.43 = (bf16[5,64,128]{2,1,0:T(8,128)(2,1)S(1)}, bf16[5,64,128]{2,1,0:T(8,128)(2,1)S(1)}, u32[]{:S(2)}, u32[]{:S(2)}) collective-permute-start(bf16[5,64,128]{2,1,0:T(8,128)(2,1)S(1)} %get-tuple-element.180), channel_id=1, source_target_pairs={{1,4},{4,1},{3,6},{6,3},{5,8},{8,5},{7,10},{10,7},{9,12},{12,9},{1... | collective-permute-start | bytes 245768 | tf_op jit(solution)/shard_map/ppermute | solution.py:454
  77.6 1.5 %scaled.15 = (bf16[8,64,128]{2,1,0:T(8,128)(2,1)S(1)}, bf16[5,64,128]{2,1,0:T(8,128)(2,1)S(1)}, bf16[5,64,128]{2,1,0:T(8,128)(2,1)S(1)}) custom-call(s32[12]{0:T(128)S(4)} %get-tuple-element.99.ints, s32[8,9]{1,0:T(8,128)S(4)} %get-tuple-element.100.index, f32[8,9]{1,0:T(8,128)S(4)} %get-tuple-element.101.signs, f32[2]{0:T(128)S(4)} %get-tuple-element.102.scal, ...), custom_call_target="tpu_custom_call" | custom-call | flops 7247757312 | bytes 56623104 | tf_op jit(solution)/shard_map/scaled/pallas_call | solution.py:475
  79.1 2.2 %collective-permute-start.39 = (bf16[5,64,128]{2,1,0:T(8,128)(2,1)S(1)}, bf16[5,64,128]{2,1,0:T(8,128)(2,1)S(1)}, u32[]{:S(2)}, u32[]{:S(2)}) collective-permute-start(bf16[5,64,128]{2,1,0:T(8,128)(2,1)S(1)} %get-tuple-element.173), channel_id=1, source_target_pairs={{1,4},{4,1},{3,6},{6,3},{5,8},{8,5},{7,10},{10,7},{9,12},{12,9},{1... | collective-permute-start | bytes 245768 | tf_op jit(solution)/shard_map/ppermute | solution.py:454
  82.1 2.1 %collective-permute-start.45 = (bf16[5,64,128]{2,1,0:T(8,128)(2,1)S(1)}, bf16[5,64,128]{2,1,0:T(8,128)(2,1)S(1)}, u32[]{:S(2)}, u32[]{:S(2)}) collective-permute-start(bf16[5,64,128]{2,1,0:T(8,128)(2,1)S(1)} %get-tuple-element.183), channel_id=1, source_target_pairs={{1,4},{4,1},{3,6},{6,3},{5,8},{8,5},{7,10},{10,7},{9,12},{12,9},{1... | collective-permute-start | bytes 245768 | tf_op jit(solution)/shard_map/ppermute | solution.py:454
  85.6 2.4 %collective-permute-start.41 = (bf16[5,64,128]{2,1,0:T(8,128)(2,1)S(1)}, bf16[5,64,128]{2,1,0:T(8,128)(2,1)S(1)}, u32[]{:S(2)}, u32[]{:S(2)}) collective-permute-start(bf16[5,64,128]{2,1,0:T(8,128)(2,1)S(1)} %get-tuple-element.176), channel_id=1, source_target_pairs={{1,4},{4,1},{3,6},{6,3},{5,8},{8,5},{7,10},{10,7},{9,12},{12,9},{1... | collective-permute-start | bytes 245768 | tf_op jit(solution)/shard_map/ppermute | solution.py:454
  88.9 2.1 %collective-permute-start.47 = (bf16[5,64,128]{2,1,0:T(8,128)(2,1)S(1)}, bf16[5,64,128]{2,1,0:T(8,128)(2,1)S(1)}, u32[]{:S(2)}, u32[]{:S(2)}) collective-permute-start(bf16[5,64,128]{2,1,0:T(8,128)(2,1)S(1)} %get-tuple-element.186), channel_id=1, source_target_pairs={{1,4},{4,1},{3,6},{6,3},{5,8},{8,5},{7,10},{10,7},{9,12},{12,9},{1... | collective-permute-start | bytes 245768 | tf_op jit(solution)/shard_map/ppermute | solution.py:454
  91.0 1.5 %collective-permute-start.49 = (bf16[8,64,128]{2,1,0:T(8,128)(2,1)S(1)}, bf16[8,64,128]{2,1,0:T(8,128)(2,1)S(1)}, u32[]{:S(2)}, u32[]{:S(2)}) collective-permute-start(bf16[8,64,128]{2,1,0:T(8,128)(2,1)S(1)} %get-tuple-element.185.own.refs_2_.refs_4_), channel_id=1, source_target_pairs={{2,0},{3,1},{0,2},{1,3},{6,4},{7,5},{4,6},{5,7},{10,8},{11,9},{8,1... | collective-permute-start | bytes 393224 | tf_op jit(solution)/shard_map/ppermute | solution.py:466
  93.4 1.6 %collective-permute-start.50 = (bf16[5,64,128]{2,1,0:T(8,128)(2,1)S(1)}, bf16[5,64,128]{2,1,0:T(8,128)(2,1)S(1)}, u32[]{:S(2)}, u32[]{:S(2)}) collective-permute-start(bf16[5,64,128]{2,1,0:T(8,128)(2,1)S(1)} %get-tuple-element.190), channel_id=1, source_target_pairs={{1,4},{4,1},{3,6},{6,3},{5,8},{8,5},{7,10},{10,7},{9,12},{12,9},{1... | collective-permute-start | bytes 245768 | tf_op jit(solution)/shard_map/ppermute | solution.py:454
  95.0 1.5 %collective-permute-start.52 = (bf16[8,64,128]{2,1,0:T(8,128)(2,1)S(1)}, bf16[8,64,128]{2,1,0:T(8,128)(2,1)S(1)}, u32[]{:S(2)}, u32[]{:S(2)}) collective-permute-start(bf16[8,64,128]{2,1,0:T(8,128)(2,1)S(1)} %get-tuple-element.189.own.refs_3_.refs_5_), channel_id=1, source_target_pairs={{2,0},{3,1},{0,2},{1,3},{6,4},{7,5},{4,6},{5,7},{10,8},{11,9},{8,1... | collective-permute-start | bytes 393224 | tf_op jit(solution)/shard_map/ppermute | solution.py:466
  96.9 1.5 %images.2.refs_0_ = bf16[2,64,1024]{2,1,0:T(8,128)(2,1)S(1)} custom-call(s32[12]{0:T(128)S(4)} %get-tuple-element.99.ints, s32[8,9]{1,0:T(8,128)S(4)} %get-tuple-element.100.index, f32[8,9]{1,0:T(8,128)S(4)} %get-tuple-element.101.signs, bf16[8,64,128]{2,1,0:T(8,128)(2,1)S(1)} %get-tuple-element.185.own.refs_2_.refs_4_, ...), custom_call_target="tpu_custom_call" | custom-call | flops 7247757312 | bytes 56623104 | tf_op jit(solution)/shard_map/images/pallas_call | solution.py:475
  99.3 1.5 %images.3.refs_1_ = bf16[2,64,1024]{2,1,0:T(8,128)(2,1)S(1)} custom-call(s32[12]{0:T(128)S(4)} %get-tuple-element.99.ints, s32[8,9]{1,0:T(8,128)S(4)} %get-tuple-element.100.index, f32[8,9]{1,0:T(8,128)S(4)} %get-tuple-element.101.signs, bf16[8,64,128]{2,1,0:T(8,128)(2,1)S(1)} %get-tuple-element.189.own.refs_3_.refs_5_, ...), custom_call_target="tpu_custom_call" | custom-call | flops 7247757312 | bytes 56623104 | tf_op jit(solution)/shard_map/images/pallas_call | solution.py:475
  101.6 1.2 collective-permute-done.53.right
  102.9 2.1 %collective-permute-start.56 = (bf16[208,128]{1,0:T(8,128)(2,1)S(1)}, bf16[208,128]{1,0:T(8,128)(2,1)S(1)}, u32[]{:S(2)}, u32[]{:S(2)}) collective-permute-start(bf16[208,128]{1,0:T(8,128)(2,1)S(1)} %add.9.refs_0_), channel_id=1, source_target_pairs={{0,12},{4,8},{8,4},{12,0},{1,13},{5,9},{9,5},{13,1},{2,14},{6,10},... | collective-permute-start | bytes 159752 | tf_op jit(solution)/shard_map/ppermute | solution.py:627
  105.0 2.3 %collective-permute-start.54 = (bf16[208,128]{1,0:T(8,128)(2,1)S(1)}, bf16[208,128]{1,0:T(8,128)(2,1)S(1)}, u32[]{:S(2)}, u32[]{:S(2)}) collective-permute-start(bf16[208,128]{1,0:T(8,128)(2,1)S(1)} %add.9.refs_0_), channel_id=1, source_target_pairs={{0,4},{4,0},{8,12},{12,8},{1,5},{5,1},{9,13},{13,9},{2,6},{6,2},{1... | collective-permute-start | bytes 159752 | tf_op jit(solution)/shard_map/ppermute | solution.py:627
  107.8 1.5 %collective-permute-done.56.refs_3_ = bf16[208,128]{1,0:T(8,128)(2,1)S(1)} collective-permute-done((bf16[208,128]{1,0:T(8,128)(2,1)S(1)}, bf16[208,128]{1,0:T(8,128)(2,1)S(1)}, u32[]{:S(2)}, u32[]{:S(2)}) %collective-permute-start.56) | collective-permute-done | bytes 53280 | tf_op jit(solution)/shard_map/ppermute | solution.py:627
  109.3 1.6 %collective-permute-done.55.refs_2_ = bf16[208,128]{1,0:T(8,128)(2,1)S(1)} collective-permute-done((bf16[208,128]{1,0:T(8,128)(2,1)S(1)}, bf16[208,128]{1,0:T(8,128)(2,1)S(1)}, u32[]{:S(2)}, u32[]{:S(2)}) %collective-permute-start.55) | collective-permute-done | bytes 53280 | tf_op jit(solution)/shard_map/ppermute | solution.py:627
  111.0 1.6 %collective-permute-start.57 = (bf16[208,128]{1,0:T(8,128)(2,1)S(1)}, bf16[208,128]{1,0:T(8,128)(2,1)S(1)}, u32[]{:S(2)}, u32[]{:S(2)}) collective-permute-start(bf16[208,128]{1,0:T(8,128)(2,1)S(1)} %sum.1.refs_0_), channel_id=1, source_target_pairs={{2,0},{3,1},{0,2},{1,3},{6,4},{7,5},{4,6},{5,7},{10,8},{11,9},{8,1... | collective-permute-start | bytes 159752 | tf_op jit(solution)/shard_map/ppermute | solution.py:466
  112.8 2.5 %collective-permute-done.57.refs_1_ = bf16[208,128]{1,0:T(8,128)(2,1)S(1)} collective-permute-done((bf16[208,128]{1,0:T(8,128)(2,1)S(1)}, bf16[208,128]{1,0:T(8,128)(2,1)S(1)}, u32[]{:S(2)}, u32[]{:S(2)}) %collective-permute-start.57) | collective-permute-done | bytes 53280 | tf_op jit(solution)/shard_map/ppermute | solution.py:466
  116.5 10.0 %finish.1 = (bf16[64,2048]{1,0:T(8,128)(2,1)}, f32[64,256]{1,0:T(8,128)}) custom-call(s32[12]{0:T(128)S(4)} %get-tuple-element.99.ints, bf16[208,128]{1,0:T(8,128)(2,1)S(1)} %sum.1.refs_0_, bf16[208,128]{1,0:T(8,128)(2,1)S(1)} %collective-permute-done.57.refs_1_, bf16[208,128]{1,0:T(8,128)(2,1)S(1)} %collective-permute-done.58.refs_2_, ...), custom_call_target="tpu_custom_call" | custom-call | flops 36238786560 | bytes 283115520 | tf_op jit(solution)/shard_map/finish/pallas_call | solution.py:475
  (116 shorter events, 24.7 us)
Async XLA Ops:
  2.3 9.1 %collective-permute-start.1 = (bf16[5,64,128]{2,1,0:T(8,128)(2,1)S(1)}, bf16[5,64,128]{2,1,0:T(8,128)(2,1)S(1)}, u32[]{:S(2)}, u32[]{:S(2)}) collective-permute-start(bf16[5,64,128]{2,1,0:T(8,128)(2,1)S(1)} %get-tuple-element.105), channel_id=1, source_target_pairs={{0,4},{1,13},{2,6},{3,15},{4,8},{5,1},{6,10},{7,3},{8,12},{9,5},{1... | collective-permute-start | bytes 245768 | tf_op jit(solution)/shard_map/ppermute | solution.py:462
  5.4 6.5 %collective-permute-start.2 = (bf16[5,64,128]{2,1,0:T(8,128)(2,1)S(1)}, bf16[5,64,128]{2,1,0:T(8,128)(2,1)S(1)}, u32[]{:S(2)}, u32[]{:S(2)}) collective-permute-start(bf16[5,64,128]{2,1,0:T(8,128)(2,1)S(1)} %get-tuple-element.106), channel_id=1, source_target_pairs={{1,4},{4,1},{3,6},{6,3},{5,8},{8,5},{7,10},{10,7},{9,12},{12,9},{1... | collective-permute-start | bytes 245768 | tf_op jit(solution)/shard_map/ppermute | solution.py:454
  7.0 4.9 %collective-permute-start = (bf16[13,64,128]{2,1,0:T(8,128)(2,1)S(1)}, bf16[13,64,128]{2,1,0:T(8,128)(2,1)S(1)}, u32[]{:S(2)}, u32[]{:S(2)}) collective-permute-start(bf16[13,64,128]{2,1,0:T(8,128)(2,1)S(1)} %get-tuple-element.103), channel_id=1, source_target_pairs={{0,1},{1,0},{2,3},{3,2},{4,5},{5,4},{6,7},{7,6},{8,9},{9,8},{10,11... | collective-permute-start | bytes 638984 | tf_op jit(solution)/shard_map/ppermute | solution.py:445
  13.5 5.8 %collective-permute-start.7 = (bf16[5,64,128]{2,1,0:T(8,128)(2,1)S(1)}, bf16[5,64,128]{2,1,0:T(8,128)(2,1)S(1)}, u32[]{:S(2)}, u32[]{:S(2)}) collective-permute-start(bf16[5,64,128]{2,1,0:T(8,128)(2,1)S(1)} %get-tuple-element.120), channel_id=1, source_target_pairs={{1,4},{4,1},{3,6},{6,3},{5,8},{8,5},{7,10},{10,7},{9,12},{12,9},{1... | collective-permute-start | bytes 245768 | tf_op jit(solution)/shard_map/ppermute | solution.py:454
  15.2 4.1 %collective-permute-start.8 = (bf16[5,64,128]{2,1,0:T(8,128)(2,1)S(1)}, bf16[5,64,128]{2,1,0:T(8,128)(2,1)S(1)}, u32[]{:S(2)}, u32[]{:S(2)}) collective-permute-start(bf16[5,64,128]{2,1,0:T(8,128)(2,1)S(1)} %get-tuple-element.121), channel_id=1, source_target_pairs={{0,1},{1,0},{2,3},{3,2},{4,5},{5,4},{6,7},{7,6},{8,9},{9,8},{10,11... | collective-permute-start | bytes 245768 | tf_op jit(solution)/shard_map/ppermute | solution.py:445
  16.7 5.9 %collective-permute-start.3 = (bf16[5,64,128]{2,1,0:T(8,128)(2,1)S(1)}, bf16[5,64,128]{2,1,0:T(8,128)(2,1)S(1)}, u32[]{:S(2)}, u32[]{:S(2)}) collective-permute-start(bf16[5,64,128]{2,1,0:T(8,128)(2,1)S(1)} %get-tuple-element.113), channel_id=1, source_target_pairs={{1,4},{4,1},{3,6},{6,3},{5,8},{8,5},{7,10},{10,7},{9,12},{12,9},{1... | collective-permute-start | bytes 245768 | tf_op jit(solution)/shard_map/ppermute | solution.py:454
  18.7 4.0 %collective-permute-start.4 = (bf16[5,64,128]{2,1,0:T(8,128)(2,1)S(1)}, bf16[5,64,128]{2,1,0:T(8,128)(2,1)S(1)}, u32[]{:S(2)}, u32[]{:S(2)}) collective-permute-start(bf16[5,64,128]{2,1,0:T(8,128)(2,1)S(1)} %get-tuple-element.114), channel_id=1, source_target_pairs={{0,1},{1,0},{2,3},{3,2},{4,5},{5,4},{6,7},{7,6},{8,9},{9,8},{10,11... | collective-permute-start | bytes 245768 | tf_op jit(solution)/shard_map/ppermute | solution.py:445
  20.2 5.7 %collective-permute-start.9 = (bf16[5,64,128]{2,1,0:T(8,128)(2,1)S(1)}, bf16[5,64,128]{2,1,0:T(8,128)(2,1)S(1)}, u32[]{:S(2)}, u32[]{:S(2)}) collective-permute-start(bf16[5,64,128]{2,1,0:T(8,128)(2,1)S(1)} %get-tuple-element.123), channel_id=1, source_target_pairs={{1,4},{4,1},{3,6},{6,3},{5,8},{8,5},{7,10},{10,7},{9,12},{12,9},{1... | collective-permute-start | bytes 245768 | tf_op jit(solution)/shard_map/ppermute | solution.py:454
  21.8 4.1 %collective-permute-start.10 = (bf16[5,64,128]{2,1,0:T(8,128)(2,1)S(1)}, bf16[5,64,128]{2,1,0:T(8,128)(2,1)S(1)}, u32[]{:S(2)}, u32[]{:S(2)}) collective-permute-start(bf16[5,64,128]{2,1,0:T(8,128)(2,1)S(1)} %get-tuple-element.124), channel_id=1, source_target_pairs={{0,1},{1,0},{2,3},{3,2},{4,5},{5,4},{6,7},{7,6},{8,9},{9,8},{10,11... | collective-permute-start | bytes 245768 | tf_op jit(solution)/shard_map/ppermute | solution.py:445
  23.5 5.8 %collective-permute-start.5 = (bf16[5,64,128]{2,1,0:T(8,128)(2,1)S(1)}, bf16[5,64,128]{2,1,0:T(8,128)(2,1)S(1)}, u32[]{:S(2)}, u32[]{:S(2)}) collective-permute-start(bf16[5,64,128]{2,1,0:T(8,128)(2,1)S(1)} %get-tuple-element.116), channel_id=1, source_target_pairs={{1,4},{4,1},{3,6},{6,3},{5,8},{8,5},{7,10},{10,7},{9,12},{12,9},{1... | collective-permute-start | bytes 245768 | tf_op jit(solution)/shard_map/ppermute | solution.py:454
  25.4 3.8 %collective-permute-start.6 = (bf16[5,64,128]{2,1,0:T(8,128)(2,1)S(1)}, bf16[5,64,128]{2,1,0:T(8,128)(2,1)S(1)}, u32[]{:S(2)}, u32[]{:S(2)}) collective-permute-start(bf16[5,64,128]{2,1,0:T(8,128)(2,1)S(1)} %get-tuple-element.117), channel_id=1, source_target_pairs={{0,1},{1,0},{2,3},{3,2},{4,5},{5,4},{6,7},{7,6},{8,9},{9,8},{10,11... | collective-permute-start | bytes 245768 | tf_op jit(solution)/shard_map/ppermute | solution.py:445
  26.8 5.7 %collective-permute-start.11 = (bf16[5,64,128]{2,1,0:T(8,128)(2,1)S(1)}, bf16[5,64,128]{2,1,0:T(8,128)(2,1)S(1)}, u32[]{:S(2)}, u32[]{:S(2)}) collective-permute-start(bf16[5,64,128]{2,1,0:T(8,128)(2,1)S(1)} %get-tuple-element.126), channel_id=1, source_target_pairs={{1,4},{4,1},{3,6},{6,3},{5,8},{8,5},{7,10},{10,7},{9,12},{12,9},{1... | collective-permute-start | bytes 245768 | tf_op jit(solution)/shard_map/ppermute | solution.py:454
  28.6 3.9 %collective-permute-start.12 = (bf16[5,64,128]{2,1,0:T(8,128)(2,1)S(1)}, bf16[5,64,128]{2,1,0:T(8,128)(2,1)S(1)}, u32[]{:S(2)}, u32[]{:S(2)}) collective-permute-start(bf16[5,64,128]{2,1,0:T(8,128)(2,1)S(1)} %get-tuple-element.127), channel_id=1, source_target_pairs={{0,1},{1,0},{2,3},{3,2},{4,5},{5,4},{6,7},{7,6},{8,9},{9,8},{10,11... | collective-permute-start | bytes 245768 | tf_op jit(solution)/shard_map/ppermute | solution.py:445
  30.1 5.9 %collective-permute-start.13 = (bf16[5,64,128]{2,1,0:T(8,128)(2,1)S(1)}, bf16[5,64,128]{2,1,0:T(8,128)(2,1)S(1)}, u32[]{:S(2)}, u32[]{:S(2)}) collective-permute-start(bf16[5,64,128]{2,1,0:T(8,128)(2,1)S(1)} %get-tuple-element.130), channel_id=1, source_target_pairs={{1,4},{4,1},{3,6},{6,3},{5,8},{8,5},{7,10},{10,7},{9,12},{12,9},{1... | collective-permute-start | bytes 245768 | tf_op jit(solution)/shard_map/ppermute | solution.py:454
  32.1 3.9 %collective-permute-start.14 = (bf16[5,64,128]{2,1,0:T(8,128)(2,1)S(1)}, bf16[5,64,128]{2,1,0:T(8,128)(2,1)S(1)}, u32[]{:S(2)}, u32[]{:S(2)}) collective-permute-start(bf16[5,64,128]{2,1,0:T(8,128)(2,1)S(1)} %get-tuple-element.131), channel_id=1, source_target_pairs={{0,1},{1,0},{2,3},{3,2},{4,5},{5,4},{6,7},{7,6},{8,9},{9,8},{10,11... | collective-permute-start | bytes 245768 | tf_op jit(solution)/shard_map/ppermute | solution.py:445
  34.0 5.7 %collective-permute-start.19 = (bf16[5,64,128]{2,1,0:T(8,128)(2,1)S(1)}, bf16[5,64,128]{2,1,0:T(8,128)(2,1)S(1)}, u32[]{:S(2)}, u32[]{:S(2)}) collective-permute-start(bf16[5,64,128]{2,1,0:T(8,128)(2,1)S(1)} %get-tuple-element.140), channel_id=1, source_target_pairs={{1,4},{4,1},{3,6},{6,3},{5,8},{8,5},{7,10},{10,7},{9,12},{12,9},{1... | collective-permute-start | bytes 245768 | tf_op jit(solution)/shard_map/ppermute | solution.py:454
  37.5 5.7 %collective-permute-start.15 = (bf16[5,64,128]{2,1,0:T(8,128)(2,1)S(1)}, bf16[5,64,128]{2,1,0:T(8,128)(2,1)S(1)}, u32[]{:S(2)}, u32[]{:S(2)}) collective-permute-start(bf16[5,64,128]{2,1,0:T(8,128)(2,1)S(1)} %get-tuple-element.133), channel_id=1, source_target_pairs={{1,4},{4,1},{3,6},{6,3},{5,8},{8,5},{7,10},{10,7},{9,12},{12,9},{1... | collective-permute-start | bytes 245768 | tf_op jit(solution)/shard_map/ppermute | solution.py:454
  39.4 3.8 %collective-permute-start.16 = (bf16[5,64,128]{2,1,0:T(8,128)(2,1)S(1)}, bf16[5,64,128]{2,1,0:T(8,128)(2,1)S(1)}, u32[]{:S(2)}, u32[]{:S(2)}) collective-permute-start(bf16[5,64,128]{2,1,0:T(8,128)(2,1)S(1)} %get-tuple-element.134), channel_id=1, source_target_pairs={{0,1},{1,0},{2,3},{3,2},{4,5},{5,4},{6,7},{7,6},{8,9},{9,8},{10,11... | collective-permute-start | bytes 245768 | tf_op jit(solution)/shard_map/ppermute | solution.py:445
  40.6 5.7 %collective-permute-start.21 = (bf16[5,64,128]{2,1,0:T(8,128)(2,1)S(1)}, bf16[5,64,128]{2,1,0:T(8,128)(2,1)S(1)}, u32[]{:S(2)}, u32[]{:S(2)}) collective-permute-start(bf16[5,64,128]{2,1,0:T(8,128)(2,1)S(1)} %get-tuple-element.143), channel_id=1, source_target_pairs={{1,4},{4,1},{3,6},{6,3},{5,8},{8,5},{7,10},{10,7},{9,12},{12,9},{1... | collective-permute-start | bytes 245768 | tf_op jit(solution)/shard_map/ppermute | solution.py:454
  44.1 5.7 %collective-permute-start.17 = (bf16[5,64,128]{2,1,0:T(8,128)(2,1)S(1)}, bf16[5,64,128]{2,1,0:T(8,128)(2,1)S(1)}, u32[]{:S(2)}, u32[]{:S(2)}) collective-permute-start(bf16[5,64,128]{2,1,0:T(8,128)(2,1)S(1)} %get-tuple-element.136), channel_id=1, source_target_pairs={{1,4},{4,1},{3,6},{6,3},{5,8},{8,5},{7,10},{10,7},{9,12},{12,9},{1... | collective-permute-start | bytes 245768 | tf_op jit(solution)/shard_map/ppermute | solution.py:454
  47.2 5.9 %collective-permute-start.23 = (bf16[5,64,128]{2,1,0:T(8,128)(2,1)S(1)}, bf16[5,64,128]{2,1,0:T(8,128)(2,1)S(1)}, u32[]{:S(2)}, u32[]{:S(2)}) collective-permute-start(bf16[5,64,128]{2,1,0:T(8,128)(2,1)S(1)} %get-tuple-element.146), channel_id=1, source_target_pairs={{1,4},{4,1},{3,6},{6,3},{5,8},{8,5},{7,10},{10,7},{9,12},{12,9},{1... | collective-permute-start | bytes 245768 | tf_op jit(solution)/shard_map/ppermute | solution.py:454
  50.7 6.1 %collective-permute-start.25 = (bf16[5,64,128]{2,1,0:T(8,128)(2,1)S(1)}, bf16[5,64,128]{2,1,0:T(8,128)(2,1)S(1)}, u32[]{:S(2)}, u32[]{:S(2)}) collective-permute-start(bf16[5,64,128]{2,1,0:T(8,128)(2,1)S(1)} %get-tuple-element.150), channel_id=1, source_target_pairs={{1,4},{4,1},{3,6},{6,3},{5,8},{8,5},{7,10},{10,7},{9,12},{12,9},{1... | collective-permute-start | bytes 245768 | tf_op jit(solution)/shard_map/ppermute | solution.py:454
  54.6 5.8 %collective-permute-start.31 = (bf16[5,64,128]{2,1,0:T(8,128)(2,1)S(1)}, bf16[5,64,128]{2,1,0:T(8,128)(2,1)S(1)}, u32[]{:S(2)}, u32[]{:S(2)}) collective-permute-start(bf16[5,64,128]{2,1,0:T(8,128)(2,1)S(1)} %get-tuple-element.160), channel_id=1, source_target_pairs={{1,4},{4,1},{3,6},{6,3},{5,8},{8,5},{7,10},{10,7},{9,12},{12,9},{1... | collective-permute-start | bytes 245768 | tf_op jit(solution)/shard_map/ppermute | solution.py:454
  58.3 5.7 %collective-permute-start.27 = (bf16[5,64,128]{2,1,0:T(8,128)(2,1)S(1)}, bf16[5,64,128]{2,1,0:T(8,128)(2,1)S(1)}, u32[]{:S(2)}, u32[]{:S(2)}) collective-permute-start(bf16[5,64,128]{2,1,0:T(8,128)(2,1)S(1)} %get-tuple-element.153), channel_id=1, source_target_pairs={{1,4},{4,1},{3,6},{6,3},{5,8},{8,5},{7,10},{10,7},{9,12},{12,9},{1... | collective-permute-start | bytes 245768 | tf_op jit(solution)/shard_map/ppermute | solution.py:454
  61.3 5.9 %collective-permute-start.33 = (bf16[5,64,128]{2,1,0:T(8,128)(2,1)S(1)}, bf16[5,64,128]{2,1,0:T(8,128)(2,1)S(1)}, u32[]{:S(2)}, u32[]{:S(2)}) collective-permute-start(bf16[5,64,128]{2,1,0:T(8,128)(2,1)S(1)} %get-tuple-element.163), channel_id=1, source_target_pairs={{1,4},{4,1},{3,6},{6,3},{5,8},{8,5},{7,10},{10,7},{9,12},{12,9},{1... | collective-permute-start | bytes 245768 | tf_op jit(solution)/shard_map/ppermute | solution.py:454
  64.9 5.7 %collective-permute-start.29 = (bf16[5,64,128]{2,1,0:T(8,128)(2,1)S(1)}, bf16[5,64,128]{2,1,0:T(8,128)(2,1)S(1)}, u32[]{:S(2)}, u32[]{:S(2)}) collective-permute-start(bf16[5,64,128]{2,1,0:T(8,128)(2,1)S(1)} %get-tuple-element.156), channel_id=1, source_target_pairs={{1,4},{4,1},{3,6},{6,3},{5,8},{8,5},{7,10},{10,7},{9,12},{12,9},{1... | collective-permute-start | bytes 245768 | tf_op jit(solution)/shard_map/ppermute | solution.py:454
  68.0 5.9 %collective-permute-start.35 = (bf16[5,64,128]{2,1,0:T(8,128)(2,1)S(1)}, bf16[5,64,128]{2,1,0:T(8,128)(2,1)S(1)}, u32[]{:S(2)}, u32[]{:S(2)}) collective-permute-start(bf16[5,64,128]{2,1,0:T(8,128)(2,1)S(1)} %get-tuple-element.166), channel_id=1, source_target_pairs={{1,4},{4,1},{3,6},{6,3},{5,8},{8,5},{7,10},{10,7},{9,12},{12,9},{1... | collective-permute-start | bytes 245768 | tf_op jit(solution)/shard_map/ppermute | solution.py:454
  71.5 6.1 %collective-permute-start.37 = (bf16[5,64,128]{2,1,0:T(8,128)(2,1)S(1)}, bf16[5,64,128]{2,1,0:T(8,128)(2,1)S(1)}, u32[]{:S(2)}, u32[]{:S(2)}) collective-permute-start(bf16[5,64,128]{2,1,0:T(8,128)(2,1)S(1)} %get-tuple-element.170), channel_id=1, source_target_pairs={{1,4},{4,1},{3,6},{6,3},{5,8},{8,5},{7,10},{10,7},{9,12},{12,9},{1... | collective-permute-start | bytes 245768 | tf_op jit(solution)/shard_map/ppermute | solution.py:454
  75.4 5.8 %collective-permute-start.43 = (bf16[5,64,128]{2,1,0:T(8,128)(2,1)S(1)}, bf16[5,64,128]{2,1,0:T(8,128)(2,1)S(1)}, u32[]{:S(2)}, u32[]{:S(2)}) collective-permute-start(bf16[5,64,128]{2,1,0:T(8,128)(2,1)S(1)} %get-tuple-element.180), channel_id=1, source_target_pairs={{1,4},{4,1},{3,6},{6,3},{5,8},{8,5},{7,10},{10,7},{9,12},{12,9},{1... | collective-permute-start | bytes 245768 | tf_op jit(solution)/shard_map/ppermute | solution.py:454
  79.1 5.7 %collective-permute-start.39 = (bf16[5,64,128]{2,1,0:T(8,128)(2,1)S(1)}, bf16[5,64,128]{2,1,0:T(8,128)(2,1)S(1)}, u32[]{:S(2)}, u32[]{:S(2)}) collective-permute-start(bf16[5,64,128]{2,1,0:T(8,128)(2,1)S(1)} %get-tuple-element.173), channel_id=1, source_target_pairs={{1,4},{4,1},{3,6},{6,3},{5,8},{8,5},{7,10},{10,7},{9,12},{12,9},{1... | collective-permute-start | bytes 245768 | tf_op jit(solution)/shard_map/ppermute | solution.py:454
  82.1 5.9 %collective-permute-start.45 = (bf16[5,64,128]{2,1,0:T(8,128)(2,1)S(1)}, bf16[5,64,128]{2,1,0:T(8,128)(2,1)S(1)}, u32[]{:S(2)}, u32[]{:S(2)}) collective-permute-start(bf16[5,64,128]{2,1,0:T(8,128)(2,1)S(1)} %get-tuple-element.183), channel_id=1, source_target_pairs={{1,4},{4,1},{3,6},{6,3},{5,8},{8,5},{7,10},{10,7},{9,12},{12,9},{1... | collective-permute-start | bytes 245768 | tf_op jit(solution)/shard_map/ppermute | solution.py:454
  84.2 3.8 %collective-permute-start.46 = (bf16[5,64,128]{2,1,0:T(8,128)(2,1)S(1)}, bf16[5,64,128]{2,1,0:T(8,128)(2,1)S(1)}, u32[]{:S(2)}, u32[]{:S(2)}) collective-permute-start(bf16[5,64,128]{2,1,0:T(8,128)(2,1)S(1)} %get-tuple-element.184), channel_id=1, source_target_pairs={{0,1},{1,0},{2,3},{3,2},{4,5},{5,4},{6,7},{7,6},{8,9},{9,8},{10,11... | collective-permute-start | bytes 245768 | tf_op jit(solution)/shard_map/ppermute | solution.py:445
  85.6 6.8 %collective-permute-start.41 = (bf16[5,64,128]{2,1,0:T(8,128)(2,1)S(1)}, bf16[5,64,128]{2,1,0:T(8,128)(2,1)S(1)}, u32[]{:S(2)}, u32[]{:S(2)}) collective-permute-start(bf16[5,64,128]{2,1,0:T(8,128)(2,1)S(1)} %get-tuple-element.176), channel_id=1, source_target_pairs={{1,4},{4,1},{3,6},{6,3},{5,8},{8,5},{7,10},{10,7},{9,12},{12,9},{1... | collective-permute-start | bytes 245768 | tf_op jit(solution)/shard_map/ppermute | solution.py:454
  88.0 4.5 %collective-permute-start.42 = (bf16[5,64,128]{2,1,0:T(8,128)(2,1)S(1)}, bf16[5,64,128]{2,1,0:T(8,128)(2,1)S(1)}, u32[]{:S(2)}, u32[]{:S(2)}) collective-permute-start(bf16[5,64,128]{2,1,0:T(8,128)(2,1)S(1)} %get-tuple-element.177), channel_id=1, source_target_pairs={{0,1},{1,0},{2,3},{3,2},{4,5},{5,4},{6,7},{7,6},{8,9},{9,8},{10,11... | collective-permute-start | bytes 245768 | tf_op jit(solution)/shard_map/ppermute | solution.py:445
  88.9 6.1 %collective-permute-start.47 = (bf16[5,64,128]{2,1,0:T(8,128)(2,1)S(1)}, bf16[5,64,128]{2,1,0:T(8,128)(2,1)S(1)}, u32[]{:S(2)}, u32[]{:S(2)}) collective-permute-start(bf16[5,64,128]{2,1,0:T(8,128)(2,1)S(1)} %get-tuple-element.186), channel_id=1, source_target_pairs={{1,4},{4,1},{3,6},{6,3},{5,8},{8,5},{7,10},{10,7},{9,12},{12,9},{1... | collective-permute-start | bytes 245768 | tf_op jit(solution)/shard_map/ppermute | solution.py:454
  91.0 5.6 %collective-permute-start.48 = (bf16[5,64,128]{2,1,0:T(8,128)(2,1)S(1)}, bf16[5,64,128]{2,1,0:T(8,128)(2,1)S(1)}, u32[]{:S(2)}, u32[]{:S(2)}) collective-permute-start(bf16[5,64,128]{2,1,0:T(8,128)(2,1)S(1)} %get-tuple-element.187), channel_id=1, source_target_pairs={{0,1},{1,0},{2,3},{3,2},{4,5},{5,4},{6,7},{7,6},{8,9},{9,8},{10,11... | collective-permute-start | bytes 245768 | tf_op jit(solution)/shard_map/ppermute | solution.py:445
  91.0 5.9 %collective-permute-start.49 = (bf16[8,64,128]{2,1,0:T(8,128)(2,1)S(1)}, bf16[8,64,128]{2,1,0:T(8,128)(2,1)S(1)}, u32[]{:S(2)}, u32[]{:S(2)}) collective-permute-start(bf16[8,64,128]{2,1,0:T(8,128)(2,1)S(1)} %get-tuple-element.185.own.refs_2_.refs_4_), channel_id=1, source_target_pairs={{2,0},{3,1},{0,2},{1,3},{6,4},{7,5},{4,6},{5,7},{10,8},{11,9},{8,1... | collective-permute-start | bytes 393224 | tf_op jit(solution)/shard_map/ppermute | solution.py:466
  93.4 6.0 %collective-permute-start.50 = (bf16[5,64,128]{2,1,0:T(8,128)(2,1)S(1)}, bf16[5,64,128]{2,1,0:T(8,128)(2,1)S(1)}, u32[]{:S(2)}, u32[]{:S(2)}) collective-permute-start(bf16[5,64,128]{2,1,0:T(8,128)(2,1)S(1)} %get-tuple-element.190), channel_id=1, source_target_pairs={{1,4},{4,1},{3,6},{6,3},{5,8},{8,5},{7,10},{10,7},{9,12},{12,9},{1... | collective-permute-start | bytes 245768 | tf_op jit(solution)/shard_map/ppermute | solution.py:454
  95.0 4.3 %collective-permute-start.51 = (bf16[5,64,128]{2,1,0:T(8,128)(2,1)S(1)}, bf16[5,64,128]{2,1,0:T(8,128)(2,1)S(1)}, u32[]{:S(2)}, u32[]{:S(2)}) collective-permute-start(bf16[5,64,128]{2,1,0:T(8,128)(2,1)S(1)} %get-tuple-element.191), channel_id=1, source_target_pairs={{0,1},{1,0},{2,3},{3,2},{4,5},{5,4},{6,7},{7,6},{8,9},{9,8},{10,11... | collective-permute-start | bytes 245768 | tf_op jit(solution)/shard_map/ppermute | solution.py:445
  95.0 5.9 %collective-permute-start.52 = (bf16[8,64,128]{2,1,0:T(8,128)(2,1)S(1)}, bf16[8,64,128]{2,1,0:T(8,128)(2,1)S(1)}, u32[]{:S(2)}, u32[]{:S(2)}) collective-permute-start(bf16[8,64,128]{2,1,0:T(8,128)(2,1)S(1)} %get-tuple-element.189.own.refs_3_.refs_5_), channel_id=1, source_target_pairs={{2,0},{3,1},{0,2},{1,3},{6,4},{7,5},{4,6},{5,7},{10,8},{11,9},{8,1... | collective-permute-start | bytes 393224 | tf_op jit(solution)/shard_map/ppermute | solution.py:466
  102.9 6.4 %collective-permute-start.56 = (bf16[208,128]{1,0:T(8,128)(2,1)S(1)}, bf16[208,128]{1,0:T(8,128)(2,1)S(1)}, u32[]{:S(2)}, u32[]{:S(2)}) collective-permute-start(bf16[208,128]{1,0:T(8,128)(2,1)S(1)} %add.9.refs_0_), channel_id=1, source_target_pairs={{0,12},{4,8},{8,4},{12,0},{1,13},{5,9},{9,5},{13,1},{2,14},{6,10},... | collective-permute-start | bytes 159752 | tf_op jit(solution)/shard_map/ppermute | solution.py:627
  105.0 5.9 %collective-permute-start.55 = (bf16[208,128]{1,0:T(8,128)(2,1)S(1)}, bf16[208,128]{1,0:T(8,128)(2,1)S(1)}, u32[]{:S(2)}, u32[]{:S(2)}) collective-permute-start(bf16[208,128]{1,0:T(8,128)(2,1)S(1)} %add.9.refs_0_), channel_id=1, source_target_pairs={{0,8},{4,12},{8,0},{12,4},{1,9},{5,13},{9,1},{13,5},{2,10},{6,14},... | collective-permute-start | bytes 159752 | tf_op jit(solution)/shard_map/ppermute | solution.py:627
  105.0 5.9 %collective-permute-start.54 = (bf16[208,128]{1,0:T(8,128)(2,1)S(1)}, bf16[208,128]{1,0:T(8,128)(2,1)S(1)}, u32[]{:S(2)}, u32[]{:S(2)}) collective-permute-start(bf16[208,128]{1,0:T(8,128)(2,1)S(1)} %add.9.refs_0_), channel_id=1, source_target_pairs={{0,4},{4,0},{8,12},{12,8},{1,5},{5,1},{9,13},{13,9},{2,6},{6,2},{1... | collective-permute-start | bytes 159752 | tf_op jit(solution)/shard_map/ppermute | solution.py:627
  107.3 5.3 %collective-permute-start.60 = (bf16[8,64,128]{2,1,0:T(8,128)(2,1)S(1)}, bf16[8,64,128]{2,1,0:T(8,128)(2,1)S(1)}, u32[]{:S(2)}, u32[]{:S(2)}) collective-permute-start(bf16[8,64,128]{2,1,0:T(8,128)(2,1)S(1)} %get-tuple-element.185.own.refs_2_.refs_4_), channel_id=1, source_target_pairs={{0,1},{1,0},{2,3},{3,2},{4,5},{5,4},{6,7},{7,6},{8,9},{9,8},{10,11... | collective-permute-start | bytes 393224 | tf_op jit(solution)/shard_map/ppermute | solution.py:445
  107.3 8.0 %collective-permute-start.61 = (bf16[8,64,128]{2,1,0:T(8,128)(2,1)S(1)}, bf16[8,64,128]{2,1,0:T(8,128)(2,1)S(1)}, u32[]{:S(2)}, u32[]{:S(2)}) collective-permute-start(bf16[8,64,128]{2,1,0:T(8,128)(2,1)S(1)} %get-tuple-element.189.own.refs_3_.refs_5_), channel_id=1, source_target_pairs={{0,1},{1,0},{2,3},{3,2},{4,5},{5,4},{6,7},{7,6},{8,9},{9,8},{10,11... | collective-permute-start | bytes 393224 | tf_op jit(solution)/shard_map/ppermute | solution.py:445
  109.3 6.0 %collective-permute-start.62 = (bf16[8,64,128]{2,1,0:T(8,128)(2,1)S(1)}, bf16[8,64,128]{2,1,0:T(8,128)(2,1)S(1)}, u32[]{:S(2)}, u32[]{:S(2)}) collective-permute-start(bf16[8,64,128]{2,1,0:T(8,128)(2,1)S(1)} %collective-permute-done.49.y_other.refs_4_.refs_6_), channel_id=1, source_target_pairs={{0,1},{1,0},{2,3},{3,2},{4,5},{5,4},{6,7},{7,6},{8,9},{9,8},{10,11... | collective-permute-start | bytes 393224 | tf_op jit(solution)/shard_map/ppermute | solution.py:445
  110.9 4.4 %collective-permute-start.63 = (bf16[8,64,128]{2,1,0:T(8,128)(2,1)S(1)}, bf16[8,64,128]{2,1,0:T(8,128)(2,1)S(1)}, u32[]{:S(2)}, u32[]{:S(2)}) collective-permute-start(bf16[8,64,128]{2,1,0:T(8,128)(2,1)S(1)} %collective-permute-done.52.refs_5_.refs_7_), channel_id=1, source_target_pairs={{0,1},{1,0},{2,3},{3,2},{4,5},{5,4},{6,7},{7,6},{8,9},{9,8},{10,11... | collective-permute-start | bytes 393224 | tf_op jit(solution)/shard_map/ppermute | solution.py:445
  111.0 4.3 %collective-permute-start.57 = (bf16[208,128]{1,0:T(8,128)(2,1)S(1)}, bf16[208,128]{1,0:T(8,128)(2,1)S(1)}, u32[]{:S(2)}, u32[]{:S(2)}) collective-permute-start(bf16[208,128]{1,0:T(8,128)(2,1)S(1)} %sum.1.refs_0_), channel_id=1, source_target_pairs={{2,0},{3,1},{0,2},{1,3},{6,4},{7,5},{4,6},{5,7},{10,8},{11,9},{8,1... | collective-permute-start | bytes 159752 | tf_op jit(solution)/shard_map/ppermute | solution.py:466
  (16 other events, 52.9 us)

commit v11 on v7

--- a/solution.py
+++ b/solution.py
@@ -68,6 +68,29 @@
 
 def one_row(table, ext, ovl, row):
     return image_of(table, ext, (ovl,), row).T
+
+
+def two_rows(table, ext, ovl, row):
+    index, signs = table
+    last = ovl.shape[1] - 1
+    tails, images = [], []
+    for r in (row, row + 1):
+        vectors = picked(table, ext, r)
+        matrix = row_matrix(ovl, r)
+        cut = last * ovl.shape[3]
+        images.append(
+            lax.dot_general(matrix[:, :cut], vectors[:, :cut], NT, preferred_element_type=F32).T
+        )
+        tails.append(vectors[:, cut:])
+    none = jnp.zeros_like(tails[0])
+    tails = jnp.concatenate(
+        [jnp.concatenate([tails[0], none], axis=1), jnp.concatenate([none, tails[1]], axis=1)],
+        axis=0,
+    )
+    matrix = jnp.concatenate([ovl[row, last], ovl[row + 1, last]], axis=1)
+    both = lax.dot_general(matrix, tails, NT, preferred_element_type=F32).T
+    vecs = none.shape[0]
+    return images[0] + both[:vecs], images[1] + both[vecs:]
 
 
 def cut_kernel(ints, sizes, trial, own, near, give, far, across, sizes_here, here, masked, sems):
@@ -152,8 +175,9 @@
 def term_kernel(ints, index, signs, own, inter, intra, ovl, out, inter_out, intra_out, ext):
     core = ints[0]
     fill_ext(core, own, intra, inter, ext)
-    for row in range(own.shape[0]):
-        out[row] = (-one_row((index, signs), ext, ovl, row)).astype(BF16)
+    for row in range(0, own.shape[0], 2):
+        for i, image in enumerate(two_rows((index, signs), ext, ovl, row)):
+            out[row + i] = (-image).astype(BF16)
     send_ends(core, out, intra_out, inter_out)
 
 
@@ -166,8 +190,10 @@
     half = own.shape[0]
     fill_ext(core, own, intra, inter, ext)
     lane = lax.broadcasted_iota(jnp.int32, own.shape[1:], 1)
-    for row in range(half):
-        image = one_row((index, signs), ext, ovl, row)
+    images = []
+    for row in range(0, half, 2):
+        images += two_rows((index, signs), ext, ovl, row)
+    for row, image in enumerate(images):
         filtered = scaled[row].astype(F32) + own[row].astype(F32) - image
         if not first:
             filtered = 2.0 * filtered - previous[row].astype(F32)

time: 127 us -> 127 us (level)
  no operation moved by 1% of the time
where the time goes in v11:
time: 127 us
  starting transfers between devices  62.6 us (49%)
  Pallas kernels  44.1 us (35%)
  waiting for transfers between devices  17.4 us (14%)
  between operations  2.31 us (2%)
    ppermute x25, starting transfers between devices, swap_chips(): return lax.ppermute(value, ('row', 'col'), pairs)  49.8 us
    pallas_call x30, Pallas kernels, call(): pl.pallas_call(kernel, name=name, out_shape=outs, in_specs=[SMEM] * len(s...  39.5 us
    ppermute x25, waiting for transfers between devices, swap_chips(): return lax.ppermute(value, ('row', 'col'), pairs)  7.83 us
    ppermute x3, starting transfers between devices, local(): lax.ppermute(summed, 'row', [(r, r ^ step) for r in range(num_rows)])  4.45 us
    ppermute x3, starting transfers between devices, from_chip(): return lax.ppermute(value, 'col', pairs)  4.29 us
    ppermute x3, waiting for transfers between devices, from_chip(): return lax.ppermute(value, 'col', pairs)  3.98 us
    ppermute x1, starting transfers between devices, next_chips(): return lax.ppermute(value, ('row', 'col'), pairs)  3.08 us
    ppermute x3, waiting for transfers between devices, local(): lax.ppermute(summed, 'row', [(r, r ^ step) for r in range(num_rows)])  3.07 us
  transfers between devices with their start and end apart: 64, of which 21 were waited for; matrix products, arithmetic and copies ran while one was open for 0% of the time, Pallas kernels for 24%

profile of v11, /device:TPU:0, one launch (start us, length us, event | category | flops | bytes accessed | tf_op | source)
XLA Modules:
  0.0 126.5 jit_solution(1256006956571442207)
XLA Ops:
  0.7 1.6 %cut.1 = (bf16[8,64,128]{2,1,0:T(8,128)(2,1)S(1)}, bf16[5,64,128]{2,1,0:T(8,128)(2,1)S(1)}, bf16[13,64,128]{2,1,0:T(8,128)(2,1)S(1)}, bf16[5,64,128]{2,1,0:T(8,128)(2,1)S(1)}, bf16[5,64,128]{2,1,0:T(8,128)(2,1)S(1)}) custom-call(s32[5]{0:T(128)S(1)} %stack.23.ints, s32[16]{0:T(128)} %sizes.3, bf16[64,2048]{1,0:T(8,128)(2,1)} %trial.1), custom_call_target="tpu_custom_call" | custom-call | tf_op jit(solution)/shard_map/cut/pallas_call | solution.py:529
  2.3 3.1 %collective-permute-start.1 = (bf16[5,64,128]{2,1,0:T(8,128)(2,1)S(1)}, bf16[5,64,128]{2,1,0:T(8,128)(2,1)S(1)}, u32[]{:S(2)}, u32[]{:S(2)}) collective-permute-start(bf16[5,64,128]{2,1,0:T(8,128)(2,1)S(1)} %get-tuple-element.105), channel_id=1, source_target_pairs={{0,4},{1,13},{2,6},{3,15},{4,8},{5,1},{6,10},{7,3},{8,12},{9,5},{1... | collective-permute-start | bytes 245768 | tf_op jit(solution)/shard_map/ppermute | solution.py:487
  5.4 1.6 %collective-permute-start.2 = (bf16[5,64,128]{2,1,0:T(8,128)(2,1)S(1)}, bf16[5,64,128]{2,1,0:T(8,128)(2,1)S(1)}, u32[]{:S(2)}, u32[]{:S(2)}) collective-permute-start(bf16[5,64,128]{2,1,0:T(8,128)(2,1)S(1)} %get-tuple-element.106), channel_id=1, source_target_pairs={{1,4},{4,1},{3,6},{6,3},{5,8},{8,5},{7,10},{10,7},{9,12},{12,9},{1... | collective-permute-start | bytes 245768 | tf_op jit(solution)/shard_map/ppermute | solution.py:479
  8.4 3.0 %load.1 = (bf16[8,9,128,128]{3,2,1,0:T(8,128)(2,1)S(1)}, bf16[8,9,128,128]{3,2,1,0:T(8,128)(2,1)S(1)}, s32[8,9]{1,0:T(8,128)S(4)}, f32[8,9]{1,0:T(8,128)S(4)}, s32[12]{0:T(128)S(4)}, /*index=5*/f32[2]{0:T(128)S(4)}) custom-call(s32[5]{0:T(128)S(1)} %stack.23.ints, f32[1]{0:T(128)S(6)} %copy.10.shift, f32[1]{0:T(128)S(6)} %copy.11.width, s32[16,9]{1,0:T(8,128)} %columns.1, ...), custom_call_target="tpu_custom_call" | custom-call | bytes 9437184 | tf_op jit(solution)/shard_map/load/pallas_call | solution.py:546
  12.0 1.5 %scaled.8 = (bf16[8,64,128]{2,1,0:T(8,128)(2,1)S(1)}, bf16[5,64,128]{2,1,0:T(8,128)(2,1)S(1)}, bf16[5,64,128]{2,1,0:T(8,128)(2,1)S(1)}) custom-call(s32[12]{0:T(128)S(4)} %get-tuple-element.99.ints, s32[8,9]{1,0:T(8,128)S(4)} %get-tuple-element.100.index, f32[8,9]{1,0:T(8,128)S(4)} %get-tuple-element.101.signs, f32[2]{0:T(128)S(4)} %get-tuple-element.102.scal, ...), custom_call_target="tpu_custom_call" | custom-call | flops 7247757312 | bytes 56623104 | tf_op jit(solution)/shard_map/scaled/pallas_call | solution.py:500
  13.5 1.7 %collective-permute-start.7 = (bf16[5,64,128]{2,1,0:T(8,128)(2,1)S(1)}, bf16[5,64,128]{2,1,0:T(8,128)(2,1)S(1)}, u32[]{:S(2)}, u32[]{:S(2)}) collective-permute-start(bf16[5,64,128]{2,1,0:T(8,128)(2,1)S(1)} %get-tuple-element.120), channel_id=1, source_target_pairs={{1,4},{4,1},{3,6},{6,3},{5,8},{8,5},{7,10},{10,7},{9,12},{12,9},{1... | collective-permute-start | bytes 245768 | tf_op jit(solution)/shard_map/ppermute | solution.py:479
  15.2 1.5 %scaled.9 = (bf16[8,64,128]{2,1,0:T(8,128)(2,1)S(1)}, bf16[5,64,128]{2,1,0:T(8,128)(2,1)S(1)}, bf16[5,64,128]{2,1,0:T(8,128)(2,1)S(1)}) custom-call(s32[12]{0:T(128)S(4)} %get-tuple-element.99.ints, s32[8,9]{1,0:T(8,128)S(4)} %get-tuple-element.100.index, f32[8,9]{1,0:T(8,128)S(4)} %get-tuple-element.101.signs, f32[2]{0:T(128)S(4)} %get-tuple-element.102.scal, ...), custom_call_target="tpu_custom_call" | custom-call | flops 7247757312 | bytes 56623104 | tf_op jit(solution)/shard_map/scaled/pallas_call | solution.py:500
  16.7 1.9 %collective-permute-start.3 = (bf16[5,64,128]{2,1,0:T(8,128)(2,1)S(1)}, bf16[5,64,128]{2,1,0:T(8,128)(2,1)S(1)}, u32[]{:S(2)}, u32[]{:S(2)}) collective-permute-start(bf16[5,64,128]{2,1,0:T(8,128)(2,1)S(1)} %get-tuple-element.113), channel_id=1, source_target_pairs={{1,4},{4,1},{3,6},{6,3},{5,8},{8,5},{7,10},{10,7},{9,12},{12,9},{1... | collective-permute-start | bytes 245768 | tf_op jit(solution)/shard_map/ppermute | solution.py:479
  20.2 1.6 %collective-permute-start.9 = (bf16[5,64,128]{2,1,0:T(8,128)(2,1)S(1)}, bf16[5,64,128]{2,1,0:T(8,128)(2,1)S(1)}, u32[]{:S(2)}, u32[]{:S(2)}) collective-permute-start(bf16[5,64,128]{2,1,0:T(8,128)(2,1)S(1)} %get-tuple-element.123), channel_id=1, source_target_pairs={{1,4},{4,1},{3,6},{6,3},{5,8},{8,5},{7,10},{10,7},{9,12},{12,9},{1... | collective-permute-start | bytes 245768 | tf_op jit(solution)/shard_map/ppermute | solution.py:479
  23.5 1.9 %collective-permute-start.5 = (bf16[5,64,128]{2,1,0:T(8,128)(2,1)S(1)}, bf16[5,64,128]{2,1,0:T(8,128)(2,1)S(1)}, u32[]{:S(2)}, u32[]{:S(2)}) collective-permute-start(bf16[5,64,128]{2,1,0:T(8,128)(2,1)S(1)} %get-tuple-element.116), channel_id=1, source_target_pairs={{1,4},{4,1},{3,6},{6,3},{5,8},{8,5},{7,10},{10,7},{9,12},{12,9},{1... | collective-permute-start | bytes 245768 | tf_op jit(solution)/shard_map/ppermute | solution.py:479
  26.8 1.8 %collective-permute-start.11 = (bf16[5,64,128]{2,1,0:T(8,128)(2,1)S(1)}, bf16[5,64,128]{2,1,0:T(8,128)(2,1)S(1)}, u32[]{:S(2)}, u32[]{:S(2)}) collective-permute-start(bf16[5,64,128]{2,1,0:T(8,128)(2,1)S(1)} %get-tuple-element.126), channel_id=1, source_target_pairs={{1,4},{4,1},{3,6},{6,3},{5,8},{8,5},{7,10},{10,7},{9,12},{12,9},{1... | collective-permute-start | bytes 245768 | tf_op jit(solution)/shard_map/ppermute | solution.py:479
  30.1 2.0 %collective-permute-start.13 = (bf16[5,64,128]{2,1,0:T(8,128)(2,1)S(1)}, bf16[5,64,128]{2,1,0:T(8,128)(2,1)S(1)}, u32[]{:S(2)}, u32[]{:S(2)}) collective-permute-start(bf16[5,64,128]{2,1,0:T(8,128)(2,1)S(1)} %get-tuple-element.130), channel_id=1, source_target_pairs={{1,4},{4,1},{3,6},{6,3},{5,8},{8,5},{7,10},{10,7},{9,12},{12,9},{1... | collective-permute-start | bytes 245768 | tf_op jit(solution)/shard_map/ppermute | solution.py:479
  32.6 1.5 %scaled.10 = (bf16[8,64,128]{2,1,0:T(8,128)(2,1)S(1)}, bf16[5,64,128]{2,1,0:T(8,128)(2,1)S(1)}, bf16[5,64,128]{2,1,0:T(8,128)(2,1)S(1)}) custom-call(s32[12]{0:T(128)S(4)} %get-tuple-element.99.ints, s32[8,9]{1,0:T(8,128)S(4)} %get-tuple-element.100.index, f32[8,9]{1,0:T(8,128)S(4)} %get-tuple-element.101.signs, f32[2]{0:T(128)S(4)} %get-tuple-element.102.scal, ...), custom_call_target="tpu_custom_call" | custom-call | flops 7247757312 | bytes 56623104 | tf_op jit(solution)/shard_map/scaled/pallas_call | solution.py:500
  34.0 1.9 %collective-permute-start.19 = (bf16[5,64,128]{2,1,0:T(8,128)(2,1)S(1)}, bf16[5,64,128]{2,1,0:T(8,128)(2,1)S(1)}, u32[]{:S(2)}, u32[]{:S(2)}) collective-permute-start(bf16[5,64,128]{2,1,0:T(8,128)(2,1)S(1)} %get-tuple-element.140), channel_id=1, source_target_pairs={{1,4},{4,1},{3,6},{6,3},{5,8},{8,5},{7,10},{10,7},{9,12},{12,9},{1... | collective-permute-start | bytes 245768 | tf_op jit(solution)/shard_map/ppermute | solution.py:479
  35.9 1.5 %scaled.11 = (bf16[8,64,128]{2,1,0:T(8,128)(2,1)S(1)}, bf16[5,64,128]{2,1,0:T(8,128)(2,1)S(1)}, bf16[5,64,128]{2,1,0:T(8,128)(2,1)S(1)}) custom-call(s32[12]{0:T(128)S(4)} %get-tuple-element.99.ints, s32[8,9]{1,0:T(8,128)S(4)} %get-tuple-element.100.index, f32[8,9]{1,0:T(8,128)S(4)} %get-tuple-element.101.signs, f32[2]{0:T(128)S(4)} %get-tuple-element.102.scal, ...), custom_call_target="tpu_custom_call" | custom-call | flops 7247757312 | bytes 56623104 | tf_op jit(solution)/shard_map/scaled/pallas_call | solution.py:500
  37.4 2.0 %collective-permute-start.15 = (bf16[5,64,128]{2,1,0:T(8,128)(2,1)S(1)}, bf16[5,64,128]{2,1,0:T(8,128)(2,1)S(1)}, u32[]{:S(2)}, u32[]{:S(2)}) collective-permute-start(bf16[5,64,128]{2,1,0:T(8,128)(2,1)S(1)} %get-tuple-element.133), channel_id=1, source_target_pairs={{1,4},{4,1},{3,6},{6,3},{5,8},{8,5},{7,10},{10,7},{9,12},{12,9},{1... | collective-permute-start | bytes 245768 | tf_op jit(solution)/shard_map/ppermute | solution.py:479
  40.7 1.9 %collective-permute-start.21 = (bf16[5,64,128]{2,1,0:T(8,128)(2,1)S(1)}, bf16[5,64,128]{2,1,0:T(8,128)(2,1)S(1)}, u32[]{:S(2)}, u32[]{:S(2)}) collective-permute-start(bf16[5,64,128]{2,1,0:T(8,128)(2,1)S(1)} %get-tuple-element.143), channel_id=1, source_target_pairs={{1,4},{4,1},{3,6},{6,3},{5,8},{8,5},{7,10},{10,7},{9,12},{12,9},{1... | collective-permute-start | bytes 245768 | tf_op jit(solution)/shard_map/ppermute | solution.py:479
  44.0 2.1 %collective-permute-start.17 = (bf16[5,64,128]{2,1,0:T(8,128)(2,1)S(1)}, bf16[5,64,128]{2,1,0:T(8,128)(2,1)S(1)}, u32[]{:S(2)}, u32[]{:S(2)}) collective-permute-start(bf16[5,64,128]{2,1,0:T(8,128)(2,1)S(1)} %get-tuple-element.136), channel_id=1, source_target_pairs={{1,4},{4,1},{3,6},{6,3},{5,8},{8,5},{7,10},{10,7},{9,12},{12,9},{1... | collective-permute-start | bytes 245768 | tf_op jit(solution)/shard_map/ppermute | solution.py:479
  47.3 2.0 %collective-permute-start.23 = (bf16[5,64,128]{2,1,0:T(8,128)(2,1)S(1)}, bf16[5,64,128]{2,1,0:T(8,128)(2,1)S(1)}, u32[]{:S(2)}, u32[]{:S(2)}) collective-permute-start(bf16[5,64,128]{2,1,0:T(8,128)(2,1)S(1)} %get-tuple-element.146), channel_id=1, source_target_pairs={{1,4},{4,1},{3,6},{6,3},{5,8},{8,5},{7,10},{10,7},{9,12},{12,9},{1... | collective-permute-start | bytes 245768 | tf_op jit(solution)/shard_map/ppermute | solution.py:479
  50.7 2.2 %collective-permute-start.25 = (bf16[5,64,128]{2,1,0:T(8,128)(2,1)S(1)}, bf16[5,64,128]{2,1,0:T(8,128)(2,1)S(1)}, u32[]{:S(2)}, u32[]{:S(2)}) collective-permute-start(bf16[5,64,128]{2,1,0:T(8,128)(2,1)S(1)} %get-tuple-element.150), channel_id=1, source_target_pairs={{1,4},{4,1},{3,6},{6,3},{5,8},{8,5},{7,10},{10,7},{9,12},{12,9},{1... | collective-permute-start | bytes 245768 | tf_op jit(solution)/shard_map/ppermute | solution.py:479
  53.0 1.5 %scaled.12 = (bf16[8,64,128]{2,1,0:T(8,128)(2,1)S(1)}, bf16[5,64,128]{2,1,0:T(8,128)(2,1)S(1)}, bf16[5,64,128]{2,1,0:T(8,128)(2,1)S(1)}) custom-call(s32[12]{0:T(128)S(4)} %get-tuple-element.99.ints, s32[8,9]{1,0:T(8,128)S(4)} %get-tuple-element.100.index, f32[8,9]{1,0:T(8,128)S(4)} %get-tuple-element.101.signs, f32[2]{0:T(128)S(4)} %get-tuple-element.102.scal, ...), custom_call_target="tpu_custom_call" | custom-call | flops 7247757312 | bytes 56623104 | tf_op jit(solution)/shard_map/scaled/pallas_call | solution.py:500
  54.5 2.2 %collective-permute-start.31 = (bf16[5,64,128]{2,1,0:T(8,128)(2,1)S(1)}, bf16[5,64,128]{2,1,0:T(8,128)(2,1)S(1)}, u32[]{:S(2)}, u32[]{:S(2)}) collective-permute-start(bf16[5,64,128]{2,1,0:T(8,128)(2,1)S(1)} %get-tuple-element.160), channel_id=1, source_target_pairs={{1,4},{4,1},{3,6},{6,3},{5,8},{8,5},{7,10},{10,7},{9,12},{12,9},{1... | collective-permute-start | bytes 245768 | tf_op jit(solution)/shard_map/ppermute | solution.py:479
  56.7 1.5 %scaled.13 = (bf16[8,64,128]{2,1,0:T(8,128)(2,1)S(1)}, bf16[5,64,128]{2,1,0:T(8,128)(2,1)S(1)}, bf16[5,64,128]{2,1,0:T(8,128)(2,1)S(1)}) custom-call(s32[12]{0:T(128)S(4)} %get-tuple-element.99.ints, s32[8,9]{1,0:T(8,128)S(4)} %get-tuple-element.100.index, f32[8,9]{1,0:T(8,128)S(4)} %get-tuple-element.101.signs, f32[2]{0:T(128)S(4)} %get-tuple-element.102.scal, ...), custom_call_target="tpu_custom_call" | custom-call | flops 7247757312 | bytes 56623104 | tf_op jit(solution)/shard_map/scaled/pallas_call | solution.py:500
  58.2 2.0 %collective-permute-start.27 = (bf16[5,64,128]{2,1,0:T(8,128)(2,1)S(1)}, bf16[5,64,128]{2,1,0:T(8,128)(2,1)S(1)}, u32[]{:S(2)}, u32[]{:S(2)}) collective-permute-start(bf16[5,64,128]{2,1,0:T(8,128)(2,1)S(1)} %get-tuple-element.153), channel_id=1, source_target_pairs={{1,4},{4,1},{3,6},{6,3},{5,8},{8,5},{7,10},{10,7},{9,12},{12,9},{1... | collective-permute-start | bytes 245768 | tf_op jit(solution)/shard_map/ppermute | solution.py:479
  61.1 2.3 %collective-permute-start.33 = (bf16[5,64,128]{2,1,0:T(8,128)(2,1)S(1)}, bf16[5,64,128]{2,1,0:T(8,128)(2,1)S(1)}, u32[]{:S(2)}, u32[]{:S(2)}) collective-permute-start(bf16[5,64,128]{2,1,0:T(8,128)(2,1)S(1)} %get-tuple-element.163), channel_id=1, source_target_pairs={{1,4},{4,1},{3,6},{6,3},{5,8},{8,5},{7,10},{10,7},{9,12},{12,9},{1... | collective-permute-start | bytes 245768 | tf_op jit(solution)/shard_map/ppermute | solution.py:479
  64.8 2.1 %collective-permute-start.29 = (bf16[5,64,128]{2,1,0:T(8,128)(2,1)S(1)}, bf16[5,64,128]{2,1,0:T(8,128)(2,1)S(1)}, u32[]{:S(2)}, u32[]{:S(2)}) collective-permute-start(bf16[5,64,128]{2,1,0:T(8,128)(2,1)S(1)} %get-tuple-element.156), channel_id=1, source_target_pairs={{1,4},{4,1},{3,6},{6,3},{5,8},{8,5},{7,10},{10,7},{9,12},{12,9},{1... | collective-permute-start | bytes 245768 | tf_op jit(solution)/shard_map/ppermute | solution.py:479
  67.8 2.3 %collective-permute-start.35 = (bf16[5,64,128]{2,1,0:T(8,128)(2,1)S(1)}, bf16[5,64,128]{2,1,0:T(8,128)(2,1)S(1)}, u32[]{:S(2)}, u32[]{:S(2)}) collective-permute-start(bf16[5,64,128]{2,1,0:T(8,128)(2,1)S(1)} %get-tuple-element.166), channel_id=1, source_target_pairs={{1,4},{4,1},{3,6},{6,3},{5,8},{8,5},{7,10},{10,7},{9,12},{12,9},{1... | collective-permute-start | bytes 245768 | tf_op jit(solution)/shard_map/ppermute | solution.py:479
  71.4 2.3 %collective-permute-start.37 = (bf16[5,64,128]{2,1,0:T(8,128)(2,1)S(1)}, bf16[5,64,128]{2,1,0:T(8,128)(2,1)S(1)}, u32[]{:S(2)}, u32[]{:S(2)}) collective-permute-start(bf16[5,64,128]{2,1,0:T(8,128)(2,1)S(1)} %get-tuple-element.170), channel_id=1, source_target_pairs={{1,4},{4,1},{3,6},{6,3},{5,8},{8,5},{7,10},{10,7},{9,12},{12,9},{1... | collective-permute-start | bytes 245768 | tf_op jit(solution)/shard_map/ppermute | solution.py:479
  73.7 1.5 %scaled.14 = (bf16[8,64,128]{2,1,0:T(8,128)(2,1)S(1)}, bf16[5,64,128]{2,1,0:T(8,128)(2,1)S(1)}, bf16[5,64,128]{2,1,0:T(8,128)(2,1)S(1)}) custom-call(s32[12]{0:T(128)S(4)} %get-tuple-element.99.ints, s32[8,9]{1,0:T(8,128)S(4)} %get-tuple-element.100.index, f32[8,9]{1,0:T(8,128)S(4)} %get-tuple-element.101.signs, f32[2]{0:T(128)S(4)} %get-tuple-element.102.scal, ...), custom_call_target="tpu_custom_call" | custom-call | flops 7247757312 | bytes 56623104 | tf_op jit(solution)/shard_map/scaled/pallas_call | solution.py:500
  75.2 2.3 %collective-permute-start.43 = (bf16[5,64,128]{2,1,0:T(8,128)(2,1)S(1)}, bf16[5,64,128]{2,1,0:T(8,128)(2,1)S(1)}, u32[]{:S(2)}, u32[]{:S(2)}) collective-permute-start(bf16[5,64,128]{2,1,0:T(8,128)(2,1)S(1)} %get-tuple-element.180), channel_id=1, source_target_pairs={{1,4},{4,1},{3,6},{6,3},{5,8},{8,5},{7,10},{10,7},{9,12},{12,9},{1... | collective-permute-start | bytes 245768 | tf_op jit(solution)/shard_map/ppermute | solution.py:479
  77.5 1.5 %scaled.15 = (bf16[8,64,128]{2,1,0:T(8,128)(2,1)S(1)}, bf16[5,64,128]{2,1,0:T(8,128)(2,1)S(1)}, bf16[5,64,128]{2,1,0:T(8,128)(2,1)S(1)}) custom-call(s32[12]{0:T(128)S(4)} %get-tuple-element.99.ints, s32[8,9]{1,0:T(8,128)S(4)} %get-tuple-element.100.index, f32[8,9]{1,0:T(8,128)S(4)} %get-tuple-element.101.signs, f32[2]{0:T(128)S(4)} %get-tuple-element.102.scal, ...), custom_call_target="tpu_custom_call" | custom-call | flops 7247757312 | bytes 56623104 | tf_op jit(solution)/shard_map/scaled/pallas_call | solution.py:500
  79.0 2.0 %collective-permute-start.39 = (bf16[5,64,128]{2,1,0:T(8,128)(2,1)S(1)}, bf16[5,64,128]{2,1,0:T(8,128)(2,1)S(1)}, u32[]{:S(2)}, u32[]{:S(2)}) collective-permute-start(bf16[5,64,128]{2,1,0:T(8,128)(2,1)S(1)} %get-tuple-element.173), channel_id=1, source_target_pairs={{1,4},{4,1},{3,6},{6,3},{5,8},{8,5},{7,10},{10,7},{9,12},{12,9},{1... | collective-permute-start | bytes 245768 | tf_op jit(solution)/shard_map/ppermute | solution.py:479
  81.9 2.3 %collective-permute-start.45 = (bf16[5,64,128]{2,1,0:T(8,128)(2,1)S(1)}, bf16[5,64,128]{2,1,0:T(8,128)(2,1)S(1)}, u32[]{:S(2)}, u32[]{:S(2)}) collective-permute-start(bf16[5,64,128]{2,1,0:T(8,128)(2,1)S(1)} %get-tuple-element.183), channel_id=1, source_target_pairs={{1,4},{4,1},{3,6},{6,3},{5,8},{8,5},{7,10},{10,7},{9,12},{12,9},{1... | collective-permute-start | bytes 245768 | tf_op jit(solution)/shard_map/ppermute | solution.py:479
  85.7 2.1 %collective-permute-start.41 = (bf16[5,64,128]{2,1,0:T(8,128)(2,1)S(1)}, bf16[5,64,128]{2,1,0:T(8,128)(2,1)S(1)}, u32[]{:S(2)}, u32[]{:S(2)}) collective-permute-start(bf16[5,64,128]{2,1,0:T(8,128)(2,1)S(1)} %get-tuple-element.176), channel_id=1, source_target_pairs={{1,4},{4,1},{3,6},{6,3},{5,8},{8,5},{7,10},{10,7},{9,12},{12,9},{1... | collective-permute-start | bytes 245768 | tf_op jit(solution)/shard_map/ppermute | solution.py:479
  88.7 2.3 %collective-permute-start.47 = (bf16[5,64,128]{2,1,0:T(8,128)(2,1)S(1)}, bf16[5,64,128]{2,1,0:T(8,128)(2,1)S(1)}, u32[]{:S(2)}, u32[]{:S(2)}) collective-permute-start(bf16[5,64,128]{2,1,0:T(8,128)(2,1)S(1)} %get-tuple-element.186), channel_id=1, source_target_pairs={{1,4},{4,1},{3,6},{6,3},{5,8},{8,5},{7,10},{10,7},{9,12},{12,9},{1... | collective-permute-start | bytes 245768 | tf_op jit(solution)/shard_map/ppermute | solution.py:479
  91.0 1.8 %collective-permute-start.49 = (bf16[8,64,128]{2,1,0:T(8,128)(2,1)S(1)}, bf16[8,64,128]{2,1,0:T(8,128)(2,1)S(1)}, u32[]{:S(2)}, u32[]{:S(2)}) collective-permute-start(bf16[8,64,128]{2,1,0:T(8,128)(2,1)S(1)} %get-tuple-element.185.own.refs_2_.refs_4_), channel_id=1, source_target_pairs={{2,0},{3,1},{0,2},{1,3},{6,4},{7,5},{4,6},{5,7},{10,8},{11,9},{8,1... | collective-permute-start | bytes 393224 | tf_op jit(solution)/shard_map/ppermute | solution.py:491
  94.6 1.4 %collective-permute-start.52 = (bf16[8,64,128]{2,1,0:T(8,128)(2,1)S(1)}, bf16[8,64,128]{2,1,0:T(8,128)(2,1)S(1)}, u32[]{:S(2)}, u32[]{:S(2)}) collective-permute-start(bf16[8,64,128]{2,1,0:T(8,128)(2,1)S(1)} %get-tuple-element.189.own.refs_3_.refs_5_), channel_id=1, source_target_pairs={{2,0},{3,1},{0,2},{1,3},{6,4},{7,5},{4,6},{5,7},{10,8},{11,9},{8,1... | collective-permute-start | bytes 393224 | tf_op jit(solution)/shard_map/ppermute | solution.py:491
  97.0 1.5 %images.2.refs_0_ = bf16[2,64,1024]{2,1,0:T(8,128)(2,1)S(1)} custom-call(s32[12]{0:T(128)S(4)} %get-tuple-element.99.ints, s32[8,9]{1,0:T(8,128)S(4)} %get-tuple-element.100.index, f32[8,9]{1,0:T(8,128)S(4)} %get-tuple-element.101.signs, bf16[8,64,128]{2,1,0:T(8,128)(2,1)S(1)} %get-tuple-element.185.own.refs_2_.refs_4_, ...), custom_call_target="tpu_custom_call" | custom-call | flops 7247757312 | bytes 56623104 | tf_op jit(solution)/shard_map/images/pallas_call | solution.py:500
  99.4 1.5 %images.3.refs_1_ = bf16[2,64,1024]{2,1,0:T(8,128)(2,1)S(1)} custom-call(s32[12]{0:T(128)S(4)} %get-tuple-element.99.ints, s32[8,9]{1,0:T(8,128)S(4)} %get-tuple-element.100.index, f32[8,9]{1,0:T(8,128)S(4)} %get-tuple-element.101.signs, bf16[8,64,128]{2,1,0:T(8,128)(2,1)S(1)} %get-tuple-element.189.own.refs_3_.refs_5_, ...), custom_call_target="tpu_custom_call" | custom-call | flops 7247757312 | bytes 56623104 | tf_op jit(solution)/shard_map/images/pallas_call | solution.py:500
  101.6 1.2 collective-permute-done.53.right
  102.9 2.2 %collective-permute-start.56 = (bf16[208,128]{1,0:T(8,128)(2,1)S(1)}, bf16[208,128]{1,0:T(8,128)(2,1)S(1)}, u32[]{:S(2)}, u32[]{:S(2)}) collective-permute-start(bf16[208,128]{1,0:T(8,128)(2,1)S(1)} %add.9.refs_0_), channel_id=1, source_target_pairs={{0,12},{4,8},{8,4},{12,0},{1,13},{5,9},{9,5},{13,1},{2,14},{6,10},... | collective-permute-start | bytes 159752 | tf_op jit(solution)/shard_map/ppermute | solution.py:652
  105.1 2.2 %collective-permute-start.54 = (bf16[208,128]{1,0:T(8,128)(2,1)S(1)}, bf16[208,128]{1,0:T(8,128)(2,1)S(1)}, u32[]{:S(2)}, u32[]{:S(2)}) collective-permute-start(bf16[208,128]{1,0:T(8,128)(2,1)S(1)} %add.9.refs_0_), channel_id=1, source_target_pairs={{0,4},{4,0},{8,12},{12,8},{1,5},{5,1},{9,13},{13,9},{2,6},{6,2},{1... | collective-permute-start | bytes 159752 | tf_op jit(solution)/shard_map/ppermute | solution.py:652
  107.8 1.5 %collective-permute-done.56.refs_3_ = bf16[208,128]{1,0:T(8,128)(2,1)S(1)} collective-permute-done((bf16[208,128]{1,0:T(8,128)(2,1)S(1)}, bf16[208,128]{1,0:T(8,128)(2,1)S(1)}, u32[]{:S(2)}, u32[]{:S(2)}) %collective-permute-start.56) | collective-permute-done | bytes 53280 | tf_op jit(solution)/shard_map/ppermute | solution.py:652
  109.3 1.6 %collective-permute-done.55.refs_2_ = bf16[208,128]{1,0:T(8,128)(2,1)S(1)} collective-permute-done((bf16[208,128]{1,0:T(8,128)(2,1)S(1)}, bf16[208,128]{1,0:T(8,128)(2,1)S(1)}, u32[]{:S(2)}, u32[]{:S(2)}) %collective-permute-start.55) | collective-permute-done | bytes 53280 | tf_op jit(solution)/shard_map/ppermute | solution.py:652
  111.0 1.1 collective-permute-start.57
  112.3 3.0 %collective-permute-done.57.refs_1_ = bf16[208,128]{1,0:T(8,128)(2,1)S(1)} collective-permute-done((bf16[208,128]{1,0:T(8,128)(2,1)S(1)}, bf16[208,128]{1,0:T(8,128)(2,1)S(1)}, u32[]{:S(2)}, u32[]{:S(2)}) %collective-permute-start.57) | collective-permute-done | bytes 53280 | tf_op jit(solution)/shard_map/ppermute | solution.py:491
  115.3 1.2 collective-permute-done.59.refs_3_
  116.5 10.0 %finish.1 = (bf16[64,2048]{1,0:T(8,128)(2,1)}, f32[64,256]{1,0:T(8,128)}) custom-call(s32[12]{0:T(128)S(4)} %get-tuple-element.99.ints, bf16[208,128]{1,0:T(8,128)(2,1)S(1)} %sum.1.refs_0_, bf16[208,128]{1,0:T(8,128)(2,1)S(1)} %collective-permute-done.57.refs_1_, bf16[208,128]{1,0:T(8,128)(2,1)S(1)} %collective-permute-done.58.refs_2_, ...), custom_call_target="tpu_custom_call" | custom-call | flops 36238786560 | bytes 283115520 | tf_op jit(solution)/shard_map/finish/pallas_call | solution.py:500
  (116 shorter events, 25.5 us)
Async XLA Ops:
  2.3 9.1 %collective-permute-start.1 = (bf16[5,64,128]{2,1,0:T(8,128)(2,1)S(1)}, bf16[5,64,128]{2,1,0:T(8,128)(2,1)S(1)}, u32[]{:S(2)}, u32[]{:S(2)}) collective-permute-start(bf16[5,64,128]{2,1,0:T(8,128)(2,1)S(1)} %get-tuple-element.105), channel_id=1, source_target_pairs={{0,4},{1,13},{2,6},{3,15},{4,8},{5,1},{6,10},{7,3},{8,12},{9,5},{1... | collective-permute-start | bytes 245768 | tf_op jit(solution)/shard_map/ppermute | solution.py:487
  5.4 6.5 %collective-permute-start.2 = (bf16[5,64,128]{2,1,0:T(8,128)(2,1)S(1)}, bf16[5,64,128]{2,1,0:T(8,128)(2,1)S(1)}, u32[]{:S(2)}, u32[]{:S(2)}) collective-permute-start(bf16[5,64,128]{2,1,0:T(8,128)(2,1)S(1)} %get-tuple-element.106), channel_id=1, source_target_pairs={{1,4},{4,1},{3,6},{6,3},{5,8},{8,5},{7,10},{10,7},{9,12},{12,9},{1... | collective-permute-start | bytes 245768 | tf_op jit(solution)/shard_map/ppermute | solution.py:479
  7.0 4.9 %collective-permute-start = (bf16[13,64,128]{2,1,0:T(8,128)(2,1)S(1)}, bf16[13,64,128]{2,1,0:T(8,128)(2,1)S(1)}, u32[]{:S(2)}, u32[]{:S(2)}) collective-permute-start(bf16[13,64,128]{2,1,0:T(8,128)(2,1)S(1)} %get-tuple-element.103), channel_id=1, source_target_pairs={{0,1},{1,0},{2,3},{3,2},{4,5},{5,4},{6,7},{7,6},{8,9},{9,8},{10,11... | collective-permute-start | bytes 638984 | tf_op jit(solution)/shard_map/ppermute | solution.py:470
  13.5 5.8 %collective-permute-start.7 = (bf16[5,64,128]{2,1,0:T(8,128)(2,1)S(1)}, bf16[5,64,128]{2,1,0:T(8,128)(2,1)S(1)}, u32[]{:S(2)}, u32[]{:S(2)}) collective-permute-start(bf16[5,64,128]{2,1,0:T(8,128)(2,1)S(1)} %get-tuple-element.120), channel_id=1, source_target_pairs={{1,4},{4,1},{3,6},{6,3},{5,8},{8,5},{7,10},{10,7},{9,12},{12,9},{1... | collective-permute-start | bytes 245768 | tf_op jit(solution)/shard_map/ppermute | solution.py:479
  15.2 4.1 %collective-permute-start.8 = (bf16[5,64,128]{2,1,0:T(8,128)(2,1)S(1)}, bf16[5,64,128]{2,1,0:T(8,128)(2,1)S(1)}, u32[]{:S(2)}, u32[]{:S(2)}) collective-permute-start(bf16[5,64,128]{2,1,0:T(8,128)(2,1)S(1)} %get-tuple-element.121), channel_id=1, source_target_pairs={{0,1},{1,0},{2,3},{3,2},{4,5},{5,4},{6,7},{7,6},{8,9},{9,8},{10,11... | collective-permute-start | bytes 245768 | tf_op jit(solution)/shard_map/ppermute | solution.py:470
  16.7 5.9 %collective-permute-start.3 = (bf16[5,64,128]{2,1,0:T(8,128)(2,1)S(1)}, bf16[5,64,128]{2,1,0:T(8,128)(2,1)S(1)}, u32[]{:S(2)}, u32[]{:S(2)}) collective-permute-start(bf16[5,64,128]{2,1,0:T(8,128)(2,1)S(1)} %get-tuple-element.113), channel_id=1, source_target_pairs={{1,4},{4,1},{3,6},{6,3},{5,8},{8,5},{7,10},{10,7},{9,12},{12,9},{1... | collective-permute-start | bytes 245768 | tf_op jit(solution)/shard_map/ppermute | solution.py:479
  18.6 4.0 %collective-permute-start.4 = (bf16[5,64,128]{2,1,0:T(8,128)(2,1)S(1)}, bf16[5,64,128]{2,1,0:T(8,128)(2,1)S(1)}, u32[]{:S(2)}, u32[]{:S(2)}) collective-permute-start(bf16[5,64,128]{2,1,0:T(8,128)(2,1)S(1)} %get-tuple-element.114), channel_id=1, source_target_pairs={{0,1},{1,0},{2,3},{3,2},{4,5},{5,4},{6,7},{7,6},{8,9},{9,8},{10,11... | collective-permute-start | bytes 245768 | tf_op jit(solution)/shard_map/ppermute | solution.py:470
  20.2 5.7 %collective-permute-start.9 = (bf16[5,64,128]{2,1,0:T(8,128)(2,1)S(1)}, bf16[5,64,128]{2,1,0:T(8,128)(2,1)S(1)}, u32[]{:S(2)}, u32[]{:S(2)}) collective-permute-start(bf16[5,64,128]{2,1,0:T(8,128)(2,1)S(1)} %get-tuple-element.123), channel_id=1, source_target_pairs={{1,4},{4,1},{3,6},{6,3},{5,8},{8,5},{7,10},{10,7},{9,12},{12,9},{1... | collective-permute-start | bytes 245768 | tf_op jit(solution)/shard_map/ppermute | solution.py:479
  21.8 4.1 %collective-permute-start.10 = (bf16[5,64,128]{2,1,0:T(8,128)(2,1)S(1)}, bf16[5,64,128]{2,1,0:T(8,128)(2,1)S(1)}, u32[]{:S(2)}, u32[]{:S(2)}) collective-permute-start(bf16[5,64,128]{2,1,0:T(8,128)(2,1)S(1)} %get-tuple-element.124), channel_id=1, source_target_pairs={{0,1},{1,0},{2,3},{3,2},{4,5},{5,4},{6,7},{7,6},{8,9},{9,8},{10,11... | collective-permute-start | bytes 245768 | tf_op jit(solution)/shard_map/ppermute | solution.py:470
  23.5 5.8 %collective-permute-start.5 = (bf16[5,64,128]{2,1,0:T(8,128)(2,1)S(1)}, bf16[5,64,128]{2,1,0:T(8,128)(2,1)S(1)}, u32[]{:S(2)}, u32[]{:S(2)}) collective-permute-start(bf16[5,64,128]{2,1,0:T(8,128)(2,1)S(1)} %get-tuple-element.116), channel_id=1, source_target_pairs={{1,4},{4,1},{3,6},{6,3},{5,8},{8,5},{7,10},{10,7},{9,12},{12,9},{1... | collective-permute-start | bytes 245768 | tf_op jit(solution)/shard_map/ppermute | solution.py:479
  25.4 3.9 %collective-permute-start.6 = (bf16[5,64,128]{2,1,0:T(8,128)(2,1)S(1)}, bf16[5,64,128]{2,1,0:T(8,128)(2,1)S(1)}, u32[]{:S(2)}, u32[]{:S(2)}) collective-permute-start(bf16[5,64,128]{2,1,0:T(8,128)(2,1)S(1)} %get-tuple-element.117), channel_id=1, source_target_pairs={{0,1},{1,0},{2,3},{3,2},{4,5},{5,4},{6,7},{7,6},{8,9},{9,8},{10,11... | collective-permute-start | bytes 245768 | tf_op jit(solution)/shard_map/ppermute | solution.py:470
  26.8 5.7 %collective-permute-start.11 = (bf16[5,64,128]{2,1,0:T(8,128)(2,1)S(1)}, bf16[5,64,128]{2,1,0:T(8,128)(2,1)S(1)}, u32[]{:S(2)}, u32[]{:S(2)}) collective-permute-start(bf16[5,64,128]{2,1,0:T(8,128)(2,1)S(1)} %get-tuple-element.126), channel_id=1, source_target_pairs={{1,4},{4,1},{3,6},{6,3},{5,8},{8,5},{7,10},{10,7},{9,12},{12,9},{1... | collective-permute-start | bytes 245768 | tf_op jit(solution)/shard_map/ppermute | solution.py:479
  28.6 4.0 %collective-permute-start.12 = (bf16[5,64,128]{2,1,0:T(8,128)(2,1)S(1)}, bf16[5,64,128]{2,1,0:T(8,128)(2,1)S(1)}, u32[]{:S(2)}, u32[]{:S(2)}) collective-permute-start(bf16[5,64,128]{2,1,0:T(8,128)(2,1)S(1)} %get-tuple-element.127), channel_id=1, source_target_pairs={{0,1},{1,0},{2,3},{3,2},{4,5},{5,4},{6,7},{7,6},{8,9},{9,8},{10,11... | collective-permute-start | bytes 245768 | tf_op jit(solution)/shard_map/ppermute | solution.py:470
  30.1 5.8 %collective-permute-start.13 = (bf16[5,64,128]{2,1,0:T(8,128)(2,1)S(1)}, bf16[5,64,128]{2,1,0:T(8,128)(2,1)S(1)}, u32[]{:S(2)}, u32[]{:S(2)}) collective-permute-start(bf16[5,64,128]{2,1,0:T(8,128)(2,1)S(1)} %get-tuple-element.130), channel_id=1, source_target_pairs={{1,4},{4,1},{3,6},{6,3},{5,8},{8,5},{7,10},{10,7},{9,12},{12,9},{1... | collective-permute-start | bytes 245768 | tf_op jit(solution)/shard_map/ppermute | solution.py:479
  34.0 5.7 %collective-permute-start.19 = (bf16[5,64,128]{2,1,0:T(8,128)(2,1)S(1)}, bf16[5,64,128]{2,1,0:T(8,128)(2,1)S(1)}, u32[]{:S(2)}, u32[]{:S(2)}) collective-permute-start(bf16[5,64,128]{2,1,0:T(8,128)(2,1)S(1)} %get-tuple-element.140), channel_id=1, source_target_pairs={{1,4},{4,1},{3,6},{6,3},{5,8},{8,5},{7,10},{10,7},{9,12},{12,9},{1... | collective-permute-start | bytes 245768 | tf_op jit(solution)/shard_map/ppermute | solution.py:479
  35.9 3.8 %collective-permute-start.20 = (bf16[5,64,128]{2,1,0:T(8,128)(2,1)S(1)}, bf16[5,64,128]{2,1,0:T(8,128)(2,1)S(1)}, u32[]{:S(2)}, u32[]{:S(2)}) collective-permute-start(bf16[5,64,128]{2,1,0:T(8,128)(2,1)S(1)} %get-tuple-element.141), channel_id=1, source_target_pairs={{0,1},{1,0},{2,3},{3,2},{4,5},{5,4},{6,7},{7,6},{8,9},{9,8},{10,11... | collective-permute-start | bytes 245768 | tf_op jit(solution)/shard_map/ppermute | solution.py:470
  37.4 5.7 %collective-permute-start.15 = (bf16[5,64,128]{2,1,0:T(8,128)(2,1)S(1)}, bf16[5,64,128]{2,1,0:T(8,128)(2,1)S(1)}, u32[]{:S(2)}, u32[]{:S(2)}) collective-permute-start(bf16[5,64,128]{2,1,0:T(8,128)(2,1)S(1)} %get-tuple-element.133), channel_id=1, source_target_pairs={{1,4},{4,1},{3,6},{6,3},{5,8},{8,5},{7,10},{10,7},{9,12},{12,9},{1... | collective-permute-start | bytes 245768 | tf_op jit(solution)/shard_map/ppermute | solution.py:479
  40.7 5.7 %collective-permute-start.21 = (bf16[5,64,128]{2,1,0:T(8,128)(2,1)S(1)}, bf16[5,64,128]{2,1,0:T(8,128)(2,1)S(1)}, u32[]{:S(2)}, u32[]{:S(2)}) collective-permute-start(bf16[5,64,128]{2,1,0:T(8,128)(2,1)S(1)} %get-tuple-element.143), channel_id=1, source_target_pairs={{1,4},{4,1},{3,6},{6,3},{5,8},{8,5},{7,10},{10,7},{9,12},{12,9},{1... | collective-permute-start | bytes 245768 | tf_op jit(solution)/shard_map/ppermute | solution.py:479
  42.6 3.8 %collective-permute-start.22 = (bf16[5,64,128]{2,1,0:T(8,128)(2,1)S(1)}, bf16[5,64,128]{2,1,0:T(8,128)(2,1)S(1)}, u32[]{:S(2)}, u32[]{:S(2)}) collective-permute-start(bf16[5,64,128]{2,1,0:T(8,128)(2,1)S(1)} %get-tuple-element.144), channel_id=1, source_target_pairs={{0,1},{1,0},{2,3},{3,2},{4,5},{5,4},{6,7},{7,6},{8,9},{9,8},{10,11... | collective-permute-start | bytes 245768 | tf_op jit(solution)/shard_map/ppermute | solution.py:470
  44.0 5.7 %collective-permute-start.17 = (bf16[5,64,128]{2,1,0:T(8,128)(2,1)S(1)}, bf16[5,64,128]{2,1,0:T(8,128)(2,1)S(1)}, u32[]{:S(2)}, u32[]{:S(2)}) collective-permute-start(bf16[5,64,128]{2,1,0:T(8,128)(2,1)S(1)} %get-tuple-element.136), channel_id=1, source_target_pairs={{1,4},{4,1},{3,6},{6,3},{5,8},{8,5},{7,10},{10,7},{9,12},{12,9},{1... | collective-permute-start | bytes 245768 | tf_op jit(solution)/shard_map/ppermute | solution.py:479
  47.3 5.7 %collective-permute-start.23 = (bf16[5,64,128]{2,1,0:T(8,128)(2,1)S(1)}, bf16[5,64,128]{2,1,0:T(8,128)(2,1)S(1)}, u32[]{:S(2)}, u32[]{:S(2)}) collective-permute-start(bf16[5,64,128]{2,1,0:T(8,128)(2,1)S(1)} %get-tuple-element.146), channel_id=1, source_target_pairs={{1,4},{4,1},{3,6},{6,3},{5,8},{8,5},{7,10},{10,7},{9,12},{12,9},{1... | collective-permute-start | bytes 245768 | tf_op jit(solution)/shard_map/ppermute | solution.py:479
  50.7 6.0 %collective-permute-start.25 = (bf16[5,64,128]{2,1,0:T(8,128)(2,1)S(1)}, bf16[5,64,128]{2,1,0:T(8,128)(2,1)S(1)}, u32[]{:S(2)}, u32[]{:S(2)}) collective-permute-start(bf16[5,64,128]{2,1,0:T(8,128)(2,1)S(1)} %get-tuple-element.150), channel_id=1, source_target_pairs={{1,4},{4,1},{3,6},{6,3},{5,8},{8,5},{7,10},{10,7},{9,12},{12,9},{1... | collective-permute-start | bytes 245768 | tf_op jit(solution)/shard_map/ppermute | solution.py:479
  54.5 5.7 %collective-permute-start.31 = (bf16[5,64,128]{2,1,0:T(8,128)(2,1)S(1)}, bf16[5,64,128]{2,1,0:T(8,128)(2,1)S(1)}, u32[]{:S(2)}, u32[]{:S(2)}) collective-permute-start(bf16[5,64,128]{2,1,0:T(8,128)(2,1)S(1)} %get-tuple-element.160), channel_id=1, source_target_pairs={{1,4},{4,1},{3,6},{6,3},{5,8},{8,5},{7,10},{10,7},{9,12},{12,9},{1... | collective-permute-start | bytes 245768 | tf_op jit(solution)/shard_map/ppermute | solution.py:479
  58.2 5.7 %collective-permute-start.27 = (bf16[5,64,128]{2,1,0:T(8,128)(2,1)S(1)}, bf16[5,64,128]{2,1,0:T(8,128)(2,1)S(1)}, u32[]{:S(2)}, u32[]{:S(2)}) collective-permute-start(bf16[5,64,128]{2,1,0:T(8,128)(2,1)S(1)} %get-tuple-element.153), channel_id=1, source_target_pairs={{1,4},{4,1},{3,6},{6,3},{5,8},{8,5},{7,10},{10,7},{9,12},{12,9},{1... | collective-permute-start | bytes 245768 | tf_op jit(solution)/shard_map/ppermute | solution.py:479
  61.1 5.8 %collective-permute-start.33 = (bf16[5,64,128]{2,1,0:T(8,128)(2,1)S(1)}, bf16[5,64,128]{2,1,0:T(8,128)(2,1)S(1)}, u32[]{:S(2)}, u32[]{:S(2)}) collective-permute-start(bf16[5,64,128]{2,1,0:T(8,128)(2,1)S(1)} %get-tuple-element.163), channel_id=1, source_target_pairs={{1,4},{4,1},{3,6},{6,3},{5,8},{8,5},{7,10},{10,7},{9,12},{12,9},{1... | collective-permute-start | bytes 245768 | tf_op jit(solution)/shard_map/ppermute | solution.py:479
  64.8 5.7 %collective-permute-start.29 = (bf16[5,64,128]{2,1,0:T(8,128)(2,1)S(1)}, bf16[5,64,128]{2,1,0:T(8,128)(2,1)S(1)}, u32[]{:S(2)}, u32[]{:S(2)}) collective-permute-start(bf16[5,64,128]{2,1,0:T(8,128)(2,1)S(1)} %get-tuple-element.156), channel_id=1, source_target_pairs={{1,4},{4,1},{3,6},{6,3},{5,8},{8,5},{7,10},{10,7},{9,12},{12,9},{1... | collective-permute-start | bytes 245768 | tf_op jit(solution)/shard_map/ppermute | solution.py:479
  67.8 5.9 %collective-permute-start.35 = (bf16[5,64,128]{2,1,0:T(8,128)(2,1)S(1)}, bf16[5,64,128]{2,1,0:T(8,128)(2,1)S(1)}, u32[]{:S(2)}, u32[]{:S(2)}) collective-permute-start(bf16[5,64,128]{2,1,0:T(8,128)(2,1)S(1)} %get-tuple-element.166), channel_id=1, source_target_pairs={{1,4},{4,1},{3,6},{6,3},{5,8},{8,5},{7,10},{10,7},{9,12},{12,9},{1... | collective-permute-start | bytes 245768 | tf_op jit(solution)/shard_map/ppermute | solution.py:479
  71.4 6.1 %collective-permute-start.37 = (bf16[5,64,128]{2,1,0:T(8,128)(2,1)S(1)}, bf16[5,64,128]{2,1,0:T(8,128)(2,1)S(1)}, u32[]{:S(2)}, u32[]{:S(2)}) collective-permute-start(bf16[5,64,128]{2,1,0:T(8,128)(2,1)S(1)} %get-tuple-element.170), channel_id=1, source_target_pairs={{1,4},{4,1},{3,6},{6,3},{5,8},{8,5},{7,10},{10,7},{9,12},{12,9},{1... | collective-permute-start | bytes 245768 | tf_op jit(solution)/shard_map/ppermute | solution.py:479
  73.7 3.8 %collective-permute-start.38 = (bf16[5,64,128]{2,1,0:T(8,128)(2,1)S(1)}, bf16[5,64,128]{2,1,0:T(8,128)(2,1)S(1)}, u32[]{:S(2)}, u32[]{:S(2)}) collective-permute-start(bf16[5,64,128]{2,1,0:T(8,128)(2,1)S(1)} %get-tuple-element.171), channel_id=1, source_target_pairs={{0,1},{1,0},{2,3},{3,2},{4,5},{5,4},{6,7},{7,6},{8,9},{9,8},{10,11... | collective-permute-start | bytes 245768 | tf_op jit(solution)/shard_map/ppermute | solution.py:470
  75.2 5.8 %collective-permute-start.43 = (bf16[5,64,128]{2,1,0:T(8,128)(2,1)S(1)}, bf16[5,64,128]{2,1,0:T(8,128)(2,1)S(1)}, u32[]{:S(2)}, u32[]{:S(2)}) collective-permute-start(bf16[5,64,128]{2,1,0:T(8,128)(2,1)S(1)} %get-tuple-element.180), channel_id=1, source_target_pairs={{1,4},{4,1},{3,6},{6,3},{5,8},{8,5},{7,10},{10,7},{9,12},{12,9},{1... | collective-permute-start | bytes 245768 | tf_op jit(solution)/shard_map/ppermute | solution.py:479
  79.0 5.7 %collective-permute-start.39 = (bf16[5,64,128]{2,1,0:T(8,128)(2,1)S(1)}, bf16[5,64,128]{2,1,0:T(8,128)(2,1)S(1)}, u32[]{:S(2)}, u32[]{:S(2)}) collective-permute-start(bf16[5,64,128]{2,1,0:T(8,128)(2,1)S(1)} %get-tuple-element.173), channel_id=1, source_target_pairs={{1,4},{4,1},{3,6},{6,3},{5,8},{8,5},{7,10},{10,7},{9,12},{12,9},{1... | collective-permute-start | bytes 245768 | tf_op jit(solution)/shard_map/ppermute | solution.py:479
  81.9 5.9 %collective-permute-start.45 = (bf16[5,64,128]{2,1,0:T(8,128)(2,1)S(1)}, bf16[5,64,128]{2,1,0:T(8,128)(2,1)S(1)}, u32[]{:S(2)}, u32[]{:S(2)}) collective-permute-start(bf16[5,64,128]{2,1,0:T(8,128)(2,1)S(1)} %get-tuple-element.183), channel_id=1, source_target_pairs={{1,4},{4,1},{3,6},{6,3},{5,8},{8,5},{7,10},{10,7},{9,12},{12,9},{1... | collective-permute-start | bytes 245768 | tf_op jit(solution)/shard_map/ppermute | solution.py:479
  85.7 7.2 %collective-permute-start.41 = (bf16[5,64,128]{2,1,0:T(8,128)(2,1)S(1)}, bf16[5,64,128]{2,1,0:T(8,128)(2,1)S(1)}, u32[]{:S(2)}, u32[]{:S(2)}) collective-permute-start(bf16[5,64,128]{2,1,0:T(8,128)(2,1)S(1)} %get-tuple-element.176), channel_id=1, source_target_pairs={{1,4},{4,1},{3,6},{6,3},{5,8},{8,5},{7,10},{10,7},{9,12},{12,9},{1... | collective-permute-start | bytes 245768 | tf_op jit(solution)/shard_map/ppermute | solution.py:479
  87.8 5.0 %collective-permute-start.42 = (bf16[5,64,128]{2,1,0:T(8,128)(2,1)S(1)}, bf16[5,64,128]{2,1,0:T(8,128)(2,1)S(1)}, u32[]{:S(2)}, u32[]{:S(2)}) collective-permute-start(bf16[5,64,128]{2,1,0:T(8,128)(2,1)S(1)} %get-tuple-element.177), channel_id=1, source_target_pairs={{0,1},{1,0},{2,3},{3,2},{4,5},{5,4},{6,7},{7,6},{8,9},{9,8},{10,11... | collective-permute-start | bytes 245768 | tf_op jit(solution)/shard_map/ppermute | solution.py:470
  88.7 5.9 %collective-permute-start.47 = (bf16[5,64,128]{2,1,0:T(8,128)(2,1)S(1)}, bf16[5,64,128]{2,1,0:T(8,128)(2,1)S(1)}, u32[]{:S(2)}, u32[]{:S(2)}) collective-permute-start(bf16[5,64,128]{2,1,0:T(8,128)(2,1)S(1)} %get-tuple-element.186), channel_id=1, source_target_pairs={{1,4},{4,1},{3,6},{6,3},{5,8},{8,5},{7,10},{10,7},{9,12},{12,9},{1... | collective-permute-start | bytes 245768 | tf_op jit(solution)/shard_map/ppermute | solution.py:479
  91.0 5.0 %collective-permute-start.48 = (bf16[5,64,128]{2,1,0:T(8,128)(2,1)S(1)}, bf16[5,64,128]{2,1,0:T(8,128)(2,1)S(1)}, u32[]{:S(2)}, u32[]{:S(2)}) collective-permute-start(bf16[5,64,128]{2,1,0:T(8,128)(2,1)S(1)} %get-tuple-element.187), channel_id=1, source_target_pairs={{0,1},{1,0},{2,3},{3,2},{4,5},{5,4},{6,7},{7,6},{8,9},{9,8},{10,11... | collective-permute-start | bytes 245768 | tf_op jit(solution)/shard_map/ppermute | solution.py:470
  91.0 6.0 %collective-permute-start.49 = (bf16[8,64,128]{2,1,0:T(8,128)(2,1)S(1)}, bf16[8,64,128]{2,1,0:T(8,128)(2,1)S(1)}, u32[]{:S(2)}, u32[]{:S(2)}) collective-permute-start(bf16[8,64,128]{2,1,0:T(8,128)(2,1)S(1)} %get-tuple-element.185.own.refs_2_.refs_4_), channel_id=1, source_target_pairs={{2,0},{3,1},{0,2},{1,3},{6,4},{7,5},{4,6},{5,7},{10,8},{11,9},{8,1... | collective-permute-start | bytes 393224 | tf_op jit(solution)/shard_map/ppermute | solution.py:491
  93.7 5.7 %collective-permute-start.50 = (bf16[5,64,128]{2,1,0:T(8,128)(2,1)S(1)}, bf16[5,64,128]{2,1,0:T(8,128)(2,1)S(1)}, u32[]{:S(2)}, u32[]{:S(2)}) collective-permute-start(bf16[5,64,128]{2,1,0:T(8,128)(2,1)S(1)} %get-tuple-element.190), channel_id=1, source_target_pairs={{1,4},{4,1},{3,6},{6,3},{5,8},{8,5},{7,10},{10,7},{9,12},{12,9},{1... | collective-permute-start | bytes 245768 | tf_op jit(solution)/shard_map/ppermute | solution.py:479
  94.6 4.9 %collective-permute-start.51 = (bf16[5,64,128]{2,1,0:T(8,128)(2,1)S(1)}, bf16[5,64,128]{2,1,0:T(8,128)(2,1)S(1)}, u32[]{:S(2)}, u32[]{:S(2)}) collective-permute-start(bf16[5,64,128]{2,1,0:T(8,128)(2,1)S(1)} %get-tuple-element.191), channel_id=1, source_target_pairs={{0,1},{1,0},{2,3},{3,2},{4,5},{5,4},{6,7},{7,6},{8,9},{9,8},{10,11... | collective-permute-start | bytes 245768 | tf_op jit(solution)/shard_map/ppermute | solution.py:470
  94.6 6.3 %collective-permute-start.52 = (bf16[8,64,128]{2,1,0:T(8,128)(2,1)S(1)}, bf16[8,64,128]{2,1,0:T(8,128)(2,1)S(1)}, u32[]{:S(2)}, u32[]{:S(2)}) collective-permute-start(bf16[8,64,128]{2,1,0:T(8,128)(2,1)S(1)} %get-tuple-element.189.own.refs_3_.refs_5_), channel_id=1, source_target_pairs={{2,0},{3,1},{0,2},{1,3},{6,4},{7,5},{4,6},{5,7},{10,8},{11,9},{8,1... | collective-permute-start | bytes 393224 | tf_op jit(solution)/shard_map/ppermute | solution.py:491
  102.9 6.4 %collective-permute-start.56 = (bf16[208,128]{1,0:T(8,128)(2,1)S(1)}, bf16[208,128]{1,0:T(8,128)(2,1)S(1)}, u32[]{:S(2)}, u32[]{:S(2)}) collective-permute-start(bf16[208,128]{1,0:T(8,128)(2,1)S(1)} %add.9.refs_0_), channel_id=1, source_target_pairs={{0,12},{4,8},{8,4},{12,0},{1,13},{5,9},{9,5},{13,1},{2,14},{6,10},... | collective-permute-start | bytes 159752 | tf_op jit(solution)/shard_map/ppermute | solution.py:652
  105.1 5.8 %collective-permute-start.55 = (bf16[208,128]{1,0:T(8,128)(2,1)S(1)}, bf16[208,128]{1,0:T(8,128)(2,1)S(1)}, u32[]{:S(2)}, u32[]{:S(2)}) collective-permute-start(bf16[208,128]{1,0:T(8,128)(2,1)S(1)} %add.9.refs_0_), channel_id=1, source_target_pairs={{0,8},{4,12},{8,0},{12,4},{1,9},{5,13},{9,1},{13,5},{2,10},{6,14},... | collective-permute-start | bytes 159752 | tf_op jit(solution)/shard_map/ppermute | solution.py:652
  105.1 5.8 %collective-permute-start.54 = (bf16[208,128]{1,0:T(8,128)(2,1)S(1)}, bf16[208,128]{1,0:T(8,128)(2,1)S(1)}, u32[]{:S(2)}, u32[]{:S(2)}) collective-permute-start(bf16[208,128]{1,0:T(8,128)(2,1)S(1)} %add.9.refs_0_), channel_id=1, source_target_pairs={{0,4},{4,0},{8,12},{12,8},{1,5},{5,1},{9,13},{13,9},{2,6},{6,2},{1... | collective-permute-start | bytes 159752 | tf_op jit(solution)/shard_map/ppermute | solution.py:652
  107.3 4.7 %collective-permute-start.60 = (bf16[8,64,128]{2,1,0:T(8,128)(2,1)S(1)}, bf16[8,64,128]{2,1,0:T(8,128)(2,1)S(1)}, u32[]{:S(2)}, u32[]{:S(2)}) collective-permute-start(bf16[8,64,128]{2,1,0:T(8,128)(2,1)S(1)} %get-tuple-element.185.own.refs_2_.refs_4_), channel_id=1, source_target_pairs={{0,1},{1,0},{2,3},{3,2},{4,5},{5,4},{6,7},{7,6},{8,9},{9,8},{10,11... | collective-permute-start | bytes 393224 | tf_op jit(solution)/shard_map/ppermute | solution.py:470
  107.3 8.0 %collective-permute-start.61 = (bf16[8,64,128]{2,1,0:T(8,128)(2,1)S(1)}, bf16[8,64,128]{2,1,0:T(8,128)(2,1)S(1)}, u32[]{:S(2)}, u32[]{:S(2)}) collective-permute-start(bf16[8,64,128]{2,1,0:T(8,128)(2,1)S(1)} %get-tuple-element.189.own.refs_3_.refs_5_), channel_id=1, source_target_pairs={{0,1},{1,0},{2,3},{3,2},{4,5},{5,4},{6,7},{7,6},{8,9},{9,8},{10,11... | collective-permute-start | bytes 393224 | tf_op jit(solution)/shard_map/ppermute | solution.py:470
  109.3 6.0 %collective-permute-start.62 = (bf16[8,64,128]{2,1,0:T(8,128)(2,1)S(1)}, bf16[8,64,128]{2,1,0:T(8,128)(2,1)S(1)}, u32[]{:S(2)}, u32[]{:S(2)}) collective-permute-start(bf16[8,64,128]{2,1,0:T(8,128)(2,1)S(1)} %collective-permute-done.49.y_other.refs_4_.refs_6_), channel_id=1, source_target_pairs={{0,1},{1,0},{2,3},{3,2},{4,5},{5,4},{6,7},{7,6},{8,9},{9,8},{10,11... | collective-permute-start | bytes 393224 | tf_op jit(solution)/shard_map/ppermute | solution.py:470
  110.9 4.4 %collective-permute-start.63 = (bf16[8,64,128]{2,1,0:T(8,128)(2,1)S(1)}, bf16[8,64,128]{2,1,0:T(8,128)(2,1)S(1)}, u32[]{:S(2)}, u32[]{:S(2)}) collective-permute-start(bf16[8,64,128]{2,1,0:T(8,128)(2,1)S(1)} %collective-permute-done.52.refs_5_.refs_7_), channel_id=1, source_target_pairs={{0,1},{1,0},{2,3},{3,2},{4,5},{5,4},{6,7},{7,6},{8,9},{9,8},{10,11... | collective-permute-start | bytes 393224 | tf_op jit(solution)/shard_map/ppermute | solution.py:470
  111.0 4.3 %collective-permute-start.57 = (bf16[208,128]{1,0:T(8,128)(2,1)S(1)}, bf16[208,128]{1,0:T(8,128)(2,1)S(1)}, u32[]{:S(2)}, u32[]{:S(2)}) collective-permute-start(bf16[208,128]{1,0:T(8,128)(2,1)S(1)} %sum.1.refs_0_), channel_id=1, source_target_pairs={{2,0},{3,1},{0,2},{1,3},{6,4},{7,5},{4,6},{5,7},{10,8},{11,9},{8,1... | collective-permute-start | bytes 159752 | tf_op jit(solution)/shard_map/ppermute | solution.py:491
  (16 other events, 53.4 us)
